TPU v7x, 32 devices: a whole 2x2x4 slice. The times are simulated.
32 devices in a mesh: gx: 4 (over x, core), gy: 8 (over z, y).
Axes of the slice: x: 2, y: 2, z: 4, core: 2. Of those that a mesh axis runs over, the one named last changes fastest.
Arguments:
- phase: float32 [4, 16, 32, 32, 128], P('gx', 'gy'), may hold values from -1 to 1
- solute: float32 [4, 16, 32, 32, 128], P('gx', 'gy'), may hold values from -2.5 to 2.5
- undercool: float32 [4, 16], P('gx', 'gy'), may hold values from -0.5 to 0.5
- mobility: float32 [4, 16], P('gx', 'gy'), may hold values from 0.03 to 0.08
- diffusivity: float32 [4, 16], P('gx', 'gy'), may hold values from 0.04 to 0.14
- owner: int32 [4, 16], P('gx', 'gy'), may hold values from 0 to 31, as said below
Outputs:
- phase_out: float32 [32, 2, 32, 32, 128], P(('gx', 'gy'))
- solute_out: float32 [32, 2, 32, 32, 128], P(('gx', 'gy'))
Inputs may be any that keep to these rules, and one draw needn't show every extreme that they name: A tile (p, q) is owned by one of the owners i*8 to i*8+8-1 with i = p. Each owner receives exactly 2 tiles; no device's tiles include more than 1 tiles of one owner, and some device's include exactly 1.
All inputs are finite; a program needn't handle non-finite values.
Results may differ from a plain program's by a relative error of at most 0.0003.
Values sent between devices are 32-bit elements; how exact they have to be, the bound alone decides.
No kernel may reach another device: no remote copies, remote signals or barrier semaphores. Data moves between devices by JAX's collectives and lax.ppermute only.
A program may use at most 192 MiB of HBM per device.

v0:
```python
import jax
import jax.numpy as jnp
from jax import lax
from jax.sharding import PartitionSpec as P

NSTEPS = 4


aniso_strength = 0.05
coupling = 2.0


def extended(block, sides, width):
    for axis, dim in sides:
        count = lax.axis_size(axis)
        forward = [(i, i + 1) for i in range(count - 1)]
        forward.append((count - 1, 0))
        backward = [(target, source) for source, target in forward]
        low = lax.ppermute(
            lax.slice_in_dim(block, block.shape[dim] - width, None, axis=dim), axis, forward
        )
        high = lax.ppermute(lax.slice_in_dim(block, 0, width, axis=dim), axis, backward)
        block = jnp.concatenate([low, block, high], axis=dim)
    return block


def step_cells(phase, solute, phase_near, solute_near, under, mobile, spread):
    lower_first, upper_first, lower_second, upper_second, lower_third, upper_third = phase_near
    slope_first = 0.5 * (upper_first - lower_first)
    slope_second = 0.5 * (upper_second - lower_second)
    slope_third = 0.5 * (upper_third - lower_third)
    lap_phase = (
        upper_first
        + lower_first
        + upper_second
        + lower_second
        + upper_third
        + lower_third
        - 6.0 * phase
    )
    sol_lf, sol_uf, sol_ls, sol_us, sol_lt, sol_ut = solute_near
    lap_solute = sol_uf + sol_lf + sol_us + sol_ls + sol_ut + sol_lt - 6.0 * solute
    square_first = slope_first * slope_first
    square_second = slope_second * slope_second
    square_third = slope_third * slope_third
    grad_two = square_first + square_second + square_third
    grad_four = (
        square_first * square_first + square_second * square_second + square_third * square_third
    )
    aniso = 1.0 + aniso_strength * (4.0 * grad_four - 3.0 * grad_two * grad_two) / (
        (1.0 + grad_two) * (1.0 + grad_two)
    )
    well = 1.0 - phase * phase
    new_phase = phase + mobile * (
        aniso * lap_phase
        + phase
        - phase * phase * phase
        - coupling * well * well * (under + solute)
    )
    new_solute = solute + spread * lap_solute + 0.5 * (new_phase - phase)
    return (new_phase, new_solute)


def neighbours(field, lower_x, upper_x, lower_y, upper_y):
    return (
        jnp.concatenate([lower_x[:, None], field[:, :-1]], 1),
        jnp.concatenate([field[:, 1:], upper_x[:, None]], 1),
        jnp.concatenate([lower_y[:, :, None], field[:, :, :-1]], 2),
        jnp.concatenate([field[:, :, 1:], upper_y[:, :, None]], 2),
        jnp.concatenate([field[..., :1], field[..., :-1]], 3),
        jnp.concatenate([field[..., 1:], field[..., -1:]], 3),
    )


def advance(phase, solute, halo_faces, coefficients):
    under = coefficients[:, 0][:, None, None, None]
    mobile = coefficients[:, 1][:, None, None, None]
    spread = coefficients[:, 2][:, None, None, None]
    phase_near = neighbours(
        phase, halo_faces[:, 0], halo_faces[:, 1], halo_faces[:, 2], halo_faces[:, 3]
    )
    solute_near = neighbours(
        solute, halo_faces[:, 4], halo_faces[:, 5], halo_faces[:, 6], halo_faces[:, 7]
    )
    return step_cells(phase, solute, phase_near, solute_near, under, mobile, spread)


def boundary_faces(phase, solute):
    return jnp.stack(
        [
            phase[:, 0],
            phase[:, -1],
            phase[:, :, 0],
            phase[:, :, -1],
            solute[:, 0],
            solute[:, -1],
            solute[:, :, 0],
            solute[:, :, -1],
        ],
        axis=1,
    )


def home_halos(grid_faces, block_x, block_y):
    padded = extended(grid_faces, (("gx", 0), ("gy", 1)), 1)
    before_x = padded[0:block_x, 1 : block_y + 1]
    after_x = padded[2 : block_x + 2, 1 : block_y + 1]
    before_y = padded[1 : block_x + 1, 0:block_y]
    after_y = padded[1 : block_x + 1, 2 : block_y + 2]
    gathered = jnp.stack(
        [
            before_x[:, :, 1],
            after_x[:, :, 0],
            before_y[:, :, 3],
            after_y[:, :, 2],
            before_x[:, :, 5],
            after_x[:, :, 4],
            before_y[:, :, 7],
            after_y[:, :, 6],
        ],
        axis=2,
    )
    return gathered.reshape((block_x * block_y,) + gathered.shape[2:])


def place(values, target, slots):
    return jnp.zeros((slots,) + values.shape[1:], values.dtype).at[target].set(values)


def pick_slots(present, tiles_here, slots):
    position = jnp.cumsum(present) - 1
    wanted = (position[None, :] == jnp.arange(tiles_here, dtype=jnp.int32)[:, None]) & (
        present[None, :] == 1
    )
    return jnp.sum(jnp.where(wanted, jnp.arange(slots, dtype=jnp.int32)[None, :], 0), axis=1)


def per_device(phase, solute, undercool, mobility, diffusivity, owner):
    block_x, block_y = owner.shape
    tiles_here = block_x * block_y
    edge = phase.shape[2]
    depth = phase.shape[4]
    mesh_y = lax.axis_size("gy")
    capacity = max(1, tiles_here // mesh_y)
    slots = mesh_y * capacity
    owner_flat = owner.reshape(tiles_here)
    peer = owner_flat % mesh_y
    matches = (peer[:, None] == jnp.arange(mesh_y, dtype=jnp.int32)[None, :]).astype(jnp.int32)
    earlier = jnp.cumsum(matches, axis=0) - matches
    sender_rank = jnp.sum(earlier * matches, axis=1)
    target = peer * capacity + sender_rank
    flag_send = jnp.zeros((slots,), jnp.int32).at[target].set(1)
    phase_tiles = phase.reshape(tiles_here, edge, edge, depth)
    solute_tiles = solute.reshape(tiles_here, edge, edge, depth)
    coefficients = jnp.stack(
        [
            undercool.reshape(tiles_here),
            mobility.reshape(tiles_here),
            diffusivity.reshape(tiles_here),
        ],
        axis=1,
    )
    grid_faces = boundary_faces(phase_tiles, solute_tiles).reshape(block_x, block_y, 8, edge, depth)
    first_halos = home_halos(grid_faces, block_x, block_y)
    arrived = (
        lax.all_to_all(
            place(phase_tiles, target, slots), "gy", split_axis=0, concat_axis=0, tiled=True
        ),
        lax.all_to_all(
            place(solute_tiles, target, slots), "gy", split_axis=0, concat_axis=0, tiled=True
        ),
        lax.all_to_all(
            place(coefficients, target, slots), "gy", split_axis=0, concat_axis=0, tiled=True
        ),
        lax.all_to_all(
            place(first_halos, target, slots), "gy", split_axis=0, concat_axis=0, tiled=True
        ),
        lax.all_to_all(flag_send, "gy", split_axis=0, concat_axis=0, tiled=True),
    )
    picked = pick_slots(arrived[4], tiles_here, slots)
    phase_owned = arrived[0][picked]
    solute_owned = arrived[1][picked]
    coeff_owned = arrived[2][picked]
    halo_owned = arrived[3][picked]
    for iteration in range(NSTEPS):
        if iteration > 0:
            returned = lax.all_to_all(
                place(boundary_faces(phase_owned, solute_owned), picked, slots),
                "gy",
                split_axis=0,
                concat_axis=0,
                tiled=True,
            )
            home_grid = returned[target].reshape(block_x, block_y, 8, edge, depth)
            outgoing = place(home_halos(home_grid, block_x, block_y), target, slots)
            halo_owned = lax.all_to_all(outgoing, "gy", split_axis=0, concat_axis=0, tiled=True)[
                picked
            ]
        phase_owned, solute_owned = advance(phase_owned, solute_owned, halo_owned, coeff_owned)
    return (
        phase_owned.reshape(1, tiles_here, edge, edge, depth),
        solute_owned.reshape(1, tiles_here, edge, edge, depth),
    )


def solution(mesh):
    in_specs = (
        P("gx", "gy", None, None, None),
        P("gx", "gy", None, None, None),
        P("gx", "gy"),
        P("gx", "gy"),
        P("gx", "gy"),
        P("gx", "gy"),
    )
    out_specs = (P(("gx", "gy"), None, None, None, None), P(("gx", "gy"), None, None, None, None))
    return jax.shard_map(
        per_device, mesh=mesh, in_specs=in_specs, out_specs=out_specs, check_vma=False
    )
```

profile of v0, /device:TPU:8, one launch (start us, length us, event | category | flops | bytes accessed | tf_op | source)
XLA Modules:
  0.0 615.9 jit_solution(6775018101167330036)
XLA Ops:
  9.9 6.3 %all-to-all-start.1 = ((s32[8,1,1]{2,1,0:T(1,128)}), s32[8,1,1]{2,1,0:T(1,128)S(1)}, u32[]{:S(2)}, u32[]{:S(2)}) async-start(s32[8,1,1]{2,1,0:T(1,128)} %copy.618), calls=%async_computation.1 | async-start | bytes 8192 | tf_op jit(solution)/shard_map/all_to_all | solution.py:178
  21.3 14.8 %collective-permute-done.2 = f32[3,1,8,32,128]{4,3,1,2,0:T(8,128)S(1)} collective-permute-done((f32[3,1,8,32,128]{4,3,1,2,0:T(8,128)S(1)}, f32[3,1,8,32,128]{4,3,1,2,0:T(8,128)S(1)}, u32[]{:S(2)}, u32[]{:S(2)}) %collective-permute-start.2) | collective-permute-done | bytes 393248 | tf_op jit(solution)/shard_map/ppermute | solution.py:19
  38.0 5.1 all-to-all-start.2
  48.1 5.0 all-to-all-start.3
  53.0 2.6 broadcast.851.clone
  55.6 2.8 scatter_fusion.2
  58.4 17.2 %all-to-all-done.3 = f32[8,8,32,128]{3,2,1,0:T(8,128)S(1)} async-done(((f32[8,8,32,128]{3,2,1,0:T(8,128)}), f32[8,8,32,128]{3,2,1,0:T(8,128)S(1)}, u32[]{:S(2)}, u32[]{:S(2)}) %all-to-all-start.3) | async-done | bytes 1048608 | tf_op jit(solution)/shard_map/all_to_all | solution.py:175
  75.5 7.0 %all-to-all-start.4 = ((f32[8,32,32,128]{3,2,1,0:T(8,128)}), f32[8,32,32,128]{3,2,1,0:T(8,128)}, u32[]{:S(2)}, u32[]{:S(2)}) async-start(f32[8,32,32,128]{3,2,1,0:T(8,128)} %scatter_fusion.2), calls=%async_computation.4 | async-start | bytes 8388608 | tf_op jit(solution)/shard_map/all_to_all | solution.py:169
  82.6 2.6 broadcast.851.clone.1
  85.2 2.8 scatter_fusion
  88.0 84.4 %all-to-all-done.4 = f32[8,32,32,128]{3,2,1,0:T(8,128)} async-done(((f32[8,32,32,128]{3,2,1,0:T(8,128)}), f32[8,32,32,128]{3,2,1,0:T(8,128)}, u32[]{:S(2)}, u32[]{:S(2)}) %all-to-all-start.4) | async-done | bytes 4194336 | tf_op jit(solution)/shard_map/all_to_all | solution.py:169
  172.4 7.0 %all-to-all-start = ((f32[8,32,32,128]{3,2,1,0:T(8,128)}), f32[8,32,32,128]{3,2,1,0:T(8,128)}, u32[]{:S(2)}, u32[]{:S(2)}) async-start(f32[8,32,32,128]{3,2,1,0:T(8,128)} %scatter_fusion), calls=%async_computation | async-start | bytes 8388608 | tf_op jit(solution)/shard_map/all_to_all | solution.py:166
  182.8 2.8 gather_fusion.3
  185.6 2.3 fusion.182
  187.9 2.4 fusion.181
  190.2 2.6 fusion.179
  192.8 2.5 fusion.180
  195.4 74.1 %all-to-all-done = f32[8,32,32,128]{3,2,1,0:T(8,128)} async-done(((f32[8,32,32,128]{3,2,1,0:T(8,128)}), f32[8,32,32,128]{3,2,1,0:T(8,128)}, u32[]{:S(2)}, u32[]{:S(2)}) %all-to-all-start) | async-done | bytes 4194336 | tf_op jit(solution)/shard_map/all_to_all | solution.py:166
  269.5 2.8 gather_fusion
  280.8 3.3 fusion.84
  286.3 2.3 scatter_fusion.3
  288.7 6.7 %all-to-all-start.5 = ((f32[8,8,32,128]{3,2,1,0:T(8,128)}), f32[8,8,32,128]{3,2,1,0:T(8,128)}, u32[]{:S(2)}, u32[]{:S(2)}) async-start(f32[8,8,32,128]{3,2,1,0:T(8,128)} %scatter_fusion.3), calls=%async_computation.5 | async-start | bytes 2097152 | tf_op jit(solution)/shard_map/all_to_all | solution.py:187
  296.0 22.6 %all-to-all-done.5 = f32[8,8,32,128]{3,2,1,0:T(8,128)} async-done(((f32[8,8,32,128]{3,2,1,0:T(8,128)}), f32[8,8,32,128]{3,2,1,0:T(8,128)}, u32[]{:S(2)}, u32[]{:S(2)}) %all-to-all-start.5) | async-done | bytes 1048608 | tf_op jit(solution)/shard_map/all_to_all | solution.py:187
  322.3 6.1 collective-permute-done.4
  329.0 2.9 collective-permute-start.7
  331.9 14.7 %collective-permute-done.6 = f32[3,1,8,32,128]{4,3,2,1,0:T(8,128)S(1)} collective-permute-done((f32[3,1,8,32,128]{4,3,2,1,0:T(8,128)S(1)}, f32[3,1,8,32,128]{4,3,2,1,0:T(8,128)S(1)}, u32[]{:S(2)}, u32[]{:S(2)}) %collective-permute-start.6) | collective-permute-done | bytes 393248 | tf_op jit(solution)/shard_map/ppermute | solution.py:19
  350.6 2.3 scatter_fusion.4
  353.0 7.5 %all-to-all-start.6 = ((f32[8,8,32,128]{3,2,1,0:T(8,128)}), f32[8,8,32,128]{3,2,1,0:T(8,128)}, u32[]{:S(2)}, u32[]{:S(2)}) async-start(f32[8,8,32,128]{3,2,1,0:T(8,128)} %scatter_fusion.4), calls=%async_computation.6 | async-start | bytes 2097152 | tf_op jit(solution)/shard_map/all_to_all | solution.py:196
  360.5 5.1 fusion.165
  365.6 3.6 fusion.166
  369.1 4.1 fusion.168
  373.3 4.1 fusion.167
  377.4 6.7 %all-to-all-done.6 = f32[8,8,32,128]{3,2,1,0:T(8,128)} async-done(((f32[8,8,32,128]{3,2,1,0:T(8,128)}), f32[8,8,32,128]{3,2,1,0:T(8,128)}, u32[]{:S(2)}, u32[]{:S(2)}) %all-to-all-start.6) | async-done | bytes 1048608 | tf_op jit(solution)/shard_map/all_to_all | solution.py:196
  386.6 8.0 %fusion.100 = (f32[2,32,32,128]{3,2,1,0:T(8,128)S(1)}, f32[2,32,32,128]{3,2,1,0:T(8,128)S(1)}) fusion(f32[2,32,32,128]{3,2,1,0:T(8,128)} %copy-done.2, f32[2,1,32,128]{3,2,1,0:T(8,128)S(1)} %get-tuple-element.184, f32[2,31,32,128]{3,2,1,0:T(8,128)} %get-tuple-element.199, f32[2,31,32,128]{3,2,1,0:T(8,128)} %get-tuple-element.202, ...), kind=kLoop, calls=%fused_computation.188 | loop fusion | flops 18087936 | bytes 16777240 | tf_op jit(solution)/shard_map/add | solution.py:60
  396.8 2.3 scatter_fusion.5
  399.1 31.0 %all_to_all.66 = f32[8,8,32,128]{3,2,1,0:T(8,128)} all-to-all(f32[8,8,32,128]{3,2,1,0:T(8,128)} %scatter_fusion.5), channel_id=1, replica_groups=mesh['gx'=4,'gy'=8] {'gy'}, dimensions={0} | all-to-all | bytes 2097152 | tf_op jit(solution)/shard_map/all_to_all | solution.py:187
  433.9 3.7 fusion.162
  440.0 2.7 collective-permute-start.11
  442.8 15.2 %collective-permute-done.10 = f32[3,1,8,32,128]{4,3,2,1,0:T(8,128)S(1)} collective-permute-done((f32[3,1,8,32,128]{4,3,2,1,0:T(8,128)S(1)}, f32[3,1,8,32,128]{4,3,2,1,0:T(8,128)S(1)}, u32[]{:S(2)}, u32[]{:S(2)}) %collective-permute-start.10) | collective-permute-done | bytes 393248 | tf_op jit(solution)/shard_map/ppermute | solution.py:19
  458.0 2.3 collective-permute-done.11
  462.1 2.3 scatter_fusion.6
  464.5 6.2 all-to-all-start.8
  470.6 2.3 fusion.155
  475.1 2.6 fusion.159
  477.7 2.5 fusion.160
  480.2 2.6 fusion.157
  482.8 2.6 fusion.158
  485.4 2.3 fusion.156
  487.7 6.6 %all-to-all-done.8 = f32[8,8,32,128]{3,2,1,0:T(8,128)} async-done(((f32[8,8,32,128]{3,2,1,0:T(8,128)}), f32[8,8,32,128]{3,2,1,0:T(8,128)}, u32[]{:S(2)}, u32[]{:S(2)}) %all-to-all-start.8) | async-done | bytes 1048608 | tf_op jit(solution)/shard_map/all_to_all | solution.py:196
  496.9 7.7 %fusion.116 = (f32[2,32,32,128]{3,2,1,0:T(8,128)S(1)}, f32[2,32,32,128]{3,2,1,0:T(8,128)S(1)}) fusion(f32[2,32,32,128]{3,2,1,0:T(8,128)} %copy-done, f32[2,1,32,128]{3,2,1,0:T(8,128)S(1)} %get-tuple-element.170, f32[2,31,32,128]{3,2,1,0:T(8,128)} %get-tuple-element.70, f32[2,31,32,128]{3,2,1,0:T(8,128)} %get-tuple-element.67, ...), kind=kLoop, calls=%fused_computation.218 | loop fusion | flops 18087936 | bytes 16777240 | tf_op jit(solution)/shard_map/add | solution.py:60
  507.2 2.3 scatter_fusion.7
  509.5 6.5 %all-to-all-start.9 = ((f32[8,8,32,128]{3,2,1,0:T(8,128)}), f32[8,8,32,128]{3,2,1,0:T(8,128)}, u32[]{:S(2)}, u32[]{:S(2)}) async-start(f32[8,8,32,128]{3,2,1,0:T(8,128)} %scatter_fusion.7), calls=%async_computation.9 | async-start | bytes 2097152 | tf_op jit(solution)/shard_map/all_to_all | solution.py:187
  516.3 7.3 %fusion.92 = (f32[1,2,32,32,128]{4,3,2,1,0:T(8,128)S(1)}, f32[1,2,32,32,128]{4,3,2,1,0:T(8,128)S(1)}) fusion(f32[1,2,1,32,128]{4,3,2,1,0:T(8,128)} %get-tuple-element.190, f32[1,2,31,32,128]{4,3,2,1,0:T(8,128)} %get-tuple-element.140, f32[1,2,31,32,128]{4,3,2,1,0:T(8,128)} %get-tuple-element.141, f32[1,2,1,32,128]{4,3,2,1,0:T(8,128)} %get-tuple-element.191, ...), kind=kLoop, calls=%fused_computation.173 | loop fusion | flops 18087936 | bytes 16777240 | tf_op jit(solution)/shard_map/add | solution.py:60
  526.4 3.4 fusion.108
  534.8 4.4 all-to-all-done.9
  544.6 4.0 collective-permute-done.12
  549.1 2.9 collective-permute-start.15
  552.0 14.9 %collective-permute-done.14 = f32[3,1,8,32,128]{4,3,2,1,0:T(8,128)S(1)} collective-permute-done((f32[3,1,8,32,128]{4,3,2,1,0:T(8,128)S(1)}, f32[3,1,8,32,128]{4,3,2,1,0:T(8,128)S(1)}, u32[]{:S(2)}, u32[]{:S(2)}) %collective-permute-start.14) | collective-permute-done | bytes 393248 | tf_op jit(solution)/shard_map/ppermute | solution.py:19
  566.9 2.4 collective-permute-done.15
  571.2 2.3 scatter_fusion.8
  573.6 7.7 %all-to-all-start.10 = ((f32[8,8,32,128]{3,2,1,0:T(8,128)}), f32[8,8,32,128]{3,2,1,0:T(8,128)}, u32[]{:S(2)}, u32[]{:S(2)}) async-start(f32[8,8,32,128]{3,2,1,0:T(8,128)} %scatter_fusion.8), calls=%async_computation.10 | async-start | bytes 2097152 | tf_op jit(solution)/shard_map/all_to_all | solution.py:196
  590.1 4.5 fusion.124
  594.7 10.4 %all-to-all-done.10 = f32[8,8,32,128]{3,2,1,0:T(8,128)} async-done(((f32[8,8,32,128]{3,2,1,0:T(8,128)}), f32[8,8,32,128]{3,2,1,0:T(8,128)}, u32[]{:S(2)}, u32[]{:S(2)}) %all-to-all-start.10) | async-done | bytes 1048608 | tf_op jit(solution)/shard_map/all_to_all | solution.py:196
  607.0 8.7 %fusion.132 = (f32[1,2,32,32,128]{4,3,2,1,0:T(8,128)}, f32[1,2,32,32,128]{4,3,2,1,0:T(8,128)}) fusion(f32[1,2,32,32,128]{4,3,2,1,0:T(8,128)S(1)} %get-tuple-element.9, f32[1,2,1,32,128]{4,3,2,1,0:T(8,128)S(1)} %get-tuple-element.158, f32[1,2,31,32,128]{4,3,2,1,0:T(8,128)} %get-tuple-element.34, f32[1,2,31,32,128]{4,3,2,1,0:T(8,128)} %get-tuple-element.33, ...), kind=kLoop, calls=%fused_computation.242 | loop fusion | flops 18087936 | bytes 16777240 | tf_op jit(solution)/shard_map/add | solution.py:60
  (322 shorter events, 90.0 us)
Async XLA Ops:
  5.2 12.9 %collective-permute-start = (f32[1,2,8,32,128]{4,3,1,2,0:T(8,128)S(1)}, f32[1,2,8,32,128]{4,3,1,2,0:T(8,128)S(1)}, u32[]{:S(2)}, u32[]{:S(2)}) collective-permute-start(f32[1,2,8,32,128]{4,3,1,2,0:T(8,128)S(1)} %bitcast.487), channel_id=1, source_target_pairs={{0,8},{8,16},{16,24},{24,0},{1,9},{9,17},{17,25},{25,1},{2,10},{10... | collective-permute-start | bytes 786440 | tf_op jit(solution)/shard_map/ppermute | solution.py:19
  5.3 12.9 %collective-permute-start.1 = (f32[1,2,8,32,128]{4,3,1,2,0:T(8,128)S(1)}, f32[1,2,8,32,128]{4,3,1,2,0:T(8,128)S(1)}, u32[]{:S(2)}, u32[]{:S(2)}) collective-permute-start(f32[1,2,8,32,128]{4,3,1,2,0:T(8,128)S(1)} %bitcast.488), channel_id=1, source_target_pairs={{8,0},{16,8},{24,16},{0,24},{9,1},{17,9},{25,17},{1,25},{10,2},{18... | collective-permute-start | bytes 786440 | tf_op jit(solution)/shard_map/ppermute | solution.py:22
  9.9 28.1 %all-to-all-start.1 = ((s32[8,1,1]{2,1,0:T(1,128)}), s32[8,1,1]{2,1,0:T(1,128)S(1)}, u32[]{:S(2)}, u32[]{:S(2)}) async-start(s32[8,1,1]{2,1,0:T(1,128)} %copy.618), calls=%async_computation.1 | async-start | bytes 8192 | tf_op jit(solution)/shard_map/all_to_all | solution.py:178
  18.3 17.8 %collective-permute-start.2 = (f32[3,1,8,32,128]{4,3,1,2,0:T(8,128)S(1)}, f32[3,1,8,32,128]{4,3,1,2,0:T(8,128)S(1)}, u32[]{:S(2)}, u32[]{:S(2)}) collective-permute-start(f32[3,1,8,32,128]{4,3,1,2,0:T(8,128)S(1)} %get-tuple-element.154), channel_id=1, source_target_pairs={{0,1},{1,2},{2,3},{3,4},{4,5},{5,6},{6,7},{7,0},{8,9},{9,10},{10,1... | collective-permute-start | bytes 1179656 | tf_op jit(solution)/shard_map/ppermute | solution.py:19
  19.8 18.2 %collective-permute-start.3 = (f32[3,1,8,32,128]{4,3,1,2,0:T(8,128)S(1)}, f32[3,1,8,32,128]{4,3,1,2,0:T(8,128)S(1)}, u32[]{:S(2)}, u32[]{:S(2)}) collective-permute-start(f32[3,1,8,32,128]{4,3,1,2,0:T(8,128)S(1)} %get-tuple-element.153), channel_id=1, source_target_pairs={{1,0},{2,1},{3,2},{4,3},{5,4},{6,5},{7,6},{0,7},{9,8},{10,9},{11,1... | collective-permute-start | bytes 1179656 | tf_op jit(solution)/shard_map/ppermute | solution.py:22
  38.0 10.0 %all-to-all-start.2 = ((f32[8,1,3]{2,1,0:T(1,128)}), f32[8,1,3]{2,1,0:T(1,128)S(1)}, u32[]{:S(2)}, u32[]{:S(2)}) async-start(f32[8,1,3]{2,1,0:T(1,128)} %bitcast.174), calls=%async_computation.2 | async-start | bytes 8192 | tf_op jit(solution)/shard_map/all_to_all | solution.py:172
  43.2 12.4 %copy-start.51 = (f32[1,2,32,32,128]{4,3,2,1,0:T(8,128)S(1)}, f32[1,2,32,32,128]{4,3,2,1,0:T(8,128)}, u32[]{:S(2)}) copy-start(f32[1,2,32,32,128]{4,3,2,1,0:T(8,128)} %param.7) | copy-start | bytes 3145732
  48.1 27.5 %all-to-all-start.3 = ((f32[8,8,32,128]{3,2,1,0:T(8,128)}), f32[8,8,32,128]{3,2,1,0:T(8,128)S(1)}, u32[]{:S(2)}, u32[]{:S(2)}) async-start(f32[8,8,32,128]{3,2,1,0:T(8,128)} %scatter_fusion.1), calls=%async_computation.3 | async-start | bytes 2097152 | tf_op jit(solution)/shard_map/all_to_all | solution.py:175
  75.5 96.8 %all-to-all-start.4 = ((f32[8,32,32,128]{3,2,1,0:T(8,128)}), f32[8,32,32,128]{3,2,1,0:T(8,128)}, u32[]{:S(2)}, u32[]{:S(2)}) async-start(f32[8,32,32,128]{3,2,1,0:T(8,128)} %scatter_fusion.2), calls=%async_computation.4 | async-start | bytes 8388608 | tf_op jit(solution)/shard_map/all_to_all | solution.py:169
  172.4 97.1 %all-to-all-start = ((f32[8,32,32,128]{3,2,1,0:T(8,128)}), f32[8,32,32,128]{3,2,1,0:T(8,128)}, u32[]{:S(2)}, u32[]{:S(2)}) async-start(f32[8,32,32,128]{3,2,1,0:T(8,128)} %scatter_fusion), calls=%async_computation | async-start | bytes 8388608 | tf_op jit(solution)/shard_map/all_to_all | solution.py:166
  180.8 88.7 %copy-start.79 = (s32[1024]{0:T(1024)}, s32[1024]{0:T(1024)S(1)}, u32[]{:S(2)}) copy-start(s32[1024]{0:T(1024)S(1)} %pad_clamp_fusion.1) | copy-start | bytes 12292
  284.1 89.2 %copy-start.2 = (f32[2,32,32,128]{3,2,1,0:T(8,128)}, f32[2,32,32,128]{3,2,1,0:T(8,128)S(1)}, u32[]{:S(2)}) copy-start(f32[2,32,32,128]{3,2,1,0:T(8,128)S(1)} %get-tuple-element.15) | copy-start | bytes 3145732
  288.7 29.9 %all-to-all-start.5 = ((f32[8,8,32,128]{3,2,1,0:T(8,128)}), f32[8,8,32,128]{3,2,1,0:T(8,128)}, u32[]{:S(2)}, u32[]{:S(2)}) async-start(f32[8,8,32,128]{3,2,1,0:T(8,128)} %scatter_fusion.3), calls=%async_computation.5 | async-start | bytes 2097152 | tf_op jit(solution)/shard_map/all_to_all | solution.py:187
  320.5 7.9 %collective-permute-start.4 = (f32[1,2,8,32,128]{4,3,2,1,0:T(8,128)S(1)}, f32[1,2,8,32,128]{4,3,2,1,0:T(8,128)S(1)}, u32[]{:S(2)}, u32[]{:S(2)}) collective-permute-start(f32[1,2,8,32,128]{4,3,2,1,0:T(8,128)S(1)} %bitcast.480), channel_id=1, source_target_pairs={{0,8},{8,16},{16,24},{24,0},{1,9},{9,17},{17,25},{25,1},{2,10},{10... | collective-permute-start | bytes 786440 | tf_op jit(solution)/shard_map/ppermute | solution.py:19
  320.6 7.8 %collective-permute-start.5 = (f32[1,2,8,32,128]{4,3,2,1,0:T(8,128)S(1)}, f32[1,2,8,32,128]{4,3,2,1,0:T(8,128)S(1)}, u32[]{:S(2)}, u32[]{:S(2)}) collective-permute-start(f32[1,2,8,32,128]{4,3,2,1,0:T(8,128)S(1)} %bitcast.481), channel_id=1, source_target_pairs={{8,0},{16,8},{24,16},{0,24},{9,1},{17,9},{25,17},{1,25},{10,2},{18... | collective-permute-start | bytes 786440 | tf_op jit(solution)/shard_map/ppermute | solution.py:22
  328.5 18.0 %collective-permute-start.6 = (f32[3,1,8,32,128]{4,3,2,1,0:T(8,128)S(1)}, f32[3,1,8,32,128]{4,3,2,1,0:T(8,128)S(1)}, u32[]{:S(2)}, u32[]{:S(2)}) collective-permute-start(f32[3,1,8,32,128]{4,3,2,1,0:T(8,128)S(1)} %get-tuple-element.152), channel_id=1, source_target_pairs={{0,1},{1,2},{2,3},{3,4},{4,5},{5,6},{6,7},{7,0},{8,9},{9,10},{10,1... | collective-permute-start | bytes 1179656 | tf_op jit(solution)/shard_map/ppermute | solution.py:19
  329.0 19.8 %collective-permute-start.7 = (f32[3,1,8,32,128]{4,3,2,1,0:T(8,128)S(1)}, f32[3,1,8,32,128]{4,3,2,1,0:T(8,128)S(1)}, u32[]{:S(2)}, u32[]{:S(2)}) collective-permute-start(f32[3,1,8,32,128]{4,3,2,1,0:T(8,128)S(1)} %get-tuple-element.151), channel_id=1, source_target_pairs={{1,0},{2,1},{3,2},{4,3},{5,4},{6,5},{7,6},{0,7},{9,8},{10,9},{11,1... | collective-permute-start | bytes 1179656 | tf_op jit(solution)/shard_map/ppermute | solution.py:22
  353.0 31.0 %all-to-all-start.6 = ((f32[8,8,32,128]{3,2,1,0:T(8,128)}), f32[8,8,32,128]{3,2,1,0:T(8,128)}, u32[]{:S(2)}, u32[]{:S(2)}) async-start(f32[8,8,32,128]{3,2,1,0:T(8,128)} %scatter_fusion.4), calls=%async_computation.6 | async-start | bytes 2097152 | tf_op jit(solution)/shard_map/all_to_all | solution.py:196
  386.6 8.0 %copy-start.55 = (f32[2,1,32,128]{3,2,1,0:T(8,128)}, f32[2,1,32,128]{3,2,1,0:T(8,128)S(1)}, u32[]{:S(2)}) copy-start(f32[2,1,32,128]{3,2,1,0:T(8,128)S(1)} %get-tuple-element.180) | copy-start | bytes 98308
  386.6 8.0 %copy-start.57 = (f32[2,1,32,128]{3,2,1,0:T(8,128)}, f32[2,1,32,128]{3,2,1,0:T(8,128)S(1)}, u32[]{:S(2)}) copy-start(f32[2,1,32,128]{3,2,1,0:T(8,128)S(1)} %get-tuple-element.181) | copy-start | bytes 98308
  386.6 8.0 %copy-start.59 = (f32[2,1,32,128]{3,2,1,0:T(8,128)}, f32[2,1,32,128]{3,2,1,0:T(8,128)S(1)}, u32[]{:S(2)}) copy-start(f32[2,1,32,128]{3,2,1,0:T(8,128)S(1)} %get-tuple-element.182) | copy-start | bytes 98308
  386.6 8.0 %copy-start.61 = (f32[2,1,32,128]{3,2,1,0:T(8,128)}, f32[2,1,32,128]{3,2,1,0:T(8,128)S(1)}, u32[]{:S(2)}) copy-start(f32[2,1,32,128]{3,2,1,0:T(8,128)S(1)} %get-tuple-element.185) | copy-start | bytes 98308
  432.1 7.6 %collective-permute-start.8 = (f32[1,2,8,32,128]{4,3,2,1,0:T(8,128)S(1)}, f32[1,2,8,32,128]{4,3,2,1,0:T(8,128)S(1)}, u32[]{:S(2)}, u32[]{:S(2)}) collective-permute-start(f32[1,2,8,32,128]{4,3,2,1,0:T(8,128)S(1)} %bitcast.466), channel_id=1, source_target_pairs={{0,8},{8,16},{16,24},{24,0},{1,9},{9,17},{17,25},{25,1},{2,10},{10... | collective-permute-start | bytes 786440 | tf_op jit(solution)/shard_map/ppermute | solution.py:19
  432.1 7.5 %collective-permute-start.9 = (f32[1,2,8,32,128]{4,3,2,1,0:T(8,128)S(1)}, f32[1,2,8,32,128]{4,3,2,1,0:T(8,128)S(1)}, u32[]{:S(2)}, u32[]{:S(2)}) collective-permute-start(f32[1,2,8,32,128]{4,3,2,1,0:T(8,128)S(1)} %bitcast.467), channel_id=1, source_target_pairs={{8,0},{16,8},{24,16},{0,24},{9,1},{17,9},{25,17},{1,25},{10,2},{18... | collective-permute-start | bytes 786440 | tf_op jit(solution)/shard_map/ppermute | solution.py:22
  439.8 18.2 %collective-permute-start.10 = (f32[3,1,8,32,128]{4,3,2,1,0:T(8,128)S(1)}, f32[3,1,8,32,128]{4,3,2,1,0:T(8,128)S(1)}, u32[]{:S(2)}, u32[]{:S(2)}) collective-permute-start(f32[3,1,8,32,128]{4,3,2,1,0:T(8,128)S(1)} %get-tuple-element.150), channel_id=1, source_target_pairs={{0,1},{1,2},{2,3},{3,4},{4,5},{5,6},{6,7},{7,0},{8,9},{9,10},{10,1... | collective-permute-start | bytes 1179656 | tf_op jit(solution)/shard_map/ppermute | solution.py:19
  440.0 20.2 %collective-permute-start.11 = (f32[3,1,8,32,128]{4,3,2,1,0:T(8,128)S(1)}, f32[3,1,8,32,128]{4,3,2,1,0:T(8,128)S(1)}, u32[]{:S(2)}, u32[]{:S(2)}) collective-permute-start(f32[3,1,8,32,128]{4,3,2,1,0:T(8,128)S(1)} %get-tuple-element.149), channel_id=1, source_target_pairs={{1,0},{2,1},{3,2},{4,3},{5,4},{6,5},{7,6},{0,7},{9,8},{10,9},{11,1... | collective-permute-start | bytes 1179656 | tf_op jit(solution)/shard_map/ppermute | solution.py:22
  464.5 29.9 %all-to-all-start.8 = ((f32[8,8,32,128]{3,2,1,0:T(8,128)}), f32[8,8,32,128]{3,2,1,0:T(8,128)}, u32[]{:S(2)}, u32[]{:S(2)}) async-start(f32[8,8,32,128]{3,2,1,0:T(8,128)} %scatter_fusion.6), calls=%async_computation.8 | async-start | bytes 2097152 | tf_op jit(solution)/shard_map/all_to_all | solution.py:196
  496.9 7.7 %copy-start.63 = (f32[2,1,32,128]{3,2,1,0:T(8,128)}, f32[2,1,32,128]{3,2,1,0:T(8,128)S(1)}, u32[]{:S(2)}) copy-start(f32[2,1,32,128]{3,2,1,0:T(8,128)S(1)} %get-tuple-element.168) | copy-start | bytes 98308
  496.9 7.7 %copy-start.65 = (f32[2,1,32,128]{3,2,1,0:T(8,128)}, f32[2,1,32,128]{3,2,1,0:T(8,128)S(1)}, u32[]{:S(2)}) copy-start(f32[2,1,32,128]{3,2,1,0:T(8,128)S(1)} %get-tuple-element.171) | copy-start | bytes 98308
  496.9 7.7 %copy-start.67 = (f32[2,1,32,128]{3,2,1,0:T(8,128)}, f32[2,1,32,128]{3,2,1,0:T(8,128)S(1)}, u32[]{:S(2)}) copy-start(f32[2,1,32,128]{3,2,1,0:T(8,128)S(1)} %get-tuple-element.172) | copy-start | bytes 98308
  496.9 7.7 %copy-start.69 = (f32[2,1,32,128]{3,2,1,0:T(8,128)}, f32[2,1,32,128]{3,2,1,0:T(8,128)S(1)}, u32[]{:S(2)}) copy-start(f32[2,1,32,128]{3,2,1,0:T(8,128)S(1)} %get-tuple-element.174) | copy-start | bytes 98308
  504.7 11.4 %copy-start.22 = (f32[1,2,32,31,128]{4,3,2,1,0:T(8,128)S(1)}, f32[1,2,32,31,128]{4,3,2,1,0:T(8,128)}, u32[]{:S(2)}) copy-start(f32[1,2,32,31,128]{4,3,2,1,0:T(8,128)} %get-tuple-element.137) | copy-start | bytes 3047428
  509.5 29.7 %all-to-all-start.9 = ((f32[8,8,32,128]{3,2,1,0:T(8,128)}), f32[8,8,32,128]{3,2,1,0:T(8,128)}, u32[]{:S(2)}, u32[]{:S(2)}) async-start(f32[8,8,32,128]{3,2,1,0:T(8,128)} %scatter_fusion.7), calls=%async_computation.9 | async-start | bytes 2097152 | tf_op jit(solution)/shard_map/all_to_all | solution.py:187
  516.1 7.6 %copy-start.15 = (f32[1,2,32,32,1]{4,3,2,1,0:T(8,128)S(1)}, f32[1,2,32,32,1]{4,3,2,1,0:T(8,128)}, u32[]{:S(2)}) copy-start(f32[1,2,32,32,1]{4,3,2,1,0:T(8,128)} %get-tuple-element.212) | copy-start | bytes 24580
  516.1 7.9 %copy-start.16 = (f32[1,2,32,32,1]{4,3,2,1,0:T(8,128)S(1)}, f32[1,2,32,32,1]{4,3,2,1,0:T(8,128)}, u32[]{:S(2)}) copy-start(f32[1,2,32,32,1]{4,3,2,1,0:T(8,128)} %get-tuple-element.213) | copy-start | bytes 24580
  516.1 8.2 %copy-start.17 = (f32[1,2,32,32,127]{4,3,2,1,0:T(8,128)S(1)}, f32[1,2,32,32,127]{4,3,2,1,0:T(8,128)}, u32[]{:S(2)}) copy-start(f32[1,2,32,32,127]{4,3,2,1,0:T(8,128)} %get-tuple-element.84) | copy-start | bytes 3121156
  516.1 8.5 %copy-start.18 = (f32[1,2,32,32,127]{4,3,2,1,0:T(8,128)S(1)}, f32[1,2,32,32,127]{4,3,2,1,0:T(8,128)}, u32[]{:S(2)}) copy-start(f32[1,2,32,32,127]{4,3,2,1,0:T(8,128)} %get-tuple-element.85) | copy-start | bytes 3121156
  516.1 8.8 %copy-start.19 = (f32[1,2,32,32,127]{4,3,2,1,0:T(8,128)S(1)}, f32[1,2,32,32,127]{4,3,2,1,0:T(8,128)}, u32[]{:S(2)}) copy-start(f32[1,2,32,32,127]{4,3,2,1,0:T(8,128)} %get-tuple-element.208) | copy-start | bytes 3121156
  516.1 9.1 %copy-start.20 = (f32[1,2,32,32,127]{4,3,2,1,0:T(8,128)S(1)}, f32[1,2,32,32,127]{4,3,2,1,0:T(8,128)}, u32[]{:S(2)}) copy-start(f32[1,2,32,32,127]{4,3,2,1,0:T(8,128)} %get-tuple-element.209) | copy-start | bytes 3121156
  516.1 9.3 %copy-start.43 = (f32[1,2,31,32,128]{4,3,2,1,0:T(8,128)S(1)}, f32[1,2,31,32,128]{4,3,2,1,0:T(8,128)}, u32[]{:S(2)}) copy-start(f32[1,2,31,32,128]{4,3,2,1,0:T(8,128)} %get-tuple-element.76) | copy-start | bytes 3047428
  516.2 9.6 %copy-start.44 = (f32[1,2,31,32,128]{4,3,2,1,0:T(8,128)S(1)}, f32[1,2,31,32,128]{4,3,2,1,0:T(8,128)}, u32[]{:S(2)}) copy-start(f32[1,2,31,32,128]{4,3,2,1,0:T(8,128)} %get-tuple-element.77) | copy-start | bytes 3047428
  516.2 9.9 %copy-start.45 = (f32[1,2,31,32,128]{4,3,2,1,0:T(8,128)S(1)}, f32[1,2,31,32,128]{4,3,2,1,0:T(8,128)}, u32[]{:S(2)}) copy-start(f32[1,2,31,32,128]{4,3,2,1,0:T(8,128)} %get-tuple-element.200) | copy-start | bytes 3047428
  516.2 10.2 %copy-start.46 = (f32[1,2,31,32,128]{4,3,2,1,0:T(8,128)S(1)}, f32[1,2,31,32,128]{4,3,2,1,0:T(8,128)}, u32[]{:S(2)}) copy-start(f32[1,2,31,32,128]{4,3,2,1,0:T(8,128)} %get-tuple-element.201) | copy-start | bytes 3047428
  516.2 10.2 %copy-start.56 = (f32[2,1,32,128]{3,2,1,0:T(8,128)S(1)}, f32[2,1,32,128]{3,2,1,0:T(8,128)}, u32[]{:S(2)}) copy-start(f32[2,1,32,128]{3,2,1,0:T(8,128)} %copy-done.55) | copy-start | bytes 98308
  516.2 10.2 %copy-start.58 = (f32[2,1,32,128]{3,2,1,0:T(8,128)S(1)}, f32[2,1,32,128]{3,2,1,0:T(8,128)}, u32[]{:S(2)}) copy-start(f32[2,1,32,128]{3,2,1,0:T(8,128)} %copy-done.57) | copy-start | bytes 98308
  516.2 10.2 %copy-start.60 = (f32[2,1,32,128]{3,2,1,0:T(8,128)S(1)}, f32[2,1,32,128]{3,2,1,0:T(8,128)}, u32[]{:S(2)}) copy-start(f32[2,1,32,128]{3,2,1,0:T(8,128)} %copy-done.59) | copy-start | bytes 98308
  516.2 10.2 %copy-start.62 = (f32[2,1,32,128]{3,2,1,0:T(8,128)S(1)}, f32[2,1,32,128]{3,2,1,0:T(8,128)}, u32[]{:S(2)}) copy-start(f32[2,1,32,128]{3,2,1,0:T(8,128)} %copy-done.61) | copy-start | bytes 98308
  516.2 10.2 %copy-start.71 = (f32[1,2,1,32,128]{4,3,2,1,0:T(8,128)S(1)}, f32[1,2,1,32,128]{4,3,2,1,0:T(8,128)}, u32[]{:S(2)}) copy-start(f32[1,2,1,32,128]{4,3,2,1,0:T(8,128)} %get-tuple-element.176) | copy-start | bytes 98308
  516.2 10.2 %copy-start.72 = (f32[1,2,1,32,128]{4,3,2,1,0:T(8,128)S(1)}, f32[1,2,1,32,128]{4,3,2,1,0:T(8,128)}, u32[]{:S(2)}) copy-start(f32[1,2,1,32,128]{4,3,2,1,0:T(8,128)} %get-tuple-element.177) | copy-start | bytes 98308
  516.2 10.2 %copy-start.73 = (f32[1,2,1,32,128]{4,3,2,1,0:T(8,128)S(1)}, f32[1,2,1,32,128]{4,3,2,1,0:T(8,128)}, u32[]{:S(2)}) copy-start(f32[1,2,1,32,128]{4,3,2,1,0:T(8,128)} %get-tuple-element.178) | copy-start | bytes 98308
  516.3 10.2 %copy-start.74 = (f32[1,2,1,32,128]{4,3,2,1,0:T(8,128)S(1)}, f32[1,2,1,32,128]{4,3,2,1,0:T(8,128)}, u32[]{:S(2)}) copy-start(f32[1,2,1,32,128]{4,3,2,1,0:T(8,128)} %get-tuple-element.179) | copy-start | bytes 98308
  541.1 7.4 %collective-permute-start.12 = (f32[1,2,8,32,128]{4,3,2,1,0:T(8,128)S(1)}, f32[1,2,8,32,128]{4,3,2,1,0:T(8,128)S(1)}, u32[]{:S(2)}, u32[]{:S(2)}) collective-permute-start(f32[1,2,8,32,128]{4,3,2,1,0:T(8,128)S(1)} %bitcast.473), channel_id=1, source_target_pairs={{0,8},{8,16},{16,24},{24,0},{1,9},{9,17},{17,25},{25,1},{2,10},{10... | collective-permute-start | bytes 786440 | tf_op jit(solution)/shard_map/ppermute | solution.py:19
  541.2 7.3 %collective-permute-start.13 = (f32[1,2,8,32,128]{4,3,2,1,0:T(8,128)S(1)}, f32[1,2,8,32,128]{4,3,2,1,0:T(8,128)S(1)}, u32[]{:S(2)}, u32[]{:S(2)}) collective-permute-start(f32[1,2,8,32,128]{4,3,2,1,0:T(8,128)S(1)} %bitcast.474), channel_id=1, source_target_pairs={{8,0},{16,8},{24,16},{0,24},{9,1},{17,9},{25,17},{1,25},{10,2},{18... | collective-permute-start | bytes 786440 | tf_op jit(solution)/shard_map/ppermute | solution.py:22
  548.7 18.3 %collective-permute-start.14 = (f32[3,1,8,32,128]{4,3,2,1,0:T(8,128)S(1)}, f32[3,1,8,32,128]{4,3,2,1,0:T(8,128)S(1)}, u32[]{:S(2)}, u32[]{:S(2)}) collective-permute-start(f32[3,1,8,32,128]{4,3,2,1,0:T(8,128)S(1)} %get-tuple-element.148), channel_id=1, source_target_pairs={{0,1},{1,2},{2,3},{3,4},{4,5},{5,6},{6,7},{7,0},{8,9},{9,10},{10,1... | collective-permute-start | bytes 1179656 | tf_op jit(solution)/shard_map/ppermute | solution.py:19
  549.1 20.3 %collective-permute-start.15 = (f32[3,1,8,32,128]{4,3,2,1,0:T(8,128)S(1)}, f32[3,1,8,32,128]{4,3,2,1,0:T(8,128)S(1)}, u32[]{:S(2)}, u32[]{:S(2)}) collective-permute-start(f32[3,1,8,32,128]{4,3,2,1,0:T(8,128)S(1)} %get-tuple-element.147), channel_id=1, source_target_pairs={{1,0},{2,1},{3,2},{4,3},{5,4},{6,5},{7,6},{0,7},{9,8},{10,9},{11,1... | collective-permute-start | bytes 1179656 | tf_op jit(solution)/shard_map/ppermute | solution.py:22
  552.0 29.3 %copy-start.8 = (f32[2,32,32,128]{3,2,1,0:T(8,128)S(1)}, f32[2,32,32,128]{3,2,1,0:T(8,128)}, u32[]{:S(2)}) copy-start(f32[2,32,32,128]{3,2,1,0:T(8,128)} %copy-done.7) | copy-start | bytes 3145732
  573.5 14.2 %copy-start.66 = (f32[2,1,32,128]{3,2,1,0:T(8,128)S(1)}, f32[2,1,32,128]{3,2,1,0:T(8,128)}, u32[]{:S(2)}) copy-start(f32[2,1,32,128]{3,2,1,0:T(8,128)} %copy-done.65) | copy-start | bytes 98308
  573.6 14.2 %copy-start.68 = (f32[2,1,32,128]{3,2,1,0:T(8,128)S(1)}, f32[2,1,32,128]{3,2,1,0:T(8,128)}, u32[]{:S(2)}) copy-start(f32[2,1,32,128]{3,2,1,0:T(8,128)} %copy-done.67) | copy-start | bytes 98308
  573.6 14.2 %copy-start.70 = (f32[2,1,32,128]{3,2,1,0:T(8,128)S(1)}, f32[2,1,32,128]{3,2,1,0:T(8,128)}, u32[]{:S(2)}) copy-start(f32[2,1,32,128]{3,2,1,0:T(8,128)} %copy-done.69) | copy-start | bytes 98308
  573.6 14.2 %copy-start.75 = (f32[1,2,1,32,128]{4,3,2,1,0:T(8,128)S(1)}, f32[1,2,1,32,128]{4,3,2,1,0:T(8,128)}, u32[]{:S(2)}) copy-start(f32[1,2,1,32,128]{4,3,2,1,0:T(8,128)} %get-tuple-element.164) | copy-start | bytes 98308
  573.6 14.2 %copy-start.76 = (f32[1,2,1,32,128]{4,3,2,1,0:T(8,128)S(1)}, f32[1,2,1,32,128]{4,3,2,1,0:T(8,128)}, u32[]{:S(2)}) copy-start(f32[1,2,1,32,128]{4,3,2,1,0:T(8,128)} %get-tuple-element.165) | copy-start | bytes 98308
  573.6 14.2 %copy-start.77 = (f32[1,2,1,32,128]{4,3,2,1,0:T(8,128)S(1)}, f32[1,2,1,32,128]{4,3,2,1,0:T(8,128)}, u32[]{:S(2)}) copy-start(f32[1,2,1,32,128]{4,3,2,1,0:T(8,128)} %get-tuple-element.166) | copy-start | bytes 98308
  573.6 14.2 %copy-start.78 = (f32[1,2,1,32,128]{4,3,2,1,0:T(8,128)S(1)}, f32[1,2,1,32,128]{4,3,2,1,0:T(8,128)}, u32[]{:S(2)}) copy-start(f32[1,2,1,32,128]{4,3,2,1,0:T(8,128)} %get-tuple-element.167) | copy-start | bytes 98308
  573.6 31.5 %all-to-all-start.10 = ((f32[8,8,32,128]{3,2,1,0:T(8,128)}), f32[8,8,32,128]{3,2,1,0:T(8,128)}, u32[]{:S(2)}, u32[]{:S(2)}) async-start(f32[8,8,32,128]{3,2,1,0:T(8,128)} %scatter_fusion.8), calls=%async_computation.10 | async-start | bytes 2097152 | tf_op jit(solution)/shard_map/all_to_all | solution.py:196
  (43 other events, 176.1 us)
where the time goes:
time: 621 us; the launch traced here: 616 us
  waiting for transfers between devices  309 us (50%)
  local copies, waits for them, and re-layouts  143 us (23%)
  starting transfers between devices  84.7 us (14%)
  other arithmetic  46.9 us (8%)
  blocking collectives  31 us (5%)
    all_to_all x1, waiting for transfers between devices, per_device(): lax.all_to_all(place(solute_tiles, target, slots), 'gy', split_axis=0, co...  84.4 us
    all_to_all x1, waiting for transfers between devices, per_device(): lax.all_to_all(place(phase_tiles, target, slots), 'gy', split_axis=0, con...  74.1 us
    ppermute x8, waiting for transfers between devices, extended(): lax.ppermute(lax.slice_in_dim(block, block.shape[dim] - width, None, axis...  71.7 us
    add x7, other arithmetic, step_cells(): new_solute = solute + spread * lap_solute + 0.5 * (new_phase - phase)  42.8 us
    all_to_all x1, blocking collectives, per_device(): lax.all_to_all(place(boundary_faces(phase_owned, solute_owned), picked, s...  31 us
    all_to_all x2, waiting for transfers between devices, per_device(): lax.all_to_all(place(boundary_faces(phase_owned, solute_owned), picked, s...  27 us
    all_to_all x3, waiting for transfers between devices, per_device(): lax.all_to_all(outgoing, 'gy', split_axis=0, concat_axis=0, tiled=True)  23.7 us
    scatter x10, local copies, waits for them, and re-layouts, place(): jnp.zeros((slots,) + values.shape[1:], values.dtype).at[target].set(values)  23 us
  transfers between devices with their start and end apart: 26, of which 20 were waited for; matrix products, arithmetic and copies ran while one was open for 16% of the time, Pallas kernels for 0%

commit v1 on v0

v1 whole, which is shorter than its diff:
```python
import functools

import jax
import jax.numpy as jnp
from jax import lax
from jax.experimental import pallas as pl
from jax.experimental.pallas import tpu as pltpu
from jax.sharding import PartitionSpec as P

NSTEPS = 4
W = NSTEPS
PAD = 8

aniso_strength = 0.05


def pack_y_kernel(coef_ref, phase_lo, phase_hi, solute_lo, solute_hi, to_prev, to_next):
    edge = phase_lo.shape[2]
    to_prev[:edge, :W, :] = phase_lo[0, 0, :, :W, :]
    to_prev[:edge, W:, :] = solute_lo[0, 0, :, :W, :]
    to_next[:edge, :W, :] = phase_hi[0, 0, :, W:, :]
    to_next[:edge, W:, :] = solute_hi[0, 0, :, W:, :]
    to_prev[edge] = jnp.zeros((2 * W, to_prev.shape[2]), jnp.float32)
    to_next[edge] = jnp.zeros((2 * W, to_prev.shape[2]), jnp.float32)
    for kind in range(3):
        to_prev[edge, kind, :] = jnp.full((to_prev.shape[2],), coef_ref[0, kind], jnp.float32)
        to_next[edge, kind, :] = jnp.full((to_prev.shape[2],), coef_ref[1, kind], jnp.float32)


def pack_y(phase, solute, coef):
    _, tiles, edge, _, depth = phase.shape
    low = pl.BlockSpec((1, 1, edge, 2 * W, depth), lambda i: (0, 0, 0, 0, 0))
    high = pl.BlockSpec((1, 1, edge, 2 * W, depth), lambda i: (0, tiles - 1, 0, edge // (2 * W) - 1, 0))
    out = jax.ShapeDtypeStruct((edge + 1, 2 * W, depth), jnp.float32)
    whole = pl.BlockSpec((edge + 1, 2 * W, depth), lambda i: (0, 0, 0))
    return pl.pallas_call(
        pack_y_kernel,
        grid=(1,),
        in_specs=[pl.BlockSpec(memory_space=pltpu.SMEM), low, high, low, high],
        out_specs=[whole, whole],
        out_shape=[out, out],
        name="pack_y",
    )(coef, phase, phase, solute, solute)


def fill_row(dst, row, phase_row, solute_row, lo, hi):
    start = PAD
    dst[0][row, start : start + W, :] = lo[:W]
    dst[1][row, start : start + W, :] = lo[W:]
    start += W
    for values in phase_row:
        size = values.shape[0]
        dst[0][row, start : start + size, :] = values
        start += size
    dst[0][row, start : start + W, :] = hi[:W]
    dst[1][row, start : start + W, :] = hi[W:]
    start = PAD + W
    for values in solute_row:
        size = values.shape[0]
        dst[1][row, start : start + size, :] = values
        start += size


def pack_x_kernel(coef_ref, phase_lo, phase_hi, solute_lo, solute_hi, y_lo, y_hi, to_prev, to_next):
    tiles, edge, depth = phase_lo.shape[1], phase_lo.shape[3], phase_lo.shape[4]
    width = tiles * edge + 2 * W
    for out, phase, solute, first in (
        (to_prev, phase_lo, solute_lo, 0),
        (to_next, phase_hi, solute_hi, edge - W),
    ):
        for row in range(W):
            for field, values, half in ((0, phase, 0), (1, solute, W)):
                at = (2 * row + field) * width
                out[at : at + W, :] = y_lo[first + row, half : half + W, :]
                for tile in range(tiles):
                    begin = at + W + tile * edge
                    out[begin : begin + edge, :] = values[0, tile, row]
                out[at + width - W : at + width, :] = y_hi[first + row, half : half + W, :]
        at = 2 * W * width
        out[at : at + 8, :] = y_lo[edge]
        out[at + 8 : at + 16, :] = y_hi[edge]
        for tile in range(tiles):
            begin = at + 16 + 8 * tile
            out[begin : begin + 8, :] = jnp.zeros((8, depth), jnp.float32)
            for kind in range(3):
                out[begin + kind : begin + kind + 1, :] = jnp.full((1, depth), coef_ref[tile, kind], jnp.float32)


def pack_x(phase, solute, coef, y_lo, y_hi):
    _, tiles, edge, _, depth = phase.shape
    low = pl.BlockSpec((1, tiles, W, edge, depth), lambda i: (0, 0, 0, 0, 0))
    high = pl.BlockSpec((1, tiles, W, edge, depth), lambda i: (0, 0, edge // W - 1, 0, 0))
    side = pl.BlockSpec((edge + 1, 2 * W, depth), lambda i: (0, 0, 0))
    rows = 2 * W * (tiles * edge + 2 * W) + 8 * (tiles + 2)
    out = jax.ShapeDtypeStruct((rows, depth), jnp.float32)
    whole = pl.BlockSpec((rows, depth), lambda i: (0, 0))
    return pl.pallas_call(
        pack_x_kernel,
        grid=(1,),
        in_specs=[pl.BlockSpec(memory_space=pltpu.SMEM), low, high, low, high, side, side],
        out_specs=[whole, whole],
        out_shape=[out, out],
        name="pack_x",
    )(coef, phase, phase, solute, solute, y_lo, y_hi)


def update(near_p, near_u, under, mobile, spread):
    p, p_xl, p_xh, p_yl, p_yh = near_p
    u, u_xl, u_xh, u_yl, u_yh = near_u
    depth = p.shape[-1]
    lane = lax.broadcasted_iota(jnp.int32, p.shape, 1)
    first, last = lane == 0, lane == depth - 1
    p_zl = jnp.where(first, p, pltpu.roll(p, 1, 1))
    p_zh = jnp.where(last, p, pltpu.roll(p, depth - 1, 1))
    u_zl = jnp.where(first, u, pltpu.roll(u, 1, 1))
    u_zh = jnp.where(last, u, pltpu.roll(u, depth - 1, 1))
    dx, dy, dz = p_xh - p_xl, p_yh - p_yl, p_zh - p_zl
    qx, qy, qz = dx * dx, dy * dy, dz * dz
    total = qx + qy + qz
    fourth = qx * qx + qy * qy + qz * qz
    base = total + 4.0
    guess = pl.reciprocal(base, approx=True)
    inverse = guess * (2.0 - base * guess)
    extra = (4.0 * aniso_strength * fourth - (3.0 * aniso_strength) * total * total) * (inverse * inverse)
    lap_p = (p_xl + p_xh) + (p_yl + p_yh) + (p_zl + p_zh) - 6.0 * p
    lap_u = (u_xl + u_xh) + (u_yl + u_yh) + (u_zl + u_zh) - 6.0 * u
    well = 1.0 - p * p
    drive = well * (under + u)
    change = mobile * (lap_p + extra * lap_p + well * (p - 2.0 * drive))
    return p + change, u + spread * lap_u + 0.5 * change


def steps_kernel(
    coef_ref, phase, solute, y_lo, y_hi, x_lo, x_hi, owner_ref, out, p_a, u_a, p_b, u_b, coefs
):
    tiles, edge, depth = phase.shape[1], phase.shape[2], phase.shape[4]
    width = tiles * edge + 2 * W
    pieces = out.shape[0]
    rows_each = edge // pieces
    for zone, source in ((0, x_lo), (1, None), (2, x_hi)):
        for kind in range(3):
            if source is None:
                parts = [y_lo[edge, kind : kind + 1, :]]
                parts += [jnp.full((1, depth), coef_ref[tile, kind], jnp.float32) for tile in range(tiles)]
                parts += [y_hi[edge, kind : kind + 1, :]]
            else:
                at = 2 * W * width + kind
                parts = [source[at : at + 1, :]]
                parts += [source[at + 16 + 8 * tile : at + 17 + 8 * tile, :] for tile in range(tiles)]
                parts += [source[at + 8 : at + 9, :]]
            coefs[zone, kind, :W, :] = jnp.broadcast_to(parts[0], (W, depth))
            for tile in range(tiles):
                begin = W + tile * edge
                coefs[zone, kind, begin : begin + edge, :] = jnp.broadcast_to(parts[1 + tile], (edge, depth))
            coefs[zone, kind, width - W :, :] = jnp.broadcast_to(parts[-1], (W, depth))
    for source, first in ((x_lo, 0), (x_hi, edge + W)):
        for row in range(W):
            for field, buffer in ((0, p_a), (1, u_a)):
                at = (2 * row + field) * width
                buffer[first + row, PAD : PAD + width, :] = source[at : at + width, :]

    def load_row(row, carry):
        fill_row(
            (p_a, u_a),
            W + row,
            [phase[0, tile, row] for tile in range(tiles)],
            [solute[0, tile, row] for tile in range(tiles)],
            y_lo[row],
            y_hi[row],
        )
        return carry

    lax.fori_loop(0, edge, load_row, 0)

    def cell_block(src_p, src_u, row, start, zone):
        size = 8
        near = []
        for src in (src_p, src_u):
            near.append(
                (
                    src[row, start : start + size, :],
                    src[row - 1, start : start + size, :],
                    src[row + 1, start : start + size, :],
                    src[row, start - 1 : start - 1 + size, :],
                    src[row, start + 1 : start + 1 + size, :],
                )
            )
        kinds = [coefs[zone, kind, start - PAD : start - PAD + size, :] for kind in range(3)]
        return update(near[0], near[1], *kinds)

    for step in range(NSTEPS - 1):
        src_p, src_u, dst_p, dst_u = (p_a, u_a, p_b, u_b) if step % 2 == 0 else (p_b, u_b, p_a, u_a)

        def one_row(row, carry, src_p=src_p, src_u=src_u, dst_p=dst_p, dst_u=dst_u):
            zone = jnp.where(row < W, 0, jnp.where(row < W + edge, 1, 2))
            for start in range(PAD, PAD + width, 8):
                new_p, new_u = cell_block(src_p, src_u, row, start, zone)
                dst_p[row, start : start + 8, :] = new_p
                dst_u[row, start : start + 8, :] = new_u
            return carry

        lax.fori_loop(step + 1, edge + 2 * W - step - 1, one_row, 0)

    src_p, src_u = (p_a, u_a) if (NSTEPS - 1) % 2 == 0 else (p_b, u_b)

    def last_row(row, carry):
        piece, inner = row // rows_each, row % rows_each
        for tile in range(tiles):
            for col in range(0, edge, 8):
                start = PAD + W + tile * edge + col
                new_p, new_u = cell_block(src_p, src_u, row + W, start, 1)
                at = pl.multiple_of(inner * edge, 8) + col
                size = rows_each * edge
                out[piece, pl.ds(pl.multiple_of((2 * tile) * size + at, 8), 8), :] = new_p
                out[piece, pl.ds(pl.multiple_of((2 * tile + 1) * size + at, 8), 8), :] = new_u
        return carry

    lax.fori_loop(0, edge, last_row, 0)
    tail = 2 * tiles * rows_each * edge
    lane = lax.broadcasted_iota(jnp.int32, (8, depth), 1)
    names = jnp.zeros((8, depth), jnp.float32)
    for tile in range(tiles):
        names = jnp.where(lane == tile, owner_ref[0, tile].astype(jnp.float32), names)
    for piece in range(pieces):
        out[piece, tail : tail + 8, :] = names


def run_steps(phase, solute, coef, y_lo, y_hi, x_lo, x_hi, owner, pieces):
    _, tiles, edge, _, depth = phase.shape
    width = tiles * edge + 2 * W
    buffer = pltpu.VMEM((edge + 2 * W, width + 2 * PAD, depth), jnp.float32)
    vmem = pl.BlockSpec(memory_space=pltpu.VMEM)
    smem = pl.BlockSpec(memory_space=pltpu.SMEM)
    rows = 2 * tiles * (edge // pieces) * edge + 8
    return pl.pallas_call(
        steps_kernel,
        in_specs=[smem] + [vmem] * 6 + [smem],
        out_specs=vmem,
        out_shape=jax.ShapeDtypeStruct((pieces, rows, depth), jnp.float32),
        scratch_shapes=[buffer] * 4 + [pltpu.VMEM((3, 3, width, depth), jnp.float32)],
        compiler_params=pltpu.CompilerParams(vmem_limit_bytes=40 * 1024 * 1024),
        name="steps",
    )(coef, phase, solute, y_lo, y_hi, x_lo, x_hi, owner)


def route_kernel(pieces, tiles, arrived, out, names, name_sem, sems):
    size = out.shape[2]
    tail = tiles * size
    names_copy = pltpu.make_async_copy(arrived.at[:, pl.ds(tail, 1), :], names, name_sem)
    names_copy.start()
    names_copy.wait()
    count = pieces * tiles
    owners = []
    for home in range(count):
        owners.append(lax.rem(names[home // tiles, 0, home % tiles].astype(jnp.int32), pieces))
    copies = []
    for home in range(count):
        slot = jnp.int32(0)
        for other in range(home):
            slot = slot + (owners[other] == owners[home]).astype(jnp.int32)
        copy = pltpu.make_async_copy(
            arrived.at[home // tiles, pl.ds((home % tiles) * size, size), :],
            out.at[owners[home], slot],
            sems.at[home],
        )
        copy.start()
        copies.append(copy)
    for copy in copies:
        copy.wait()


def route(arrived, pieces, tiles):
    depth = arrived.shape[2]
    size = (arrived.shape[1] - 8) // tiles
    return pl.pallas_call(
        functools.partial(route_kernel, pieces, tiles),
        in_specs=[pl.BlockSpec(memory_space=pl.ANY)],
        out_specs=pl.BlockSpec(memory_space=pl.ANY),
        out_shape=jax.ShapeDtypeStruct((pieces, tiles, size, depth), jnp.float32),
        scratch_shapes=[
            pltpu.SMEM((pieces, 1, depth), jnp.float32),
            pltpu.SemaphoreType.DMA,
            pltpu.SemaphoreType.DMA((pieces * tiles,)),
        ],
        name="route",
    )(arrived)


def settle_kernel(pieces, arrived, phase, solute, sems):
    tiles, edge, depth = phase.shape[1], phase.shape[2], phase.shape[4]
    rows_each = edge // pieces
    copies = []
    for piece in range(pieces):
        for tile in range(tiles):
            for field, out in ((0, phase), (1, solute)):
                copy = pltpu.make_async_copy(
                    arrived.at[piece, tile, field],
                    out.at[0, tile, pl.ds(piece * rows_each, rows_each)],
                    sems.at[len(copies)],
                )
                copy.start()
                copies.append(copy)
    for copy in copies:
        copy.wait()


def settle(arrived, pieces, tiles, edge, depth):
    arrived = arrived.reshape(pieces, tiles, 2, edge // pieces, edge, depth)
    out = jax.ShapeDtypeStruct((1, tiles, edge, edge, depth), jnp.float32)
    hbm = pl.BlockSpec(memory_space=pl.ANY)
    return pl.pallas_call(
        functools.partial(settle_kernel, pieces),
        in_specs=[hbm],
        out_specs=[hbm, hbm],
        out_shape=[out, out],
        scratch_shapes=[pltpu.SemaphoreType.DMA((pieces * tiles * 2,))],
        name="settle",
    )(arrived)


def ring(axis, step):
    count = lax.axis_size(axis)
    return [(i, (i + step) % count) for i in range(count)]


def per_device(phase, solute, undercool, mobility, diffusivity, owner):
    _, tiles, edge, _, depth = phase.shape
    pieces = lax.axis_size("gy")
    coef = jnp.stack([undercool[0], mobility[0], diffusivity[0]], axis=1)
    to_prev, to_next = pack_y(phase, solute, coef)
    y_lo = lax.ppermute(to_next, "gy", ring("gy", 1))
    y_hi = lax.ppermute(to_prev, "gy", ring("gy", -1))
    to_prev, to_next = pack_x(phase, solute, coef, y_lo, y_hi)
    x_lo = lax.ppermute(to_next, "gx", ring("gx", 1))
    x_hi = lax.ppermute(to_prev, "gx", ring("gx", -1))
    cut = run_steps(phase, solute, coef, y_lo, y_hi, x_lo, x_hi, owner, pieces)
    spread = lax.all_to_all(cut, "gy", split_axis=0, concat_axis=0, tiled=True)
    sent = route(spread, pieces, tiles)
    arrived = lax.all_to_all(sent, "gy", split_axis=0, concat_axis=0, tiled=True)
    return tuple(settle(arrived, pieces, tiles, edge, depth))


def solution(mesh):
    tile_spec = P("gx", "gy", None, None, None)
    in_specs = (tile_spec, tile_spec) + (P("gx", "gy"),) * 4
    out_spec = P(("gx", "gy"), None, None, None, None)
    return jax.shard_map(
        per_device, mesh=mesh, in_specs=in_specs, out_specs=(out_spec, out_spec), check_vma=False
    )
```

time: 621 us -> 287 us (0.46)
  waiting for transfers between devices: 309 us -> 13.6 us
  Pallas kernels: 0 us -> 152 us
  local copies, waits for them, and re-layouts: 143 us -> 4.7 us
  starting transfers between devices: 84.7 us -> 4.72 us
  blocking collectives: 31 us -> 108 us
  other arithmetic: 46.9 us -> 0.67 us
    all_to_all x10 -> x0, waiting for transfers between devices: 228 us -> none  [the longest x1 84.4 us: per_device(): lax.all_to_all(place(solute_tiles, target, slots), 'gy', split_axis=0, co...]
    pallas_call x0 -> x5, Pallas kernels: none -> 152 us  [the longest x1 65.6 us: route(): pl.pallas_call(functools.partial(route_kernel, pieces, tiles), in_specs=[...]
    all_to_all x1 -> x2, blocking collectives: 31 us -> 108 us  [the longest x1 55.1 us: per_device(): spread = lax.all_to_all(cut, 'gy', split_axis=0, concat_axis=0, tiled=True)]
    ppermute x16 -> x4, waiting for transfers between devices: 80.5 us -> 13.6 us  [the longest x1 6.27 us: per_device(): x_lo = lax.ppermute(to_next, 'gx', ring('gx', 1))]
    all_to_all x10 -> x0, starting transfers between devices: 65 us -> none  [the longest x3 21.3 us: per_device(): lax.all_to_all(outgoing, 'gy', split_axis=0, concat_axis=0, tiled=True)]
    slice x35 -> x0, local copies, waits for them, and re-layouts: 57.9 us -> none  [the longest x3 8.93 us: neighbours(): field[:, 1:]]
    add x7 -> x0, other arithmetic: 42.8 us -> none  [step_cells(): new_solute = solute + spread * lap_solute + 0.5 * (new_phase - phase)]
    scatter x11 -> x0, local copies, waits for them, and re-layouts: 23.6 us -> none  [the longest x10 23 us: place(): jnp.zeros((slots,) + values.shape[1:], values.dtype).at[target].set(values)]
  transfers between devices with their start and end apart: 26 -> 4, of which waited for: 20 -> 4; matrix products, arithmetic and copies ran while one was open for 16% -> 0% of each run, Pallas kernels for 0% -> 0%
where the time goes in v1:
time: 287 us; the launch traced here: 285 us
  Pallas kernels  152 us (53%)
  blocking collectives  108 us (38%)
  waiting for transfers between devices  13.6 us (5%)
  starting transfers between devices  4.72 us (2%)
  local copies, waits for them, and re-layouts  4.7 us (2%)
    pallas_call x1, Pallas kernels, route(): pl.pallas_call(functools.partial(route_kernel, pieces, tiles), in_specs=[...  65.6 us
    pallas_call x1, Pallas kernels, settle(): pl.pallas_call(functools.partial(settle_kernel, pieces), in_specs=[hbm],...  64.9 us
    all_to_all x1, blocking collectives, per_device(): spread = lax.all_to_all(cut, 'gy', split_axis=0, concat_axis=0, tiled=True)  55.1 us
    all_to_all x1, blocking collectives, per_device(): lax.all_to_all(sent, 'gy', split_axis=0, concat_axis=0, tiled=True)  52.7 us
    pallas_call x1, Pallas kernels, run_steps(): pl.pallas_call(steps_kernel, in_specs=[smem] + [vmem] * 6 + [smem], out_s...  18 us
    ppermute x1, waiting for transfers between devices, per_device(): x_lo = lax.ppermute(to_next, 'gx', ring('gx', 1))  6.27 us
  transfers between devices with their start and end apart: 4, of which 4 were waited for; matrix products, arithmetic and copies ran while one was open for 0% of the time, Pallas kernels for 0%

profile of v1, /device:TPU:8, one launch (start us, length us, event | category | flops | bytes accessed | tf_op | source)
XLA Modules:
  0.0 284.5 jit_solution(15558019566291670754)
XLA Ops:
  0.6 0.7 copy.8
  1.4 0.7 copy.9
  2.1 0.7 copy.10
  2.9 0.7 pad_maximum_fusion.coef_ref
  3.5 1.9 pack_y.1
  5.4 1.5 collective-permute-start
  6.9 0.0 copy-start
  6.9 0.0 copy-start.1
  6.9 0.0 copy-start.6
  6.9 0.0 copy-start.7
  6.9 1.5 collective-permute-start.1
  8.4 4.6 %collective-permute-done.y_lo = f32[33,8,128]{2,1,0:T(8,128)S(1)} collective-permute-done((f32[33,8,128]{2,1,0:T(8,128)}, f32[33,8,128]{2,1,0:T(8,128)S(1)}, u32[]{:S(2)}, u32[]{:S(2)}) %collective-permute-start) | collective-permute-done | bytes 135200 | tf_op jit(solution)/shard_map/ppermute | solution.py:331
  13.0 0.0 copy-start.2
  13.0 1.7 collective-permute-done.1.y_hi
  14.7 0.0 copy-done.2
  14.7 0.0 copy-start.4
  14.7 0.6 copy-done.4
  15.4 2.1 pack_x.1
  17.4 0.0 collective-permute-start.2
  17.4 1.7 collective-permute-start.3
  19.2 6.3 %collective-permute-done.2.x_lo = f32[608,128]{1,0:T(8,128)S(1)} collective-permute-done((f32[608,128]{1,0:T(8,128)}, f32[608,128]{1,0:T(8,128)S(1)}, u32[]{:S(2)}, u32[]{:S(2)}) %collective-permute-start.2) | collective-permute-done | bytes 311328 | tf_op jit(solution)/shard_map/ppermute | solution.py:334
  25.4 1.0 collective-permute-done.3.x_hi
  26.4 0.0 copy-done
  26.4 0.0 copy-done.1
  26.4 0.0 copy-done.6
  26.4 0.0 copy-done.7
  26.4 0.0 copy-start.3
  26.4 0.9 copy-done.3
  27.3 0.0 copy-start.5
  27.3 0.9 copy-done.5
  28.2 18.0 %steps.1 = f32[8,520,128]{2,1,0:T(8,128)S(1)} custom-call(f32[2,3]{1,0:T(2,128)S(1)} %copy-done.6, f32[1,2,32,32,128]{4,3,2,1,0:T(8,128)S(1)} %copy-done, f32[1,2,32,32,128]{4,3,2,1,0:T(8,128)S(1)} %copy-done.1, f32[33,8,128]{2,1,0:T(8,128)S(1)} %copy-done.3, f32[33,8,128]{2,1,0:T(8,128)S(1)} %copy-done.5, f32[608,128]{1,0:T(8,128)S(1)} %collective-permute-done.2.x_lo, ...), custom_call_target="tpu_custom_call" | custom-call | tf_op jit(solution)/shard_map/steps/pallas_call | solution.py:235
  46.2 55.1 %all_to_all.10.arrived = f32[8,520,128]{2,1,0:T(8,128)} all-to-all(f32[8,520,128]{2,1,0:T(8,128)S(1)} %steps.1), channel_id=1, replica_groups=mesh['gx'=4,'gy'=8] {'gy'}, dimensions={0} | all-to-all | bytes 4259840 | tf_op jit(solution)/shard_map/all_to_all | solution.py:337
  101.3 65.6 %route.1 = f32[8,2,256,128]{3,2,1,0:T(8,128)} custom-call(f32[8,520,128]{2,1,0:T(8,128)} %all_to_all.10.arrived), custom_call_target="tpu_custom_call" | custom-call | tf_op jit(solution)/shard_map/route/pallas_call | solution.py:275
  166.9 52.7 %all_to_all.11 = f32[8,2,256,128]{3,2,1,0:T(8,128)} all-to-all(f32[8,2,256,128]{3,2,1,0:T(8,128)} %route.1), channel_id=1, replica_groups=mesh['gx'=4,'gy'=8] {'gy'}, dimensions={0} | all-to-all | bytes 4194304 | tf_op jit(solution)/shard_map/all_to_all | solution.py:339
  219.6 64.9 %settle.1 = (f32[1,2,32,32,128]{4,3,2,1,0:T(8,128)}, f32[1,2,32,32,128]{4,3,2,1,0:T(8,128)}) custom-call(f32[8,2,2,4,32,128]{5,4,3,2,1,0:T(8,128)} %bitcast.4), custom_call_target="tpu_custom_call" | custom-call | tf_op jit(solution)/shard_map/settle/pallas_call | solution.py:311
Async XLA Ops:
  5.4 7.6 %collective-permute-start = (f32[33,8,128]{2,1,0:T(8,128)}, f32[33,8,128]{2,1,0:T(8,128)S(1)}, u32[]{:S(2)}, u32[]{:S(2)}) collective-permute-start(f32[33,8,128]{2,1,0:T(8,128)} %get-tuple-element.6), channel_id=1, source_target_pairs={{0,1},{1,2},{2,3},{3,4},{4,5},{5,6},{6,7},{7,0},{8,9},{9,10},{10,1... | collective-permute-start | bytes 405512 | tf_op jit(solution)/shard_map/ppermute | solution.py:331
  6.9 19.5 %copy-start = (f32[1,2,32,32,128]{4,3,2,1,0:T(8,128)S(1)}, f32[1,2,32,32,128]{4,3,2,1,0:T(8,128)}, u32[]{:S(2)}) copy-start(f32[1,2,32,32,128]{4,3,2,1,0:T(8,128)} %phase.1) | copy-start | bytes 3145732
  6.9 19.5 %copy-start.1 = (f32[1,2,32,32,128]{4,3,2,1,0:T(8,128)S(1)}, f32[1,2,32,32,128]{4,3,2,1,0:T(8,128)}, u32[]{:S(2)}) copy-start(f32[1,2,32,32,128]{4,3,2,1,0:T(8,128)} %solute.1) | copy-start | bytes 3145732
  6.9 19.5 %copy-start.6 = (f32[2,3]{1,0:T(2,128)S(1)}, f32[2,3]{1,0:T(2,128)}, u32[]{:S(2)}) copy-start(f32[2,3]{1,0:T(2,128)} %pad_maximum_fusion.coef_ref) | copy-start | bytes 76
  6.9 19.5 %copy-start.7 = (s32[1,2]{1,0:T(1,128)S(1)}, s32[1,2]{1,0:T(1,128)}, u32[]{:S(2)}) copy-start(s32[1,2]{1,0:T(1,128)} %owner_ref.1) | copy-start | bytes 28
  6.9 7.8 %collective-permute-start.1 = (f32[33,8,128]{2,1,0:T(8,128)}, f32[33,8,128]{2,1,0:T(8,128)S(1)}, u32[]{:S(2)}, u32[]{:S(2)}) collective-permute-start(f32[33,8,128]{2,1,0:T(8,128)} %get-tuple-element.7), channel_id=1, source_target_pairs={{0,7},{1,0},{2,1},{3,2},{4,3},{5,4},{6,5},{7,6},{8,15},{9,8},{10,9... | collective-permute-start | bytes 405512 | tf_op jit(solution)/shard_map/ppermute | solution.py:332
  13.0 1.7 copy-start.2
  14.7 0.7 copy-start.4
  17.4 8.0 %collective-permute-start.2 = (f32[608,128]{1,0:T(8,128)}, f32[608,128]{1,0:T(8,128)S(1)}, u32[]{:S(2)}, u32[]{:S(2)}) collective-permute-start(f32[608,128]{1,0:T(8,128)} %get-tuple-element.8), channel_id=1, source_target_pairs={{0,8},{8,16},{16,24},{24,0},{1,9},{9,17},{17,25},{25,1},{2,10},{10... | collective-permute-start | bytes 933896 | tf_op jit(solution)/shard_map/ppermute | solution.py:334
  17.4 9.0 %collective-permute-start.3 = (f32[608,128]{1,0:T(8,128)}, f32[608,128]{1,0:T(8,128)S(1)}, u32[]{:S(2)}, u32[]{:S(2)}) collective-permute-start(f32[608,128]{1,0:T(8,128)} %get-tuple-element.9), channel_id=1, source_target_pairs={{0,24},{8,0},{16,8},{24,16},{1,25},{9,1},{17,9},{25,17},{2,26},{10... | collective-permute-start | bytes 933896 | tf_op jit(solution)/shard_map/ppermute | solution.py:335
  26.4 0.9 copy-start.3
  27.3 0.9 copy-start.5

commit v2 on v1

v2 whole, which is shorter than its diff:
```python
import functools

import jax
import jax.numpy as jnp
from jax import lax
from jax.experimental import pallas as pl
from jax.experimental.pallas import tpu as pltpu
from jax.sharding import PartitionSpec as P

NSTEPS = 4
W = NSTEPS
PAD = 8

aniso_strength = 0.05


def pack_y_kernel(under, mobile, spread, phase_lo, phase_hi, solute_lo, solute_hi, to_prev, to_next):
    edge = phase_lo.shape[2]
    to_prev[:edge, :W, :] = phase_lo[0, 0, :, :W, :]
    to_prev[:edge, W:, :] = solute_lo[0, 0, :, :W, :]
    to_next[:edge, :W, :] = phase_hi[0, 0, :, W:, :]
    to_next[:edge, W:, :] = solute_hi[0, 0, :, W:, :]
    to_prev[edge] = jnp.zeros((2 * W, to_prev.shape[2]), jnp.float32)
    to_next[edge] = jnp.zeros((2 * W, to_prev.shape[2]), jnp.float32)
    for kind, own in enumerate((under, mobile, spread)):
        to_prev[edge, kind, :] = jnp.full((to_prev.shape[2],), own[0, 0], jnp.float32)
        to_next[edge, kind, :] = jnp.full((to_prev.shape[2],), own[0, own.shape[1] - 1], jnp.float32)


def pack_y(phase, solute, coef):
    _, tiles, edge, _, depth = phase.shape
    low = pl.BlockSpec((1, 1, edge, 2 * W, depth), lambda i: (0, 0, 0, 0, 0))
    high = pl.BlockSpec((1, 1, edge, 2 * W, depth), lambda i: (0, tiles - 1, 0, edge // (2 * W) - 1, 0))
    out = jax.ShapeDtypeStruct((edge + 1, 2 * W, depth), jnp.float32)
    whole = pl.BlockSpec((edge + 1, 2 * W, depth), lambda i: (0, 0, 0))
    return pl.pallas_call(
        pack_y_kernel,
        grid=(1,),
        in_specs=[pl.BlockSpec(memory_space=pltpu.SMEM)] * 3 + [low, high, low, high],
        out_specs=[whole, whole],
        out_shape=[out, out],
        name="pack_y",
    )(*coef, phase, phase, solute, solute)


def fill_row(dst, row, phase_row, solute_row, lo, hi):
    start = PAD
    dst[0][row, start : start + W, :] = lo[:W]
    dst[1][row, start : start + W, :] = lo[W:]
    start += W
    for values in phase_row:
        size = values.shape[0]
        dst[0][row, start : start + size, :] = values
        start += size
    dst[0][row, start : start + W, :] = hi[:W]
    dst[1][row, start : start + W, :] = hi[W:]
    start = PAD + W
    for values in solute_row:
        size = values.shape[0]
        dst[1][row, start : start + size, :] = values
        start += size


def pack_x_kernel(under, mobile, spread, phase_lo, phase_hi, solute_lo, solute_hi, y_lo, y_hi, to_prev, to_next):
    tiles, edge, depth = phase_lo.shape[1], phase_lo.shape[3], phase_lo.shape[4]
    width = tiles * edge + 2 * W
    for out, phase, solute, first in (
        (to_prev, phase_lo, solute_lo, 0),
        (to_next, phase_hi, solute_hi, edge - W),
    ):
        for row in range(W):
            for field, values, half in ((0, phase, 0), (1, solute, W)):
                at = (2 * row + field) * width
                out[at : at + W, :] = y_lo[first + row, half : half + W, :]
                for tile in range(tiles):
                    begin = at + W + tile * edge
                    out[begin : begin + edge, :] = values[0, tile, row]
                out[at + width - W : at + width, :] = y_hi[first + row, half : half + W, :]
        at = 2 * W * width
        out[at : at + 8, :] = y_lo[edge]
        out[at + 8 : at + 16, :] = y_hi[edge]
        for tile in range(tiles):
            begin = at + 16 + 8 * tile
            out[begin : begin + 8, :] = jnp.zeros((8, depth), jnp.float32)
            for kind, own in enumerate((under, mobile, spread)):
                out[begin + kind : begin + kind + 1, :] = jnp.full((1, depth), own[0, tile], jnp.float32)


def pack_x(phase, solute, coef, y_lo, y_hi):
    _, tiles, edge, _, depth = phase.shape
    low = pl.BlockSpec((1, tiles, W, edge, depth), lambda i: (0, 0, 0, 0, 0))
    high = pl.BlockSpec((1, tiles, W, edge, depth), lambda i: (0, 0, edge // W - 1, 0, 0))
    side = pl.BlockSpec((edge + 1, 2 * W, depth), lambda i: (0, 0, 0))
    rows = 2 * W * (tiles * edge + 2 * W) + 8 * (tiles + 2)
    out = jax.ShapeDtypeStruct((rows, depth), jnp.float32)
    whole = pl.BlockSpec((rows, depth), lambda i: (0, 0))
    return pl.pallas_call(
        pack_x_kernel,
        grid=(1,),
        in_specs=[pl.BlockSpec(memory_space=pltpu.SMEM)] * 3 + [low, high, low, high, side, side],
        out_specs=[whole, whole],
        out_shape=[out, out],
        name="pack_x",
    )(*coef, phase, phase, solute, solute, y_lo, y_hi)


def update(near_p, near_u, under, mobile, spread):
    p, p_xl, p_xh, p_yl, p_yh = near_p
    u, u_xl, u_xh, u_yl, u_yh = near_u
    depth = p.shape[-1]
    lane = lax.broadcasted_iota(jnp.int32, p.shape, 1)
    first, last = lane == 0, lane == depth - 1
    p_zl = jnp.where(first, p, pltpu.roll(p, 1, 1))
    p_zh = jnp.where(last, p, pltpu.roll(p, depth - 1, 1))
    u_zl = jnp.where(first, u, pltpu.roll(u, 1, 1))
    u_zh = jnp.where(last, u, pltpu.roll(u, depth - 1, 1))
    dx, dy, dz = p_xh - p_xl, p_yh - p_yl, p_zh - p_zl
    qx, qy, qz = dx * dx, dy * dy, dz * dz
    total = qx + qy + qz
    fourth = qx * qx + qy * qy + qz * qz
    base = total + 4.0
    guess = pl.reciprocal(base, approx=True)
    inverse = guess * (2.0 - base * guess)
    extra = (4.0 * aniso_strength * fourth - (3.0 * aniso_strength) * total * total) * (inverse * inverse)
    lap_p = (p_xl + p_xh) + (p_yl + p_yh) + (p_zl + p_zh) - 6.0 * p
    lap_u = (u_xl + u_xh) + (u_yl + u_yh) + (u_zl + u_zh) - 6.0 * u
    well = 1.0 - p * p
    drive = well * (under + u)
    change = mobile * (lap_p + extra * lap_p + well * (p - 2.0 * drive))
    return p + change, u + spread * lap_u + 0.5 * change


class Plan:
    def __init__(self, pieces, tiles, edge, depth):
        self.pieces, self.tiles, self.edge, self.depth = pieces, tiles, edge, depth
        self.half = pieces // 2
        self.inner = (edge - 2 * W) // pieces * pieces
        self.low = (edge - self.inner) // 2
        self.rows_a = self.inner // pieces
        self.rows_b = (edge - self.inner) // pieces
        self.cols_a = edge - 8
        self.size_a = self.rows_a * self.cols_a
        self.size_b = self.rows_b * edge + self.rows_a * 8
        self.size = self.size_a + self.size_b


AUX = 8


def cells(src_p, src_u, row, start, coefs):
    near = []
    for src in (src_p, src_u):
        near.append(
            (
                src[row, start : start + 8, :],
                src[row - 1, start : start + 8, :],
                src[row + 1, start : start + 8, :],
                src[row, start - 1 : start + 7, :],
                src[row, start + 1 : start + 9, :],
            )
        )
    return update(near[0], near[1], *coefs)


def inner_kernel(plan, under, mobile, spread, phase, solute, *rest):
    half, tiles, edge = plan.half, plan.tiles, plan.edge
    outs, (p_a, u_a, p_b, u_b) = rest[:half], rest[half:]
    count = half * plan.rows_a
    me = lax.axis_index("gy")
    other = 1 - me // half
    base = plan.low - W + other * count

    def load_row(row, carry):
        for tile in range(tiles):
            start = PAD + tile * edge
            p_a[row, start : start + edge, :] = phase[0, tile, base + row]
            u_a[row, start : start + edge, :] = solute[0, tile, base + row]
        return carry

    lax.fori_loop(0, count + 2 * W, load_row, 0)
    for step in range(NSTEPS):
        src_p, src_u, dst_p, dst_u = (p_a, u_a, p_b, u_b) if step % 2 == 0 else (p_b, u_b, p_a, u_a)

        def one_row(row, carry, src_p=src_p, src_u=src_u, dst_p=dst_p, dst_u=dst_u):
            for start in range(PAD, PAD + tiles * edge, 8):
                tile = (start - PAD) // edge
                kinds = (under[0, tile], mobile[0, tile], spread[0, tile])
                new_p, new_u = cells(src_p, src_u, row, start, kinds)
                dst_p[row, start : start + 8, :] = new_p
                dst_u[row, start : start + 8, :] = new_u
            return carry

        lax.fori_loop(step + 1, count + 2 * W - step - 1, one_row, 0, unroll=UNROLL)
    done_p, done_u = (p_a, u_a) if NSTEPS % 2 == 0 else (p_b, u_b)
    for index, out in enumerate(outs):
        piece = (me ^ (half + index)) - other * half
        for tile in range(tiles):
            start = PAD + tile * edge + (8 if tile == 0 else 0)
            for field, done in ((0, done_p), (1, done_u)):
                for row in range(plan.rows_a):
                    at = (2 * tile + field) * plan.size_a + row * plan.cols_a
                    out[at : at + plan.cols_a, :] = done[
                        W + piece * plan.rows_a + row, start : start + plan.cols_a, :
                    ]


UNROLL = 4


def run_inner(plan, coef, phase, solute):
    rows = plan.half * plan.rows_a + 2 * W
    buffer = pltpu.VMEM((rows, plan.tiles * plan.edge + 2 * PAD, plan.depth), jnp.float32)
    vmem = pl.BlockSpec(memory_space=pltpu.VMEM)
    smem = pl.BlockSpec(memory_space=pltpu.SMEM)
    shape = jax.ShapeDtypeStruct((2 * plan.tiles * plan.size_a, plan.depth), jnp.float32)
    return pl.pallas_call(
        functools.partial(inner_kernel, plan),
        in_specs=[smem] * 3 + [vmem] * 2,
        out_specs=[vmem] * plan.half,
        out_shape=[shape] * plan.half,
        scratch_shapes=[buffer] * 4,
        compiler_params=pltpu.CompilerParams(vmem_limit_bytes=40 * 1024 * 1024),
        cost_estimate=pl.CostEstimate(flops=10**8, bytes_accessed=24 * 1024 * 1024, transcendentals=0),
        name="inner",
    )(*coef, phase, solute)


def steps_kernel(plan, under, mobile, spread, owner_ref, phase, solute, y_lo, y_hi, x_lo, x_hi, *rest):
    tiles, edge, depth, half = plan.tiles, plan.edge, plan.depth, plan.half
    outs, (p_a, u_a, p_b, u_b, coefs) = rest[: plan.pieces], rest[plan.pieces :]
    width = tiles * edge + 2 * W
    me = lax.axis_index("gy")
    for zone, source in ((0, x_lo), (1, None), (2, x_hi)):
        for kind, own in enumerate((under, mobile, spread)):
            if source is None:
                parts = [y_lo[edge, kind : kind + 1, :]]
                parts += [jnp.full((1, depth), own[0, tile], jnp.float32) for tile in range(tiles)]
                parts += [y_hi[edge, kind : kind + 1, :]]
            else:
                at = 2 * W * width + kind
                parts = [source[at : at + 1, :]]
                parts += [source[at + 16 + 8 * tile : at + 17 + 8 * tile, :] for tile in range(tiles)]
                parts += [source[at + 8 : at + 9, :]]
            coefs[zone, kind, :W, :] = jnp.broadcast_to(parts[0], (W, depth))
            for tile in range(tiles):
                begin = W + tile * edge
                coefs[zone, kind, begin : begin + edge, :] = jnp.broadcast_to(parts[1 + tile], (edge, depth))
            coefs[zone, kind, width - W :, :] = jnp.broadcast_to(parts[-1], (W, depth))
    for source, first in ((x_lo, 0), (x_hi, edge + W)):
        for row in range(W):
            for field, buffer in ((0, p_a), (1, u_a)):
                at = (2 * row + field) * width
                buffer[first + row, PAD : PAD + width, :] = source[at : at + width, :]

    def load_row(row, carry):
        fill_row(
            (p_a, u_a),
            W + row,
            [phase[0, tile, row] for tile in range(tiles)],
            [solute[0, tile, row] for tile in range(tiles)],
            y_lo[row],
            y_hi[row],
        )
        return carry

    lax.fori_loop(0, edge, load_row, 0)
    for step in range(NSTEPS):
        src_p, src_u, dst_p, dst_u = (p_a, u_a, p_b, u_b) if step % 2 == 0 else (p_b, u_b, p_a, u_a)

        def one_row(row, carry, src_p=src_p, src_u=src_u, dst_p=dst_p, dst_u=dst_u):
            zone = jnp.where(row < W, 0, jnp.where(row < W + edge, 1, 2))
            for start in range(PAD, PAD + width, 8):
                kinds = [coefs[zone, kind, start - PAD : start - PAD + 8, :] for kind in range(3)]
                new_p, new_u = cells(src_p, src_u, row, start, kinds)
                dst_p[row, start : start + 8, :] = new_p
                dst_u[row, start : start + 8, :] = new_u
            return carry

        lax.fori_loop(step + 1, edge + 2 * W - step - 1, one_row, 0, unroll=UNROLL)
    done_p, done_u = (p_a, u_a) if NSTEPS % 2 == 0 else (p_b, u_b)
    lane = lax.broadcasted_iota(jnp.int32, (AUX, depth), 1)
    names = jnp.zeros((AUX, depth), jnp.float32)
    for tile in range(tiles):
        names = jnp.where(lane == tile, owner_ref[0, tile].astype(jnp.float32), names)
    for mask, out in enumerate(outs):
        piece = me ^ mask
        begin = 0 if mask >= half else plan.size_a
        each = plan.size_b + begin
        for tile in range(tiles):
            start = PAD + W + tile * edge
            start_a, start_e = (start + 8, start) if tile == 0 else (start, start + plan.cols_a)
            for field, done in ((0, done_p), (1, done_u)):
                at = (2 * tile + field) * each
                for row in range(plan.rows_a):
                    x = W + plan.low + piece * plan.rows_a + row
                    if mask < half:
                        to = at + row * plan.cols_a
                        out[to : to + plan.cols_a, :] = done[x, start_a : start_a + plan.cols_a, :]
                    to = at + begin + plan.rows_b * edge + row * 8
                    out[to : to + 8, :] = done[x, start_e : start_e + 8, :]
                for row in range(plan.rows_b):
                    index = piece * plan.rows_b + row
                    x = W + index + jnp.where(index < plan.low, 0, plan.inner)
                    to = at + begin + row * edge
                    out[to : to + edge, :] = done[x, start : start + edge, :]
        tail = 2 * tiles * each
        out[tail : tail + AUX, :] = names


def run_steps(plan, coef, owner, phase, solute, y_lo, y_hi, x_lo, x_hi):
    tiles, edge, depth = plan.tiles, plan.edge, plan.depth
    width = tiles * edge + 2 * W
    buffer = pltpu.VMEM((edge + 2 * W, width + 2 * PAD, depth), jnp.float32)
    vmem = pl.BlockSpec(memory_space=pltpu.VMEM)
    smem = pl.BlockSpec(memory_space=pltpu.SMEM)
    near = jax.ShapeDtypeStruct((2 * tiles * plan.size + AUX, depth), jnp.float32)
    far = jax.ShapeDtypeStruct((2 * tiles * plan.size_b + AUX, depth), jnp.float32)
    return pl.pallas_call(
        functools.partial(steps_kernel, plan),
        in_specs=[smem] * 4 + [vmem] * 6,
        out_specs=[vmem] * plan.pieces,
        out_shape=[near] * plan.half + [far] * plan.half,
        scratch_shapes=[buffer] * 4 + [pltpu.VMEM((3, 3, width, depth), jnp.float32)],
        compiler_params=pltpu.CompilerParams(vmem_limit_bytes=40 * 1024 * 1024),
        cost_estimate=pl.CostEstimate(flops=10**8, bytes_accessed=40 * 1024 * 1024, transcendentals=0),
        name="steps",
    )(*coef, owner, phase, solute, y_lo, y_hi, x_lo, x_hi)


def route_kernel(plan, *refs):
    pieces, tiles, half, each = plan.pieces, plan.tiles, plan.half, 2 * plan.size
    near, far_a, far_b = refs[:half], refs[half : 2 * half], refs[2 * half : 3 * half]
    outs = refs[3 * half : 3 * half + pieces]
    held, names, table, name_sems, in_sems, out_sems = refs[3 * half + pieces :]
    me = lax.axis_index("gy")
    name_copies, copies = [], []
    for mask in range(pieces):
        source = near[mask] if mask < half else far_b[mask - half]
        tail = tiles * (each if mask < half else 2 * plan.size_b)
        copy = pltpu.make_async_copy(source.at[pl.ds(tail, 1), :], names.at[mask], name_sems.at[mask])
        copy.start()
        name_copies.append(copy)
    for mask in range(pieces):
        for tile in range(tiles):
            for field in range(2):
                index = 2 * tile + field
                if mask < half:
                    parts = [(near[mask], index * plan.size, 0, plan.size)]
                else:
                    parts = [
                        (far_a[mask - half], index * plan.size_a, 0, plan.size_a),
                        (far_b[mask - half], index * plan.size_b, plan.size_a, plan.size_b),
                    ]
                for source, begin, to, size in parts:
                    copy = pltpu.make_async_copy(
                        source.at[pl.ds(begin, size), :],
                        held.at[mask * tiles + tile, pl.ds(field * plan.size + to, size), :],
                        in_sems.at[len(copies)],
                    )
                    copy.start()
                    copies.append(copy)
    for mask in range(pieces):
        for tile in range(tiles):
            held[mask * tiles + tile, each : each + AUX, :] = jnp.full((AUX, plan.depth), tile, jnp.float32)
    for copy in name_copies:
        copy.wait()
    peers, homes = [], []
    for mask in range(pieces):
        for tile in range(tiles):
            peers.append(lax.rem(names[mask, 0, tile].astype(jnp.int32), pieces))
            homes.append((me ^ mask) * tiles + tile)
    for index in range(pieces * tiles):
        slot = jnp.int32(0)
        for other in range(pieces * tiles):
            if other != index:
                ahead = (peers[other] == peers[index]) & (homes[other] < homes[index])
                slot = slot + ahead.astype(jnp.int32)
        table[(peers[index] ^ me) * tiles + slot] = index
    for copy in copies:
        copy.wait()
    sends = []
    for mask in range(pieces):
        for slot in range(tiles):
            copy = pltpu.make_async_copy(
                held.at[table[mask * tiles + slot]], outs[mask].at[slot], out_sems.at[len(sends)]
            )
            copy.start()
            sends.append(copy)
    for copy in sends:
        copy.wait()


def route(plan, near, far_a, far_b):
    pieces, tiles, depth = plan.pieces, plan.tiles, plan.depth
    rows = 2 * plan.size + AUX
    count = 2 * tiles * (plan.half + 2 * plan.half)
    hbm = pl.BlockSpec(memory_space=pl.ANY)
    return pl.pallas_call(
        functools.partial(route_kernel, plan),
        in_specs=[hbm] * (3 * plan.half),
        out_specs=[hbm] * pieces,
        out_shape=[jax.ShapeDtypeStruct((tiles, rows, depth), jnp.float32)] * pieces,
        scratch_shapes=[
            pltpu.VMEM((pieces * tiles, rows, depth), jnp.float32),
            pltpu.SMEM((pieces, 1, depth), jnp.float32),
            pltpu.SMEM((pieces * tiles,), jnp.int32),
            pltpu.SemaphoreType.DMA((pieces,)),
            pltpu.SemaphoreType.DMA((count,)),
            pltpu.SemaphoreType.DMA((pieces * tiles,)),
        ],
        compiler_params=pltpu.CompilerParams(vmem_limit_bytes=16 * 1024 * 1024),
        name="route",
    )(*near, *far_a, *far_b)


def settle_kernel(plan, *refs):
    pieces, tiles, edge = plan.pieces, plan.tiles, plan.edge
    arrived, (phase, solute), (sides, side_sems, sems) = refs[:pieces], refs[pieces : pieces + 2], refs[pieces + 2 :]
    me = lax.axis_index("gy")
    side_copies = []
    for mask in range(pieces):
        for slot in range(tiles):
            copy = pltpu.make_async_copy(
                arrived[mask].at[slot, pl.ds(2 * plan.size, 1), :],
                sides.at[mask, slot],
                side_sems.at[len(side_copies)],
            )
            copy.start()
            side_copies.append(copy)
    copies = []

    def move(mask, slot, begin, rows, cols, out, row, col):
        copy = pltpu.make_async_copy(
            arrived[mask].at[slot, pl.ds(begin, rows * cols), :].reshape(rows, cols, plan.depth),
            out.at[0, slot, pl.ds(row, rows), pl.ds(col, cols), :],
            sems.at[len(copies)],
        )
        copy.start()
        copies.append(copy)

    for mask in range(pieces):
        piece = me ^ mask
        for slot in range(tiles):
            for field, out in ((0, phase), (1, solute)):
                for row in range(plan.rows_b):
                    index = piece * plan.rows_b + row
                    x = index + jnp.where(index < plan.low, 0, plan.inner)
                    begin = field * plan.size + plan.size_a + row * edge
                    move(mask, slot, begin, 1, edge, out, x, 0)
    for copy in side_copies:
        copy.wait()
    for mask in range(pieces):
        piece = me ^ mask
        for slot in range(tiles):
            side = sides[mask, slot, 0, 0].astype(jnp.int32)
            col_a = pl.multiple_of((1 - side) * 8, 8)
            col_e = pl.multiple_of(side * plan.cols_a, 8)
            x = plan.low + piece * plan.rows_a
            for field, out in ((0, phase), (1, solute)):
                move(mask, slot, field * plan.size, plan.rows_a, plan.cols_a, out, x, col_a)
                begin = field * plan.size + plan.size_a + plan.rows_b * edge
                move(mask, slot, begin, plan.rows_a, 8, out, x, col_e)
    for copy in copies:
        copy.wait()


def settle(plan, arrived):
    pieces, tiles, edge, depth = plan.pieces, plan.tiles, plan.edge, plan.depth
    out = jax.ShapeDtypeStruct((1, tiles, edge, edge, depth), jnp.float32)
    hbm = pl.BlockSpec(memory_space=pl.ANY)
    vmem = pl.BlockSpec(memory_space=pltpu.VMEM)
    return pl.pallas_call(
        functools.partial(settle_kernel, plan),
        in_specs=[hbm] * pieces,
        out_specs=[vmem, vmem],
        out_shape=[out, out],
        scratch_shapes=[
            pltpu.SMEM((pieces, tiles, 1, depth), jnp.float32),
            pltpu.SemaphoreType.DMA((pieces * tiles,)),
            pltpu.SemaphoreType.DMA((pieces * tiles * 2 * (plan.rows_b + 2),)),
        ],
        compiler_params=pltpu.CompilerParams(vmem_limit_bytes=16 * 1024 * 1024),
        name="settle",
    )(*arrived)


def ring(axis, step):
    count = lax.axis_size(axis)
    return [(i, (i + step) % count) for i in range(count)]


def swap(values, mask):
    return lax.ppermute(values, "gy", [(i, i ^ mask) for i in range(lax.axis_size("gy"))])


def per_device(phase, solute, undercool, mobility, diffusivity, owner):
    _, tiles, edge, _, depth = phase.shape
    plan = Plan(lax.axis_size("gy"), tiles, edge, depth)
    half = plan.half
    coef = (undercool, mobility, diffusivity)
    to_prev, to_next = pack_y(phase, solute, coef)
    y_lo = lax.ppermute(to_next, "gy", ring("gy", 1))
    y_hi = lax.ppermute(to_prev, "gy", ring("gy", -1))
    first = run_inner(plan, coef, phase, solute)
    far_a = [swap(values, half + index) for index, values in enumerate(first)]
    to_prev, to_next = pack_x(phase, solute, coef, y_lo, y_hi)
    x_lo = lax.ppermute(to_next, "gx", ring("gx", 1))
    x_hi = lax.ppermute(to_prev, "gx", ring("gx", -1))
    second = run_steps(plan, coef, owner, phase, solute, y_lo, y_hi, x_lo, x_hi)
    spread = [second[0]] + [swap(second[mask], mask) for mask in range(1, plan.pieces)]
    sent = route(plan, spread[:half], far_a, spread[half:])
    arrived = [sent[0]] + [swap(sent[mask], mask) for mask in range(1, plan.pieces)]
    return tuple(settle(plan, arrived))


def solution(mesh):
    tile_spec = P("gx", "gy", None, None, None)
    in_specs = (tile_spec, tile_spec) + (P("gx", "gy"),) * 4
    out_spec = P(("gx", "gy"), None, None, None, None)
    return jax.shard_map(
        per_device, mesh=mesh, in_specs=in_specs, out_specs=(out_spec, out_spec), check_vma=False
    )
```

time: 287 us -> 136 us (0.47)
  Pallas kernels: 152 us -> 34 us
  blocking collectives: 108 us -> 0 us
  waiting for transfers between devices: 13.6 us -> 70.7 us
  starting transfers between devices: 4.72 us -> 29.4 us
  local copies, waits for them, and re-layouts: 4.7 us -> 0.69 us
    pallas_call x3 -> x4, Pallas kernels: 148 us -> 30.1 us  [the longest x1 12.9 us: run_steps(): pl.pallas_call(functools.partial(steps_kernel, plan), in_specs=[smem] * 4...]
    all_to_all x2 -> x0, blocking collectives: 108 us -> none  [the longest x1 55.1 us: per_device(): spread = lax.all_to_all(cut, 'gy', split_axis=0, concat_axis=0, tiled=True)]
    ppermute x0 -> x18, waiting for transfers between devices: none -> 64.3 us  [swap(): lax.ppermute(values, 'gy', [(i, i ^ mask) for i in range(lax.axis_size('g...]
    ppermute x0 -> x18, starting transfers between devices: none -> 24.7 us  [swap(): lax.ppermute(values, 'gy', [(i, i ^ mask) for i in range(lax.axis_size('g...]
    ppermute x1, waiting for transfers between devices: 6.27 us -> 0.01 us  [per_device(): x_lo = lax.ppermute(to_next, 'gx', ring('gx', 1))]
  transfers between devices with their start and end apart: 4 -> 22, of which waited for: 4 -> 14; matrix products, arithmetic and copies ran while one was open for 0% -> 0% of each run, Pallas kernels for 0% -> 13%
where the time goes in v2:
time: 136 us
  waiting for transfers between devices  70.7 us (52%)
  Pallas kernels  34 us (25%)
  starting transfers between devices  29.4 us (22%)
    ppermute x18, waiting for transfers between devices, swap(): lax.ppermute(values, 'gy', [(i, i ^ mask) for i in range(lax.axis_size('g...  64.3 us
    ppermute x18, starting transfers between devices, swap(): lax.ppermute(values, 'gy', [(i, i ^ mask) for i in range(lax.axis_size('g...  24.7 us
    pallas_call x1, Pallas kernels, run_steps(): pl.pallas_call(functools.partial(steps_kernel, plan), in_specs=[smem] * 4...  12.9 us
    pallas_call x1, Pallas kernels, route(): pl.pallas_call(functools.partial(route_kernel, plan), in_specs=[hbm] * (3...  7.67 us
    pallas_call x1, Pallas kernels, run_inner(): pl.pallas_call(functools.partial(inner_kernel, plan), in_specs=[smem] * 3...  5.32 us
    ppermute x1, waiting for transfers between devices, per_device(): y_lo = lax.ppermute(to_next, 'gy', ring('gy', 1))  4.65 us
    pallas_call x1, Pallas kernels, settle(): pl.pallas_call(functools.partial(settle_kernel, plan), in_specs=[hbm] * p...  4.16 us
  transfers between devices with their start and end apart: 22, of which 14 were waited for; matrix products, arithmetic and copies ran while one was open for 0% of the time, Pallas kernels for 13%

profile of v2, /device:TPU:8, one launch (start us, length us, event | category | flops | bytes accessed | tf_op | source)
XLA Modules:
  0.0 135.6 jit_solution(15505547551350415462)
XLA Ops:
  0.6 1.9 %pack_y.1 = (f32[33,8,128]{2,1,0:T(8,128)}, f32[33,8,128]{2,1,0:T(8,128)}) custom-call(f32[1,2]{1,0:T(1,128)} %under.7, f32[1,2]{1,0:T(1,128)} %mobile.7, f32[1,2]{1,0:T(1,128)} %spread.7, f32[1,2,32,32,128]{4,3,2,1,0:T(8,128)} %phase.3, f32[1,2,32,32,128]{4,3,2,1,0:T(8,128)} %phase.3, f32[1,2,32,32,128]{4,3,2,1,0:T(8,128)} %solute.3, ...), custom_call_target="tpu_custom_call" | custom-call | tf_op jit(solution)/shard_map/pack_y/pallas_call | solution.py:36
  2.5 1.5 %collective-permute-start = (f32[33,8,128]{2,1,0:T(8,128)}, f32[33,8,128]{2,1,0:T(8,128)S(1)}, u32[]{:S(2)}, u32[]{:S(2)}) collective-permute-start(f32[33,8,128]{2,1,0:T(8,128)} %get-tuple-element.26), channel_id=1, source_target_pairs={{0,1},{1,2},{2,3},{3,4},{4,5},{5,6},{6,7},{7,0},{8,9},{9,10},{10,1... | collective-permute-start | bytes 405512 | tf_op jit(solution)/shard_map/ppermute | solution.py:502
  4.0 0.0 copy-start
  4.0 0.0 copy-start.1
  4.0 1.4 %collective-permute-start.1 = (f32[33,8,128]{2,1,0:T(8,128)}, f32[33,8,128]{2,1,0:T(8,128)S(1)}, u32[]{:S(2)}, u32[]{:S(2)}) collective-permute-start(f32[33,8,128]{2,1,0:T(8,128)} %get-tuple-element.27), channel_id=1, source_target_pairs={{0,7},{1,0},{2,1},{3,2},{4,3},{5,4},{6,5},{7,6},{8,15},{9,8},{10,9... | collective-permute-start | bytes 405512 | tf_op jit(solution)/shard_map/ppermute | solution.py:503
  5.4 4.6 %collective-permute-done.y_lo = f32[33,8,128]{2,1,0:T(8,128)S(1)} collective-permute-done((f32[33,8,128]{2,1,0:T(8,128)}, f32[33,8,128]{2,1,0:T(8,128)S(1)}, u32[]{:S(2)}, u32[]{:S(2)}) %collective-permute-start) | collective-permute-done | bytes 135200 | tf_op jit(solution)/shard_map/ppermute | solution.py:502
  10.1 0.0 copy-start.2
  10.1 1.8 %collective-permute-done.1.y_hi = f32[33,8,128]{2,1,0:T(8,128)S(1)} collective-permute-done((f32[33,8,128]{2,1,0:T(8,128)}, f32[33,8,128]{2,1,0:T(8,128)S(1)}, u32[]{:S(2)}, u32[]{:S(2)}) %collective-permute-start.1) | collective-permute-done | bytes 135200 | tf_op jit(solution)/shard_map/ppermute | solution.py:503
  11.8 0.0 copy-done.2
  11.8 0.7 copy-done.4
  12.5 2.1 %pack_x.1 = (f32[608,128]{1,0:T(8,128)}, f32[608,128]{1,0:T(8,128)}) custom-call(f32[1,2]{1,0:T(1,128)} %under.7, f32[1,2]{1,0:T(1,128)} %mobile.7, f32[1,2]{1,0:T(1,128)} %spread.7, f32[1,2,32,32,128]{4,3,2,1,0:T(8,128)} %phase.3, f32[1,2,32,32,128]{4,3,2,1,0:T(8,128)} %phase.3, f32[1,2,32,32,128]{4,3,2,1,0:T(8,128)} %solute.3, ...), custom_call_target="tpu_custom_call" | custom-call | tf_op jit(solution)/shard_map/pack_x/pallas_call | solution.py:97
  14.6 0.1 collective-permute-start.2
  14.6 0.0 copy-start.5
  14.7 1.7 %collective-permute-start.3 = (f32[608,128]{1,0:T(8,128)}, f32[608,128]{1,0:T(8,128)S(1)}, u32[]{:S(2)}, u32[]{:S(2)}) collective-permute-start(f32[608,128]{1,0:T(8,128)} %get-tuple-element.29), channel_id=1, source_target_pairs={{0,24},{8,0},{16,8},{24,16},{1,25},{9,1},{17,9},{25,17},{2,26},{10... | collective-permute-start | bytes 933896 | tf_op jit(solution)/shard_map/ppermute | solution.py:508
  16.4 0.0 copy-done
  16.4 0.0 copy-done.1
  16.4 0.0 copy-done.6
  16.4 0.0 copy-done.7
  16.4 0.0 copy-done.8
  16.4 5.3 %inner.1 = (f32[288,128]{1,0:T(8,128)S(1)}, f32[288,128]{1,0:T(8,128)S(1)}, f32[288,128]{1,0:T(8,128)S(1)}, f32[288,128]{1,0:T(8,128)S(1)}) custom-call(f32[1,2]{1,0:T(1,128)S(1)} %copy-done.6, f32[1,2]{1,0:T(1,128)S(1)} %copy-done.7, f32[1,2]{1,0:T(1,128)S(1)} %copy-done.8, f32[1,2,32,32,128]{4,3,2,1,0:T(8,128)S(1)} %copy-done, ...), custom_call_target="tpu_custom_call" | custom-call | flops 100000000 | bytes 25165824 | tf_op jit(solution)/shard_map/inner/pallas_call | solution.py:216
  21.7 2.7 %collective-permute-start.7 = (f32[288,128]{1,0:T(8,128)S(1)}, f32[288,128]{1,0:T(8,128)S(1)}, u32[]{:S(2)}, u32[]{:S(2)}) collective-permute-start(f32[288,128]{1,0:T(8,128)S(1)} %get-tuple-element.34), channel_id=1, source_target_pairs={{0,4},{1,5},{2,6},{3,7},{4,0},{5,1},{6,2},{7,3},{8,12},{9,13},{10,... | collective-permute-start | bytes 442376 | tf_op jit(solution)/shard_map/ppermute | solution.py:493
  24.4 1.0 collective-permute-start.8
  25.4 1.6 %collective-permute-start.9 = (f32[288,128]{1,0:T(8,128)S(1)}, f32[288,128]{1,0:T(8,128)S(1)}, u32[]{:S(2)}, u32[]{:S(2)}) collective-permute-start(f32[288,128]{1,0:T(8,128)S(1)} %get-tuple-element.36), channel_id=1, source_target_pairs={{0,6},{1,7},{2,4},{3,5},{4,2},{5,3},{6,0},{7,1},{8,14},{9,15},{10,... | collective-permute-start | bytes 442376 | tf_op jit(solution)/shard_map/ppermute | solution.py:493
  27.0 0.0 collective-permute-done.2.x_lo
  27.0 0.6 collective-permute-start.10
  27.6 0.0 collective-permute-done.3.x_hi
  27.6 0.0 copy-done.3
  27.7 0.0 copy-done.5
  27.7 0.0 copy-done.9
  27.7 12.9 %steps.1 = (f32[520,128]{1,0:T(8,128)S(1)}, f32[520,128]{1,0:T(8,128)S(1)}, f32[520,128]{1,0:T(8,128)S(1)}, f32[520,128]{1,0:T(8,128)S(1)}, f32[232,128]{1,0:T(8...) custom-call(f32[1,2]{1,0:T(1,128)S(1)} %copy-done.6, f32[1,2]{1,0:T(1,128)S(1)} %copy-done.7, ...), custom_call_target="tpu_custom_call" | custom-call | flops 100000000 | bytes 41943040 | tf_op jit(solution)/shard_map/steps/pallas_call | solution.py:318
  40.6 1.3 collective-permute-start.4
  41.9 0.0 collective-permute-done.7.refs_4_
  41.9 2.2 %collective-permute-start.5 = (f32[520,128]{1,0:T(8,128)S(1)}, f32[520,128]{1,0:T(8,128)S(1)}, u32[]{:S(2)}, u32[]{:S(2)}) collective-permute-start(f32[520,128]{1,0:T(8,128)S(1)} %get-tuple-element.32), channel_id=1, source_target_pairs={{0,2},{1,3},{2,0},{3,1},{4,6},{5,7},{6,4},{7,5},{8,10},{9,11},{10,... | collective-permute-start | bytes 798728 | tf_op jit(solution)/shard_map/ppermute | solution.py:493
  44.2 0.0 collective-permute-done.8.refs_5_
  44.2 2.4 %collective-permute-start.6 = (f32[520,128]{1,0:T(8,128)S(1)}, f32[520,128]{1,0:T(8,128)S(1)}, u32[]{:S(2)}, u32[]{:S(2)}) collective-permute-start(f32[520,128]{1,0:T(8,128)S(1)} %get-tuple-element.33), channel_id=1, source_target_pairs={{0,3},{1,2},{2,1},{3,0},{4,7},{5,6},{6,5},{7,4},{8,11},{9,10},{10,... | collective-permute-start | bytes 798728 | tf_op jit(solution)/shard_map/ppermute | solution.py:493
  46.6 0.8 collective-permute-done.9.refs_6_
  47.4 1.2 collective-permute-start.11
  48.6 3.1 %collective-permute-done.10.refs_7_ = f32[288,128]{1,0:T(8,128)S(1)} collective-permute-done((f32[288,128]{1,0:T(8,128)S(1)}, f32[288,128]{1,0:T(8,128)S(1)}, u32[]{:S(2)}, u32[]{:S(2)}) %collective-permute-start.10) | collective-permute-done | bytes 147488 | tf_op jit(solution)/shard_map/ppermute | solution.py:493
  51.6 0.0 collective-permute-start.12
  51.6 10.5 %collective-permute-done.11.refs_8_ = f32[232,128]{1,0:T(8,128)S(1)} collective-permute-done((f32[232,128]{1,0:T(8,128)S(1)}, f32[232,128]{1,0:T(8,128)S(1)}, u32[]{:S(2)}, u32[]{:S(2)}) %collective-permute-start.11) | collective-permute-done | bytes 118816 | tf_op jit(solution)/shard_map/ppermute | solution.py:493
  62.1 0.0 collective-permute-start.13
  62.1 2.2 %collective-permute-done.12.refs_9_ = f32[232,128]{1,0:T(8,128)S(1)} collective-permute-done((f32[232,128]{1,0:T(8,128)S(1)}, f32[232,128]{1,0:T(8,128)S(1)}, u32[]{:S(2)}, u32[]{:S(2)}) %collective-permute-start.12) | collective-permute-done | bytes 118816 | tf_op jit(solution)/shard_map/ppermute | solution.py:493
  64.3 0.5 collective-permute-start.14
  64.8 4.8 %collective-permute-done.13.refs_10_ = f32[232,128]{1,0:T(8,128)S(1)} collective-permute-done((f32[232,128]{1,0:T(8,128)S(1)}, f32[232,128]{1,0:T(8,128)S(1)}, u32[]{:S(2)}, u32[]{:S(2)}) %collective-permute-start.13) | collective-permute-done | bytes 118816 | tf_op jit(solution)/shard_map/ppermute | solution.py:493
  69.6 3.5 %collective-permute-done.14.refs_11_ = f32[232,128]{1,0:T(8,128)S(1)} collective-permute-done((f32[232,128]{1,0:T(8,128)S(1)}, f32[232,128]{1,0:T(8,128)S(1)}, u32[]{:S(2)}, u32[]{:S(2)}) %collective-permute-start.14) | collective-permute-done | bytes 118816 | tf_op jit(solution)/shard_map/ppermute | solution.py:493
  73.1 0.0 collective-permute-done.4.refs_1_
  73.1 0.0 collective-permute-done.5.refs_2_
  73.1 0.0 collective-permute-done.6.refs_3_
  73.1 7.7 %route.1 = (f32[2,264,128]{2,1,0:T(8,128)S(1)}, f32[2,264,128]{2,1,0:T(8,128)S(1)}, f32[2,264,128]{2,1,0:T(8,128)S(1)}, f32[2,264,128]{2,1,0:T(8,128)S(1)}, f32[...) custom-call(f32[520,128]{1,0:T(8,128)S(1)} %get-tuple-element.30.ref, ...), custom_call_target="tpu_custom_call" | custom-call | tf_op jit(solution)/shard_map/route/pallas_call | solution.py:398
  80.8 0.1 collective-permute-start.15
  80.9 2.8 %collective-permute-start.16 = (f32[2,264,128]{2,1,0:T(8,128)S(1)}, f32[2,264,128]{2,1,0:T(8,128)S(1)}, u32[]{:S(2)}, u32[]{:S(2)}) collective-permute-start(f32[2,264,128]{2,1,0:T(8,128)S(1)} %get-tuple-element.44), channel_id=1, source_target_pairs={{0,2},{1,3},{2,0},{3,1},{4,6},{5,7},{6,4},{7,5},{8,10},{9,11},{10,... | collective-permute-start | bytes 811016 | tf_op jit(solution)/shard_map/ppermute | solution.py:493
  83.7 0.6 collective-permute-start.17
  84.3 1.0 collective-permute-start.18
  85.3 2.2 %collective-permute-start.19 = (f32[2,264,128]{2,1,0:T(8,128)S(1)}, f32[2,264,128]{2,1,0:T(8,128)S(1)}, u32[]{:S(2)}, u32[]{:S(2)}) collective-permute-start(f32[2,264,128]{2,1,0:T(8,128)S(1)} %get-tuple-element.47), channel_id=1, source_target_pairs={{0,5},{1,4},{2,7},{3,6},{4,1},{5,0},{6,3},{7,2},{8,13},{9,12},{10,... | collective-permute-start | bytes 811016 | tf_op jit(solution)/shard_map/ppermute | solution.py:493
  87.5 1.8 %collective-permute-done.15.refs_1_ = f32[2,264,128]{2,1,0:T(8,128)S(1)} collective-permute-done((f32[2,264,128]{2,1,0:T(8,128)S(1)}, f32[2,264,128]{2,1,0:T(8,128)S(1)}, u32[]{:S(2)}, u32[]{:S(2)}) %collective-permute-start.15) | collective-permute-done | bytes 270368 | tf_op jit(solution)/shard_map/ppermute | solution.py:493
  89.4 1.6 %collective-permute-start.20 = (f32[2,264,128]{2,1,0:T(8,128)S(1)}, f32[2,264,128]{2,1,0:T(8,128)S(1)}, u32[]{:S(2)}, u32[]{:S(2)}) collective-permute-start(f32[2,264,128]{2,1,0:T(8,128)S(1)} %get-tuple-element.48), channel_id=1, source_target_pairs={{0,6},{1,7},{2,4},{3,5},{4,2},{5,3},{6,0},{7,1},{8,14},{9,15},{10,... | collective-permute-start | bytes 811016 | tf_op jit(solution)/shard_map/ppermute | solution.py:493
  90.9 6.8 %collective-permute-done.16.refs_2_ = f32[2,264,128]{2,1,0:T(8,128)S(1)} collective-permute-done((f32[2,264,128]{2,1,0:T(8,128)S(1)}, f32[2,264,128]{2,1,0:T(8,128)S(1)}, u32[]{:S(2)}, u32[]{:S(2)}) %collective-permute-start.16) | collective-permute-done | bytes 270368 | tf_op jit(solution)/shard_map/ppermute | solution.py:493
  97.8 2.9 %collective-permute-start.21 = (f32[2,264,128]{2,1,0:T(8,128)S(1)}, f32[2,264,128]{2,1,0:T(8,128)S(1)}, u32[]{:S(2)}, u32[]{:S(2)}) collective-permute-start(f32[2,264,128]{2,1,0:T(8,128)S(1)} %get-tuple-element.49), channel_id=1, source_target_pairs={{0,7},{1,6},{2,5},{3,4},{4,3},{5,2},{6,1},{7,0},{8,15},{9,14},{10,... | collective-permute-start | bytes 811016 | tf_op jit(solution)/shard_map/ppermute | solution.py:493
  100.6 0.0 collective-permute-done.17.refs_3_
  100.6 2.4 %collective-permute-done.18.refs_4_ = f32[2,264,128]{2,1,0:T(8,128)S(1)} collective-permute-done((f32[2,264,128]{2,1,0:T(8,128)S(1)}, f32[2,264,128]{2,1,0:T(8,128)S(1)}, u32[]{:S(2)}, u32[]{:S(2)}) %collective-permute-start.18) | collective-permute-done | bytes 270368 | tf_op jit(solution)/shard_map/ppermute | solution.py:493
  103.0 18.2 %collective-permute-done.19.refs_5_ = f32[2,264,128]{2,1,0:T(8,128)S(1)} collective-permute-done((f32[2,264,128]{2,1,0:T(8,128)S(1)}, f32[2,264,128]{2,1,0:T(8,128)S(1)}, u32[]{:S(2)}, u32[]{:S(2)}) %collective-permute-start.19) | collective-permute-done | bytes 270368 | tf_op jit(solution)/shard_map/ppermute | solution.py:493
  121.2 7.3 %collective-permute-done.20.refs_6_ = f32[2,264,128]{2,1,0:T(8,128)S(1)} collective-permute-done((f32[2,264,128]{2,1,0:T(8,128)S(1)}, f32[2,264,128]{2,1,0:T(8,128)S(1)}, u32[]{:S(2)}, u32[]{:S(2)}) %collective-permute-start.20) | collective-permute-done | bytes 270368 | tf_op jit(solution)/shard_map/ppermute | solution.py:493
  128.5 2.9 %collective-permute-done.21.refs_7_ = f32[2,264,128]{2,1,0:T(8,128)S(1)} collective-permute-done((f32[2,264,128]{2,1,0:T(8,128)S(1)}, f32[2,264,128]{2,1,0:T(8,128)S(1)}, u32[]{:S(2)}, u32[]{:S(2)}) %collective-permute-start.21) | collective-permute-done | bytes 270368 | tf_op jit(solution)/shard_map/ppermute | solution.py:493
  131.4 4.2 %settle.1 = (f32[1,2,32,32,128]{4,3,2,1,0:T(8,128)}, f32[1,2,32,32,128]{4,3,2,1,0:T(8,128)}) custom-call(f32[2,264,128]{2,1,0:T(8,128)S(1)} %get-tuple-element.42.refs_0_, f32[2,264,128]{2,1,0:T(8,128)S(1)} %collective-permute-done.15.refs_1_, f32[2,264,128]{2,1,0:T(8,128)S(1)} %collective-permute-done.16.refs_2_, ...), custom_call_target="tpu_custom_call" | custom-call | tf_op jit(solution)/shard_map/settle/pallas_call | solution.py:472
  (6 shorter events, 0.0 us)
Async XLA Ops:
  2.5 7.6 %collective-permute-start = (f32[33,8,128]{2,1,0:T(8,128)}, f32[33,8,128]{2,1,0:T(8,128)S(1)}, u32[]{:S(2)}, u32[]{:S(2)}) collective-permute-start(f32[33,8,128]{2,1,0:T(8,128)} %get-tuple-element.26), channel_id=1, source_target_pairs={{0,1},{1,2},{2,3},{3,4},{4,5},{5,6},{6,7},{7,0},{8,9},{9,10},{10,1... | collective-permute-start | bytes 405512 | tf_op jit(solution)/shard_map/ppermute | solution.py:502
  4.0 12.4 %copy-start = (f32[1,2,32,32,128]{4,3,2,1,0:T(8,128)S(1)}, f32[1,2,32,32,128]{4,3,2,1,0:T(8,128)}, u32[]{:S(2)}) copy-start(f32[1,2,32,32,128]{4,3,2,1,0:T(8,128)} %phase.3) | copy-start | bytes 3145732
  4.0 12.4 %copy-start.1 = (f32[1,2,32,32,128]{4,3,2,1,0:T(8,128)S(1)}, f32[1,2,32,32,128]{4,3,2,1,0:T(8,128)}, u32[]{:S(2)}) copy-start(f32[1,2,32,32,128]{4,3,2,1,0:T(8,128)} %solute.3) | copy-start | bytes 3145732
  4.0 7.8 %collective-permute-start.1 = (f32[33,8,128]{2,1,0:T(8,128)}, f32[33,8,128]{2,1,0:T(8,128)S(1)}, u32[]{:S(2)}, u32[]{:S(2)}) collective-permute-start(f32[33,8,128]{2,1,0:T(8,128)} %get-tuple-element.27), channel_id=1, source_target_pairs={{0,7},{1,0},{2,1},{3,2},{4,3},{5,4},{6,5},{7,6},{8,15},{9,8},{10,9... | collective-permute-start | bytes 405512 | tf_op jit(solution)/shard_map/ppermute | solution.py:503
  10.1 1.8 %copy-start.2 = (f32[33,8,128]{2,1,0:T(8,128)}, f32[33,8,128]{2,1,0:T(8,128)S(1)}, u32[]{:S(2)}) copy-start(f32[33,8,128]{2,1,0:T(8,128)S(1)} %collective-permute-done.y_lo) | copy-start | bytes 405508
  11.8 0.7 copy-start.4
  14.6 1.8 %copy-start.6 = (f32[1,2]{1,0:T(1,128)S(1)}, f32[1,2]{1,0:T(1,128)}, u32[]{:S(2)}) copy-start(f32[1,2]{1,0:T(1,128)} %under.7) | copy-start | bytes 28
  14.6 1.8 %copy-start.7 = (f32[1,2]{1,0:T(1,128)S(1)}, f32[1,2]{1,0:T(1,128)}, u32[]{:S(2)}) copy-start(f32[1,2]{1,0:T(1,128)} %mobile.7) | copy-start | bytes 28
  14.6 1.8 %copy-start.8 = (f32[1,2]{1,0:T(1,128)S(1)}, f32[1,2]{1,0:T(1,128)}, u32[]{:S(2)}) copy-start(f32[1,2]{1,0:T(1,128)} %spread.7) | copy-start | bytes 28
  14.6 12.4 %collective-permute-start.2 = (f32[608,128]{1,0:T(8,128)}, f32[608,128]{1,0:T(8,128)S(1)}, u32[]{:S(2)}, u32[]{:S(2)}) collective-permute-start(f32[608,128]{1,0:T(8,128)} %get-tuple-element.28), channel_id=1, source_target_pairs={{0,8},{8,16},{16,24},{24,0},{1,9},{9,17},{17,25},{25,1},{2,10},{10... | collective-permute-start | bytes 933896 | tf_op jit(solution)/shard_map/ppermute | solution.py:507
  14.6 13.0 %copy-start.3 = (f32[33,8,128]{2,1,0:T(8,128)S(1)}, f32[33,8,128]{2,1,0:T(8,128)}, u32[]{:S(2)}) copy-start(f32[33,8,128]{2,1,0:T(8,128)} %copy-done.2) | copy-start | bytes 405508
  14.6 13.0 %copy-start.5 = (f32[33,8,128]{2,1,0:T(8,128)S(1)}, f32[33,8,128]{2,1,0:T(8,128)}, u32[]{:S(2)}) copy-start(f32[33,8,128]{2,1,0:T(8,128)} %copy-done.4) | copy-start | bytes 405508
  14.7 13.0 %collective-permute-start.3 = (f32[608,128]{1,0:T(8,128)}, f32[608,128]{1,0:T(8,128)S(1)}, u32[]{:S(2)}, u32[]{:S(2)}) collective-permute-start(f32[608,128]{1,0:T(8,128)} %get-tuple-element.29), channel_id=1, source_target_pairs={{0,24},{8,0},{16,8},{24,16},{1,25},{9,1},{17,9},{25,17},{2,26},{10... | collective-permute-start | bytes 933896 | tf_op jit(solution)/shard_map/ppermute | solution.py:508
  21.7 20.2 %collective-permute-start.7 = (f32[288,128]{1,0:T(8,128)S(1)}, f32[288,128]{1,0:T(8,128)S(1)}, u32[]{:S(2)}, u32[]{:S(2)}) collective-permute-start(f32[288,128]{1,0:T(8,128)S(1)} %get-tuple-element.34), channel_id=1, source_target_pairs={{0,4},{1,5},{2,6},{3,7},{4,0},{5,1},{6,2},{7,3},{8,12},{9,13},{10,... | collective-permute-start | bytes 442376 | tf_op jit(solution)/shard_map/ppermute | solution.py:493
  24.4 19.8 %collective-permute-start.8 = (f32[288,128]{1,0:T(8,128)S(1)}, f32[288,128]{1,0:T(8,128)S(1)}, u32[]{:S(2)}, u32[]{:S(2)}) collective-permute-start(f32[288,128]{1,0:T(8,128)S(1)} %get-tuple-element.35), channel_id=1, source_target_pairs={{0,5},{1,4},{2,7},{3,6},{4,1},{5,0},{6,3},{7,2},{8,13},{9,12},{10,... | collective-permute-start | bytes 442376 | tf_op jit(solution)/shard_map/ppermute | solution.py:493
  25.4 2.2 %copy-start.9 = (s32[1,2]{1,0:T(1,128)S(1)}, s32[1,2]{1,0:T(1,128)}, u32[]{:S(2)}) copy-start(s32[1,2]{1,0:T(1,128)} %owner_ref.1) | copy-start | bytes 28
  25.4 22.0 %collective-permute-start.9 = (f32[288,128]{1,0:T(8,128)S(1)}, f32[288,128]{1,0:T(8,128)S(1)}, u32[]{:S(2)}, u32[]{:S(2)}) collective-permute-start(f32[288,128]{1,0:T(8,128)S(1)} %get-tuple-element.36), channel_id=1, source_target_pairs={{0,6},{1,7},{2,4},{3,5},{4,2},{5,3},{6,0},{7,1},{8,14},{9,15},{10,... | collective-permute-start | bytes 442376 | tf_op jit(solution)/shard_map/ppermute | solution.py:493
  27.0 24.6 %collective-permute-start.10 = (f32[288,128]{1,0:T(8,128)S(1)}, f32[288,128]{1,0:T(8,128)S(1)}, u32[]{:S(2)}, u32[]{:S(2)}) collective-permute-start(f32[288,128]{1,0:T(8,128)S(1)} %get-tuple-element.37), channel_id=1, source_target_pairs={{0,7},{1,6},{2,5},{3,4},{4,3},{5,2},{6,1},{7,0},{8,15},{9,14},{10,... | collective-permute-start | bytes 442376 | tf_op jit(solution)/shard_map/ppermute | solution.py:493
  40.6 32.5 %collective-permute-start.4 = (f32[520,128]{1,0:T(8,128)S(1)}, f32[520,128]{1,0:T(8,128)S(1)}, u32[]{:S(2)}, u32[]{:S(2)}) collective-permute-start(f32[520,128]{1,0:T(8,128)S(1)} %get-tuple-element.31), channel_id=1, source_target_pairs={{0,1},{1,0},{2,3},{3,2},{4,5},{5,4},{6,7},{7,6},{8,9},{9,8},{10,11... | collective-permute-start | bytes 798728 | tf_op jit(solution)/shard_map/ppermute | solution.py:493
  41.9 31.1 %collective-permute-start.5 = (f32[520,128]{1,0:T(8,128)S(1)}, f32[520,128]{1,0:T(8,128)S(1)}, u32[]{:S(2)}, u32[]{:S(2)}) collective-permute-start(f32[520,128]{1,0:T(8,128)S(1)} %get-tuple-element.32), channel_id=1, source_target_pairs={{0,2},{1,3},{2,0},{3,1},{4,6},{5,7},{6,4},{7,5},{8,10},{9,11},{10,... | collective-permute-start | bytes 798728 | tf_op jit(solution)/shard_map/ppermute | solution.py:493
  44.2 28.9 %collective-permute-start.6 = (f32[520,128]{1,0:T(8,128)S(1)}, f32[520,128]{1,0:T(8,128)S(1)}, u32[]{:S(2)}, u32[]{:S(2)}) collective-permute-start(f32[520,128]{1,0:T(8,128)S(1)} %get-tuple-element.33), channel_id=1, source_target_pairs={{0,3},{1,2},{2,1},{3,0},{4,7},{5,6},{6,5},{7,4},{8,11},{9,10},{10,... | collective-permute-start | bytes 798728 | tf_op jit(solution)/shard_map/ppermute | solution.py:493
  47.4 14.7 %collective-permute-start.11 = (f32[232,128]{1,0:T(8,128)S(1)}, f32[232,128]{1,0:T(8,128)S(1)}, u32[]{:S(2)}, u32[]{:S(2)}) collective-permute-start(f32[232,128]{1,0:T(8,128)S(1)} %get-tuple-element.38), channel_id=1, source_target_pairs={{0,4},{1,5},{2,6},{3,7},{4,0},{5,1},{6,2},{7,3},{8,12},{9,13},{10,... | collective-permute-start | bytes 356360 | tf_op jit(solution)/shard_map/ppermute | solution.py:493
  51.6 12.6 %collective-permute-start.12 = (f32[232,128]{1,0:T(8,128)S(1)}, f32[232,128]{1,0:T(8,128)S(1)}, u32[]{:S(2)}, u32[]{:S(2)}) collective-permute-start(f32[232,128]{1,0:T(8,128)S(1)} %get-tuple-element.39), channel_id=1, source_target_pairs={{0,5},{1,4},{2,7},{3,6},{4,1},{5,0},{6,3},{7,2},{8,13},{9,12},{10,... | collective-permute-start | bytes 356360 | tf_op jit(solution)/shard_map/ppermute | solution.py:493
  62.1 7.4 %collective-permute-start.13 = (f32[232,128]{1,0:T(8,128)S(1)}, f32[232,128]{1,0:T(8,128)S(1)}, u32[]{:S(2)}, u32[]{:S(2)}) collective-permute-start(f32[232,128]{1,0:T(8,128)S(1)} %get-tuple-element.40), channel_id=1, source_target_pairs={{0,6},{1,7},{2,4},{3,5},{4,2},{5,3},{6,0},{7,1},{8,14},{9,15},{10,... | collective-permute-start | bytes 356360 | tf_op jit(solution)/shard_map/ppermute | solution.py:493
  64.3 8.8 %collective-permute-start.14 = (f32[232,128]{1,0:T(8,128)S(1)}, f32[232,128]{1,0:T(8,128)S(1)}, u32[]{:S(2)}, u32[]{:S(2)}) collective-permute-start(f32[232,128]{1,0:T(8,128)S(1)} %get-tuple-element.41), channel_id=1, source_target_pairs={{0,7},{1,6},{2,5},{3,4},{4,3},{5,2},{6,1},{7,0},{8,15},{9,14},{10,... | collective-permute-start | bytes 356360 | tf_op jit(solution)/shard_map/ppermute | solution.py:493
  80.8 8.6 %collective-permute-start.15 = (f32[2,264,128]{2,1,0:T(8,128)S(1)}, f32[2,264,128]{2,1,0:T(8,128)S(1)}, u32[]{:S(2)}, u32[]{:S(2)}) collective-permute-start(f32[2,264,128]{2,1,0:T(8,128)S(1)} %get-tuple-element.43), channel_id=1, source_target_pairs={{0,1},{1,0},{2,3},{3,2},{4,5},{5,4},{6,7},{7,6},{8,9},{9,8},{10,11... | collective-permute-start | bytes 811016 | tf_op jit(solution)/shard_map/ppermute | solution.py:493
  80.9 16.9 %collective-permute-start.16 = (f32[2,264,128]{2,1,0:T(8,128)S(1)}, f32[2,264,128]{2,1,0:T(8,128)S(1)}, u32[]{:S(2)}, u32[]{:S(2)}) collective-permute-start(f32[2,264,128]{2,1,0:T(8,128)S(1)} %get-tuple-element.44), channel_id=1, source_target_pairs={{0,2},{1,3},{2,0},{3,1},{4,6},{5,7},{6,4},{7,5},{8,10},{9,11},{10,... | collective-permute-start | bytes 811016 | tf_op jit(solution)/shard_map/ppermute | solution.py:493
  83.7 16.9 %collective-permute-start.17 = (f32[2,264,128]{2,1,0:T(8,128)S(1)}, f32[2,264,128]{2,1,0:T(8,128)S(1)}, u32[]{:S(2)}, u32[]{:S(2)}) collective-permute-start(f32[2,264,128]{2,1,0:T(8,128)S(1)} %get-tuple-element.45), channel_id=1, source_target_pairs={{0,3},{1,2},{2,1},{3,0},{4,7},{5,6},{6,5},{7,4},{8,11},{9,10},{10,... | collective-permute-start | bytes 811016 | tf_op jit(solution)/shard_map/ppermute | solution.py:493
  84.3 18.7 %collective-permute-start.18 = (f32[2,264,128]{2,1,0:T(8,128)S(1)}, f32[2,264,128]{2,1,0:T(8,128)S(1)}, u32[]{:S(2)}, u32[]{:S(2)}) collective-permute-start(f32[2,264,128]{2,1,0:T(8,128)S(1)} %get-tuple-element.46), channel_id=1, source_target_pairs={{0,4},{1,5},{2,6},{3,7},{4,0},{5,1},{6,2},{7,3},{8,12},{9,13},{10,... | collective-permute-start | bytes 811016 | tf_op jit(solution)/shard_map/ppermute | solution.py:493
  85.3 35.9 %collective-permute-start.19 = (f32[2,264,128]{2,1,0:T(8,128)S(1)}, f32[2,264,128]{2,1,0:T(8,128)S(1)}, u32[]{:S(2)}, u32[]{:S(2)}) collective-permute-start(f32[2,264,128]{2,1,0:T(8,128)S(1)} %get-tuple-element.47), channel_id=1, source_target_pairs={{0,5},{1,4},{2,7},{3,6},{4,1},{5,0},{6,3},{7,2},{8,13},{9,12},{10,... | collective-permute-start | bytes 811016 | tf_op jit(solution)/shard_map/ppermute | solution.py:493
  89.4 39.2 %collective-permute-start.20 = (f32[2,264,128]{2,1,0:T(8,128)S(1)}, f32[2,264,128]{2,1,0:T(8,128)S(1)}, u32[]{:S(2)}, u32[]{:S(2)}) collective-permute-start(f32[2,264,128]{2,1,0:T(8,128)S(1)} %get-tuple-element.48), channel_id=1, source_target_pairs={{0,6},{1,7},{2,4},{3,5},{4,2},{5,3},{6,0},{7,1},{8,14},{9,15},{10,... | collective-permute-start | bytes 811016 | tf_op jit(solution)/shard_map/ppermute | solution.py:493
  97.8 33.7 %collective-permute-start.21 = (f32[2,264,128]{2,1,0:T(8,128)S(1)}, f32[2,264,128]{2,1,0:T(8,128)S(1)}, u32[]{:S(2)}, u32[]{:S(2)}) collective-permute-start(f32[2,264,128]{2,1,0:T(8,128)S(1)} %get-tuple-element.49), channel_id=1, source_target_pairs={{0,7},{1,6},{2,5},{3,4},{4,3},{5,2},{6,1},{7,0},{8,15},{9,14},{10,... | collective-permute-start | bytes 811016 | tf_op jit(solution)/shard_map/ppermute | solution.py:493

commit v3 on v2

v3 whole, which is shorter than its diff:
```python
import functools

import jax
import jax.numpy as jnp
from jax import lax
from jax.experimental import pallas as pl
from jax.experimental.pallas import tpu as pltpu
from jax.sharding import PartitionSpec as P

NSTEPS = 4
W = NSTEPS
PAD = 8

aniso_strength = 0.05


def pack_y_kernel(under, mobile, spread, phase_lo, phase_hi, solute_lo, solute_hi, to_prev, to_next):
    edge = phase_lo.shape[2]
    to_prev[:edge, :W, :] = phase_lo[0, 0, :, :W, :]
    to_prev[:edge, W:, :] = solute_lo[0, 0, :, :W, :]
    to_next[:edge, :W, :] = phase_hi[0, 0, :, W:, :]
    to_next[:edge, W:, :] = solute_hi[0, 0, :, W:, :]
    to_prev[edge] = jnp.zeros((2 * W, to_prev.shape[2]), jnp.float32)
    to_next[edge] = jnp.zeros((2 * W, to_prev.shape[2]), jnp.float32)
    for kind, own in enumerate((under, mobile, spread)):
        to_prev[edge, kind, :] = jnp.full((to_prev.shape[2],), own[0, 0], jnp.float32)
        to_next[edge, kind, :] = jnp.full((to_prev.shape[2],), own[0, own.shape[1] - 1], jnp.float32)


def pack_y(phase, solute, coef):
    _, tiles, edge, _, depth = phase.shape
    low = pl.BlockSpec((1, 1, edge, 2 * W, depth), lambda i: (0, 0, 0, 0, 0))
    high = pl.BlockSpec((1, 1, edge, 2 * W, depth), lambda i: (0, tiles - 1, 0, edge // (2 * W) - 1, 0))
    out = jax.ShapeDtypeStruct((edge + 1, 2 * W, depth), jnp.float32)
    whole = pl.BlockSpec((edge + 1, 2 * W, depth), lambda i: (0, 0, 0))
    return pl.pallas_call(
        pack_y_kernel,
        grid=(1,),
        in_specs=[pl.BlockSpec(memory_space=pltpu.SMEM)] * 3 + [low, high, low, high],
        out_specs=[whole, whole],
        out_shape=[out, out],
        name="pack_y",
    )(*coef, phase, phase, solute, solute)


def pack_x_kernel(under, mobile, spread, phase_lo, phase_hi, solute_lo, solute_hi, y_lo, y_hi, _, to_prev, to_next):
    tiles, edge, depth = phase_lo.shape[1], phase_lo.shape[3], phase_lo.shape[4]
    width = tiles * edge + 2 * W
    for out, phase, solute, first in (
        (to_prev, phase_lo, solute_lo, 0),
        (to_next, phase_hi, solute_hi, edge - W),
    ):
        for row in range(W):
            for field, values, half in ((0, phase, 0), (1, solute, W)):
                at = (2 * row + field) * width
                out[at : at + W, :] = y_lo[first + row, half : half + W, :]
                for tile in range(tiles):
                    begin = at + W + tile * edge
                    out[begin : begin + edge, :] = values[0, tile, row]
                out[at + width - W : at + width, :] = y_hi[first + row, half : half + W, :]
        at = 2 * W * width
        out[at : at + 8, :] = y_lo[edge]
        out[at + 8 : at + 16, :] = y_hi[edge]
        for tile in range(tiles):
            begin = at + 16 + 8 * tile
            out[begin : begin + 8, :] = jnp.zeros((8, depth), jnp.float32)
            for kind, own in enumerate((under, mobile, spread)):
                out[begin + kind : begin + kind + 1, :] = jnp.full((1, depth), own[0, tile], jnp.float32)


def pack_x(phase, solute, coef, y_lo, y_hi, after):
    _, tiles, edge, _, depth = phase.shape
    low = pl.BlockSpec((1, tiles, W, edge, depth), lambda i: (0, 0, 0, 0, 0))
    high = pl.BlockSpec((1, tiles, W, edge, depth), lambda i: (0, 0, edge // W - 1, 0, 0))
    side = pl.BlockSpec((edge + 1, 2 * W, depth), lambda i: (0, 0, 0))
    rows = 2 * W * (tiles * edge + 2 * W) + 8 * (tiles + 2)
    out = jax.ShapeDtypeStruct((rows, depth), jnp.float32)
    whole = pl.BlockSpec((rows, depth), lambda i: (0, 0))
    return pl.pallas_call(
        pack_x_kernel,
        grid=(1,),
        in_specs=[pl.BlockSpec(memory_space=pltpu.SMEM)] * 3 + [low, high, low, high, side, side, pl.BlockSpec(memory_space=pl.ANY)],
        out_specs=[whole, whole],
        out_shape=[out, out],
        name="pack_x",
    )(*coef, phase, phase, solute, solute, y_lo, y_hi, after)


def update(near_p, near_u, under, mobile, spread):
    p, p_xl, p_xh, p_yl, p_yh = near_p
    u, u_xl, u_xh, u_yl, u_yh = near_u
    depth = p.shape[-1]
    lane = lax.broadcasted_iota(jnp.int32, p.shape, 1)
    first, last = lane == 0, lane == depth - 1
    p_zl = jnp.where(first, p, pltpu.roll(p, 1, 1))
    p_zh = jnp.where(last, p, pltpu.roll(p, depth - 1, 1))
    u_zl = jnp.where(first, u, pltpu.roll(u, 1, 1))
    u_zh = jnp.where(last, u, pltpu.roll(u, depth - 1, 1))
    dx, dy, dz = p_xh - p_xl, p_yh - p_yl, p_zh - p_zl
    qx, qy, qz = dx * dx, dy * dy, dz * dz
    total = qx + qy + qz
    fourth = qx * qx + qy * qy + qz * qz
    base = total + 4.0
    guess = pl.reciprocal(base, approx=True)
    inverse = guess * (2.0 - base * guess)
    extra = (4.0 * aniso_strength * fourth - (3.0 * aniso_strength) * total * total) * (inverse * inverse)
    lap_p = (p_xl + p_xh) + (p_yl + p_yh) + (p_zl + p_zh) - 6.0 * p
    lap_u = (u_xl + u_xh) + (u_yl + u_yh) + (u_zl + u_zh) - 6.0 * u
    well = 1.0 - p * p
    drive = well * (under + u)
    change = mobile * (lap_p + extra * lap_p + well * (p - 2.0 * drive))
    return p + change, u + spread * lap_u + 0.5 * change


class Plan:
    def __init__(self, pieces, tiles, edge, depth):
        self.pieces, self.tiles, self.edge, self.depth = pieces, tiles, edge, depth
        self.half = pieces // 2
        self.inner = (edge - 2 * W) // pieces * pieces
        self.low = (edge - self.inner) // 2
        self.rows_a = self.inner // pieces
        self.rows_b = (edge - self.inner) // pieces
        self.cols_a = edge - 8
        self.size_a = self.rows_a * self.cols_a
        self.size_b = self.rows_b * edge + self.rows_a * 8
        self.size = self.size_a + self.size_b


AUX = 8


def cells(src_p, src_u, row, start, coefs):
    near = []
    for src in (src_p, src_u):
        near.append(
            (
                src[row, start : start + 8, :],
                src[row - 1, start : start + 8, :],
                src[row + 1, start : start + 8, :],
                src[row, start - 1 : start + 7, :],
                src[row, start + 1 : start + 9, :],
            )
        )
    return update(near[0], near[1], *coefs)


UNROLL = 4


def march(first, last, starts, source, target, coefs_of):
    def one_row(row, carry):
        for start in starts:
            new_p, new_u = cells(source[0], source[1], row, start, coefs_of(row, start))
            target[0][row, start : start + 8, :] = new_p
            target[1][row, start : start + 8, :] = new_u
        return carry

    lax.fori_loop(first, last, one_row, 0, unroll=UNROLL)


def inner_kernel(plan, under, mobile, spread, owner, phase, solute, *rest):
    tiles, edge, depth, pieces = plan.tiles, plan.edge, plan.depth, plan.pieces
    outs, fields = rest[:pieces], rest[pieces:]
    pairs = [fields[2 * NSTEPS - 2 : 2 * NSTEPS]]
    pairs += [fields[2 * step : 2 * step + 2] for step in range(NSTEPS - 1)]
    pairs += [fields[2 * NSTEPS :]]
    me = lax.axis_index("gy")

    def load_row(row, carry):
        for tile in range(tiles):
            start = PAD + tile * edge
            pairs[0][0][row, start : start + edge, :] = phase[0, tile, row]
            pairs[0][1][row, start : start + edge, :] = solute[0, tile, row]
        return carry

    lax.fori_loop(plan.low - W, edge - plan.low + W, load_row, 0, unroll=UNROLL)

    def coefs_of(row, start):
        tile = (start - PAD) // edge
        return under[0, tile], mobile[0, tile], spread[0, tile]

    for step in range(NSTEPS):
        margin = plan.low - W + step + 1
        starts = range(PAD, PAD + tiles * edge, 8)
        march(margin, edge - margin, starts, pairs[step], pairs[step + 1], coefs_of)
    lane = lax.broadcasted_iota(jnp.int32, (AUX, depth), 1)
    names = jnp.zeros((AUX, depth), jnp.float32)
    for tile in range(tiles):
        names = jnp.where(lane == tile, owner[0, tile].astype(jnp.float32), names)
    for mask, out in enumerate(outs):
        piece = me ^ mask
        for tile in range(tiles):
            start = PAD + tile * edge + (8 if tile == 0 else 0)
            for field, done in enumerate(pairs[-1]):
                for row in range(plan.rows_a):
                    at = (2 * tile + field) * plan.size_a + row * plan.cols_a
                    out[at : at + plan.cols_a, :] = done[
                        plan.low + piece * plan.rows_a + row, start : start + plan.cols_a, :
                    ]
        at = 2 * tiles * plan.size_a
        out[at : at + AUX, :] = names


def run_inner(plan, coef, owner, phase, solute):
    shape = (plan.edge, plan.tiles * plan.edge + 2 * PAD, plan.depth)
    vmem = pl.BlockSpec(memory_space=pltpu.VMEM)
    smem = pl.BlockSpec(memory_space=pltpu.SMEM)
    piece = jax.ShapeDtypeStruct((2 * plan.tiles * plan.size_a + AUX, plan.depth), jnp.float32)
    kept = 2 * (NSTEPS - 1)
    results = pl.pallas_call(
        functools.partial(inner_kernel, plan),
        in_specs=[smem] * 4 + [vmem] * 2,
        out_specs=[vmem] * (plan.pieces + kept),
        out_shape=[piece] * plan.pieces + [jax.ShapeDtypeStruct(shape, jnp.float32)] * kept,
        scratch_shapes=[pltpu.VMEM(shape, jnp.float32)] * 4,
        compiler_params=pltpu.CompilerParams(vmem_limit_bytes=40 * 1024 * 1024),
        cost_estimate=pl.CostEstimate(flops=10**8, bytes_accessed=24 * 1024 * 1024, transcendentals=0),
        name="inner",
    )(*coef, owner, phase, solute)
    return results[: plan.pieces], results[plan.pieces :]


def ring_kernel(plan, under, mobile, spread, phase, solute, y_lo, y_hi, x_lo, x_hi, *rest):
    tiles, edge, depth, pieces, low = plan.tiles, plan.edge, plan.depth, plan.pieces, plan.low
    kept = 2 * (NSTEPS - 1)
    fields, outs, scratch = rest[:kept], rest[kept : kept + pieces], rest[kept + pieces :]
    pairs, coefs = [scratch[2 * step : 2 * step + 2] for step in range(NSTEPS + 1)], scratch[-1]
    cols = tiles * edge
    width = cols + 2 * W
    own = 2 * PAD
    me = lax.axis_index("gy")
    for zone, source in ((0, x_lo), (1, None), (2, x_hi)):
        for kind, here in enumerate((under, mobile, spread)):
            if source is None:
                parts = [y_lo[edge, kind : kind + 1, :]]
                parts += [jnp.full((1, depth), here[0, tile], jnp.float32) for tile in range(tiles)]
                parts += [y_hi[edge, kind : kind + 1, :]]
            else:
                at = 2 * W * width + kind
                parts = [source[at : at + 1, :]]
                parts += [source[at + 16 + 8 * tile : at + 17 + 8 * tile, :] for tile in range(tiles)]
                parts += [source[at + 8 : at + 9, :]]
            coefs[zone, kind, :8, :] = jnp.broadcast_to(parts[0], (8, depth))
            for tile in range(tiles):
                begin = 8 + tile * edge
                coefs[zone, kind, begin : begin + edge, :] = jnp.broadcast_to(parts[1 + tile], (edge, depth))
            coefs[zone, kind, 8 + cols :, :] = jnp.broadcast_to(parts[-1], (8, depth))
    for source, first in ((x_lo, 0), (x_hi, edge + W)):
        for row in range(W):
            for field in range(2):
                at = (2 * row + field) * width
                pairs[0][field][first + row, own - W : own + cols + W, :] = source[at : at + width, :]

    def load_sides(row, carry):
        for field, values in ((0, phase), (1, solute)):
            buffer = pairs[0][field]
            half = field * W
            buffer[W + row, own - W : own, :] = y_lo[row, half : half + W, :]
            buffer[W + row, own + cols : own + cols + W, :] = y_hi[row, half : half + W, :]
            buffer[W + row, own : own + 16, :] = values[0, 0, row, :16, :]
            buffer[W + row, own + cols - 16 : own + cols, :] = values[0, tiles - 1, row, edge - 16 :, :]
        return carry

    lax.fori_loop(0, edge, load_sides, 0, unroll=UNROLL)
    for row in list(range(low - 2)) + list(range(edge - low + 2, edge)):
        for field, values in ((0, phase), (1, solute)):
            for tile in range(tiles):
                start = own + tile * edge
                pairs[0][field][W + row, start : start + edge, :] = values[0, tile, row]
    for step in range(1, NSTEPS):
        margin = low - W + step
        for field in range(2):
            kept_field, buffer = fields[2 * (step - 1) + field], pairs[step][field]
            for row in (margin, margin + 1, edge - margin - 2, edge - margin - 1):
                buffer[W + row, own + 8 : own + cols - 8, :] = kept_field[row, PAD + 8 : PAD + cols - 8, :]

            def copy_sides(row, carry, kept_field=kept_field, buffer=buffer):
                for start in (8, cols - 16):
                    buffer[W + row, own + start : own + start + 8, :] = kept_field[
                        row, PAD + start : PAD + start + 8, :
                    ]
                return carry

            lax.fori_loop(margin, edge - margin, copy_sides, 0, unroll=UNROLL)

    def coefs_of(zone):
        def found(row, start):
            return tuple(coefs[zone(row), kind, start - PAD : start - PAD + 8, :] for kind in range(3))

        return found

    any_zone = coefs_of(lambda row: jnp.where(row < W, 0, jnp.where(row < W + edge, 1, 2)))
    own_zone = coefs_of(lambda row: 1)
    for step in range(1, NSTEPS + 1):
        source, target = pairs[step - 1], pairs[step]
        if step < NSTEPS:
            across = range(own - 8, own + cols + 8, 8)
            sides = (own - 8, own, own + cols - 8, own + cols)
        else:
            across, sides = range(own, own + cols, 8), (own, own + cols - 8)
        margin = low - W + step
        march(W - (W - step), W + margin, across, source, target, any_zone)
        march(W + edge - margin, W + edge + W - step, across, source, target, any_zone)
        march(W + margin, W + edge - margin, sides, source, target, own_zone)
    for mask, out in enumerate(outs):
        piece = me ^ mask
        for tile in range(tiles):
            start = own + tile * edge
            side = start if tile == 0 else start + plan.cols_a
            for field, done in enumerate(pairs[NSTEPS]):
                at = (2 * tile + field) * plan.size_b
                for row in range(plan.rows_b):
                    index = piece * plan.rows_b + row
                    x = W + index + jnp.where(index < low, 0, plan.inner)
                    out[at : at + edge, :] = done[x, start : start + edge, :]
                    at += edge
                for row in range(plan.rows_a):
                    x = W + low + piece * plan.rows_a + row
                    out[at : at + 8, :] = done[x, side : side + 8, :]
                    at += 8


def run_ring(plan, coef, phase, solute, halos, fields):
    cols = plan.tiles * plan.edge
    buffer = pltpu.VMEM((plan.edge + 2 * W, cols + 4 * PAD, plan.depth), jnp.float32)
    vmem = pl.BlockSpec(memory_space=pltpu.VMEM)
    smem = pl.BlockSpec(memory_space=pltpu.SMEM)
    piece = jax.ShapeDtypeStruct((2 * plan.tiles * plan.size_b, plan.depth), jnp.float32)
    return pl.pallas_call(
        functools.partial(ring_kernel, plan),
        in_specs=[smem] * 3 + [vmem] * (6 + len(fields)),
        out_specs=[vmem] * plan.pieces,
        out_shape=[piece] * plan.pieces,
        scratch_shapes=[buffer] * (2 * NSTEPS + 2) + [pltpu.VMEM((3, 3, cols + 16, plan.depth), jnp.float32)],
        compiler_params=pltpu.CompilerParams(vmem_limit_bytes=40 * 1024 * 1024),
        cost_estimate=pl.CostEstimate(flops=10**8, bytes_accessed=24 * 1024 * 1024, transcendentals=0),
        name="rest",
    )(*coef, phase, solute, *halos, *fields)


def table_kernel(plan, *refs):
    pieces, tiles = plan.pieces, plan.tiles
    arrived, (table, names, sems) = refs[:pieces], refs[pieces + 1 :]
    me = lax.axis_index("gy")
    copies = []
    for mask in range(pieces):
        tail = 2 * tiles * plan.size_a
        copy = pltpu.make_async_copy(arrived[mask].at[pl.ds(tail, 1), :], names.at[mask], sems.at[mask])
        copy.start()
        copies.append(copy)
    for copy in copies:
        copy.wait()
    peers, homes = [], []
    for mask in range(pieces):
        for tile in range(tiles):
            peers.append(lax.rem(names[mask, 0, tile].astype(jnp.int32), pieces))
            homes.append((me ^ mask) * tiles + tile)
    for index in range(pieces * tiles):
        slot = jnp.int32(0)
        for other in range(pieces * tiles):
            if other != index:
                ahead = (peers[other] == peers[index]) & (homes[other] < homes[index])
                slot = slot + ahead.astype(jnp.int32)
        table[(peers[index] ^ me) * tiles + slot] = index


def find_table(plan, arrived, after):
    pieces, tiles = plan.pieces, plan.tiles
    return pl.pallas_call(
        functools.partial(table_kernel, plan),
        in_specs=[pl.BlockSpec(memory_space=pl.ANY)] * (pieces + 1),
        out_specs=pl.BlockSpec(memory_space=pltpu.SMEM),
        out_shape=jax.ShapeDtypeStruct((pieces * tiles,), jnp.int32),
        scratch_shapes=[
            pltpu.SMEM((pieces, 1, plan.depth), jnp.float32),
            pltpu.SemaphoreType.DMA((pieces,)),
        ],
        name="table",
    )(*arrived, after)


def route_kernel(plan, size, aux, table, *refs):
    pieces, tiles = plan.pieces, plan.tiles
    arrived, outs, (held,) = refs[:pieces], refs[pieces : 2 * pieces], refs[2 * pieces :]
    for mask in range(pieces):
        for tile in range(tiles):
            held[mask * tiles + tile] = arrived[mask][tile * size : (tile + 1) * size, :]
    for mask in range(pieces):
        for slot in range(tiles):
            index = table[mask * tiles + slot]
            outs[mask][slot, :size, :] = held[index]
            if aux:
                side = lax.rem(index, tiles).astype(jnp.float32)
                outs[mask][slot, size : size + aux, :] = jnp.full((aux, plan.depth), side, jnp.float32)


def route(plan, size, aux, table, arrived):
    pieces, tiles, depth = plan.pieces, plan.tiles, plan.depth
    vmem = pl.BlockSpec(memory_space=pltpu.VMEM)
    return pl.pallas_call(
        functools.partial(route_kernel, plan, size, aux),
        in_specs=[pl.BlockSpec(memory_space=pltpu.SMEM)] + [vmem] * pieces,
        out_specs=[vmem] * pieces,
        out_shape=[jax.ShapeDtypeStruct((tiles, size + aux, depth), jnp.float32)] * pieces,
        scratch_shapes=[pltpu.VMEM((pieces * tiles, size, depth), jnp.float32)],
        compiler_params=pltpu.CompilerParams(vmem_limit_bytes=16 * 1024 * 1024),
        name="route",
    )(table, *arrived)


def settle_kernel(plan, *refs):
    pieces, tiles, edge, depth = plan.pieces, plan.tiles, plan.edge, plan.depth
    part_a, part_b, outs = refs[:pieces], refs[pieces : 2 * pieces], refs[2 * pieces :]
    me = lax.axis_index("gy")
    for mask in range(pieces):
        piece = me ^ mask
        for slot in range(tiles):
            last = part_a[mask][slot, 2 * plan.size_a : 2 * plan.size_a + 8, :] > 0.5
            for field, out in enumerate(outs):
                at = field * plan.size_b
                for row in range(plan.rows_b):
                    index = piece * plan.rows_b + row
                    x = index + jnp.where(index < plan.low, 0, plan.inner)
                    out[0, slot, x] = part_b[mask][slot, at : at + edge, :]
                    at += edge
                for row in range(plan.rows_a):
                    x = plan.low + piece * plan.rows_a + row
                    begin = field * plan.size_a + row * plan.cols_a
                    side = part_b[mask][slot, at : at + 8, :]
                    at += 8
                    blocks = [
                        part_a[mask][slot, begin + col : begin + col + 8, :] for col in range(0, plan.cols_a, 8)
                    ]
                    for index, (low, high) in enumerate(zip([side] + blocks, blocks + [side])):
                        out[0, slot, x, 8 * index : 8 * index + 8, :] = jnp.where(last, high, low)


def settle(plan, part_a, part_b):
    out = jax.ShapeDtypeStruct((1, plan.tiles, plan.edge, plan.edge, plan.depth), jnp.float32)
    vmem = pl.BlockSpec(memory_space=pltpu.VMEM)
    return pl.pallas_call(
        functools.partial(settle_kernel, plan),
        in_specs=[vmem] * (2 * plan.pieces),
        out_specs=[vmem, vmem],
        out_shape=[out, out],
        compiler_params=pltpu.CompilerParams(vmem_limit_bytes=16 * 1024 * 1024),
        name="settle",
    )(*part_a, *part_b)


def ring(axis, step):
    count = lax.axis_size(axis)
    return [(i, (i + step) % count) for i in range(count)]


def exchange(plan, values):
    moved = [values[0]] + [None] * (plan.pieces - 1)
    for mask in list(range(plan.half, plan.pieces)) + list(range(1, plan.half)):
        moved[mask] = lax.ppermute(values[mask], "gy", [(i, i ^ mask) for i in range(plan.pieces)])
    return moved


def per_device(phase, solute, undercool, mobility, diffusivity, owner):
    _, tiles, edge, _, depth = phase.shape
    plan = Plan(lax.axis_size("gy"), tiles, edge, depth)
    coef = (undercool, mobility, diffusivity)
    to_prev, to_next = pack_y(phase, solute, coef)
    y_lo = lax.ppermute(to_next, "gy", ring("gy", 1))
    y_hi = lax.ppermute(to_prev, "gy", ring("gy", -1))
    first, fields = run_inner(plan, coef, owner, phase, solute)
    part_a = exchange(plan, first)
    to_prev, to_next = pack_x(phase, solute, coef, y_lo, y_hi, fields[0])
    x_lo = lax.ppermute(to_next, "gx", ring("gx", 1))
    x_hi = lax.ppermute(to_prev, "gx", ring("gx", -1))
    second = run_ring(plan, coef, phase, solute, (y_lo, y_hi, x_lo, x_hi), fields)
    part_b = exchange(plan, second)
    table = find_table(plan, part_a, second[0])
    sent_a = exchange(plan, route(plan, 2 * plan.size_a, AUX, table, part_a))
    sent_b = exchange(plan, route(plan, 2 * plan.size_b, 0, table, part_b))
    return tuple(settle(plan, sent_a, sent_b))


def solution(mesh):
    tile_spec = P("gx", "gy", None, None, None)
    in_specs = (tile_spec, tile_spec) + (P("gx", "gy"),) * 4
    out_spec = P(("gx", "gy"), None, None, None, None)
    return jax.shard_map(
        per_device, mesh=mesh, in_specs=in_specs, out_specs=(out_spec, out_spec), check_vma=False
    )
```

time: 136 us -> 134 us (0.985)
  waiting for transfers between devices: 70.7 us -> 39.2 us
  local copies, waits for them, and re-layouts: 0.69 us -> 21 us
  starting transfers between devices: 29.4 us -> 45.4 us
  Pallas kernels: 34 us -> 27.2 us
    ppermute x18 -> x28, waiting for transfers between devices: 64.3 us -> 39.1 us  [exchange(): lax.ppermute(values[mask], 'gy', [(i, i ^ mask) for i in range(plan.piece...]
    unnamed x20 -> x88, local copies, waits for them, and re-layouts: 0.69 us -> 21 us
    ppermute x18 -> x28, starting transfers between devices: 24.7 us -> 40.8 us  [exchange(): lax.ppermute(values[mask], 'gy', [(i, i ^ mask) for i in range(plan.piece...]
    pallas_call x4 -> x6, Pallas kernels: 30.1 us -> 23 us  [the longest x1 8.94 us: run_inner(): pl.pallas_call(functools.partial(inner_kernel, plan), in_specs=[smem] * 4...]
    ppermute x1, waiting for transfers between devices: 4.65 us -> 0.01 us  [per_device(): y_lo = lax.ppermute(to_next, 'gy', ring('gy', 1))]
    ppermute x1, waiting for transfers between devices: 1.75 us -> 0.01 us  [per_device(): y_hi = lax.ppermute(to_prev, 'gy', ring('gy', -1))]
  transfers between devices with their start and end apart: 22 -> 32, of which waited for: 14 -> 10; matrix products, arithmetic and copies ran while one was open for 0% -> 0% of each run, Pallas kernels for 13% -> 16%
where the time goes in v3:
time: 134 us
  starting transfers between devices  45.4 us (34%)
  waiting for transfers between devices  39.2 us (29%)
  Pallas kernels  27.2 us (20%)
  local copies, waits for them, and re-layouts  21 us (16%)
    ppermute x28, starting transfers between devices, exchange(): lax.ppermute(values[mask], 'gy', [(i, i ^ mask) for i in range(plan.piece...  40.8 us
    ppermute x28, waiting for transfers between devices, exchange(): lax.ppermute(values[mask], 'gy', [(i, i ^ mask) for i in range(plan.piece...  39.1 us
    unnamed x88, local copies, waits for them, and re-layouts  21 us
    pallas_call x1, Pallas kernels, run_inner(): pl.pallas_call(functools.partial(inner_kernel, plan), in_specs=[smem] * 4...  8.94 us
    pallas_call x1, Pallas kernels, run_ring(): pl.pallas_call(functools.partial(ring_kernel, plan), in_specs=[smem] * 3...  8.7 us
  transfers between devices with their start and end apart: 32, of which 10 were waited for; matrix products, arithmetic and copies ran while one was open for 0% of the time, Pallas kernels for 16%

profile of v3, /device:TPU:8, one launch (start us, length us, event | category | flops | bytes accessed | tf_op | source)
XLA Modules:
  0.0 133.8 jit_solution(8680136115063295025)
XLA Ops:
  0.7 2.0 %pack_y.1 = (f32[33,8,128]{2,1,0:T(8,128)}, f32[33,8,128]{2,1,0:T(8,128)}) custom-call(f32[1,2]{1,0:T(1,128)} %under.7, f32[1,2]{1,0:T(1,128)} %mobile.7, f32[1,2]{1,0:T(1,128)} %spread.7, f32[1,2,32,32,128]{4,3,2,1,0:T(8,128)} %phase.3, f32[1,2,32,32,128]{4,3,2,1,0:T(8,128)} %phase.3, f32[1,2,32,32,128]{4,3,2,1,0:T(8,128)} %solute.3, ...), custom_call_target="tpu_custom_call" | custom-call | tf_op jit(solution)/shard_map/pack_y/pallas_call | solution.py:36
  2.7 1.5 %collective-permute-start.7 = (f32[33,8,128]{2,1,0:T(8,128)}, f32[33,8,128]{2,1,0:T(8,128)S(1)}, u32[]{:S(2)}, u32[]{:S(2)}) collective-permute-start(f32[33,8,128]{2,1,0:T(8,128)} %get-tuple-element.52), channel_id=1, source_target_pairs={{0,1},{1,2},{2,3},{3,4},{4,5},{5,6},{6,7},{7,0},{8,9},{9,10},{10,1... | collective-permute-start | bytes 405512 | tf_op jit(solution)/shard_map/ppermute | solution.py:468
  4.2 1.4 %collective-permute-start.8 = (f32[33,8,128]{2,1,0:T(8,128)}, f32[33,8,128]{2,1,0:T(8,128)S(1)}, u32[]{:S(2)}, u32[]{:S(2)}) collective-permute-start(f32[33,8,128]{2,1,0:T(8,128)} %get-tuple-element.53), channel_id=1, source_target_pairs={{0,7},{1,0},{2,1},{3,2},{4,3},{5,4},{6,5},{7,6},{8,15},{9,8},{10,9... | collective-permute-start | bytes 405512 | tf_op jit(solution)/shard_map/ppermute | solution.py:469
  5.7 8.9 %inner.1 = (f32[296,128]{1,0:T(8,128)S(1)}, f32[296,128]{1,0:T(8,128)S(1)}, f32[296,128]{1,0:T(8,128)S(1)}, f32[296,128]{1,0:T(8,128)S(1)}, f32[296,128]{1,0:T(8...) custom-call(f32[1,2]{1,0:T(1,128)S(1)} %copy-done.28, ...), custom_call_target="tpu_custom_call" | custom-call | flops 100000000 | bytes 25165824 | tf_op jit(solution)/shard_map/inner/pallas_call | solution.py:210
  14.6 1.1 copy-done.4
  15.7 1.1 copy-done.6
  16.8 1.1 copy-done.8
  17.9 1.1 copy-done.10
  19.0 1.1 copy-done.12
  20.0 1.2 copy-done.14
  21.2 0.7 copy-done.16
  21.8 0.7 copy-done.41
  22.5 0.7 copy-done.42
  23.2 0.7 copy-done.43
  23.9 0.6 copy-done.37
  24.7 0.6 copy-done.24
  25.4 2.2 %pack_x.1 = (f32[608,128]{1,0:T(8,128)}, f32[608,128]{1,0:T(8,128)}) custom-call(f32[1,2]{1,0:T(1,128)} %under.7, f32[1,2]{1,0:T(1,128)} %mobile.7, f32[1,2]{1,0:T(1,128)} %spread.7, f32[1,2,32,32,128]{4,3,2,1,0:T(8,128)} %phase.3, f32[1,2,32,32,128]{4,3,2,1,0:T(8,128)} %phase.3, f32[1,2,32,32,128]{4,3,2,1,0:T(8,128)} %solute.3, ...), custom_call_target="tpu_custom_call" | custom-call | tf_op jit(solution)/shard_map/pack_x/pallas_call | solution.py:79
  27.6 1.7 %collective-permute-start.10 = (f32[608,128]{1,0:T(8,128)}, f32[608,128]{1,0:T(8,128)S(1)}, u32[]{:S(2)}, u32[]{:S(2)}) collective-permute-start(f32[608,128]{1,0:T(8,128)} %get-tuple-element.56), channel_id=1, source_target_pairs={{0,24},{8,0},{16,8},{24,16},{1,25},{9,1},{17,9},{25,17},{2,26},{10... | collective-permute-start | bytes 933896 | tf_op jit(solution)/shard_map/ppermute | solution.py:474
  29.3 0.6 collective-permute-start
  29.9 1.5 %collective-permute-start.1 = (f32[296,128]{1,0:T(8,128)}, f32[296,128]{1,0:T(8,128)S(1)}, u32[]{:S(2)}, u32[]{:S(2)}) collective-permute-start(f32[296,128]{1,0:T(8,128)} %copy-done.42), channel_id=1, source_target_pairs={{0,2},{1,3},{2,0},{3,1},{4,6},{5,7},{6,4},{7,5},{8,10},{9,11},{10,... | collective-permute-start | bytes 454664 | tf_op jit(solution)/shard_map/ppermute | solution.py:459
  31.4 1.5 %collective-permute-start.2 = (f32[296,128]{1,0:T(8,128)}, f32[296,128]{1,0:T(8,128)}, u32[]{:S(2)}, u32[]{:S(2)}) collective-permute-start(f32[296,128]{1,0:T(8,128)} %copy-done.41), channel_id=1, source_target_pairs={{0,3},{1,2},{2,1},{3,0},{4,7},{5,6},{6,5},{7,4},{8,11},{9,10},{10,... | collective-permute-start | bytes 454664 | tf_op jit(solution)/shard_map/ppermute | solution.py:459
  32.9 2.4 %collective-permute-done.refs_1_ = f32[296,128]{1,0:T(8,128)S(1)} collective-permute-done((f32[296,128]{1,0:T(8,128)}, f32[296,128]{1,0:T(8,128)S(1)}, u32[]{:S(2)}, u32[]{:S(2)}) %collective-permute-start) | collective-permute-done | bytes 151584 | tf_op jit(solution)/shard_map/ppermute | solution.py:459
  35.2 2.8 %collective-permute-start.3 = (f32[296,128]{1,0:T(8,128)}, f32[296,128]{1,0:T(8,128)}, u32[]{:S(2)}, u32[]{:S(2)}) collective-permute-start(f32[296,128]{1,0:T(8,128)} %copy-done.40), channel_id=1, source_target_pairs={{0,4},{1,5},{2,6},{3,7},{4,0},{5,1},{6,2},{7,3},{8,12},{9,13},{10,... | collective-permute-start | bytes 454664 | tf_op jit(solution)/shard_map/ppermute | solution.py:459
  38.1 2.4 %collective-permute-start.4 = (f32[296,128]{1,0:T(8,128)}, f32[296,128]{1,0:T(8,128)}, u32[]{:S(2)}, u32[]{:S(2)}) collective-permute-start(f32[296,128]{1,0:T(8,128)} %copy-done.39), channel_id=1, source_target_pairs={{0,5},{1,4},{2,7},{3,6},{4,1},{5,0},{6,3},{7,2},{8,13},{9,12},{10,... | collective-permute-start | bytes 454664 | tf_op jit(solution)/shard_map/ppermute | solution.py:459
  40.4 0.9 collective-permute-start.5
  41.4 1.1 collective-permute-start.6
  42.6 1.3 copy-done.7
  43.9 1.3 copy-done.9
  45.2 1.3 copy-done.11
  46.5 1.3 copy-done.13
  47.9 1.3 copy-done.15
  49.2 0.9 copy-done.23
  50.1 0.9 copy-done.25
  51.0 8.7 %rest.1 = (f32[224,128]{1,0:T(8,128)S(1)}, f32[224,128]{1,0:T(8,128)S(1)}, f32[224,128]{1,0:T(8,128)}, f32[224,128]{1,0:T(8,128)}, f32[224,128]{1,0:T(8,128)}, /...) custom-call(f32[1,2]{1,0:T(1,128)S(1)} %copy-done.29, f32[1,2]{1,0:T(1,128)S(1)} %copy-done.31, ...), custom_call_target="tpu_custom_call" | custom-call | flops 100000000 | bytes 25165824 | tf_op jit(solution)/shard_map/rest/pallas_call | solution.py:329
  59.7 0.6 copy-done.26
  60.4 1.5 %collective-permute-start.18 = (f32[224,128]{1,0:T(8,128)S(1)}, f32[224,128]{1,0:T(8,128)S(1)}, u32[]{:S(2)}, u32[]{:S(2)}) collective-permute-start(f32[224,128]{1,0:T(8,128)S(1)} %get-tuple-element.71), channel_id=1, source_target_pairs={{0,1},{1,0},{2,3},{3,2},{4,5},{5,4},{6,7},{7,6},{8,9},{9,8},{10,11... | collective-permute-start | bytes 344072 | tf_op jit(solution)/shard_map/ppermute | solution.py:459
  61.8 2.2 %collective-permute-start.19 = (f32[224,128]{1,0:T(8,128)}, f32[224,128]{1,0:T(8,128)S(1)}, u32[]{:S(2)}, u32[]{:S(2)}) collective-permute-start(f32[224,128]{1,0:T(8,128)} %get-tuple-element.72), channel_id=1, source_target_pairs={{0,2},{1,3},{2,0},{3,1},{4,6},{5,7},{6,4},{7,5},{8,10},{9,11},{10,... | collective-permute-start | bytes 344072 | tf_op jit(solution)/shard_map/ppermute | solution.py:459
  64.6 2.5 %collective-permute-start.21 = (f32[224,128]{1,0:T(8,128)}, f32[224,128]{1,0:T(8,128)S(1)}, u32[]{:S(2)}, u32[]{:S(2)}) collective-permute-start(f32[224,128]{1,0:T(8,128)} %get-tuple-element.74), channel_id=1, source_target_pairs={{0,4},{1,5},{2,6},{3,7},{4,0},{5,1},{6,2},{7,3},{8,12},{9,13},{10,... | collective-permute-start | bytes 344072 | tf_op jit(solution)/shard_map/ppermute | solution.py:459
  67.1 0.9 collective-permute-start.22
  68.0 0.7 collective-permute-start.23
  68.7 1.8 %table.1 = s32[16]{0:T(128)} custom-call(f32[296,128]{1,0:T(8,128)} %copy-done.16, f32[296,128]{1,0:T(8,128)} %copy-done.18, f32[296,128]{1,0:T(8,128)} %copy-done.20, f32[296,128]{1,0:T(8,128)} %collective-permute-done.2.refs_3_, f32[296,128]{1,0:T(8,128)} %collective-permute-done.3.refs_4_, f32[296,128]{1,0:T(8,128)} %collective-permute-done.4.refs_5_, ...), custom_call_target="tpu_custom_call" | custom-call | tf_op jit(solution)/shard_map/table/pallas_call | solution.py:369
  70.6 0.6 copy-done.34
  71.2 1.4 %route.2 = (f32[2,152,128]{2,1,0:T(8,128)S(1)}, f32[2,152,128]{2,1,0:T(8,128)S(1)}, f32[2,152,128]{2,1,0:T(8,128)S(1)}, f32[2,152,128]{2,1,0:T(8,128)S(1)}, f32[...) custom-call(s32[16]{0:T(128)S(1)} %copy-done.34, ...), custom_call_target="tpu_custom_call" | custom-call | tf_op jit(solution)/shard_map/route/pallas_call | solution.py:400
  72.6 1.5 %collective-permute-start.11 = (f32[2,152,128]{2,1,0:T(8,128)S(1)}, f32[2,152,128]{2,1,0:T(8,128)S(1)}, u32[]{:S(2)}, u32[]{:S(2)}) collective-permute-start(f32[2,152,128]{2,1,0:T(8,128)S(1)} %get-tuple-element.64), channel_id=1, source_target_pairs={{0,1},{1,0},{2,3},{3,2},{4,5},{5,4},{6,7},{7,6},{8,9},{9,8},{10,11... | collective-permute-start | bytes 466952 | tf_op jit(solution)/shard_map/ppermute | solution.py:459
  74.1 2.9 %collective-permute-start.12 = (f32[2,152,128]{2,1,0:T(8,128)S(1)}, f32[2,152,128]{2,1,0:T(8,128)S(1)}, u32[]{:S(2)}, u32[]{:S(2)}) collective-permute-start(f32[2,152,128]{2,1,0:T(8,128)S(1)} %get-tuple-element.65), channel_id=1, source_target_pairs={{0,2},{1,3},{2,0},{3,1},{4,6},{5,7},{6,4},{7,5},{8,10},{9,11},{10,... | collective-permute-start | bytes 466952 | tf_op jit(solution)/shard_map/ppermute | solution.py:459
  77.0 1.4 %collective-permute-start.24 = (f32[224,128]{1,0:T(8,128)S(1)}, f32[224,128]{1,0:T(8,128)S(1)}, u32[]{:S(2)}, u32[]{:S(2)}) collective-permute-start(f32[224,128]{1,0:T(8,128)S(1)} %get-tuple-element.77), channel_id=1, source_target_pairs={{0,7},{1,6},{2,5},{3,4},{4,3},{5,2},{6,1},{7,0},{8,15},{9,14},{10,... | collective-permute-start | bytes 344072 | tf_op jit(solution)/shard_map/ppermute | solution.py:459
  78.3 2.0 %collective-permute-done.22.refs_5_ = f32[224,128]{1,0:T(8,128)S(1)} collective-permute-done((f32[224,128]{1,0:T(8,128)}, f32[224,128]{1,0:T(8,128)S(1)}, u32[]{:S(2)}, u32[]{:S(2)}) %collective-permute-start.22) | collective-permute-done | bytes 114720 | tf_op jit(solution)/shard_map/ppermute | solution.py:459
  80.3 3.5 %collective-permute-start.13 = (f32[2,152,128]{2,1,0:T(8,128)S(1)}, f32[2,152,128]{2,1,0:T(8,128)S(1)}, u32[]{:S(2)}, u32[]{:S(2)}) collective-permute-start(f32[2,152,128]{2,1,0:T(8,128)S(1)} %get-tuple-element.66), channel_id=1, source_target_pairs={{0,3},{1,2},{2,1},{3,0},{4,7},{5,6},{6,5},{7,4},{8,11},{9,10},{10,... | collective-permute-start | bytes 466952 | tf_op jit(solution)/shard_map/ppermute | solution.py:459
  83.9 3.1 %collective-permute-done.23.refs_6_ = f32[224,128]{1,0:T(8,128)S(1)} collective-permute-done((f32[224,128]{1,0:T(8,128)}, f32[224,128]{1,0:T(8,128)S(1)}, u32[]{:S(2)}, u32[]{:S(2)}) %collective-permute-start.23) | collective-permute-done | bytes 114720 | tf_op jit(solution)/shard_map/ppermute | solution.py:459
  87.0 9.4 %collective-permute-done.24.refs_7_ = f32[224,128]{1,0:T(8,128)S(1)} collective-permute-done((f32[224,128]{1,0:T(8,128)S(1)}, f32[224,128]{1,0:T(8,128)S(1)}, u32[]{:S(2)}, u32[]{:S(2)}) %collective-permute-start.24) | collective-permute-done | bytes 114720 | tf_op jit(solution)/shard_map/ppermute | solution.py:459
  96.4 0.9 collective-permute-start.16
  97.3 1.6 %collective-permute-start.17 = (f32[2,152,128]{2,1,0:T(8,128)S(1)}, f32[2,152,128]{2,1,0:T(8,128)S(1)}, u32[]{:S(2)}, u32[]{:S(2)}) collective-permute-start(f32[2,152,128]{2,1,0:T(8,128)S(1)} %get-tuple-element.70), channel_id=1, source_target_pairs={{0,7},{1,6},{2,5},{3,4},{4,3},{5,2},{6,1},{7,0},{8,15},{9,14},{10,... | collective-permute-start | bytes 466952 | tf_op jit(solution)/shard_map/ppermute | solution.py:459
  98.9 0.6 copy-done.35
  99.6 0.7 route.3
  100.2 1.1 collective-permute-start.25
  101.3 4.6 %collective-permute-start.26 = (f32[2,112,128]{2,1,0:T(8,128)S(1)}, f32[2,112,128]{2,1,0:T(8,128)S(1)}, u32[]{:S(2)}, u32[]{:S(2)}) collective-permute-start(f32[2,112,128]{2,1,0:T(8,128)S(1)} %get-tuple-element.80), channel_id=1, source_target_pairs={{0,2},{1,3},{2,0},{3,1},{4,6},{5,7},{6,4},{7,5},{8,10},{9,11},{10,... | collective-permute-start | bytes 344072 | tf_op jit(solution)/shard_map/ppermute | solution.py:459
  105.9 4.1 %collective-permute-start.27 = (f32[2,112,128]{2,1,0:T(8,128)S(1)}, f32[2,112,128]{2,1,0:T(8,128)S(1)}, u32[]{:S(2)}, u32[]{:S(2)}) collective-permute-start(f32[2,112,128]{2,1,0:T(8,128)S(1)} %get-tuple-element.81), channel_id=1, source_target_pairs={{0,3},{1,2},{2,1},{3,0},{4,7},{5,6},{6,5},{7,4},{8,11},{9,10},{10,... | collective-permute-start | bytes 344072 | tf_op jit(solution)/shard_map/ppermute | solution.py:459
  110.0 2.2 %collective-permute-done.16.refs_6_ = f32[2,152,128]{2,1,0:T(8,128)S(1)} collective-permute-done((f32[2,152,128]{2,1,0:T(8,128)S(1)}, f32[2,152,128]{2,1,0:T(8,128)S(1)}, u32[]{:S(2)}, u32[]{:S(2)}) %collective-permute-start.16) | collective-permute-done | bytes 155680 | tf_op jit(solution)/shard_map/ppermute | solution.py:459
  112.2 7.7 %collective-permute-done.17.refs_7_ = f32[2,152,128]{2,1,0:T(8,128)S(1)} collective-permute-done((f32[2,152,128]{2,1,0:T(8,128)S(1)}, f32[2,152,128]{2,1,0:T(8,128)S(1)}, u32[]{:S(2)}, u32[]{:S(2)}) %collective-permute-start.17) | collective-permute-done | bytes 155680 | tf_op jit(solution)/shard_map/ppermute | solution.py:459
  120.0 3.7 %collective-permute-done.28.refs_12_ = f32[2,112,128]{2,1,0:T(8,128)S(1)} collective-permute-done((f32[2,112,128]{2,1,0:T(8,128)S(1)}, f32[2,112,128]{2,1,0:T(8,128)S(1)}, u32[]{:S(2)}, u32[]{:S(2)}) %collective-permute-start.28) | collective-permute-done | bytes 114720 | tf_op jit(solution)/shard_map/ppermute | solution.py:459
  123.8 2.8 %collective-permute-done.29.refs_13_ = f32[2,112,128]{2,1,0:T(8,128)S(1)} collective-permute-done((f32[2,112,128]{2,1,0:T(8,128)S(1)}, f32[2,112,128]{2,1,0:T(8,128)S(1)}, u32[]{:S(2)}, u32[]{:S(2)}) %collective-permute-start.29) | collective-permute-done | bytes 114720 | tf_op jit(solution)/shard_map/ppermute | solution.py:459
  126.6 4.2 %collective-permute-done.30.refs_14_ = f32[2,112,128]{2,1,0:T(8,128)S(1)} collective-permute-done((f32[2,112,128]{2,1,0:T(8,128)S(1)}, f32[2,112,128]{2,1,0:T(8,128)S(1)}, u32[]{:S(2)}, u32[]{:S(2)}) %collective-permute-start.30) | collective-permute-done | bytes 114720 | tf_op jit(solution)/shard_map/ppermute | solution.py:459
  130.8 1.6 %collective-permute-done.31.refs_15_ = f32[2,112,128]{2,1,0:T(8,128)S(1)} collective-permute-done((f32[2,112,128]{2,1,0:T(8,128)S(1)}, f32[2,112,128]{2,1,0:T(8,128)S(1)}, u32[]{:S(2)}, u32[]{:S(2)}) %collective-permute-start.31) | collective-permute-done | bytes 114720 | tf_op jit(solution)/shard_map/ppermute | solution.py:459
  132.3 1.5 %settle.1 = (f32[1,2,32,32,128]{4,3,2,1,0:T(8,128)}, f32[1,2,32,32,128]{4,3,2,1,0:T(8,128)}) custom-call(f32[2,152,128]{2,1,0:T(8,128)S(1)} %get-tuple-element.63.refs_0_, f32[2,152,128]{2,1,0:T(8,128)S(1)} %collective-permute-done.11.refs_1_, f32[2,152,128]{2,1,0:T(8,128)S(1)} %collective-permute-done.12.refs_2_, ...), custom_call_target="tpu_custom_call" | custom-call | tf_op jit(solution)/shard_map/settle/pallas_call | solution.py:441
  (96 shorter events, 1.0 us)
Async XLA Ops:
  0.6 5.0 %copy-start.32 = (f32[1,2]{1,0:T(1,128)S(1)}, f32[1,2]{1,0:T(1,128)}, u32[]{:S(2)}) copy-start(f32[1,2]{1,0:T(1,128)} %spread.7) | copy-start | bytes 28
  0.6 5.0 %copy-start.30 = (f32[1,2]{1,0:T(1,128)S(1)}, f32[1,2]{1,0:T(1,128)}, u32[]{:S(2)}) copy-start(f32[1,2]{1,0:T(1,128)} %mobile.7) | copy-start | bytes 28
  0.7 5.0 %copy-start.28 = (f32[1,2]{1,0:T(1,128)S(1)}, f32[1,2]{1,0:T(1,128)}, u32[]{:S(2)}) copy-start(f32[1,2]{1,0:T(1,128)} %under.7) | copy-start | bytes 28
  0.7 5.0 %copy-start.2 = (f32[1,2,32,32,128]{4,3,2,1,0:T(8,128)S(1)}, f32[1,2,32,32,128]{4,3,2,1,0:T(8,128)}, u32[]{:S(2)}) copy-start(f32[1,2,32,32,128]{4,3,2,1,0:T(8,128)} %solute.3) | copy-start | bytes 3145732
  0.7 5.0 %copy-start = (f32[1,2,32,32,128]{4,3,2,1,0:T(8,128)S(1)}, f32[1,2,32,32,128]{4,3,2,1,0:T(8,128)}, u32[]{:S(2)}) copy-start(f32[1,2,32,32,128]{4,3,2,1,0:T(8,128)} %phase.3) | copy-start | bytes 3145732
  0.7 5.0 %copy-start.36 = (s32[1,2]{1,0:T(1,128)S(1)}, s32[1,2]{1,0:T(1,128)}, u32[]{:S(2)}) copy-start(s32[1,2]{1,0:T(1,128)} %owner.1) | copy-start | bytes 28
  2.7 21.1 %collective-permute-start.7 = (f32[33,8,128]{2,1,0:T(8,128)}, f32[33,8,128]{2,1,0:T(8,128)S(1)}, u32[]{:S(2)}, u32[]{:S(2)}) collective-permute-start(f32[33,8,128]{2,1,0:T(8,128)} %get-tuple-element.52), channel_id=1, source_target_pairs={{0,1},{1,2},{2,3},{3,4},{4,5},{5,6},{6,7},{7,0},{8,9},{9,10},{10,1... | collective-permute-start | bytes 405512 | tf_op jit(solution)/shard_map/ppermute | solution.py:468
  4.2 19.6 %collective-permute-start.8 = (f32[33,8,128]{2,1,0:T(8,128)}, f32[33,8,128]{2,1,0:T(8,128)S(1)}, u32[]{:S(2)}, u32[]{:S(2)}) collective-permute-start(f32[33,8,128]{2,1,0:T(8,128)} %get-tuple-element.53), channel_id=1, source_target_pairs={{0,7},{1,0},{2,1},{3,2},{4,3},{5,4},{6,5},{7,6},{8,15},{9,8},{10,9... | collective-permute-start | bytes 405512 | tf_op jit(solution)/shard_map/ppermute | solution.py:469
  14.6 1.1 copy-start.4
  15.7 1.1 copy-start.6
  16.8 1.1 copy-start.8
  17.9 1.1 copy-start.10
  19.0 1.1 copy-start.12
  20.0 1.2 copy-start.14
  23.9 1.5 %copy-start.22 = (f32[33,8,128]{2,1,0:T(8,128)}, f32[33,8,128]{2,1,0:T(8,128)S(1)}, u32[]{:S(2)}) copy-start(f32[33,8,128]{2,1,0:T(8,128)S(1)} %collective-permute-done.7.y_lo) | copy-start | bytes 405508
  25.3 17.2 %copy-start.1 = (f32[1,2,32,32,128]{4,3,2,1,0:T(8,128)S(1)}, f32[1,2,32,32,128]{4,3,2,1,0:T(8,128)}, u32[]{:S(2)}) copy-start(f32[1,2,32,32,128]{4,3,2,1,0:T(8,128)} %phase.3) | copy-start | bytes 3145732
  25.3 17.2 %copy-start.3 = (f32[1,2,32,32,128]{4,3,2,1,0:T(8,128)S(1)}, f32[1,2,32,32,128]{4,3,2,1,0:T(8,128)}, u32[]{:S(2)}) copy-start(f32[1,2,32,32,128]{4,3,2,1,0:T(8,128)} %solute.3) | copy-start | bytes 3145732
  25.3 17.2 %copy-start.5 = (f32[32,80,128]{2,1,0:T(8,128)S(1)}, f32[32,80,128]{2,1,0:T(8,128)}, u32[]{:S(2)}) copy-start(f32[32,80,128]{2,1,0:T(8,128)} %copy-done.4) | copy-start | bytes 3932164
  25.3 17.2 %copy-start.29 = (f32[1,2]{1,0:T(1,128)S(1)}, f32[1,2]{1,0:T(1,128)}, u32[]{:S(2)}) copy-start(f32[1,2]{1,0:T(1,128)} %under.7) | copy-start | bytes 28
  25.3 17.2 %copy-start.31 = (f32[1,2]{1,0:T(1,128)S(1)}, f32[1,2]{1,0:T(1,128)}, u32[]{:S(2)}) copy-start(f32[1,2]{1,0:T(1,128)} %mobile.7) | copy-start | bytes 28
  25.3 17.2 %copy-start.33 = (f32[1,2]{1,0:T(1,128)S(1)}, f32[1,2]{1,0:T(1,128)}, u32[]{:S(2)}) copy-start(f32[1,2]{1,0:T(1,128)} %spread.7) | copy-start | bytes 28
  27.6 12.9 %collective-permute-start.9 = (f32[608,128]{1,0:T(8,128)}, f32[608,128]{1,0:T(8,128)S(1)}, u32[]{:S(2)}, u32[]{:S(2)}) collective-permute-start(f32[608,128]{1,0:T(8,128)} %get-tuple-element.55), channel_id=1, source_target_pairs={{0,8},{8,16},{16,24},{24,0},{1,9},{9,17},{17,25},{25,1},{2,10},{10... | collective-permute-start | bytes 933896 | tf_op jit(solution)/shard_map/ppermute | solution.py:473
  27.6 13.8 %collective-permute-start.10 = (f32[608,128]{1,0:T(8,128)}, f32[608,128]{1,0:T(8,128)S(1)}, u32[]{:S(2)}, u32[]{:S(2)}) collective-permute-start(f32[608,128]{1,0:T(8,128)} %get-tuple-element.56), channel_id=1, source_target_pairs={{0,24},{8,0},{16,8},{24,16},{1,25},{9,1},{17,9},{25,17},{2,26},{10... | collective-permute-start | bytes 933896 | tf_op jit(solution)/shard_map/ppermute | solution.py:474
  29.3 5.9 %collective-permute-start = (f32[296,128]{1,0:T(8,128)}, f32[296,128]{1,0:T(8,128)S(1)}, u32[]{:S(2)}, u32[]{:S(2)}) collective-permute-start(f32[296,128]{1,0:T(8,128)} %copy-done.43), channel_id=1, source_target_pairs={{0,1},{1,0},{2,3},{3,2},{4,5},{5,4},{6,7},{7,6},{8,9},{9,8},{10,11... | collective-permute-start | bytes 454664 | tf_op jit(solution)/shard_map/ppermute | solution.py:459
  29.9 8.1 %collective-permute-start.1 = (f32[296,128]{1,0:T(8,128)}, f32[296,128]{1,0:T(8,128)S(1)}, u32[]{:S(2)}, u32[]{:S(2)}) collective-permute-start(f32[296,128]{1,0:T(8,128)} %copy-done.42), channel_id=1, source_target_pairs={{0,2},{1,3},{2,0},{3,1},{4,6},{5,7},{6,4},{7,5},{8,10},{9,11},{10,... | collective-permute-start | bytes 454664 | tf_op jit(solution)/shard_map/ppermute | solution.py:459
  31.4 28.9 %collective-permute-start.2 = (f32[296,128]{1,0:T(8,128)}, f32[296,128]{1,0:T(8,128)}, u32[]{:S(2)}, u32[]{:S(2)}) collective-permute-start(f32[296,128]{1,0:T(8,128)} %copy-done.41), channel_id=1, source_target_pairs={{0,3},{1,2},{2,1},{3,0},{4,7},{5,6},{6,5},{7,4},{8,11},{9,10},{10,... | collective-permute-start | bytes 454664 | tf_op jit(solution)/shard_map/ppermute | solution.py:459
  35.2 7.3 %copy-start.18 = (f32[296,128]{1,0:T(8,128)}, f32[296,128]{1,0:T(8,128)S(1)}, u32[]{:S(2)}) copy-start(f32[296,128]{1,0:T(8,128)S(1)} %collective-permute-done.refs_1_) | copy-start | bytes 454660
  35.2 26.6 %collective-permute-start.3 = (f32[296,128]{1,0:T(8,128)}, f32[296,128]{1,0:T(8,128)}, u32[]{:S(2)}, u32[]{:S(2)}) collective-permute-start(f32[296,128]{1,0:T(8,128)} %copy-done.40), channel_id=1, source_target_pairs={{0,4},{1,5},{2,6},{3,7},{4,0},{5,1},{6,2},{7,3},{8,12},{9,13},{10,... | collective-permute-start | bytes 454664 | tf_op jit(solution)/shard_map/ppermute | solution.py:459
  38.1 4.5 %copy-start.20 = (f32[296,128]{1,0:T(8,128)}, f32[296,128]{1,0:T(8,128)S(1)}, u32[]{:S(2)}) copy-start(f32[296,128]{1,0:T(8,128)S(1)} %collective-permute-done.1.refs_2_) | copy-start | bytes 454660
  38.1 26.0 %collective-permute-start.4 = (f32[296,128]{1,0:T(8,128)}, f32[296,128]{1,0:T(8,128)}, u32[]{:S(2)}, u32[]{:S(2)}) collective-permute-start(f32[296,128]{1,0:T(8,128)} %copy-done.39), channel_id=1, source_target_pairs={{0,5},{1,4},{2,7},{3,6},{4,1},{5,0},{6,3},{7,2},{8,13},{9,12},{10,... | collective-permute-start | bytes 454664 | tf_op jit(solution)/shard_map/ppermute | solution.py:459
  40.4 24.2 %collective-permute-start.5 = (f32[296,128]{1,0:T(8,128)}, f32[296,128]{1,0:T(8,128)}, u32[]{:S(2)}, u32[]{:S(2)}) collective-permute-start(f32[296,128]{1,0:T(8,128)} %copy-done.38), channel_id=1, source_target_pairs={{0,6},{1,7},{2,4},{3,5},{4,2},{5,3},{6,0},{7,1},{8,14},{9,15},{10,... | collective-permute-start | bytes 454664 | tf_op jit(solution)/shard_map/ppermute | solution.py:459
  41.4 25.7 %collective-permute-start.6 = (f32[296,128]{1,0:T(8,128)}, f32[296,128]{1,0:T(8,128)}, u32[]{:S(2)}, u32[]{:S(2)}) collective-permute-start(f32[296,128]{1,0:T(8,128)} %copy-done.37), channel_id=1, source_target_pairs={{0,7},{1,6},{2,5},{3,4},{4,3},{5,2},{6,1},{7,0},{8,15},{9,14},{10,... | collective-permute-start | bytes 454664 | tf_op jit(solution)/shard_map/ppermute | solution.py:459
  42.6 1.3 copy-start.7
  43.9 1.3 copy-start.9
  45.2 1.3 copy-start.11
  46.5 1.3 copy-start.13
  47.9 1.3 copy-start.15
  49.2 0.9 copy-start.23
  50.1 0.9 copy-start.25
  60.3 10.2 %copy-start.17 = (f32[296,128]{1,0:T(8,128)S(1)}, f32[296,128]{1,0:T(8,128)}, u32[]{:S(2)}) copy-start(f32[296,128]{1,0:T(8,128)} %copy-done.16) | copy-start | bytes 454660
  60.3 10.2 %copy-start.19 = (f32[296,128]{1,0:T(8,128)S(1)}, f32[296,128]{1,0:T(8,128)}, u32[]{:S(2)}) copy-start(f32[296,128]{1,0:T(8,128)} %copy-done.18) | copy-start | bytes 454660
  60.3 10.3 %copy-start.21 = (f32[296,128]{1,0:T(8,128)S(1)}, f32[296,128]{1,0:T(8,128)}, u32[]{:S(2)}) copy-start(f32[296,128]{1,0:T(8,128)} %copy-done.20) | copy-start | bytes 454660
  60.3 38.6 %copy-start.27 = (f32[224,128]{1,0:T(8,128)S(1)}, f32[224,128]{1,0:T(8,128)}, u32[]{:S(2)}) copy-start(f32[224,128]{1,0:T(8,128)} %copy-done.26) | copy-start | bytes 344068
  60.4 7.6 %collective-permute-start.18 = (f32[224,128]{1,0:T(8,128)S(1)}, f32[224,128]{1,0:T(8,128)S(1)}, u32[]{:S(2)}, u32[]{:S(2)}) collective-permute-start(f32[224,128]{1,0:T(8,128)S(1)} %get-tuple-element.71), channel_id=1, source_target_pairs={{0,1},{1,0},{2,3},{3,2},{4,5},{5,4},{6,7},{7,6},{8,9},{9,8},{10,11... | collective-permute-start | bytes 344072 | tf_op jit(solution)/shard_map/ppermute | solution.py:459
  61.8 10.8 %collective-permute-start.19 = (f32[224,128]{1,0:T(8,128)}, f32[224,128]{1,0:T(8,128)S(1)}, u32[]{:S(2)}, u32[]{:S(2)}) collective-permute-start(f32[224,128]{1,0:T(8,128)} %get-tuple-element.72), channel_id=1, source_target_pairs={{0,2},{1,3},{2,0},{3,1},{4,6},{5,7},{6,4},{7,5},{8,10},{9,11},{10,... | collective-permute-start | bytes 344072 | tf_op jit(solution)/shard_map/ppermute | solution.py:459
  64.1 10.0 %collective-permute-start.20 = (f32[224,128]{1,0:T(8,128)}, f32[224,128]{1,0:T(8,128)S(1)}, u32[]{:S(2)}, u32[]{:S(2)}) collective-permute-start(f32[224,128]{1,0:T(8,128)} %get-tuple-element.73), channel_id=1, source_target_pairs={{0,3},{1,2},{2,1},{3,0},{4,7},{5,6},{6,5},{7,4},{8,11},{9,10},{10,... | collective-permute-start | bytes 344072 | tf_op jit(solution)/shard_map/ppermute | solution.py:459
  64.6 12.3 %collective-permute-start.21 = (f32[224,128]{1,0:T(8,128)}, f32[224,128]{1,0:T(8,128)S(1)}, u32[]{:S(2)}, u32[]{:S(2)}) collective-permute-start(f32[224,128]{1,0:T(8,128)} %get-tuple-element.74), channel_id=1, source_target_pairs={{0,4},{1,5},{2,6},{3,7},{4,0},{5,1},{6,2},{7,3},{8,12},{9,13},{10,... | collective-permute-start | bytes 344072 | tf_op jit(solution)/shard_map/ppermute | solution.py:459
  67.1 13.2 %collective-permute-start.22 = (f32[224,128]{1,0:T(8,128)}, f32[224,128]{1,0:T(8,128)S(1)}, u32[]{:S(2)}, u32[]{:S(2)}) collective-permute-start(f32[224,128]{1,0:T(8,128)} %get-tuple-element.75), channel_id=1, source_target_pairs={{0,5},{1,4},{2,7},{3,6},{4,1},{5,0},{6,3},{7,2},{8,13},{9,12},{10,... | collective-permute-start | bytes 344072 | tf_op jit(solution)/shard_map/ppermute | solution.py:459
  68.0 19.0 %collective-permute-start.23 = (f32[224,128]{1,0:T(8,128)}, f32[224,128]{1,0:T(8,128)S(1)}, u32[]{:S(2)}, u32[]{:S(2)}) collective-permute-start(f32[224,128]{1,0:T(8,128)} %get-tuple-element.76), channel_id=1, source_target_pairs={{0,6},{1,7},{2,4},{3,5},{4,2},{5,3},{6,0},{7,1},{8,14},{9,15},{10,... | collective-permute-start | bytes 344072 | tf_op jit(solution)/shard_map/ppermute | solution.py:459
  72.6 23.8 %collective-permute-start.11 = (f32[2,152,128]{2,1,0:T(8,128)S(1)}, f32[2,152,128]{2,1,0:T(8,128)S(1)}, u32[]{:S(2)}, u32[]{:S(2)}) collective-permute-start(f32[2,152,128]{2,1,0:T(8,128)S(1)} %get-tuple-element.64), channel_id=1, source_target_pairs={{0,1},{1,0},{2,3},{3,2},{4,5},{5,4},{6,7},{7,6},{8,9},{9,8},{10,11... | collective-permute-start | bytes 466952 | tf_op jit(solution)/shard_map/ppermute | solution.py:459
  74.1 23.2 %collective-permute-start.12 = (f32[2,152,128]{2,1,0:T(8,128)S(1)}, f32[2,152,128]{2,1,0:T(8,128)S(1)}, u32[]{:S(2)}, u32[]{:S(2)}) collective-permute-start(f32[2,152,128]{2,1,0:T(8,128)S(1)} %get-tuple-element.65), channel_id=1, source_target_pairs={{0,2},{1,3},{2,0},{3,1},{4,6},{5,7},{6,4},{7,5},{8,10},{9,11},{10,... | collective-permute-start | bytes 466952 | tf_op jit(solution)/shard_map/ppermute | solution.py:459
  77.0 19.4 %collective-permute-start.24 = (f32[224,128]{1,0:T(8,128)S(1)}, f32[224,128]{1,0:T(8,128)S(1)}, u32[]{:S(2)}, u32[]{:S(2)}) collective-permute-start(f32[224,128]{1,0:T(8,128)S(1)} %get-tuple-element.77), channel_id=1, source_target_pairs={{0,7},{1,6},{2,5},{3,4},{4,3},{5,2},{6,1},{7,0},{8,15},{9,14},{10,... | collective-permute-start | bytes 344072 | tf_op jit(solution)/shard_map/ppermute | solution.py:459
  80.3 19.9 %collective-permute-start.13 = (f32[2,152,128]{2,1,0:T(8,128)S(1)}, f32[2,152,128]{2,1,0:T(8,128)S(1)}, u32[]{:S(2)}, u32[]{:S(2)}) collective-permute-start(f32[2,152,128]{2,1,0:T(8,128)S(1)} %get-tuple-element.66), channel_id=1, source_target_pairs={{0,3},{1,2},{2,1},{3,0},{4,7},{5,6},{6,5},{7,4},{8,11},{9,10},{10,... | collective-permute-start | bytes 466952 | tf_op jit(solution)/shard_map/ppermute | solution.py:459
  87.0 14.3 %collective-permute-start.14 = (f32[2,152,128]{2,1,0:T(8,128)S(1)}, f32[2,152,128]{2,1,0:T(8,128)S(1)}, u32[]{:S(2)}, u32[]{:S(2)}) collective-permute-start(f32[2,152,128]{2,1,0:T(8,128)S(1)} %get-tuple-element.67), channel_id=1, source_target_pairs={{0,4},{1,5},{2,6},{3,7},{4,0},{5,1},{6,2},{7,3},{8,12},{9,13},{10,... | collective-permute-start | bytes 466952 | tf_op jit(solution)/shard_map/ppermute | solution.py:459
  96.4 9.5 %collective-permute-start.15 = (f32[2,152,128]{2,1,0:T(8,128)S(1)}, f32[2,152,128]{2,1,0:T(8,128)S(1)}, u32[]{:S(2)}, u32[]{:S(2)}) collective-permute-start(f32[2,152,128]{2,1,0:T(8,128)S(1)} %get-tuple-element.68), channel_id=1, source_target_pairs={{0,5},{1,4},{2,7},{3,6},{4,1},{5,0},{6,3},{7,2},{8,13},{9,12},{10,... | collective-permute-start | bytes 466952 | tf_op jit(solution)/shard_map/ppermute | solution.py:459
  96.4 15.8 %collective-permute-start.16 = (f32[2,152,128]{2,1,0:T(8,128)S(1)}, f32[2,152,128]{2,1,0:T(8,128)S(1)}, u32[]{:S(2)}, u32[]{:S(2)}) collective-permute-start(f32[2,152,128]{2,1,0:T(8,128)S(1)} %get-tuple-element.69), channel_id=1, source_target_pairs={{0,6},{1,7},{2,4},{3,5},{4,2},{5,3},{6,0},{7,1},{8,14},{9,15},{10,... | collective-permute-start | bytes 466952 | tf_op jit(solution)/shard_map/ppermute | solution.py:459
  97.3 22.6 %collective-permute-start.17 = (f32[2,152,128]{2,1,0:T(8,128)S(1)}, f32[2,152,128]{2,1,0:T(8,128)S(1)}, u32[]{:S(2)}, u32[]{:S(2)}) collective-permute-start(f32[2,152,128]{2,1,0:T(8,128)S(1)} %get-tuple-element.70), channel_id=1, source_target_pairs={{0,7},{1,6},{2,5},{3,4},{4,3},{5,2},{6,1},{7,0},{8,15},{9,14},{10,... | collective-permute-start | bytes 466952 | tf_op jit(solution)/shard_map/ppermute | solution.py:459
  100.2 19.7 %collective-permute-start.25 = (f32[2,112,128]{2,1,0:T(8,128)S(1)}, f32[2,112,128]{2,1,0:T(8,128)S(1)}, u32[]{:S(2)}, u32[]{:S(2)}) collective-permute-start(f32[2,112,128]{2,1,0:T(8,128)S(1)} %get-tuple-element.79), channel_id=1, source_target_pairs={{0,1},{1,0},{2,3},{3,2},{4,5},{5,4},{6,7},{7,6},{8,9},{9,8},{10,11... | collective-permute-start | bytes 344072 | tf_op jit(solution)/shard_map/ppermute | solution.py:459
  101.3 18.6 %collective-permute-start.26 = (f32[2,112,128]{2,1,0:T(8,128)S(1)}, f32[2,112,128]{2,1,0:T(8,128)S(1)}, u32[]{:S(2)}, u32[]{:S(2)}) collective-permute-start(f32[2,112,128]{2,1,0:T(8,128)S(1)} %get-tuple-element.80), channel_id=1, source_target_pairs={{0,2},{1,3},{2,0},{3,1},{4,6},{5,7},{6,4},{7,5},{8,10},{9,11},{10,... | collective-permute-start | bytes 344072 | tf_op jit(solution)/shard_map/ppermute | solution.py:459
  105.9 14.1 %collective-permute-start.27 = (f32[2,112,128]{2,1,0:T(8,128)S(1)}, f32[2,112,128]{2,1,0:T(8,128)S(1)}, u32[]{:S(2)}, u32[]{:S(2)}) collective-permute-start(f32[2,112,128]{2,1,0:T(8,128)S(1)} %get-tuple-element.81), channel_id=1, source_target_pairs={{0,3},{1,2},{2,1},{3,0},{4,7},{5,6},{6,5},{7,4},{8,11},{9,10},{10,... | collective-permute-start | bytes 344072 | tf_op jit(solution)/shard_map/ppermute | solution.py:459
  112.2 11.5 %collective-permute-start.28 = (f32[2,112,128]{2,1,0:T(8,128)S(1)}, f32[2,112,128]{2,1,0:T(8,128)S(1)}, u32[]{:S(2)}, u32[]{:S(2)}) collective-permute-start(f32[2,112,128]{2,1,0:T(8,128)S(1)} %get-tuple-element.82), channel_id=1, source_target_pairs={{0,4},{1,5},{2,6},{3,7},{4,0},{5,1},{6,2},{7,3},{8,12},{9,13},{10,... | collective-permute-start | bytes 344072 | tf_op jit(solution)/shard_map/ppermute | solution.py:459
  119.9 6.7 %collective-permute-start.29 = (f32[2,112,128]{2,1,0:T(8,128)S(1)}, f32[2,112,128]{2,1,0:T(8,128)S(1)}, u32[]{:S(2)}, u32[]{:S(2)}) collective-permute-start(f32[2,112,128]{2,1,0:T(8,128)S(1)} %get-tuple-element.83), channel_id=1, source_target_pairs={{0,5},{1,4},{2,7},{3,6},{4,1},{5,0},{6,3},{7,2},{8,13},{9,12},{10,... | collective-permute-start | bytes 344072 | tf_op jit(solution)/shard_map/ppermute | solution.py:459
  119.9 10.9 %collective-permute-start.30 = (f32[2,112,128]{2,1,0:T(8,128)S(1)}, f32[2,112,128]{2,1,0:T(8,128)S(1)}, u32[]{:S(2)}, u32[]{:S(2)}) collective-permute-start(f32[2,112,128]{2,1,0:T(8,128)S(1)} %get-tuple-element.84), channel_id=1, source_target_pairs={{0,6},{1,7},{2,4},{3,5},{4,2},{5,3},{6,0},{7,1},{8,14},{9,15},{10,... | collective-permute-start | bytes 344072 | tf_op jit(solution)/shard_map/ppermute | solution.py:459
  119.9 12.4 %collective-permute-start.31 = (f32[2,112,128]{2,1,0:T(8,128)S(1)}, f32[2,112,128]{2,1,0:T(8,128)S(1)}, u32[]{:S(2)}, u32[]{:S(2)}) collective-permute-start(f32[2,112,128]{2,1,0:T(8,128)S(1)} %get-tuple-element.85), channel_id=1, source_target_pairs={{0,7},{1,6},{2,5},{3,4},{4,3},{5,2},{6,1},{7,0},{8,15},{9,14},{10,... | collective-permute-start | bytes 344072 | tf_op jit(solution)/shard_map/ppermute | solution.py:459
  (12 other events, 8.2 us)

commit v4 on v3

--- a/solution.py
+++ b/solution.py
@@ -14,36 +14,56 @@
 aniso_strength = 0.05
 
 
-def pack_y_kernel(under, mobile, spread, phase_lo, phase_hi, solute_lo, solute_hi, to_prev, to_next):
-    edge = phase_lo.shape[2]
+def pack_y_kernel(under, mobile, spread, owner, phase_lo, phase_hi, solute_lo, solute_hi, to_prev, to_next, own, *scratch):
+    copies = []
+    for index, source in enumerate((under, mobile, spread, owner)):
+        copies.append(pltpu.make_async_copy(source, scratch[index], scratch[-1].at[index]))
+        copies[-1].start()
+    edge, depth = phase_lo.shape[2], phase_lo.shape[4]
+    tiles = own.shape[0] // 8 - 1
     to_prev[:edge, :W, :] = phase_lo[0, 0, :, :W, :]
     to_prev[:edge, W:, :] = solute_lo[0, 0, :, :W, :]
     to_next[:edge, :W, :] = phase_hi[0, 0, :, W:, :]
     to_next[:edge, W:, :] = solute_hi[0, 0, :, W:, :]
-    to_prev[edge] = jnp.zeros((2 * W, to_prev.shape[2]), jnp.float32)
-    to_next[edge] = jnp.zeros((2 * W, to_prev.shape[2]), jnp.float32)
-    for kind, own in enumerate((under, mobile, spread)):
-        to_prev[edge, kind, :] = jnp.full((to_prev.shape[2],), own[0, 0], jnp.float32)
-        to_next[edge, kind, :] = jnp.full((to_prev.shape[2],), own[0, own.shape[1] - 1], jnp.float32)
-
-
-def pack_y(phase, solute, coef):
+    for copy in copies:
+        copy.wait()
+    line = lax.broadcasted_iota(jnp.int32, (8, depth), 0)
+    lane = lax.broadcasted_iota(jnp.int32, (8, depth), 1)
+    names = jnp.zeros((8, depth), jnp.float32)
+    for tile in range(tiles):
+        rows = jnp.zeros((8, depth), jnp.float32)
+        for kind in range(3):
+            rows = jnp.where(line == kind, scratch[kind][0, tile], rows)
+        own[8 * tile : 8 * tile + 8, :] = rows
+        if tile == 0:
+            to_prev[edge] = rows
+        if tile == tiles - 1:
+            to_next[edge] = rows
+        names = jnp.where(lane == tile, scratch[3][0, tile].astype(jnp.float32), names)
+    own[8 * tiles :, :] = names
+
+
+def pack_y(phase, solute, coef, owner):
     _, tiles, edge, _, depth = phase.shape
     low = pl.BlockSpec((1, 1, edge, 2 * W, depth), lambda i: (0, 0, 0, 0, 0))
     high = pl.BlockSpec((1, 1, edge, 2 * W, depth), lambda i: (0, tiles - 1, 0, edge // (2 * W) - 1, 0))
-    out = jax.ShapeDtypeStruct((edge + 1, 2 * W, depth), jnp.float32)
+    face = jax.ShapeDtypeStruct((edge + 1, 2 * W, depth), jnp.float32)
+    own = jax.ShapeDtypeStruct((8 * tiles + 8, depth), jnp.float32)
     whole = pl.BlockSpec((edge + 1, 2 * W, depth), lambda i: (0, 0, 0))
     return pl.pallas_call(
         pack_y_kernel,
         grid=(1,),
-        in_specs=[pl.BlockSpec(memory_space=pltpu.SMEM)] * 3 + [low, high, low, high],
-        out_specs=[whole, whole],
-        out_shape=[out, out],
+        in_specs=[pl.BlockSpec(memory_space=pl.ANY)] * 4 + [low, high, low, high],
+        out_specs=[whole, whole, pl.BlockSpec((8 * tiles + 8, depth), lambda i: (0, 0))],
+        out_shape=[face, face, own],
+        scratch_shapes=[pltpu.SMEM((1, tiles), jnp.float32)] * 3
+        + [pltpu.SMEM((1, tiles), jnp.int32), pltpu.SemaphoreType.DMA((4,))],
+        compiler_params=pltpu.CompilerParams(vmem_limit_bytes=8 * 1024 * 1024),
         name="pack_y",
-    )(*coef, phase, phase, solute, solute)
-
-
-def pack_x_kernel(under, mobile, spread, phase_lo, phase_hi, solute_lo, solute_hi, y_lo, y_hi, _, to_prev, to_next):
+    )(*coef, owner, phase, phase, solute, solute)
+
+
+def pack_x_kernel(own, phase_lo, phase_hi, solute_lo, solute_hi, y_lo, y_hi, _, to_prev, to_next):
     tiles, edge, depth = phase_lo.shape[1], phase_lo.shape[3], phase_lo.shape[4]
     width = tiles * edge + 2 * W
     for out, phase, solute, first in (
@@ -61,14 +81,10 @@
         at = 2 * W * width
         out[at : at + 8, :] = y_lo[edge]
         out[at + 8 : at + 16, :] = y_hi[edge]
-        for tile in range(tiles):
-            begin = at + 16 + 8 * tile
-            out[begin : begin + 8, :] = jnp.zeros((8, depth), jnp.float32)
-            for kind, own in enumerate((under, mobile, spread)):
-                out[begin + kind : begin + kind + 1, :] = jnp.full((1, depth), own[0, tile], jnp.float32)
-
-
-def pack_x(phase, solute, coef, y_lo, y_hi, after):
+        out[at + 16 : at + 16 + 8 * tiles, :] = own[: 8 * tiles, :]
+
+
+def pack_x(phase, solute, own, y_lo, y_hi, after):
     _, tiles, edge, _, depth = phase.shape
     low = pl.BlockSpec((1, tiles, W, edge, depth), lambda i: (0, 0, 0, 0, 0))
     high = pl.BlockSpec((1, tiles, W, edge, depth), lambda i: (0, 0, edge // W - 1, 0, 0))
@@ -79,11 +95,12 @@
     return pl.pallas_call(
         pack_x_kernel,
         grid=(1,),
-        in_specs=[pl.BlockSpec(memory_space=pltpu.SMEM)] * 3 + [low, high, low, high, side, side, pl.BlockSpec(memory_space=pl.ANY)],
+        in_specs=[pl.BlockSpec((8 * tiles + 8, depth), lambda i: (0, 0)), low, high, low, high, side, side, pl.BlockSpec(memory_space=pl.ANY)],
         out_specs=[whole, whole],
         out_shape=[out, out],
+        compiler_params=pltpu.CompilerParams(vmem_limit_bytes=8 * 1024 * 1024),
         name="pack_x",
-    )(*coef, phase, phase, solute, solute, y_lo, y_hi, after)
+    )(own, phase, phase, solute, solute, y_lo, y_hi, after)
 
 
 def update(near_p, near_u, under, mobile, spread):
@@ -125,6 +142,12 @@
         self.size_b = self.rows_b * edge + self.rows_a * 8
         self.size = self.size_a + self.size_b
 
+    def far_first(self, values):
+        return [*values[self.half :], *values[1 : self.half], values[0]]
+
+    def by_mask(self, values):
+        return [values[-1], *values[self.half : -1], *values[: self.half]]
+
 
 AUX = 8
 
@@ -158,7 +181,7 @@
     lax.fori_loop(first, last, one_row, 0, unroll=UNROLL)
 
 
-def inner_kernel(plan, under, mobile, spread, owner, phase, solute, *rest):
+def inner_kernel(plan, own, phase, solute, *rest):
     tiles, edge, depth, pieces = plan.tiles, plan.edge, plan.depth, plan.pieces
     outs, fields = rest[:pieces], rest[pieces:]
     pairs = [fields[2 * NSTEPS - 2 : 2 * NSTEPS]]
@@ -177,16 +200,12 @@
 
     def coefs_of(row, start):
         tile = (start - PAD) // edge
-        return under[0, tile], mobile[0, tile], spread[0, tile]
+        return tuple(own[8 * tile + kind : 8 * tile + kind + 1, :] for kind in range(3))
 
     for step in range(NSTEPS):
         margin = plan.low - W + step + 1
         starts = range(PAD, PAD + tiles * edge, 8)
         march(margin, edge - margin, starts, pairs[step], pairs[step + 1], coefs_of)
-    lane = lax.broadcasted_iota(jnp.int32, (AUX, depth), 1)
-    names = jnp.zeros((AUX, depth), jnp.float32)
-    for tile in range(tiles):
-        names = jnp.where(lane == tile, owner[0, tile].astype(jnp.float32), names)
     for mask, out in enumerate(outs):
         piece = me ^ mask
         for tile in range(tiles):
@@ -198,42 +217,42 @@
                         plan.low + piece * plan.rows_a + row, start : start + plan.cols_a, :
                     ]
         at = 2 * tiles * plan.size_a
-        out[at : at + AUX, :] = names
-
-
-def run_inner(plan, coef, owner, phase, solute):
+        out[at : at + AUX, :] = own[8 * tiles : 8 * tiles + AUX, :]
+
+
+def run_inner(plan, own, phase, solute):
     shape = (plan.edge, plan.tiles * plan.edge + 2 * PAD, plan.depth)
     vmem = pl.BlockSpec(memory_space=pltpu.VMEM)
-    smem = pl.BlockSpec(memory_space=pltpu.SMEM)
     piece = jax.ShapeDtypeStruct((2 * plan.tiles * plan.size_a + AUX, plan.depth), jnp.float32)
     kept = 2 * (NSTEPS - 1)
     results = pl.pallas_call(
         functools.partial(inner_kernel, plan),
-        in_specs=[smem] * 4 + [vmem] * 2,
+        in_specs=[vmem] * 3,
         out_specs=[vmem] * (plan.pieces + kept),
         out_shape=[piece] * plan.pieces + [jax.ShapeDtypeStruct(shape, jnp.float32)] * kept,
         scratch_shapes=[pltpu.VMEM(shape, jnp.float32)] * 4,
-        compiler_params=pltpu.CompilerParams(vmem_limit_bytes=40 * 1024 * 1024),
+        compiler_params=pltpu.CompilerParams(vmem_limit_bytes=12 * 1024 * 1024),
         cost_estimate=pl.CostEstimate(flops=10**8, bytes_accessed=24 * 1024 * 1024, transcendentals=0),
         name="inner",
-    )(*coef, owner, phase, solute)
+    )(own, phase, solute)
     return results[: plan.pieces], results[plan.pieces :]
 
 
-def ring_kernel(plan, under, mobile, spread, phase, solute, y_lo, y_hi, x_lo, x_hi, *rest):
+def ring_kernel(plan, own_rows, phase, solute, y_lo, y_hi, x_lo, x_hi, *rest):
     tiles, edge, depth, pieces, low = plan.tiles, plan.edge, plan.depth, plan.pieces, plan.low
     kept = 2 * (NSTEPS - 1)
     fields, outs, scratch = rest[:kept], rest[kept : kept + pieces], rest[kept + pieces :]
-    pairs, coefs = [scratch[2 * step : 2 * step + 2] for step in range(NSTEPS + 1)], scratch[-1]
+    pairs = [scratch[2 * (step % 2) : 2 * (step % 2) + 2] for step in range(NSTEPS + 1)]
+    coefs = scratch[-1]
     cols = tiles * edge
     width = cols + 2 * W
     own = 2 * PAD
     me = lax.axis_index("gy")
     for zone, source in ((0, x_lo), (1, None), (2, x_hi)):
-        for kind, here in enumerate((under, mobile, spread)):
+        for kind in range(3):
             if source is None:
                 parts = [y_lo[edge, kind : kind + 1, :]]
-                parts += [jnp.full((1, depth), here[0, tile], jnp.float32) for tile in range(tiles)]
+                parts += [own_rows[8 * tile + kind : 8 * tile + kind + 1, :] for tile in range(tiles)]
                 parts += [y_hi[edge, kind : kind + 1, :]]
             else:
                 at = 2 * W * width + kind
@@ -267,22 +286,6 @@
             for tile in range(tiles):
                 start = own + tile * edge
                 pairs[0][field][W + row, start : start + edge, :] = values[0, tile, row]
-    for step in range(1, NSTEPS):
-        margin = low - W + step
-        for field in range(2):
-            kept_field, buffer = fields[2 * (step - 1) + field], pairs[step][field]
-            for row in (margin, margin + 1, edge - margin - 2, edge - margin - 1):
-                buffer[W + row, own + 8 : own + cols - 8, :] = kept_field[row, PAD + 8 : PAD + cols - 8, :]
-
-            def copy_sides(row, carry, kept_field=kept_field, buffer=buffer):
-                for start in (8, cols - 16):
-                    buffer[W + row, own + start : own + start + 8, :] = kept_field[
-                        row, PAD + start : PAD + start + 8, :
-                    ]
-                return carry
-
-            lax.fori_loop(margin, edge - margin, copy_sides, 0, unroll=UNROLL)
-
     def coefs_of(zone):
         def found(row, start):
             return tuple(coefs[zone(row), kind, start - PAD : start - PAD + 8, :] for kind in range(3))
@@ -302,6 +305,20 @@
         march(W - (W - step), W + margin, across, source, target, any_zone)
         march(W + edge - margin, W + edge + W - step, across, source, target, any_zone)
         march(W + margin, W + edge - margin, sides, source, target, own_zone)
+        if step < NSTEPS:
+            for field in range(2):
+                kept_field, buffer = fields[2 * (step - 1) + field], pairs[step][field]
+                for row in (margin, margin + 1, edge - margin - 2, edge - margin - 1):
+                    buffer[W + row, own + 8 : own + cols - 8, :] = kept_field[row, PAD + 8 : PAD + cols - 8, :]
+
+                def copy_sides(row, carry, kept_field=kept_field, buffer=buffer):
+                    for start in (8, cols - 16):
+                        buffer[W + row, own + start : own + start + 8, :] = kept_field[
+                            row, PAD + start : PAD + start + 8, :
+                        ]
+                    return carry
+
+                lax.fori_loop(margin, edge - margin, copy_sides, 0, unroll=UNROLL)
     for mask, out in enumerate(outs):
         piece = me ^ mask
         for tile in range(tiles):
@@ -320,27 +337,26 @@
                     at += 8
 
 
-def run_ring(plan, coef, phase, solute, halos, fields):
+def run_ring(plan, own, phase, solute, halos, fields):
     cols = plan.tiles * plan.edge
     buffer = pltpu.VMEM((plan.edge + 2 * W, cols + 4 * PAD, plan.depth), jnp.float32)
     vmem = pl.BlockSpec(memory_space=pltpu.VMEM)
-    smem = pl.BlockSpec(memory_space=pltpu.SMEM)
     piece = jax.ShapeDtypeStruct((2 * plan.tiles * plan.size_b, plan.depth), jnp.float32)
     return pl.pallas_call(
         functools.partial(ring_kernel, plan),
-        in_specs=[smem] * 3 + [vmem] * (6 + len(fields)),
+        in_specs=[vmem] * (7 + len(fields)),
         out_specs=[vmem] * plan.pieces,
         out_shape=[piece] * plan.pieces,
-        scratch_shapes=[buffer] * (2 * NSTEPS + 2) + [pltpu.VMEM((3, 3, cols + 16, plan.depth), jnp.float32)],
-        compiler_params=pltpu.CompilerParams(vmem_limit_bytes=40 * 1024 * 1024),
+        scratch_shapes=[buffer] * 4 + [pltpu.VMEM((3, 3, cols + 16, plan.depth), jnp.float32)],
+        compiler_params=pltpu.CompilerParams(vmem_limit_bytes=12 * 1024 * 1024),
         cost_estimate=pl.CostEstimate(flops=10**8, bytes_accessed=24 * 1024 * 1024, transcendentals=0),
         name="rest",
-    )(*coef, phase, solute, *halos, *fields)
+    )(own, phase, solute, *halos, *fields)
 
 
 def table_kernel(plan, *refs):
     pieces, tiles = plan.pieces, plan.tiles
-    arrived, (table, names, sems) = refs[:pieces], refs[pieces + 1 :]
+    arrived, (table, names, sems) = plan.by_mask(refs[:pieces]), refs[pieces + 1 :]
     me = lax.axis_index("gy")
     copies = []
     for mask in range(pieces):
@@ -376,12 +392,12 @@
             pltpu.SemaphoreType.DMA((pieces,)),
         ],
         name="table",
-    )(*arrived, after)
+    )(*plan.far_first(arrived), after)
 
 
 def route_kernel(plan, size, aux, table, *refs):
     pieces, tiles = plan.pieces, plan.tiles
-    arrived, outs, (held,) = refs[:pieces], refs[pieces : 2 * pieces], refs[2 * pieces :]
+    arrived, outs, (held,) = plan.by_mask(refs[:pieces]), refs[pieces : 2 * pieces], refs[2 * pieces :]
     for mask in range(pieces):
         for tile in range(tiles):
             held[mask * tiles + tile] = arrived[mask][tile * size : (tile + 1) * size, :]
@@ -403,14 +419,15 @@
         out_specs=[vmem] * pieces,
         out_shape=[jax.ShapeDtypeStruct((tiles, size + aux, depth), jnp.float32)] * pieces,
         scratch_shapes=[pltpu.VMEM((pieces * tiles, size, depth), jnp.float32)],
-        compiler_params=pltpu.CompilerParams(vmem_limit_bytes=16 * 1024 * 1024),
+        compiler_params=pltpu.CompilerParams(vmem_limit_bytes=8 * 1024 * 1024),
         name="route",
-    )(table, *arrived)
+    )(table, *plan.far_first(arrived))
 
 
 def settle_kernel(plan, *refs):
     pieces, tiles, edge, depth = plan.pieces, plan.tiles, plan.edge, plan.depth
-    part_a, part_b, outs = refs[:pieces], refs[pieces : 2 * pieces], refs[2 * pieces :]
+    part_a, part_b = plan.by_mask(refs[:pieces]), plan.by_mask(refs[pieces : 2 * pieces])
+    outs = refs[2 * pieces :]
     me = lax.axis_index("gy")
     for mask in range(pieces):
         piece = me ^ mask
@@ -443,9 +460,9 @@
         in_specs=[vmem] * (2 * plan.pieces),
         out_specs=[vmem, vmem],
         out_shape=[out, out],
-        compiler_params=pltpu.CompilerParams(vmem_limit_bytes=16 * 1024 * 1024),
+        compiler_params=pltpu.CompilerParams(vmem_limit_bytes=8 * 1024 * 1024),
         name="settle",
-    )(*part_a, *part_b)
+    )(*plan.far_first(part_a), *plan.far_first(part_b))
 
 
 def ring(axis, step):
@@ -464,15 +481,15 @@
     _, tiles, edge, _, depth = phase.shape
     plan = Plan(lax.axis_size("gy"), tiles, edge, depth)
     coef = (undercool, mobility, diffusivity)
-    to_prev, to_next = pack_y(phase, solute, coef)
+    to_prev, to_next, own = pack_y(phase, solute, coef, owner)
     y_lo = lax.ppermute(to_next, "gy", ring("gy", 1))
     y_hi = lax.ppermute(to_prev, "gy", ring("gy", -1))
-    first, fields = run_inner(plan, coef, owner, phase, solute)
+    first, fields = run_inner(plan, own, phase, solute)
     part_a = exchange(plan, first)
-    to_prev, to_next = pack_x(phase, solute, coef, y_lo, y_hi, fields[0])
+    to_prev, to_next = pack_x(phase, solute, own, y_lo, y_hi, fields[0])
     x_lo = lax.ppermute(to_next, "gx", ring("gx", 1))
     x_hi = lax.ppermute(to_prev, "gx", ring("gx", -1))
-    second = run_ring(plan, coef, phase, solute, (y_lo, y_hi, x_lo, x_hi), fields)
+    second = run_ring(plan, own, phase, solute, (y_lo, y_hi, x_lo, x_hi), fields)
     part_b = exchange(plan, second)
     table = find_table(plan, part_a, second[0])
     sent_a = exchange(plan, route(plan, 2 * plan.size_a, AUX, table, part_a))

time: 134 us -> 131 us (0.978)
  the two profiles are of different devices: /device:TPU:8 before, /device:TPU:0 now
where the time goes in v4:
time: 131 us
  starting transfers between devices  53.3 us (41%)
  waiting for transfers between devices  43.7 us (33%)
  Pallas kernels  21.1 us (16%)
  local copies, waits for them, and re-layouts  12.1 us (9%)
    ppermute x28, starting transfers between devices, exchange(): lax.ppermute(values[mask], 'gy', [(i, i ^ mask) for i in range(plan.piece...  45.5 us
    ppermute x28, waiting for transfers between devices, exchange(): lax.ppermute(values[mask], 'gy', [(i, i ^ mask) for i in range(plan.piece...  43.6 us
    unnamed x56, local copies, waits for them, and re-layouts  12.1 us
    pallas_call x1, Pallas kernels, run_inner(): pl.pallas_call(functools.partial(inner_kernel, plan), in_specs=[vmem] * 3...  8.41 us
    pallas_call x1, Pallas kernels, run_ring(): pl.pallas_call(functools.partial(ring_kernel, plan), in_specs=[vmem] * (7...  7.34 us
    ppermute x1, starting transfers between devices, per_device(): y_hi = lax.ppermute(to_prev, 'gy', ring('gy', -1))  3.1 us
    ppermute x1, starting transfers between devices, per_device(): y_lo = lax.ppermute(to_next, 'gy', ring('gy', 1))  3.02 us
  transfers between devices with their start and end apart: 32, of which 9 were waited for; matrix products, arithmetic and copies ran while one was open for 0% of the time, Pallas kernels for 14%

profile of v4, /device:TPU:0, one launch (start us, length us, event | category | flops | bytes accessed | tf_op | source)
XLA Modules:
  0.0 131.1 jit_solution(1360216180244929606)
XLA Ops:
  0.6 1.2 copy-done
  1.9 1.2 copy-done.2
  3.1 0.7 copy-done.24
  3.7 0.7 copy-done.25
  4.4 0.7 copy-done.26
  5.1 0.7 copy-done.27
  5.7 0.6 pack_y.1
  6.3 3.0 %collective-permute-start.7 = (f32[33,8,128]{2,1,0:T(8,128)S(1)}, f32[33,8,128]{2,1,0:T(8,128)S(1)}, u32[]{:S(2)}, u32[]{:S(2)}) collective-permute-start(f32[33,8,128]{2,1,0:T(8,128)S(1)} %get-tuple-element.54), channel_id=1, source_target_pairs={{0,1},{1,2},{2,3},{3,4},{4,5},{5,6},{6,7},{7,0},{8,9},{9,10},{10,1... | collective-permute-start | bytes 405512 | tf_op jit(solution)/shard_map/ppermute | solution.py:485
  9.3 3.1 %collective-permute-start.8 = (f32[33,8,128]{2,1,0:T(8,128)S(1)}, f32[33,8,128]{2,1,0:T(8,128)S(1)}, u32[]{:S(2)}, u32[]{:S(2)}) collective-permute-start(f32[33,8,128]{2,1,0:T(8,128)S(1)} %get-tuple-element.55), channel_id=1, source_target_pairs={{0,7},{1,0},{2,1},{3,2},{4,3},{5,4},{6,5},{7,6},{8,15},{9,8},{10,9... | collective-permute-start | bytes 405512 | tf_op jit(solution)/shard_map/ppermute | solution.py:486
  12.5 8.4 %inner.1 = (f32[296,128]{1,0:T(8,128)S(1)}, f32[296,128]{1,0:T(8,128)S(1)}, f32[296,128]{1,0:T(8,128)S(1)}, f32[296,128]{1,0:T(8,128)S(1)}, f32[296,128]{1,0:T(8...) custom-call(f32[24,128]{1,0:T(8,128)S(1)} %get-tuple-element.45.own., ...), custom_call_target="tpu_custom_call" | custom-call | flops 100000000 | bytes 25165824 | tf_op jit(solution)/shard_map/inner/pallas_call | solution.py:228
  20.9 0.0 collective-permute-done.7.y_lo
  21.0 0.6 copy-done.4
  21.5 0.0 collective-permute-start.9
  21.5 1.7 %collective-permute-start.10 = (f32[608,128]{1,0:T(8,128)S(1)}, f32[608,128]{1,0:T(8,128)S(1)}, u32[]{:S(2)}, u32[]{:S(2)}) collective-permute-start(f32[608,128]{1,0:T(8,128)S(1)} %get-tuple-element.58), channel_id=1, source_target_pairs={{0,24},{8,0},{16,8},{24,16},{1,25},{9,1},{17,9},{25,17},{2,26},{10... | collective-permute-start | bytes 933896 | tf_op jit(solution)/shard_map/ppermute | solution.py:491
  23.3 0.9 collective-permute-start
  24.2 0.4 collective-permute-start.1
  24.6 3.6 %collective-permute-start.2 = (f32[296,128]{1,0:T(8,128)S(1)}, f32[296,128]{1,0:T(8,128)S(1)}, u32[]{:S(2)}, u32[]{:S(2)}) collective-permute-start(f32[296,128]{1,0:T(8,128)S(1)} %get-tuple-element.48), channel_id=1, source_target_pairs={{0,6},{1,7},{2,4},{3,5},{4,2},{5,3},{6,0},{7,1},{8,14},{9,15},{10,... | collective-permute-start | bytes 454664 | tf_op jit(solution)/shard_map/ppermute | solution.py:476
  28.2 10.9 %collective-permute-done.refs_0_ = f32[296,128]{1,0:T(8,128)S(1)} collective-permute-done((f32[296,128]{1,0:T(8,128)S(1)}, f32[296,128]{1,0:T(8,128)S(1)}, u32[]{:S(2)}, u32[]{:S(2)}) %collective-permute-start) | collective-permute-done | bytes 151584 | tf_op jit(solution)/shard_map/ppermute | solution.py:476
  39.0 2.5 %collective-permute-start.3 = (f32[296,128]{1,0:T(8,128)S(1)}, f32[296,128]{1,0:T(8,128)S(1)}, u32[]{:S(2)}, u32[]{:S(2)}) collective-permute-start(f32[296,128]{1,0:T(8,128)S(1)} %get-tuple-element.49), channel_id=1, source_target_pairs={{0,7},{1,6},{2,5},{3,4},{4,3},{5,2},{6,1},{7,0},{8,15},{9,14},{10,... | collective-permute-start | bytes 454664 | tf_op jit(solution)/shard_map/ppermute | solution.py:476
  41.6 0.8 collective-permute-done.1.refs_1_
  42.3 1.4 %collective-permute-start.4 = (f32[296,128]{1,0:T(8,128)S(1)}, f32[296,128]{1,0:T(8,128)S(1)}, u32[]{:S(2)}, u32[]{:S(2)}) collective-permute-start(f32[296,128]{1,0:T(8,128)S(1)} %get-tuple-element.50), channel_id=1, source_target_pairs={{0,1},{1,0},{2,3},{3,2},{4,5},{5,4},{6,7},{7,6},{8,9},{9,8},{10,11... | collective-permute-start | bytes 454664 | tf_op jit(solution)/shard_map/ppermute | solution.py:476
  43.7 0.0 collective-permute-done.10.x_hi
  43.7 2.1 %collective-permute-start.6 = (f32[296,128]{1,0:T(8,128)S(1)}, f32[296,128]{1,0:T(8,128)S(1)}, u32[]{:S(2)}, u32[]{:S(2)}) collective-permute-start(f32[296,128]{1,0:T(8,128)S(1)} %get-tuple-element.52), channel_id=1, source_target_pairs={{0,3},{1,2},{2,1},{3,0},{4,7},{5,6},{6,5},{7,4},{8,11},{9,10},{10,... | collective-permute-start | bytes 454664 | tf_op jit(solution)/shard_map/ppermute | solution.py:476
  45.8 7.3 %rest.1 = (f32[224,128]{1,0:T(8,128)S(1)}, f32[224,128]{1,0:T(8,128)S(1)}, f32[224,128]{1,0:T(8,128)S(1)}, f32[224,128]{1,0:T(8,128)S(1)}, f32[224,128]{1,0:T(8,...) custom-call(f32[24,128]{1,0:T(8,128)S(1)} %get-tuple-element.45.own.own_rows, ...), custom_call_target="tpu_custom_call" | custom-call | flops 100000000 | bytes 25165824 | tf_op jit(solution)/shard_map/rest/pallas_call | solution.py:345
  53.2 0.6 copy-done.20
  53.9 0.0 copy-start.9
  53.9 1.2 collective-permute-start.18
  55.0 2.7 %collective-permute-start.19 = (f32[224,128]{1,0:T(8,128)S(1)}, f32[224,128]{1,0:T(8,128)S(1)}, u32[]{:S(2)}, u32[]{:S(2)}) collective-permute-start(f32[224,128]{1,0:T(8,128)S(1)} %get-tuple-element.74), channel_id=1, source_target_pairs={{0,5},{1,4},{2,7},{3,6},{4,1},{5,0},{6,3},{7,2},{8,13},{9,12},{10,... | collective-permute-start | bytes 344072 | tf_op jit(solution)/shard_map/ppermute | solution.py:476
  57.7 0.0 collective-permute-done.4.refs_4_
  57.7 2.5 %collective-permute-start.20 = (f32[224,128]{1,0:T(8,128)S(1)}, f32[224,128]{1,0:T(8,128)S(1)}, u32[]{:S(2)}, u32[]{:S(2)}) collective-permute-start(f32[224,128]{1,0:T(8,128)S(1)} %get-tuple-element.75), channel_id=1, source_target_pairs={{0,6},{1,7},{2,4},{3,5},{4,2},{5,3},{6,0},{7,1},{8,14},{9,15},{10,... | collective-permute-start | bytes 344072 | tf_op jit(solution)/shard_map/ppermute | solution.py:476
  60.2 0.0 collective-permute-done.5.refs_5_
  60.2 1.4 %collective-permute-start.21 = (f32[224,128]{1,0:T(8,128)S(1)}, f32[224,128]{1,0:T(8,128)S(1)}, u32[]{:S(2)}, u32[]{:S(2)}) collective-permute-start(f32[224,128]{1,0:T(8,128)S(1)} %get-tuple-element.76), channel_id=1, source_target_pairs={{0,7},{1,6},{2,5},{3,4},{4,3},{5,2},{6,1},{7,0},{8,15},{9,14},{10,... | collective-permute-start | bytes 344072 | tf_op jit(solution)/shard_map/ppermute | solution.py:476
  61.6 0.0 collective-permute-done.6.refs_6_
  61.6 1.4 %collective-permute-start.22 = (f32[224,128]{1,0:T(8,128)S(1)}, f32[224,128]{1,0:T(8,128)S(1)}, u32[]{:S(2)}, u32[]{:S(2)}) collective-permute-start(f32[224,128]{1,0:T(8,128)S(1)} %get-tuple-element.77), channel_id=1, source_target_pairs={{0,1},{1,0},{2,3},{3,2},{4,5},{5,4},{6,7},{7,6},{8,9},{9,8},{10,11... | collective-permute-start | bytes 344072 | tf_op jit(solution)/shard_map/ppermute | solution.py:476
  63.0 6.1 %collective-permute-done.18.refs_0_ = f32[224,128]{1,0:T(8,128)S(1)} collective-permute-done((f32[224,128]{1,0:T(8,128)S(1)}, f32[224,128]{1,0:T(8,128)S(1)}, u32[]{:S(2)}, u32[]{:S(2)}) %collective-permute-start.18) | collective-permute-done | bytes 114720 | tf_op jit(solution)/shard_map/ppermute | solution.py:476
  69.2 1.8 %table.1 = s32[16]{0:T(128)} custom-call(f32[296,128]{1,0:T(8,128)} %copy-done.6, f32[296,128]{1,0:T(8,128)} %copy-done.8, f32[296,128]{1,0:T(8,128)} %copy-done.10, f32[296,128]{1,0:T(8,128)} %copy-done.12, f32[296,128]{1,0:T(8,128)} %copy-done.14, f32[296,128]{1,0:T(8,128)} %copy-done.16, f32[296,128]{1,0:T(8,128)} %copy-done.18, f32[296,128]{1,0:T(8,128)} %copy-done.4, ...), custom_call_target="tpu_custom_call" | custom-call | tf_op jit(solution)/shard_map/table/pallas_call | solution.py:385
  71.1 0.9 copy-done.11
  72.0 0.9 copy-done.13
  72.9 0.9 copy-done.15
  73.8 0.9 copy-done.17
  74.7 0.9 copy-done.19
  75.6 0.6 copy-done.22
  76.2 0.7 route.2
  76.9 3.0 %collective-permute-start.11 = (f32[2,152,128]{2,1,0:T(8,128)S(1)}, f32[2,152,128]{2,1,0:T(8,128)S(1)}, u32[]{:S(2)}, u32[]{:S(2)}) collective-permute-start(f32[2,152,128]{2,1,0:T(8,128)S(1)} %get-tuple-element.65), channel_id=1, source_target_pairs={{0,4},{1,5},{2,6},{3,7},{4,0},{5,1},{6,2},{7,3},{8,12},{9,13},{10,... | collective-permute-start | bytes 466952 | tf_op jit(solution)/shard_map/ppermute | solution.py:476
  79.9 0.8 collective-permute-start.12
  80.7 2.1 %collective-permute-start.24 = (f32[224,128]{1,0:T(8,128)S(1)}, f32[224,128]{1,0:T(8,128)S(1)}, u32[]{:S(2)}, u32[]{:S(2)}) collective-permute-start(f32[224,128]{1,0:T(8,128)S(1)} %get-tuple-element.79), channel_id=1, source_target_pairs={{0,3},{1,2},{2,1},{3,0},{4,7},{5,6},{6,5},{7,4},{8,11},{9,10},{10,... | collective-permute-start | bytes 344072 | tf_op jit(solution)/shard_map/ppermute | solution.py:476
  82.9 2.4 %collective-permute-start.13 = (f32[2,152,128]{2,1,0:T(8,128)S(1)}, f32[2,152,128]{2,1,0:T(8,128)S(1)}, u32[]{:S(2)}, u32[]{:S(2)}) collective-permute-start(f32[2,152,128]{2,1,0:T(8,128)S(1)} %get-tuple-element.67), channel_id=1, source_target_pairs={{0,6},{1,7},{2,4},{3,5},{4,2},{5,3},{6,0},{7,1},{8,14},{9,15},{10,... | collective-permute-start | bytes 466952 | tf_op jit(solution)/shard_map/ppermute | solution.py:476
  85.2 2.2 %collective-permute-start.14 = (f32[2,152,128]{2,1,0:T(8,128)S(1)}, f32[2,152,128]{2,1,0:T(8,128)S(1)}, u32[]{:S(2)}, u32[]{:S(2)}) collective-permute-start(f32[2,152,128]{2,1,0:T(8,128)S(1)} %get-tuple-element.68), channel_id=1, source_target_pairs={{0,7},{1,6},{2,5},{3,4},{4,3},{5,2},{6,1},{7,0},{8,15},{9,14},{10,... | collective-permute-start | bytes 466952 | tf_op jit(solution)/shard_map/ppermute | solution.py:476
  87.5 2.7 %collective-permute-done.24.refs_6_ = f32[224,128]{1,0:T(8,128)S(1)} collective-permute-done((f32[224,128]{1,0:T(8,128)S(1)}, f32[224,128]{1,0:T(8,128)S(1)}, u32[]{:S(2)}, u32[]{:S(2)}) %collective-permute-start.24) | collective-permute-done | bytes 114720 | tf_op jit(solution)/shard_map/ppermute | solution.py:476
  90.2 1.1 collective-permute-start.15
  91.3 5.1 %collective-permute-done.11.refs_0_ = f32[2,152,128]{2,1,0:T(8,128)S(1)} collective-permute-done((f32[2,152,128]{2,1,0:T(8,128)S(1)}, f32[2,152,128]{2,1,0:T(8,128)S(1)}, u32[]{:S(2)}, u32[]{:S(2)}) %collective-permute-start.11) | collective-permute-done | bytes 155680 | tf_op jit(solution)/shard_map/ppermute | solution.py:476
  96.4 5.4 %collective-permute-done.12.refs_1_ = f32[2,152,128]{2,1,0:T(8,128)S(1)} collective-permute-done((f32[2,152,128]{2,1,0:T(8,128)S(1)}, f32[2,152,128]{2,1,0:T(8,128)S(1)}, u32[]{:S(2)}, u32[]{:S(2)}) %collective-permute-start.12) | collective-permute-done | bytes 155680 | tf_op jit(solution)/shard_map/ppermute | solution.py:476
  101.9 0.6 copy-done.23
  102.5 0.7 route.3
  103.2 3.1 %collective-permute-start.25 = (f32[2,112,128]{2,1,0:T(8,128)S(1)}, f32[2,112,128]{2,1,0:T(8,128)S(1)}, u32[]{:S(2)}, u32[]{:S(2)}) collective-permute-start(f32[2,112,128]{2,1,0:T(8,128)S(1)} %get-tuple-element.80), channel_id=1, source_target_pairs={{0,4},{1,5},{2,6},{3,7},{4,0},{5,1},{6,2},{7,3},{8,12},{9,13},{10,... | collective-permute-start | bytes 344072 | tf_op jit(solution)/shard_map/ppermute | solution.py:476
  106.3 5.3 %collective-permute-start.26 = (f32[2,112,128]{2,1,0:T(8,128)S(1)}, f32[2,112,128]{2,1,0:T(8,128)S(1)}, u32[]{:S(2)}, u32[]{:S(2)}) collective-permute-start(f32[2,112,128]{2,1,0:T(8,128)S(1)} %get-tuple-element.81), channel_id=1, source_target_pairs={{0,5},{1,4},{2,7},{3,6},{4,1},{5,0},{6,3},{7,2},{8,13},{9,12},{10,... | collective-permute-start | bytes 344072 | tf_op jit(solution)/shard_map/ppermute | solution.py:476
  111.6 2.8 %collective-permute-start.27 = (f32[2,112,128]{2,1,0:T(8,128)S(1)}, f32[2,112,128]{2,1,0:T(8,128)S(1)}, u32[]{:S(2)}, u32[]{:S(2)}) collective-permute-start(f32[2,112,128]{2,1,0:T(8,128)S(1)} %get-tuple-element.82), channel_id=1, source_target_pairs={{0,6},{1,7},{2,4},{3,5},{4,2},{5,3},{6,0},{7,1},{8,14},{9,15},{10,... | collective-permute-start | bytes 344072 | tf_op jit(solution)/shard_map/ppermute | solution.py:476
  114.4 2.1 %collective-permute-start.28 = (f32[2,112,128]{2,1,0:T(8,128)S(1)}, f32[2,112,128]{2,1,0:T(8,128)S(1)}, u32[]{:S(2)}, u32[]{:S(2)}) collective-permute-start(f32[2,112,128]{2,1,0:T(8,128)S(1)} %get-tuple-element.83), channel_id=1, source_target_pairs={{0,7},{1,6},{2,5},{3,4},{4,3},{5,2},{6,1},{7,0},{8,15},{9,14},{10,... | collective-permute-start | bytes 344072 | tf_op jit(solution)/shard_map/ppermute | solution.py:476
  116.5 0.4 collective-permute-start.29
  116.9 0.1 collective-permute-start.30
  117.0 6.9 %collective-permute-done.26.refs_9_ = f32[2,112,128]{2,1,0:T(8,128)S(1)} collective-permute-done((f32[2,112,128]{2,1,0:T(8,128)S(1)}, f32[2,112,128]{2,1,0:T(8,128)S(1)}, u32[]{:S(2)}, u32[]{:S(2)}) %collective-permute-start.26) | collective-permute-done | bytes 114720 | tf_op jit(solution)/shard_map/ppermute | solution.py:476
  123.9 0.8 collective-permute-done.30.refs_13_
  124.7 4.9 %collective-permute-done.31.refs_14_ = f32[2,112,128]{2,1,0:T(8,128)S(1)} collective-permute-done((f32[2,112,128]{2,1,0:T(8,128)S(1)}, f32[2,112,128]{2,1,0:T(8,128)S(1)}, u32[]{:S(2)}, u32[]{:S(2)}) %collective-permute-start.31) | collective-permute-done | bytes 114720 | tf_op jit(solution)/shard_map/ppermute | solution.py:476
  129.6 1.5 %settle.1 = (f32[1,2,32,32,128]{4,3,2,1,0:T(8,128)}, f32[1,2,32,32,128]{4,3,2,1,0:T(8,128)}) custom-call(f32[2,152,128]{2,1,0:T(8,128)S(1)} %collective-permute-done.11.refs_0_, f32[2,152,128]{2,1,0:T(8,128)S(1)} %collective-permute-done.12.refs_1_, f32[2,152,128]{2,1,0:T(8,128)S(1)} %collective-permute-done.13.refs_2_, ...), custom_call_target="tpu_custom_call" | custom-call | tf_op jit(solution)/shard_map/settle/pallas_call | solution.py:458
  (64 shorter events, 0.2 us)
Async XLA Ops:
  0.6 1.2 copy-start
  1.9 1.2 copy-start.2
  3.1 0.7 copy-start.24
  3.7 0.7 copy-start.25
  4.4 0.7 copy-start.26
  5.0 0.7 copy-start.27
  5.7 6.7 %copy-start.1 = (f32[1,2,32,32,128]{4,3,2,1,0:T(8,128)S(1)}, f32[1,2,32,32,128]{4,3,2,1,0:T(8,128)}, u32[]{:S(2)}) copy-start(f32[1,2,32,32,128]{4,3,2,1,0:T(8,128)} %phase.3) | copy-start | bytes 3145732
  5.7 6.7 %copy-start.3 = (f32[1,2,32,32,128]{4,3,2,1,0:T(8,128)S(1)}, f32[1,2,32,32,128]{4,3,2,1,0:T(8,128)}, u32[]{:S(2)}) copy-start(f32[1,2,32,32,128]{4,3,2,1,0:T(8,128)} %solute.3) | copy-start | bytes 3145732
  6.3 14.6 %collective-permute-start.7 = (f32[33,8,128]{2,1,0:T(8,128)S(1)}, f32[33,8,128]{2,1,0:T(8,128)S(1)}, u32[]{:S(2)}, u32[]{:S(2)}) collective-permute-start(f32[33,8,128]{2,1,0:T(8,128)S(1)} %get-tuple-element.54), channel_id=1, source_target_pairs={{0,1},{1,2},{2,3},{3,4},{4,5},{5,6},{6,7},{7,0},{8,9},{9,10},{10,1... | collective-permute-start | bytes 405512 | tf_op jit(solution)/shard_map/ppermute | solution.py:485
  9.3 11.5 %collective-permute-start.8 = (f32[33,8,128]{2,1,0:T(8,128)S(1)}, f32[33,8,128]{2,1,0:T(8,128)S(1)}, u32[]{:S(2)}, u32[]{:S(2)}) collective-permute-start(f32[33,8,128]{2,1,0:T(8,128)S(1)} %get-tuple-element.55), channel_id=1, source_target_pairs={{0,7},{1,0},{2,1},{3,2},{4,3},{5,4},{6,5},{7,6},{8,15},{9,8},{10,9... | collective-permute-start | bytes 405512 | tf_op jit(solution)/shard_map/ppermute | solution.py:486
  20.9 0.7 copy-start.4
  21.5 22.2 %collective-permute-start.9 = (f32[608,128]{1,0:T(8,128)S(1)}, f32[608,128]{1,0:T(8,128)S(1)}, u32[]{:S(2)}, u32[]{:S(2)}) collective-permute-start(f32[608,128]{1,0:T(8,128)S(1)} %get-tuple-element.57), channel_id=1, source_target_pairs={{0,8},{8,16},{16,24},{24,0},{1,9},{9,17},{17,25},{25,1},{2,10},{10... | collective-permute-start | bytes 933896 | tf_op jit(solution)/shard_map/ppermute | solution.py:490
  21.5 22.2 %collective-permute-start.10 = (f32[608,128]{1,0:T(8,128)S(1)}, f32[608,128]{1,0:T(8,128)S(1)}, u32[]{:S(2)}, u32[]{:S(2)}) collective-permute-start(f32[608,128]{1,0:T(8,128)S(1)} %get-tuple-element.58), channel_id=1, source_target_pairs={{0,24},{8,0},{16,8},{24,16},{1,25},{9,1},{17,9},{25,17},{2,26},{10... | collective-permute-start | bytes 933896 | tf_op jit(solution)/shard_map/ppermute | solution.py:491
  23.3 15.8 %collective-permute-start = (f32[296,128]{1,0:T(8,128)S(1)}, f32[296,128]{1,0:T(8,128)S(1)}, u32[]{:S(2)}, u32[]{:S(2)}) collective-permute-start(f32[296,128]{1,0:T(8,128)S(1)} %get-tuple-element.46), channel_id=1, source_target_pairs={{0,4},{1,5},{2,6},{3,7},{4,0},{5,1},{6,2},{7,3},{8,12},{9,13},{10,... | collective-permute-start | bytes 454664 | tf_op jit(solution)/shard_map/ppermute | solution.py:476
  24.2 18.2 %collective-permute-start.1 = (f32[296,128]{1,0:T(8,128)S(1)}, f32[296,128]{1,0:T(8,128)S(1)}, u32[]{:S(2)}, u32[]{:S(2)}) collective-permute-start(f32[296,128]{1,0:T(8,128)S(1)} %get-tuple-element.47), channel_id=1, source_target_pairs={{0,5},{1,4},{2,7},{3,6},{4,1},{5,0},{6,3},{7,2},{8,13},{9,12},{10,... | collective-permute-start | bytes 454664 | tf_op jit(solution)/shard_map/ppermute | solution.py:476
  24.6 29.3 %collective-permute-start.2 = (f32[296,128]{1,0:T(8,128)S(1)}, f32[296,128]{1,0:T(8,128)S(1)}, u32[]{:S(2)}, u32[]{:S(2)}) collective-permute-start(f32[296,128]{1,0:T(8,128)S(1)} %get-tuple-element.48), channel_id=1, source_target_pairs={{0,6},{1,7},{2,4},{3,5},{4,2},{5,3},{6,0},{7,1},{8,14},{9,15},{10,... | collective-permute-start | bytes 454664 | tf_op jit(solution)/shard_map/ppermute | solution.py:476
  39.0 14.2 %copy-start.6 = (f32[296,128]{1,0:T(8,128)}, f32[296,128]{1,0:T(8,128)S(1)}, u32[]{:S(2)}) copy-start(f32[296,128]{1,0:T(8,128)S(1)} %collective-permute-done.refs_0_) | copy-start | bytes 454660
  39.0 16.0 %collective-permute-start.3 = (f32[296,128]{1,0:T(8,128)S(1)}, f32[296,128]{1,0:T(8,128)S(1)}, u32[]{:S(2)}, u32[]{:S(2)}) collective-permute-start(f32[296,128]{1,0:T(8,128)S(1)} %get-tuple-element.49), channel_id=1, source_target_pairs={{0,7},{1,6},{2,5},{3,4},{4,3},{5,2},{6,1},{7,0},{8,15},{9,14},{10,... | collective-permute-start | bytes 454664 | tf_op jit(solution)/shard_map/ppermute | solution.py:476
  42.3 10.9 %copy-start.8 = (f32[296,128]{1,0:T(8,128)}, f32[296,128]{1,0:T(8,128)S(1)}, u32[]{:S(2)}) copy-start(f32[296,128]{1,0:T(8,128)S(1)} %collective-permute-done.1.refs_1_) | copy-start | bytes 454660
  42.3 15.4 %collective-permute-start.4 = (f32[296,128]{1,0:T(8,128)S(1)}, f32[296,128]{1,0:T(8,128)S(1)}, u32[]{:S(2)}, u32[]{:S(2)}) collective-permute-start(f32[296,128]{1,0:T(8,128)S(1)} %get-tuple-element.50), channel_id=1, source_target_pairs={{0,1},{1,0},{2,3},{3,2},{4,5},{5,4},{6,7},{7,6},{8,9},{9,8},{10,11... | collective-permute-start | bytes 454664 | tf_op jit(solution)/shard_map/ppermute | solution.py:476
  43.7 16.5 %collective-permute-start.5 = (f32[296,128]{1,0:T(8,128)S(1)}, f32[296,128]{1,0:T(8,128)S(1)}, u32[]{:S(2)}, u32[]{:S(2)}) collective-permute-start(f32[296,128]{1,0:T(8,128)S(1)} %get-tuple-element.51), channel_id=1, source_target_pairs={{0,2},{1,3},{2,0},{3,1},{4,6},{5,7},{6,4},{7,5},{8,10},{9,11},{10,... | collective-permute-start | bytes 454664 | tf_op jit(solution)/shard_map/ppermute | solution.py:476
  43.7 17.9 %collective-permute-start.6 = (f32[296,128]{1,0:T(8,128)S(1)}, f32[296,128]{1,0:T(8,128)S(1)}, u32[]{:S(2)}, u32[]{:S(2)}) collective-permute-start(f32[296,128]{1,0:T(8,128)S(1)} %get-tuple-element.52), channel_id=1, source_target_pairs={{0,3},{1,2},{2,1},{3,0},{4,7},{5,6},{6,5},{7,4},{8,11},{9,10},{10,... | collective-permute-start | bytes 454664 | tf_op jit(solution)/shard_map/ppermute | solution.py:476
  53.2 0.7 copy-start.20
  53.8 17.2 %copy-start.5 = (f32[296,128]{1,0:T(8,128)S(1)}, f32[296,128]{1,0:T(8,128)}, u32[]{:S(2)}) copy-start(f32[296,128]{1,0:T(8,128)} %copy-done.4) | copy-start | bytes 454660
  53.9 15.3 %copy-start.10 = (f32[296,128]{1,0:T(8,128)}, f32[296,128]{1,0:T(8,128)S(1)}, u32[]{:S(2)}) copy-start(f32[296,128]{1,0:T(8,128)S(1)} %collective-permute-done.2.refs_2_) | copy-start | bytes 454660
  53.9 17.2 %copy-start.7 = (f32[296,128]{1,0:T(8,128)S(1)}, f32[296,128]{1,0:T(8,128)}, u32[]{:S(2)}) copy-start(f32[296,128]{1,0:T(8,128)} %copy-done.6) | copy-start | bytes 454660
  53.9 17.2 %copy-start.9 = (f32[296,128]{1,0:T(8,128)S(1)}, f32[296,128]{1,0:T(8,128)}, u32[]{:S(2)}) copy-start(f32[296,128]{1,0:T(8,128)} %copy-done.8) | copy-start | bytes 454660
  53.9 48.0 %copy-start.21 = (f32[224,128]{1,0:T(8,128)S(1)}, f32[224,128]{1,0:T(8,128)}, u32[]{:S(2)}) copy-start(f32[224,128]{1,0:T(8,128)} %copy-done.20) | copy-start | bytes 344068
  53.9 15.3 %collective-permute-start.18 = (f32[224,128]{1,0:T(8,128)S(1)}, f32[224,128]{1,0:T(8,128)S(1)}, u32[]{:S(2)}, u32[]{:S(2)}) collective-permute-start(f32[224,128]{1,0:T(8,128)S(1)} %get-tuple-element.73), channel_id=1, source_target_pairs={{0,4},{1,5},{2,6},{3,7},{4,0},{5,1},{6,2},{7,3},{8,12},{9,13},{10,... | collective-permute-start | bytes 344072 | tf_op jit(solution)/shard_map/ppermute | solution.py:476
  55.0 14.1 %copy-start.12 = (f32[296,128]{1,0:T(8,128)}, f32[296,128]{1,0:T(8,128)S(1)}, u32[]{:S(2)}) copy-start(f32[296,128]{1,0:T(8,128)S(1)} %collective-permute-done.3.refs_3_) | copy-start | bytes 454660
  55.0 21.9 %collective-permute-start.19 = (f32[224,128]{1,0:T(8,128)S(1)}, f32[224,128]{1,0:T(8,128)S(1)}, u32[]{:S(2)}, u32[]{:S(2)}) collective-permute-start(f32[224,128]{1,0:T(8,128)S(1)} %get-tuple-element.74), channel_id=1, source_target_pairs={{0,5},{1,4},{2,7},{3,6},{4,1},{5,0},{6,3},{7,2},{8,13},{9,12},{10,... | collective-permute-start | bytes 344072 | tf_op jit(solution)/shard_map/ppermute | solution.py:476
  57.7 11.4 %copy-start.14 = (f32[296,128]{1,0:T(8,128)}, f32[296,128]{1,0:T(8,128)S(1)}, u32[]{:S(2)}) copy-start(f32[296,128]{1,0:T(8,128)S(1)} %collective-permute-done.4.refs_4_) | copy-start | bytes 454660
  57.7 22.2 %collective-permute-start.20 = (f32[224,128]{1,0:T(8,128)S(1)}, f32[224,128]{1,0:T(8,128)S(1)}, u32[]{:S(2)}, u32[]{:S(2)}) collective-permute-start(f32[224,128]{1,0:T(8,128)S(1)} %get-tuple-element.75), channel_id=1, source_target_pairs={{0,6},{1,7},{2,4},{3,5},{4,2},{5,3},{6,0},{7,1},{8,14},{9,15},{10,... | collective-permute-start | bytes 344072 | tf_op jit(solution)/shard_map/ppermute | solution.py:476
  60.2 8.9 %copy-start.16 = (f32[296,128]{1,0:T(8,128)}, f32[296,128]{1,0:T(8,128)S(1)}, u32[]{:S(2)}) copy-start(f32[296,128]{1,0:T(8,128)S(1)} %collective-permute-done.5.refs_5_) | copy-start | bytes 454660
  60.2 20.5 %collective-permute-start.21 = (f32[224,128]{1,0:T(8,128)S(1)}, f32[224,128]{1,0:T(8,128)S(1)}, u32[]{:S(2)}, u32[]{:S(2)}) collective-permute-start(f32[224,128]{1,0:T(8,128)S(1)} %get-tuple-element.76), channel_id=1, source_target_pairs={{0,7},{1,6},{2,5},{3,4},{4,3},{5,2},{6,1},{7,0},{8,15},{9,14},{10,... | collective-permute-start | bytes 344072 | tf_op jit(solution)/shard_map/ppermute | solution.py:476
  61.6 7.6 %copy-start.18 = (f32[296,128]{1,0:T(8,128)}, f32[296,128]{1,0:T(8,128)S(1)}, u32[]{:S(2)}) copy-start(f32[296,128]{1,0:T(8,128)S(1)} %collective-permute-done.6.refs_6_) | copy-start | bytes 454660
  61.6 21.2 %collective-permute-start.22 = (f32[224,128]{1,0:T(8,128)S(1)}, f32[224,128]{1,0:T(8,128)S(1)}, u32[]{:S(2)}, u32[]{:S(2)}) collective-permute-start(f32[224,128]{1,0:T(8,128)S(1)} %get-tuple-element.77), channel_id=1, source_target_pairs={{0,1},{1,0},{2,3},{3,2},{4,5},{5,4},{6,7},{7,6},{8,9},{9,8},{10,11... | collective-permute-start | bytes 344072 | tf_op jit(solution)/shard_map/ppermute | solution.py:476
  69.1 16.1 %collective-permute-start.23 = (f32[224,128]{1,0:T(8,128)S(1)}, f32[224,128]{1,0:T(8,128)S(1)}, u32[]{:S(2)}, u32[]{:S(2)}) collective-permute-start(f32[224,128]{1,0:T(8,128)S(1)} %get-tuple-element.78), channel_id=1, source_target_pairs={{0,2},{1,3},{2,0},{3,1},{4,6},{5,7},{6,4},{7,5},{8,10},{9,11},{10,... | collective-permute-start | bytes 344072 | tf_op jit(solution)/shard_map/ppermute | solution.py:476
  71.1 0.9 copy-start.11
  72.0 0.9 copy-start.13
  72.9 0.9 copy-start.15
  73.8 0.9 copy-start.17
  74.7 0.9 copy-start.19
  75.6 0.6 copy-start.22
  76.9 19.5 %collective-permute-start.11 = (f32[2,152,128]{2,1,0:T(8,128)S(1)}, f32[2,152,128]{2,1,0:T(8,128)S(1)}, u32[]{:S(2)}, u32[]{:S(2)}) collective-permute-start(f32[2,152,128]{2,1,0:T(8,128)S(1)} %get-tuple-element.65), channel_id=1, source_target_pairs={{0,4},{1,5},{2,6},{3,7},{4,0},{5,1},{6,2},{7,3},{8,12},{9,13},{10,... | collective-permute-start | bytes 466952 | tf_op jit(solution)/shard_map/ppermute | solution.py:476
  79.9 22.0 %collective-permute-start.12 = (f32[2,152,128]{2,1,0:T(8,128)S(1)}, f32[2,152,128]{2,1,0:T(8,128)S(1)}, u32[]{:S(2)}, u32[]{:S(2)}) collective-permute-start(f32[2,152,128]{2,1,0:T(8,128)S(1)} %get-tuple-element.66), channel_id=1, source_target_pairs={{0,5},{1,4},{2,7},{3,6},{4,1},{5,0},{6,3},{7,2},{8,13},{9,12},{10,... | collective-permute-start | bytes 466952 | tf_op jit(solution)/shard_map/ppermute | solution.py:476
  80.7 9.5 %collective-permute-start.24 = (f32[224,128]{1,0:T(8,128)S(1)}, f32[224,128]{1,0:T(8,128)S(1)}, u32[]{:S(2)}, u32[]{:S(2)}) collective-permute-start(f32[224,128]{1,0:T(8,128)S(1)} %get-tuple-element.79), channel_id=1, source_target_pairs={{0,3},{1,2},{2,1},{3,0},{4,7},{5,6},{6,5},{7,4},{8,11},{9,10},{10,... | collective-permute-start | bytes 344072 | tf_op jit(solution)/shard_map/ppermute | solution.py:476
  82.9 20.3 %collective-permute-start.13 = (f32[2,152,128]{2,1,0:T(8,128)S(1)}, f32[2,152,128]{2,1,0:T(8,128)S(1)}, u32[]{:S(2)}, u32[]{:S(2)}) collective-permute-start(f32[2,152,128]{2,1,0:T(8,128)S(1)} %get-tuple-element.67), channel_id=1, source_target_pairs={{0,6},{1,7},{2,4},{3,5},{4,2},{5,3},{6,0},{7,1},{8,14},{9,15},{10,... | collective-permute-start | bytes 466952 | tf_op jit(solution)/shard_map/ppermute | solution.py:476
  85.2 21.1 %collective-permute-start.14 = (f32[2,152,128]{2,1,0:T(8,128)S(1)}, f32[2,152,128]{2,1,0:T(8,128)S(1)}, u32[]{:S(2)}, u32[]{:S(2)}) collective-permute-start(f32[2,152,128]{2,1,0:T(8,128)S(1)} %get-tuple-element.68), channel_id=1, source_target_pairs={{0,7},{1,6},{2,5},{3,4},{4,3},{5,2},{6,1},{7,0},{8,15},{9,14},{10,... | collective-permute-start | bytes 466952 | tf_op jit(solution)/shard_map/ppermute | solution.py:476
  90.2 21.4 %collective-permute-start.15 = (f32[2,152,128]{2,1,0:T(8,128)S(1)}, f32[2,152,128]{2,1,0:T(8,128)S(1)}, u32[]{:S(2)}, u32[]{:S(2)}) collective-permute-start(f32[2,152,128]{2,1,0:T(8,128)S(1)} %get-tuple-element.69), channel_id=1, source_target_pairs={{0,1},{1,0},{2,3},{3,2},{4,5},{5,4},{6,7},{7,6},{8,9},{9,8},{10,11... | collective-permute-start | bytes 466952 | tf_op jit(solution)/shard_map/ppermute | solution.py:476
  96.4 18.0 %collective-permute-start.16 = (f32[2,152,128]{2,1,0:T(8,128)S(1)}, f32[2,152,128]{2,1,0:T(8,128)S(1)}, u32[]{:S(2)}, u32[]{:S(2)}) collective-permute-start(f32[2,152,128]{2,1,0:T(8,128)S(1)} %get-tuple-element.70), channel_id=1, source_target_pairs={{0,2},{1,3},{2,0},{3,1},{4,6},{5,7},{6,4},{7,5},{8,10},{9,11},{10,... | collective-permute-start | bytes 466952 | tf_op jit(solution)/shard_map/ppermute | solution.py:476
  101.9 14.6 %collective-permute-start.17 = (f32[2,152,128]{2,1,0:T(8,128)S(1)}, f32[2,152,128]{2,1,0:T(8,128)S(1)}, u32[]{:S(2)}, u32[]{:S(2)}) collective-permute-start(f32[2,152,128]{2,1,0:T(8,128)S(1)} %get-tuple-element.71), channel_id=1, source_target_pairs={{0,3},{1,2},{2,1},{3,0},{4,7},{5,6},{6,5},{7,4},{8,11},{9,10},{10,... | collective-permute-start | bytes 466952 | tf_op jit(solution)/shard_map/ppermute | solution.py:476
  101.9 0.6 copy-start.23
  103.2 13.7 %collective-permute-start.25 = (f32[2,112,128]{2,1,0:T(8,128)S(1)}, f32[2,112,128]{2,1,0:T(8,128)S(1)}, u32[]{:S(2)}, u32[]{:S(2)}) collective-permute-start(f32[2,112,128]{2,1,0:T(8,128)S(1)} %get-tuple-element.80), channel_id=1, source_target_pairs={{0,4},{1,5},{2,6},{3,7},{4,0},{5,1},{6,2},{7,3},{8,12},{9,13},{10,... | collective-permute-start | bytes 344072 | tf_op jit(solution)/shard_map/ppermute | solution.py:476
  106.3 17.6 %collective-permute-start.26 = (f32[2,112,128]{2,1,0:T(8,128)S(1)}, f32[2,112,128]{2,1,0:T(8,128)S(1)}, u32[]{:S(2)}, u32[]{:S(2)}) collective-permute-start(f32[2,112,128]{2,1,0:T(8,128)S(1)} %get-tuple-element.81), channel_id=1, source_target_pairs={{0,5},{1,4},{2,7},{3,6},{4,1},{5,0},{6,3},{7,2},{8,13},{9,12},{10,... | collective-permute-start | bytes 344072 | tf_op jit(solution)/shard_map/ppermute | solution.py:476
  111.6 12.3 %collective-permute-start.27 = (f32[2,112,128]{2,1,0:T(8,128)S(1)}, f32[2,112,128]{2,1,0:T(8,128)S(1)}, u32[]{:S(2)}, u32[]{:S(2)}) collective-permute-start(f32[2,112,128]{2,1,0:T(8,128)S(1)} %get-tuple-element.82), channel_id=1, source_target_pairs={{0,6},{1,7},{2,4},{3,5},{4,2},{5,3},{6,0},{7,1},{8,14},{9,15},{10,... | collective-permute-start | bytes 344072 | tf_op jit(solution)/shard_map/ppermute | solution.py:476
  114.4 9.5 %collective-permute-start.28 = (f32[2,112,128]{2,1,0:T(8,128)S(1)}, f32[2,112,128]{2,1,0:T(8,128)S(1)}, u32[]{:S(2)}, u32[]{:S(2)}) collective-permute-start(f32[2,112,128]{2,1,0:T(8,128)S(1)} %get-tuple-element.83), channel_id=1, source_target_pairs={{0,7},{1,6},{2,5},{3,4},{4,3},{5,2},{6,1},{7,0},{8,15},{9,14},{10,... | collective-permute-start | bytes 344072 | tf_op jit(solution)/shard_map/ppermute | solution.py:476
  116.5 7.4 %collective-permute-start.29 = (f32[2,112,128]{2,1,0:T(8,128)S(1)}, f32[2,112,128]{2,1,0:T(8,128)S(1)}, u32[]{:S(2)}, u32[]{:S(2)}) collective-permute-start(f32[2,112,128]{2,1,0:T(8,128)S(1)} %get-tuple-element.84), channel_id=1, source_target_pairs={{0,1},{1,0},{2,3},{3,2},{4,5},{5,4},{6,7},{7,6},{8,9},{9,8},{10,11... | collective-permute-start | bytes 344072 | tf_op jit(solution)/shard_map/ppermute | solution.py:476
  116.9 7.8 %collective-permute-start.30 = (f32[2,112,128]{2,1,0:T(8,128)S(1)}, f32[2,112,128]{2,1,0:T(8,128)S(1)}, u32[]{:S(2)}, u32[]{:S(2)}) collective-permute-start(f32[2,112,128]{2,1,0:T(8,128)S(1)} %get-tuple-element.85), channel_id=1, source_target_pairs={{0,2},{1,3},{2,0},{3,1},{4,6},{5,7},{6,4},{7,5},{8,10},{9,11},{10,... | collective-permute-start | bytes 344072 | tf_op jit(solution)/shard_map/ppermute | solution.py:476
  123.9 5.7 %collective-permute-start.31 = (f32[2,112,128]{2,1,0:T(8,128)S(1)}, f32[2,112,128]{2,1,0:T(8,128)S(1)}, u32[]{:S(2)}, u32[]{:S(2)}) collective-permute-start(f32[2,112,128]{2,1,0:T(8,128)S(1)} %get-tuple-element.86), channel_id=1, source_target_pairs={{0,3},{1,2},{2,1},{3,0},{4,7},{5,6},{6,5},{7,4},{8,11},{9,10},{10,... | collective-permute-start | bytes 344072 | tf_op jit(solution)/shard_map/ppermute | solution.py:476

commit v5 on v1

v5 whole, which is shorter than its diff:
```python
import functools

import jax
import jax.numpy as jnp
from jax import lax
from jax.experimental import pallas as pl
from jax.experimental.pallas import tpu as pltpu
from jax.sharding import PartitionSpec as P

NSTEPS = 4
W = NSTEPS
PAD = 8

aniso_strength = 0.05


def pack_y_kernel(under, mobile, spread, owner, phase_lo, phase_hi, solute_lo, solute_hi, to_prev, to_next, own):
    edge, depth = phase_lo.shape[2], phase_lo.shape[4]
    tiles = own.shape[0] // 8 - 1
    to_prev[:edge, :W, :] = phase_lo[0, 0, :, :W, :]
    to_prev[:edge, W:, :] = solute_lo[0, 0, :, :W, :]
    to_next[:edge, :W, :] = phase_hi[0, 0, :, W:, :]
    to_next[:edge, W:, :] = solute_hi[0, 0, :, W:, :]
    line = lax.broadcasted_iota(jnp.int32, (8, depth), 0)
    lane = lax.broadcasted_iota(jnp.int32, (8, depth), 1)
    names = jnp.zeros((8, depth), jnp.float32)
    for tile in range(tiles):
        rows = jnp.zeros((8, depth), jnp.float32)
        for kind, coef in enumerate((under, mobile, spread)):
            rows = jnp.where(line == kind, coef[0, tile], rows)
        own[8 * tile : 8 * tile + 8, :] = rows
        if tile == 0:
            to_prev[edge] = rows
        if tile == tiles - 1:
            to_next[edge] = rows
        names = jnp.where(lane == tile, owner[0, tile].astype(jnp.float32), names)
    own[8 * tiles :, :] = names


def pack_y(phase, solute, coef, owner):
    _, tiles, edge, _, depth = phase.shape
    low = pl.BlockSpec((1, 1, edge, 2 * W, depth), lambda i: (0, 0, 0, 0, 0))
    high = pl.BlockSpec((1, 1, edge, 2 * W, depth), lambda i: (0, tiles - 1, 0, edge // (2 * W) - 1, 0))
    face = jax.ShapeDtypeStruct((edge + 1, 2 * W, depth), jnp.float32)
    own = jax.ShapeDtypeStruct((8 * tiles + 8, depth), jnp.float32)
    whole = pl.BlockSpec((edge + 1, 2 * W, depth), lambda i: (0, 0, 0))
    return pl.pallas_call(
        pack_y_kernel,
        grid=(1,),
        in_specs=[pl.BlockSpec(memory_space=pltpu.SMEM)] * 4 + [low, high, low, high],
        out_specs=[whole, whole, pl.BlockSpec((8 * tiles + 8, depth), lambda i: (0, 0))],
        out_shape=[face, face, own],
        name="pack_y",
    )(*coef, owner, phase, phase, solute, solute)


def fill_row(dst, row, phase_row, solute_row, lo, hi):
    start = PAD
    dst[0][row, start : start + W, :] = lo[:W]
    dst[1][row, start : start + W, :] = lo[W:]
    start += W
    for values in phase_row:
        size = values.shape[0]
        dst[0][row, start : start + size, :] = values
        start += size
    dst[0][row, start : start + W, :] = hi[:W]
    dst[1][row, start : start + W, :] = hi[W:]
    start = PAD + W
    for values in solute_row:
        size = values.shape[0]
        dst[1][row, start : start + size, :] = values
        start += size


def pack_x_kernel(own, phase_lo, phase_hi, solute_lo, solute_hi, y_lo, y_hi, _, to_prev, to_next):
    tiles, edge, depth = phase_lo.shape[1], phase_lo.shape[3], phase_lo.shape[4]
    width = tiles * edge + 2 * W
    for out, phase, solute, first in (
        (to_prev, phase_lo, solute_lo, 0),
        (to_next, phase_hi, solute_hi, edge - W),
    ):
        for row in range(W):
            for field, values, half in ((0, phase, 0), (1, solute, W)):
                at = (2 * row + field) * width
                out[at : at + W, :] = y_lo[first + row, half : half + W, :]
                for tile in range(tiles):
                    begin = at + W + tile * edge
                    out[begin : begin + edge, :] = values[0, tile, row]
                out[at + width - W : at + width, :] = y_hi[first + row, half : half + W, :]
        at = 2 * W * width
        out[at : at + 8, :] = y_lo[edge]
        out[at + 8 : at + 16, :] = y_hi[edge]
        out[at + 16 : at + 16 + 8 * tiles, :] = own[: 8 * tiles, :]


def pack_x(phase, solute, own, y_lo, y_hi, after):
    _, tiles, edge, _, depth = phase.shape
    low = pl.BlockSpec((1, tiles, W, edge, depth), lambda i: (0, 0, 0, 0, 0))
    high = pl.BlockSpec((1, tiles, W, edge, depth), lambda i: (0, 0, edge // W - 1, 0, 0))
    side = pl.BlockSpec((edge + 1, 2 * W, depth), lambda i: (0, 0, 0))
    rows = 2 * W * (tiles * edge + 2 * W) + 8 * (tiles + 2)
    out = jax.ShapeDtypeStruct((rows, depth), jnp.float32)
    whole = pl.BlockSpec((rows, depth), lambda i: (0, 0))
    return pl.pallas_call(
        pack_x_kernel,
        grid=(1,),
        in_specs=[pl.BlockSpec((8 * tiles + 8, depth), lambda i: (0, 0)), low, high, low, high, side, side, pl.BlockSpec(memory_space=pl.ANY)],
        out_specs=[whole, whole],
        out_shape=[out, out],
        compiler_params=pltpu.CompilerParams(vmem_limit_bytes=8 * 1024 * 1024),
        name="pack_x",
    )(own, phase, phase, solute, solute, y_lo, y_hi, after)


def update(near_p, near_u, under, mobile, spread):
    p, p_xl, p_xh, p_yl, p_yh = near_p
    u, u_xl, u_xh, u_yl, u_yh = near_u
    depth = p.shape[-1]
    lane = lax.broadcasted_iota(jnp.int32, p.shape, 1)
    first, last = lane == 0, lane == depth - 1
    p_zl = jnp.where(first, p, pltpu.roll(p, 1, 1))
    p_zh = jnp.where(last, p, pltpu.roll(p, depth - 1, 1))
    u_zl = jnp.where(first, u, pltpu.roll(u, 1, 1))
    u_zh = jnp.where(last, u, pltpu.roll(u, depth - 1, 1))
    dx, dy, dz = p_xh - p_xl, p_yh - p_yl, p_zh - p_zl
    qx, qy, qz = dx * dx, dy * dy, dz * dz
    total = qx + qy + qz
    fourth = qx * qx + qy * qy + qz * qz
    base = total + 4.0
    guess = pl.reciprocal(base, approx=True)
    inverse = guess * (2.0 - base * guess)
    extra = (4.0 * aniso_strength * fourth - (3.0 * aniso_strength) * total * total) * (inverse * inverse)
    lap_p = (p_xl + p_xh) + (p_yl + p_yh) + (p_zl + p_zh) - 6.0 * p
    lap_u = (u_xl + u_xh) + (u_yl + u_yh) + (u_zl + u_zh) - 6.0 * u
    well = 1.0 - p * p
    drive = well * (under + u)
    change = mobile * (lap_p + extra * lap_p + well * (p - 2.0 * drive))
    return p + change, u + spread * lap_u + 0.5 * change


def cells(src_p, src_u, row, start, coefs):
    near = []
    for src in (src_p, src_u):
        near.append(
            (
                src[row, start : start + 8, :],
                src[row - 1, start : start + 8, :],
                src[row + 1, start : start + 8, :],
                src[row, start - 1 : start + 7, :],
                src[row, start + 1 : start + 9, :],
            )
        )
    return update(near[0], near[1], *coefs)


class Plan:
    def __init__(self, pieces, tiles, edge, depth):
        self.pieces, self.tiles, self.edge, self.depth = pieces, tiles, edge, depth
        self.half = pieces // 2
        self.inner = edge - 2 * W
        self.rows = self.inner // self.half
        self.rows_far = (self.inner - 2 * W) // self.half
        self.rows_near = 2 * W // self.half
        self.middle = edge - 16
        self.size = self.rows * self.middle + self.rows_far * 8

    def near_row(self, piece, row, gap):
        index = piece * self.rows_near + row
        return index + jnp.where(index < W, 0, gap)

    def parts(self, far, piece):
        at, found = 0, []
        if far:
            for row in range(self.rows):
                found.append((at, W + piece * self.rows + row, "middle"))
                at += self.middle
            for row in range(self.rows_far):
                found.append((at, 2 * W + piece * self.rows_far + row, "last"))
                at += 8
        else:
            for row in range(self.rows_near):
                found.append((at, self.near_row(piece, row, self.inner), "whole"))
                at += self.edge
            for row in range(self.rows):
                found.append((at, W + piece * self.rows + row, "side"))
                at += 8
            for row in range(self.rows_near):
                found.append((at, W + self.near_row(piece, row, self.inner - 2 * W), "last"))
                at += 8
        assert at == self.size
        return found

    def columns(self, name, tile):
        if name == "whole":
            return 0, self.edge
        if name == "middle":
            return 8, self.middle
        low, high = (tile, 1 - tile) if name == "side" else (1 - tile, tile)
        return low * (self.edge - 8), 8


AUX = 8
UNROLL = 4


def march(first, last, starts, source, target, coefs_of):
    def one_row(row, carry):
        for start in starts:
            new_p, new_u = cells(source[0], source[1], row, start, coefs_of(row, start))
            target[0][row, start : start + 8, :] = new_p
            target[1][row, start : start + 8, :] = new_u
        return carry

    lax.fori_loop(first, last, one_row, 0, unroll=UNROLL)


def inner_kernel(plan, own, phase, solute, *rest):
    half, tiles, edge = plan.half, plan.tiles, plan.edge
    outs, scratch = rest[:half], rest[half:]
    pairs = (scratch[:2], scratch[2:])
    me = lax.axis_index("gy")

    def load_row(row, carry):
        for tile in range(tiles):
            start = PAD + tile * edge
            pairs[0][0][row, start : start + edge, :] = phase[0, tile, row]
            pairs[0][1][row, start : start + edge, :] = solute[0, tile, row]
        return carry

    lax.fori_loop(0, edge, load_row, 0, unroll=UNROLL)

    def coefs_of(row, start):
        tile = (start - PAD) // edge
        return tuple(own[8 * tile + kind : 8 * tile + kind + 1, :] for kind in range(3))

    for step in range(NSTEPS):
        starts = range(PAD, PAD + tiles * edge, 8)
        march(step + 1, edge - step - 1, starts, pairs[step % 2], pairs[(step + 1) % 2], coefs_of)
    for index, out in enumerate(outs):
        piece = lax.rem(me ^ (half + index), half)
        for tile in range(tiles):
            for field, done in enumerate(pairs[NSTEPS % 2]):
                begin = (2 * tile + field) * plan.size
                for at, row, name in plan.parts(True, piece):
                    col, count = plan.columns(name, tile)
                    start = PAD + tile * edge + col
                    out[begin + at : begin + at + count, :] = done[row, start : start + count, :]


def run_inner(plan, own, phase, solute):
    buffer = pltpu.VMEM((plan.edge, plan.tiles * plan.edge + 2 * PAD, plan.depth), jnp.float32)
    vmem = pl.BlockSpec(memory_space=pltpu.VMEM)
    shape = jax.ShapeDtypeStruct((2 * plan.tiles * plan.size, plan.depth), jnp.float32)
    return pl.pallas_call(
        functools.partial(inner_kernel, plan),
        in_specs=[vmem] * 3,
        out_specs=[vmem] * plan.half,
        out_shape=[shape] * plan.half,
        scratch_shapes=[buffer] * 4,
        compiler_params=pltpu.CompilerParams(vmem_limit_bytes=16 * 1024 * 1024),
        cost_estimate=pl.CostEstimate(flops=10**8, bytes_accessed=24 * 1024 * 1024, transcendentals=0),
        name="inner",
    )(own, phase, solute)


def outer_kernel(plan, own, phase, solute, y_lo, y_hi, x_lo, x_hi, partner, out, *scratch):
    tiles, edge, depth, half = plan.tiles, plan.edge, plan.depth, plan.half
    pairs, coefs = (scratch[:2], scratch[2:4]), scratch[4]
    cols = tiles * edge
    width = cols + 2 * W
    for zone, source in ((0, x_lo), (1, None), (2, x_hi)):
        for kind in range(3):
            if source is None:
                parts = [y_lo[edge, kind : kind + 1, :]]
                parts += [own[8 * tile + kind : 8 * tile + kind + 1, :] for tile in range(tiles)]
                parts += [y_hi[edge, kind : kind + 1, :]]
            else:
                at = 2 * W * width + kind
                parts = [source[at : at + 1, :]]
                parts += [source[at + 16 + 8 * tile : at + 17 + 8 * tile, :] for tile in range(tiles)]
                parts += [source[at + 8 : at + 9, :]]
            coefs[zone, kind, :W, :] = jnp.broadcast_to(parts[0], (W, depth))
            for tile in range(tiles):
                begin = W + tile * edge
                coefs[zone, kind, begin : begin + edge, :] = jnp.broadcast_to(parts[1 + tile], (edge, depth))
            coefs[zone, kind, width - W :, :] = jnp.broadcast_to(parts[-1], (W, depth))
    for source, first in ((x_lo, 0), (x_hi, edge + W)):
        for row in range(W):
            for field in range(2):
                at = (2 * row + field) * width
                pairs[0][field][first + row, PAD : PAD + width, :] = source[at : at + width, :]

    def load_row(row, carry):
        fill_row(
            pairs[0],
            W + row,
            [phase[0, tile, row] for tile in range(tiles)],
            [solute[0, tile, row] for tile in range(tiles)],
            y_lo[row],
            y_hi[row],
        )
        return carry

    lax.fori_loop(0, edge, load_row, 0, unroll=UNROLL)

    def coefs_of(zone):
        def found(row, start):
            return tuple(coefs[zone(row), kind, start - PAD : start - PAD + 8, :] for kind in range(3))

        return found

    any_zone = coefs_of(lambda row: jnp.where(row < W, 0, jnp.where(row < W + edge, 1, 2)))
    own_zone = coefs_of(lambda row: 1)

    def blocks(first, last):
        shift = W if step == NSTEPS else 0
        low, high = (first + W - shift) // 8 * 8, -(-(last + W - shift) // 8) * 8
        return list(range(PAD + shift + low, PAD + shift + high, 8))

    for step in range(1, NSTEPS + 1):
        source, target = pairs[(step - 1) % 2], pairs[step % 2]
        left = NSTEPS - step
        strip = W + left
        whole = blocks(-left, cols + left)
        sides = blocks(-left, 8 + left) + blocks(cols - 8 - left, cols + left)
        lasts = []
        for tile in range(tiles):
            col, count = plan.columns("last", tile)
            lasts += blocks(tile * edge + col - left, tile * edge + col + count + left)
        ends = sorted(set(sides + lasts))
        march(W - left, W + strip, whole, source, target, any_zone)
        march(W + strip, W + strip + W, ends, source, target, own_zone)
        march(W + strip + W, W + edge - strip - W, sides, source, target, own_zone)
        march(W + edge - strip - W, W + edge - strip, ends, source, target, own_zone)
        march(W + edge - strip, W + edge + left, whole, source, target, any_zone)
    tail = 2 * tiles * plan.size
    for piece in range(half):
        for tile in range(tiles):
            for field, done in enumerate(pairs[NSTEPS % 2]):
                begin = (2 * tile + field) * plan.size
                for at, row, name in plan.parts(False, piece):
                    col, count = plan.columns(name, tile)
                    start = PAD + W + tile * edge + col
                    out[piece, begin + at : begin + at + count, :] = done[W + row, start : start + count, :]
        out[piece, tail : tail + AUX, :] = own[8 * tiles : 8 * tiles + AUX, :]
        out[piece, tail + AUX : tail + 2 * AUX, :] = partner[...]


def run_outer(plan, own, phase, solute, halos, partner):
    tiles, edge, depth = plan.tiles, plan.edge, plan.depth
    width = tiles * edge + 2 * W
    buffer = pltpu.VMEM((edge + 2 * W, width + 2 * PAD, depth), jnp.float32)
    vmem = pl.BlockSpec(memory_space=pltpu.VMEM)
    return pl.pallas_call(
        functools.partial(outer_kernel, plan),
        in_specs=[vmem] * 8,
        out_specs=vmem,
        out_shape=jax.ShapeDtypeStruct((plan.half, 2 * tiles * plan.size + 2 * AUX, depth), jnp.float32),
        scratch_shapes=[buffer] * 4 + [pltpu.VMEM((3, 3, width, depth), jnp.float32)],
        compiler_params=pltpu.CompilerParams(vmem_limit_bytes=16 * 1024 * 1024),
        cost_estimate=pl.CostEstimate(flops=10**8, bytes_accessed=40 * 1024 * 1024, transcendentals=0),
        name="outer",
    )(own, phase, solute, *halos, partner)


def table_kernel(plan, near, table, names, count, sems):
    pieces, tiles, half = plan.pieces, plan.tiles, plan.half
    me = lax.axis_index("gy")
    base = me - lax.rem(me, half)
    tail = 2 * tiles * plan.size
    copies = []
    for piece in range(half):
        for index in range(2):
            copy = pltpu.make_async_copy(
                near.at[piece, pl.ds(tail + index * AUX, 1), :], names.at[index, piece], sems.at[index, piece]
            )
            copy.start()
            copies.append(copy)
    for peer in range(pieces):
        count[peer] = 0
    for copy in copies:
        copy.wait()
    for home in range(pieces):
        other = (home // half != base // half).astype(jnp.int32)
        for tile in range(tiles):
            peer = lax.rem(names[other, home % half, 0, tile].astype(jnp.int32), pieces)
            slot = count[peer]
            table[peer * tiles + slot] = home * tiles + tile
            count[peer] = slot + 1


def find_table(plan, near):
    return pl.pallas_call(
        functools.partial(table_kernel, plan),
        in_specs=[pl.BlockSpec(memory_space=pl.ANY)],
        out_specs=pl.BlockSpec(memory_space=pltpu.SMEM),
        out_shape=jax.ShapeDtypeStruct((plan.pieces * plan.tiles,), jnp.int32),
        scratch_shapes=[
            pltpu.SMEM((2, plan.half, 1, plan.depth), jnp.float32),
            pltpu.SMEM((plan.pieces,), jnp.int32),
            pltpu.SemaphoreType.DMA((2, plan.half)),
        ],
        name="table",
    )(near)


def route_kernel(plan, table, near, *refs):
    tiles, half, size = plan.tiles, plan.half, 2 * plan.size
    far, near_out, far_outs, held = refs[:half], refs[half], refs[half + 1 : 2 * half + 1], refs[-1]
    me = lax.axis_index("gy")
    base = me - lax.rem(me, half)
    for piece in range(half):
        for tile in range(tiles):
            held[(base + piece) * tiles + tile] = near[piece, tile * size : (tile + 1) * size, :]
    for index in range(half):
        for tile in range(tiles):
            held[(me ^ (half + index)) * tiles + tile] = far[index][tile * size : (tile + 1) * size, :]
    for index in range(half):
        for slot in range(tiles):
            far_outs[index][slot] = held[table[(me ^ (half + index)) * tiles + slot]]
            near_out[index, slot] = held[table[(base + index) * tiles + slot]]


def route(plan, table, near, far):
    tiles, half, size, depth = plan.tiles, plan.half, 2 * plan.size, plan.depth
    vmem = pl.BlockSpec(memory_space=pltpu.VMEM)
    one = jax.ShapeDtypeStruct((tiles, size, depth), jnp.float32)
    results = pl.pallas_call(
        functools.partial(route_kernel, plan),
        in_specs=[pl.BlockSpec(memory_space=pltpu.SMEM)] + [vmem] * (half + 1),
        out_specs=[vmem] * (half + 1),
        out_shape=[jax.ShapeDtypeStruct((half, tiles, size, depth), jnp.float32)] + [one] * half,
        scratch_shapes=[pltpu.VMEM((plan.pieces * tiles, size, depth), jnp.float32)],
        compiler_params=pltpu.CompilerParams(vmem_limit_bytes=16 * 1024 * 1024),
        name="route",
    )(table, near, *far)
    return results[0], results[1:]


def settle_kernel(plan, table, near, *refs):
    tiles, half = plan.tiles, plan.half
    far, outs = refs[:half], refs[half:]
    me = lax.axis_index("gy")
    mine = lax.rem(me, half)
    for slot in range(tiles):
        home = table[me * tiles + slot]
        tile = lax.rem(home, tiles)
        at_home = home // (tiles * half) == me // half

        def put(source, piece, is_far, slot=slot, tile=tile):
            for field, out in enumerate(outs):
                for at, row, name in plan.parts(is_far, piece):
                    col, count = plan.columns(name, tile)
                    if not isinstance(col, int):
                        col = pl.multiple_of(col, 8)
                    out[0, slot, row, pl.ds(col, count), :] = source[
                        slot, field * plan.size + at : field * plan.size + at + count, :
                    ]

        def put_all(same, put=put):
            for index in range(half):
                put(near.at[index], index, not same)
                put(far[index], mine ^ index, same)

        @pl.when(at_home)
        def _(put_all=put_all):
            put_all(True)

        @pl.when(jnp.logical_not(at_home))
        def _(put_all=put_all):
            put_all(False)


def settle(plan, table, near, far):
    out = jax.ShapeDtypeStruct((1, plan.tiles, plan.edge, plan.edge, plan.depth), jnp.float32)
    vmem = pl.BlockSpec(memory_space=pltpu.VMEM)
    return pl.pallas_call(
        functools.partial(settle_kernel, plan),
        in_specs=[pl.BlockSpec(memory_space=pltpu.SMEM)] + [vmem] * (plan.half + 1),
        out_specs=[vmem, vmem],
        out_shape=[out, out],
        compiler_params=pltpu.CompilerParams(vmem_limit_bytes=16 * 1024 * 1024),
        name="settle",
    )(table, near, *far)


def ring(axis, step):
    count = lax.axis_size(axis)
    return [(i, (i + step) % count) for i in range(count)]


def swap(values, mask):
    return lax.ppermute(values, "gy", [(i, i ^ mask) for i in range(lax.axis_size("gy"))])


def among_half(plan, values):
    groups = [list(range(plan.half)), list(range(plan.half, plan.pieces))]
    return lax.all_to_all(values, "gy", 0, 0, axis_index_groups=groups, tiled=True)


def per_device(phase, solute, undercool, mobility, diffusivity, owner):
    _, tiles, edge, _, depth = phase.shape
    plan = Plan(lax.axis_size("gy"), tiles, edge, depth)
    half = plan.half
    to_prev, to_next, own = pack_y(phase, solute, (undercool, mobility, diffusivity), owner)
    y_lo = lax.ppermute(to_next, "gy", ring("gy", 1))
    y_hi = lax.ppermute(to_prev, "gy", ring("gy", -1))
    first = run_inner(plan, own, phase, solute)
    far = [swap(values, half + index) for index, values in enumerate(first)]
    partner = swap(own[8 * tiles :], half)
    to_prev, to_next = pack_x(phase, solute, own, y_lo, y_hi, first[0])
    x_lo = lax.ppermute(to_next, "gx", ring("gx", 1))
    x_hi = lax.ppermute(to_prev, "gx", ring("gx", -1))
    near = run_outer(plan, own, phase, solute, (y_lo, y_hi, x_lo, x_hi), partner)
    near = among_half(plan, near)
    table = find_table(plan, near)
    near, far = route(plan, table, near, far)
    far = [swap(values, half + index) for index, values in enumerate(far)]
    near = among_half(plan, near)
    return tuple(settle(plan, table, near, far))


def solution(mesh):
    tile_spec = P("gx", "gy", None, None, None)
    in_specs = (tile_spec, tile_spec) + (P("gx", "gy"),) * 4
    out_spec = P(("gx", "gy"), None, None, None, None)
    return jax.shard_map(
        per_device, mesh=mesh, in_specs=in_specs, out_specs=(out_spec, out_spec), check_vma=False
    )
```

time: 287 us -> 147 us (0.51)
  Pallas kernels: 152 us -> 25.8 us
  blocking collectives: 108 us -> 0 us
  waiting for transfers between devices: 13.6 us -> 83.6 us
  starting transfers between devices: 4.72 us -> 33.2 us
    pallas_call x4 -> x6, Pallas kernels: 151 us -> 23.7 us  [the longest x1 10.1 us: run_outer(): pl.pallas_call(functools.partial(outer_kernel, plan), in_specs=[vmem] * 8...]
    all_to_all x2 -> x0, blocking collectives: 108 us -> none  [the longest x1 55.1 us: per_device(): spread = lax.all_to_all(cut, 'gy', split_axis=0, concat_axis=0, tiled=True)]
    ppermute x0 -> x9, waiting for transfers between devices: none -> 70.4 us  [swap(): lax.ppermute(values, 'gy', [(i, i ^ mask) for i in range(lax.axis_size('g...]
    ppermute x0 -> x9, starting transfers between devices: none -> 16.1 us  [swap(): lax.ppermute(values, 'gy', [(i, i ^ mask) for i in range(lax.axis_size('g...]
    all_to_all x0 -> x2, starting transfers between devices: none -> 12.4 us  [among_half(): lax.all_to_all(values, 'gy', 0, 0, axis_index_groups=groups, tiled=True)]
    all_to_all x0 -> x2, waiting for transfers between devices: none -> 10.7 us  [among_half(): lax.all_to_all(values, 'gy', 0, 0, axis_index_groups=groups, tiled=True)]
    ppermute x1, waiting for transfers between devices: 6.27 us -> 1.55 us  [per_device(): x_lo = lax.ppermute(to_next, 'gx', ring('gx', 1))]
    ppermute x1, waiting for transfers between devices: 4.62 us -> 0.01 us  [per_device(): y_lo = lax.ppermute(to_next, 'gy', ring('gy', 1))]
  transfers between devices with their start and end apart: 4 -> 15, of which waited for: 4 -> 11; matrix products, arithmetic and copies ran while one was open for 0% -> 0% of each run, Pallas kernels for 0% -> 7%
where the time goes in v5:
time: 147 us
  waiting for transfers between devices  83.6 us (57%)
  starting transfers between devices  33.2 us (23%)
  Pallas kernels  25.8 us (18%)
  local copies, waits for them, and re-layouts  3.62 us (2%)
    ppermute x9, waiting for transfers between devices, swap(): lax.ppermute(values, 'gy', [(i, i ^ mask) for i in range(lax.axis_size('g...  70.4 us
    ppermute x9, starting transfers between devices, swap(): lax.ppermute(values, 'gy', [(i, i ^ mask) for i in range(lax.axis_size('g...  16.1 us
    all_to_all x2, starting transfers between devices, among_half(): lax.all_to_all(values, 'gy', 0, 0, axis_index_groups=groups, tiled=True)  12.4 us
    all_to_all x2, waiting for transfers between devices, among_half(): lax.all_to_all(values, 'gy', 0, 0, axis_index_groups=groups, tiled=True)  10.7 us
    pallas_call x1, Pallas kernels, run_outer(): pl.pallas_call(functools.partial(outer_kernel, plan), in_specs=[vmem] * 8...  10.1 us
    pallas_call x1, Pallas kernels, run_inner(): pl.pallas_call(functools.partial(inner_kernel, plan), in_specs=[vmem] * 3...  8.35 us
    unnamed x14, local copies, waits for them, and re-layouts  3.62 us
  transfers between devices with their start and end apart: 15, of which 11 were waited for; matrix products, arithmetic and copies ran while one was open for 0% of the time, Pallas kernels for 7%

profile of v5, /device:TPU:8, one launch (start us, length us, event | category | flops | bytes accessed | tf_op | source)
XLA Modules:
  0.0 146.9 jit_solution(9652900208118196051)
XLA Ops:
  0.6 0.0 copy-start.1
  0.6 0.0 copy-start
  0.7 2.0 %pack_y.1 = (f32[33,8,128]{2,1,0:T(8,128)}, f32[33,8,128]{2,1,0:T(8,128)}, f32[24,128]{1,0:T(8,128)}) custom-call(f32[1,2]{1,0:T(1,128)} %under.1, f32[1,2]{1,0:T(1,128)} %mobile.1, f32[1,2]{1,0:T(1,128)} %spread.1, s32[1,2]{1,0:T(1,128)} %owner.1, f32[1,2,32,32,128]{4,3,2,1,0:T(8,128)} %phase.3, f32[1,2,32,32,128]{4,3,2,1,0:T(8,128)} %phase.3, ...), custom_call_target="tpu_custom_call" | custom-call | tf_op jit(solution)/shard_map/pack_y/pallas_call | solution.py:47
  2.7 1.5 %collective-permute-start = (f32[33,8,128]{2,1,0:T(8,128)}, f32[33,8,128]{2,1,0:T(8,128)S(1)}, u32[]{:S(2)}, u32[]{:S(2)}) collective-permute-start(f32[33,8,128]{2,1,0:T(8,128)} %get-tuple-element.17), channel_id=1, source_target_pairs={{0,1},{1,2},{2,3},{3,4},{4,5},{5,6},{6,7},{7,0},{8,9},{9,10},{10,1... | collective-permute-start | bytes 405512 | tf_op jit(solution)/shard_map/ppermute | solution.py:506
  4.2 1.4 collective-permute-start.1
  5.6 0.0 copy-done.1
  5.6 0.0 copy-done
  5.6 0.0 copy-start.4
  5.6 0.7 copy-done.4
  6.3 8.3 %inner.1 = (f32[512,128]{1,0:T(8,128)S(1)}, f32[512,128]{1,0:T(8,128)S(1)}, f32[512,128]{1,0:T(8,128)S(1)}, f32[512,128]{1,0:T(8,128)S(1)}) custom-call(f32[24,128]{1,0:T(8,128)S(1)} %copy-done.4, f32[1,2,32,32,128]{4,3,2,1,0:T(8,128)S(1)} %copy-done, f32[1,2,32,32,128]{4,3,2,1,0:T(8,128)S(1)} %copy-done.1), custom_call_target="tpu_custom_call" | custom-call | flops 100000000 | bytes 25165824 | tf_op jit(solution)/shard_map/inner/pallas_call | solution.py:254
  14.7 0.0 collective-permute-done.y_lo
  14.7 0.0 collective-permute-done.1.y_hi
  14.7 0.1 collective-permute-start.2
  14.8 1.7 %collective-permute-start.3 = (f32[608,128]{1,0:T(8,128)S(1)}, f32[608,128]{1,0:T(8,128)S(1)}, u32[]{:S(2)}, u32[]{:S(2)}) collective-permute-start(f32[608,128]{1,0:T(8,128)S(1)} %get-tuple-element.21), channel_id=1, source_target_pairs={{0,24},{8,0},{16,8},{24,16},{1,25},{9,1},{17,9},{25,17},{2,26},{10... | collective-permute-start | bytes 933896 | tf_op jit(solution)/shard_map/ppermute | solution.py:513
  16.5 2.6 %collective-permute-start.4 = (f32[8,128]{1,0:T(8,128)S(1)}, f32[8,128]{1,0:T(8,128)S(1)}, u32[]{:S(2)}, u32[]{:S(2)}) collective-permute-start(f32[8,128]{1,0:T(8,128)S(1)} %slice.3), channel_id=1, source_target_pairs={{0,4},{1,5},{2,6},{3,7},{4,0},{5,1},{6,2},{7,3},{8,12},{9,13},{10,... | collective-permute-start | bytes 12296 | tf_op jit(solution)/shard_map/ppermute | solution.py:493
  19.1 1.9 %collective-permute-done.4.partner = f32[8,128]{1,0:T(8,128)S(1)} collective-permute-done((f32[8,128]{1,0:T(8,128)S(1)}, f32[8,128]{1,0:T(8,128)S(1)}, u32[]{:S(2)}, u32[]{:S(2)}) %collective-permute-start.4) | collective-permute-done | bytes 4128 | tf_op jit(solution)/shard_map/ppermute | solution.py:493
  21.0 1.5 %collective-permute-done.2.x_lo = f32[608,128]{1,0:T(8,128)S(1)} collective-permute-done((f32[608,128]{1,0:T(8,128)S(1)}, f32[608,128]{1,0:T(8,128)S(1)}, u32[]{:S(2)}, u32[]{:S(2)}) %collective-permute-start.2) | collective-permute-done | bytes 311328 | tf_op jit(solution)/shard_map/ppermute | solution.py:512
  22.6 0.9 collective-permute-done.3.x_hi
  23.5 10.1 %outer.1 = f32[4,528,128]{2,1,0:T(8,128)} custom-call(f32[24,128]{1,0:T(8,128)S(1)} %copy-done.4, f32[1,2,32,32,128]{4,3,2,1,0:T(8,128)S(1)} %copy-done, f32[1,2,32,32,128]{4,3,2,1,0:T(8,128)S(1)} %copy-done.1, f32[33,8,128]{2,1,0:T(8,128)S(1)} %collective-permute-done.y_lo, f32[33,8,128]{2,1,0:T(8,128)S(1)} %collective-permute-done.1.y_hi, ...), custom_call_target="tpu_custom_call" | custom-call | flops 100000000 | bytes 41943040 | tf_op jit(solution)/shard_map/outer/pallas_call | solution.py:354
  33.5 5.7 %all-to-all-start = ((f32[4,528,128]{2,1,0:T(8,128)}), f32[4,528,128]{2,1,0:T(8,128)S(1)}, u32[]{:S(2)}, u32[]{:S(2)}) async-start(f32[4,528,128]{2,1,0:T(8,128)} %outer.1), calls=%async_computation | async-start | bytes 2162688 | tf_op jit(solution)/shard_map/all_to_all | solution.py:498
  39.3 1.7 %collective-permute-start.6 = (f32[512,128]{1,0:T(8,128)S(1)}, f32[512,128]{1,0:T(8,128)S(1)}, u32[]{:S(2)}, u32[]{:S(2)}) collective-permute-start(f32[512,128]{1,0:T(8,128)S(1)} %get-tuple-element.22), channel_id=1, source_target_pairs={{0,5},{1,4},{2,7},{3,6},{4,1},{5,0},{6,3},{7,2},{8,13},{9,12},{10,... | collective-permute-start | bytes 786440 | tf_op jit(solution)/shard_map/ppermute | solution.py:493
  41.0 1.2 collective-permute-start.7
  42.2 0.8 collective-permute-start.8
  43.0 3.9 %collective-permute-start.5 = (f32[512,128]{1,0:T(8,128)S(1)}, f32[512,128]{1,0:T(8,128)S(1)}, u32[]{:S(2)}, u32[]{:S(2)}) collective-permute-start(f32[512,128]{1,0:T(8,128)S(1)} %get-tuple-element.19._), channel_id=1, source_target_pairs={{0,4},{1,5},{2,6},{3,7},{4,0},{5,1},{6,2},{7,3},{8,12},{9,13},{10,... | collective-permute-start | bytes 786440 | tf_op jit(solution)/shard_map/ppermute | solution.py:493
  46.9 10.7 %all-to-all-done.near = f32[4,528,128]{2,1,0:T(8,128)S(1)} async-done(((f32[4,528,128]{2,1,0:T(8,128)}), f32[4,528,128]{2,1,0:T(8,128)S(1)}, u32[]{:S(2)}, u32[]{:S(2)}) %all-to-all-start) | async-done | bytes 1081376 | tf_op jit(solution)/shard_map/all_to_all | solution.py:498
  57.6 0.0 copy-start.2
  57.6 1.0 copy-done.2
  58.7 1.4 table.1
  60.1 0.0 collective-permute-done.6.refs_1_
  60.1 17.3 %collective-permute-done.7.refs_2_ = f32[512,128]{1,0:T(8,128)S(1)} collective-permute-done((f32[512,128]{1,0:T(8,128)S(1)}, f32[512,128]{1,0:T(8,128)S(1)}, u32[]{:S(2)}, u32[]{:S(2)}) %collective-permute-start.7) | collective-permute-done | bytes 262176 | tf_op jit(solution)/shard_map/ppermute | solution.py:493
  77.4 5.3 %collective-permute-done.8.refs_3_ = f32[512,128]{1,0:T(8,128)S(1)} collective-permute-done((f32[512,128]{1,0:T(8,128)S(1)}, f32[512,128]{1,0:T(8,128)S(1)}, u32[]{:S(2)}, u32[]{:S(2)}) %collective-permute-start.8) | collective-permute-done | bytes 262176 | tf_op jit(solution)/shard_map/ppermute | solution.py:493
  82.7 3.9 %collective-permute-done.5.refs_0_ = f32[512,128]{1,0:T(8,128)S(1)} collective-permute-done((f32[512,128]{1,0:T(8,128)S(1)}, f32[512,128]{1,0:T(8,128)S(1)}, u32[]{:S(2)}, u32[]{:S(2)}) %collective-permute-start.5) | collective-permute-done | bytes 262176 | tf_op jit(solution)/shard_map/ppermute | solution.py:493
  86.6 0.0 copy-start.3
  86.6 1.2 copy-done.3
  87.8 0.0 copy-start.5
  87.8 0.7 copy-done.5
  88.5 1.8 %route.1 = (f32[4,2,256,128]{3,2,1,0:T(8,128)}, f32[2,256,128]{2,1,0:T(8,128)S(1)}, f32[2,256,128]{2,1,0:T(8,128)S(1)}, f32[2,256,128]{2,1,0:T(8,128)S(1)}, f32[2,256,128]{2,1,0:T(8,128)S(1)}) custom-call(s32[16]{0:T(128)S(1)} %copy-done.5, f32[4,528,128]{2,1,0:T(8,128)S(1)} %copy-done.3, f32[512,128]{1,0:T(8,128)S(1)} %collective-permute-done.5.refs_0_, ...), custom_call_target="tpu_custom_call" | custom-call | tf_op jit(solution)/shard_map/route/pallas_call | solution.py:428
  90.3 0.0 copy-start.6
  90.3 6.7 %all-to-all-start.1 = ((f32[4,2,256,128]{3,2,1,0:T(8,128)}), f32[4,2,256,128]{3,2,1,0:T(8,128)S(1)}, u32[]{:S(2)}, u32[]{:S(2)}) async-start(f32[4,2,256,128]{3,2,1,0:T(8,128)} %get-tuple-element.25), calls=%async_computation.1 | async-start | bytes 2097152 | tf_op jit(solution)/shard_map/all_to_all | solution.py:498
  96.9 0.4 collective-permute-start.9
  97.4 3.4 %collective-permute-start.10 = (f32[2,256,128]{2,1,0:T(8,128)S(1)}, f32[2,256,128]{2,1,0:T(8,128)S(1)}, u32[]{:S(2)}, u32[]{:S(2)}) collective-permute-start(f32[2,256,128]{2,1,0:T(8,128)S(1)} %get-tuple-element.27), channel_id=1, source_target_pairs={{0,5},{1,4},{2,7},{3,6},{4,1},{5,0},{6,3},{7,2},{8,13},{9,12},{10,... | collective-permute-start | bytes 786440 | tf_op jit(solution)/shard_map/ppermute | solution.py:493
  100.8 0.0 collective-permute-start.11
  100.8 2.0 %collective-permute-start.12 = (f32[2,256,128]{2,1,0:T(8,128)S(1)}, f32[2,256,128]{2,1,0:T(8,128)S(1)}, u32[]{:S(2)}, u32[]{:S(2)}) collective-permute-start(f32[2,256,128]{2,1,0:T(8,128)S(1)} %get-tuple-element.29), channel_id=1, source_target_pairs={{0,7},{1,6},{2,5},{3,4},{4,3},{5,2},{6,1},{7,0},{8,15},{9,14},{10,... | collective-permute-start | bytes 786440 | tf_op jit(solution)/shard_map/ppermute | solution.py:493
  102.8 13.2 %collective-permute-done.9.refs_0_ = f32[2,256,128]{2,1,0:T(8,128)S(1)} collective-permute-done((f32[2,256,128]{2,1,0:T(8,128)S(1)}, f32[2,256,128]{2,1,0:T(8,128)S(1)}, u32[]{:S(2)}, u32[]{:S(2)}) %collective-permute-start.9) | collective-permute-done | bytes 262176 | tf_op jit(solution)/shard_map/ppermute | solution.py:493
  116.0 16.2 %collective-permute-done.10.refs_1_ = f32[2,256,128]{2,1,0:T(8,128)S(1)} collective-permute-done((f32[2,256,128]{2,1,0:T(8,128)S(1)}, f32[2,256,128]{2,1,0:T(8,128)S(1)}, u32[]{:S(2)}, u32[]{:S(2)}) %collective-permute-start.10) | collective-permute-done | bytes 262176 | tf_op jit(solution)/shard_map/ppermute | solution.py:493
  132.2 7.2 %collective-permute-done.11.refs_2_ = f32[2,256,128]{2,1,0:T(8,128)S(1)} collective-permute-done((f32[2,256,128]{2,1,0:T(8,128)S(1)}, f32[2,256,128]{2,1,0:T(8,128)S(1)}, u32[]{:S(2)}, u32[]{:S(2)}) %collective-permute-start.11) | collective-permute-done | bytes 262176 | tf_op jit(solution)/shard_map/ppermute | solution.py:493
  139.4 5.4 %collective-permute-done.12.refs_3_ = f32[2,256,128]{2,1,0:T(8,128)S(1)} collective-permute-done((f32[2,256,128]{2,1,0:T(8,128)S(1)}, f32[2,256,128]{2,1,0:T(8,128)S(1)}, u32[]{:S(2)}, u32[]{:S(2)}) %collective-permute-start.12) | collective-permute-done | bytes 262176 | tf_op jit(solution)/shard_map/ppermute | solution.py:493
  144.8 0.0 all-to-all-done.1.near
  144.8 0.0 copy-done.6
  144.8 2.1 %settle.1 = (f32[1,2,32,32,128]{4,3,2,1,0:T(8,128)}, f32[1,2,32,32,128]{4,3,2,1,0:T(8,128)}) custom-call(s32[16]{0:T(128)S(1)} %copy-done.6, f32[4,2,256,128]{3,2,1,0:T(8,128)S(1)} %all-to-all-done.1.near, f32[2,256,128]{2,1,0:T(8,128)S(1)} %collective-permute-done.9.refs_0_, f32[2,256,128]{2,1,0:T(8,128)S(1)} %collective-permute-done.10.refs_1_, ...), custom_call_target="tpu_custom_call" | custom-call | tf_op jit(solution)/shard_map/settle/pallas_call | solution.py:477
  (2 shorter events, 0.1 us)
Async XLA Ops:
  0.6 5.0 %copy-start.1 = (f32[1,2,32,32,128]{4,3,2,1,0:T(8,128)S(1)}, f32[1,2,32,32,128]{4,3,2,1,0:T(8,128)}, u32[]{:S(2)}) copy-start(f32[1,2,32,32,128]{4,3,2,1,0:T(8,128)} %solute.3) | copy-start | bytes 3145732
  0.6 5.0 %copy-start = (f32[1,2,32,32,128]{4,3,2,1,0:T(8,128)S(1)}, f32[1,2,32,32,128]{4,3,2,1,0:T(8,128)}, u32[]{:S(2)}) copy-start(f32[1,2,32,32,128]{4,3,2,1,0:T(8,128)} %phase.3) | copy-start | bytes 3145732
  2.7 12.0 %collective-permute-start = (f32[33,8,128]{2,1,0:T(8,128)}, f32[33,8,128]{2,1,0:T(8,128)S(1)}, u32[]{:S(2)}, u32[]{:S(2)}) collective-permute-start(f32[33,8,128]{2,1,0:T(8,128)} %get-tuple-element.17), channel_id=1, source_target_pairs={{0,1},{1,2},{2,3},{3,4},{4,5},{5,6},{6,7},{7,0},{8,9},{9,10},{10,1... | collective-permute-start | bytes 405512 | tf_op jit(solution)/shard_map/ppermute | solution.py:506
  4.2 10.5 %collective-permute-start.1 = (f32[33,8,128]{2,1,0:T(8,128)}, f32[33,8,128]{2,1,0:T(8,128)S(1)}, u32[]{:S(2)}, u32[]{:S(2)}) collective-permute-start(f32[33,8,128]{2,1,0:T(8,128)} %get-tuple-element.18), channel_id=1, source_target_pairs={{0,7},{1,0},{2,1},{3,2},{4,3},{5,4},{6,5},{7,6},{8,15},{9,8},{10,9... | collective-permute-start | bytes 405512 | tf_op jit(solution)/shard_map/ppermute | solution.py:507
  5.6 0.7 copy-start.4
  14.7 7.9 %collective-permute-start.2 = (f32[608,128]{1,0:T(8,128)S(1)}, f32[608,128]{1,0:T(8,128)S(1)}, u32[]{:S(2)}, u32[]{:S(2)}) collective-permute-start(f32[608,128]{1,0:T(8,128)S(1)} %get-tuple-element.20), channel_id=1, source_target_pairs={{0,8},{8,16},{16,24},{24,0},{1,9},{9,17},{17,25},{25,1},{2,10},{10... | collective-permute-start | bytes 933896 | tf_op jit(solution)/shard_map/ppermute | solution.py:512
  14.8 8.7 %collective-permute-start.3 = (f32[608,128]{1,0:T(8,128)S(1)}, f32[608,128]{1,0:T(8,128)S(1)}, u32[]{:S(2)}, u32[]{:S(2)}) collective-permute-start(f32[608,128]{1,0:T(8,128)S(1)} %get-tuple-element.21), channel_id=1, source_target_pairs={{0,24},{8,0},{16,8},{24,16},{1,25},{9,1},{17,9},{25,17},{2,26},{10... | collective-permute-start | bytes 933896 | tf_op jit(solution)/shard_map/ppermute | solution.py:513
  16.5 4.5 %collective-permute-start.4 = (f32[8,128]{1,0:T(8,128)S(1)}, f32[8,128]{1,0:T(8,128)S(1)}, u32[]{:S(2)}, u32[]{:S(2)}) collective-permute-start(f32[8,128]{1,0:T(8,128)S(1)} %slice.3), channel_id=1, source_target_pairs={{0,4},{1,5},{2,6},{3,7},{4,0},{5,1},{6,2},{7,3},{8,12},{9,13},{10,... | collective-permute-start | bytes 12296 | tf_op jit(solution)/shard_map/ppermute | solution.py:493
  33.5 24.1 %all-to-all-start = ((f32[4,528,128]{2,1,0:T(8,128)}), f32[4,528,128]{2,1,0:T(8,128)S(1)}, u32[]{:S(2)}, u32[]{:S(2)}) async-start(f32[4,528,128]{2,1,0:T(8,128)} %outer.1), calls=%async_computation | async-start | bytes 2162688 | tf_op jit(solution)/shard_map/all_to_all | solution.py:498
  39.3 20.8 %collective-permute-start.6 = (f32[512,128]{1,0:T(8,128)S(1)}, f32[512,128]{1,0:T(8,128)S(1)}, u32[]{:S(2)}, u32[]{:S(2)}) collective-permute-start(f32[512,128]{1,0:T(8,128)S(1)} %get-tuple-element.22), channel_id=1, source_target_pairs={{0,5},{1,4},{2,7},{3,6},{4,1},{5,0},{6,3},{7,2},{8,13},{9,12},{10,... | collective-permute-start | bytes 786440 | tf_op jit(solution)/shard_map/ppermute | solution.py:493
  41.0 36.5 %collective-permute-start.7 = (f32[512,128]{1,0:T(8,128)S(1)}, f32[512,128]{1,0:T(8,128)S(1)}, u32[]{:S(2)}, u32[]{:S(2)}) collective-permute-start(f32[512,128]{1,0:T(8,128)S(1)} %get-tuple-element.23), channel_id=1, source_target_pairs={{0,6},{1,7},{2,4},{3,5},{4,2},{5,3},{6,0},{7,1},{8,14},{9,15},{10,... | collective-permute-start | bytes 786440 | tf_op jit(solution)/shard_map/ppermute | solution.py:493
  42.2 40.5 %collective-permute-start.8 = (f32[512,128]{1,0:T(8,128)S(1)}, f32[512,128]{1,0:T(8,128)S(1)}, u32[]{:S(2)}, u32[]{:S(2)}) collective-permute-start(f32[512,128]{1,0:T(8,128)S(1)} %get-tuple-element.24), channel_id=1, source_target_pairs={{0,7},{1,6},{2,5},{3,4},{4,3},{5,2},{6,1},{7,0},{8,15},{9,14},{10,... | collective-permute-start | bytes 786440 | tf_op jit(solution)/shard_map/ppermute | solution.py:493
  43.0 43.6 %collective-permute-start.5 = (f32[512,128]{1,0:T(8,128)S(1)}, f32[512,128]{1,0:T(8,128)S(1)}, u32[]{:S(2)}, u32[]{:S(2)}) collective-permute-start(f32[512,128]{1,0:T(8,128)S(1)} %get-tuple-element.19._), channel_id=1, source_target_pairs={{0,4},{1,5},{2,6},{3,7},{4,0},{5,1},{6,2},{7,3},{8,12},{9,13},{10,... | collective-permute-start | bytes 786440 | tf_op jit(solution)/shard_map/ppermute | solution.py:493
  57.6 1.0 copy-start.2
  86.6 1.2 copy-start.3
  87.8 0.7 copy-start.5
  90.3 54.5 %copy-start.6 = (s32[16]{0:T(128)S(1)}, s32[16]{0:T(128)}, u32[]{:S(2)}) copy-start(s32[16]{0:T(128)} %table.1) | copy-start | bytes 196
  90.3 54.5 %all-to-all-start.1 = ((f32[4,2,256,128]{3,2,1,0:T(8,128)}), f32[4,2,256,128]{3,2,1,0:T(8,128)S(1)}, u32[]{:S(2)}, u32[]{:S(2)}) async-start(f32[4,2,256,128]{3,2,1,0:T(8,128)} %get-tuple-element.25), calls=%async_computation.1 | async-start | bytes 2097152 | tf_op jit(solution)/shard_map/all_to_all | solution.py:498
  96.9 19.1 %collective-permute-start.9 = (f32[2,256,128]{2,1,0:T(8,128)S(1)}, f32[2,256,128]{2,1,0:T(8,128)S(1)}, u32[]{:S(2)}, u32[]{:S(2)}) collective-permute-start(f32[2,256,128]{2,1,0:T(8,128)S(1)} %get-tuple-element.26), channel_id=1, source_target_pairs={{0,4},{1,5},{2,6},{3,7},{4,0},{5,1},{6,2},{7,3},{8,12},{9,13},{10,... | collective-permute-start | bytes 786440 | tf_op jit(solution)/shard_map/ppermute | solution.py:493
  97.4 34.8 %collective-permute-start.10 = (f32[2,256,128]{2,1,0:T(8,128)S(1)}, f32[2,256,128]{2,1,0:T(8,128)S(1)}, u32[]{:S(2)}, u32[]{:S(2)}) collective-permute-start(f32[2,256,128]{2,1,0:T(8,128)S(1)} %get-tuple-element.27), channel_id=1, source_target_pairs={{0,5},{1,4},{2,7},{3,6},{4,1},{5,0},{6,3},{7,2},{8,13},{9,12},{10,... | collective-permute-start | bytes 786440 | tf_op jit(solution)/shard_map/ppermute | solution.py:493
  100.8 38.6 %collective-permute-start.11 = (f32[2,256,128]{2,1,0:T(8,128)S(1)}, f32[2,256,128]{2,1,0:T(8,128)S(1)}, u32[]{:S(2)}, u32[]{:S(2)}) collective-permute-start(f32[2,256,128]{2,1,0:T(8,128)S(1)} %get-tuple-element.28), channel_id=1, source_target_pairs={{0,6},{1,7},{2,4},{3,5},{4,2},{5,3},{6,0},{7,1},{8,14},{9,15},{10,... | collective-permute-start | bytes 786440 | tf_op jit(solution)/shard_map/ppermute | solution.py:493
  100.8 44.0 %collective-permute-start.12 = (f32[2,256,128]{2,1,0:T(8,128)S(1)}, f32[2,256,128]{2,1,0:T(8,128)S(1)}, u32[]{:S(2)}, u32[]{:S(2)}) collective-permute-start(f32[2,256,128]{2,1,0:T(8,128)S(1)} %get-tuple-element.29), channel_id=1, source_target_pairs={{0,7},{1,6},{2,5},{3,4},{4,3},{5,2},{6,1},{7,0},{8,15},{9,14},{10,... | collective-permute-start | bytes 786440 | tf_op jit(solution)/shard_map/ppermute | solution.py:493

commit v6 on v5

--- a/solution.py
+++ b/solution.py
@@ -493,9 +493,20 @@
     return lax.ppermute(values, "gy", [(i, i ^ mask) for i in range(lax.axis_size("gy"))])
 
 
-def among_half(plan, values):
-    groups = [list(range(plan.half)), list(range(plan.half, plan.pieces))]
-    return lax.all_to_all(values, "gy", 0, 0, axis_index_groups=groups, tiled=True)
+def among_half(plan, values, together):
+    def at_once(values):
+        groups = [list(range(plan.half)), list(range(plan.half, plan.pieces))]
+        return lax.all_to_all(values, "gy", 0, 0, axis_index_groups=groups, tiled=True)
+
+    def pairwise(values):
+        mine = lax.rem(lax.axis_index("gy"), plan.half)
+        found = values
+        for mask in range(1, plan.half):
+            moved = swap(lax.dynamic_index_in_dim(values, mine ^ mask, 0, keepdims=False), mask)
+            found = lax.dynamic_update_index_in_dim(found, moved, mine ^ mask, 0)
+        return found
+
+    return lax.cond(together, at_once, pairwise, values)
 
 
 def per_device(phase, solute, undercool, mobility, diffusivity, owner):
@@ -512,11 +523,12 @@
     x_lo = lax.ppermute(to_next, "gx", ring("gx", 1))
     x_hi = lax.ppermute(to_prev, "gx", ring("gx", -1))
     near = run_outer(plan, own, phase, solute, (y_lo, y_hi, x_lo, x_hi), partner)
-    near = among_half(plan, near)
+    together = owner[0, 0] >= 0
+    near = among_half(plan, near, together)
     table = find_table(plan, near)
     near, far = route(plan, table, near, far)
     far = [swap(values, half + index) for index, values in enumerate(far)]
-    near = among_half(plan, near)
+    near = among_half(plan, near, together)
     return tuple(settle(plan, table, near, far))
 
 

time: 147 us -> 133 us (0.905)
  waiting for transfers between devices: 83.6 us -> 28.9 us
  blocking collectives: 0 us -> 54.1 us
  starting transfers between devices: 33.2 us -> 17.8 us
    all_to_all x0 -> x2, blocking collectives: none -> 54.1 us  [at_once(): lax.all_to_all(values, 'gy', 0, 0, axis_index_groups=groups, tiled=True)]
    ppermute x9, waiting for transfers between devices: 70.4 us -> 28.1 us  [swap(): lax.ppermute(values, 'gy', [(i, i ^ mask) for i in range(lax.axis_size('g...]
    all_to_all x2 -> x0, starting transfers between devices: 12.4 us -> none  [among_half(): lax.all_to_all(values, 'gy', 0, 0, axis_index_groups=groups, tiled=True)]
    all_to_all x2 -> x0, waiting for transfers between devices: 10.7 us -> none  [among_half(): lax.all_to_all(values, 'gy', 0, 0, axis_index_groups=groups, tiled=True)]
    ppermute x9, starting transfers between devices: 16.1 us -> 13.1 us  [swap(): lax.ppermute(values, 'gy', [(i, i ^ mask) for i in range(lax.axis_size('g...]
    cond x0 -> x4, local copies, waits for them, and re-layouts: none -> 2.46 us
    unnamed x14 -> x16, local copies, waits for them, and re-layouts: 3.62 us -> 1.36 us
    ppermute x1, waiting for transfers between devices: 1.55 us -> 0.01 us  [per_device(): x_lo = lax.ppermute(to_next, 'gx', ring('gx', 1))]
  transfers between devices with their start and end apart: 15 -> 13, of which waited for: 11 -> 6; matrix products, arithmetic and copies ran while one was open for 0% -> 0% of each run, Pallas kernels for 7% -> 16%
where the time goes in v6:
time: 133 us
  blocking collectives  54.1 us (41%)
  waiting for transfers between devices  28.9 us (22%)
  Pallas kernels  27.2 us (20%)
  starting transfers between devices  17.8 us (13%)
  local copies, waits for them, and re-layouts  3.82 us (3%)
    all_to_all x2, blocking collectives, at_once(): lax.all_to_all(values, 'gy', 0, 0, axis_index_groups=groups, tiled=True)  54.1 us
    ppermute x9, waiting for transfers between devices, swap(): lax.ppermute(values, 'gy', [(i, i ^ mask) for i in range(lax.axis_size('g...  28.1 us
    ppermute x9, starting transfers between devices, swap(): lax.ppermute(values, 'gy', [(i, i ^ mask) for i in range(lax.axis_size('g...  13.1 us
    pallas_call x1, Pallas kernels, run_outer(): pl.pallas_call(functools.partial(outer_kernel, plan), in_specs=[vmem] * 8...  10 us
    pallas_call x1, Pallas kernels, run_inner(): pl.pallas_call(functools.partial(inner_kernel, plan), in_specs=[vmem] * 3...  9.14 us
    pallas_call x1, Pallas kernels, settle(): pl.pallas_call(functools.partial(settle_kernel, plan), in_specs=[pl.Block...  2.77 us
  transfers between devices with their start and end apart: 13, of which 6 were waited for; matrix products, arithmetic and copies ran while one was open for 0% of the time, Pallas kernels for 16%

profile of v6, /device:TPU:8, one launch (start us, length us, event | category | flops | bytes accessed | tf_op | source)
XLA Modules:
  0.0 132.7 jit_solution(14007057210832339178)
XLA Ops:
  0.6 0.0 copy-start.1
  0.6 0.0 copy-start
  0.7 2.0 %pack_y.1 = (f32[33,8,128]{2,1,0:T(8,128)}, f32[33,8,128]{2,1,0:T(8,128)}, f32[24,128]{1,0:T(8,128)}) custom-call(f32[1,2]{1,0:T(1,128)} %under.1, f32[1,2]{1,0:T(1,128)} %mobile.1, f32[1,2]{1,0:T(1,128)} %spread.1, s32[1,2]{1,0:T(1,128)} %owner.1, f32[1,2,32,32,128]{4,3,2,1,0:T(8,128)} %phase.3, f32[1,2,32,32,128]{4,3,2,1,0:T(8,128)} %phase.3, ...), custom_call_target="tpu_custom_call" | custom-call | tf_op jit(solution)/shard_map/pack_y/pallas_call | solution.py:47
  2.7 1.5 %collective-permute-start.6 = (f32[33,8,128]{2,1,0:T(8,128)}, f32[33,8,128]{2,1,0:T(8,128)S(1)}, u32[]{:S(2)}, u32[]{:S(2)}) collective-permute-start(f32[33,8,128]{2,1,0:T(8,128)} %get-tuple-element.27), channel_id=1, source_target_pairs={{0,1},{1,2},{2,3},{3,4},{4,5},{5,6},{6,7},{7,0},{8,9},{9,10},{10,1... | collective-permute-start | bytes 405512 | tf_op jit(solution)/shard_map/ppermute | solution.py:517
  4.2 1.4 %collective-permute-start.7 = (f32[33,8,128]{2,1,0:T(8,128)}, f32[33,8,128]{2,1,0:T(8,128)S(1)}, u32[]{:S(2)}, u32[]{:S(2)}) collective-permute-start(f32[33,8,128]{2,1,0:T(8,128)} %get-tuple-element.28), channel_id=1, source_target_pairs={{0,7},{1,0},{2,1},{3,2},{4,3},{5,4},{6,5},{7,6},{8,15},{9,8},{10,9... | collective-permute-start | bytes 405512 | tf_op jit(solution)/shard_map/ppermute | solution.py:518
  5.6 0.0 copy-done.1
  5.6 0.0 copy-done
  5.6 0.0 copy-start.2
  5.6 0.7 copy-done.2
  6.3 9.1 %inner.1 = (f32[512,128]{1,0:T(8,128)S(1)}, f32[512,128]{1,0:T(8,128)}, f32[512,128]{1,0:T(8,128)}, f32[512,128]{1,0:T(8,128)S(1)}) custom-call(f32[24,128]{1,0:T(8,128)S(1)} %copy-done.2, f32[1,2,32,32,128]{4,3,2,1,0:T(8,128)S(1)} %copy-done, f32[1,2,32,32,128]{4,3,2,1,0:T(8,128)S(1)} %copy-done.1), custom_call_target="tpu_custom_call" | custom-call | flops 100000000 | bytes 25165824 | tf_op jit(solution)/shard_map/inner/pallas_call | solution.py:254
  15.5 0.0 collective-permute-done.6.y_lo
  15.5 0.0 collective-permute-done.7.y_hi
  15.5 0.0 copy-start.9
  15.5 0.0 copy-start.3
  15.5 0.1 collective-permute-start.8
  15.6 1.7 %collective-permute-start.9 = (f32[608,128]{1,0:T(8,128)S(1)}, f32[608,128]{1,0:T(8,128)S(1)}, u32[]{:S(2)}, u32[]{:S(2)}) collective-permute-start(f32[608,128]{1,0:T(8,128)S(1)} %get-tuple-element.31), channel_id=1, source_target_pairs={{0,24},{8,0},{16,8},{24,16},{1,25},{9,1},{17,9},{25,17},{2,26},{10... | collective-permute-start | bytes 933896 | tf_op jit(solution)/shard_map/ppermute | solution.py:524
  17.3 2.6 %collective-permute-start.10 = (f32[8,128]{1,0:T(8,128)S(1)}, f32[8,128]{1,0:T(8,128)S(1)}, u32[]{:S(2)}, u32[]{:S(2)}) collective-permute-start(f32[8,128]{1,0:T(8,128)S(1)} %slice.7), channel_id=1, source_target_pairs={{0,4},{1,5},{2,6},{3,7},{4,0},{5,1},{6,2},{7,3},{8,12},{9,13},{10,... | collective-permute-start | bytes 12296 | tf_op jit(solution)/shard_map/ppermute | solution.py:493
  19.9 0.4 collective-permute-start.12
  20.3 1.6 %collective-permute-start.13 = (f32[512,128]{1,0:T(8,128)}, f32[512,128]{1,0:T(8,128)S(1)}, u32[]{:S(2)}, u32[]{:S(2)}) collective-permute-start(f32[512,128]{1,0:T(8,128)} %get-tuple-element.33), channel_id=1, source_target_pairs={{0,6},{1,7},{2,4},{3,5},{4,2},{5,3},{6,0},{7,1},{8,14},{9,15},{10,... | collective-permute-start | bytes 786440 | tf_op jit(solution)/shard_map/ppermute | solution.py:493
  21.9 0.0 copy-done.9
  21.9 0.0 collective-permute-done.10.partner
  21.9 1.5 %collective-permute-start.14 = (f32[512,128]{1,0:T(8,128)S(1)}, f32[512,128]{1,0:T(8,128)S(1)}, u32[]{:S(2)}, u32[]{:S(2)}) collective-permute-start(f32[512,128]{1,0:T(8,128)S(1)} %get-tuple-element.34), channel_id=1, source_target_pairs={{0,7},{1,6},{2,5},{3,4},{4,3},{5,2},{6,1},{7,0},{8,15},{9,14},{10,... | collective-permute-start | bytes 786440 | tf_op jit(solution)/shard_map/ppermute | solution.py:493
  23.5 0.0 collective-permute-done.8.x_lo
  23.5 0.8 collective-permute-done.9.x_hi
  24.3 0.0 copy-done.3
  24.3 10.0 %outer.1 = f32[4,528,128]{2,1,0:T(8,128)} custom-call(f32[24,128]{1,0:T(8,128)S(1)} %copy-done.3, f32[1,2,32,32,128]{4,3,2,1,0:T(8,128)S(1)} %copy-done, f32[1,2,32,32,128]{4,3,2,1,0:T(8,128)S(1)} %copy-done.1, f32[33,8,128]{2,1,0:T(8,128)S(1)} %collective-permute-done.6.y_lo, f32[33,8,128]{2,1,0:T(8,128)S(1)} %collective-permute-done.7.y_hi, ...), custom_call_target="tpu_custom_call" | custom-call | flops 100000000 | bytes 41943040 | tf_op jit(solution)/shard_map/outer/pallas_call | solution.py:354
  34.3 31.3 %conditional.2 = (f32[4,528,128]{2,1,0:T(8,128)}) conditional(s32[]{:T(128)} %bitcast.12, f32[4,528,128]{2,1,0:T(8,128)} %outer.1, f32[4,528,128]{2,1,0:T(8,128)} %outer.1), branch_computations={%region_0.1_spmd, %region_1.2_spmd} | conditional | flops 20 | bytes 6488437 | solution.py:509
  34.3 0.0 copy-start.7
  34.3 1.2 copy-done.7
  35.5 30.0 %all_to_all.8 = f32[4,528,128]{2,1,0:T(8,128)} all-to-all(f32[4,528,128]{2,1,0:T(8,128)S(1)} %copy-done.7), channel_id=1, replica_groups={{0,1,2,3},{4,5,6,7},{8,9,10,11},{12,13,14,15},{16,17,18,19},{20,21,22,2..., dimensions={0} | all-to-all | bytes 2162688 | tf_op jit(solution)/shard_map/cond/branch_1_fun/all_to_all | solution.py:499
  65.6 0.0 copy-start.6
  65.6 1.2 collective-permute-start.11
  66.8 1.4 %table.1 = s32[16]{0:T(128)} custom-call(f32[4,528,128]{2,1,0:T(8,128)} %get-tuple-element.46.near), custom_call_target="tpu_custom_call" | custom-call | tf_op jit(solution)/shard_map/table/pallas_call | solution.py:393
  68.2 0.0 collective-permute-done.12.refs_1_
  68.2 0.0 collective-permute-done.13.refs_2_
  68.2 0.0 collective-permute-done.14.refs_3_
  68.2 6.1 %collective-permute-done.11.refs_0_ = f32[512,128]{1,0:T(8,128)S(1)} collective-permute-done((f32[512,128]{1,0:T(8,128)S(1)}, f32[512,128]{1,0:T(8,128)S(1)}, u32[]{:S(2)}, u32[]{:S(2)}) %collective-permute-start.11) | collective-permute-done | bytes 262176 | tf_op jit(solution)/shard_map/ppermute | solution.py:493
  74.4 0.0 copy-done.6
  74.4 0.0 copy-start.4
  74.4 0.6 copy-done.4
  75.0 1.8 %route.1 = (f32[4,2,256,128]{3,2,1,0:T(8,128)}, f32[2,256,128]{2,1,0:T(8,128)S(1)}, f32[2,256,128]{2,1,0:T(8,128)S(1)}, f32[2,256,128]{2,1,0:T(8,128)S(1)}, f32[2,256,128]{2,1,0:T(8,128)S(1)}) custom-call(s32[16]{0:T(128)S(1)} %copy-done.4, f32[4,528,128]{2,1,0:T(8,128)S(1)} %copy-done.6, f32[512,128]{1,0:T(8,128)S(1)} %collective-permute-done.11.refs_0_, ...), custom_call_target="tpu_custom_call" | custom-call | tf_op jit(solution)/shard_map/route/pallas_call | solution.py:428
  76.8 0.0 copy-start.5
  76.8 25.3 %conditional.3 = (f32[4,2,256,128]{3,2,1,0:T(8,128)}) conditional(s32[]{:T(128)} %bitcast.12, f32[4,2,256,128]{3,2,1,0:T(8,128)} %get-tuple-element.35, f32[4,2,256,128]{3,2,1,0:T(8,128)} %get-tuple-element.35), branch_computations={%region_2.3_spmd, %region_3.4_spmd} | conditional | flops 20 | bytes 6291829 | solution.py:509
  76.8 0.0 copy-start.8
  76.8 1.2 copy-done.8
  78.0 24.1 %all_to_all.9 = f32[4,2,256,128]{3,2,1,0:T(8,128)} all-to-all(f32[4,2,256,128]{3,2,1,0:T(8,128)S(1)} %copy-done.8), channel_id=1, replica_groups={{0,1,2,3},{4,5,6,7},{8,9,10,11},{12,13,14,15},{16,17,18,19},{20,21,22,2..., dimensions={0} | all-to-all | bytes 2097152 | tf_op jit(solution)/shard_map/cond/branch_1_fun/all_to_all | solution.py:499
  102.1 1.1 collective-permute-start.15
  103.2 2.7 %collective-permute-start.16 = (f32[2,256,128]{2,1,0:T(8,128)S(1)}, f32[2,256,128]{2,1,0:T(8,128)S(1)}, u32[]{:S(2)}, u32[]{:S(2)}) collective-permute-start(f32[2,256,128]{2,1,0:T(8,128)S(1)} %get-tuple-element.37), channel_id=1, source_target_pairs={{0,5},{1,4},{2,7},{3,6},{4,1},{5,0},{6,3},{7,2},{8,13},{9,12},{10,... | collective-permute-start | bytes 786440 | tf_op jit(solution)/shard_map/ppermute | solution.py:493
  105.9 1.1 collective-permute-start.17
  107.0 0.9 collective-permute-start.18
  107.9 10.4 %collective-permute-done.15.refs_0_ = f32[2,256,128]{2,1,0:T(8,128)S(1)} collective-permute-done((f32[2,256,128]{2,1,0:T(8,128)S(1)}, f32[2,256,128]{2,1,0:T(8,128)S(1)}, u32[]{:S(2)}, u32[]{:S(2)}) %collective-permute-start.15) | collective-permute-done | bytes 262176 | tf_op jit(solution)/shard_map/ppermute | solution.py:493
  118.3 2.8 %collective-permute-done.16.refs_1_ = f32[2,256,128]{2,1,0:T(8,128)S(1)} collective-permute-done((f32[2,256,128]{2,1,0:T(8,128)S(1)}, f32[2,256,128]{2,1,0:T(8,128)S(1)}, u32[]{:S(2)}, u32[]{:S(2)}) %collective-permute-start.16) | collective-permute-done | bytes 262176 | tf_op jit(solution)/shard_map/ppermute | solution.py:493
  121.1 5.1 %collective-permute-done.17.refs_2_ = f32[2,256,128]{2,1,0:T(8,128)S(1)} collective-permute-done((f32[2,256,128]{2,1,0:T(8,128)S(1)}, f32[2,256,128]{2,1,0:T(8,128)S(1)}, u32[]{:S(2)}, u32[]{:S(2)}) %collective-permute-start.17) | collective-permute-done | bytes 262176 | tf_op jit(solution)/shard_map/ppermute | solution.py:493
  126.2 3.7 %collective-permute-done.18.refs_3_ = f32[2,256,128]{2,1,0:T(8,128)S(1)} collective-permute-done((f32[2,256,128]{2,1,0:T(8,128)S(1)}, f32[2,256,128]{2,1,0:T(8,128)S(1)}, u32[]{:S(2)}, u32[]{:S(2)}) %collective-permute-start.18) | collective-permute-done | bytes 262176 | tf_op jit(solution)/shard_map/ppermute | solution.py:493
  129.9 0.0 copy-done.5
  129.9 2.8 %settle.1 = (f32[1,2,32,32,128]{4,3,2,1,0:T(8,128)}, f32[1,2,32,32,128]{4,3,2,1,0:T(8,128)}) custom-call(s32[16]{0:T(128)S(1)} %copy-done.5, f32[4,2,256,128]{3,2,1,0:T(8,128)} %get-tuple-element.47.near, f32[2,256,128]{2,1,0:T(8,128)S(1)} %collective-permute-done.15.refs_0_, f32[2,256,128]{2,1,0:T(8,128)S(1)} %collective-permute-done.16.refs_1_, ...), custom_call_target="tpu_custom_call" | custom-call | tf_op jit(solution)/shard_map/settle/pallas_call | solution.py:477
  (2 shorter events, 0.1 us)
Async XLA Ops:
  0.6 5.0 %copy-start.1 = (f32[1,2,32,32,128]{4,3,2,1,0:T(8,128)S(1)}, f32[1,2,32,32,128]{4,3,2,1,0:T(8,128)}, u32[]{:S(2)}) copy-start(f32[1,2,32,32,128]{4,3,2,1,0:T(8,128)} %solute.3) | copy-start | bytes 3145732
  0.6 5.0 %copy-start = (f32[1,2,32,32,128]{4,3,2,1,0:T(8,128)S(1)}, f32[1,2,32,32,128]{4,3,2,1,0:T(8,128)}, u32[]{:S(2)}) copy-start(f32[1,2,32,32,128]{4,3,2,1,0:T(8,128)} %phase.3) | copy-start | bytes 3145732
  2.7 12.8 %collective-permute-start.6 = (f32[33,8,128]{2,1,0:T(8,128)}, f32[33,8,128]{2,1,0:T(8,128)S(1)}, u32[]{:S(2)}, u32[]{:S(2)}) collective-permute-start(f32[33,8,128]{2,1,0:T(8,128)} %get-tuple-element.27), channel_id=1, source_target_pairs={{0,1},{1,2},{2,3},{3,4},{4,5},{5,6},{6,7},{7,0},{8,9},{9,10},{10,1... | collective-permute-start | bytes 405512 | tf_op jit(solution)/shard_map/ppermute | solution.py:517
  4.2 11.3 %collective-permute-start.7 = (f32[33,8,128]{2,1,0:T(8,128)}, f32[33,8,128]{2,1,0:T(8,128)S(1)}, u32[]{:S(2)}, u32[]{:S(2)}) collective-permute-start(f32[33,8,128]{2,1,0:T(8,128)} %get-tuple-element.28), channel_id=1, source_target_pairs={{0,7},{1,0},{2,1},{3,2},{4,3},{5,4},{6,5},{7,6},{8,15},{9,8},{10,9... | collective-permute-start | bytes 405512 | tf_op jit(solution)/shard_map/ppermute | solution.py:518
  5.6 0.7 copy-start.2
  15.5 6.4 %copy-start.9 = (s32[1,2]{1,0:T(1,128)S(1)}, s32[1,2]{1,0:T(1,128)}, u32[]{:S(2)}) copy-start(s32[1,2]{1,0:T(1,128)} %owner.1) | copy-start | bytes 28
  15.5 8.8 %copy-start.3 = (f32[24,128]{1,0:T(8,128)S(1)}, f32[24,128]{1,0:T(8,128)}, u32[]{:S(2)}) copy-start(f32[24,128]{1,0:T(8,128)} %get-tuple-element.26.own) | copy-start | bytes 36868
  15.5 7.9 %collective-permute-start.8 = (f32[608,128]{1,0:T(8,128)S(1)}, f32[608,128]{1,0:T(8,128)S(1)}, u32[]{:S(2)}, u32[]{:S(2)}) collective-permute-start(f32[608,128]{1,0:T(8,128)S(1)} %get-tuple-element.30), channel_id=1, source_target_pairs={{0,8},{8,16},{16,24},{24,0},{1,9},{9,17},{17,25},{25,1},{2,10},{10... | collective-permute-start | bytes 933896 | tf_op jit(solution)/shard_map/ppermute | solution.py:523
  15.6 8.7 %collective-permute-start.9 = (f32[608,128]{1,0:T(8,128)S(1)}, f32[608,128]{1,0:T(8,128)S(1)}, u32[]{:S(2)}, u32[]{:S(2)}) collective-permute-start(f32[608,128]{1,0:T(8,128)S(1)} %get-tuple-element.31), channel_id=1, source_target_pairs={{0,24},{8,0},{16,8},{24,16},{1,25},{9,1},{17,9},{25,17},{2,26},{10... | collective-permute-start | bytes 933896 | tf_op jit(solution)/shard_map/ppermute | solution.py:524
  17.3 4.6 %collective-permute-start.10 = (f32[8,128]{1,0:T(8,128)S(1)}, f32[8,128]{1,0:T(8,128)S(1)}, u32[]{:S(2)}, u32[]{:S(2)}) collective-permute-start(f32[8,128]{1,0:T(8,128)S(1)} %slice.7), channel_id=1, source_target_pairs={{0,4},{1,5},{2,6},{3,7},{4,0},{5,1},{6,2},{7,3},{8,12},{9,13},{10,... | collective-permute-start | bytes 12296 | tf_op jit(solution)/shard_map/ppermute | solution.py:493
  19.9 48.3 %collective-permute-start.12 = (f32[512,128]{1,0:T(8,128)}, f32[512,128]{1,0:T(8,128)S(1)}, u32[]{:S(2)}, u32[]{:S(2)}) collective-permute-start(f32[512,128]{1,0:T(8,128)} %get-tuple-element.32), channel_id=1, source_target_pairs={{0,5},{1,4},{2,7},{3,6},{4,1},{5,0},{6,3},{7,2},{8,13},{9,12},{10,... | collective-permute-start | bytes 786440 | tf_op jit(solution)/shard_map/ppermute | solution.py:493
  20.3 47.9 %collective-permute-start.13 = (f32[512,128]{1,0:T(8,128)}, f32[512,128]{1,0:T(8,128)S(1)}, u32[]{:S(2)}, u32[]{:S(2)}) collective-permute-start(f32[512,128]{1,0:T(8,128)} %get-tuple-element.33), channel_id=1, source_target_pairs={{0,6},{1,7},{2,4},{3,5},{4,2},{5,3},{6,0},{7,1},{8,14},{9,15},{10,... | collective-permute-start | bytes 786440 | tf_op jit(solution)/shard_map/ppermute | solution.py:493
  21.9 46.3 %collective-permute-start.14 = (f32[512,128]{1,0:T(8,128)S(1)}, f32[512,128]{1,0:T(8,128)S(1)}, u32[]{:S(2)}, u32[]{:S(2)}) collective-permute-start(f32[512,128]{1,0:T(8,128)S(1)} %get-tuple-element.34), channel_id=1, source_target_pairs={{0,7},{1,6},{2,5},{3,4},{4,3},{5,2},{6,1},{7,0},{8,15},{9,14},{10,... | collective-permute-start | bytes 786440 | tf_op jit(solution)/shard_map/ppermute | solution.py:493
  34.3 1.2 copy-start.7
  65.6 8.8 %copy-start.6 = (f32[4,528,128]{2,1,0:T(8,128)S(1)}, f32[4,528,128]{2,1,0:T(8,128)}, u32[]{:S(2)}) copy-start(f32[4,528,128]{2,1,0:T(8,128)} %get-tuple-element.46.near) | copy-start | bytes 3244036
  65.6 8.8 %collective-permute-start.11 = (f32[512,128]{1,0:T(8,128)S(1)}, f32[512,128]{1,0:T(8,128)S(1)}, u32[]{:S(2)}, u32[]{:S(2)}) collective-permute-start(f32[512,128]{1,0:T(8,128)S(1)} %get-tuple-element.29._), channel_id=1, source_target_pairs={{0,4},{1,5},{2,6},{3,7},{4,0},{5,1},{6,2},{7,3},{8,12},{9,13},{10,... | collective-permute-start | bytes 786440 | tf_op jit(solution)/shard_map/ppermute | solution.py:493
  74.4 0.6 copy-start.4
  76.8 53.1 %copy-start.5 = (s32[16]{0:T(128)S(1)}, s32[16]{0:T(128)}, u32[]{:S(2)}) copy-start(s32[16]{0:T(128)} %table.1) | copy-start | bytes 196
  76.8 1.2 copy-start.8
  102.1 16.2 %collective-permute-start.15 = (f32[2,256,128]{2,1,0:T(8,128)S(1)}, f32[2,256,128]{2,1,0:T(8,128)S(1)}, u32[]{:S(2)}, u32[]{:S(2)}) collective-permute-start(f32[2,256,128]{2,1,0:T(8,128)S(1)} %get-tuple-element.36), channel_id=1, source_target_pairs={{0,4},{1,5},{2,6},{3,7},{4,0},{5,1},{6,2},{7,3},{8,12},{9,13},{10,... | collective-permute-start | bytes 786440 | tf_op jit(solution)/shard_map/ppermute | solution.py:493
  103.2 17.9 %collective-permute-start.16 = (f32[2,256,128]{2,1,0:T(8,128)S(1)}, f32[2,256,128]{2,1,0:T(8,128)S(1)}, u32[]{:S(2)}, u32[]{:S(2)}) collective-permute-start(f32[2,256,128]{2,1,0:T(8,128)S(1)} %get-tuple-element.37), channel_id=1, source_target_pairs={{0,5},{1,4},{2,7},{3,6},{4,1},{5,0},{6,3},{7,2},{8,13},{9,12},{10,... | collective-permute-start | bytes 786440 | tf_op jit(solution)/shard_map/ppermute | solution.py:493
  105.9 20.3 %collective-permute-start.17 = (f32[2,256,128]{2,1,0:T(8,128)S(1)}, f32[2,256,128]{2,1,0:T(8,128)S(1)}, u32[]{:S(2)}, u32[]{:S(2)}) collective-permute-start(f32[2,256,128]{2,1,0:T(8,128)S(1)} %get-tuple-element.38), channel_id=1, source_target_pairs={{0,6},{1,7},{2,4},{3,5},{4,2},{5,3},{6,0},{7,1},{8,14},{9,15},{10,... | collective-permute-start | bytes 786440 | tf_op jit(solution)/shard_map/ppermute | solution.py:493
  107.0 22.9 %collective-permute-start.18 = (f32[2,256,128]{2,1,0:T(8,128)S(1)}, f32[2,256,128]{2,1,0:T(8,128)S(1)}, u32[]{:S(2)}, u32[]{:S(2)}) collective-permute-start(f32[2,256,128]{2,1,0:T(8,128)S(1)} %get-tuple-element.39), channel_id=1, source_target_pairs={{0,7},{1,6},{2,5},{3,4},{4,3},{5,2},{6,1},{7,0},{8,15},{9,14},{10,... | collective-permute-start | bytes 786440 | tf_op jit(solution)/shard_map/ppermute | solution.py:493

commit v7 on v6

--- a/solution.py
+++ b/solution.py
@@ -494,19 +494,11 @@
 
 
 def among_half(plan, values, together):
-    def at_once(values):
+    def exchange(values):
         groups = [list(range(plan.half)), list(range(plan.half, plan.pieces))]
         return lax.all_to_all(values, "gy", 0, 0, axis_index_groups=groups, tiled=True)
 
-    def pairwise(values):
-        mine = lax.rem(lax.axis_index("gy"), plan.half)
-        found = values
-        for mask in range(1, plan.half):
-            moved = swap(lax.dynamic_index_in_dim(values, mine ^ mask, 0, keepdims=False), mask)
-            found = lax.dynamic_update_index_in_dim(found, moved, mine ^ mask, 0)
-        return found
-
-    return lax.cond(together, at_once, pairwise, values)
+    return lax.cond(together, exchange, exchange, values)
 
 
 def per_device(phase, solute, undercool, mobility, diffusivity, owner):

time: 133 us -> 119 us (0.89)
  waiting for transfers between devices: 28.9 us -> 6.1 us
  starting transfers between devices: 17.8 us -> 39.4 us
  blocking collectives: 54.1 us -> 45.6 us
  local copies, waits for them, and re-layouts: 3.82 us -> 1.41 us
  Pallas kernels: 27.2 us -> 25.3 us
    ppermute x9, waiting for transfers between devices: 28.1 us -> 6.09 us  [swap(): lax.ppermute(values, 'gy', [(i, i ^ mask) for i in range(lax.axis_size('g...]
    ppermute x9, starting transfers between devices: 13.1 us -> 34.6 us  [swap(): lax.ppermute(values, 'gy', [(i, i ^ mask) for i in range(lax.axis_size('g...]
    all_to_all x2, blocking collectives: 54.1 us -> 45.6 us  [exchange(): lax.all_to_all(values, 'gy', 0, 0, axis_index_groups=groups, tiled=True)]
    cond x4 -> x0, local copies, waits for them, and re-layouts: 2.46 us -> none
  transfers between devices with their start and end apart: 13 -> 13, of which waited for: 6 -> 2; matrix products, arithmetic and copies ran while one was open for 0% -> 0% of each run, Pallas kernels for 16% -> 17%
where the time goes in v7:
time: 119 us
  blocking collectives  45.6 us (38%)
  starting transfers between devices  39.4 us (33%)
  Pallas kernels  25.3 us (21%)
  waiting for transfers between devices  6.1 us (5%)
  local copies, waits for them, and re-layouts  1.41 us (1%)
    all_to_all x2, blocking collectives, exchange(): lax.all_to_all(values, 'gy', 0, 0, axis_index_groups=groups, tiled=True)  45.6 us
    ppermute x9, starting transfers between devices, swap(): lax.ppermute(values, 'gy', [(i, i ^ mask) for i in range(lax.axis_size('g...  34.6 us
    pallas_call x1, Pallas kernels, run_inner(): pl.pallas_call(functools.partial(inner_kernel, plan), in_specs=[vmem] * 3...  9.27 us
    pallas_call x1, Pallas kernels, run_outer(): pl.pallas_call(functools.partial(outer_kernel, plan), in_specs=[vmem] * 8...  9.07 us
    ppermute x9, waiting for transfers between devices, swap(): lax.ppermute(values, 'gy', [(i, i ^ mask) for i in range(lax.axis_size('g...  6.09 us
  transfers between devices with their start and end apart: 13, of which 2 were waited for; matrix products, arithmetic and copies ran while one was open for 0% of the time, Pallas kernels for 17%

profile of v7, /device:TPU:8, one launch (start us, length us, event | category | flops | bytes accessed | tf_op | source)
XLA Modules:
  0.0 118.5 jit_solution(4674587012470944347)
XLA Ops:
  0.6 0.0 copy-start.1
  0.6 0.0 copy-start
  0.7 2.0 %pack_y.1 = (f32[33,8,128]{2,1,0:T(8,128)}, f32[33,8,128]{2,1,0:T(8,128)}, f32[24,128]{1,0:T(8,128)}) custom-call(f32[1,2]{1,0:T(1,128)} %under.1, f32[1,2]{1,0:T(1,128)} %mobile.1, f32[1,2]{1,0:T(1,128)} %spread.1, s32[1,2]{1,0:T(1,128)} %owner.1, f32[1,2,32,32,128]{4,3,2,1,0:T(8,128)} %phase.3, f32[1,2,32,32,128]{4,3,2,1,0:T(8,128)} %phase.3, ...), custom_call_target="tpu_custom_call" | custom-call | tf_op jit(solution)/shard_map/pack_y/pallas_call | solution.py:47
  2.7 1.5 %collective-permute-start = (f32[33,8,128]{2,1,0:T(8,128)}, f32[33,8,128]{2,1,0:T(8,128)S(1)}, u32[]{:S(2)}, u32[]{:S(2)}) collective-permute-start(f32[33,8,128]{2,1,0:T(8,128)} %get-tuple-element.27), channel_id=1, source_target_pairs={{0,1},{1,2},{2,3},{3,4},{4,5},{5,6},{6,7},{7,0},{8,9},{9,10},{10,1... | collective-permute-start | bytes 405512 | tf_op jit(solution)/shard_map/ppermute | solution.py:509
  4.2 1.4 %collective-permute-start.1 = (f32[33,8,128]{2,1,0:T(8,128)}, f32[33,8,128]{2,1,0:T(8,128)S(1)}, u32[]{:S(2)}, u32[]{:S(2)}) collective-permute-start(f32[33,8,128]{2,1,0:T(8,128)} %get-tuple-element.28), channel_id=1, source_target_pairs={{0,7},{1,0},{2,1},{3,2},{4,3},{5,4},{6,5},{7,6},{8,15},{9,8},{10,9... | collective-permute-start | bytes 405512 | tf_op jit(solution)/shard_map/ppermute | solution.py:510
  5.6 0.0 copy-done.1
  5.6 0.0 copy-done
  5.6 0.0 copy-start.2
  5.6 0.7 copy-done.2
  6.3 9.3 %inner.1 = (f32[512,128]{1,0:T(8,128)S(1)}, f32[512,128]{1,0:T(8,128)}, f32[512,128]{1,0:T(8,128)}, f32[512,128]{1,0:T(8,128)}) custom-call(f32[24,128]{1,0:T(8,128)S(1)} %copy-done.2, f32[1,2,32,32,128]{4,3,2,1,0:T(8,128)S(1)} %copy-done, f32[1,2,32,32,128]{4,3,2,1,0:T(8,128)S(1)} %copy-done.1), custom_call_target="tpu_custom_call" | custom-call | flops 100000000 | bytes 25165824 | tf_op jit(solution)/shard_map/inner/pallas_call | solution.py:254
  15.6 0.0 collective-permute-done.y_lo
  15.6 0.0 collective-permute-done.1.y_hi
  15.6 0.0 copy-start.7
  15.6 0.0 copy-start.3
  15.7 0.1 collective-permute-start.2
  15.7 1.7 %collective-permute-start.3 = (f32[608,128]{1,0:T(8,128)S(1)}, f32[608,128]{1,0:T(8,128)S(1)}, u32[]{:S(2)}, u32[]{:S(2)}) collective-permute-start(f32[608,128]{1,0:T(8,128)S(1)} %get-tuple-element.31), channel_id=1, source_target_pairs={{0,24},{8,0},{16,8},{24,16},{1,25},{9,1},{17,9},{25,17},{2,26},{10... | collective-permute-start | bytes 933896 | tf_op jit(solution)/shard_map/ppermute | solution.py:516
  17.5 2.6 %collective-permute-start.4 = (f32[8,128]{1,0:T(8,128)S(1)}, f32[8,128]{1,0:T(8,128)S(1)}, u32[]{:S(2)}, u32[]{:S(2)}) collective-permute-start(f32[8,128]{1,0:T(8,128)S(1)} %slice.7), channel_id=1, source_target_pairs={{0,4},{1,5},{2,6},{3,7},{4,0},{5,1},{6,2},{7,3},{8,12},{9,13},{10,... | collective-permute-start | bytes 12296 | tf_op jit(solution)/shard_map/ppermute | solution.py:493
  20.0 0.4 collective-permute-start.6
  20.4 1.6 %collective-permute-start.7 = (f32[512,128]{1,0:T(8,128)}, f32[512,128]{1,0:T(8,128)S(1)}, u32[]{:S(2)}, u32[]{:S(2)}) collective-permute-start(f32[512,128]{1,0:T(8,128)} %get-tuple-element.33), channel_id=1, source_target_pairs={{0,6},{1,7},{2,4},{3,5},{4,2},{5,3},{6,0},{7,1},{8,14},{9,15},{10,... | collective-permute-start | bytes 786440 | tf_op jit(solution)/shard_map/ppermute | solution.py:493
  22.0 0.0 collective-permute-done.4.partner
  22.0 1.6 %collective-permute-start.8 = (f32[512,128]{1,0:T(8,128)}, f32[512,128]{1,0:T(8,128)S(1)}, u32[]{:S(2)}, u32[]{:S(2)}) collective-permute-start(f32[512,128]{1,0:T(8,128)} %get-tuple-element.34), channel_id=1, source_target_pairs={{0,7},{1,6},{2,5},{3,4},{4,3},{5,2},{6,1},{7,0},{8,15},{9,14},{10,... | collective-permute-start | bytes 786440 | tf_op jit(solution)/shard_map/ppermute | solution.py:493
  23.6 0.0 collective-permute-done.2.x_lo
  23.6 21.4 %collective-permute-start.5 = (f32[512,128]{1,0:T(8,128)S(1)}, f32[512,128]{1,0:T(8,128)S(1)}, u32[]{:S(2)}, u32[]{:S(2)}) collective-permute-start(f32[512,128]{1,0:T(8,128)S(1)} %get-tuple-element.29._), channel_id=1, source_target_pairs={{0,4},{1,5},{2,6},{3,7},{4,0},{5,1},{6,2},{7,3},{8,12},{9,13},{10,... | collective-permute-start | bytes 786440 | tf_op jit(solution)/shard_map/ppermute | solution.py:493
  45.0 0.0 copy-done.7
  45.1 0.0 collective-permute-done.3.x_hi
  45.1 0.0 copy-done.3
  45.1 9.1 %outer.1 = f32[4,528,128]{2,1,0:T(8,128)S(1)} custom-call(f32[24,128]{1,0:T(8,128)S(1)} %copy-done.3, f32[1,2,32,32,128]{4,3,2,1,0:T(8,128)S(1)} %copy-done, f32[1,2,32,32,128]{4,3,2,1,0:T(8,128)S(1)} %copy-done.1, f32[33,8,128]{2,1,0:T(8,128)S(1)} %collective-permute-done.y_lo, f32[33,8,128]{2,1,0:T(8,128)S(1)} %collective-permute-done.1.y_hi, ...), custom_call_target="tpu_custom_call" | custom-call | flops 100000000 | bytes 41943040 | tf_op jit(solution)/shard_map/outer/pallas_call | solution.py:354
  54.2 16.7 %conditional.2 = (f32[4,528,128]{2,1,0:T(8,128)S(1)}) conditional(s32[]{:T(128)} %bitcast, f32[4,528,128]{2,1,0:T(8,128)S(1)} %outer.1, f32[4,528,128]{2,1,0:T(8,128)S(1)} %outer.1), branch_computations={%region_0.0_spmd, %region_1.0_spmd} | conditional | bytes 2162696 | solution.py:501
  54.2 16.7 %all_to_all.17 = f32[4,528,128]{2,1,0:T(8,128)S(1)} all-to-all(f32[4,528,128]{2,1,0:T(8,128)S(1)} %param.1), channel_id=1, replica_groups={{0,1,2,3},{4,5,6,7},{8,9,10,11},{12,13,14,15},{16,17,18,19},{20,21,22,2..., dimensions={0} | all-to-all | bytes 2162688 | tf_op jit(solution)/shard_map/cond/branch_1_fun/all_to_all | solution.py:499
  70.9 0.0 copy-start.6
  70.9 1.3 %table.1 = s32[16]{0:T(128)} custom-call(f32[4,528,128]{2,1,0:T(8,128)S(1)} %get-tuple-element.40.near), custom_call_target="tpu_custom_call" | custom-call | tf_op jit(solution)/shard_map/table/pallas_call | solution.py:393
  72.2 0.0 collective-permute-done.6.refs_1_
  72.2 0.0 collective-permute-done.7.refs_2_
  72.2 0.0 collective-permute-done.8.refs_3_
  72.2 0.0 copy-done.6
  72.2 0.0 collective-permute-done.5.refs_0_
  72.2 0.0 copy-start.4
  72.3 0.7 copy-done.4
  72.9 1.5 %route.1 = (f32[4,2,256,128]{3,2,1,0:T(8,128)S(1)}, f32[2,256,128]{2,1,0:T(8,128)S(1)}, f32[2,256,128]{2,1,0:T(8,128)S(1)}, f32[2,256,128]{2,1,0:T(8,128)S(1)}, f32[2,256,128]{2,1,0:T(8,128)S(1)}) custom-call(s32[16]{0:T(128)S(1)} %copy-done.4, f32[4,528,128]{2,1,0:T(8,128)} %copy-done.6, f32[512,128]{1,0:T(8,128)S(1)} %collective-permute-done.5.refs_0_, ...), custom_call_target="tpu_custom_call" | custom-call | tf_op jit(solution)/shard_map/route/pallas_call | solution.py:428
  74.5 4.1 %collective-permute-start.9 = (f32[2,256,128]{2,1,0:T(8,128)S(1)}, f32[2,256,128]{2,1,0:T(8,128)S(1)}, u32[]{:S(2)}, u32[]{:S(2)}) collective-permute-start(f32[2,256,128]{2,1,0:T(8,128)S(1)} %get-tuple-element.36), channel_id=1, source_target_pairs={{0,4},{1,5},{2,6},{3,7},{4,0},{5,1},{6,2},{7,3},{8,12},{9,13},{10,... | collective-permute-start | bytes 786440 | tf_op jit(solution)/shard_map/ppermute | solution.py:493
  78.5 0.3 collective-permute-start.10
  78.8 0.9 collective-permute-start.11
  79.7 1.9 %collective-permute-start.12 = (f32[2,256,128]{2,1,0:T(8,128)S(1)}, f32[2,256,128]{2,1,0:T(8,128)S(1)}, u32[]{:S(2)}, u32[]{:S(2)}) collective-permute-start(f32[2,256,128]{2,1,0:T(8,128)S(1)} %get-tuple-element.39), channel_id=1, source_target_pairs={{0,7},{1,6},{2,5},{3,4},{4,3},{5,2},{6,1},{7,0},{8,15},{9,14},{10,... | collective-permute-start | bytes 786440 | tf_op jit(solution)/shard_map/ppermute | solution.py:493
  81.5 0.0 copy-start.5
  81.5 28.9 %conditional.3 = (f32[4,2,256,128]{3,2,1,0:T(8,128)S(1)}) conditional(s32[]{:T(128)} %bitcast, f32[4,2,256,128]{3,2,1,0:T(8,128)S(1)} %get-tuple-element.35, f32[4,2,256,128]{3,2,1,0:T(8,128)S(1)} %get-tuple-element.35), branch_computations={%region_2.0_spmd, %region_3.0_spmd} | conditional | bytes 2097160 | solution.py:501
  81.5 28.9 %all_to_all.19 = f32[4,2,256,128]{3,2,1,0:T(8,128)S(1)} all-to-all(f32[4,2,256,128]{3,2,1,0:T(8,128)S(1)} %param.3), channel_id=1, replica_groups={{0,1,2,3},{4,5,6,7},{8,9,10,11},{12,13,14,15},{16,17,18,19},{20,21,22,2..., dimensions={0} | all-to-all | bytes 2097152 | tf_op jit(solution)/shard_map/cond/branch_1_fun/all_to_all | solution.py:499
  110.4 0.0 collective-permute-done.9.refs_0_
  110.4 0.0 collective-permute-done.10.refs_1_
  110.4 0.9 collective-permute-done.11.refs_2_
  111.3 5.1 %collective-permute-done.12.refs_3_ = f32[2,256,128]{2,1,0:T(8,128)S(1)} collective-permute-done((f32[2,256,128]{2,1,0:T(8,128)S(1)}, f32[2,256,128]{2,1,0:T(8,128)S(1)}, u32[]{:S(2)}, u32[]{:S(2)}) %collective-permute-start.12) | collective-permute-done | bytes 262176 | tf_op jit(solution)/shard_map/ppermute | solution.py:493
  116.5 0.0 copy-done.5
  116.5 2.1 %settle.1 = (f32[1,2,32,32,128]{4,3,2,1,0:T(8,128)}, f32[1,2,32,32,128]{4,3,2,1,0:T(8,128)}) custom-call(s32[16]{0:T(128)S(1)} %copy-done.5, f32[4,2,256,128]{3,2,1,0:T(8,128)S(1)} %get-tuple-element.41.near, f32[2,256,128]{2,1,0:T(8,128)S(1)} %collective-permute-done.9.refs_0_, f32[2,256,128]{2,1,0:T(8,128)S(1)} %collective-permute-done.10.refs_1_, ...), custom_call_target="tpu_custom_call" | custom-call | tf_op jit(solution)/shard_map/settle/pallas_call | solution.py:477
  (2 shorter events, 0.1 us)
Async XLA Ops:
  0.6 5.0 %copy-start.1 = (f32[1,2,32,32,128]{4,3,2,1,0:T(8,128)S(1)}, f32[1,2,32,32,128]{4,3,2,1,0:T(8,128)}, u32[]{:S(2)}) copy-start(f32[1,2,32,32,128]{4,3,2,1,0:T(8,128)} %solute.3) | copy-start | bytes 3145732
  0.6 4.9 %copy-start = (f32[1,2,32,32,128]{4,3,2,1,0:T(8,128)S(1)}, f32[1,2,32,32,128]{4,3,2,1,0:T(8,128)}, u32[]{:S(2)}) copy-start(f32[1,2,32,32,128]{4,3,2,1,0:T(8,128)} %phase.3) | copy-start | bytes 3145732
  2.7 12.9 %collective-permute-start = (f32[33,8,128]{2,1,0:T(8,128)}, f32[33,8,128]{2,1,0:T(8,128)S(1)}, u32[]{:S(2)}, u32[]{:S(2)}) collective-permute-start(f32[33,8,128]{2,1,0:T(8,128)} %get-tuple-element.27), channel_id=1, source_target_pairs={{0,1},{1,2},{2,3},{3,4},{4,5},{5,6},{6,7},{7,0},{8,9},{9,10},{10,1... | collective-permute-start | bytes 405512 | tf_op jit(solution)/shard_map/ppermute | solution.py:509
  4.2 11.4 %collective-permute-start.1 = (f32[33,8,128]{2,1,0:T(8,128)}, f32[33,8,128]{2,1,0:T(8,128)S(1)}, u32[]{:S(2)}, u32[]{:S(2)}) collective-permute-start(f32[33,8,128]{2,1,0:T(8,128)} %get-tuple-element.28), channel_id=1, source_target_pairs={{0,7},{1,0},{2,1},{3,2},{4,3},{5,4},{6,5},{7,6},{8,15},{9,8},{10,9... | collective-permute-start | bytes 405512 | tf_op jit(solution)/shard_map/ppermute | solution.py:510
  5.6 0.7 copy-start.2
  15.6 29.5 %copy-start.7 = (s32[1,2]{1,0:T(1,128)S(1)}, s32[1,2]{1,0:T(1,128)}, u32[]{:S(2)}) copy-start(s32[1,2]{1,0:T(1,128)} %owner.1) | copy-start | bytes 28
  15.6 29.5 %copy-start.3 = (f32[24,128]{1,0:T(8,128)S(1)}, f32[24,128]{1,0:T(8,128)}, u32[]{:S(2)}) copy-start(f32[24,128]{1,0:T(8,128)} %get-tuple-element.26.own) | copy-start | bytes 36868
  15.7 7.9 %collective-permute-start.2 = (f32[608,128]{1,0:T(8,128)S(1)}, f32[608,128]{1,0:T(8,128)S(1)}, u32[]{:S(2)}, u32[]{:S(2)}) collective-permute-start(f32[608,128]{1,0:T(8,128)S(1)} %get-tuple-element.30), channel_id=1, source_target_pairs={{0,8},{8,16},{16,24},{24,0},{1,9},{9,17},{17,25},{25,1},{2,10},{10... | collective-permute-start | bytes 933896 | tf_op jit(solution)/shard_map/ppermute | solution.py:515
  15.7 29.4 %collective-permute-start.3 = (f32[608,128]{1,0:T(8,128)S(1)}, f32[608,128]{1,0:T(8,128)S(1)}, u32[]{:S(2)}, u32[]{:S(2)}) collective-permute-start(f32[608,128]{1,0:T(8,128)S(1)} %get-tuple-element.31), channel_id=1, source_target_pairs={{0,24},{8,0},{16,8},{24,16},{1,25},{9,1},{17,9},{25,17},{2,26},{10... | collective-permute-start | bytes 933896 | tf_op jit(solution)/shard_map/ppermute | solution.py:516
  17.5 4.6 %collective-permute-start.4 = (f32[8,128]{1,0:T(8,128)S(1)}, f32[8,128]{1,0:T(8,128)S(1)}, u32[]{:S(2)}, u32[]{:S(2)}) collective-permute-start(f32[8,128]{1,0:T(8,128)S(1)} %slice.7), channel_id=1, source_target_pairs={{0,4},{1,5},{2,6},{3,7},{4,0},{5,1},{6,2},{7,3},{8,12},{9,13},{10,... | collective-permute-start | bytes 12296 | tf_op jit(solution)/shard_map/ppermute | solution.py:493
  20.0 52.2 %collective-permute-start.6 = (f32[512,128]{1,0:T(8,128)}, f32[512,128]{1,0:T(8,128)S(1)}, u32[]{:S(2)}, u32[]{:S(2)}) collective-permute-start(f32[512,128]{1,0:T(8,128)} %get-tuple-element.32), channel_id=1, source_target_pairs={{0,5},{1,4},{2,7},{3,6},{4,1},{5,0},{6,3},{7,2},{8,13},{9,12},{10,... | collective-permute-start | bytes 786440 | tf_op jit(solution)/shard_map/ppermute | solution.py:493
  20.4 51.8 %collective-permute-start.7 = (f32[512,128]{1,0:T(8,128)}, f32[512,128]{1,0:T(8,128)S(1)}, u32[]{:S(2)}, u32[]{:S(2)}) collective-permute-start(f32[512,128]{1,0:T(8,128)} %get-tuple-element.33), channel_id=1, source_target_pairs={{0,6},{1,7},{2,4},{3,5},{4,2},{5,3},{6,0},{7,1},{8,14},{9,15},{10,... | collective-permute-start | bytes 786440 | tf_op jit(solution)/shard_map/ppermute | solution.py:493
  22.0 50.2 %collective-permute-start.8 = (f32[512,128]{1,0:T(8,128)}, f32[512,128]{1,0:T(8,128)S(1)}, u32[]{:S(2)}, u32[]{:S(2)}) collective-permute-start(f32[512,128]{1,0:T(8,128)} %get-tuple-element.34), channel_id=1, source_target_pairs={{0,7},{1,6},{2,5},{3,4},{4,3},{5,2},{6,1},{7,0},{8,15},{9,14},{10,... | collective-permute-start | bytes 786440 | tf_op jit(solution)/shard_map/ppermute | solution.py:493
  23.6 48.6 %collective-permute-start.5 = (f32[512,128]{1,0:T(8,128)S(1)}, f32[512,128]{1,0:T(8,128)S(1)}, u32[]{:S(2)}, u32[]{:S(2)}) collective-permute-start(f32[512,128]{1,0:T(8,128)S(1)} %get-tuple-element.29._), channel_id=1, source_target_pairs={{0,4},{1,5},{2,6},{3,7},{4,0},{5,1},{6,2},{7,3},{8,12},{9,13},{10,... | collective-permute-start | bytes 786440 | tf_op jit(solution)/shard_map/ppermute | solution.py:493
  70.9 1.3 %copy-start.6 = (f32[4,528,128]{2,1,0:T(8,128)}, f32[4,528,128]{2,1,0:T(8,128)S(1)}, u32[]{:S(2)}) copy-start(f32[4,528,128]{2,1,0:T(8,128)S(1)} %get-tuple-element.40.near) | copy-start | bytes 3244036
  72.2 0.7 copy-start.4
  74.5 35.9 %collective-permute-start.9 = (f32[2,256,128]{2,1,0:T(8,128)S(1)}, f32[2,256,128]{2,1,0:T(8,128)S(1)}, u32[]{:S(2)}, u32[]{:S(2)}) collective-permute-start(f32[2,256,128]{2,1,0:T(8,128)S(1)} %get-tuple-element.36), channel_id=1, source_target_pairs={{0,4},{1,5},{2,6},{3,7},{4,0},{5,1},{6,2},{7,3},{8,12},{9,13},{10,... | collective-permute-start | bytes 786440 | tf_op jit(solution)/shard_map/ppermute | solution.py:493
  78.5 31.9 %collective-permute-start.10 = (f32[2,256,128]{2,1,0:T(8,128)S(1)}, f32[2,256,128]{2,1,0:T(8,128)S(1)}, u32[]{:S(2)}, u32[]{:S(2)}) collective-permute-start(f32[2,256,128]{2,1,0:T(8,128)S(1)} %get-tuple-element.37), channel_id=1, source_target_pairs={{0,5},{1,4},{2,7},{3,6},{4,1},{5,0},{6,3},{7,2},{8,13},{9,12},{10,... | collective-permute-start | bytes 786440 | tf_op jit(solution)/shard_map/ppermute | solution.py:493
  78.8 32.5 %collective-permute-start.11 = (f32[2,256,128]{2,1,0:T(8,128)S(1)}, f32[2,256,128]{2,1,0:T(8,128)S(1)}, u32[]{:S(2)}, u32[]{:S(2)}) collective-permute-start(f32[2,256,128]{2,1,0:T(8,128)S(1)} %get-tuple-element.38), channel_id=1, source_target_pairs={{0,6},{1,7},{2,4},{3,5},{4,2},{5,3},{6,0},{7,1},{8,14},{9,15},{10,... | collective-permute-start | bytes 786440 | tf_op jit(solution)/shard_map/ppermute | solution.py:493
  79.7 36.8 %collective-permute-start.12 = (f32[2,256,128]{2,1,0:T(8,128)S(1)}, f32[2,256,128]{2,1,0:T(8,128)S(1)}, u32[]{:S(2)}, u32[]{:S(2)}) collective-permute-start(f32[2,256,128]{2,1,0:T(8,128)S(1)} %get-tuple-element.39), channel_id=1, source_target_pairs={{0,7},{1,6},{2,5},{3,4},{4,3},{5,2},{6,1},{7,0},{8,15},{9,14},{10,... | collective-permute-start | bytes 786440 | tf_op jit(solution)/shard_map/ppermute | solution.py:493
  81.5 34.9 %copy-start.5 = (s32[16]{0:T(128)S(1)}, s32[16]{0:T(128)}, u32[]{:S(2)}) copy-start(s32[16]{0:T(128)} %table.1) | copy-start | bytes 196

commit v8 on v7

--- a/solution.py
+++ b/solution.py
@@ -215,19 +215,20 @@
 
 
 def inner_kernel(plan, own, phase, solute, *rest):
-    half, tiles, edge = plan.half, plan.tiles, plan.edge
-    outs, scratch = rest[:half], rest[half:]
+    tiles, edge, count = plan.tiles, plan.edge, plan.inner // 2
+    outs, scratch = rest[: plan.half // 2], rest[plan.half // 2 :]
     pairs = (scratch[:2], scratch[2:])
-    me = lax.axis_index("gy")
+    mine = lax.rem(lax.axis_index("gy"), plan.half)
+    base = mine // (plan.half // 2) * count
 
     def load_row(row, carry):
         for tile in range(tiles):
             start = PAD + tile * edge
-            pairs[0][0][row, start : start + edge, :] = phase[0, tile, row]
-            pairs[0][1][row, start : start + edge, :] = solute[0, tile, row]
+            pairs[0][0][row, start : start + edge, :] = phase[0, tile, base + row]
+            pairs[0][1][row, start : start + edge, :] = solute[0, tile, base + row]
         return carry
 
-    lax.fori_loop(0, edge, load_row, 0, unroll=UNROLL)
+    lax.fori_loop(0, count + 2 * W, load_row, 0, unroll=UNROLL)
 
     def coefs_of(row, start):
         tile = (start - PAD) // edge
@@ -235,27 +236,31 @@
 
     for step in range(NSTEPS):
         starts = range(PAD, PAD + tiles * edge, 8)
-        march(step + 1, edge - step - 1, starts, pairs[step % 2], pairs[(step + 1) % 2], coefs_of)
+        march(step + 1, count + 2 * W - step - 1, starts, pairs[step % 2], pairs[(step + 1) % 2], coefs_of)
     for index, out in enumerate(outs):
-        piece = lax.rem(me ^ (half + index), half)
-        for tile in range(tiles):
-            for field, done in enumerate(pairs[NSTEPS % 2]):
-                begin = (2 * tile + field) * plan.size
-                for at, row, name in plan.parts(True, piece):
-                    col, count = plan.columns(name, tile)
-                    start = PAD + tile * edge + col
-                    out[begin + at : begin + at + count, :] = done[row, start : start + count, :]
+        pack(plan, True, mine ^ index, pairs[NSTEPS % 2], -base, PAD, out)
+
+
+def pack(plan, far, piece, done, row_shift, col_shift, out):
+    for tile in range(plan.tiles):
+        for field, values in enumerate(done):
+            begin = (2 * tile + field) * plan.size
+            for at, row, name in plan.parts(far, piece):
+                col, count = plan.columns(name, tile)
+                start = col_shift + tile * plan.edge + col
+                out[begin + at : begin + at + count, :] = values[row + row_shift, start : start + count, :]
 
 
 def run_inner(plan, own, phase, solute):
-    buffer = pltpu.VMEM((plan.edge, plan.tiles * plan.edge + 2 * PAD, plan.depth), jnp.float32)
+    rows = plan.inner // 2 + 2 * W
+    buffer = pltpu.VMEM((rows, plan.tiles * plan.edge + 2 * PAD, plan.depth), jnp.float32)
     vmem = pl.BlockSpec(memory_space=pltpu.VMEM)
     shape = jax.ShapeDtypeStruct((2 * plan.tiles * plan.size, plan.depth), jnp.float32)
     return pl.pallas_call(
         functools.partial(inner_kernel, plan),
         in_specs=[vmem] * 3,
-        out_specs=[vmem] * plan.half,
-        out_shape=[shape] * plan.half,
+        out_specs=[vmem] * (plan.half // 2),
+        out_shape=[shape] * (plan.half // 2),
         scratch_shapes=[buffer] * 4,
         compiler_params=pltpu.CompilerParams(vmem_limit_bytes=16 * 1024 * 1024),
         cost_estimate=pl.CostEstimate(flops=10**8, bytes_accessed=24 * 1024 * 1024, transcendentals=0),
@@ -263,8 +268,9 @@
     )(own, phase, solute)
 
 
-def outer_kernel(plan, own, phase, solute, y_lo, y_hi, x_lo, x_hi, partner, out, *scratch):
+def outer_kernel(plan, own, phase, solute, y_lo, y_hi, x_lo, x_hi, partner, out, *rest):
     tiles, edge, depth, half = plan.tiles, plan.edge, plan.depth, plan.half
+    far_outs, scratch = rest[: half // 2], rest[half // 2 :]
     pairs, coefs = (scratch[:2], scratch[2:4]), scratch[4]
     cols = tiles * edge
     width = cols + 2 * W
@@ -310,38 +316,19 @@
         return found
 
     any_zone = coefs_of(lambda row: jnp.where(row < W, 0, jnp.where(row < W + edge, 1, 2)))
-    own_zone = coefs_of(lambda row: 1)
-
-    def blocks(first, last):
+
+    for step in range(1, NSTEPS + 1):
+        left = NSTEPS - step
         shift = W if step == NSTEPS else 0
-        low, high = (first + W - shift) // 8 * 8, -(-(last + W - shift) // 8) * 8
-        return list(range(PAD + shift + low, PAD + shift + high, 8))
-
-    for step in range(1, NSTEPS + 1):
-        source, target = pairs[(step - 1) % 2], pairs[step % 2]
-        left = NSTEPS - step
-        strip = W + left
-        whole = blocks(-left, cols + left)
-        sides = blocks(-left, 8 + left) + blocks(cols - 8 - left, cols + left)
-        lasts = []
-        for tile in range(tiles):
-            col, count = plan.columns("last", tile)
-            lasts += blocks(tile * edge + col - left, tile * edge + col + count + left)
-        ends = sorted(set(sides + lasts))
-        march(W - left, W + strip, whole, source, target, any_zone)
-        march(W + strip, W + strip + W, ends, source, target, own_zone)
-        march(W + strip + W, W + edge - strip - W, sides, source, target, own_zone)
-        march(W + edge - strip - W, W + edge - strip, ends, source, target, own_zone)
-        march(W + edge - strip, W + edge + left, whole, source, target, any_zone)
+        starts = range(PAD + shift, PAD + width - shift, 8)
+        march(W - left, W + edge + left, starts, pairs[(step - 1) % 2], pairs[step % 2], any_zone)
+    done = pairs[NSTEPS % 2]
+    mine = lax.rem(lax.axis_index("gy"), half)
+    for index, far_out in enumerate(far_outs):
+        pack(plan, True, mine ^ (half // 2 + index), done, W, PAD + W, far_out)
     tail = 2 * tiles * plan.size
     for piece in range(half):
-        for tile in range(tiles):
-            for field, done in enumerate(pairs[NSTEPS % 2]):
-                begin = (2 * tile + field) * plan.size
-                for at, row, name in plan.parts(False, piece):
-                    col, count = plan.columns(name, tile)
-                    start = PAD + W + tile * edge + col
-                    out[piece, begin + at : begin + at + count, :] = done[W + row, start : start + count, :]
+        pack(plan, False, piece, done, W, PAD + W, out.at[piece])
         out[piece, tail : tail + AUX, :] = own[8 * tiles : 8 * tiles + AUX, :]
         out[piece, tail + AUX : tail + 2 * AUX, :] = partner[...]
 
@@ -351,11 +338,13 @@
     width = tiles * edge + 2 * W
     buffer = pltpu.VMEM((edge + 2 * W, width + 2 * PAD, depth), jnp.float32)
     vmem = pl.BlockSpec(memory_space=pltpu.VMEM)
+    near = jax.ShapeDtypeStruct((plan.half, 2 * tiles * plan.size + 2 * AUX, depth), jnp.float32)
+    far = jax.ShapeDtypeStruct((2 * tiles * plan.size, depth), jnp.float32)
     return pl.pallas_call(
         functools.partial(outer_kernel, plan),
         in_specs=[vmem] * 8,
-        out_specs=vmem,
-        out_shape=jax.ShapeDtypeStruct((plan.half, 2 * tiles * plan.size + 2 * AUX, depth), jnp.float32),
+        out_specs=[vmem] * (1 + plan.half // 2),
+        out_shape=[near] + [far] * (plan.half // 2),
         scratch_shapes=[buffer] * 4 + [pltpu.VMEM((3, 3, width, depth), jnp.float32)],
         compiler_params=pltpu.CompilerParams(vmem_limit_bytes=16 * 1024 * 1024),
         cost_estimate=pl.CostEstimate(flops=10**8, bytes_accessed=40 * 1024 * 1024, transcendentals=0),
@@ -514,7 +503,8 @@
     to_prev, to_next = pack_x(phase, solute, own, y_lo, y_hi, first[0])
     x_lo = lax.ppermute(to_next, "gx", ring("gx", 1))
     x_hi = lax.ppermute(to_prev, "gx", ring("gx", -1))
-    near = run_outer(plan, own, phase, solute, (y_lo, y_hi, x_lo, x_hi), partner)
+    near, *second = run_outer(plan, own, phase, solute, (y_lo, y_hi, x_lo, x_hi), partner)
+    far += [swap(values, half + half // 2 + index) for index, values in enumerate(second)]
     together = owner[0, 0] >= 0
     near = among_half(plan, near, together)
     table = find_table(plan, near)

time: 119 us -> 117 us (0.983)
  starting transfers between devices: 39.4 us -> 19.5 us
  blocking collectives: 45.6 us -> 63.2 us
    ppermute x9, starting transfers between devices: 34.6 us -> 14.7 us  [swap(): lax.ppermute(values, 'gy', [(i, i ^ mask) for i in range(lax.axis_size('g...]
    all_to_all x2, blocking collectives: 45.6 us -> 63.2 us  [exchange(): lax.all_to_all(values, 'gy', 0, 0, axis_index_groups=groups, tiled=True)]
    pallas_call x1, Pallas kernels: 9.27 us -> 4.72 us  [run_inner(): pl.pallas_call(functools.partial(inner_kernel, plan), in_specs=[vmem] * 3...]
    pallas_call x1, Pallas kernels: 9.07 us -> 12.7 us  [run_outer(): pl.pallas_call(functools.partial(outer_kernel, plan), in_specs=[vmem] * 8...]
    ppermute x9, waiting for transfers between devices: 6.09 us -> 4.74 us  [swap(): lax.ppermute(values, 'gy', [(i, i ^ mask) for i in range(lax.axis_size('g...]
  transfers between devices with their start and end apart: 13 -> 13, of which waited for: 2 -> 5; matrix products, arithmetic and copies ran while one was open for 0% -> 0% of each run, Pallas kernels for 17% -> 16%
where the time goes in v8:
time: 117 us; the launch traced here: 116 us
  blocking collectives  63.2 us (54%)
  Pallas kernels  24.3 us (21%)
  starting transfers between devices  19.5 us (17%)
  waiting for transfers between devices  7.03 us (6%)
  local copies, waits for them, and re-layouts  1.34 us (1%)
    all_to_all x2, blocking collectives, exchange(): lax.all_to_all(values, 'gy', 0, 0, axis_index_groups=groups, tiled=True)  63.2 us
    ppermute x9, starting transfers between devices, swap(): lax.ppermute(values, 'gy', [(i, i ^ mask) for i in range(lax.axis_size('g...  14.7 us
    pallas_call x1, Pallas kernels, run_outer(): pl.pallas_call(functools.partial(outer_kernel, plan), in_specs=[vmem] * 8...  12.7 us
    ppermute x9, waiting for transfers between devices, swap(): lax.ppermute(values, 'gy', [(i, i ^ mask) for i in range(lax.axis_size('g...  4.74 us
    pallas_call x1, Pallas kernels, run_inner(): pl.pallas_call(functools.partial(inner_kernel, plan), in_specs=[vmem] * 3...  4.72 us
  transfers between devices with their start and end apart: 13, of which 5 were waited for; matrix products, arithmetic and copies ran while one was open for 0% of the time, Pallas kernels for 16%

profile of v8, /device:TPU:8, one launch (start us, length us, event | category | flops | bytes accessed | tf_op | source)
XLA Modules:
  0.0 116.2 jit_solution(2251233374142006649)
XLA Ops:
  0.6 0.0 copy-start.1
  0.6 0.0 copy-start
  0.7 2.0 %pack_y.1 = (f32[33,8,128]{2,1,0:T(8,128)}, f32[33,8,128]{2,1,0:T(8,128)}, f32[24,128]{1,0:T(8,128)}) custom-call(f32[1,2]{1,0:T(1,128)} %under.1, f32[1,2]{1,0:T(1,128)} %mobile.1, f32[1,2]{1,0:T(1,128)} %spread.1, s32[1,2]{1,0:T(1,128)} %owner.1, f32[1,2,32,32,128]{4,3,2,1,0:T(8,128)} %phase.3, f32[1,2,32,32,128]{4,3,2,1,0:T(8,128)} %phase.3, ...), custom_call_target="tpu_custom_call" | custom-call | tf_op jit(solution)/shard_map/pack_y/pallas_call | solution.py:47
  2.7 1.5 %collective-permute-start = (f32[33,8,128]{2,1,0:T(8,128)}, f32[33,8,128]{2,1,0:T(8,128)S(1)}, u32[]{:S(2)}, u32[]{:S(2)}) collective-permute-start(f32[33,8,128]{2,1,0:T(8,128)} %get-tuple-element.28), channel_id=1, source_target_pairs={{0,1},{1,2},{2,3},{3,4},{4,5},{5,6},{6,7},{7,0},{8,9},{9,10},{10,1... | collective-permute-start | bytes 405512 | tf_op jit(solution)/shard_map/ppermute | solution.py:498
  4.2 1.4 %collective-permute-start.1 = (f32[33,8,128]{2,1,0:T(8,128)}, f32[33,8,128]{2,1,0:T(8,128)S(1)}, u32[]{:S(2)}, u32[]{:S(2)}) collective-permute-start(f32[33,8,128]{2,1,0:T(8,128)} %get-tuple-element.29), channel_id=1, source_target_pairs={{0,7},{1,0},{2,1},{3,2},{4,3},{5,4},{6,5},{7,6},{8,15},{9,8},{10,9... | collective-permute-start | bytes 405512 | tf_op jit(solution)/shard_map/ppermute | solution.py:499
  5.6 0.0 copy-done.1
  5.6 0.0 copy-done
  5.6 0.0 copy-start.2
  5.6 0.7 copy-done.2
  6.3 4.7 %inner.1 = (f32[512,128]{1,0:T(8,128)S(1)}, f32[512,128]{1,0:T(8,128)S(1)}) custom-call(f32[24,128]{1,0:T(8,128)S(1)} %copy-done.2, f32[1,2,32,32,128]{4,3,2,1,0:T(8,128)S(1)} %copy-done, f32[1,2,32,32,128]{4,3,2,1,0:T(8,128)S(1)} %copy-done.1), custom_call_target="tpu_custom_call" | custom-call | flops 100000000 | bytes 25165824 | tf_op jit(solution)/shard_map/inner/pallas_call | solution.py:259
  11.0 0.0 collective-permute-done.y_lo
  11.0 1.0 collective-permute-done.1.y_hi
  12.0 0.0 copy-start.3
  12.0 0.1 collective-permute-start.2
  12.1 1.7 %collective-permute-start.3 = (f32[608,128]{1,0:T(8,128)S(1)}, f32[608,128]{1,0:T(8,128)S(1)}, u32[]{:S(2)}, u32[]{:S(2)}) collective-permute-start(f32[608,128]{1,0:T(8,128)S(1)} %get-tuple-element.32), channel_id=1, source_target_pairs={{0,24},{8,0},{16,8},{24,16},{1,25},{9,1},{17,9},{25,17},{2,26},{10... | collective-permute-start | bytes 933896 | tf_op jit(solution)/shard_map/ppermute | solution.py:505
  13.8 2.6 %collective-permute-start.4 = (f32[8,128]{1,0:T(8,128)S(1)}, f32[8,128]{1,0:T(8,128)S(1)}, u32[]{:S(2)}, u32[]{:S(2)}) collective-permute-start(f32[8,128]{1,0:T(8,128)S(1)} %slice.7), channel_id=1, source_target_pairs={{0,4},{1,5},{2,6},{3,7},{4,0},{5,1},{6,2},{7,3},{8,12},{9,13},{10,... | collective-permute-start | bytes 12296 | tf_op jit(solution)/shard_map/ppermute | solution.py:482
  16.4 0.3 collective-permute-start.5
  16.8 0.0 copy-start.7
  16.8 2.7 %collective-permute-start.6 = (f32[512,128]{1,0:T(8,128)S(1)}, f32[512,128]{1,0:T(8,128)S(1)}, u32[]{:S(2)}, u32[]{:S(2)}) collective-permute-start(f32[512,128]{1,0:T(8,128)S(1)} %get-tuple-element.34), channel_id=1, source_target_pairs={{0,5},{1,4},{2,7},{3,6},{4,1},{5,0},{6,3},{7,2},{8,13},{9,12},{10,... | collective-permute-start | bytes 786440 | tf_op jit(solution)/shard_map/ppermute | solution.py:482
  19.4 0.0 collective-permute-done.4.partner
  19.4 0.5 collective-permute-done.2.x_lo
  19.9 0.9 collective-permute-done.3.x_hi
  20.8 0.0 copy-done.3
  20.8 12.7 %outer.1 = (f32[4,528,128]{2,1,0:T(8,128)S(1)}, f32[512,128]{1,0:T(8,128)}, f32[512,128]{1,0:T(8,128)S(1)}) custom-call(f32[24,128]{1,0:T(8,128)S(1)} %copy-done.3, f32[1,2,32,32,128]{4,3,2,1,0:T(8,128)S(1)} %copy-done, f32[1,2,32,32,128]{4,3,2,1,0:T(8,128)S(1)} %copy-done.1, f32[33,8,128]{2,1,0:T(8,128)S(1)} %collective-permute-done.y_lo, ...), custom_call_target="tpu_custom_call" | custom-call | flops 100000000 | bytes 41943040 | tf_op jit(solution)/shard_map/outer/pallas_call | solution.py:343
  33.5 1.6 %collective-permute-start.7 = (f32[512,128]{1,0:T(8,128)}, f32[512,128]{1,0:T(8,128)S(1)}, u32[]{:S(2)}, u32[]{:S(2)}) collective-permute-start(f32[512,128]{1,0:T(8,128)} %get-tuple-element.35), channel_id=1, source_target_pairs={{0,6},{1,7},{2,4},{3,5},{4,2},{5,3},{6,0},{7,1},{8,14},{9,15},{10,... | collective-permute-start | bytes 786440 | tf_op jit(solution)/shard_map/ppermute | solution.py:482
  35.0 0.5 collective-permute-start.8
  35.5 0.0 copy-done.7
  35.6 27.2 %conditional.2 = (f32[4,528,128]{2,1,0:T(8,128)S(1)}) conditional(s32[]{:T(128)} %bitcast, f32[4,528,128]{2,1,0:T(8,128)S(1)} %get-tuple-element.33, f32[4,528,128]{2,1,0:T(8,128)S(1)} %get-tuple-element.33), branch_computations={%region_0.0_spmd, %region_1.0_spmd} | conditional | bytes 2162696 | solution.py:490
  35.6 27.2 %all_to_all.17 = f32[4,528,128]{2,1,0:T(8,128)S(1)} all-to-all(f32[4,528,128]{2,1,0:T(8,128)S(1)} %param.1), channel_id=1, replica_groups={{0,1,2,3},{4,5,6,7},{8,9,10,11},{12,13,14,15},{16,17,18,19},{20,21,22,2..., dimensions={0} | all-to-all | bytes 2162688 | tf_op jit(solution)/shard_map/cond/branch_1_fun/all_to_all | solution.py:488
  62.8 0.0 copy-start.6
  62.8 1.3 %table.1 = s32[16]{0:T(128)} custom-call(f32[4,528,128]{2,1,0:T(8,128)S(1)} %get-tuple-element.42.near), custom_call_target="tpu_custom_call" | custom-call | tf_op jit(solution)/shard_map/table/pallas_call | solution.py:382
  64.1 0.0 collective-permute-done.6.refs_1_
  64.1 0.0 collective-permute-done.5.refs_0_
  64.1 0.0 collective-permute-done.7.refs_2_
  64.1 0.0 copy-done.6
  64.2 0.9 collective-permute-done.8.refs_3_
  65.1 0.0 copy-start.4
  65.1 0.6 copy-done.4
  65.7 1.5 %route.1 = (f32[4,2,256,128]{3,2,1,0:T(8,128)S(1)}, f32[2,256,128]{2,1,0:T(8,128)S(1)}, f32[2,256,128]{2,1,0:T(8,128)S(1)}, f32[2,256,128]{2,1,0:T(8,128)S(1)}, f32[2,256,128]{2,1,0:T(8,128)S(1)}) custom-call(s32[16]{0:T(128)S(1)} %copy-done.4, f32[4,528,128]{2,1,0:T(8,128)} %copy-done.6, f32[512,128]{1,0:T(8,128)S(1)} %collective-permute-done.5.refs_0_, ...), custom_call_target="tpu_custom_call" | custom-call | tf_op jit(solution)/shard_map/route/pallas_call | solution.py:417
  67.2 1.7 %collective-permute-start.9 = (f32[2,256,128]{2,1,0:T(8,128)S(1)}, f32[2,256,128]{2,1,0:T(8,128)S(1)}, u32[]{:S(2)}, u32[]{:S(2)}) collective-permute-start(f32[2,256,128]{2,1,0:T(8,128)S(1)} %get-tuple-element.38), channel_id=1, source_target_pairs={{0,4},{1,5},{2,6},{3,7},{4,0},{5,1},{6,2},{7,3},{8,12},{9,13},{10,... | collective-permute-start | bytes 786440 | tf_op jit(solution)/shard_map/ppermute | solution.py:482
  68.9 2.1 %collective-permute-start.10 = (f32[2,256,128]{2,1,0:T(8,128)S(1)}, f32[2,256,128]{2,1,0:T(8,128)S(1)}, u32[]{:S(2)}, u32[]{:S(2)}) collective-permute-start(f32[2,256,128]{2,1,0:T(8,128)S(1)} %get-tuple-element.39), channel_id=1, source_target_pairs={{0,5},{1,4},{2,7},{3,6},{4,1},{5,0},{6,3},{7,2},{8,13},{9,12},{10,... | collective-permute-start | bytes 786440 | tf_op jit(solution)/shard_map/ppermute | solution.py:482
  71.0 1.4 %collective-permute-start.11 = (f32[2,256,128]{2,1,0:T(8,128)S(1)}, f32[2,256,128]{2,1,0:T(8,128)S(1)}, u32[]{:S(2)}, u32[]{:S(2)}) collective-permute-start(f32[2,256,128]{2,1,0:T(8,128)S(1)} %get-tuple-element.40), channel_id=1, source_target_pairs={{0,6},{1,7},{2,4},{3,5},{4,2},{5,3},{6,0},{7,1},{8,14},{9,15},{10,... | collective-permute-start | bytes 786440 | tf_op jit(solution)/shard_map/ppermute | solution.py:482
  72.4 1.9 %collective-permute-start.12 = (f32[2,256,128]{2,1,0:T(8,128)S(1)}, f32[2,256,128]{2,1,0:T(8,128)S(1)}, u32[]{:S(2)}, u32[]{:S(2)}) collective-permute-start(f32[2,256,128]{2,1,0:T(8,128)S(1)} %get-tuple-element.41), channel_id=1, source_target_pairs={{0,7},{1,6},{2,5},{3,4},{4,3},{5,2},{6,1},{7,0},{8,15},{9,14},{10,... | collective-permute-start | bytes 786440 | tf_op jit(solution)/shard_map/ppermute | solution.py:482
  74.3 0.0 copy-start.5
  74.3 36.0 %conditional.3 = (f32[4,2,256,128]{3,2,1,0:T(8,128)S(1)}) conditional(s32[]{:T(128)} %bitcast, f32[4,2,256,128]{3,2,1,0:T(8,128)S(1)} %get-tuple-element.37, f32[4,2,256,128]{3,2,1,0:T(8,128)S(1)} %get-tuple-element.37), branch_computations={%region_2.0_spmd, %region_3.0_spmd} | conditional | bytes 2097160 | solution.py:490
  74.3 36.0 %all_to_all.19 = f32[4,2,256,128]{3,2,1,0:T(8,128)S(1)} all-to-all(f32[4,2,256,128]{3,2,1,0:T(8,128)S(1)} %param.3), channel_id=1, replica_groups={{0,1,2,3},{4,5,6,7},{8,9,10,11},{12,13,14,15},{16,17,18,19},{20,21,22,2..., dimensions={0} | all-to-all | bytes 2097152 | tf_op jit(solution)/shard_map/cond/branch_1_fun/all_to_all | solution.py:488
  110.3 0.0 collective-permute-done.9.refs_0_
  110.3 0.0 collective-permute-done.10.refs_1_
  110.3 0.0 collective-permute-done.11.refs_2_
  110.3 3.8 %collective-permute-done.12.refs_3_ = f32[2,256,128]{2,1,0:T(8,128)S(1)} collective-permute-done((f32[2,256,128]{2,1,0:T(8,128)S(1)}, f32[2,256,128]{2,1,0:T(8,128)S(1)}, u32[]{:S(2)}, u32[]{:S(2)}) %collective-permute-start.12) | collective-permute-done | bytes 262176 | tf_op jit(solution)/shard_map/ppermute | solution.py:482
  114.1 0.0 copy-done.5
  114.1 2.1 %settle.1 = (f32[1,2,32,32,128]{4,3,2,1,0:T(8,128)}, f32[1,2,32,32,128]{4,3,2,1,0:T(8,128)}) custom-call(s32[16]{0:T(128)S(1)} %copy-done.5, f32[4,2,256,128]{3,2,1,0:T(8,128)S(1)} %get-tuple-element.43.near, f32[2,256,128]{2,1,0:T(8,128)S(1)} %collective-permute-done.9.refs_0_, f32[2,256,128]{2,1,0:T(8,128)S(1)} %collective-permute-done.10.refs_1_, ...), custom_call_target="tpu_custom_call" | custom-call | tf_op jit(solution)/shard_map/settle/pallas_call | solution.py:466
  (2 shorter events, 0.0 us)
Async XLA Ops:
  0.6 5.0 %copy-start.1 = (f32[1,2,32,32,128]{4,3,2,1,0:T(8,128)S(1)}, f32[1,2,32,32,128]{4,3,2,1,0:T(8,128)}, u32[]{:S(2)}) copy-start(f32[1,2,32,32,128]{4,3,2,1,0:T(8,128)} %solute.3) | copy-start | bytes 3145732
  0.6 5.0 %copy-start = (f32[1,2,32,32,128]{4,3,2,1,0:T(8,128)S(1)}, f32[1,2,32,32,128]{4,3,2,1,0:T(8,128)}, u32[]{:S(2)}) copy-start(f32[1,2,32,32,128]{4,3,2,1,0:T(8,128)} %phase.3) | copy-start | bytes 3145732
  2.7 8.4 %collective-permute-start = (f32[33,8,128]{2,1,0:T(8,128)}, f32[33,8,128]{2,1,0:T(8,128)S(1)}, u32[]{:S(2)}, u32[]{:S(2)}) collective-permute-start(f32[33,8,128]{2,1,0:T(8,128)} %get-tuple-element.28), channel_id=1, source_target_pairs={{0,1},{1,2},{2,3},{3,4},{4,5},{5,6},{6,7},{7,0},{8,9},{9,10},{10,1... | collective-permute-start | bytes 405512 | tf_op jit(solution)/shard_map/ppermute | solution.py:498
  4.2 7.8 %collective-permute-start.1 = (f32[33,8,128]{2,1,0:T(8,128)}, f32[33,8,128]{2,1,0:T(8,128)S(1)}, u32[]{:S(2)}, u32[]{:S(2)}) collective-permute-start(f32[33,8,128]{2,1,0:T(8,128)} %get-tuple-element.29), channel_id=1, source_target_pairs={{0,7},{1,0},{2,1},{3,2},{4,3},{5,4},{6,5},{7,6},{8,15},{9,8},{10,9... | collective-permute-start | bytes 405512 | tf_op jit(solution)/shard_map/ppermute | solution.py:499
  5.6 0.7 copy-start.2
  12.0 8.8 %copy-start.3 = (f32[24,128]{1,0:T(8,128)S(1)}, f32[24,128]{1,0:T(8,128)}, u32[]{:S(2)}) copy-start(f32[24,128]{1,0:T(8,128)} %get-tuple-element.27.own) | copy-start | bytes 36868
  12.0 7.9 %collective-permute-start.2 = (f32[608,128]{1,0:T(8,128)S(1)}, f32[608,128]{1,0:T(8,128)S(1)}, u32[]{:S(2)}, u32[]{:S(2)}) collective-permute-start(f32[608,128]{1,0:T(8,128)S(1)} %get-tuple-element.31), channel_id=1, source_target_pairs={{0,8},{8,16},{16,24},{24,0},{1,9},{9,17},{17,25},{25,1},{2,10},{10... | collective-permute-start | bytes 933896 | tf_op jit(solution)/shard_map/ppermute | solution.py:504
  12.1 8.7 %collective-permute-start.3 = (f32[608,128]{1,0:T(8,128)S(1)}, f32[608,128]{1,0:T(8,128)S(1)}, u32[]{:S(2)}, u32[]{:S(2)}) collective-permute-start(f32[608,128]{1,0:T(8,128)S(1)} %get-tuple-element.32), channel_id=1, source_target_pairs={{0,24},{8,0},{16,8},{24,16},{1,25},{9,1},{17,9},{25,17},{2,26},{10... | collective-permute-start | bytes 933896 | tf_op jit(solution)/shard_map/ppermute | solution.py:505
  13.8 5.6 %collective-permute-start.4 = (f32[8,128]{1,0:T(8,128)S(1)}, f32[8,128]{1,0:T(8,128)S(1)}, u32[]{:S(2)}, u32[]{:S(2)}) collective-permute-start(f32[8,128]{1,0:T(8,128)S(1)} %slice.7), channel_id=1, source_target_pairs={{0,4},{1,5},{2,6},{3,7},{4,0},{5,1},{6,2},{7,3},{8,12},{9,13},{10,... | collective-permute-start | bytes 12296 | tf_op jit(solution)/shard_map/ppermute | solution.py:482
  16.4 47.7 %collective-permute-start.5 = (f32[512,128]{1,0:T(8,128)S(1)}, f32[512,128]{1,0:T(8,128)S(1)}, u32[]{:S(2)}, u32[]{:S(2)}) collective-permute-start(f32[512,128]{1,0:T(8,128)S(1)} %get-tuple-element.30._), channel_id=1, source_target_pairs={{0,4},{1,5},{2,6},{3,7},{4,0},{5,1},{6,2},{7,3},{8,12},{9,13},{10,... | collective-permute-start | bytes 786440 | tf_op jit(solution)/shard_map/ppermute | solution.py:482
  16.8 18.8 %copy-start.7 = (s32[1,2]{1,0:T(1,128)S(1)}, s32[1,2]{1,0:T(1,128)}, u32[]{:S(2)}) copy-start(s32[1,2]{1,0:T(1,128)} %owner.1) | copy-start | bytes 28
  16.8 47.3 %collective-permute-start.6 = (f32[512,128]{1,0:T(8,128)S(1)}, f32[512,128]{1,0:T(8,128)S(1)}, u32[]{:S(2)}, u32[]{:S(2)}) collective-permute-start(f32[512,128]{1,0:T(8,128)S(1)} %get-tuple-element.34), channel_id=1, source_target_pairs={{0,5},{1,4},{2,7},{3,6},{4,1},{5,0},{6,3},{7,2},{8,13},{9,12},{10,... | collective-permute-start | bytes 786440 | tf_op jit(solution)/shard_map/ppermute | solution.py:482
  33.5 30.7 %collective-permute-start.7 = (f32[512,128]{1,0:T(8,128)}, f32[512,128]{1,0:T(8,128)S(1)}, u32[]{:S(2)}, u32[]{:S(2)}) collective-permute-start(f32[512,128]{1,0:T(8,128)} %get-tuple-element.35), channel_id=1, source_target_pairs={{0,6},{1,7},{2,4},{3,5},{4,2},{5,3},{6,0},{7,1},{8,14},{9,15},{10,... | collective-permute-start | bytes 786440 | tf_op jit(solution)/shard_map/ppermute | solution.py:482
  35.0 30.0 %collective-permute-start.8 = (f32[512,128]{1,0:T(8,128)S(1)}, f32[512,128]{1,0:T(8,128)S(1)}, u32[]{:S(2)}, u32[]{:S(2)}) collective-permute-start(f32[512,128]{1,0:T(8,128)S(1)} %get-tuple-element.36), channel_id=1, source_target_pairs={{0,7},{1,6},{2,5},{3,4},{4,3},{5,2},{6,1},{7,0},{8,15},{9,14},{10,... | collective-permute-start | bytes 786440 | tf_op jit(solution)/shard_map/ppermute | solution.py:482
  62.8 1.3 %copy-start.6 = (f32[4,528,128]{2,1,0:T(8,128)}, f32[4,528,128]{2,1,0:T(8,128)S(1)}, u32[]{:S(2)}) copy-start(f32[4,528,128]{2,1,0:T(8,128)S(1)} %get-tuple-element.42.near) | copy-start | bytes 3244036
  65.1 0.6 copy-start.4
  67.2 43.1 %collective-permute-start.9 = (f32[2,256,128]{2,1,0:T(8,128)S(1)}, f32[2,256,128]{2,1,0:T(8,128)S(1)}, u32[]{:S(2)}, u32[]{:S(2)}) collective-permute-start(f32[2,256,128]{2,1,0:T(8,128)S(1)} %get-tuple-element.38), channel_id=1, source_target_pairs={{0,4},{1,5},{2,6},{3,7},{4,0},{5,1},{6,2},{7,3},{8,12},{9,13},{10,... | collective-permute-start | bytes 786440 | tf_op jit(solution)/shard_map/ppermute | solution.py:482
  68.9 41.4 %collective-permute-start.10 = (f32[2,256,128]{2,1,0:T(8,128)S(1)}, f32[2,256,128]{2,1,0:T(8,128)S(1)}, u32[]{:S(2)}, u32[]{:S(2)}) collective-permute-start(f32[2,256,128]{2,1,0:T(8,128)S(1)} %get-tuple-element.39), channel_id=1, source_target_pairs={{0,5},{1,4},{2,7},{3,6},{4,1},{5,0},{6,3},{7,2},{8,13},{9,12},{10,... | collective-permute-start | bytes 786440 | tf_op jit(solution)/shard_map/ppermute | solution.py:482
  71.0 39.3 %collective-permute-start.11 = (f32[2,256,128]{2,1,0:T(8,128)S(1)}, f32[2,256,128]{2,1,0:T(8,128)S(1)}, u32[]{:S(2)}, u32[]{:S(2)}) collective-permute-start(f32[2,256,128]{2,1,0:T(8,128)S(1)} %get-tuple-element.40), channel_id=1, source_target_pairs={{0,6},{1,7},{2,4},{3,5},{4,2},{5,3},{6,0},{7,1},{8,14},{9,15},{10,... | collective-permute-start | bytes 786440 | tf_op jit(solution)/shard_map/ppermute | solution.py:482
  72.4 41.7 %collective-permute-start.12 = (f32[2,256,128]{2,1,0:T(8,128)S(1)}, f32[2,256,128]{2,1,0:T(8,128)S(1)}, u32[]{:S(2)}, u32[]{:S(2)}) collective-permute-start(f32[2,256,128]{2,1,0:T(8,128)S(1)} %get-tuple-element.41), channel_id=1, source_target_pairs={{0,7},{1,6},{2,5},{3,4},{4,3},{5,2},{6,1},{7,0},{8,15},{9,14},{10,... | collective-permute-start | bytes 786440 | tf_op jit(solution)/shard_map/ppermute | solution.py:482
  74.3 39.8 %copy-start.5 = (s32[16]{0:T(128)S(1)}, s32[16]{0:T(128)}, u32[]{:S(2)}) copy-start(s32[16]{0:T(128)} %table.1) | copy-start | bytes 196

commit v9 on v8

--- a/solution.py
+++ b/solution.py
@@ -164,6 +164,20 @@
         self.middle = edge - 16
         self.size = self.rows * self.middle + self.rows_far * 8
 
+        begins = [min(W + p * self.rows, 2 * W + p * self.rows_far) for p in range(self.half)]
+        ends = [max(W + p * self.rows + self.rows, 2 * W + (p + 1) * self.rows_far) for p in range(self.half)]
+        self.span = max(end - begin for begin, end in zip(begins, ends))
+
+    def first_row(self, piece):
+        begin = jnp.minimum(W + piece * self.rows, 2 * W + piece * self.rows_far)
+        return jnp.minimum(begin, self.edge - W - self.span)
+
+    def indices(self, early):
+        return [0] if early else list(range(self.half // 2, self.half))
+
+    def late(self):
+        return list(range(1, self.half // 2))
+
     def near_row(self, piece, row, gap):
         index = piece * self.rows_near + row
         return index + jnp.where(index < W, 0, gap)
@@ -203,8 +217,9 @@
 UNROLL = 4
 
 
-def march(first, last, starts, source, target, coefs_of):
-    def one_row(row, carry):
+def march(first, last, starts, source, target, coefs_of, base=0):
+    def one_row(index, carry):
+        row = base + index
         for start in starts:
             new_p, new_u = cells(source[0], source[1], row, start, coefs_of(row, start))
             target[0][row, start : start + 8, :] = new_p
@@ -214,12 +229,18 @@
     lax.fori_loop(first, last, one_row, 0, unroll=UNROLL)
 
 
-def inner_kernel(plan, own, phase, solute, *rest):
-    tiles, edge, count = plan.tiles, plan.edge, plan.inner // 2
-    outs, scratch = rest[: plan.half // 2], rest[plan.half // 2 :]
+def inner_kernel(plan, early, own, phase, solute, _, *rest):
+    tiles, edge = plan.tiles, plan.edge
+    indices = plan.indices(early)
+    outs, scratch = rest[: len(indices)], rest[len(indices) :]
     pairs = (scratch[:2], scratch[2:])
     mine = lax.rem(lax.axis_index("gy"), plan.half)
-    base = mine // (plan.half // 2) * count
+    if early:
+        count = plan.span
+        base = plan.first_row(mine) - W
+    else:
+        count = plan.inner // 2
+        base = (1 - mine // (plan.half // 2)) * count
 
     def load_row(row, carry):
         for tile in range(tiles):
@@ -237,8 +258,11 @@
     for step in range(NSTEPS):
         starts = range(PAD, PAD + tiles * edge, 8)
         march(step + 1, count + 2 * W - step - 1, starts, pairs[step % 2], pairs[(step + 1) % 2], coefs_of)
-    for index, out in enumerate(outs):
+    for index, out in zip(indices, outs):
         pack(plan, True, mine ^ index, pairs[NSTEPS % 2], -base, PAD, out)
+    if early:
+        tail = 2 * tiles * plan.size
+        outs[0][tail : tail + AUX, :] = own[8 * tiles : 8 * tiles + AUX, :]
 
 
 def pack(plan, far, piece, done, row_shift, col_shift, out):
@@ -251,26 +275,28 @@
                 out[begin + at : begin + at + count, :] = values[row + row_shift, start : start + count, :]
 
 
-def run_inner(plan, own, phase, solute):
-    rows = plan.inner // 2 + 2 * W
+def run_inner(plan, early, own, phase, solute, after):
+    rows = (plan.span if early else plan.inner // 2) + 2 * W
     buffer = pltpu.VMEM((rows, plan.tiles * plan.edge + 2 * PAD, plan.depth), jnp.float32)
     vmem = pl.BlockSpec(memory_space=pltpu.VMEM)
-    shape = jax.ShapeDtypeStruct((2 * plan.tiles * plan.size, plan.depth), jnp.float32)
+    shape = jax.ShapeDtypeStruct((2 * plan.tiles * plan.size + (AUX if early else 0), plan.depth), jnp.float32)
+    count = len(plan.indices(early))
     return pl.pallas_call(
-        functools.partial(inner_kernel, plan),
-        in_specs=[vmem] * 3,
-        out_specs=[vmem] * (plan.half // 2),
-        out_shape=[shape] * (plan.half // 2),
+        functools.partial(inner_kernel, plan, early),
+        in_specs=[vmem] * 3 + [pl.BlockSpec(memory_space=pl.ANY)],
+        out_specs=[vmem] * count,
+        out_shape=[shape] * count,
         scratch_shapes=[buffer] * 4,
         compiler_params=pltpu.CompilerParams(vmem_limit_bytes=16 * 1024 * 1024),
-        cost_estimate=pl.CostEstimate(flops=10**8, bytes_accessed=24 * 1024 * 1024, transcendentals=0),
-        name="inner",
-    )(own, phase, solute)
+        cost_estimate=pl.CostEstimate(flops=10**8, bytes_accessed=16 * 1024 * 1024, transcendentals=0),
+        name="first" if early else "inner",
+    )(own, phase, solute, after)
 
 
 def outer_kernel(plan, own, phase, solute, y_lo, y_hi, x_lo, x_hi, partner, out, *rest):
     tiles, edge, depth, half = plan.tiles, plan.edge, plan.depth, plan.half
-    far_outs, scratch = rest[: half // 2], rest[half // 2 :]
+    late = plan.late()
+    far_outs, scratch = rest[: len(late)], rest[len(late) :]
     pairs, coefs = (scratch[:2], scratch[2:4]), scratch[4]
     cols = tiles * edge
     width = cols + 2 * W
@@ -317,23 +343,45 @@
 
     any_zone = coefs_of(lambda row: jnp.where(row < W, 0, jnp.where(row < W + edge, 1, 2)))
 
+    own_zone = coefs_of(lambda row: 1)
+
+    def blocks(first, last):
+        low, high = (first + W - shift) // 8 * 8, -(-(last + W - shift) // 8) * 8
+        return list(range(PAD + shift + low, PAD + shift + high, 8))
+
+    mine = lax.rem(lax.axis_index("gy"), half)
     for step in range(1, NSTEPS + 1):
+        source, target = pairs[(step - 1) % 2], pairs[step % 2]
         left = NSTEPS - step
         shift = W if step == NSTEPS else 0
-        starts = range(PAD + shift, PAD + width - shift, 8)
-        march(W - left, W + edge + left, starts, pairs[(step - 1) % 2], pairs[step % 2], any_zone)
+        strip = W + left
+        whole = blocks(-left, cols + left)
+        sides = blocks(-left, 8 + left) + blocks(cols - 8 - left, cols + left)
+        lasts = []
+        for tile in range(tiles):
+            col, count = plan.columns("last", tile)
+            lasts += blocks(tile * edge + col - left, tile * edge + col + count + left)
+        ends = sorted(set(sides + lasts))
+        march(W - left, W + strip, whole, source, target, any_zone)
+        march(W + strip, W + strip + W, ends, source, target, own_zone)
+        march(W + strip + W, W + edge - strip - W, sides, source, target, own_zone)
+        march(W + edge - strip - W, W + edge - strip, ends, source, target, own_zone)
+        march(W + edge - strip, W + edge + left, whole, source, target, any_zone)
+        middle = [start for start in whole if start not in sides]
+        for index in late:
+            base = W + plan.first_row(mine ^ index)
+            march(-left, plan.span + left, middle, source, target, own_zone, base)
     done = pairs[NSTEPS % 2]
-    mine = lax.rem(lax.axis_index("gy"), half)
-    for index, far_out in enumerate(far_outs):
-        pack(plan, True, mine ^ (half // 2 + index), done, W, PAD + W, far_out)
+    for index, far_out in zip(late, far_outs):
+        pack(plan, True, mine ^ index, done, W, PAD + W, far_out)
     tail = 2 * tiles * plan.size
     for piece in range(half):
         pack(plan, False, piece, done, W, PAD + W, out.at[piece])
         out[piece, tail : tail + AUX, :] = own[8 * tiles : 8 * tiles + AUX, :]
-        out[piece, tail + AUX : tail + 2 * AUX, :] = partner[...]
-
-
-def run_outer(plan, own, phase, solute, halos, partner):
+        out[piece, tail + AUX : tail + 2 * AUX, :] = partner[tail : tail + AUX, :]
+
+
+def run_outer(plan, own, phase, solute, halos, first):
     tiles, edge, depth = plan.tiles, plan.edge, plan.depth
     width = tiles * edge + 2 * W
     buffer = pltpu.VMEM((edge + 2 * W, width + 2 * PAD, depth), jnp.float32)
@@ -343,87 +391,67 @@
     return pl.pallas_call(
         functools.partial(outer_kernel, plan),
         in_specs=[vmem] * 8,
-        out_specs=[vmem] * (1 + plan.half // 2),
-        out_shape=[near] + [far] * (plan.half // 2),
+        out_specs=[vmem] * (1 + len(plan.late())),
+        out_shape=[near] + [far] * len(plan.late()),
         scratch_shapes=[buffer] * 4 + [pltpu.VMEM((3, 3, width, depth), jnp.float32)],
         compiler_params=pltpu.CompilerParams(vmem_limit_bytes=16 * 1024 * 1024),
         cost_estimate=pl.CostEstimate(flops=10**8, bytes_accessed=40 * 1024 * 1024, transcendentals=0),
         name="outer",
-    )(own, phase, solute, *halos, partner)
-
-
-def table_kernel(plan, near, table, names, count, sems):
-    pieces, tiles, half = plan.pieces, plan.tiles, plan.half
+    )(own, phase, solute, *halos, first)
+
+
+def route_kernel(plan, near, *refs):
+    pieces, tiles, half, size = plan.pieces, plan.tiles, plan.half, 2 * plan.size
+    far, near_out, far_outs, table = refs[:half], refs[half], refs[half + 1 : 2 * half + 1], refs[2 * half + 1]
+    held, names, count, sem = refs[2 * half + 2 :]
     me = lax.axis_index("gy")
     base = me - lax.rem(me, half)
-    tail = 2 * tiles * plan.size
-    copies = []
-    for piece in range(half):
-        for index in range(2):
-            copy = pltpu.make_async_copy(
-                near.at[piece, pl.ds(tail + index * AUX, 1), :], names.at[index, piece], sems.at[index, piece]
-            )
-            copy.start()
-            copies.append(copy)
+    copy = pltpu.make_async_copy(near.at[:, pl.ds(tiles * size, 2 * AUX), :], names, sem)
+    copy.start()
     for peer in range(pieces):
         count[peer] = 0
-    for copy in copies:
-        copy.wait()
-    for home in range(pieces):
-        other = (home // half != base // half).astype(jnp.int32)
-        for tile in range(tiles):
-            peer = lax.rem(names[other, home % half, 0, tile].astype(jnp.int32), pieces)
-            slot = count[peer]
-            table[peer * tiles + slot] = home * tiles + tile
-            count[peer] = slot + 1
-
-
-def find_table(plan, near):
-    return pl.pallas_call(
-        functools.partial(table_kernel, plan),
-        in_specs=[pl.BlockSpec(memory_space=pl.ANY)],
-        out_specs=pl.BlockSpec(memory_space=pltpu.SMEM),
-        out_shape=jax.ShapeDtypeStruct((plan.pieces * plan.tiles,), jnp.int32),
-        scratch_shapes=[
-            pltpu.SMEM((2, plan.half, 1, plan.depth), jnp.float32),
-            pltpu.SMEM((plan.pieces,), jnp.int32),
-            pltpu.SemaphoreType.DMA((2, plan.half)),
-        ],
-        name="table",
-    )(near)
-
-
-def route_kernel(plan, table, near, *refs):
-    tiles, half, size = plan.tiles, plan.half, 2 * plan.size
-    far, near_out, far_outs, held = refs[:half], refs[half], refs[half + 1 : 2 * half + 1], refs[-1]
-    me = lax.axis_index("gy")
-    base = me - lax.rem(me, half)
     for piece in range(half):
         for tile in range(tiles):
             held[(base + piece) * tiles + tile] = near[piece, tile * size : (tile + 1) * size, :]
     for index in range(half):
         for tile in range(tiles):
             held[(me ^ (half + index)) * tiles + tile] = far[index][tile * size : (tile + 1) * size, :]
+    copy.wait()
+    for home in range(pieces):
+        other = (home // half != base // half).astype(jnp.int32)
+        for tile in range(tiles):
+            peer = lax.rem(names[home % half, other * AUX, tile].astype(jnp.int32), pieces)
+            slot = count[peer]
+            table[peer * tiles + slot] = home * tiles + tile
+            count[peer] = slot + 1
     for index in range(half):
         for slot in range(tiles):
             far_outs[index][slot] = held[table[(me ^ (half + index)) * tiles + slot]]
             near_out[index, slot] = held[table[(base + index) * tiles + slot]]
 
 
-def route(plan, table, near, far):
+def route(plan, near, far):
     tiles, half, size, depth = plan.tiles, plan.half, 2 * plan.size, plan.depth
     vmem = pl.BlockSpec(memory_space=pltpu.VMEM)
     one = jax.ShapeDtypeStruct((tiles, size, depth), jnp.float32)
+    count = plan.pieces * tiles
     results = pl.pallas_call(
         functools.partial(route_kernel, plan),
-        in_specs=[pl.BlockSpec(memory_space=pltpu.SMEM)] + [vmem] * (half + 1),
-        out_specs=[vmem] * (half + 1),
-        out_shape=[jax.ShapeDtypeStruct((half, tiles, size, depth), jnp.float32)] + [one] * half,
-        scratch_shapes=[pltpu.VMEM((plan.pieces * tiles, size, depth), jnp.float32)],
+        in_specs=[vmem] * (half + 1),
+        out_specs=[vmem] * (half + 1) + [pl.BlockSpec(memory_space=pltpu.SMEM)],
+        out_shape=[jax.ShapeDtypeStruct((half, tiles, size, depth), jnp.float32)]
+        + [one] * half
+        + [jax.ShapeDtypeStruct((count,), jnp.int32)],
+        scratch_shapes=[
+            pltpu.VMEM((count, size, depth), jnp.float32),
+            pltpu.SMEM((half, 2 * AUX, depth), jnp.float32),
+            pltpu.SMEM((plan.pieces,), jnp.int32),
+            pltpu.SemaphoreType.DMA,
+        ],
         compiler_params=pltpu.CompilerParams(vmem_limit_bytes=16 * 1024 * 1024),
         name="route",
-    )(table, near, *far)
-    return results[0], results[1:]
+    )(near, *far)
+    return results[0], results[1 : half + 1], results[-1]
 
 
 def settle_kernel(plan, table, near, *refs):
@@ -482,12 +510,21 @@
     return lax.ppermute(values, "gy", [(i, i ^ mask) for i in range(lax.axis_size("gy"))])
 
 
+def around(axis, low, high):
+    return lax.ppermute(low, axis, ring(axis, 1)), lax.ppermute(high, axis, ring(axis, -1))
+
+
+def at_once(exchange, together, *values):
+    return lax.cond(together, exchange, exchange, *values)
+
+
 def among_half(plan, values, together):
+    groups = [list(range(plan.half)), list(range(plan.half, plan.pieces))]
+
     def exchange(values):
-        groups = [list(range(plan.half)), list(range(plan.half, plan.pieces))]
         return lax.all_to_all(values, "gy", 0, 0, axis_index_groups=groups, tiled=True)
 
-    return lax.cond(together, exchange, exchange, values)
+    return at_once(exchange, together, values)
 
 
 def per_device(phase, solute, undercool, mobility, diffusivity, owner):
@@ -495,20 +532,21 @@
     plan = Plan(lax.axis_size("gy"), tiles, edge, depth)
     half = plan.half
     to_prev, to_next, own = pack_y(phase, solute, (undercool, mobility, diffusivity), owner)
-    y_lo = lax.ppermute(to_next, "gy", ring("gy", 1))
-    y_hi = lax.ppermute(to_prev, "gy", ring("gy", -1))
-    first = run_inner(plan, own, phase, solute)
-    far = [swap(values, half + index) for index, values in enumerate(first)]
-    partner = swap(own[8 * tiles :], half)
-    to_prev, to_next = pack_x(phase, solute, own, y_lo, y_hi, first[0])
-    x_lo = lax.ppermute(to_next, "gx", ring("gx", 1))
-    x_hi = lax.ppermute(to_prev, "gx", ring("gx", -1))
-    near, *second = run_outer(plan, own, phase, solute, (y_lo, y_hi, x_lo, x_hi), partner)
-    far += [swap(values, half + half // 2 + index) for index, values in enumerate(second)]
+    y_lo, y_hi = around("gy", to_next, to_prev)
     together = owner[0, 0] >= 0
+    far = {}
+    (first,) = run_inner(plan, True, own, phase, solute, own)
+    far[0] = swap(first, half)
+    inner = run_inner(plan, False, own, phase, solute, first)
+    for index, values in zip(plan.indices(False), inner):
+        far[index] = swap(values, half + index)
+    to_prev, to_next = pack_x(phase, solute, own, y_lo, y_hi, inner[0])
+    x_lo, x_hi = at_once(lambda low, high: around("gx", low, high), together, to_next, to_prev)
+    near, *late = run_outer(plan, own, phase, solute, (y_lo, y_hi, x_lo, x_hi), far[0])
+    for index, values in zip(plan.late(), late):
+        far[index] = swap(values, half + index)
     near = among_half(plan, near, together)
-    table = find_table(plan, near)
-    near, far = route(plan, table, near, far)
+    near, far, table = route(plan, near, [far[index] for index in range(half)])
     far = [swap(values, half + index) for index, values in enumerate(far)]
     near = among_half(plan, near, together)
     return tuple(settle(plan, table, near, far))

time: 117 us -> 137 us (1.17)
  waiting for transfers between devices: 7.03 us -> 17 us
  blocking collectives: 63.2 us -> 71.5 us
  Pallas kernels: 24.3 us -> 29.5 us
  starting transfers between devices: 19.5 us -> 16.9 us
    all_to_all x2, blocking collectives: 63.2 us -> 71.5 us  [exchange(): lax.all_to_all(values, 'gy', 0, 0, axis_index_groups=groups, tiled=True)]
    ppermute x9 -> x8, waiting for transfers between devices: 4.74 us -> 10.1 us  [swap(): lax.ppermute(values, 'gy', [(i, i ^ mask) for i in range(lax.axis_size('g...]
    ppermute x4, waiting for transfers between devices: 2.29 us -> 6.93 us  [the longest x2 6.17 us: around(): lax.ppermute(low, axis, ring(axis, 1))]
    pallas_call x3, Pallas kernels: 7.54 us -> 12.1 us  [the longest x2 9.07 us: run_inner(): pl.pallas_call(functools.partial(inner_kernel, plan, early), in_specs=[vm...]
    ppermute x9 -> x8, starting transfers between devices: 14.7 us -> 12.1 us  [swap(): lax.ppermute(values, 'gy', [(i, i ^ mask) for i in range(lax.axis_size('g...]
  transfers between devices with their start and end apart: 13 -> 12, of which waited for: 5 -> 4; matrix products, arithmetic and copies ran while one was open for 0% -> 0% of each run, Pallas kernels for 16% -> 13%
where the time goes in v9:
time: 137 us; the launch traced here: 136 us
  blocking collectives  71.5 us (52%)
  Pallas kernels  29.5 us (22%)
  waiting for transfers between devices  17 us (12%)
  starting transfers between devices  16.9 us (12%)
    all_to_all x2, blocking collectives, exchange(): lax.all_to_all(values, 'gy', 0, 0, axis_index_groups=groups, tiled=True)  71.5 us
    pallas_call x1, Pallas kernels, run_outer(): pl.pallas_call(functools.partial(outer_kernel, plan), in_specs=[vmem] * 8...  12.6 us
    ppermute x8, starting transfers between devices, swap(): lax.ppermute(values, 'gy', [(i, i ^ mask) for i in range(lax.axis_size('g...  12.1 us
    ppermute x8, waiting for transfers between devices, swap(): lax.ppermute(values, 'gy', [(i, i ^ mask) for i in range(lax.axis_size('g...  10.1 us
    pallas_call x2, Pallas kernels, run_inner(): pl.pallas_call(functools.partial(inner_kernel, plan, early), in_specs=[vm...  9.07 us
    ppermute x2, waiting for transfers between devices, around(): lax.ppermute(low, axis, ring(axis, 1))  6.17 us
    ppermute x2, starting transfers between devices, around(): lax.ppermute(high, axis, ring(axis, -1))  3.14 us
    pallas_call x1, Pallas kernels, route(): pl.pallas_call(functools.partial(route_kernel, plan), in_specs=[vmem] * (...  3.06 us
  transfers between devices with their start and end apart: 12, of which 4 were waited for; matrix products, arithmetic and copies ran while one was open for 0% of the time, Pallas kernels for 13%

profile of v9, /device:TPU:8, one launch (start us, length us, event | category | flops | bytes accessed | tf_op | source)
XLA Modules:
  0.0 136.4 jit_solution(10596624333581559865)
XLA Ops:
  0.6 0.0 copy-start.1
  0.6 0.0 copy-start
  0.7 2.0 %pack_y.1 = (f32[33,8,128]{2,1,0:T(8,128)}, f32[33,8,128]{2,1,0:T(8,128)}, f32[24,128]{1,0:T(8,128)}) custom-call(f32[1,2]{1,0:T(1,128)} %under.1, f32[1,2]{1,0:T(1,128)} %mobile.1, f32[1,2]{1,0:T(1,128)} %spread.1, s32[1,2]{1,0:T(1,128)} %owner.1, f32[1,2,32,32,128]{4,3,2,1,0:T(8,128)} %phase.5, f32[1,2,32,32,128]{4,3,2,1,0:T(8,128)} %phase.5, ...), custom_call_target="tpu_custom_call" | custom-call | tf_op jit(solution)/shard_map/pack_y/pallas_call | solution.py:47
  2.7 0.0 copy-done.1
  2.7 0.0 copy-done
  2.7 0.0 copy-start.2
  2.7 0.7 copy-done.2
  3.4 0.0 copy-start.6
  3.4 0.0 copy-start.5
  3.4 3.5 %first.1._ = f32[520,128]{1,0:T(8,128)S(1)} custom-call(f32[24,128]{1,0:T(8,128)S(1)} %copy-done.2, f32[1,2,32,32,128]{4,3,2,1,0:T(8,128)S(1)} %copy-done, f32[1,2,32,32,128]{4,3,2,1,0:T(8,128)S(1)} %copy-done.1, f32[24,128]{1,0:T(8,128)S(1)} %copy-done.2), custom_call_target="tpu_custom_call" | custom-call | flops 100000000 | bytes 16777216 | tf_op jit(solution)/shard_map/first/pallas_call | solution.py:284
  6.9 2.7 %collective-permute-start.6 = (f32[520,128]{1,0:T(8,128)S(1)}, f32[520,128]{1,0:T(8,128)S(1)}, u32[]{:S(2)}, u32[]{:S(2)}) collective-permute-start(f32[520,128]{1,0:T(8,128)S(1)} %first.1._), channel_id=1, source_target_pairs={{0,4},{1,5},{2,6},{3,7},{4,0},{5,1},{6,2},{7,3},{8,12},{9,13},{10,... | collective-permute-start | bytes 798728 | tf_op jit(solution)/shard_map/ppermute | solution.py:510
  9.6 0.0 copy-done.6
  9.6 1.5 %collective-permute-start.4 = (f32[33,8,128]{2,1,0:T(8,128)S(1)}, f32[33,8,128]{2,1,0:T(8,128)S(1)}, u32[]{:S(2)}, u32[]{:S(2)}) collective-permute-start(f32[33,8,128]{2,1,0:T(8,128)S(1)} %copy-done.6), channel_id=1, source_target_pairs={{0,1},{1,2},{2,3},{3,4},{4,5},{5,6},{6,7},{7,0},{8,9},{9,10},{10,1... | collective-permute-start | bytes 405512 | tf_op jit(solution)/shard_map/ppermute | solution.py:514
  11.1 0.0 copy-done.5
  11.1 0.0 copy-start.4
  11.1 1.4 %collective-permute-start.5 = (f32[33,8,128]{2,1,0:T(8,128)S(1)}, f32[33,8,128]{2,1,0:T(8,128)S(1)}, u32[]{:S(2)}, u32[]{:S(2)}) collective-permute-start(f32[33,8,128]{2,1,0:T(8,128)S(1)} %copy-done.5), channel_id=1, source_target_pairs={{0,7},{1,0},{2,1},{3,2},{4,3},{5,4},{6,5},{7,6},{8,15},{9,8},{10,9... | collective-permute-start | bytes 405512 | tf_op jit(solution)/shard_map/ppermute | solution.py:514
  12.5 5.5 %inner.1 = (f32[512,128]{1,0:T(8,128)}, f32[512,128]{1,0:T(8,128)}) custom-call(f32[24,128]{1,0:T(8,128)S(1)} %copy-done.2, f32[1,2,32,32,128]{4,3,2,1,0:T(8,128)S(1)} %copy-done, f32[1,2,32,32,128]{4,3,2,1,0:T(8,128)S(1)} %copy-done.1, f32[520,128]{1,0:T(8,128)S(1)} %first.1._), custom_call_target="tpu_custom_call" | custom-call | flops 100000000 | bytes 16777216 | tf_op jit(solution)/shard_map/inner/pallas_call | solution.py:284
  18.0 0.0 collective-permute-start.9
  18.1 2.1 %collective-permute-start.8 = (f32[512,128]{1,0:T(8,128)}, f32[512,128]{1,0:T(8,128)S(1)}, u32[]{:S(2)}, u32[]{:S(2)}) collective-permute-start(f32[512,128]{1,0:T(8,128)} %get-tuple-element.44._), channel_id=1, source_target_pairs={{0,6},{1,7},{2,4},{3,5},{4,2},{5,3},{6,0},{7,1},{8,14},{9,15},{10,... | collective-permute-start | bytes 786440 | tf_op jit(solution)/shard_map/ppermute | solution.py:510
  20.1 0.0 copy-done.4
  20.2 0.0 copy-start.3
  20.2 0.0 collective-permute-done.4.y_lo
  20.2 0.0 collective-permute-done.5.y_hi
  20.3 8.7 %conditional.3 = (f32[608,128]{1,0:T(8,128)}, f32[608,128]{1,0:T(8,128)}) conditional(s32[]{:T(128)} %bitcast, (f32[608,128]{1,0:T(8,128)S(1)}, f32[608,128]{1,0:T(8,128)S(1)}) %tuple.27, (f32[608,128]{1,0:T(8,128)S(1)}, f32[608,128]{1,0:T(8,128)S(1)}) %tuple.27), branch_computations={%region_0.0_spmd, %region_1.0_spmd} | conditional | bytes 2490464 | solution.py:518
  20.3 0.1 collective-permute-start.2
  20.3 1.7 %collective-permute-start.3 = (f32[608,128]{1,0:T(8,128)S(1)}, f32[608,128]{1,0:T(8,128)}, u32[]{:S(2)}, u32[]{:S(2)}) collective-permute-start(f32[608,128]{1,0:T(8,128)S(1)} %get-tuple-element.21), channel_id=1, source_target_pairs={{0,24},{8,0},{16,8},{24,16},{1,25},{9,1},{17,9},{25,17},{2,26},{10... | collective-permute-start | bytes 933896 | tf_op jit(solution)/shard_map/cond/branch_1_fun/ppermute | solution.py:514
  22.1 6.2 %collective-permute-done.2 = f32[608,128]{1,0:T(8,128)} collective-permute-done((f32[608,128]{1,0:T(8,128)S(1)}, f32[608,128]{1,0:T(8,128)}, u32[]{:S(2)}, u32[]{:S(2)}) %collective-permute-start.2) | collective-permute-done | bytes 311328 | tf_op jit(solution)/shard_map/cond/branch_1_fun/ppermute | solution.py:514
  28.2 0.8 collective-permute-done.3
  29.0 6.0 %collective-permute-done.6.partner.refs_0_ = f32[520,128]{1,0:T(8,128)S(1)} collective-permute-done((f32[520,128]{1,0:T(8,128)S(1)}, f32[520,128]{1,0:T(8,128)S(1)}, u32[]{:S(2)}, u32[]{:S(2)}) %collective-permute-start.6) | collective-permute-done | bytes 266272 | tf_op jit(solution)/shard_map/ppermute | solution.py:510
  35.0 0.0 copy-done.3
  35.0 12.6 %outer.1 = (f32[4,528,128]{2,1,0:T(8,128)S(1)}, f32[512,128]{1,0:T(8,128)S(1)}) custom-call(f32[24,128]{1,0:T(8,128)S(1)} %copy-done.3, f32[1,2,32,32,128]{4,3,2,1,0:T(8,128)S(1)} %copy-done, f32[1,2,32,32,128]{4,3,2,1,0:T(8,128)S(1)} %copy-done.1, f32[33,8,128]{2,1,0:T(8,128)S(1)} %collective-permute-done.4.y_lo, ...), custom_call_target="tpu_custom_call" | custom-call | flops 100000000 | bytes 41943040 | tf_op jit(solution)/shard_map/outer/pallas_call | solution.py:391
  47.6 1.5 %collective-permute-start.7 = (f32[512,128]{1,0:T(8,128)S(1)}, f32[512,128]{1,0:T(8,128)S(1)}, u32[]{:S(2)}, u32[]{:S(2)}) collective-permute-start(f32[512,128]{1,0:T(8,128)S(1)} %get-tuple-element.50), channel_id=1, source_target_pairs={{0,5},{1,4},{2,7},{3,6},{4,1},{5,0},{6,3},{7,2},{8,13},{9,12},{10,... | collective-permute-start | bytes 786440 | tf_op jit(solution)/shard_map/ppermute | solution.py:510
  49.1 32.6 %conditional.4 = (f32[4,528,128]{2,1,0:T(8,128)}) conditional(s32[]{:T(128)} %bitcast, f32[4,528,128]{2,1,0:T(8,128)S(1)} %get-tuple-element.49, f32[4,528,128]{2,1,0:T(8,128)S(1)} %get-tuple-element.49), branch_computations={%region_2.0_spmd, %region_3.0_spmd} | conditional | bytes 2162696 | solution.py:518
  49.1 32.6 %all_to_all.17 = f32[4,528,128]{2,1,0:T(8,128)} all-to-all(f32[4,528,128]{2,1,0:T(8,128)S(1)} %param.3), channel_id=1, replica_groups={{0,1,2,3},{4,5,6,7},{8,9,10,11},{12,13,14,15},{16,17,18,19},{20,21,22,2..., dimensions={0} | all-to-all | bytes 2162688 | tf_op jit(solution)/shard_map/cond/branch_1_fun/all_to_all | solution.py:525
  81.7 0.0 collective-permute-done.9.refs_3_
  81.8 0.0 collective-permute-done.8.refs_2_
  81.8 0.0 collective-permute-done.7.refs_1_
  81.8 3.1 %route.1 = (f32[4,2,256,128]{3,2,1,0:T(8,128)S(1)}, f32[2,256,128]{2,1,0:T(8,128)S(1)}, f32[2,256,128]{2,1,0:T(8,128)S(1)}, f32[2,256,128]{2,1,0:T(8,128)S(1)}, ...) custom-call(f32[4,528,128]{2,1,0:T(8,128)} %get-tuple-element.62.near, f32[520,128]{1,0:T(8,128)S(1)} %collective-permute-done.6.partner.refs_0_, ...), custom_call_target="tpu_custom_call" | custom-call | tf_op jit(solution)/shard_map/route/pallas_call | solution.py:438
  84.8 0.1 collective-permute-start.10
  84.9 3.1 %collective-permute-start.11 = (f32[2,256,128]{2,1,0:T(8,128)S(1)}, f32[2,256,128]{2,1,0:T(8,128)S(1)}, u32[]{:S(2)}, u32[]{:S(2)}) collective-permute-start(f32[2,256,128]{2,1,0:T(8,128)S(1)} %get-tuple-element.55), channel_id=1, source_target_pairs={{0,5},{1,4},{2,7},{3,6},{4,1},{5,0},{6,3},{7,2},{8,13},{9,12},{10,... | collective-permute-start | bytes 786440 | tf_op jit(solution)/shard_map/ppermute | solution.py:510
  88.0 0.9 collective-permute-start.12
  88.9 1.9 %collective-permute-start.13 = (f32[2,256,128]{2,1,0:T(8,128)S(1)}, f32[2,256,128]{2,1,0:T(8,128)S(1)}, u32[]{:S(2)}, u32[]{:S(2)}) collective-permute-start(f32[2,256,128]{2,1,0:T(8,128)S(1)} %get-tuple-element.57), channel_id=1, source_target_pairs={{0,7},{1,6},{2,5},{3,4},{4,3},{5,2},{6,1},{7,0},{8,15},{9,14},{10,... | collective-permute-start | bytes 786440 | tf_op jit(solution)/shard_map/ppermute | solution.py:510
  90.7 38.9 %conditional.5 = (f32[4,2,256,128]{3,2,1,0:T(8,128)}) conditional(s32[]{:T(128)} %bitcast, f32[4,2,256,128]{3,2,1,0:T(8,128)S(1)} %get-tuple-element.53, f32[4,2,256,128]{3,2,1,0:T(8,128)S(1)} %get-tuple-element.53), branch_computations={%region_4.0_spmd, %region_5.0_spmd} | conditional | bytes 2097160 | solution.py:518
  90.7 38.9 %all_to_all.19 = f32[4,2,256,128]{3,2,1,0:T(8,128)} all-to-all(f32[4,2,256,128]{3,2,1,0:T(8,128)S(1)} %param.5), channel_id=1, replica_groups={{0,1,2,3},{4,5,6,7},{8,9,10,11},{12,13,14,15},{16,17,18,19},{20,21,22,2..., dimensions={0} | all-to-all | bytes 2097152 | tf_op jit(solution)/shard_map/cond/branch_1_fun/all_to_all | solution.py:525
  129.6 0.0 collective-permute-done.10.refs_0_
  129.6 0.0 collective-permute-done.11.refs_1_
  129.6 0.0 collective-permute-done.12.refs_2_
  129.6 4.0 %collective-permute-done.13.refs_3_ = f32[2,256,128]{2,1,0:T(8,128)S(1)} collective-permute-done((f32[2,256,128]{2,1,0:T(8,128)S(1)}, f32[2,256,128]{2,1,0:T(8,128)S(1)}, u32[]{:S(2)}, u32[]{:S(2)}) %collective-permute-start.13) | collective-permute-done | bytes 262176 | tf_op jit(solution)/shard_map/ppermute | solution.py:510
  133.7 2.8 %settle.1 = (f32[1,2,32,32,128]{4,3,2,1,0:T(8,128)}, f32[1,2,32,32,128]{4,3,2,1,0:T(8,128)}) custom-call(s32[16]{0:T(128)S(1)} %get-tuple-element.52.table, f32[4,2,256,128]{3,2,1,0:T(8,128)} %get-tuple-element.63.near, f32[2,256,128]{2,1,0:T(8,128)S(1)} %collective-permute-done.10.refs_0_, f32[2,256,128]{2,1,0:T(8,128)S(1)} %collective-permute-done.11.refs_1_, ...), custom_call_target="tpu_custom_call" | custom-call | tf_op jit(solution)/shard_map/settle/pallas_call | solution.py:494
  (1 shorter events, 0.0 us)
Async XLA Ops:
  0.6 2.0 %copy-start.1 = (f32[1,2,32,32,128]{4,3,2,1,0:T(8,128)S(1)}, f32[1,2,32,32,128]{4,3,2,1,0:T(8,128)}, u32[]{:S(2)}) copy-start(f32[1,2,32,32,128]{4,3,2,1,0:T(8,128)} %solute.5) | copy-start | bytes 3145732
  0.6 2.0 %copy-start = (f32[1,2,32,32,128]{4,3,2,1,0:T(8,128)S(1)}, f32[1,2,32,32,128]{4,3,2,1,0:T(8,128)}, u32[]{:S(2)}) copy-start(f32[1,2,32,32,128]{4,3,2,1,0:T(8,128)} %phase.5) | copy-start | bytes 3145732
  2.7 0.7 copy-start.2
  3.4 6.2 %copy-start.6 = (f32[33,8,128]{2,1,0:T(8,128)S(1)}, f32[33,8,128]{2,1,0:T(8,128)}, u32[]{:S(2)}) copy-start(f32[33,8,128]{2,1,0:T(8,128)} %get-tuple-element.42) | copy-start | bytes 405508
  3.4 7.7 %copy-start.5 = (f32[33,8,128]{2,1,0:T(8,128)S(1)}, f32[33,8,128]{2,1,0:T(8,128)}, u32[]{:S(2)}) copy-start(f32[33,8,128]{2,1,0:T(8,128)} %get-tuple-element.43) | copy-start | bytes 405508
  6.9 28.1 %collective-permute-start.6 = (f32[520,128]{1,0:T(8,128)S(1)}, f32[520,128]{1,0:T(8,128)S(1)}, u32[]{:S(2)}, u32[]{:S(2)}) collective-permute-start(f32[520,128]{1,0:T(8,128)S(1)} %first.1._), channel_id=1, source_target_pairs={{0,4},{1,5},{2,6},{3,7},{4,0},{5,1},{6,2},{7,3},{8,12},{9,13},{10,... | collective-permute-start | bytes 798728 | tf_op jit(solution)/shard_map/ppermute | solution.py:510
  9.6 10.6 %collective-permute-start.4 = (f32[33,8,128]{2,1,0:T(8,128)S(1)}, f32[33,8,128]{2,1,0:T(8,128)S(1)}, u32[]{:S(2)}, u32[]{:S(2)}) collective-permute-start(f32[33,8,128]{2,1,0:T(8,128)S(1)} %copy-done.6), channel_id=1, source_target_pairs={{0,1},{1,2},{2,3},{3,4},{4,5},{5,6},{6,7},{7,0},{8,9},{9,10},{10,1... | collective-permute-start | bytes 405512 | tf_op jit(solution)/shard_map/ppermute | solution.py:514
  11.1 9.0 %copy-start.4 = (s32[1,2]{1,0:T(1,128)S(1)}, s32[1,2]{1,0:T(1,128)}, u32[]{:S(2)}) copy-start(s32[1,2]{1,0:T(1,128)} %owner.1) | copy-start | bytes 28
  11.1 9.1 %collective-permute-start.5 = (f32[33,8,128]{2,1,0:T(8,128)S(1)}, f32[33,8,128]{2,1,0:T(8,128)S(1)}, u32[]{:S(2)}, u32[]{:S(2)}) collective-permute-start(f32[33,8,128]{2,1,0:T(8,128)S(1)} %copy-done.5), channel_id=1, source_target_pairs={{0,7},{1,0},{2,1},{3,2},{4,3},{5,4},{6,5},{7,6},{8,15},{9,8},{10,9... | collective-permute-start | bytes 405512 | tf_op jit(solution)/shard_map/ppermute | solution.py:514
  18.0 63.7 %collective-permute-start.9 = (f32[512,128]{1,0:T(8,128)}, f32[512,128]{1,0:T(8,128)S(1)}, u32[]{:S(2)}, u32[]{:S(2)}) collective-permute-start(f32[512,128]{1,0:T(8,128)} %get-tuple-element.51), channel_id=1, source_target_pairs={{0,7},{1,6},{2,5},{3,4},{4,3},{5,2},{6,1},{7,0},{8,15},{9,14},{10,... | collective-permute-start | bytes 786440 | tf_op jit(solution)/shard_map/ppermute | solution.py:510
  18.1 63.7 %collective-permute-start.8 = (f32[512,128]{1,0:T(8,128)}, f32[512,128]{1,0:T(8,128)S(1)}, u32[]{:S(2)}, u32[]{:S(2)}) collective-permute-start(f32[512,128]{1,0:T(8,128)} %get-tuple-element.44._), channel_id=1, source_target_pairs={{0,6},{1,7},{2,4},{3,5},{4,2},{5,3},{6,0},{7,1},{8,14},{9,15},{10,... | collective-permute-start | bytes 786440 | tf_op jit(solution)/shard_map/ppermute | solution.py:510
  20.2 14.9 %copy-start.3 = (f32[24,128]{1,0:T(8,128)S(1)}, f32[24,128]{1,0:T(8,128)}, u32[]{:S(2)}) copy-start(f32[24,128]{1,0:T(8,128)} %get-tuple-element.41.own._) | copy-start | bytes 36868
  20.3 8.0 %collective-permute-start.2 = (f32[608,128]{1,0:T(8,128)S(1)}, f32[608,128]{1,0:T(8,128)}, u32[]{:S(2)}, u32[]{:S(2)}) collective-permute-start(f32[608,128]{1,0:T(8,128)S(1)} %get-tuple-element.20), channel_id=1, source_target_pairs={{0,8},{8,16},{16,24},{24,0},{1,9},{9,17},{17,25},{25,1},{2,10},{10... | collective-permute-start | bytes 933896 | tf_op jit(solution)/shard_map/cond/branch_1_fun/ppermute | solution.py:514
  20.3 8.7 %collective-permute-start.3 = (f32[608,128]{1,0:T(8,128)S(1)}, f32[608,128]{1,0:T(8,128)}, u32[]{:S(2)}, u32[]{:S(2)}) collective-permute-start(f32[608,128]{1,0:T(8,128)S(1)} %get-tuple-element.21), channel_id=1, source_target_pairs={{0,24},{8,0},{16,8},{24,16},{1,25},{9,1},{17,9},{25,17},{2,26},{10... | collective-permute-start | bytes 933896 | tf_op jit(solution)/shard_map/cond/branch_1_fun/ppermute | solution.py:514
  47.6 34.1 %collective-permute-start.7 = (f32[512,128]{1,0:T(8,128)S(1)}, f32[512,128]{1,0:T(8,128)S(1)}, u32[]{:S(2)}, u32[]{:S(2)}) collective-permute-start(f32[512,128]{1,0:T(8,128)S(1)} %get-tuple-element.50), channel_id=1, source_target_pairs={{0,5},{1,4},{2,7},{3,6},{4,1},{5,0},{6,3},{7,2},{8,13},{9,12},{10,... | collective-permute-start | bytes 786440 | tf_op jit(solution)/shard_map/ppermute | solution.py:510
  84.8 44.8 %collective-permute-start.10 = (f32[2,256,128]{2,1,0:T(8,128)S(1)}, f32[2,256,128]{2,1,0:T(8,128)S(1)}, u32[]{:S(2)}, u32[]{:S(2)}) collective-permute-start(f32[2,256,128]{2,1,0:T(8,128)S(1)} %get-tuple-element.54), channel_id=1, source_target_pairs={{0,4},{1,5},{2,6},{3,7},{4,0},{5,1},{6,2},{7,3},{8,12},{9,13},{10,... | collective-permute-start | bytes 786440 | tf_op jit(solution)/shard_map/ppermute | solution.py:510
  84.9 44.7 %collective-permute-start.11 = (f32[2,256,128]{2,1,0:T(8,128)S(1)}, f32[2,256,128]{2,1,0:T(8,128)S(1)}, u32[]{:S(2)}, u32[]{:S(2)}) collective-permute-start(f32[2,256,128]{2,1,0:T(8,128)S(1)} %get-tuple-element.55), channel_id=1, source_target_pairs={{0,5},{1,4},{2,7},{3,6},{4,1},{5,0},{6,3},{7,2},{8,13},{9,12},{10,... | collective-permute-start | bytes 786440 | tf_op jit(solution)/shard_map/ppermute | solution.py:510
  88.0 41.6 %collective-permute-start.12 = (f32[2,256,128]{2,1,0:T(8,128)S(1)}, f32[2,256,128]{2,1,0:T(8,128)S(1)}, u32[]{:S(2)}, u32[]{:S(2)}) collective-permute-start(f32[2,256,128]{2,1,0:T(8,128)S(1)} %get-tuple-element.56), channel_id=1, source_target_pairs={{0,6},{1,7},{2,4},{3,5},{4,2},{5,3},{6,0},{7,1},{8,14},{9,15},{10,... | collective-permute-start | bytes 786440 | tf_op jit(solution)/shard_map/ppermute | solution.py:510
  88.9 44.8 %collective-permute-start.13 = (f32[2,256,128]{2,1,0:T(8,128)S(1)}, f32[2,256,128]{2,1,0:T(8,128)S(1)}, u32[]{:S(2)}, u32[]{:S(2)}) collective-permute-start(f32[2,256,128]{2,1,0:T(8,128)S(1)} %get-tuple-element.57), channel_id=1, source_target_pairs={{0,7},{1,6},{2,5},{3,4},{4,3},{5,2},{6,1},{7,0},{8,15},{9,14},{10,... | collective-permute-start | bytes 786440 | tf_op jit(solution)/shard_map/ppermute | solution.py:510

commit v10 on v8

--- a/solution.py
+++ b/solution.py
@@ -72,7 +72,8 @@
         start += size
 
 
-def pack_x_kernel(own, phase_lo, phase_hi, solute_lo, solute_hi, y_lo, y_hi, _, to_prev, to_next):
+def pack_x_kernel(own, phase_lo, phase_hi, solute_lo, solute_hi, y_lo, y_hi, *rest):
+    to_prev, to_next = rest[-2:]
     tiles, edge, depth = phase_lo.shape[1], phase_lo.shape[3], phase_lo.shape[4]
     width = tiles * edge + 2 * W
     for out, phase, solute, first in (
@@ -93,7 +94,7 @@
         out[at + 16 : at + 16 + 8 * tiles, :] = own[: 8 * tiles, :]
 
 
-def pack_x(phase, solute, own, y_lo, y_hi, after):
+def pack_x(phase, solute, own, y_lo, y_hi, *after):
     _, tiles, edge, _, depth = phase.shape
     low = pl.BlockSpec((1, tiles, W, edge, depth), lambda i: (0, 0, 0, 0, 0))
     high = pl.BlockSpec((1, tiles, W, edge, depth), lambda i: (0, 0, edge // W - 1, 0, 0))
@@ -104,12 +105,12 @@
     return pl.pallas_call(
         pack_x_kernel,
         grid=(1,),
-        in_specs=[pl.BlockSpec((8 * tiles + 8, depth), lambda i: (0, 0)), low, high, low, high, side, side, pl.BlockSpec(memory_space=pl.ANY)],
+        in_specs=[pl.BlockSpec((8 * tiles + 8, depth), lambda i: (0, 0)), low, high, low, high, side, side] + [pl.BlockSpec(memory_space=pl.ANY)] * len(after),
         out_specs=[whole, whole],
         out_shape=[out, out],
         compiler_params=pltpu.CompilerParams(vmem_limit_bytes=8 * 1024 * 1024),
         name="pack_x",
-    )(own, phase, phase, solute, solute, y_lo, y_hi, after)
+    )(own, phase, phase, solute, solute, y_lo, y_hi, *after)
 
 
 def update(near_p, near_u, under, mobile, spread):
@@ -497,10 +498,10 @@
     to_prev, to_next, own = pack_y(phase, solute, (undercool, mobility, diffusivity), owner)
     y_lo = lax.ppermute(to_next, "gy", ring("gy", 1))
     y_hi = lax.ppermute(to_prev, "gy", ring("gy", -1))
+    partner = swap(own[8 * tiles :], half)
     first = run_inner(plan, own, phase, solute)
     far = [swap(values, half + index) for index, values in enumerate(first)]
-    partner = swap(own[8 * tiles :], half)
-    to_prev, to_next = pack_x(phase, solute, own, y_lo, y_hi, first[0])
+    to_prev, to_next = pack_x(phase, solute, own, y_lo, y_hi, first[0], partner)
     x_lo = lax.ppermute(to_next, "gx", ring("gx", 1))
     x_hi = lax.ppermute(to_prev, "gx", ring("gx", -1))
     near, *second = run_outer(plan, own, phase, solute, (y_lo, y_hi, x_lo, x_hi), partner)

time: 117 us -> 118 us (level)
  starting transfers between devices: 19.5 us -> 18.3 us
    ppermute x1, waiting for transfers between devices: 0.47 us -> 3.07 us  [per_device(): x_lo = lax.ppermute(to_next, 'gx', ring('gx', 1))]
  transfers between devices with their start and end apart: 13 -> 13, of which waited for: 5 -> 4; matrix products, arithmetic and copies ran while one was open for 0% -> 1% of each run, Pallas kernels for 16% -> 16%
where the time goes in v10:
time: 118 us
  blocking collectives  64.3 us (54%)
  Pallas kernels  24.3 us (21%)
  starting transfers between devices  18.3 us (16%)
  waiting for transfers between devices  7.98 us (7%)
  local copies, waits for them, and re-layouts  2.02 us (2%)
    all_to_all x2, blocking collectives, exchange(): lax.all_to_all(values, 'gy', 0, 0, axis_index_groups=groups, tiled=True)  64.3 us
    ppermute x9, starting transfers between devices, swap(): lax.ppermute(values, 'gy', [(i, i ^ mask) for i in range(lax.axis_size('g...  13.6 us
    pallas_call x1, Pallas kernels, run_outer(): pl.pallas_call(functools.partial(outer_kernel, plan), in_specs=[vmem] * 8...  12.7 us
    pallas_call x1, Pallas kernels, run_inner(): pl.pallas_call(functools.partial(inner_kernel, plan), in_specs=[vmem] * 3...  4.72 us
    ppermute x9, waiting for transfers between devices, swap(): lax.ppermute(values, 'gy', [(i, i ^ mask) for i in range(lax.axis_size('g...  4.03 us
    ppermute x1, waiting for transfers between devices, per_device(): x_lo = lax.ppermute(to_next, 'gx', ring('gx', 1))  3.07 us
  transfers between devices with their start and end apart: 13, of which 4 were waited for; matrix products, arithmetic and copies ran while one was open for 1% of the time, Pallas kernels for 16%

profile of v10, /device:TPU:8, one launch (start us, length us, event | category | flops | bytes accessed | tf_op | source)
XLA Modules:
  0.0 117.8 jit_solution(4922038437939856573)
XLA Ops:
  0.6 0.0 copy-start.1
  0.6 0.0 copy-start
  0.7 2.0 %pack_y.1 = (f32[33,8,128]{2,1,0:T(8,128)}, f32[33,8,128]{2,1,0:T(8,128)}, f32[24,128]{1,0:T(8,128)}) custom-call(f32[1,2]{1,0:T(1,128)} %under.1, f32[1,2]{1,0:T(1,128)} %mobile.1, f32[1,2]{1,0:T(1,128)} %spread.1, s32[1,2]{1,0:T(1,128)} %owner.1, f32[1,2,32,32,128]{4,3,2,1,0:T(8,128)} %phase.3, f32[1,2,32,32,128]{4,3,2,1,0:T(8,128)} %phase.3, ...), custom_call_target="tpu_custom_call" | custom-call | tf_op jit(solution)/shard_map/pack_y/pallas_call | solution.py:47
  2.7 1.5 %collective-permute-start = (f32[33,8,128]{2,1,0:T(8,128)}, f32[33,8,128]{2,1,0:T(8,128)S(1)}, u32[]{:S(2)}, u32[]{:S(2)}) collective-permute-start(f32[33,8,128]{2,1,0:T(8,128)} %get-tuple-element.28), channel_id=1, source_target_pairs={{0,1},{1,2},{2,3},{3,4},{4,5},{5,6},{6,7},{7,0},{8,9},{9,10},{10,1... | collective-permute-start | bytes 405512 | tf_op jit(solution)/shard_map/ppermute | solution.py:499
  4.2 1.4 %collective-permute-start.1 = (f32[33,8,128]{2,1,0:T(8,128)}, f32[33,8,128]{2,1,0:T(8,128)S(1)}, u32[]{:S(2)}, u32[]{:S(2)}) collective-permute-start(f32[33,8,128]{2,1,0:T(8,128)} %get-tuple-element.29), channel_id=1, source_target_pairs={{0,7},{1,0},{2,1},{3,2},{4,3},{5,4},{6,5},{7,6},{8,15},{9,8},{10,9... | collective-permute-start | bytes 405512 | tf_op jit(solution)/shard_map/ppermute | solution.py:500
  5.6 0.7 slice.7
  6.3 2.6 %collective-permute-start.2 = (f32[8,128]{1,0:T(8,128)S(1)}, f32[8,128]{1,0:T(8,128)S(1)}, u32[]{:S(2)}, u32[]{:S(2)}) collective-permute-start(f32[8,128]{1,0:T(8,128)S(1)} %slice.7), channel_id=1, source_target_pairs={{0,4},{1,5},{2,6},{3,7},{4,0},{5,1},{6,2},{7,3},{8,12},{9,13},{10,... | collective-permute-start | bytes 12296 | tf_op jit(solution)/shard_map/ppermute | solution.py:483
  8.9 0.0 copy-done.1
  8.9 0.0 copy-done
  8.9 0.0 copy-start.2
  8.9 0.7 copy-done.2
  9.6 4.7 %inner.1 = (f32[512,128]{1,0:T(8,128)S(1)}, f32[512,128]{1,0:T(8,128)S(1)}) custom-call(f32[24,128]{1,0:T(8,128)S(1)} %copy-done.2, f32[1,2,32,32,128]{4,3,2,1,0:T(8,128)S(1)} %copy-done, f32[1,2,32,32,128]{4,3,2,1,0:T(8,128)S(1)} %copy-done.1), custom_call_target="tpu_custom_call" | custom-call | flops 100000000 | bytes 25165824 | tf_op jit(solution)/shard_map/inner/pallas_call | solution.py:260
  14.3 0.0 collective-permute-done.2.rest_1_.partner
  14.3 0.0 collective-permute-done.y_lo
  14.3 0.0 collective-permute-done.1.y_hi
  14.3 0.0 copy-start.3
  14.4 0.1 collective-permute-start.3
  14.5 1.7 %collective-permute-start.4 = (f32[608,128]{1,0:T(8,128)S(1)}, f32[608,128]{1,0:T(8,128)S(1)}, u32[]{:S(2)}, u32[]{:S(2)}) collective-permute-start(f32[608,128]{1,0:T(8,128)S(1)} %get-tuple-element.32), channel_id=1, source_target_pairs={{0,24},{8,0},{16,8},{24,16},{1,25},{9,1},{17,9},{25,17},{2,26},{10... | collective-permute-start | bytes 933896 | tf_op jit(solution)/shard_map/ppermute | solution.py:506
  16.2 0.3 collective-permute-start.5
  16.5 0.0 copy-start.7
  16.5 2.6 %collective-permute-start.6 = (f32[512,128]{1,0:T(8,128)S(1)}, f32[512,128]{1,0:T(8,128)S(1)}, u32[]{:S(2)}, u32[]{:S(2)}) collective-permute-start(f32[512,128]{1,0:T(8,128)S(1)} %get-tuple-element.34), channel_id=1, source_target_pairs={{0,5},{1,4},{2,7},{3,6},{4,1},{5,0},{6,3},{7,2},{8,13},{9,12},{10,... | collective-permute-start | bytes 786440 | tf_op jit(solution)/shard_map/ppermute | solution.py:483
  19.2 3.1 %collective-permute-done.3.x_lo = f32[608,128]{1,0:T(8,128)S(1)} collective-permute-done((f32[608,128]{1,0:T(8,128)S(1)}, f32[608,128]{1,0:T(8,128)S(1)}, u32[]{:S(2)}, u32[]{:S(2)}) %collective-permute-start.3) | collective-permute-done | bytes 311328 | tf_op jit(solution)/shard_map/ppermute | solution.py:505
  22.3 0.9 collective-permute-done.4.x_hi
  23.1 0.0 copy-done.3
  23.1 12.7 %outer.1 = (f32[4,528,128]{2,1,0:T(8,128)S(1)}, f32[512,128]{1,0:T(8,128)}, f32[512,128]{1,0:T(8,128)S(1)}) custom-call(f32[24,128]{1,0:T(8,128)S(1)} %copy-done.3, f32[1,2,32,32,128]{4,3,2,1,0:T(8,128)S(1)} %copy-done, f32[1,2,32,32,128]{4,3,2,1,0:T(8,128)S(1)} %copy-done.1, f32[33,8,128]{2,1,0:T(8,128)S(1)} %collective-permute-done.y_lo, ...), custom_call_target="tpu_custom_call" | custom-call | flops 100000000 | bytes 41943040 | tf_op jit(solution)/shard_map/outer/pallas_call | solution.py:344
  35.8 1.1 collective-permute-start.7
  36.9 1.0 collective-permute-start.8
  37.9 0.0 copy-done.7
  37.9 25.2 %conditional.2 = (f32[4,528,128]{2,1,0:T(8,128)S(1)}) conditional(s32[]{:T(128)} %bitcast, f32[4,528,128]{2,1,0:T(8,128)S(1)} %get-tuple-element.33, f32[4,528,128]{2,1,0:T(8,128)S(1)} %get-tuple-element.33), branch_computations={%region_0.0_spmd, %region_1.0_spmd} | conditional | bytes 2162696 | solution.py:491
  38.0 25.2 %all_to_all.17 = f32[4,528,128]{2,1,0:T(8,128)S(1)} all-to-all(f32[4,528,128]{2,1,0:T(8,128)S(1)} %param.1), channel_id=1, replica_groups={{0,1,2,3},{4,5,6,7},{8,9,10,11},{12,13,14,15},{16,17,18,19},{20,21,22,2..., dimensions={0} | all-to-all | bytes 2162688 | tf_op jit(solution)/shard_map/cond/branch_1_fun/all_to_all | solution.py:489
  63.2 0.0 copy-start.6
  63.2 1.3 %table.1 = s32[16]{0:T(128)} custom-call(f32[4,528,128]{2,1,0:T(8,128)S(1)} %get-tuple-element.42.near), custom_call_target="tpu_custom_call" | custom-call | tf_op jit(solution)/shard_map/table/pallas_call | solution.py:383
  64.5 0.0 collective-permute-done.6.refs_1_
  64.5 0.0 collective-permute-done.5.refs_0_
  64.5 0.0 collective-permute-done.7.refs_2_
  64.5 0.0 copy-done.6
  64.5 0.5 collective-permute-done.8.refs_3_
  65.1 0.0 copy-start.4
  65.1 0.6 copy-done.4
  65.7 1.5 %route.1 = (f32[4,2,256,128]{3,2,1,0:T(8,128)S(1)}, f32[2,256,128]{2,1,0:T(8,128)S(1)}, f32[2,256,128]{2,1,0:T(8,128)S(1)}, f32[2,256,128]{2,1,0:T(8,128)S(1)}, f32[2,256,128]{2,1,0:T(8,128)S(1)}) custom-call(s32[16]{0:T(128)S(1)} %copy-done.4, f32[4,528,128]{2,1,0:T(8,128)} %copy-done.6, f32[512,128]{1,0:T(8,128)S(1)} %collective-permute-done.5.refs_0_, ...), custom_call_target="tpu_custom_call" | custom-call | tf_op jit(solution)/shard_map/route/pallas_call | solution.py:418
  67.2 1.7 %collective-permute-start.9 = (f32[2,256,128]{2,1,0:T(8,128)S(1)}, f32[2,256,128]{2,1,0:T(8,128)S(1)}, u32[]{:S(2)}, u32[]{:S(2)}) collective-permute-start(f32[2,256,128]{2,1,0:T(8,128)S(1)} %get-tuple-element.38), channel_id=1, source_target_pairs={{0,4},{1,5},{2,6},{3,7},{4,0},{5,1},{6,2},{7,3},{8,12},{9,13},{10,... | collective-permute-start | bytes 786440 | tf_op jit(solution)/shard_map/ppermute | solution.py:483
  68.9 2.3 %collective-permute-start.10 = (f32[2,256,128]{2,1,0:T(8,128)S(1)}, f32[2,256,128]{2,1,0:T(8,128)S(1)}, u32[]{:S(2)}, u32[]{:S(2)}) collective-permute-start(f32[2,256,128]{2,1,0:T(8,128)S(1)} %get-tuple-element.39), channel_id=1, source_target_pairs={{0,5},{1,4},{2,7},{3,6},{4,1},{5,0},{6,3},{7,2},{8,13},{9,12},{10,... | collective-permute-start | bytes 786440 | tf_op jit(solution)/shard_map/ppermute | solution.py:483
  71.2 1.2 %collective-permute-start.11 = (f32[2,256,128]{2,1,0:T(8,128)S(1)}, f32[2,256,128]{2,1,0:T(8,128)S(1)}, u32[]{:S(2)}, u32[]{:S(2)}) collective-permute-start(f32[2,256,128]{2,1,0:T(8,128)S(1)} %get-tuple-element.40), channel_id=1, source_target_pairs={{0,6},{1,7},{2,4},{3,5},{4,2},{5,3},{6,0},{7,1},{8,14},{9,15},{10,... | collective-permute-start | bytes 786440 | tf_op jit(solution)/shard_map/ppermute | solution.py:483
  72.4 0.7 collective-permute-start.12
  73.1 0.0 copy-start.5
  73.1 39.1 %conditional.3 = (f32[4,2,256,128]{3,2,1,0:T(8,128)S(1)}) conditional(s32[]{:T(128)} %bitcast, f32[4,2,256,128]{3,2,1,0:T(8,128)S(1)} %get-tuple-element.37, f32[4,2,256,128]{3,2,1,0:T(8,128)S(1)} %get-tuple-element.37), branch_computations={%region_2.0_spmd, %region_3.0_spmd} | conditional | bytes 2097160 | solution.py:491
  73.1 39.1 %all_to_all.19 = f32[4,2,256,128]{3,2,1,0:T(8,128)S(1)} all-to-all(f32[4,2,256,128]{3,2,1,0:T(8,128)S(1)} %param.3), channel_id=1, replica_groups={{0,1,2,3},{4,5,6,7},{8,9,10,11},{12,13,14,15},{16,17,18,19},{20,21,22,2..., dimensions={0} | all-to-all | bytes 2097152 | tf_op jit(solution)/shard_map/cond/branch_1_fun/all_to_all | solution.py:489
  112.3 0.0 collective-permute-done.9.refs_0_
  112.3 0.0 collective-permute-done.10.refs_1_
  112.3 0.0 collective-permute-done.11.refs_2_
  112.3 3.5 %collective-permute-done.12.refs_3_ = f32[2,256,128]{2,1,0:T(8,128)S(1)} collective-permute-done((f32[2,256,128]{2,1,0:T(8,128)S(1)}, f32[2,256,128]{2,1,0:T(8,128)S(1)}, u32[]{:S(2)}, u32[]{:S(2)}) %collective-permute-start.12) | collective-permute-done | bytes 262176 | tf_op jit(solution)/shard_map/ppermute | solution.py:483
  115.7 0.0 copy-done.5
  115.7 2.1 %settle.1 = (f32[1,2,32,32,128]{4,3,2,1,0:T(8,128)}, f32[1,2,32,32,128]{4,3,2,1,0:T(8,128)}) custom-call(s32[16]{0:T(128)S(1)} %copy-done.5, f32[4,2,256,128]{3,2,1,0:T(8,128)S(1)} %get-tuple-element.43.near, f32[2,256,128]{2,1,0:T(8,128)S(1)} %collective-permute-done.9.refs_0_, f32[2,256,128]{2,1,0:T(8,128)S(1)} %collective-permute-done.10.refs_1_, ...), custom_call_target="tpu_custom_call" | custom-call | tf_op jit(solution)/shard_map/settle/pallas_call | solution.py:467
  (1 shorter events, 0.0 us)
Async XLA Ops:
  0.6 8.2 %copy-start.1 = (f32[1,2,32,32,128]{4,3,2,1,0:T(8,128)S(1)}, f32[1,2,32,32,128]{4,3,2,1,0:T(8,128)}, u32[]{:S(2)}) copy-start(f32[1,2,32,32,128]{4,3,2,1,0:T(8,128)} %solute.3) | copy-start | bytes 3145732
  0.6 8.2 %copy-start = (f32[1,2,32,32,128]{4,3,2,1,0:T(8,128)S(1)}, f32[1,2,32,32,128]{4,3,2,1,0:T(8,128)}, u32[]{:S(2)}) copy-start(f32[1,2,32,32,128]{4,3,2,1,0:T(8,128)} %phase.3) | copy-start | bytes 3145732
  2.7 11.7 %collective-permute-start = (f32[33,8,128]{2,1,0:T(8,128)}, f32[33,8,128]{2,1,0:T(8,128)S(1)}, u32[]{:S(2)}, u32[]{:S(2)}) collective-permute-start(f32[33,8,128]{2,1,0:T(8,128)} %get-tuple-element.28), channel_id=1, source_target_pairs={{0,1},{1,2},{2,3},{3,4},{4,5},{5,6},{6,7},{7,0},{8,9},{9,10},{10,1... | collective-permute-start | bytes 405512 | tf_op jit(solution)/shard_map/ppermute | solution.py:499
  4.2 10.1 %collective-permute-start.1 = (f32[33,8,128]{2,1,0:T(8,128)}, f32[33,8,128]{2,1,0:T(8,128)S(1)}, u32[]{:S(2)}, u32[]{:S(2)}) collective-permute-start(f32[33,8,128]{2,1,0:T(8,128)} %get-tuple-element.29), channel_id=1, source_target_pairs={{0,7},{1,0},{2,1},{3,2},{4,3},{5,4},{6,5},{7,6},{8,15},{9,8},{10,9... | collective-permute-start | bytes 405512 | tf_op jit(solution)/shard_map/ppermute | solution.py:500
  6.3 8.0 %collective-permute-start.2 = (f32[8,128]{1,0:T(8,128)S(1)}, f32[8,128]{1,0:T(8,128)S(1)}, u32[]{:S(2)}, u32[]{:S(2)}) collective-permute-start(f32[8,128]{1,0:T(8,128)S(1)} %slice.7), channel_id=1, source_target_pairs={{0,4},{1,5},{2,6},{3,7},{4,0},{5,1},{6,2},{7,3},{8,12},{9,13},{10,... | collective-permute-start | bytes 12296 | tf_op jit(solution)/shard_map/ppermute | solution.py:483
  8.9 0.7 copy-start.2
  14.3 8.8 %copy-start.3 = (f32[24,128]{1,0:T(8,128)S(1)}, f32[24,128]{1,0:T(8,128)}, u32[]{:S(2)}) copy-start(f32[24,128]{1,0:T(8,128)} %get-tuple-element.27.own) | copy-start | bytes 36868
  14.4 7.9 %collective-permute-start.3 = (f32[608,128]{1,0:T(8,128)S(1)}, f32[608,128]{1,0:T(8,128)S(1)}, u32[]{:S(2)}, u32[]{:S(2)}) collective-permute-start(f32[608,128]{1,0:T(8,128)S(1)} %get-tuple-element.31), channel_id=1, source_target_pairs={{0,8},{8,16},{16,24},{24,0},{1,9},{9,17},{17,25},{25,1},{2,10},{10... | collective-permute-start | bytes 933896 | tf_op jit(solution)/shard_map/ppermute | solution.py:505
  14.5 8.7 %collective-permute-start.4 = (f32[608,128]{1,0:T(8,128)S(1)}, f32[608,128]{1,0:T(8,128)S(1)}, u32[]{:S(2)}, u32[]{:S(2)}) collective-permute-start(f32[608,128]{1,0:T(8,128)S(1)} %get-tuple-element.32), channel_id=1, source_target_pairs={{0,24},{8,0},{16,8},{24,16},{1,25},{9,1},{17,9},{25,17},{2,26},{10... | collective-permute-start | bytes 933896 | tf_op jit(solution)/shard_map/ppermute | solution.py:506
  16.2 48.3 %collective-permute-start.5 = (f32[512,128]{1,0:T(8,128)S(1)}, f32[512,128]{1,0:T(8,128)S(1)}, u32[]{:S(2)}, u32[]{:S(2)}) collective-permute-start(f32[512,128]{1,0:T(8,128)S(1)} %get-tuple-element.30.rest_0_), channel_id=1, source_target_pairs={{0,4},{1,5},{2,6},{3,7},{4,0},{5,1},{6,2},{7,3},{8,12},{9,13},{10,... | collective-permute-start | bytes 786440 | tf_op jit(solution)/shard_map/ppermute | solution.py:483
  16.5 21.4 %copy-start.7 = (s32[1,2]{1,0:T(1,128)S(1)}, s32[1,2]{1,0:T(1,128)}, u32[]{:S(2)}) copy-start(s32[1,2]{1,0:T(1,128)} %owner.1) | copy-start | bytes 28
  16.5 47.9 %collective-permute-start.6 = (f32[512,128]{1,0:T(8,128)S(1)}, f32[512,128]{1,0:T(8,128)S(1)}, u32[]{:S(2)}, u32[]{:S(2)}) collective-permute-start(f32[512,128]{1,0:T(8,128)S(1)} %get-tuple-element.34), channel_id=1, source_target_pairs={{0,5},{1,4},{2,7},{3,6},{4,1},{5,0},{6,3},{7,2},{8,13},{9,12},{10,... | collective-permute-start | bytes 786440 | tf_op jit(solution)/shard_map/ppermute | solution.py:483
  35.8 28.7 %collective-permute-start.7 = (f32[512,128]{1,0:T(8,128)}, f32[512,128]{1,0:T(8,128)S(1)}, u32[]{:S(2)}, u32[]{:S(2)}) collective-permute-start(f32[512,128]{1,0:T(8,128)} %get-tuple-element.35), channel_id=1, source_target_pairs={{0,6},{1,7},{2,4},{3,5},{4,2},{5,3},{6,0},{7,1},{8,14},{9,15},{10,... | collective-permute-start | bytes 786440 | tf_op jit(solution)/shard_map/ppermute | solution.py:483
  36.9 28.1 %collective-permute-start.8 = (f32[512,128]{1,0:T(8,128)S(1)}, f32[512,128]{1,0:T(8,128)S(1)}, u32[]{:S(2)}, u32[]{:S(2)}) collective-permute-start(f32[512,128]{1,0:T(8,128)S(1)} %get-tuple-element.36), channel_id=1, source_target_pairs={{0,7},{1,6},{2,5},{3,4},{4,3},{5,2},{6,1},{7,0},{8,15},{9,14},{10,... | collective-permute-start | bytes 786440 | tf_op jit(solution)/shard_map/ppermute | solution.py:483
  63.2 1.3 %copy-start.6 = (f32[4,528,128]{2,1,0:T(8,128)}, f32[4,528,128]{2,1,0:T(8,128)S(1)}, u32[]{:S(2)}) copy-start(f32[4,528,128]{2,1,0:T(8,128)S(1)} %get-tuple-element.42.near) | copy-start | bytes 3244036
  65.1 0.6 copy-start.4
  67.2 45.1 %collective-permute-start.9 = (f32[2,256,128]{2,1,0:T(8,128)S(1)}, f32[2,256,128]{2,1,0:T(8,128)S(1)}, u32[]{:S(2)}, u32[]{:S(2)}) collective-permute-start(f32[2,256,128]{2,1,0:T(8,128)S(1)} %get-tuple-element.38), channel_id=1, source_target_pairs={{0,4},{1,5},{2,6},{3,7},{4,0},{5,1},{6,2},{7,3},{8,12},{9,13},{10,... | collective-permute-start | bytes 786440 | tf_op jit(solution)/shard_map/ppermute | solution.py:483
  68.9 43.4 %collective-permute-start.10 = (f32[2,256,128]{2,1,0:T(8,128)S(1)}, f32[2,256,128]{2,1,0:T(8,128)S(1)}, u32[]{:S(2)}, u32[]{:S(2)}) collective-permute-start(f32[2,256,128]{2,1,0:T(8,128)S(1)} %get-tuple-element.39), channel_id=1, source_target_pairs={{0,5},{1,4},{2,7},{3,6},{4,1},{5,0},{6,3},{7,2},{8,13},{9,12},{10,... | collective-permute-start | bytes 786440 | tf_op jit(solution)/shard_map/ppermute | solution.py:483
  71.2 41.1 %collective-permute-start.11 = (f32[2,256,128]{2,1,0:T(8,128)S(1)}, f32[2,256,128]{2,1,0:T(8,128)S(1)}, u32[]{:S(2)}, u32[]{:S(2)}) collective-permute-start(f32[2,256,128]{2,1,0:T(8,128)S(1)} %get-tuple-element.40), channel_id=1, source_target_pairs={{0,6},{1,7},{2,4},{3,5},{4,2},{5,3},{6,0},{7,1},{8,14},{9,15},{10,... | collective-permute-start | bytes 786440 | tf_op jit(solution)/shard_map/ppermute | solution.py:483
  72.4 43.3 %collective-permute-start.12 = (f32[2,256,128]{2,1,0:T(8,128)S(1)}, f32[2,256,128]{2,1,0:T(8,128)S(1)}, u32[]{:S(2)}, u32[]{:S(2)}) collective-permute-start(f32[2,256,128]{2,1,0:T(8,128)S(1)} %get-tuple-element.41), channel_id=1, source_target_pairs={{0,7},{1,6},{2,5},{3,4},{4,3},{5,2},{6,1},{7,0},{8,15},{9,14},{10,... | collective-permute-start | bytes 786440 | tf_op jit(solution)/shard_map/ppermute | solution.py:483
  73.1 42.6 %copy-start.5 = (s32[16]{0:T(128)S(1)}, s32[16]{0:T(128)}, u32[]{:S(2)}) copy-start(s32[16]{0:T(128)} %table.1) | copy-start | bytes 196

commit v11 on v8

--- a/solution.py
+++ b/solution.py
@@ -26,8 +26,9 @@
     names = jnp.zeros((8, depth), jnp.float32)
     for tile in range(tiles):
         rows = jnp.zeros((8, depth), jnp.float32)
-        for kind, coef in enumerate((under, mobile, spread)):
-            rows = jnp.where(line == kind, coef[0, tile], rows)
+        ready = (2.0 * under[0, tile], mobile[0, tile], spread[0, tile], 1.0 - 6.0 * spread[0, tile])
+        for kind, coef in enumerate(ready):
+            rows = jnp.where(line == kind, coef, rows)
         own[8 * tile : 8 * tile + 8, :] = rows
         if tile == 0:
             to_prev[edge] = rows
@@ -57,18 +58,18 @@
 def fill_row(dst, row, phase_row, solute_row, lo, hi):
     start = PAD
     dst[0][row, start : start + W, :] = lo[:W]
-    dst[1][row, start : start + W, :] = lo[W:]
+    dst[1][row, start : start + W, :] = 2.0 * lo[W:]
     start += W
     for values in phase_row:
         size = values.shape[0]
         dst[0][row, start : start + size, :] = values
         start += size
     dst[0][row, start : start + W, :] = hi[:W]
-    dst[1][row, start : start + W, :] = hi[W:]
+    dst[1][row, start : start + W, :] = 2.0 * hi[W:]
     start = PAD + W
     for values in solute_row:
         size = values.shape[0]
-        dst[1][row, start : start + size, :] = values
+        dst[1][row, start : start + size, :] = 2.0 * values
         start += size
 
 
@@ -112,30 +113,33 @@
     )(own, phase, phase, solute, solute, y_lo, y_hi, after)
 
 
-def update(near_p, near_u, under, mobile, spread):
+def update(near_p, near_v, under, mobile, spread, keep):
     p, p_xl, p_xh, p_yl, p_yh = near_p
-    u, u_xl, u_xh, u_yl, u_yh = near_u
+    v, v_xl, v_xh, v_yl, v_yh = near_v
     depth = p.shape[-1]
     lane = lax.broadcasted_iota(jnp.int32, p.shape, 1)
     first, last = lane == 0, lane == depth - 1
     p_zl = jnp.where(first, p, pltpu.roll(p, 1, 1))
     p_zh = jnp.where(last, p, pltpu.roll(p, depth - 1, 1))
-    u_zl = jnp.where(first, u, pltpu.roll(u, 1, 1))
-    u_zh = jnp.where(last, u, pltpu.roll(u, depth - 1, 1))
+    v_zl = jnp.where(first, v, pltpu.roll(v, 1, 1))
+    v_zh = jnp.where(last, v, pltpu.roll(v, depth - 1, 1))
     dx, dy, dz = p_xh - p_xl, p_yh - p_yl, p_zh - p_zl
     qx, qy, qz = dx * dx, dy * dy, dz * dz
-    total = qx + qy + qz
-    fourth = qx * qx + qy * qy + qz * qz
+    flat = qx + qy
+    total = flat + qz
+    pairs = qx * qy + flat * qz
     base = total + 4.0
     guess = pl.reciprocal(base, approx=True)
     inverse = guess * (2.0 - base * guess)
-    extra = (4.0 * aniso_strength * fourth - (3.0 * aniso_strength) * total * total) * (inverse * inverse)
+    extra = (aniso_strength * total * total - (8.0 * aniso_strength) * pairs) * (inverse * inverse)
     lap_p = (p_xl + p_xh) + (p_yl + p_yh) + (p_zl + p_zh) - 6.0 * p
-    lap_u = (u_xl + u_xh) + (u_yl + u_yh) + (u_zl + u_zh) - 6.0 * u
+    sum_v = (v_xl + v_xh) + (v_yl + v_yh) + (v_zl + v_zh)
     well = 1.0 - p * p
-    drive = well * (under + u)
-    change = mobile * (lap_p + extra * lap_p + well * (p - 2.0 * drive))
-    return p + change, u + spread * lap_u + 0.5 * change
+    change = mobile * (lap_p + extra * lap_p + well * (p - well * (under + v)))
+    return p + change, keep * v + spread * sum_v + change
+
+
+KINDS = 4
 
 
 def cells(src_p, src_u, row, start, coefs):
@@ -225,37 +229,40 @@
         for tile in range(tiles):
             start = PAD + tile * edge
             pairs[0][0][row, start : start + edge, :] = phase[0, tile, base + row]
-            pairs[0][1][row, start : start + edge, :] = solute[0, tile, base + row]
+            pairs[0][1][row, start : start + edge, :] = 2.0 * solute[0, tile, base + row]
         return carry
 
     lax.fori_loop(0, count + 2 * W, load_row, 0, unroll=UNROLL)
 
     def coefs_of(row, start):
         tile = (start - PAD) // edge
-        return tuple(own[8 * tile + kind : 8 * tile + kind + 1, :] for kind in range(3))
+        return tuple(own[8 * tile + kind : 8 * tile + kind + 1, :] for kind in range(KINDS))
 
     for step in range(NSTEPS):
         starts = range(PAD, PAD + tiles * edge, 8)
         march(step + 1, count + 2 * W - step - 1, starts, pairs[step % 2], pairs[(step + 1) % 2], coefs_of)
     for index, out in enumerate(outs):
-        pack(plan, True, mine ^ index, pairs[NSTEPS % 2], -base, PAD, out)
-
-
-def pack(plan, far, piece, done, row_shift, col_shift, out):
+        pack(plan, True, mine ^ index, pairs[NSTEPS % 2], -base, PAD, own, out)
+
+
+def pack(plan, far, piece, done, row_shift, col_shift, own, out):
     for tile in range(plan.tiles):
         for field, values in enumerate(done):
             begin = (2 * tile + field) * plan.size
             for at, row, name in plan.parts(far, piece):
                 col, count = plan.columns(name, tile)
                 start = col_shift + tile * plan.edge + col
-                out[begin + at : begin + at + count, :] = values[row + row_shift, start : start + count, :]
+                cells = values[row + row_shift, start : start + count, :]
+                out[begin + at : begin + at + count, :] = 0.5 * cells if field else cells
+    tail = 2 * plan.tiles * plan.size
+    out[tail : tail + AUX, :] = own[8 * plan.tiles : 8 * plan.tiles + AUX, :]
 
 
 def run_inner(plan, own, phase, solute):
     rows = plan.inner // 2 + 2 * W
     buffer = pltpu.VMEM((rows, plan.tiles * plan.edge + 2 * PAD, plan.depth), jnp.float32)
     vmem = pl.BlockSpec(memory_space=pltpu.VMEM)
-    shape = jax.ShapeDtypeStruct((2 * plan.tiles * plan.size, plan.depth), jnp.float32)
+    shape = jax.ShapeDtypeStruct((2 * plan.tiles * plan.size + AUX, plan.depth), jnp.float32)
     return pl.pallas_call(
         functools.partial(inner_kernel, plan),
         in_specs=[vmem] * 3,
@@ -268,14 +275,14 @@
     )(own, phase, solute)
 
 
-def outer_kernel(plan, own, phase, solute, y_lo, y_hi, x_lo, x_hi, partner, out, *rest):
+def outer_kernel(plan, own, phase, solute, y_lo, y_hi, x_lo, x_hi, out, *rest):
     tiles, edge, depth, half = plan.tiles, plan.edge, plan.depth, plan.half
     far_outs, scratch = rest[: half // 2], rest[half // 2 :]
     pairs, coefs = (scratch[:2], scratch[2:4]), scratch[4]
     cols = tiles * edge
     width = cols + 2 * W
     for zone, source in ((0, x_lo), (1, None), (2, x_hi)):
-        for kind in range(3):
+        for kind in range(KINDS):
             if source is None:
                 parts = [y_lo[edge, kind : kind + 1, :]]
                 parts += [own[8 * tile + kind : 8 * tile + kind + 1, :] for tile in range(tiles)]
@@ -294,7 +301,8 @@
         for row in range(W):
             for field in range(2):
                 at = (2 * row + field) * width
-                pairs[0][field][first + row, PAD : PAD + width, :] = source[at : at + width, :]
+                values = source[at : at + width, :]
+                pairs[0][field][first + row, PAD : PAD + width, :] = 2.0 * values if field else values
 
     def load_row(row, carry):
         fill_row(
@@ -311,7 +319,7 @@
 
     def coefs_of(zone):
         def found(row, start):
-            return tuple(coefs[zone(row), kind, start - PAD : start - PAD + 8, :] for kind in range(3))
+            return tuple(coefs[zone(row), kind, start - PAD : start - PAD + 8, :] for kind in range(KINDS))
 
         return found
 
@@ -325,105 +333,84 @@
     done = pairs[NSTEPS % 2]
     mine = lax.rem(lax.axis_index("gy"), half)
     for index, far_out in enumerate(far_outs):
-        pack(plan, True, mine ^ (half // 2 + index), done, W, PAD + W, far_out)
-    tail = 2 * tiles * plan.size
+        pack(plan, True, mine ^ (half // 2 + index), done, W, PAD + W, own, far_out)
     for piece in range(half):
-        pack(plan, False, piece, done, W, PAD + W, out.at[piece])
-        out[piece, tail : tail + AUX, :] = own[8 * tiles : 8 * tiles + AUX, :]
-        out[piece, tail + AUX : tail + 2 * AUX, :] = partner[...]
-
-
-def run_outer(plan, own, phase, solute, halos, partner):
+        pack(plan, False, piece, done, W, PAD + W, own, out.at[piece])
+
+
+def run_outer(plan, own, phase, solute, halos):
     tiles, edge, depth = plan.tiles, plan.edge, plan.depth
     width = tiles * edge + 2 * W
     buffer = pltpu.VMEM((edge + 2 * W, width + 2 * PAD, depth), jnp.float32)
     vmem = pl.BlockSpec(memory_space=pltpu.VMEM)
-    near = jax.ShapeDtypeStruct((plan.half, 2 * tiles * plan.size + 2 * AUX, depth), jnp.float32)
-    far = jax.ShapeDtypeStruct((2 * tiles * plan.size, depth), jnp.float32)
+    near = jax.ShapeDtypeStruct((plan.half, 2 * tiles * plan.size + AUX, depth), jnp.float32)
+    far = jax.ShapeDtypeStruct((2 * tiles * plan.size + AUX, depth), jnp.float32)
     return pl.pallas_call(
         functools.partial(outer_kernel, plan),
-        in_specs=[vmem] * 8,
+        in_specs=[vmem] * 7,
         out_specs=[vmem] * (1 + plan.half // 2),
         out_shape=[near] + [far] * (plan.half // 2),
-        scratch_shapes=[buffer] * 4 + [pltpu.VMEM((3, 3, width, depth), jnp.float32)],
+        scratch_shapes=[buffer] * 4 + [pltpu.VMEM((3, KINDS, width, depth), jnp.float32)],
         compiler_params=pltpu.CompilerParams(vmem_limit_bytes=16 * 1024 * 1024),
         cost_estimate=pl.CostEstimate(flops=10**8, bytes_accessed=40 * 1024 * 1024, transcendentals=0),
         name="outer",
-    )(own, phase, solute, *halos, partner)
-
-
-def table_kernel(plan, near, table, names, count, sems):
-    pieces, tiles, half = plan.pieces, plan.tiles, plan.half
+    )(own, phase, solute, *halos)
+
+
+def route_kernel(plan, near, *refs):
+    pieces, tiles, half, size = plan.pieces, plan.tiles, plan.half, 2 * plan.size
+    far, near_out, far_outs, table = refs[:half], refs[half], refs[half + 1 : 2 * half + 1], refs[2 * half + 1]
+    held, peers, count = refs[2 * half + 2 :]
     me = lax.axis_index("gy")
     base = me - lax.rem(me, half)
-    tail = 2 * tiles * plan.size
-    copies = []
-    for piece in range(half):
-        for index in range(2):
-            copy = pltpu.make_async_copy(
-                near.at[piece, pl.ds(tail + index * AUX, 1), :], names.at[index, piece], sems.at[index, piece]
-            )
-            copy.start()
-            copies.append(copy)
-    for peer in range(pieces):
-        count[peer] = 0
-    for copy in copies:
-        copy.wait()
-    for home in range(pieces):
-        other = (home // half != base // half).astype(jnp.int32)
-        for tile in range(tiles):
-            peer = lax.rem(names[other, home % half, 0, tile].astype(jnp.int32), pieces)
-            slot = count[peer]
-            table[peer * tiles + slot] = home * tiles + tile
-            count[peer] = slot + 1
-
-
-def find_table(plan, near):
-    return pl.pallas_call(
-        functools.partial(table_kernel, plan),
-        in_specs=[pl.BlockSpec(memory_space=pl.ANY)],
-        out_specs=pl.BlockSpec(memory_space=pltpu.SMEM),
-        out_shape=jax.ShapeDtypeStruct((plan.pieces * plan.tiles,), jnp.int32),
-        scratch_shapes=[
-            pltpu.SMEM((2, plan.half, 1, plan.depth), jnp.float32),
-            pltpu.SMEM((plan.pieces,), jnp.int32),
-            pltpu.SemaphoreType.DMA((2, plan.half)),
-        ],
-        name="table",
-    )(near)
-
-
-def route_kernel(plan, table, near, *refs):
-    tiles, half, size = plan.tiles, plan.half, 2 * plan.size
-    far, near_out, far_outs, held = refs[:half], refs[half], refs[half + 1 : 2 * half + 1], refs[-1]
-    me = lax.axis_index("gy")
-    base = me - lax.rem(me, half)
+    tail = tiles * size
+    for tile in range(tiles):
+        for piece in range(half):
+            peer = lax.rem(near[piece, tail, tile].astype(jnp.int32), pieces)
+            peers[(base + piece) * tiles + tile] = peer
+        for index in range(half):
+            peer = lax.rem(far[index][tail, tile].astype(jnp.int32), pieces)
+            peers[(me ^ (half + index)) * tiles + tile] = peer
     for piece in range(half):
         for tile in range(tiles):
             held[(base + piece) * tiles + tile] = near[piece, tile * size : (tile + 1) * size, :]
     for index in range(half):
         for tile in range(tiles):
             held[(me ^ (half + index)) * tiles + tile] = far[index][tile * size : (tile + 1) * size, :]
+    for peer in range(pieces):
+        count[peer] = 0
+    for home in range(pieces * tiles):
+        peer = peers[home]
+        slot = count[peer]
+        table[peer * tiles + slot] = home
+        count[peer] = slot + 1
     for index in range(half):
         for slot in range(tiles):
             far_outs[index][slot] = held[table[(me ^ (half + index)) * tiles + slot]]
             near_out[index, slot] = held[table[(base + index) * tiles + slot]]
 
 
-def route(plan, table, near, far):
+def route(plan, near, far):
     tiles, half, size, depth = plan.tiles, plan.half, 2 * plan.size, plan.depth
     vmem = pl.BlockSpec(memory_space=pltpu.VMEM)
     one = jax.ShapeDtypeStruct((tiles, size, depth), jnp.float32)
+    count = plan.pieces * tiles
     results = pl.pallas_call(
         functools.partial(route_kernel, plan),
-        in_specs=[pl.BlockSpec(memory_space=pltpu.SMEM)] + [vmem] * (half + 1),
-        out_specs=[vmem] * (half + 1),
-        out_shape=[jax.ShapeDtypeStruct((half, tiles, size, depth), jnp.float32)] + [one] * half,
-        scratch_shapes=[pltpu.VMEM((plan.pieces * tiles, size, depth), jnp.float32)],
+        in_specs=[vmem] * (half + 1),
+        out_specs=[vmem] * (half + 1) + [pl.BlockSpec(memory_space=pltpu.SMEM)],
+        out_shape=[jax.ShapeDtypeStruct((half, tiles, size, depth), jnp.float32)]
+        + [one] * half
+        + [jax.ShapeDtypeStruct((count,), jnp.int32)],
+        scratch_shapes=[
+            pltpu.VMEM((count, size, depth), jnp.float32),
+            pltpu.SMEM((count,), jnp.int32),
+            pltpu.SMEM((plan.pieces,), jnp.int32),
+        ],
         compiler_params=pltpu.CompilerParams(vmem_limit_bytes=16 * 1024 * 1024),
         name="route",
-    )(table, near, *far)
-    return results[0], results[1:]
+    )(near, *far)
+    return results[0], results[1 : half + 1], results[-1]
 
 
 def settle_kernel(plan, table, near, *refs):
@@ -499,16 +486,14 @@
     y_hi = lax.ppermute(to_prev, "gy", ring("gy", -1))
     first = run_inner(plan, own, phase, solute)
     far = [swap(values, half + index) for index, values in enumerate(first)]
-    partner = swap(own[8 * tiles :], half)
     to_prev, to_next = pack_x(phase, solute, own, y_lo, y_hi, first[0])
     x_lo = lax.ppermute(to_next, "gx", ring("gx", 1))
     x_hi = lax.ppermute(to_prev, "gx", ring("gx", -1))
-    near, *second = run_outer(plan, own, phase, solute, (y_lo, y_hi, x_lo, x_hi), partner)
+    near, *second = run_outer(plan, own, phase, solute, (y_lo, y_hi, x_lo, x_hi))
     far += [swap(values, half + half // 2 + index) for index, values in enumerate(second)]
     together = owner[0, 0] >= 0
     near = among_half(plan, near, together)
-    table = find_table(plan, near)
-    near, far = route(plan, table, near, far)
+    near, far, table = route(plan, near, far)
     far = [swap(values, half + index) for index, values in enumerate(far)]
     near = among_half(plan, near, together)
     return tuple(settle(plan, table, near, far))

time: 117 us -> 117 us (level)
  waiting for transfers between devices: 7.03 us -> 12.1 us
  starting transfers between devices: 19.5 us -> 15.7 us
  Pallas kernels: 24.3 us -> 23 us
  blocking collectives: 63.2 us -> 64.4 us
    ppermute x9 -> x8, starting transfers between devices: 14.7 us -> 11 us  [swap(): lax.ppermute(values, 'gy', [(i, i ^ mask) for i in range(lax.axis_size('g...]
    ppermute x1, waiting for transfers between devices: 0.47 us -> 3.07 us  [per_device(): x_lo = lax.ppermute(to_next, 'gx', ring('gx', 1))]
    ppermute x9 -> x8, waiting for transfers between devices: 4.74 us -> 6.94 us  [swap(): lax.ppermute(values, 'gy', [(i, i ^ mask) for i in range(lax.axis_size('g...]
    all_to_all x2, blocking collectives: 63.2 us -> 64.4 us  [exchange(): lax.all_to_all(values, 'gy', 0, 0, axis_index_groups=groups, tiled=True)]
    pallas_call x3 -> x2, Pallas kernels: 15.5 us -> 14.3 us  [the longest x1 12.2 us: run_outer(): pl.pallas_call(functools.partial(outer_kernel, plan), in_specs=[vmem] * 7...]
  transfers between devices with their start and end apart: 13 -> 12, of which waited for: 5 -> 5; matrix products, arithmetic and copies ran while one was open for 0% -> 0% of each run, Pallas kernels for 16% -> 14%
where the time goes in v11:
time: 117 us
  blocking collectives  64.4 us (55%)
  Pallas kernels  23 us (20%)
  starting transfers between devices  15.7 us (13%)
  waiting for transfers between devices  12.1 us (10%)
    all_to_all x2, blocking collectives, exchange(): lax.all_to_all(values, 'gy', 0, 0, axis_index_groups=groups, tiled=True)  64.4 us
    pallas_call x1, Pallas kernels, run_outer(): pl.pallas_call(functools.partial(outer_kernel, plan), in_specs=[vmem] * 7...  12.2 us
    ppermute x8, starting transfers between devices, swap(): lax.ppermute(values, 'gy', [(i, i ^ mask) for i in range(lax.axis_size('g...  11 us
    ppermute x8, waiting for transfers between devices, swap(): lax.ppermute(values, 'gy', [(i, i ^ mask) for i in range(lax.axis_size('g...  6.94 us
    pallas_call x1, Pallas kernels, run_inner(): pl.pallas_call(functools.partial(inner_kernel, plan), in_specs=[vmem] * 3...  4.49 us
    ppermute x1, waiting for transfers between devices, per_device(): x_lo = lax.ppermute(to_next, 'gx', ring('gx', 1))  3.07 us
  transfers between devices with their start and end apart: 12, of which 5 were waited for; matrix products, arithmetic and copies ran while one was open for 0% of the time, Pallas kernels for 14%

profile of v11, /device:TPU:8, one launch (start us, length us, event | category | flops | bytes accessed | tf_op | source)
XLA Modules:
  0.0 116.6 jit_solution(4355299539964885664)
XLA Ops:
  0.6 0.0 copy-start.1
  0.6 0.0 copy-start
  0.7 2.0 %pack_y.1 = (f32[33,8,128]{2,1,0:T(8,128)}, f32[33,8,128]{2,1,0:T(8,128)}, f32[24,128]{1,0:T(8,128)}) custom-call(f32[1,2]{1,0:T(1,128)} %under.1, f32[1,2]{1,0:T(1,128)} %mobile.1, f32[1,2]{1,0:T(1,128)} %spread.1, s32[1,2]{1,0:T(1,128)} %owner.1, f32[1,2,32,32,128]{4,3,2,1,0:T(8,128)} %phase.3, f32[1,2,32,32,128]{4,3,2,1,0:T(8,128)} %phase.3, ...), custom_call_target="tpu_custom_call" | custom-call | tf_op jit(solution)/shard_map/pack_y/pallas_call | solution.py:48
  2.7 1.5 %collective-permute-start = (f32[33,8,128]{2,1,0:T(8,128)}, f32[33,8,128]{2,1,0:T(8,128)S(1)}, u32[]{:S(2)}, u32[]{:S(2)}) collective-permute-start(f32[33,8,128]{2,1,0:T(8,128)} %get-tuple-element.29), channel_id=1, source_target_pairs={{0,1},{1,2},{2,3},{3,4},{4,5},{5,6},{6,7},{7,0},{8,9},{9,10},{10,1... | collective-permute-start | bytes 405512 | tf_op jit(solution)/shard_map/ppermute | solution.py:485
  4.2 1.4 %collective-permute-start.1 = (f32[33,8,128]{2,1,0:T(8,128)}, f32[33,8,128]{2,1,0:T(8,128)S(1)}, u32[]{:S(2)}, u32[]{:S(2)}) collective-permute-start(f32[33,8,128]{2,1,0:T(8,128)} %get-tuple-element.30), channel_id=1, source_target_pairs={{0,7},{1,0},{2,1},{3,2},{4,3},{5,4},{6,5},{7,6},{8,15},{9,8},{10,9... | collective-permute-start | bytes 405512 | tf_op jit(solution)/shard_map/ppermute | solution.py:486
  5.6 0.0 copy-done.1
  5.6 0.0 copy-done
  5.6 0.0 copy-start.2
  5.6 0.7 copy-done.2
  6.3 4.5 %inner.1 = (f32[520,128]{1,0:T(8,128)S(1)}, f32[520,128]{1,0:T(8,128)S(1)}) custom-call(f32[24,128]{1,0:T(8,128)S(1)} %copy-done.2, f32[1,2,32,32,128]{4,3,2,1,0:T(8,128)S(1)} %copy-done, f32[1,2,32,32,128]{4,3,2,1,0:T(8,128)S(1)} %copy-done.1), custom_call_target="tpu_custom_call" | custom-call | flops 100000000 | bytes 25165824 | tf_op jit(solution)/shard_map/inner/pallas_call | solution.py:266
  10.8 0.0 collective-permute-done.y_lo
  10.8 1.2 %collective-permute-done.1.y_hi = f32[33,8,128]{2,1,0:T(8,128)S(1)} collective-permute-done((f32[33,8,128]{2,1,0:T(8,128)}, f32[33,8,128]{2,1,0:T(8,128)S(1)}, u32[]{:S(2)}, u32[]{:S(2)}) %collective-permute-start.1) | collective-permute-done | bytes 135200 | tf_op jit(solution)/shard_map/ppermute | solution.py:486
  12.0 0.0 copy-start.3
  12.0 0.1 collective-permute-start.2
  12.1 1.7 %collective-permute-start.3 = (f32[608,128]{1,0:T(8,128)S(1)}, f32[608,128]{1,0:T(8,128)S(1)}, u32[]{:S(2)}, u32[]{:S(2)}) collective-permute-start(f32[608,128]{1,0:T(8,128)S(1)} %get-tuple-element.33), channel_id=1, source_target_pairs={{0,24},{8,0},{16,8},{24,16},{1,25},{9,1},{17,9},{25,17},{2,26},{10... | collective-permute-start | bytes 933896 | tf_op jit(solution)/shard_map/ppermute | solution.py:491
  13.8 2.6 %collective-permute-start.4 = (f32[520,128]{1,0:T(8,128)S(1)}, f32[520,128]{1,0:T(8,128)S(1)}, u32[]{:S(2)}, u32[]{:S(2)}) collective-permute-start(f32[520,128]{1,0:T(8,128)S(1)} %get-tuple-element.31._), channel_id=1, source_target_pairs={{0,4},{1,5},{2,6},{3,7},{4,0},{5,1},{6,2},{7,3},{8,12},{9,13},{10,... | collective-permute-start | bytes 798728 | tf_op jit(solution)/shard_map/ppermute | solution.py:469
  16.4 0.0 copy-start.4
  16.4 0.4 collective-permute-start.5
  16.8 3.1 %collective-permute-done.2.x_lo = f32[608,128]{1,0:T(8,128)S(1)} collective-permute-done((f32[608,128]{1,0:T(8,128)S(1)}, f32[608,128]{1,0:T(8,128)S(1)}, u32[]{:S(2)}, u32[]{:S(2)}) %collective-permute-start.2) | collective-permute-done | bytes 311328 | tf_op jit(solution)/shard_map/ppermute | solution.py:490
  19.9 0.9 collective-permute-done.3.x_hi
  20.8 0.0 copy-done.3
  20.8 12.2 %outer.1 = (f32[4,520,128]{2,1,0:T(8,128)S(1)}, f32[520,128]{1,0:T(8,128)}, f32[520,128]{1,0:T(8,128)S(1)}) custom-call(f32[24,128]{1,0:T(8,128)S(1)} %copy-done.3, f32[1,2,32,32,128]{4,3,2,1,0:T(8,128)S(1)} %copy-done, f32[1,2,32,32,128]{4,3,2,1,0:T(8,128)S(1)} %copy-done.1, f32[33,8,128]{2,1,0:T(8,128)S(1)} %collective-permute-done.y_lo, ...), custom_call_target="tpu_custom_call" | custom-call | flops 100000000 | bytes 41943040 | tf_op jit(solution)/shard_map/outer/pallas_call | solution.py:348
  32.9 1.6 %collective-permute-start.6 = (f32[520,128]{1,0:T(8,128)}, f32[520,128]{1,0:T(8,128)S(1)}, u32[]{:S(2)}, u32[]{:S(2)}) collective-permute-start(f32[520,128]{1,0:T(8,128)} %get-tuple-element.36), channel_id=1, source_target_pairs={{0,6},{1,7},{2,4},{3,5},{4,2},{5,3},{6,0},{7,1},{8,14},{9,15},{10,... | collective-permute-start | bytes 798728 | tf_op jit(solution)/shard_map/ppermute | solution.py:469
  34.5 0.5 collective-permute-start.7
  35.0 0.0 copy-done.4
  35.1 27.4 %conditional.2 = (f32[4,520,128]{2,1,0:T(8,128)}) conditional(s32[]{:T(128)} %bitcast, f32[4,520,128]{2,1,0:T(8,128)S(1)} %get-tuple-element.34, f32[4,520,128]{2,1,0:T(8,128)S(1)} %get-tuple-element.34), branch_computations={%region_0.0_spmd, %region_1.0_spmd} | conditional | bytes 2129928 | solution.py:477
  35.1 27.4 %all_to_all.17 = f32[4,520,128]{2,1,0:T(8,128)} all-to-all(f32[4,520,128]{2,1,0:T(8,128)S(1)} %param.1), channel_id=1, replica_groups={{0,1,2,3},{4,5,6,7},{8,9,10,11},{12,13,14,15},{16,17,18,19},{20,21,22,2..., dimensions={0} | all-to-all | bytes 2129920 | tf_op jit(solution)/shard_map/cond/branch_1_fun/all_to_all | solution.py:475
  62.5 0.0 collective-permute-done.5.refs_1_
  62.5 0.0 collective-permute-done.4.refs_0_
  62.5 0.0 collective-permute-done.6.refs_2_
  62.5 1.5 %collective-permute-done.7.refs_3_ = f32[520,128]{1,0:T(8,128)S(1)} collective-permute-done((f32[520,128]{1,0:T(8,128)S(1)}, f32[520,128]{1,0:T(8,128)S(1)}, u32[]{:S(2)}, u32[]{:S(2)}) %collective-permute-start.7) | collective-permute-done | bytes 266272 | tf_op jit(solution)/shard_map/ppermute | solution.py:469
  64.0 2.2 %route.1 = (f32[4,2,256,128]{3,2,1,0:T(8,128)S(1)}, f32[2,256,128]{2,1,0:T(8,128)S(1)}, f32[2,256,128]{2,1,0:T(8,128)S(1)}, f32[2,256,128]{2,1,0:T(8,128)S(1)}, ...) custom-call(f32[4,520,128]{2,1,0:T(8,128)} %get-tuple-element.44.near, f32[520,128]{1,0:T(8,128)S(1)} %collective-permute-done.4.refs_0_, ...), custom_call_target="tpu_custom_call" | custom-call | tf_op jit(solution)/shard_map/route/pallas_call | solution.py:398
  66.2 1.6 %collective-permute-start.8 = (f32[2,256,128]{2,1,0:T(8,128)S(1)}, f32[2,256,128]{2,1,0:T(8,128)S(1)}, u32[]{:S(2)}, u32[]{:S(2)}) collective-permute-start(f32[2,256,128]{2,1,0:T(8,128)S(1)} %get-tuple-element.40), channel_id=1, source_target_pairs={{0,4},{1,5},{2,6},{3,7},{4,0},{5,1},{6,2},{7,3},{8,12},{9,13},{10,... | collective-permute-start | bytes 786440 | tf_op jit(solution)/shard_map/ppermute | solution.py:469
  67.8 2.9 %collective-permute-start.9 = (f32[2,256,128]{2,1,0:T(8,128)S(1)}, f32[2,256,128]{2,1,0:T(8,128)S(1)}, u32[]{:S(2)}, u32[]{:S(2)}) collective-permute-start(f32[2,256,128]{2,1,0:T(8,128)S(1)} %get-tuple-element.41), channel_id=1, source_target_pairs={{0,5},{1,4},{2,7},{3,6},{4,1},{5,0},{6,3},{7,2},{8,13},{9,12},{10,... | collective-permute-start | bytes 786440 | tf_op jit(solution)/shard_map/ppermute | solution.py:469
  70.7 1.0 collective-permute-start.10
  71.7 0.4 collective-permute-start.11
  72.1 37.0 %conditional.3 = (f32[4,2,256,128]{3,2,1,0:T(8,128)S(1)}) conditional(s32[]{:T(128)} %bitcast, f32[4,2,256,128]{3,2,1,0:T(8,128)S(1)} %get-tuple-element.39, f32[4,2,256,128]{3,2,1,0:T(8,128)S(1)} %get-tuple-element.39), branch_computations={%region_2.0_spmd, %region_3.0_spmd} | conditional | bytes 2097160 | solution.py:477
  72.1 37.0 %all_to_all.19 = f32[4,2,256,128]{3,2,1,0:T(8,128)S(1)} all-to-all(f32[4,2,256,128]{3,2,1,0:T(8,128)S(1)} %param.3), channel_id=1, replica_groups={{0,1,2,3},{4,5,6,7},{8,9,10,11},{12,13,14,15},{16,17,18,19},{20,21,22,2..., dimensions={0} | all-to-all | bytes 2097152 | tf_op jit(solution)/shard_map/cond/branch_1_fun/all_to_all | solution.py:475
  109.1 0.0 collective-permute-done.8.refs_0_
  109.1 0.0 collective-permute-done.9.refs_1_
  109.1 0.0 collective-permute-done.10.refs_2_
  109.1 5.4 %collective-permute-done.11.refs_3_ = f32[2,256,128]{2,1,0:T(8,128)S(1)} collective-permute-done((f32[2,256,128]{2,1,0:T(8,128)S(1)}, f32[2,256,128]{2,1,0:T(8,128)S(1)}, u32[]{:S(2)}, u32[]{:S(2)}) %collective-permute-start.11) | collective-permute-done | bytes 262176 | tf_op jit(solution)/shard_map/ppermute | solution.py:469
  114.5 2.1 %settle.1 = (f32[1,2,32,32,128]{4,3,2,1,0:T(8,128)}, f32[1,2,32,32,128]{4,3,2,1,0:T(8,128)}) custom-call(s32[16]{0:T(128)S(1)} %get-tuple-element.38.table, f32[4,2,256,128]{3,2,1,0:T(8,128)S(1)} %get-tuple-element.45.near, f32[2,256,128]{2,1,0:T(8,128)S(1)} %collective-permute-done.8.refs_0_, f32[2,256,128]{2,1,0:T(8,128)S(1)} %collective-permute-done.9.refs_1_, ...), custom_call_target="tpu_custom_call" | custom-call | tf_op jit(solution)/shard_map/settle/pallas_call | solution.py:453
  (1 shorter events, 0.0 us)
Async XLA Ops:
  0.6 5.0 %copy-start.1 = (f32[1,2,32,32,128]{4,3,2,1,0:T(8,128)S(1)}, f32[1,2,32,32,128]{4,3,2,1,0:T(8,128)}, u32[]{:S(2)}) copy-start(f32[1,2,32,32,128]{4,3,2,1,0:T(8,128)} %solute.3) | copy-start | bytes 3145732
  0.6 5.0 %copy-start = (f32[1,2,32,32,128]{4,3,2,1,0:T(8,128)S(1)}, f32[1,2,32,32,128]{4,3,2,1,0:T(8,128)}, u32[]{:S(2)}) copy-start(f32[1,2,32,32,128]{4,3,2,1,0:T(8,128)} %phase.3) | copy-start | bytes 3145732
  2.7 8.1 %collective-permute-start = (f32[33,8,128]{2,1,0:T(8,128)}, f32[33,8,128]{2,1,0:T(8,128)S(1)}, u32[]{:S(2)}, u32[]{:S(2)}) collective-permute-start(f32[33,8,128]{2,1,0:T(8,128)} %get-tuple-element.29), channel_id=1, source_target_pairs={{0,1},{1,2},{2,3},{3,4},{4,5},{5,6},{6,7},{7,0},{8,9},{9,10},{10,1... | collective-permute-start | bytes 405512 | tf_op jit(solution)/shard_map/ppermute | solution.py:485
  4.2 7.8 %collective-permute-start.1 = (f32[33,8,128]{2,1,0:T(8,128)}, f32[33,8,128]{2,1,0:T(8,128)S(1)}, u32[]{:S(2)}, u32[]{:S(2)}) collective-permute-start(f32[33,8,128]{2,1,0:T(8,128)} %get-tuple-element.30), channel_id=1, source_target_pairs={{0,7},{1,0},{2,1},{3,2},{4,3},{5,4},{6,5},{7,6},{8,15},{9,8},{10,9... | collective-permute-start | bytes 405512 | tf_op jit(solution)/shard_map/ppermute | solution.py:486
  5.6 0.7 copy-start.2
  12.0 8.8 %copy-start.3 = (f32[24,128]{1,0:T(8,128)S(1)}, f32[24,128]{1,0:T(8,128)}, u32[]{:S(2)}) copy-start(f32[24,128]{1,0:T(8,128)} %get-tuple-element.28.own) | copy-start | bytes 36868
  12.0 7.9 %collective-permute-start.2 = (f32[608,128]{1,0:T(8,128)S(1)}, f32[608,128]{1,0:T(8,128)S(1)}, u32[]{:S(2)}, u32[]{:S(2)}) collective-permute-start(f32[608,128]{1,0:T(8,128)S(1)} %get-tuple-element.32), channel_id=1, source_target_pairs={{0,8},{8,16},{16,24},{24,0},{1,9},{9,17},{17,25},{25,1},{2,10},{10... | collective-permute-start | bytes 933896 | tf_op jit(solution)/shard_map/ppermute | solution.py:490
  12.1 8.7 %collective-permute-start.3 = (f32[608,128]{1,0:T(8,128)S(1)}, f32[608,128]{1,0:T(8,128)S(1)}, u32[]{:S(2)}, u32[]{:S(2)}) collective-permute-start(f32[608,128]{1,0:T(8,128)S(1)} %get-tuple-element.33), channel_id=1, source_target_pairs={{0,24},{8,0},{16,8},{24,16},{1,25},{9,1},{17,9},{25,17},{2,26},{10... | collective-permute-start | bytes 933896 | tf_op jit(solution)/shard_map/ppermute | solution.py:491
  13.8 48.6 %collective-permute-start.4 = (f32[520,128]{1,0:T(8,128)S(1)}, f32[520,128]{1,0:T(8,128)S(1)}, u32[]{:S(2)}, u32[]{:S(2)}) collective-permute-start(f32[520,128]{1,0:T(8,128)S(1)} %get-tuple-element.31._), channel_id=1, source_target_pairs={{0,4},{1,5},{2,6},{3,7},{4,0},{5,1},{6,2},{7,3},{8,12},{9,13},{10,... | collective-permute-start | bytes 798728 | tf_op jit(solution)/shard_map/ppermute | solution.py:469
  16.4 18.6 %copy-start.4 = (s32[1,2]{1,0:T(1,128)S(1)}, s32[1,2]{1,0:T(1,128)}, u32[]{:S(2)}) copy-start(s32[1,2]{1,0:T(1,128)} %owner.1) | copy-start | bytes 28
  16.4 46.0 %collective-permute-start.5 = (f32[520,128]{1,0:T(8,128)S(1)}, f32[520,128]{1,0:T(8,128)S(1)}, u32[]{:S(2)}, u32[]{:S(2)}) collective-permute-start(f32[520,128]{1,0:T(8,128)S(1)} %get-tuple-element.35), channel_id=1, source_target_pairs={{0,5},{1,4},{2,7},{3,6},{4,1},{5,0},{6,3},{7,2},{8,13},{9,12},{10,... | collective-permute-start | bytes 798728 | tf_op jit(solution)/shard_map/ppermute | solution.py:469
  32.9 29.6 %collective-permute-start.6 = (f32[520,128]{1,0:T(8,128)}, f32[520,128]{1,0:T(8,128)S(1)}, u32[]{:S(2)}, u32[]{:S(2)}) collective-permute-start(f32[520,128]{1,0:T(8,128)} %get-tuple-element.36), channel_id=1, source_target_pairs={{0,6},{1,7},{2,4},{3,5},{4,2},{5,3},{6,0},{7,1},{8,14},{9,15},{10,... | collective-permute-start | bytes 798728 | tf_op jit(solution)/shard_map/ppermute | solution.py:469
  34.5 29.5 %collective-permute-start.7 = (f32[520,128]{1,0:T(8,128)S(1)}, f32[520,128]{1,0:T(8,128)S(1)}, u32[]{:S(2)}, u32[]{:S(2)}) collective-permute-start(f32[520,128]{1,0:T(8,128)S(1)} %get-tuple-element.37), channel_id=1, source_target_pairs={{0,7},{1,6},{2,5},{3,4},{4,3},{5,2},{6,1},{7,0},{8,15},{9,14},{10,... | collective-permute-start | bytes 798728 | tf_op jit(solution)/shard_map/ppermute | solution.py:469
  66.2 42.9 %collective-permute-start.8 = (f32[2,256,128]{2,1,0:T(8,128)S(1)}, f32[2,256,128]{2,1,0:T(8,128)S(1)}, u32[]{:S(2)}, u32[]{:S(2)}) collective-permute-start(f32[2,256,128]{2,1,0:T(8,128)S(1)} %get-tuple-element.40), channel_id=1, source_target_pairs={{0,4},{1,5},{2,6},{3,7},{4,0},{5,1},{6,2},{7,3},{8,12},{9,13},{10,... | collective-permute-start | bytes 786440 | tf_op jit(solution)/shard_map/ppermute | solution.py:469
  67.8 41.3 %collective-permute-start.9 = (f32[2,256,128]{2,1,0:T(8,128)S(1)}, f32[2,256,128]{2,1,0:T(8,128)S(1)}, u32[]{:S(2)}, u32[]{:S(2)}) collective-permute-start(f32[2,256,128]{2,1,0:T(8,128)S(1)} %get-tuple-element.41), channel_id=1, source_target_pairs={{0,5},{1,4},{2,7},{3,6},{4,1},{5,0},{6,3},{7,2},{8,13},{9,12},{10,... | collective-permute-start | bytes 786440 | tf_op jit(solution)/shard_map/ppermute | solution.py:469
  70.7 38.4 %collective-permute-start.10 = (f32[2,256,128]{2,1,0:T(8,128)S(1)}, f32[2,256,128]{2,1,0:T(8,128)S(1)}, u32[]{:S(2)}, u32[]{:S(2)}) collective-permute-start(f32[2,256,128]{2,1,0:T(8,128)S(1)} %get-tuple-element.42), channel_id=1, source_target_pairs={{0,6},{1,7},{2,4},{3,5},{4,2},{5,3},{6,0},{7,1},{8,14},{9,15},{10,... | collective-permute-start | bytes 786440 | tf_op jit(solution)/shard_map/ppermute | solution.py:469
  71.7 42.9 %collective-permute-start.11 = (f32[2,256,128]{2,1,0:T(8,128)S(1)}, f32[2,256,128]{2,1,0:T(8,128)S(1)}, u32[]{:S(2)}, u32[]{:S(2)}) collective-permute-start(f32[2,256,128]{2,1,0:T(8,128)S(1)} %get-tuple-element.43), channel_id=1, source_target_pairs={{0,7},{1,6},{2,5},{3,4},{4,3},{5,2},{6,1},{7,0},{8,15},{9,14},{10,... | collective-permute-start | bytes 786440 | tf_op jit(solution)/shard_map/ppermute | solution.py:469

commit v12 on v11

--- a/solution.py
+++ b/solution.py
@@ -469,12 +469,17 @@
     return lax.ppermute(values, "gy", [(i, i ^ mask) for i in range(lax.axis_size("gy"))])
 
 
-def among_half(plan, values, together):
-    def exchange(values):
-        groups = [list(range(plan.half)), list(range(plan.half, plan.pieces))]
-        return lax.all_to_all(values, "gy", 0, 0, axis_index_groups=groups, tiled=True)
-
-    return lax.cond(together, exchange, exchange, values)
+def exchange_near(plan, values):
+    groups = [list(range(plan.half)), list(range(plan.half, plan.pieces))]
+    return lax.all_to_all(values, "gy", 0, 0, axis_index_groups=groups, tiled=True)
+
+
+def exchange_far(plan, index, values):
+    return swap(values, plan.half + index)
+
+
+def at_once(together, exchange, *values):
+    return lax.cond(together, exchange, exchange, *values)
 
 
 def per_device(phase, solute, undercool, mobility, diffusivity, owner):
@@ -485,17 +490,21 @@
     y_lo = lax.ppermute(to_next, "gy", ring("gy", 1))
     y_hi = lax.ppermute(to_prev, "gy", ring("gy", -1))
     first = run_inner(plan, own, phase, solute)
-    far = [swap(values, half + index) for index, values in enumerate(first)]
+    far = [exchange_far(plan, index, values) for index, values in enumerate(first)]
     to_prev, to_next = pack_x(phase, solute, own, y_lo, y_hi, first[0])
     x_lo = lax.ppermute(to_next, "gx", ring("gx", 1))
     x_hi = lax.ppermute(to_prev, "gx", ring("gx", -1))
     near, *second = run_outer(plan, own, phase, solute, (y_lo, y_hi, x_lo, x_hi))
-    far += [swap(values, half + half // 2 + index) for index, values in enumerate(second)]
     together = owner[0, 0] >= 0
-    near = among_half(plan, near, together)
-    near, far, table = route(plan, near, far)
-    far = [swap(values, half + index) for index, values in enumerate(far)]
-    near = among_half(plan, near, together)
+
+    def exchange_late(near, *second):
+        late = [exchange_far(plan, half // 2 + index, values) for index, values in enumerate(second)]
+        return exchange_near(plan, near), late
+
+    near, late = at_once(together, exchange_late, near, *second)
+    near, far, table = route(plan, near, far + late)
+    far = [exchange_far(plan, index, values) for index, values in enumerate(far)]
+    near = at_once(together, functools.partial(exchange_near, plan), near)
     return tuple(settle(plan, table, near, far))
 
 

time: 117 us -> 119 us (1.017); the launches traced: 117 us -> 117 us
  blocking collectives: 64.4 us -> 39.8 us
  waiting for transfers between devices: 12.1 us -> 28.6 us
  starting transfers between devices: 15.7 us -> 23.9 us
    all_to_all x2 -> x1, blocking collectives: 64.4 us -> 39.8 us  [exchange_near(): lax.all_to_all(values, 'gy', 0, 0, axis_index_groups=groups, tiled=True)]
    ppermute x8, waiting for transfers between devices: 6.94 us -> 23.6 us  [swap(): lax.ppermute(values, 'gy', [(i, i ^ mask) for i in range(lax.axis_size('g...]
    all_to_all x0 -> x1, starting transfers between devices: none -> 5.44 us  [exchange_near(): lax.all_to_all(values, 'gy', 0, 0, axis_index_groups=groups, tiled=True)]
    ppermute x8, starting transfers between devices: 11 us -> 13.7 us  [swap(): lax.ppermute(values, 'gy', [(i, i ^ mask) for i in range(lax.axis_size('g...]
  transfers between devices with their start and end apart: 12 -> 13, of which waited for: 5 -> 6; matrix products, arithmetic and copies ran while one was open for 0% -> 0% of each run, Pallas kernels for 14% -> 15%
where the time goes in v12:
time: 119 us; the launch traced here: 117 us
  blocking collectives  39.8 us (33%)
  waiting for transfers between devices  28.6 us (24%)
  starting transfers between devices  23.9 us (20%)
  Pallas kernels  23.5 us (20%)
    all_to_all x1, blocking collectives, exchange_near(): lax.all_to_all(values, 'gy', 0, 0, axis_index_groups=groups, tiled=True)  39.8 us
    ppermute x8, waiting for transfers between devices, swap(): lax.ppermute(values, 'gy', [(i, i ^ mask) for i in range(lax.axis_size('g...  23.6 us
    ppermute x8, starting transfers between devices, swap(): lax.ppermute(values, 'gy', [(i, i ^ mask) for i in range(lax.axis_size('g...  13.7 us
    pallas_call x1, Pallas kernels, run_outer(): pl.pallas_call(functools.partial(outer_kernel, plan), in_specs=[vmem] * 7...  12.5 us
    all_to_all x1, starting transfers between devices, exchange_near(): lax.all_to_all(values, 'gy', 0, 0, axis_index_groups=groups, tiled=True)  5.44 us
    pallas_call x1, Pallas kernels, run_inner(): pl.pallas_call(functools.partial(inner_kernel, plan), in_specs=[vmem] * 3...  4.49 us
    ppermute x1, waiting for transfers between devices, per_device(): x_lo = lax.ppermute(to_next, 'gx', ring('gx', 1))  3.02 us
  transfers between devices with their start and end apart: 13, of which 6 were waited for; matrix products, arithmetic and copies ran while one was open for 0% of the time, Pallas kernels for 15%

profile of v12, /device:TPU:8, one launch (start us, length us, event | category | flops | bytes accessed | tf_op | source)
XLA Modules:
  0.0 117.2 jit_solution(11647551942107728221)
XLA Ops:
  0.6 0.0 copy-start.1
  0.6 0.0 copy-start
  0.7 2.0 %pack_y.1 = (f32[33,8,128]{2,1,0:T(8,128)}, f32[33,8,128]{2,1,0:T(8,128)}, f32[24,128]{1,0:T(8,128)}) custom-call(f32[1,2]{1,0:T(1,128)} %under.1, f32[1,2]{1,0:T(1,128)} %mobile.1, f32[1,2]{1,0:T(1,128)} %spread.1, s32[1,2]{1,0:T(1,128)} %owner.1, f32[1,2,32,32,128]{4,3,2,1,0:T(8,128)} %phase.3, f32[1,2,32,32,128]{4,3,2,1,0:T(8,128)} %phase.3, ...), custom_call_target="tpu_custom_call" | custom-call | tf_op jit(solution)/shard_map/pack_y/pallas_call | solution.py:48
  2.7 1.5 %collective-permute-start.4 = (f32[33,8,128]{2,1,0:T(8,128)}, f32[33,8,128]{2,1,0:T(8,128)S(1)}, u32[]{:S(2)}, u32[]{:S(2)}) collective-permute-start(f32[33,8,128]{2,1,0:T(8,128)} %get-tuple-element.42), channel_id=1, source_target_pairs={{0,1},{1,2},{2,3},{3,4},{4,5},{5,6},{6,7},{7,0},{8,9},{9,10},{10,1... | collective-permute-start | bytes 405512 | tf_op jit(solution)/shard_map/ppermute | solution.py:490
  4.2 1.4 %collective-permute-start.5 = (f32[33,8,128]{2,1,0:T(8,128)}, f32[33,8,128]{2,1,0:T(8,128)S(1)}, u32[]{:S(2)}, u32[]{:S(2)}) collective-permute-start(f32[33,8,128]{2,1,0:T(8,128)} %get-tuple-element.43), channel_id=1, source_target_pairs={{0,7},{1,0},{2,1},{3,2},{4,3},{5,4},{6,5},{7,6},{8,15},{9,8},{10,9... | collective-permute-start | bytes 405512 | tf_op jit(solution)/shard_map/ppermute | solution.py:491
  5.6 0.0 copy-done.1
  5.6 0.0 copy-done
  5.6 0.0 copy-start.2
  5.6 0.7 copy-done.2
  6.3 4.5 %inner.1 = (f32[520,128]{1,0:T(8,128)S(1)}, f32[520,128]{1,0:T(8,128)S(1)}) custom-call(f32[24,128]{1,0:T(8,128)S(1)} %copy-done.2, f32[1,2,32,32,128]{4,3,2,1,0:T(8,128)S(1)} %copy-done, f32[1,2,32,32,128]{4,3,2,1,0:T(8,128)S(1)} %copy-done.1), custom_call_target="tpu_custom_call" | custom-call | flops 100000000 | bytes 25165824 | tf_op jit(solution)/shard_map/inner/pallas_call | solution.py:266
  10.8 0.0 collective-permute-done.4.y_lo
  10.8 1.2 %collective-permute-done.5.y_hi = f32[33,8,128]{2,1,0:T(8,128)S(1)} collective-permute-done((f32[33,8,128]{2,1,0:T(8,128)}, f32[33,8,128]{2,1,0:T(8,128)S(1)}, u32[]{:S(2)}, u32[]{:S(2)}) %collective-permute-start.5) | collective-permute-done | bytes 135200 | tf_op jit(solution)/shard_map/ppermute | solution.py:491
  12.0 0.0 copy-start.4
  12.0 0.0 copy-start.3
  12.1 0.1 collective-permute-start.6
  12.1 1.7 %collective-permute-start.7 = (f32[608,128]{1,0:T(8,128)S(1)}, f32[608,128]{1,0:T(8,128)S(1)}, u32[]{:S(2)}, u32[]{:S(2)}) collective-permute-start(f32[608,128]{1,0:T(8,128)S(1)} %get-tuple-element.46), channel_id=1, source_target_pairs={{0,24},{8,0},{16,8},{24,16},{1,25},{9,1},{17,9},{25,17},{2,26},{10... | collective-permute-start | bytes 933896 | tf_op jit(solution)/shard_map/ppermute | solution.py:496
  13.8 2.7 %collective-permute-start.9 = (f32[520,128]{1,0:T(8,128)S(1)}, f32[520,128]{1,0:T(8,128)S(1)}, u32[]{:S(2)}, u32[]{:S(2)}) collective-permute-start(f32[520,128]{1,0:T(8,128)S(1)} %get-tuple-element.48), channel_id=1, source_target_pairs={{0,5},{1,4},{2,7},{3,6},{4,1},{5,0},{6,3},{7,2},{8,13},{9,12},{10,... | collective-permute-start | bytes 798728 | tf_op jit(solution)/shard_map/ppermute | solution.py:469
  16.5 0.3 collective-permute-start.8
  16.8 0.0 copy-done.4
  16.9 3.0 %collective-permute-done.6.x_lo = f32[608,128]{1,0:T(8,128)S(1)} collective-permute-done((f32[608,128]{1,0:T(8,128)S(1)}, f32[608,128]{1,0:T(8,128)S(1)}, u32[]{:S(2)}, u32[]{:S(2)}) %collective-permute-start.6) | collective-permute-done | bytes 311328 | tf_op jit(solution)/shard_map/ppermute | solution.py:495
  19.9 0.9 collective-permute-done.7.x_hi
  20.8 0.0 copy-done.3
  20.8 12.5 %outer.1 = (f32[4,520,128]{2,1,0:T(8,128)}, f32[520,128]{1,0:T(8,128)S(1)}, f32[520,128]{1,0:T(8,128)}) custom-call(f32[24,128]{1,0:T(8,128)S(1)} %copy-done.3, f32[1,2,32,32,128]{4,3,2,1,0:T(8,128)S(1)} %copy-done, f32[1,2,32,32,128]{4,3,2,1,0:T(8,128)S(1)} %copy-done.1, f32[33,8,128]{2,1,0:T(8,128)S(1)} %collective-permute-done.4.y_lo, ...), custom_call_target="tpu_custom_call" | custom-call | flops 100000000 | bytes 41943040 | tf_op jit(solution)/shard_map/outer/pallas_call | solution.py:348
  33.3 29.8 %conditional.2 = (f32[4,520,128]{2,1,0:T(8,128)}, f32[520,128]{1,0:T(8,128)}, f32[520,128]{1,0:T(8,128)}) conditional(s32[]{:T(128)} %bitcast, (f32[4,520,128]{2,1,0:T(8,128)}, f32[520,128]{1,0:T(8,128)S(1)}, f32[520,128]{1,0:T(8,128)}) %outer.1, (f32[4,520,128]{2,1,0:T(8,128)}, f32[520,128]{1,0:T(8,128)S(1)}, f32[520,128]{1,0:T(8,128)}) %outer.1), branch_computations={%region_0.0_spmd, %region_1.0_spmd} | conditional | bytes 6389924 | solution.py:482
  33.3 0.0 copy-start.6
  33.3 5.4 %all-to-all-start.1 = ((f32[4,520,128]{2,1,0:T(8,128)}), f32[4,520,128]{2,1,0:T(8,128)}, u32[]{:S(2)}, u32[]{:S(2)}) async-start(f32[4,520,128]{2,1,0:T(8,128)} %get-tuple-element.20), calls=%async_computation.1 | async-start | bytes 2129920 | tf_op jit(solution)/shard_map/cond/branch_1_fun/all_to_all | solution.py:474
  38.7 0.6 collective-permute-start.2
  39.3 0.0 copy-done.6
  39.3 2.3 %collective-permute-start.3 = (f32[520,128]{1,0:T(8,128)S(1)}, f32[520,128]{1,0:T(8,128)}, u32[]{:S(2)}, u32[]{:S(2)}) collective-permute-start(f32[520,128]{1,0:T(8,128)S(1)} %copy-done.6), channel_id=1, source_target_pairs={{0,7},{1,6},{2,5},{3,4},{4,3},{5,2},{6,1},{7,0},{8,15},{9,14},{10,... | collective-permute-start | bytes 798728 | tf_op jit(solution)/shard_map/cond/branch_1_fun/ppermute | solution.py:469
  41.7 6.4 %collective-permute-done.2 = f32[520,128]{1,0:T(8,128)} collective-permute-done((f32[520,128]{1,0:T(8,128)S(1)}, f32[520,128]{1,0:T(8,128)}, u32[]{:S(2)}, u32[]{:S(2)}) %collective-permute-start.2) | collective-permute-done | bytes 266272 | tf_op jit(solution)/shard_map/cond/branch_1_fun/ppermute | solution.py:469
  48.0 15.1 %collective-permute-done.3 = f32[520,128]{1,0:T(8,128)} collective-permute-done((f32[520,128]{1,0:T(8,128)S(1)}, f32[520,128]{1,0:T(8,128)}, u32[]{:S(2)}, u32[]{:S(2)}) %collective-permute-start.3) | collective-permute-done | bytes 266272 | tf_op jit(solution)/shard_map/cond/branch_1_fun/ppermute | solution.py:469
  63.1 0.0 all-to-all-done.1
  63.1 0.0 collective-permute-done.9.refs_1_
  63.1 0.0 collective-permute-done.8.refs_0_
  63.1 2.3 %route.1 = (f32[4,2,256,128]{3,2,1,0:T(8,128)S(1)}, f32[2,256,128]{2,1,0:T(8,128)S(1)}, f32[2,256,128]{2,1,0:T(8,128)S(1)}, f32[2,256,128]{2,1,0:T(8,128)S(1)}, ...) custom-call(f32[4,520,128]{2,1,0:T(8,128)} %get-tuple-element.47.near, f32[520,128]{1,0:T(8,128)S(1)} %collective-permute-done.8.refs_0_, ...), custom_call_target="tpu_custom_call" | custom-call | tf_op jit(solution)/shard_map/route/pallas_call | solution.py:398
  65.4 4.1 %collective-permute-start.10 = (f32[2,256,128]{2,1,0:T(8,128)S(1)}, f32[2,256,128]{2,1,0:T(8,128)S(1)}, u32[]{:S(2)}, u32[]{:S(2)}) collective-permute-start(f32[2,256,128]{2,1,0:T(8,128)S(1)} %get-tuple-element.53), channel_id=1, source_target_pairs={{0,4},{1,5},{2,6},{3,7},{4,0},{5,1},{6,2},{7,3},{8,12},{9,13},{10,... | collective-permute-start | bytes 786440 | tf_op jit(solution)/shard_map/ppermute | solution.py:469
  69.5 0.3 collective-permute-start.11
  69.8 2.3 %collective-permute-start.12 = (f32[2,256,128]{2,1,0:T(8,128)S(1)}, f32[2,256,128]{2,1,0:T(8,128)S(1)}, u32[]{:S(2)}, u32[]{:S(2)}) collective-permute-start(f32[2,256,128]{2,1,0:T(8,128)S(1)} %get-tuple-element.55), channel_id=1, source_target_pairs={{0,6},{1,7},{2,4},{3,5},{4,2},{5,3},{6,0},{7,1},{8,14},{9,15},{10,... | collective-permute-start | bytes 786440 | tf_op jit(solution)/shard_map/ppermute | solution.py:469
  72.1 1.2 %collective-permute-start.13 = (f32[2,256,128]{2,1,0:T(8,128)S(1)}, f32[2,256,128]{2,1,0:T(8,128)S(1)}, u32[]{:S(2)}, u32[]{:S(2)}) collective-permute-start(f32[2,256,128]{2,1,0:T(8,128)S(1)} %get-tuple-element.56), channel_id=1, source_target_pairs={{0,7},{1,6},{2,5},{3,4},{4,3},{5,2},{6,1},{7,0},{8,15},{9,14},{10,... | collective-permute-start | bytes 786440 | tf_op jit(solution)/shard_map/ppermute | solution.py:469
  73.3 39.8 %conditional.3 = (f32[4,2,256,128]{3,2,1,0:T(8,128)S(1)}) conditional(s32[]{:T(128)} %bitcast, f32[4,2,256,128]{3,2,1,0:T(8,128)S(1)} %get-tuple-element.52, f32[4,2,256,128]{3,2,1,0:T(8,128)S(1)} %get-tuple-element.52), branch_computations={%region_2.0_spmd, %region_3.0_spmd} | conditional | bytes 2097160 | solution.py:482
  73.3 39.8 %all_to_all.17 = f32[4,2,256,128]{3,2,1,0:T(8,128)S(1)} all-to-all(f32[4,2,256,128]{3,2,1,0:T(8,128)S(1)} %param.3), channel_id=1, replica_groups={{0,1,2,3},{4,5,6,7},{8,9,10,11},{12,13,14,15},{16,17,18,19},{20,21,22,2..., dimensions={0} | all-to-all | bytes 2097152 | tf_op jit(solution)/shard_map/cond/branch_1_fun/all_to_all | solution.py:474
  113.0 0.0 collective-permute-done.10.refs_0_
  113.0 0.0 collective-permute-done.11.refs_1_
  113.0 0.0 collective-permute-done.12.refs_2_
  113.0 2.1 %collective-permute-done.13.refs_3_ = f32[2,256,128]{2,1,0:T(8,128)S(1)} collective-permute-done((f32[2,256,128]{2,1,0:T(8,128)S(1)}, f32[2,256,128]{2,1,0:T(8,128)S(1)}, u32[]{:S(2)}, u32[]{:S(2)}) %collective-permute-start.13) | collective-permute-done | bytes 262176 | tf_op jit(solution)/shard_map/ppermute | solution.py:469
  115.2 2.1 %settle.1 = (f32[1,2,32,32,128]{4,3,2,1,0:T(8,128)}, f32[1,2,32,32,128]{4,3,2,1,0:T(8,128)}) custom-call(s32[16]{0:T(128)S(1)} %get-tuple-element.51.table, f32[4,2,256,128]{3,2,1,0:T(8,128)S(1)} %get-tuple-element.63.near, f32[2,256,128]{2,1,0:T(8,128)S(1)} %collective-permute-done.10.refs_0_, f32[2,256,128]{2,1,0:T(8,128)S(1)} %collective-permute-done.11.refs_1_, ...), custom_call_target="tpu_custom_call" | custom-call | tf_op jit(solution)/shard_map/settle/pallas_call | solution.py:453
  (1 shorter events, 0.0 us)
Async XLA Ops:
  0.6 5.0 %copy-start.1 = (f32[1,2,32,32,128]{4,3,2,1,0:T(8,128)S(1)}, f32[1,2,32,32,128]{4,3,2,1,0:T(8,128)}, u32[]{:S(2)}) copy-start(f32[1,2,32,32,128]{4,3,2,1,0:T(8,128)} %solute.3) | copy-start | bytes 3145732
  0.6 5.0 %copy-start = (f32[1,2,32,32,128]{4,3,2,1,0:T(8,128)S(1)}, f32[1,2,32,32,128]{4,3,2,1,0:T(8,128)}, u32[]{:S(2)}) copy-start(f32[1,2,32,32,128]{4,3,2,1,0:T(8,128)} %phase.3) | copy-start | bytes 3145732
  2.7 8.1 %collective-permute-start.4 = (f32[33,8,128]{2,1,0:T(8,128)}, f32[33,8,128]{2,1,0:T(8,128)S(1)}, u32[]{:S(2)}, u32[]{:S(2)}) collective-permute-start(f32[33,8,128]{2,1,0:T(8,128)} %get-tuple-element.42), channel_id=1, source_target_pairs={{0,1},{1,2},{2,3},{3,4},{4,5},{5,6},{6,7},{7,0},{8,9},{9,10},{10,1... | collective-permute-start | bytes 405512 | tf_op jit(solution)/shard_map/ppermute | solution.py:490
  4.2 7.8 %collective-permute-start.5 = (f32[33,8,128]{2,1,0:T(8,128)}, f32[33,8,128]{2,1,0:T(8,128)S(1)}, u32[]{:S(2)}, u32[]{:S(2)}) collective-permute-start(f32[33,8,128]{2,1,0:T(8,128)} %get-tuple-element.43), channel_id=1, source_target_pairs={{0,7},{1,0},{2,1},{3,2},{4,3},{5,4},{6,5},{7,6},{8,15},{9,8},{10,9... | collective-permute-start | bytes 405512 | tf_op jit(solution)/shard_map/ppermute | solution.py:491
  5.6 0.7 copy-start.2
  12.0 4.8 %copy-start.4 = (s32[1,2]{1,0:T(1,128)S(1)}, s32[1,2]{1,0:T(1,128)}, u32[]{:S(2)}) copy-start(s32[1,2]{1,0:T(1,128)} %owner.1) | copy-start | bytes 28
  12.0 8.8 %copy-start.3 = (f32[24,128]{1,0:T(8,128)S(1)}, f32[24,128]{1,0:T(8,128)}, u32[]{:S(2)}) copy-start(f32[24,128]{1,0:T(8,128)} %get-tuple-element.41.own) | copy-start | bytes 36868
  12.1 7.9 %collective-permute-start.6 = (f32[608,128]{1,0:T(8,128)S(1)}, f32[608,128]{1,0:T(8,128)S(1)}, u32[]{:S(2)}, u32[]{:S(2)}) collective-permute-start(f32[608,128]{1,0:T(8,128)S(1)} %get-tuple-element.45), channel_id=1, source_target_pairs={{0,8},{8,16},{16,24},{24,0},{1,9},{9,17},{17,25},{25,1},{2,10},{10... | collective-permute-start | bytes 933896 | tf_op jit(solution)/shard_map/ppermute | solution.py:495
  12.1 8.7 %collective-permute-start.7 = (f32[608,128]{1,0:T(8,128)S(1)}, f32[608,128]{1,0:T(8,128)S(1)}, u32[]{:S(2)}, u32[]{:S(2)}) collective-permute-start(f32[608,128]{1,0:T(8,128)S(1)} %get-tuple-element.46), channel_id=1, source_target_pairs={{0,24},{8,0},{16,8},{24,16},{1,25},{9,1},{17,9},{25,17},{2,26},{10... | collective-permute-start | bytes 933896 | tf_op jit(solution)/shard_map/ppermute | solution.py:496
  13.8 49.2 %collective-permute-start.9 = (f32[520,128]{1,0:T(8,128)S(1)}, f32[520,128]{1,0:T(8,128)S(1)}, u32[]{:S(2)}, u32[]{:S(2)}) collective-permute-start(f32[520,128]{1,0:T(8,128)S(1)} %get-tuple-element.48), channel_id=1, source_target_pairs={{0,5},{1,4},{2,7},{3,6},{4,1},{5,0},{6,3},{7,2},{8,13},{9,12},{10,... | collective-permute-start | bytes 798728 | tf_op jit(solution)/shard_map/ppermute | solution.py:469
  16.5 46.6 %collective-permute-start.8 = (f32[520,128]{1,0:T(8,128)S(1)}, f32[520,128]{1,0:T(8,128)S(1)}, u32[]{:S(2)}, u32[]{:S(2)}) collective-permute-start(f32[520,128]{1,0:T(8,128)S(1)} %get-tuple-element.44._), channel_id=1, source_target_pairs={{0,4},{1,5},{2,6},{3,7},{4,0},{5,1},{6,2},{7,3},{8,12},{9,13},{10,... | collective-permute-start | bytes 798728 | tf_op jit(solution)/shard_map/ppermute | solution.py:469
  33.3 6.0 %copy-start.6 = (f32[520,128]{1,0:T(8,128)S(1)}, f32[520,128]{1,0:T(8,128)}, u32[]{:S(2)}) copy-start(f32[520,128]{1,0:T(8,128)} %get-tuple-element.22) | copy-start | bytes 798724 | tf_op jit(solution)/shard_map/cond
  33.3 29.8 %all-to-all-start.1 = ((f32[4,520,128]{2,1,0:T(8,128)}), f32[4,520,128]{2,1,0:T(8,128)}, u32[]{:S(2)}, u32[]{:S(2)}) async-start(f32[4,520,128]{2,1,0:T(8,128)} %get-tuple-element.20), calls=%async_computation.1 | async-start | bytes 2129920 | tf_op jit(solution)/shard_map/cond/branch_1_fun/all_to_all | solution.py:474
  38.7 9.3 %collective-permute-start.2 = (f32[520,128]{1,0:T(8,128)S(1)}, f32[520,128]{1,0:T(8,128)}, u32[]{:S(2)}, u32[]{:S(2)}) collective-permute-start(f32[520,128]{1,0:T(8,128)S(1)} %get-tuple-element.21), channel_id=1, source_target_pairs={{0,6},{1,7},{2,4},{3,5},{4,2},{5,3},{6,0},{7,1},{8,14},{9,15},{10,... | collective-permute-start | bytes 798728 | tf_op jit(solution)/shard_map/cond/branch_1_fun/ppermute | solution.py:469
  39.3 23.8 %collective-permute-start.3 = (f32[520,128]{1,0:T(8,128)S(1)}, f32[520,128]{1,0:T(8,128)}, u32[]{:S(2)}, u32[]{:S(2)}) collective-permute-start(f32[520,128]{1,0:T(8,128)S(1)} %copy-done.6), channel_id=1, source_target_pairs={{0,7},{1,6},{2,5},{3,4},{4,3},{5,2},{6,1},{7,0},{8,15},{9,14},{10,... | collective-permute-start | bytes 798728 | tf_op jit(solution)/shard_map/cond/branch_1_fun/ppermute | solution.py:469
  65.4 47.6 %collective-permute-start.10 = (f32[2,256,128]{2,1,0:T(8,128)S(1)}, f32[2,256,128]{2,1,0:T(8,128)S(1)}, u32[]{:S(2)}, u32[]{:S(2)}) collective-permute-start(f32[2,256,128]{2,1,0:T(8,128)S(1)} %get-tuple-element.53), channel_id=1, source_target_pairs={{0,4},{1,5},{2,6},{3,7},{4,0},{5,1},{6,2},{7,3},{8,12},{9,13},{10,... | collective-permute-start | bytes 786440 | tf_op jit(solution)/shard_map/ppermute | solution.py:469
  69.5 43.5 %collective-permute-start.11 = (f32[2,256,128]{2,1,0:T(8,128)S(1)}, f32[2,256,128]{2,1,0:T(8,128)S(1)}, u32[]{:S(2)}, u32[]{:S(2)}) collective-permute-start(f32[2,256,128]{2,1,0:T(8,128)S(1)} %get-tuple-element.54), channel_id=1, source_target_pairs={{0,5},{1,4},{2,7},{3,6},{4,1},{5,0},{6,3},{7,2},{8,13},{9,12},{10,... | collective-permute-start | bytes 786440 | tf_op jit(solution)/shard_map/ppermute | solution.py:469
  69.8 43.3 %collective-permute-start.12 = (f32[2,256,128]{2,1,0:T(8,128)S(1)}, f32[2,256,128]{2,1,0:T(8,128)S(1)}, u32[]{:S(2)}, u32[]{:S(2)}) collective-permute-start(f32[2,256,128]{2,1,0:T(8,128)S(1)} %get-tuple-element.55), channel_id=1, source_target_pairs={{0,6},{1,7},{2,4},{3,5},{4,2},{5,3},{6,0},{7,1},{8,14},{9,15},{10,... | collective-permute-start | bytes 786440 | tf_op jit(solution)/shard_map/ppermute | solution.py:469
  72.1 43.1 %collective-permute-start.13 = (f32[2,256,128]{2,1,0:T(8,128)S(1)}, f32[2,256,128]{2,1,0:T(8,128)S(1)}, u32[]{:S(2)}, u32[]{:S(2)}) collective-permute-start(f32[2,256,128]{2,1,0:T(8,128)S(1)} %get-tuple-element.56), channel_id=1, source_target_pairs={{0,7},{1,6},{2,5},{3,4},{4,3},{5,2},{6,1},{7,0},{8,15},{9,14},{10,... | collective-permute-start | bytes 786440 | tf_op jit(solution)/shard_map/ppermute | solution.py:469

commit v13 on v11

--- a/solution.py
+++ b/solution.py
@@ -204,18 +204,19 @@
 
 
 AUX = 8
-UNROLL = 4
-
-
-def march(first, last, starts, source, target, coefs_of):
-    def one_row(row, carry):
+UNROLL = 8
+
+
+def march(count, row_of, starts, source, target, coefs_of):
+    def one_row(index, carry):
+        row = row_of(index)
         for start in starts:
             new_p, new_u = cells(source[0], source[1], row, start, coefs_of(row, start))
             target[0][row, start : start + 8, :] = new_p
             target[1][row, start : start + 8, :] = new_u
         return carry
 
-    lax.fori_loop(first, last, one_row, 0, unroll=UNROLL)
+    lax.fori_loop(0, count, one_row, 0, unroll=UNROLL)
 
 
 def inner_kernel(plan, own, phase, solute, *rest):
@@ -234,13 +235,20 @@
 
     lax.fori_loop(0, count + 2 * W, load_row, 0, unroll=UNROLL)
 
+    line = lax.broadcasted_iota(jnp.int32, (8, plan.depth), 0)
+
     def coefs_of(row, start):
-        tile = (start - PAD) // edge
-        return tuple(own[8 * tile + kind : 8 * tile + kind + 1, :] for kind in range(KINDS))
+        low, high = (start - PAD) // edge, (start + 7 - PAD) // edge
+        rows = [[own[8 * tile + kind : 8 * tile + kind + 1, :] for tile in (low, high)] for kind in range(KINDS)]
+        if low == high:
+            return tuple(pair[0] for pair in rows)
+        return tuple(jnp.where(line < W, *pair) for pair in rows)
 
     for step in range(NSTEPS):
-        starts = range(PAD, PAD + tiles * edge, 8)
-        march(step + 1, count + 2 * W - step - 1, starts, pairs[step % 2], pairs[(step + 1) % 2], coefs_of)
+        margin = 8 if step == NSTEPS - 1 else W
+        starts = range(PAD + margin, PAD + tiles * edge - margin, 8)
+        rows = count + 2 * W - 2 * (step + 1)
+        march(rows, lambda i, step=step: step + 1 + i, starts, pairs[step % 2], pairs[(step + 1) % 2], coefs_of)
     for index, out in enumerate(outs):
         pack(plan, True, mine ^ index, pairs[NSTEPS % 2], -base, PAD, own, out)
 
@@ -325,13 +333,33 @@
 
     any_zone = coefs_of(lambda row: jnp.where(row < W, 0, jnp.where(row < W + edge, 1, 2)))
 
+    own_zone = coefs_of(lambda row: 1)
+    mine = lax.rem(lax.axis_index("gy"), half)
+    made = plan.inner // 2
+    first_made = 2 * W + mine // (half // 2) * made
+
+    def blocks(first, last):
+        low, high = (first + W - shift) // 8 * 8, -(-(last + W - shift) // 8) * 8
+        return list(range(PAD + shift + low, PAD + shift + high, 8))
+
     for step in range(1, NSTEPS + 1):
+        source, target = pairs[(step - 1) % 2], pairs[step % 2]
         left = NSTEPS - step
         shift = W if step == NSTEPS else 0
-        starts = range(PAD + shift, PAD + width - shift, 8)
-        march(W - left, W + edge + left, starts, pairs[(step - 1) % 2], pairs[step % 2], any_zone)
+        whole = blocks(-left, cols + left)
+        ends = blocks(-left, 8 + left) + blocks(cols - 8 - left, cols + left)
+        for tile in range(tiles):
+            col, count = plan.columns("last", tile)
+            ends += blocks(tile * edge + col - left, tile * edge + col + count + left)
+        gap, gap_rows = first_made + left, made - 2 * left
+
+        def outside(index, left=left, gap=gap, gap_rows=gap_rows):
+            row = W - left + index
+            return row + jnp.where(row < gap, 0, gap_rows)
+
+        march(edge + 2 * left - gap_rows, outside, whole, source, target, any_zone)
+        march(gap_rows, lambda i, gap=gap: gap + i, sorted(set(ends)), source, target, own_zone)
     done = pairs[NSTEPS % 2]
-    mine = lax.rem(lax.axis_index("gy"), half)
     for index, far_out in enumerate(far_outs):
         pack(plan, True, mine ^ (half // 2 + index), done, W, PAD + W, own, far_out)
     for piece in range(half):
@@ -415,21 +443,22 @@
 
 def settle_kernel(plan, table, near, *refs):
     tiles, half = plan.tiles, plan.half
-    far, outs = refs[:half], refs[half:]
+    far, outs, (ready, sems) = refs[:half], refs[half : half + 2], refs[half + 2 :]
     me = lax.axis_index("gy")
     mine = lax.rem(me, half)
+    copies = []
     for slot in range(tiles):
         home = table[me * tiles + slot]
         tile = lax.rem(home, tiles)
         at_home = home // (tiles * half) == me // half
 
         def put(source, piece, is_far, slot=slot, tile=tile):
-            for field, out in enumerate(outs):
+            for field in range(2):
                 for at, row, name in plan.parts(is_far, piece):
                     col, count = plan.columns(name, tile)
                     if not isinstance(col, int):
                         col = pl.multiple_of(col, 8)
-                    out[0, slot, row, pl.ds(col, count), :] = source[
+                    ready[field, slot, row, pl.ds(col, count), :] = source[
                         slot, field * plan.size + at : field * plan.size + at + count, :
                     ]
 
@@ -446,15 +475,27 @@
         def _(put_all=put_all):
             put_all(False)
 
+        for field, out in enumerate(outs):
+            copy = pltpu.make_async_copy(ready.at[field, slot], out.at[0, slot], sems.at[field, slot])
+            copy.start()
+            copies.append(copy)
+    for copy in copies:
+        copy.wait()
+
 
 def settle(plan, table, near, far):
-    out = jax.ShapeDtypeStruct((1, plan.tiles, plan.edge, plan.edge, plan.depth), jnp.float32)
+    tiles, edge, depth = plan.tiles, plan.edge, plan.depth
+    out = jax.ShapeDtypeStruct((1, tiles, edge, edge, depth), jnp.float32)
     vmem = pl.BlockSpec(memory_space=pltpu.VMEM)
     return pl.pallas_call(
         functools.partial(settle_kernel, plan),
         in_specs=[pl.BlockSpec(memory_space=pltpu.SMEM)] + [vmem] * (plan.half + 1),
-        out_specs=[vmem, vmem],
+        out_specs=[pl.BlockSpec(memory_space=pl.ANY)] * 2,
         out_shape=[out, out],
+        scratch_shapes=[
+            pltpu.VMEM((2, tiles, edge, edge, depth), jnp.float32),
+            pltpu.SemaphoreType.DMA((2, tiles)),
+        ],
         compiler_params=pltpu.CompilerParams(vmem_limit_bytes=16 * 1024 * 1024),
         name="settle",
     )(table, near, *far)

time: 117 us -> 117 us (level)
  Pallas kernels: 23 us -> 21.3 us
  waiting for transfers between devices: 12.1 us -> 13.3 us
  transfers between devices with their start and end apart: 12 -> 12, of which waited for: 5 -> 5; matrix products, arithmetic and copies ran while one was open for 0% -> 0% of each run, Pallas kernels for 14% -> 13%
where the time goes in v13:
time: 117 us; the launch traced here: 116 us
  blocking collectives  64.3 us (55%)
  Pallas kernels  21.3 us (18%)
  starting transfers between devices  15.7 us (13%)
  waiting for transfers between devices  13.3 us (11%)
    all_to_all x2, blocking collectives, exchange(): lax.all_to_all(values, 'gy', 0, 0, axis_index_groups=groups, tiled=True)  64.3 us
    pallas_call x1, Pallas kernels, run_outer(): pl.pallas_call(functools.partial(outer_kernel, plan), in_specs=[vmem] * 7...  11.1 us
    ppermute x8, starting transfers between devices, swap(): lax.ppermute(values, 'gy', [(i, i ^ mask) for i in range(lax.axis_size('g...  11 us
    ppermute x8, waiting for transfers between devices, swap(): lax.ppermute(values, 'gy', [(i, i ^ mask) for i in range(lax.axis_size('g...  7.66 us
    pallas_call x1, Pallas kernels, run_inner(): pl.pallas_call(functools.partial(inner_kernel, plan), in_specs=[vmem] * 3...  4.01 us
    ppermute x1, waiting for transfers between devices, per_device(): x_lo = lax.ppermute(to_next, 'gx', ring('gx', 1))  3.07 us
  transfers between devices with their start and end apart: 12, of which 5 were waited for; matrix products, arithmetic and copies ran while one was open for 0% of the time, Pallas kernels for 13%

profile of v13, /device:TPU:8, one launch (start us, length us, event | category | flops | bytes accessed | tf_op | source)
XLA Modules:
  0.0 116.1 jit_solution(3929680873993192754)
XLA Ops:
  0.6 0.0 copy-start.1
  0.6 0.0 copy-start
  0.7 2.0 %pack_y.1 = (f32[33,8,128]{2,1,0:T(8,128)}, f32[33,8,128]{2,1,0:T(8,128)}, f32[24,128]{1,0:T(8,128)}) custom-call(f32[1,2]{1,0:T(1,128)} %under.1, f32[1,2]{1,0:T(1,128)} %mobile.1, f32[1,2]{1,0:T(1,128)} %spread.1, s32[1,2]{1,0:T(1,128)} %owner.1, f32[1,2,32,32,128]{4,3,2,1,0:T(8,128)} %phase.3, f32[1,2,32,32,128]{4,3,2,1,0:T(8,128)} %phase.3, ...), custom_call_target="tpu_custom_call" | custom-call | tf_op jit(solution)/shard_map/pack_y/pallas_call | solution.py:48
  2.7 1.5 %collective-permute-start = (f32[33,8,128]{2,1,0:T(8,128)}, f32[33,8,128]{2,1,0:T(8,128)S(1)}, u32[]{:S(2)}, u32[]{:S(2)}) collective-permute-start(f32[33,8,128]{2,1,0:T(8,128)} %get-tuple-element.29), channel_id=1, source_target_pairs={{0,1},{1,2},{2,3},{3,4},{4,5},{5,6},{6,7},{7,0},{8,9},{9,10},{10,1... | collective-permute-start | bytes 405512 | tf_op jit(solution)/shard_map/ppermute | solution.py:526
  4.2 1.4 %collective-permute-start.1 = (f32[33,8,128]{2,1,0:T(8,128)}, f32[33,8,128]{2,1,0:T(8,128)S(1)}, u32[]{:S(2)}, u32[]{:S(2)}) collective-permute-start(f32[33,8,128]{2,1,0:T(8,128)} %get-tuple-element.30), channel_id=1, source_target_pairs={{0,7},{1,0},{2,1},{3,2},{4,3},{5,4},{6,5},{7,6},{8,15},{9,8},{10,9... | collective-permute-start | bytes 405512 | tf_op jit(solution)/shard_map/ppermute | solution.py:527
  5.6 0.0 copy-done.1
  5.6 0.0 copy-done
  5.6 0.0 copy-start.2
  5.6 0.7 copy-done.2
  6.3 4.0 %inner.1 = (f32[520,128]{1,0:T(8,128)S(1)}, f32[520,128]{1,0:T(8,128)S(1)}) custom-call(f32[24,128]{1,0:T(8,128)S(1)} %copy-done.2, f32[1,2,32,32,128]{4,3,2,1,0:T(8,128)S(1)} %copy-done, f32[1,2,32,32,128]{4,3,2,1,0:T(8,128)S(1)} %copy-done.1), custom_call_target="tpu_custom_call" | custom-call | flops 100000000 | bytes 25165824 | tf_op jit(solution)/shard_map/inner/pallas_call | solution.py:274
  10.3 0.0 collective-permute-done.y_lo
  10.3 1.7 %collective-permute-done.1.y_hi = f32[33,8,128]{2,1,0:T(8,128)S(1)} collective-permute-done((f32[33,8,128]{2,1,0:T(8,128)}, f32[33,8,128]{2,1,0:T(8,128)S(1)}, u32[]{:S(2)}, u32[]{:S(2)}) %collective-permute-start.1) | collective-permute-done | bytes 135200 | tf_op jit(solution)/shard_map/ppermute | solution.py:527
  12.0 0.0 copy-start.3
  12.0 0.1 collective-permute-start.2
  12.1 1.7 %collective-permute-start.3 = (f32[608,128]{1,0:T(8,128)S(1)}, f32[608,128]{1,0:T(8,128)S(1)}, u32[]{:S(2)}, u32[]{:S(2)}) collective-permute-start(f32[608,128]{1,0:T(8,128)S(1)} %get-tuple-element.33), channel_id=1, source_target_pairs={{0,24},{8,0},{16,8},{24,16},{1,25},{9,1},{17,9},{25,17},{2,26},{10... | collective-permute-start | bytes 933896 | tf_op jit(solution)/shard_map/ppermute | solution.py:532
  13.8 2.6 %collective-permute-start.4 = (f32[520,128]{1,0:T(8,128)S(1)}, f32[520,128]{1,0:T(8,128)S(1)}, u32[]{:S(2)}, u32[]{:S(2)}) collective-permute-start(f32[520,128]{1,0:T(8,128)S(1)} %get-tuple-element.31._), channel_id=1, source_target_pairs={{0,4},{1,5},{2,6},{3,7},{4,0},{5,1},{6,2},{7,3},{8,12},{9,13},{10,... | collective-permute-start | bytes 798728 | tf_op jit(solution)/shard_map/ppermute | solution.py:510
  16.4 0.0 copy-start.4
  16.4 0.4 collective-permute-start.5
  16.8 3.1 %collective-permute-done.2.x_lo = f32[608,128]{1,0:T(8,128)S(1)} collective-permute-done((f32[608,128]{1,0:T(8,128)S(1)}, f32[608,128]{1,0:T(8,128)S(1)}, u32[]{:S(2)}, u32[]{:S(2)}) %collective-permute-start.2) | collective-permute-done | bytes 311328 | tf_op jit(solution)/shard_map/ppermute | solution.py:531
  19.9 0.9 collective-permute-done.3.x_hi
  20.8 0.0 copy-done.3
  20.8 11.1 %outer.1 = (f32[4,520,128]{2,1,0:T(8,128)S(1)}, f32[520,128]{1,0:T(8,128)}, f32[520,128]{1,0:T(8,128)S(1)}) custom-call(f32[24,128]{1,0:T(8,128)S(1)} %copy-done.3, f32[1,2,32,32,128]{4,3,2,1,0:T(8,128)S(1)} %copy-done, f32[1,2,32,32,128]{4,3,2,1,0:T(8,128)S(1)} %copy-done.1, f32[33,8,128]{2,1,0:T(8,128)S(1)} %collective-permute-done.y_lo, ...), custom_call_target="tpu_custom_call" | custom-call | flops 100000000 | bytes 41943040 | tf_op jit(solution)/shard_map/outer/pallas_call | solution.py:376
  31.8 1.7 %collective-permute-start.6 = (f32[520,128]{1,0:T(8,128)}, f32[520,128]{1,0:T(8,128)S(1)}, u32[]{:S(2)}, u32[]{:S(2)}) collective-permute-start(f32[520,128]{1,0:T(8,128)} %get-tuple-element.36), channel_id=1, source_target_pairs={{0,6},{1,7},{2,4},{3,5},{4,2},{5,3},{6,0},{7,1},{8,14},{9,15},{10,... | collective-permute-start | bytes 798728 | tf_op jit(solution)/shard_map/ppermute | solution.py:510
  33.6 0.4 collective-permute-start.7
  33.9 0.0 copy-done.4
  34.0 27.3 %conditional.2 = (f32[4,520,128]{2,1,0:T(8,128)}) conditional(s32[]{:T(128)} %bitcast, f32[4,520,128]{2,1,0:T(8,128)S(1)} %get-tuple-element.34, f32[4,520,128]{2,1,0:T(8,128)S(1)} %get-tuple-element.34), branch_computations={%region_0.0_spmd, %region_1.0_spmd} | conditional | bytes 2129928 | solution.py:518
  34.0 27.3 %all_to_all.17 = f32[4,520,128]{2,1,0:T(8,128)} all-to-all(f32[4,520,128]{2,1,0:T(8,128)S(1)} %param.1), channel_id=1, replica_groups={{0,1,2,3},{4,5,6,7},{8,9,10,11},{12,13,14,15},{16,17,18,19},{20,21,22,2..., dimensions={0} | all-to-all | bytes 2129920 | tf_op jit(solution)/shard_map/cond/branch_1_fun/all_to_all | solution.py:516
  61.3 0.0 collective-permute-done.5.refs_1_
  61.3 0.0 collective-permute-done.4.refs_0_
  61.3 0.0 collective-permute-done.6.refs_2_
  61.3 2.1 %collective-permute-done.7.refs_3_ = f32[520,128]{1,0:T(8,128)S(1)} collective-permute-done((f32[520,128]{1,0:T(8,128)S(1)}, f32[520,128]{1,0:T(8,128)S(1)}, u32[]{:S(2)}, u32[]{:S(2)}) %collective-permute-start.7) | collective-permute-done | bytes 266272 | tf_op jit(solution)/shard_map/ppermute | solution.py:510
  63.4 2.2 %route.1 = (f32[4,2,256,128]{3,2,1,0:T(8,128)S(1)}, f32[2,256,128]{2,1,0:T(8,128)S(1)}, f32[2,256,128]{2,1,0:T(8,128)S(1)}, f32[2,256,128]{2,1,0:T(8,128)S(1)}, ...) custom-call(f32[4,520,128]{2,1,0:T(8,128)} %get-tuple-element.44.near, f32[520,128]{1,0:T(8,128)S(1)} %collective-permute-done.4.refs_0_, ...), custom_call_target="tpu_custom_call" | custom-call | tf_op jit(solution)/shard_map/route/pallas_call | solution.py:426
  65.6 2.1 %collective-permute-start.8 = (f32[2,256,128]{2,1,0:T(8,128)S(1)}, f32[2,256,128]{2,1,0:T(8,128)S(1)}, u32[]{:S(2)}, u32[]{:S(2)}) collective-permute-start(f32[2,256,128]{2,1,0:T(8,128)S(1)} %get-tuple-element.40), channel_id=1, source_target_pairs={{0,4},{1,5},{2,6},{3,7},{4,0},{5,1},{6,2},{7,3},{8,12},{9,13},{10,... | collective-permute-start | bytes 786440 | tf_op jit(solution)/shard_map/ppermute | solution.py:510
  67.8 2.0 %collective-permute-start.9 = (f32[2,256,128]{2,1,0:T(8,128)S(1)}, f32[2,256,128]{2,1,0:T(8,128)S(1)}, u32[]{:S(2)}, u32[]{:S(2)}) collective-permute-start(f32[2,256,128]{2,1,0:T(8,128)S(1)} %get-tuple-element.41), channel_id=1, source_target_pairs={{0,5},{1,4},{2,7},{3,6},{4,1},{5,0},{6,3},{7,2},{8,13},{9,12},{10,... | collective-permute-start | bytes 786440 | tf_op jit(solution)/shard_map/ppermute | solution.py:510
  69.8 1.4 %collective-permute-start.10 = (f32[2,256,128]{2,1,0:T(8,128)S(1)}, f32[2,256,128]{2,1,0:T(8,128)S(1)}, u32[]{:S(2)}, u32[]{:S(2)}) collective-permute-start(f32[2,256,128]{2,1,0:T(8,128)S(1)} %get-tuple-element.42), channel_id=1, source_target_pairs={{0,6},{1,7},{2,4},{3,5},{4,2},{5,3},{6,0},{7,1},{8,14},{9,15},{10,... | collective-permute-start | bytes 786440 | tf_op jit(solution)/shard_map/ppermute | solution.py:510
  71.2 0.4 collective-permute-start.11
  71.5 37.0 %conditional.3 = (f32[4,2,256,128]{3,2,1,0:T(8,128)S(1)}) conditional(s32[]{:T(128)} %bitcast, f32[4,2,256,128]{3,2,1,0:T(8,128)S(1)} %get-tuple-element.39, f32[4,2,256,128]{3,2,1,0:T(8,128)S(1)} %get-tuple-element.39), branch_computations={%region_2.0_spmd, %region_3.0_spmd} | conditional | bytes 2097160 | solution.py:518
  71.5 37.0 %all_to_all.19 = f32[4,2,256,128]{3,2,1,0:T(8,128)S(1)} all-to-all(f32[4,2,256,128]{3,2,1,0:T(8,128)S(1)} %param.3), channel_id=1, replica_groups={{0,1,2,3},{4,5,6,7},{8,9,10,11},{12,13,14,15},{16,17,18,19},{20,21,22,2..., dimensions={0} | all-to-all | bytes 2097152 | tf_op jit(solution)/shard_map/cond/branch_1_fun/all_to_all | solution.py:516
  108.5 0.0 collective-permute-done.8.refs_0_
  108.5 0.0 collective-permute-done.9.refs_1_
  108.6 0.0 collective-permute-done.10.refs_2_
  108.6 5.5 %collective-permute-done.11.refs_3_ = f32[2,256,128]{2,1,0:T(8,128)S(1)} collective-permute-done((f32[2,256,128]{2,1,0:T(8,128)S(1)}, f32[2,256,128]{2,1,0:T(8,128)S(1)}, u32[]{:S(2)}, u32[]{:S(2)}) %collective-permute-start.11) | collective-permute-done | bytes 262176 | tf_op jit(solution)/shard_map/ppermute | solution.py:510
  114.1 2.0 %settle.1 = (f32[1,2,32,32,128]{4,3,2,1,0:T(8,128)}, f32[1,2,32,32,128]{4,3,2,1,0:T(8,128)}) custom-call(s32[16]{0:T(128)S(1)} %get-tuple-element.38.table, f32[4,2,256,128]{3,2,1,0:T(8,128)S(1)} %get-tuple-element.45.near, f32[2,256,128]{2,1,0:T(8,128)S(1)} %collective-permute-done.8.refs_0_, f32[2,256,128]{2,1,0:T(8,128)S(1)} %collective-permute-done.9.refs_1_, ...), custom_call_target="tpu_custom_call" | custom-call | tf_op jit(solution)/shard_map/settle/pallas_call | solution.py:490
  (1 shorter events, 0.0 us)
Async XLA Ops:
  0.6 5.0 %copy-start.1 = (f32[1,2,32,32,128]{4,3,2,1,0:T(8,128)S(1)}, f32[1,2,32,32,128]{4,3,2,1,0:T(8,128)}, u32[]{:S(2)}) copy-start(f32[1,2,32,32,128]{4,3,2,1,0:T(8,128)} %solute.3) | copy-start | bytes 3145732
  0.6 5.0 %copy-start = (f32[1,2,32,32,128]{4,3,2,1,0:T(8,128)S(1)}, f32[1,2,32,32,128]{4,3,2,1,0:T(8,128)}, u32[]{:S(2)}) copy-start(f32[1,2,32,32,128]{4,3,2,1,0:T(8,128)} %phase.3) | copy-start | bytes 3145732
  2.7 7.7 %collective-permute-start = (f32[33,8,128]{2,1,0:T(8,128)}, f32[33,8,128]{2,1,0:T(8,128)S(1)}, u32[]{:S(2)}, u32[]{:S(2)}) collective-permute-start(f32[33,8,128]{2,1,0:T(8,128)} %get-tuple-element.29), channel_id=1, source_target_pairs={{0,1},{1,2},{2,3},{3,4},{4,5},{5,6},{6,7},{7,0},{8,9},{9,10},{10,1... | collective-permute-start | bytes 405512 | tf_op jit(solution)/shard_map/ppermute | solution.py:526
  4.2 7.8 %collective-permute-start.1 = (f32[33,8,128]{2,1,0:T(8,128)}, f32[33,8,128]{2,1,0:T(8,128)S(1)}, u32[]{:S(2)}, u32[]{:S(2)}) collective-permute-start(f32[33,8,128]{2,1,0:T(8,128)} %get-tuple-element.30), channel_id=1, source_target_pairs={{0,7},{1,0},{2,1},{3,2},{4,3},{5,4},{6,5},{7,6},{8,15},{9,8},{10,9... | collective-permute-start | bytes 405512 | tf_op jit(solution)/shard_map/ppermute | solution.py:527
  5.6 0.7 copy-start.2
  12.0 8.8 %copy-start.3 = (f32[24,128]{1,0:T(8,128)S(1)}, f32[24,128]{1,0:T(8,128)}, u32[]{:S(2)}) copy-start(f32[24,128]{1,0:T(8,128)} %get-tuple-element.28.own) | copy-start | bytes 36868
  12.0 7.9 %collective-permute-start.2 = (f32[608,128]{1,0:T(8,128)S(1)}, f32[608,128]{1,0:T(8,128)S(1)}, u32[]{:S(2)}, u32[]{:S(2)}) collective-permute-start(f32[608,128]{1,0:T(8,128)S(1)} %get-tuple-element.32), channel_id=1, source_target_pairs={{0,8},{8,16},{16,24},{24,0},{1,9},{9,17},{17,25},{25,1},{2,10},{10... | collective-permute-start | bytes 933896 | tf_op jit(solution)/shard_map/ppermute | solution.py:531
  12.1 8.7 %collective-permute-start.3 = (f32[608,128]{1,0:T(8,128)S(1)}, f32[608,128]{1,0:T(8,128)S(1)}, u32[]{:S(2)}, u32[]{:S(2)}) collective-permute-start(f32[608,128]{1,0:T(8,128)S(1)} %get-tuple-element.33), channel_id=1, source_target_pairs={{0,24},{8,0},{16,8},{24,16},{1,25},{9,1},{17,9},{25,17},{2,26},{10... | collective-permute-start | bytes 933896 | tf_op jit(solution)/shard_map/ppermute | solution.py:532
  13.8 47.4 %collective-permute-start.4 = (f32[520,128]{1,0:T(8,128)S(1)}, f32[520,128]{1,0:T(8,128)S(1)}, u32[]{:S(2)}, u32[]{:S(2)}) collective-permute-start(f32[520,128]{1,0:T(8,128)S(1)} %get-tuple-element.31._), channel_id=1, source_target_pairs={{0,4},{1,5},{2,6},{3,7},{4,0},{5,1},{6,2},{7,3},{8,12},{9,13},{10,... | collective-permute-start | bytes 798728 | tf_op jit(solution)/shard_map/ppermute | solution.py:510
  16.4 17.5 %copy-start.4 = (s32[1,2]{1,0:T(1,128)S(1)}, s32[1,2]{1,0:T(1,128)}, u32[]{:S(2)}) copy-start(s32[1,2]{1,0:T(1,128)} %owner.1) | copy-start | bytes 28
  16.4 44.8 %collective-permute-start.5 = (f32[520,128]{1,0:T(8,128)S(1)}, f32[520,128]{1,0:T(8,128)S(1)}, u32[]{:S(2)}, u32[]{:S(2)}) collective-permute-start(f32[520,128]{1,0:T(8,128)S(1)} %get-tuple-element.35), channel_id=1, source_target_pairs={{0,5},{1,4},{2,7},{3,6},{4,1},{5,0},{6,3},{7,2},{8,13},{9,12},{10,... | collective-permute-start | bytes 798728 | tf_op jit(solution)/shard_map/ppermute | solution.py:510
  31.8 29.5 %collective-permute-start.6 = (f32[520,128]{1,0:T(8,128)}, f32[520,128]{1,0:T(8,128)S(1)}, u32[]{:S(2)}, u32[]{:S(2)}) collective-permute-start(f32[520,128]{1,0:T(8,128)} %get-tuple-element.36), channel_id=1, source_target_pairs={{0,6},{1,7},{2,4},{3,5},{4,2},{5,3},{6,0},{7,1},{8,14},{9,15},{10,... | collective-permute-start | bytes 798728 | tf_op jit(solution)/shard_map/ppermute | solution.py:510
  33.6 29.9 %collective-permute-start.7 = (f32[520,128]{1,0:T(8,128)S(1)}, f32[520,128]{1,0:T(8,128)S(1)}, u32[]{:S(2)}, u32[]{:S(2)}) collective-permute-start(f32[520,128]{1,0:T(8,128)S(1)} %get-tuple-element.37), channel_id=1, source_target_pairs={{0,7},{1,6},{2,5},{3,4},{4,3},{5,2},{6,1},{7,0},{8,15},{9,14},{10,... | collective-permute-start | bytes 798728 | tf_op jit(solution)/shard_map/ppermute | solution.py:510
  65.6 42.9 %collective-permute-start.8 = (f32[2,256,128]{2,1,0:T(8,128)S(1)}, f32[2,256,128]{2,1,0:T(8,128)S(1)}, u32[]{:S(2)}, u32[]{:S(2)}) collective-permute-start(f32[2,256,128]{2,1,0:T(8,128)S(1)} %get-tuple-element.40), channel_id=1, source_target_pairs={{0,4},{1,5},{2,6},{3,7},{4,0},{5,1},{6,2},{7,3},{8,12},{9,13},{10,... | collective-permute-start | bytes 786440 | tf_op jit(solution)/shard_map/ppermute | solution.py:510
  67.8 40.8 %collective-permute-start.9 = (f32[2,256,128]{2,1,0:T(8,128)S(1)}, f32[2,256,128]{2,1,0:T(8,128)S(1)}, u32[]{:S(2)}, u32[]{:S(2)}) collective-permute-start(f32[2,256,128]{2,1,0:T(8,128)S(1)} %get-tuple-element.41), channel_id=1, source_target_pairs={{0,5},{1,4},{2,7},{3,6},{4,1},{5,0},{6,3},{7,2},{8,13},{9,12},{10,... | collective-permute-start | bytes 786440 | tf_op jit(solution)/shard_map/ppermute | solution.py:510
  69.8 38.7 %collective-permute-start.10 = (f32[2,256,128]{2,1,0:T(8,128)S(1)}, f32[2,256,128]{2,1,0:T(8,128)S(1)}, u32[]{:S(2)}, u32[]{:S(2)}) collective-permute-start(f32[2,256,128]{2,1,0:T(8,128)S(1)} %get-tuple-element.42), channel_id=1, source_target_pairs={{0,6},{1,7},{2,4},{3,5},{4,2},{5,3},{6,0},{7,1},{8,14},{9,15},{10,... | collective-permute-start | bytes 786440 | tf_op jit(solution)/shard_map/ppermute | solution.py:510
  71.2 42.9 %collective-permute-start.11 = (f32[2,256,128]{2,1,0:T(8,128)S(1)}, f32[2,256,128]{2,1,0:T(8,128)S(1)}, u32[]{:S(2)}, u32[]{:S(2)}) collective-permute-start(f32[2,256,128]{2,1,0:T(8,128)S(1)} %get-tuple-element.43), channel_id=1, source_target_pairs={{0,7},{1,6},{2,5},{3,4},{4,3},{5,2},{6,1},{7,0},{8,15},{9,14},{10,... | collective-permute-start | bytes 786440 | tf_op jit(solution)/shard_map/ppermute | solution.py:510

commit v14 on v13

--- a/solution.py
+++ b/solution.py
@@ -528,11 +528,14 @@
     first = run_inner(plan, own, phase, solute)
     far = [swap(values, half + index) for index, values in enumerate(first)]
     to_prev, to_next = pack_x(phase, solute, own, y_lo, y_hi, first[0])
-    x_lo = lax.ppermute(to_next, "gx", ring("gx", 1))
-    x_hi = lax.ppermute(to_prev, "gx", ring("gx", -1))
+    together = owner[0, 0] >= 0
+
+    def around(low, high):
+        return lax.ppermute(low, "gx", ring("gx", 1)), lax.ppermute(high, "gx", ring("gx", -1))
+
+    x_lo, x_hi = lax.cond(together, around, around, to_next, to_prev)
     near, *second = run_outer(plan, own, phase, solute, (y_lo, y_hi, x_lo, x_hi))
     far += [swap(values, half + half // 2 + index) for index, values in enumerate(second)]
-    together = owner[0, 0] >= 0
     near = among_half(plan, near, together)
     near, far, table = route(plan, near, far)
     far = [swap(values, half + index) for index, values in enumerate(far)]

time: 117 us -> 116 us (level)
    ppermute x2, waiting for transfers between devices: 3.93 us -> 6.92 us  [the longest x1 6.16 us: around(): lax.ppermute(low, 'gx', ring('gx', 1))]
    ppermute x8, waiting for transfers between devices: 7.66 us -> 5.6 us  [swap(): lax.ppermute(values, 'gy', [(i, i ^ mask) for i in range(lax.axis_size('g...]
    ppermute x1, waiting for transfers between devices: 1.67 us -> 0.01 us  [per_device(): y_hi = lax.ppermute(to_prev, 'gy', ring('gy', -1))]
    pallas_call x1, Pallas kernels: 2.19 us -> 0.89 us  [route(): pl.pallas_call(functools.partial(route_kernel, plan), in_specs=[vmem] * (...]
  transfers between devices with their start and end apart: 12 -> 12, of which waited for: 5 -> 5; matrix products, arithmetic and copies ran while one was open for 0% -> 0% of each run, Pallas kernels for 13% -> 14%
where the time goes in v14:
time: 116 us
  blocking collectives  64.4 us (56%)
  Pallas kernels  21.1 us (18%)
  starting transfers between devices  16.5 us (14%)
  waiting for transfers between devices  12.5 us (11%)
    all_to_all x2, blocking collectives, exchange(): lax.all_to_all(values, 'gy', 0, 0, axis_index_groups=groups, tiled=True)  64.4 us
    pallas_call x1, Pallas kernels, run_outer(): pl.pallas_call(functools.partial(outer_kernel, plan), in_specs=[vmem] * 7...  12.2 us
    ppermute x8, starting transfers between devices, swap(): lax.ppermute(values, 'gy', [(i, i ^ mask) for i in range(lax.axis_size('g...  11.8 us
    ppermute x1, waiting for transfers between devices, around(): lax.ppermute(low, 'gx', ring('gx', 1))  6.16 us
    ppermute x8, waiting for transfers between devices, swap(): lax.ppermute(values, 'gy', [(i, i ^ mask) for i in range(lax.axis_size('g...  5.6 us
    pallas_call x1, Pallas kernels, run_inner(): pl.pallas_call(functools.partial(inner_kernel, plan), in_specs=[vmem] * 3...  3.97 us
  transfers between devices with their start and end apart: 12, of which 5 were waited for; matrix products, arithmetic and copies ran while one was open for 0% of the time, Pallas kernels for 14%

profile of v14, /device:TPU:8, one launch (start us, length us, event | category | flops | bytes accessed | tf_op | source)
XLA Modules:
  0.0 116.1 jit_solution(15274930243594091453)
XLA Ops:
  0.6 0.0 copy-start.1
  0.6 0.0 copy-start
  0.7 2.0 %pack_y.1 = (f32[33,8,128]{2,1,0:T(8,128)}, f32[33,8,128]{2,1,0:T(8,128)}, f32[24,128]{1,0:T(8,128)}) custom-call(f32[1,2]{1,0:T(1,128)} %under.1, f32[1,2]{1,0:T(1,128)} %mobile.1, f32[1,2]{1,0:T(1,128)} %spread.1, s32[1,2]{1,0:T(1,128)} %owner.1, f32[1,2,32,32,128]{4,3,2,1,0:T(8,128)} %phase.3, f32[1,2,32,32,128]{4,3,2,1,0:T(8,128)} %phase.3, ...), custom_call_target="tpu_custom_call" | custom-call | tf_op jit(solution)/shard_map/pack_y/pallas_call | solution.py:48
  2.7 0.0 copy-start.4
  2.7 1.5 %collective-permute-start.4 = (f32[33,8,128]{2,1,0:T(8,128)}, f32[33,8,128]{2,1,0:T(8,128)S(1)}, u32[]{:S(2)}, u32[]{:S(2)}) collective-permute-start(f32[33,8,128]{2,1,0:T(8,128)} %get-tuple-element.43), channel_id=1, source_target_pairs={{0,1},{1,2},{2,3},{3,4},{4,5},{5,6},{6,7},{7,0},{8,9},{9,10},{10,1... | collective-permute-start | bytes 405512 | tf_op jit(solution)/shard_map/ppermute | solution.py:526
  4.2 1.4 %collective-permute-start.5 = (f32[33,8,128]{2,1,0:T(8,128)}, f32[33,8,128]{2,1,0:T(8,128)S(1)}, u32[]{:S(2)}, u32[]{:S(2)}) collective-permute-start(f32[33,8,128]{2,1,0:T(8,128)} %get-tuple-element.44), channel_id=1, source_target_pairs={{0,7},{1,0},{2,1},{3,2},{4,3},{5,4},{6,5},{7,6},{8,15},{9,8},{10,9... | collective-permute-start | bytes 405512 | tf_op jit(solution)/shard_map/ppermute | solution.py:527
  5.6 0.0 copy-done.1
  5.6 0.0 copy-done
  5.6 0.0 copy-start.2
  5.6 0.7 copy-done.2
  6.3 4.0 %inner.1 = (f32[520,128]{1,0:T(8,128)S(1)}, f32[520,128]{1,0:T(8,128)S(1)}) custom-call(f32[24,128]{1,0:T(8,128)S(1)} %copy-done.2, f32[1,2,32,32,128]{4,3,2,1,0:T(8,128)S(1)} %copy-done, f32[1,2,32,32,128]{4,3,2,1,0:T(8,128)S(1)} %copy-done.1), custom_call_target="tpu_custom_call" | custom-call | flops 100000000 | bytes 25165824 | tf_op jit(solution)/shard_map/inner/pallas_call | solution.py:274
  10.3 2.7 %collective-permute-start.7 = (f32[520,128]{1,0:T(8,128)S(1)}, f32[520,128]{1,0:T(8,128)S(1)}, u32[]{:S(2)}, u32[]{:S(2)}) collective-permute-start(f32[520,128]{1,0:T(8,128)S(1)} %get-tuple-element.51), channel_id=1, source_target_pairs={{0,5},{1,4},{2,7},{3,6},{4,1},{5,0},{6,3},{7,2},{8,13},{9,12},{10,... | collective-permute-start | bytes 798728 | tf_op jit(solution)/shard_map/ppermute | solution.py:510
  13.0 0.3 collective-permute-start.6
  13.3 0.0 copy-done.4
  13.4 0.0 copy-start.3
  13.4 0.0 collective-permute-done.4.y_lo
  13.4 0.0 collective-permute-done.5.y_hi
  13.5 8.7 %conditional.3 = (f32[608,128]{1,0:T(8,128)}, f32[608,128]{1,0:T(8,128)}) conditional(s32[]{:T(128)} %bitcast, (f32[608,128]{1,0:T(8,128)S(1)}, f32[608,128]{1,0:T(8,128)S(1)}) %tuple.27, (f32[608,128]{1,0:T(8,128)S(1)}, f32[608,128]{1,0:T(8,128)S(1)}) %tuple.27), branch_computations={%region_0.0_spmd, %region_1.0_spmd} | conditional | bytes 2490464 | solution.py:536
  13.5 0.1 collective-permute-start.2
  13.6 1.7 %collective-permute-start.3 = (f32[608,128]{1,0:T(8,128)S(1)}, f32[608,128]{1,0:T(8,128)}, u32[]{:S(2)}, u32[]{:S(2)}) collective-permute-start(f32[608,128]{1,0:T(8,128)S(1)} %get-tuple-element.21), channel_id=1, source_target_pairs={{0,24},{8,0},{16,8},{24,16},{1,25},{9,1},{17,9},{25,17},{2,26},{10... | collective-permute-start | bytes 933896 | tf_op jit(solution)/shard_map/cond/branch_1_fun/ppermute | solution.py:534
  15.3 6.2 %collective-permute-done.2 = f32[608,128]{1,0:T(8,128)} collective-permute-done((f32[608,128]{1,0:T(8,128)S(1)}, f32[608,128]{1,0:T(8,128)}, u32[]{:S(2)}, u32[]{:S(2)}) %collective-permute-start.2) | collective-permute-done | bytes 311328 | tf_op jit(solution)/shard_map/cond/branch_1_fun/ppermute | solution.py:534
  21.4 0.8 collective-permute-done.3
  22.2 0.0 copy-done.3
  22.2 12.2 %outer.1 = (f32[4,520,128]{2,1,0:T(8,128)S(1)}, f32[520,128]{1,0:T(8,128)}, f32[520,128]{1,0:T(8,128)}) custom-call(f32[24,128]{1,0:T(8,128)S(1)} %copy-done.3, f32[1,2,32,32,128]{4,3,2,1,0:T(8,128)S(1)} %copy-done, f32[1,2,32,32,128]{4,3,2,1,0:T(8,128)S(1)} %copy-done.1, f32[33,8,128]{2,1,0:T(8,128)S(1)} %collective-permute-done.4.y_lo, ...), custom_call_target="tpu_custom_call" | custom-call | flops 100000000 | bytes 41943040 | tf_op jit(solution)/shard_map/outer/pallas_call | solution.py:376
  34.4 1.7 %collective-permute-start.8 = (f32[520,128]{1,0:T(8,128)}, f32[520,128]{1,0:T(8,128)S(1)}, u32[]{:S(2)}, u32[]{:S(2)}) collective-permute-start(f32[520,128]{1,0:T(8,128)} %get-tuple-element.52), channel_id=1, source_target_pairs={{0,6},{1,7},{2,4},{3,5},{4,2},{5,3},{6,0},{7,1},{8,14},{9,15},{10,... | collective-permute-start | bytes 798728 | tf_op jit(solution)/shard_map/ppermute | solution.py:510
  36.2 1.1 collective-permute-start.9
  37.3 27.7 %conditional.4 = (f32[4,520,128]{2,1,0:T(8,128)S(1)}) conditional(s32[]{:T(128)} %bitcast, f32[4,520,128]{2,1,0:T(8,128)S(1)} %get-tuple-element.50, f32[4,520,128]{2,1,0:T(8,128)S(1)} %get-tuple-element.50), branch_computations={%region_2.0_spmd, %region_3.0_spmd} | conditional | bytes 2129928 | solution.py:518
  37.3 27.7 %all_to_all.17 = f32[4,520,128]{2,1,0:T(8,128)S(1)} all-to-all(f32[4,520,128]{2,1,0:T(8,128)S(1)} %param.3), channel_id=1, replica_groups={{0,1,2,3},{4,5,6,7},{8,9,10,11},{12,13,14,15},{16,17,18,19},{20,21,22,2..., dimensions={0} | all-to-all | bytes 2129920 | tf_op jit(solution)/shard_map/cond/branch_1_fun/all_to_all | solution.py:516
  65.0 0.0 collective-permute-done.7.refs_1_
  65.0 0.0 collective-permute-done.6.refs_0_
  65.0 0.0 collective-permute-done.8.refs_2_
  65.0 0.3 collective-permute-done.9.refs_3_
  65.3 0.9 route.1
  66.2 1.1 collective-permute-start.10
  67.3 2.0 %collective-permute-start.11 = (f32[2,256,128]{2,1,0:T(8,128)S(1)}, f32[2,256,128]{2,1,0:T(8,128)S(1)}, u32[]{:S(2)}, u32[]{:S(2)}) collective-permute-start(f32[2,256,128]{2,1,0:T(8,128)S(1)} %get-tuple-element.57), channel_id=1, source_target_pairs={{0,5},{1,4},{2,7},{3,6},{4,1},{5,0},{6,3},{7,2},{8,13},{9,12},{10,... | collective-permute-start | bytes 786440 | tf_op jit(solution)/shard_map/ppermute | solution.py:510
  69.3 0.8 collective-permute-start.12
  70.1 2.0 %collective-permute-start.13 = (f32[2,256,128]{2,1,0:T(8,128)S(1)}, f32[2,256,128]{2,1,0:T(8,128)S(1)}, u32[]{:S(2)}, u32[]{:S(2)}) collective-permute-start(f32[2,256,128]{2,1,0:T(8,128)S(1)} %get-tuple-element.59), channel_id=1, source_target_pairs={{0,7},{1,6},{2,5},{3,4},{4,3},{5,2},{6,1},{7,0},{8,15},{9,14},{10,... | collective-permute-start | bytes 786440 | tf_op jit(solution)/shard_map/ppermute | solution.py:510
  72.1 36.6 %conditional.5 = (f32[4,2,256,128]{3,2,1,0:T(8,128)S(1)}) conditional(s32[]{:T(128)} %bitcast, f32[4,2,256,128]{3,2,1,0:T(8,128)S(1)} %get-tuple-element.55, f32[4,2,256,128]{3,2,1,0:T(8,128)S(1)} %get-tuple-element.55), branch_computations={%region_4.0_spmd, %region_5.0_spmd} | conditional | bytes 2097160 | solution.py:518
  72.1 36.6 %all_to_all.19 = f32[4,2,256,128]{3,2,1,0:T(8,128)S(1)} all-to-all(f32[4,2,256,128]{3,2,1,0:T(8,128)S(1)} %param.5), channel_id=1, replica_groups={{0,1,2,3},{4,5,6,7},{8,9,10,11},{12,13,14,15},{16,17,18,19},{20,21,22,2..., dimensions={0} | all-to-all | bytes 2097152 | tf_op jit(solution)/shard_map/cond/branch_1_fun/all_to_all | solution.py:516
  108.7 0.0 collective-permute-done.10.refs_0_
  108.7 0.0 collective-permute-done.11.refs_1_
  108.7 0.5 collective-permute-done.12.refs_2_
  109.2 4.9 %collective-permute-done.13.refs_3_ = f32[2,256,128]{2,1,0:T(8,128)S(1)} collective-permute-done((f32[2,256,128]{2,1,0:T(8,128)S(1)}, f32[2,256,128]{2,1,0:T(8,128)S(1)}, u32[]{:S(2)}, u32[]{:S(2)}) %collective-permute-start.13) | collective-permute-done | bytes 262176 | tf_op jit(solution)/shard_map/ppermute | solution.py:510
  114.1 2.0 %settle.1 = (f32[1,2,32,32,128]{4,3,2,1,0:T(8,128)}, f32[1,2,32,32,128]{4,3,2,1,0:T(8,128)}) custom-call(s32[16]{0:T(128)S(1)} %get-tuple-element.54.table, f32[4,2,256,128]{3,2,1,0:T(8,128)S(1)} %get-tuple-element.65.near, f32[2,256,128]{2,1,0:T(8,128)S(1)} %collective-permute-done.10.refs_0_, f32[2,256,128]{2,1,0:T(8,128)S(1)} %collective-permute-done.11.refs_1_, ...), custom_call_target="tpu_custom_call" | custom-call | tf_op jit(solution)/shard_map/settle/pallas_call | solution.py:490
  (1 shorter events, 0.0 us)
Async XLA Ops:
  0.6 5.0 %copy-start.1 = (f32[1,2,32,32,128]{4,3,2,1,0:T(8,128)S(1)}, f32[1,2,32,32,128]{4,3,2,1,0:T(8,128)}, u32[]{:S(2)}) copy-start(f32[1,2,32,32,128]{4,3,2,1,0:T(8,128)} %solute.3) | copy-start | bytes 3145732
  0.6 5.0 %copy-start = (f32[1,2,32,32,128]{4,3,2,1,0:T(8,128)S(1)}, f32[1,2,32,32,128]{4,3,2,1,0:T(8,128)}, u32[]{:S(2)}) copy-start(f32[1,2,32,32,128]{4,3,2,1,0:T(8,128)} %phase.3) | copy-start | bytes 3145732
  2.7 10.7 %copy-start.4 = (s32[1,2]{1,0:T(1,128)S(1)}, s32[1,2]{1,0:T(1,128)}, u32[]{:S(2)}) copy-start(s32[1,2]{1,0:T(1,128)} %owner.1) | copy-start | bytes 28
  2.7 10.7 %collective-permute-start.4 = (f32[33,8,128]{2,1,0:T(8,128)}, f32[33,8,128]{2,1,0:T(8,128)S(1)}, u32[]{:S(2)}, u32[]{:S(2)}) collective-permute-start(f32[33,8,128]{2,1,0:T(8,128)} %get-tuple-element.43), channel_id=1, source_target_pairs={{0,1},{1,2},{2,3},{3,4},{4,5},{5,6},{6,7},{7,0},{8,9},{9,10},{10,1... | collective-permute-start | bytes 405512 | tf_op jit(solution)/shard_map/ppermute | solution.py:526
  4.2 9.2 %collective-permute-start.5 = (f32[33,8,128]{2,1,0:T(8,128)}, f32[33,8,128]{2,1,0:T(8,128)S(1)}, u32[]{:S(2)}, u32[]{:S(2)}) collective-permute-start(f32[33,8,128]{2,1,0:T(8,128)} %get-tuple-element.44), channel_id=1, source_target_pairs={{0,7},{1,0},{2,1},{3,2},{4,3},{5,4},{6,5},{7,6},{8,15},{9,8},{10,9... | collective-permute-start | bytes 405512 | tf_op jit(solution)/shard_map/ppermute | solution.py:527
  5.6 0.7 copy-start.2
  10.3 54.7 %collective-permute-start.7 = (f32[520,128]{1,0:T(8,128)S(1)}, f32[520,128]{1,0:T(8,128)S(1)}, u32[]{:S(2)}, u32[]{:S(2)}) collective-permute-start(f32[520,128]{1,0:T(8,128)S(1)} %get-tuple-element.51), channel_id=1, source_target_pairs={{0,5},{1,4},{2,7},{3,6},{4,1},{5,0},{6,3},{7,2},{8,13},{9,12},{10,... | collective-permute-start | bytes 798728 | tf_op jit(solution)/shard_map/ppermute | solution.py:510
  13.0 52.0 %collective-permute-start.6 = (f32[520,128]{1,0:T(8,128)S(1)}, f32[520,128]{1,0:T(8,128)S(1)}, u32[]{:S(2)}, u32[]{:S(2)}) collective-permute-start(f32[520,128]{1,0:T(8,128)S(1)} %get-tuple-element.45._), channel_id=1, source_target_pairs={{0,4},{1,5},{2,6},{3,7},{4,0},{5,1},{6,2},{7,3},{8,12},{9,13},{10,... | collective-permute-start | bytes 798728 | tf_op jit(solution)/shard_map/ppermute | solution.py:510
  13.4 8.8 %copy-start.3 = (f32[24,128]{1,0:T(8,128)S(1)}, f32[24,128]{1,0:T(8,128)}, u32[]{:S(2)}) copy-start(f32[24,128]{1,0:T(8,128)} %get-tuple-element.42.own) | copy-start | bytes 36868
  13.5 8.0 %collective-permute-start.2 = (f32[608,128]{1,0:T(8,128)S(1)}, f32[608,128]{1,0:T(8,128)}, u32[]{:S(2)}, u32[]{:S(2)}) collective-permute-start(f32[608,128]{1,0:T(8,128)S(1)} %get-tuple-element.20), channel_id=1, source_target_pairs={{0,8},{8,16},{16,24},{24,0},{1,9},{9,17},{17,25},{25,1},{2,10},{10... | collective-permute-start | bytes 933896 | tf_op jit(solution)/shard_map/cond/branch_1_fun/ppermute | solution.py:534
  13.6 8.7 %collective-permute-start.3 = (f32[608,128]{1,0:T(8,128)S(1)}, f32[608,128]{1,0:T(8,128)}, u32[]{:S(2)}, u32[]{:S(2)}) collective-permute-start(f32[608,128]{1,0:T(8,128)S(1)} %get-tuple-element.21), channel_id=1, source_target_pairs={{0,24},{8,0},{16,8},{24,16},{1,25},{9,1},{17,9},{25,17},{2,26},{10... | collective-permute-start | bytes 933896 | tf_op jit(solution)/shard_map/cond/branch_1_fun/ppermute | solution.py:534
  34.4 30.6 %collective-permute-start.8 = (f32[520,128]{1,0:T(8,128)}, f32[520,128]{1,0:T(8,128)S(1)}, u32[]{:S(2)}, u32[]{:S(2)}) collective-permute-start(f32[520,128]{1,0:T(8,128)} %get-tuple-element.52), channel_id=1, source_target_pairs={{0,6},{1,7},{2,4},{3,5},{4,2},{5,3},{6,0},{7,1},{8,14},{9,15},{10,... | collective-permute-start | bytes 798728 | tf_op jit(solution)/shard_map/ppermute | solution.py:510
  36.2 29.1 %collective-permute-start.9 = (f32[520,128]{1,0:T(8,128)}, f32[520,128]{1,0:T(8,128)S(1)}, u32[]{:S(2)}, u32[]{:S(2)}) collective-permute-start(f32[520,128]{1,0:T(8,128)} %get-tuple-element.53), channel_id=1, source_target_pairs={{0,7},{1,6},{2,5},{3,4},{4,3},{5,2},{6,1},{7,0},{8,15},{9,14},{10,... | collective-permute-start | bytes 798728 | tf_op jit(solution)/shard_map/ppermute | solution.py:510
  66.2 42.5 %collective-permute-start.10 = (f32[2,256,128]{2,1,0:T(8,128)S(1)}, f32[2,256,128]{2,1,0:T(8,128)S(1)}, u32[]{:S(2)}, u32[]{:S(2)}) collective-permute-start(f32[2,256,128]{2,1,0:T(8,128)S(1)} %get-tuple-element.56), channel_id=1, source_target_pairs={{0,4},{1,5},{2,6},{3,7},{4,0},{5,1},{6,2},{7,3},{8,12},{9,13},{10,... | collective-permute-start | bytes 786440 | tf_op jit(solution)/shard_map/ppermute | solution.py:510
  67.3 41.5 %collective-permute-start.11 = (f32[2,256,128]{2,1,0:T(8,128)S(1)}, f32[2,256,128]{2,1,0:T(8,128)S(1)}, u32[]{:S(2)}, u32[]{:S(2)}) collective-permute-start(f32[2,256,128]{2,1,0:T(8,128)S(1)} %get-tuple-element.57), channel_id=1, source_target_pairs={{0,5},{1,4},{2,7},{3,6},{4,1},{5,0},{6,3},{7,2},{8,13},{9,12},{10,... | collective-permute-start | bytes 786440 | tf_op jit(solution)/shard_map/ppermute | solution.py:510
  69.3 40.0 %collective-permute-start.12 = (f32[2,256,128]{2,1,0:T(8,128)S(1)}, f32[2,256,128]{2,1,0:T(8,128)S(1)}, u32[]{:S(2)}, u32[]{:S(2)}) collective-permute-start(f32[2,256,128]{2,1,0:T(8,128)S(1)} %get-tuple-element.58), channel_id=1, source_target_pairs={{0,6},{1,7},{2,4},{3,5},{4,2},{5,3},{6,0},{7,1},{8,14},{9,15},{10,... | collective-permute-start | bytes 786440 | tf_op jit(solution)/shard_map/ppermute | solution.py:510
  70.1 44.0 %collective-permute-start.13 = (f32[2,256,128]{2,1,0:T(8,128)S(1)}, f32[2,256,128]{2,1,0:T(8,128)S(1)}, u32[]{:S(2)}, u32[]{:S(2)}) collective-permute-start(f32[2,256,128]{2,1,0:T(8,128)S(1)} %get-tuple-element.59), channel_id=1, source_target_pairs={{0,7},{1,6},{2,5},{3,4},{4,3},{5,2},{6,1},{7,0},{8,15},{9,14},{10,... | collective-permute-start | bytes 786440 | tf_op jit(solution)/shard_map/ppermute | solution.py:510

commit v15 on v14

--- a/solution.py
+++ b/solution.py
@@ -168,6 +168,20 @@
         self.middle = edge - 16
         self.size = self.rows * self.middle + self.rows_far * 8
 
+        begins = [min(W + p * self.rows, 2 * W + p * self.rows_far) for p in range(self.half)]
+        ends = [max(W + p * self.rows + self.rows, 2 * W + (p + 1) * self.rows_far) for p in range(self.half)]
+        self.span = max(end - begin for begin, end in zip(begins, ends))
+        side = self.half // 2
+        self.batches = (list(range(side)), [side], list(range(side + 1, self.half)))
+
+    def batch_rows(self, batch, mine):
+        if batch == 0:
+            count = self.inner // 2
+            return W + mine // (self.half // 2) * count, count
+        piece = mine ^ self.batches[1][0]
+        begin = jnp.minimum(W + piece * self.rows, 2 * W + piece * self.rows_far)
+        return jnp.minimum(begin, self.edge - W - self.span), self.span
+
     def near_row(self, piece, row, gap):
         index = piece * self.rows_near + row
         return index + jnp.where(index < W, 0, gap)
@@ -219,12 +233,13 @@
     lax.fori_loop(0, count, one_row, 0, unroll=UNROLL)
 
 
-def inner_kernel(plan, own, phase, solute, *rest):
-    tiles, edge, count = plan.tiles, plan.edge, plan.inner // 2
-    outs, scratch = rest[: plan.half // 2], rest[plan.half // 2 :]
+def inner_kernel(plan, batch, own, phase, solute, *rest):
+    tiles, edge, indices = plan.tiles, plan.edge, plan.batches[batch]
+    outs, scratch = rest[: len(indices)], rest[len(indices) :]
     pairs = (scratch[:2], scratch[2:])
     mine = lax.rem(lax.axis_index("gy"), plan.half)
-    base = mine // (plan.half // 2) * count
+    begin, count = plan.batch_rows(batch, mine)
+    base = begin - W
 
     def load_row(row, carry):
         for tile in range(tiles):
@@ -249,7 +264,7 @@
         starts = range(PAD + margin, PAD + tiles * edge - margin, 8)
         rows = count + 2 * W - 2 * (step + 1)
         march(rows, lambda i, step=step: step + 1 + i, starts, pairs[step % 2], pairs[(step + 1) % 2], coefs_of)
-    for index, out in enumerate(outs):
+    for index, out in zip(indices, outs):
         pack(plan, True, mine ^ index, pairs[NSTEPS % 2], -base, PAD, own, out)
 
 
@@ -266,16 +281,17 @@
     out[tail : tail + AUX, :] = own[8 * plan.tiles : 8 * plan.tiles + AUX, :]
 
 
-def run_inner(plan, own, phase, solute):
-    rows = plan.inner // 2 + 2 * W
+def run_inner(plan, batch, own, phase, solute):
+    rows = plan.batch_rows(batch, 0)[1] + 2 * W
+    count = len(plan.batches[batch])
     buffer = pltpu.VMEM((rows, plan.tiles * plan.edge + 2 * PAD, plan.depth), jnp.float32)
     vmem = pl.BlockSpec(memory_space=pltpu.VMEM)
     shape = jax.ShapeDtypeStruct((2 * plan.tiles * plan.size + AUX, plan.depth), jnp.float32)
     return pl.pallas_call(
-        functools.partial(inner_kernel, plan),
+        functools.partial(inner_kernel, plan, batch),
         in_specs=[vmem] * 3,
-        out_specs=[vmem] * (plan.half // 2),
-        out_shape=[shape] * (plan.half // 2),
+        out_specs=[vmem] * count,
+        out_shape=[shape] * count,
         scratch_shapes=[buffer] * 4,
         compiler_params=pltpu.CompilerParams(vmem_limit_bytes=16 * 1024 * 1024),
         cost_estimate=pl.CostEstimate(flops=10**8, bytes_accessed=24 * 1024 * 1024, transcendentals=0),
@@ -285,7 +301,8 @@
 
 def outer_kernel(plan, own, phase, solute, y_lo, y_hi, x_lo, x_hi, out, *rest):
     tiles, edge, depth, half = plan.tiles, plan.edge, plan.depth, plan.half
-    far_outs, scratch = rest[: half // 2], rest[half // 2 :]
+    late = plan.batches[2]
+    far_outs, scratch = rest[: len(late)], rest[len(late) :]
     pairs, coefs = (scratch[:2], scratch[2:4]), scratch[4]
     cols = tiles * edge
     width = cols + 2 * W
@@ -360,8 +377,8 @@
         march(edge + 2 * left - gap_rows, outside, whole, source, target, any_zone)
         march(gap_rows, lambda i, gap=gap: gap + i, sorted(set(ends)), source, target, own_zone)
     done = pairs[NSTEPS % 2]
-    for index, far_out in enumerate(far_outs):
-        pack(plan, True, mine ^ (half // 2 + index), done, W, PAD + W, own, far_out)
+    for index, far_out in zip(late, far_outs):
+        pack(plan, True, mine ^ index, done, W, PAD + W, own, far_out)
     for piece in range(half):
         pack(plan, False, piece, done, W, PAD + W, own, out.at[piece])
 
@@ -376,8 +393,8 @@
     return pl.pallas_call(
         functools.partial(outer_kernel, plan),
         in_specs=[vmem] * 7,
-        out_specs=[vmem] * (1 + plan.half // 2),
-        out_shape=[near] + [far] * (plan.half // 2),
+        out_specs=[vmem] * (1 + len(plan.batches[2])),
+        out_shape=[near] + [far] * len(plan.batches[2]),
         scratch_shapes=[buffer] * 4 + [pltpu.VMEM((3, KINDS, width, depth), jnp.float32)],
         compiler_params=pltpu.CompilerParams(vmem_limit_bytes=16 * 1024 * 1024),
         cost_estimate=pl.CostEstimate(flops=10**8, bytes_accessed=40 * 1024 * 1024, transcendentals=0),
@@ -525,17 +542,28 @@
     to_prev, to_next, own = pack_y(phase, solute, (undercool, mobility, diffusivity), owner)
     y_lo = lax.ppermute(to_next, "gy", ring("gy", 1))
     y_hi = lax.ppermute(to_prev, "gy", ring("gy", -1))
-    first = run_inner(plan, own, phase, solute)
-    far = [swap(values, half + index) for index, values in enumerate(first)]
+    far = {}
+
+    def send_far(batch, values):
+        for index, value in zip(plan.batches[batch], values):
+            far[index] = swap(value, half + index)
+
+    first = run_inner(plan, 0, own, phase, solute)
+    send_far(0, first)
     to_prev, to_next = pack_x(phase, solute, own, y_lo, y_hi, first[0])
     together = owner[0, 0] >= 0
 
-    def around(low, high):
+    def around(low, high, *values):
+        return ring_swap(low, high), run_inner(plan, 1, *values)
+
+    def ring_swap(low, high):
         return lax.ppermute(low, "gx", ring("gx", 1)), lax.ppermute(high, "gx", ring("gx", -1))
 
-    x_lo, x_hi = lax.cond(together, around, around, to_next, to_prev)
-    near, *second = run_outer(plan, own, phase, solute, (y_lo, y_hi, x_lo, x_hi))
-    far += [swap(values, half + half // 2 + index) for index, values in enumerate(second)]
+    (x_lo, x_hi), second = lax.cond(together, around, around, to_next, to_prev, own, phase, solute)
+    send_far(1, second)
+    near, *third = run_outer(plan, own, phase, solute, (y_lo, y_hi, x_lo, x_hi))
+    send_far(2, third)
+    far = [far[index] for index in range(half)]
     near = among_half(plan, near, together)
     near, far, table = route(plan, near, far)
     far = [swap(values, half + index) for index, values in enumerate(far)]

time: 116 us -> 114 us (0.983)
  blocking collectives: 64.4 us -> 59.6 us
  Pallas kernels: 21.1 us -> 25.9 us
  waiting for transfers between devices: 12.5 us -> 10.3 us
    all_to_all x2, blocking collectives: 64.4 us -> 59.6 us  [exchange(): lax.all_to_all(values, 'gy', 0, 0, axis_index_groups=groups, tiled=True)]
    pallas_call x1 -> x2, Pallas kernels: 3.97 us -> 7.82 us  [run_inner(): pl.pallas_call(functools.partial(inner_kernel, plan, batch), in_specs=[vm...]
    ppermute x2, waiting for transfers between devices: 6.92 us -> 3.1 us  [the longest x1 2.35 us: ring_swap(): lax.ppermute(low, 'gx', ring('gx', 1))]
    ppermute x8, waiting for transfers between devices: 5.6 us -> 7.22 us  [swap(): lax.ppermute(values, 'gy', [(i, i ^ mask) for i in range(lax.axis_size('g...]
    pallas_call x1, Pallas kernels: 0.89 us -> 2.2 us  [route(): pl.pallas_call(functools.partial(route_kernel, plan), in_specs=[vmem] * (...]
  transfers between devices with their start and end apart: 12 -> 12, of which waited for: 5 -> 4; matrix products, arithmetic and copies ran while one was open for 0% -> 0% of each run, Pallas kernels for 14% -> 17%
where the time goes in v15:
time: 114 us; the launch traced here: 113 us
  blocking collectives  59.6 us (52%)
  Pallas kernels  25.9 us (23%)
  starting transfers between devices  16.8 us (15%)
  waiting for transfers between devices  10.3 us (9%)
    all_to_all x2, blocking collectives, exchange(): lax.all_to_all(values, 'gy', 0, 0, axis_index_groups=groups, tiled=True)  59.6 us
    ppermute x8, starting transfers between devices, swap(): lax.ppermute(values, 'gy', [(i, i ^ mask) for i in range(lax.axis_size('g...  12.1 us
    pallas_call x1, Pallas kernels, run_outer(): pl.pallas_call(functools.partial(outer_kernel, plan), in_specs=[vmem] * 7...  11.8 us
    pallas_call x2, Pallas kernels, run_inner(): pl.pallas_call(functools.partial(inner_kernel, plan, batch), in_specs=[vm...  7.82 us
    ppermute x8, waiting for transfers between devices, swap(): lax.ppermute(values, 'gy', [(i, i ^ mask) for i in range(lax.axis_size('g...  7.22 us
    ppermute x1, waiting for transfers between devices, ring_swap(): lax.ppermute(low, 'gx', ring('gx', 1))  2.35 us
  transfers between devices with their start and end apart: 12, of which 4 were waited for; matrix products, arithmetic and copies ran while one was open for 0% of the time, Pallas kernels for 17%

profile of v15, /device:TPU:8, one launch (start us, length us, event | category | flops | bytes accessed | tf_op | source)
XLA Modules:
  0.0 113.4 jit_solution(16399361756891167489)
XLA Ops:
  0.6 0.0 copy-start.1
  0.6 0.0 copy-start
  0.7 2.0 %pack_y.1 = (f32[33,8,128]{2,1,0:T(8,128)}, f32[33,8,128]{2,1,0:T(8,128)}, f32[24,128]{1,0:T(8,128)S(1)}) custom-call(f32[1,2]{1,0:T(1,128)} %under.1, f32[1,2]{1,0:T(1,128)} %mobile.1, f32[1,2]{1,0:T(1,128)} %spread.1, s32[1,2]{1,0:T(1,128)} %owner.1, f32[1,2,32,32,128]{4,3,2,1,0:T(8,128)} %phase.3, f32[1,2,32,32,128]{4,3,2,1,0:T(8,128)} %phase.3, ...), custom_call_target="tpu_custom_call" | custom-call | tf_op jit(solution)/shard_map/pack_y/pallas_call | solution.py:48
  2.7 0.0 copy-start.2
  2.7 1.5 %collective-permute-start.4 = (f32[33,8,128]{2,1,0:T(8,128)}, f32[33,8,128]{2,1,0:T(8,128)S(1)}, u32[]{:S(2)}, u32[]{:S(2)}) collective-permute-start(f32[33,8,128]{2,1,0:T(8,128)} %get-tuple-element.61), channel_id=1, source_target_pairs={{0,1},{1,2},{2,3},{3,4},{4,5},{5,6},{6,7},{7,0},{8,9},{9,10},{10,1... | collective-permute-start | bytes 405512 | tf_op jit(solution)/shard_map/ppermute | solution.py:543
  4.2 1.4 %collective-permute-start.5 = (f32[33,8,128]{2,1,0:T(8,128)}, f32[33,8,128]{2,1,0:T(8,128)S(1)}, u32[]{:S(2)}, u32[]{:S(2)}) collective-permute-start(f32[33,8,128]{2,1,0:T(8,128)} %get-tuple-element.62), channel_id=1, source_target_pairs={{0,7},{1,0},{2,1},{3,2},{4,3},{5,4},{6,5},{7,6},{8,15},{9,8},{10,9... | collective-permute-start | bytes 405512 | tf_op jit(solution)/shard_map/ppermute | solution.py:544
  5.6 0.0 copy-done.1
  5.6 0.0 copy-done
  5.6 4.0 %inner.5 = (f32[520,128]{1,0:T(8,128)S(1)}, f32[520,128]{1,0:T(8,128)S(1)}) custom-call(f32[24,128]{1,0:T(8,128)S(1)} %get-tuple-element.60.own, f32[1,2,32,32,128]{4,3,2,1,0:T(8,128)S(1)} %copy-done, f32[1,2,32,32,128]{4,3,2,1,0:T(8,128)S(1)} %copy-done.1), custom_call_target="tpu_custom_call" | custom-call | flops 100000000 | bytes 25165824 | tf_op jit(solution)/shard_map/inner/pallas_call | solution.py:290
  9.6 2.7 %collective-permute-start.7 = (f32[520,128]{1,0:T(8,128)S(1)}, f32[520,128]{1,0:T(8,128)S(1)}, u32[]{:S(2)}, u32[]{:S(2)}) collective-permute-start(f32[520,128]{1,0:T(8,128)S(1)} %get-tuple-element.69), channel_id=1, source_target_pairs={{0,5},{1,4},{2,7},{3,6},{4,1},{5,0},{6,3},{7,2},{8,13},{9,12},{10,... | collective-permute-start | bytes 798728 | tf_op jit(solution)/shard_map/ppermute | solution.py:527
  12.3 0.3 collective-permute-start.6
  12.7 0.0 copy-done.2
  12.7 0.0 collective-permute-done.4.y_lo
  12.7 0.0 collective-permute-done.5.y_hi
  12.8 8.7 %conditional.3 = (f32[608,128]{1,0:T(8,128)}, f32[608,128]{1,0:T(8,128)}, f32[520,128]{1,0:T(8,128)}) conditional(s32[]{:T(128)} %bitcast, (f32[608,128]{1,0:T(8,128)S(1)}, f32[608,128]{1,0:T(8,128)S(1)}, f32[24,128]{1,0:T(8,128)S(1)}, f32[1,2,32,32,128]{4,3,2,1,0:T(8,128)S(1)}, f32[1,2,32,32,128]{4,3,2,1,0:T(8,128)S(1)}) %tuple.36, ...), branch_computations={%region_0.0_spmd, %region_1.0_spmd} | conditional | flops 100000000 | bytes 27656296 | solution.py:562
  12.8 0.1 collective-permute-start.2
  12.9 1.7 %collective-permute-start.3 = (f32[608,128]{1,0:T(8,128)S(1)}, f32[608,128]{1,0:T(8,128)}, u32[]{:S(2)}, u32[]{:S(2)}) collective-permute-start(f32[608,128]{1,0:T(8,128)S(1)} %get-tuple-element.36), channel_id=1, source_target_pairs={{0,24},{8,0},{16,8},{24,16},{1,25},{9,1},{17,9},{25,17},{2,26},{10... | collective-permute-start | bytes 933896 | tf_op jit(solution)/shard_map/cond/branch_1_fun/ppermute | solution.py:560
  14.6 3.8 %inner.4 = f32[520,128]{1,0:T(8,128)} custom-call(f32[24,128]{1,0:T(8,128)S(1)} %get-tuple-element.37.own, f32[1,2,32,32,128]{4,3,2,1,0:T(8,128)S(1)} %get-tuple-element.38.phase, f32[1,2,32,32,128]{4,3,2,1,0:T(8,128)S(1)} %get-tuple-element.39.solute), custom_call_target="tpu_custom_call" | custom-call | flops 100000000 | bytes 25165824 | tf_op jit(solution)/shard_map/cond/branch_1_fun/inner/pallas_call | solution.py:290
  18.4 2.3 %collective-permute-done.2 = f32[608,128]{1,0:T(8,128)} collective-permute-done((f32[608,128]{1,0:T(8,128)S(1)}, f32[608,128]{1,0:T(8,128)}, u32[]{:S(2)}, u32[]{:S(2)}) %collective-permute-start.2) | collective-permute-done | bytes 311328 | tf_op jit(solution)/shard_map/cond/branch_1_fun/ppermute | solution.py:560
  20.8 0.8 collective-permute-done.3
  21.5 1.6 %collective-permute-start.8 = (f32[520,128]{1,0:T(8,128)}, f32[520,128]{1,0:T(8,128)S(1)}, u32[]{:S(2)}, u32[]{:S(2)}) collective-permute-start(f32[520,128]{1,0:T(8,128)} %get-tuple-element.70), channel_id=1, source_target_pairs={{0,6},{1,7},{2,4},{3,5},{4,2},{5,3},{6,0},{7,1},{8,14},{9,15},{10,... | collective-permute-start | bytes 798728 | tf_op jit(solution)/shard_map/ppermute | solution.py:527
  23.1 11.8 %outer.1 = (f32[4,520,128]{2,1,0:T(8,128)S(1)}, f32[520,128]{1,0:T(8,128)S(1)}) custom-call(f32[24,128]{1,0:T(8,128)S(1)} %get-tuple-element.60.own, f32[1,2,32,32,128]{4,3,2,1,0:T(8,128)S(1)} %copy-done, f32[1,2,32,32,128]{4,3,2,1,0:T(8,128)} %solute.3, f32[33,8,128]{2,1,0:T(8,128)S(1)} %collective-permute-done.4.y_lo, ...), custom_call_target="tpu_custom_call" | custom-call | flops 100000000 | bytes 41943040 | tf_op jit(solution)/shard_map/outer/pallas_call | solution.py:393
  34.9 1.5 %collective-permute-start.9 = (f32[520,128]{1,0:T(8,128)S(1)}, f32[520,128]{1,0:T(8,128)S(1)}, u32[]{:S(2)}, u32[]{:S(2)}) collective-permute-start(f32[520,128]{1,0:T(8,128)S(1)} %get-tuple-element.71), channel_id=1, source_target_pairs={{0,7},{1,6},{2,5},{3,4},{4,3},{5,2},{6,1},{7,0},{8,15},{9,14},{10,... | collective-permute-start | bytes 798728 | tf_op jit(solution)/shard_map/ppermute | solution.py:527
  36.4 26.6 %conditional.4 = (f32[4,520,128]{2,1,0:T(8,128)}) conditional(s32[]{:T(128)} %bitcast, f32[4,520,128]{2,1,0:T(8,128)S(1)} %get-tuple-element.68, f32[4,520,128]{2,1,0:T(8,128)S(1)} %get-tuple-element.68), branch_computations={%region_2.0_spmd, %region_3.0_spmd} | conditional | bytes 2129928 | solution.py:535
  36.4 26.6 %all_to_all.17 = f32[4,520,128]{2,1,0:T(8,128)} all-to-all(f32[4,520,128]{2,1,0:T(8,128)S(1)} %param.3), channel_id=1, replica_groups={{0,1,2,3},{4,5,6,7},{8,9,10,11},{12,13,14,15},{16,17,18,19},{20,21,22,2..., dimensions={0} | all-to-all | bytes 2129920 | tf_op jit(solution)/shard_map/cond/branch_1_fun/all_to_all | solution.py:533
  63.0 0.0 collective-permute-done.7.refs_1_
  63.0 0.0 collective-permute-done.6.refs_0_
  63.0 0.0 collective-permute-done.8.refs_2_
  63.0 0.0 collective-permute-done.9.refs_3_
  63.0 2.2 %route.1 = (f32[4,2,256,128]{3,2,1,0:T(8,128)S(1)}, f32[2,256,128]{2,1,0:T(8,128)S(1)}, f32[2,256,128]{2,1,0:T(8,128)S(1)}, f32[2,256,128]{2,1,0:T(8,128)S(1)}, ...) custom-call(f32[4,520,128]{2,1,0:T(8,128)} %get-tuple-element.84.near, f32[520,128]{1,0:T(8,128)S(1)} %collective-permute-done.6.refs_0_, ...), custom_call_target="tpu_custom_call" | custom-call | tf_op jit(solution)/shard_map/route/pallas_call | solution.py:443
  65.2 0.1 collective-permute-start.10
  65.3 2.9 %collective-permute-start.11 = (f32[2,256,128]{2,1,0:T(8,128)S(1)}, f32[2,256,128]{2,1,0:T(8,128)S(1)}, u32[]{:S(2)}, u32[]{:S(2)}) collective-permute-start(f32[2,256,128]{2,1,0:T(8,128)S(1)} %get-tuple-element.75), channel_id=1, source_target_pairs={{0,5},{1,4},{2,7},{3,6},{4,1},{5,0},{6,3},{7,2},{8,13},{9,12},{10,... | collective-permute-start | bytes 786440 | tf_op jit(solution)/shard_map/ppermute | solution.py:527
  68.2 0.2 collective-permute-start.12
  68.5 2.7 %collective-permute-start.13 = (f32[2,256,128]{2,1,0:T(8,128)S(1)}, f32[2,256,128]{2,1,0:T(8,128)S(1)}, u32[]{:S(2)}, u32[]{:S(2)}) collective-permute-start(f32[2,256,128]{2,1,0:T(8,128)S(1)} %get-tuple-element.77), channel_id=1, source_target_pairs={{0,7},{1,6},{2,5},{3,4},{4,3},{5,2},{6,1},{7,0},{8,15},{9,14},{10,... | collective-permute-start | bytes 786440 | tf_op jit(solution)/shard_map/ppermute | solution.py:527
  71.2 33.0 %conditional.5 = (f32[4,2,256,128]{3,2,1,0:T(8,128)S(1)}) conditional(s32[]{:T(128)} %bitcast, f32[4,2,256,128]{3,2,1,0:T(8,128)S(1)} %get-tuple-element.73, f32[4,2,256,128]{3,2,1,0:T(8,128)S(1)} %get-tuple-element.73), branch_computations={%region_4.0_spmd, %region_5.0_spmd} | conditional | bytes 2097160 | solution.py:535
  71.2 33.0 %all_to_all.19 = f32[4,2,256,128]{3,2,1,0:T(8,128)S(1)} all-to-all(f32[4,2,256,128]{3,2,1,0:T(8,128)S(1)} %param.5), channel_id=1, replica_groups={{0,1,2,3},{4,5,6,7},{8,9,10,11},{12,13,14,15},{16,17,18,19},{20,21,22,2..., dimensions={0} | all-to-all | bytes 2097152 | tf_op jit(solution)/shard_map/cond/branch_1_fun/all_to_all | solution.py:533
  104.2 0.0 collective-permute-done.10.refs_0_
  104.2 0.0 collective-permute-done.11.refs_1_
  104.2 1.8 %collective-permute-done.12.refs_2_ = f32[2,256,128]{2,1,0:T(8,128)S(1)} collective-permute-done((f32[2,256,128]{2,1,0:T(8,128)S(1)}, f32[2,256,128]{2,1,0:T(8,128)S(1)}, u32[]{:S(2)}, u32[]{:S(2)}) %collective-permute-start.12) | collective-permute-done | bytes 262176 | tf_op jit(solution)/shard_map/ppermute | solution.py:527
  106.0 5.4 %collective-permute-done.13.refs_3_ = f32[2,256,128]{2,1,0:T(8,128)S(1)} collective-permute-done((f32[2,256,128]{2,1,0:T(8,128)S(1)}, f32[2,256,128]{2,1,0:T(8,128)S(1)}, u32[]{:S(2)}, u32[]{:S(2)}) %collective-permute-start.13) | collective-permute-done | bytes 262176 | tf_op jit(solution)/shard_map/ppermute | solution.py:527
  111.4 2.0 %settle.1 = (f32[1,2,32,32,128]{4,3,2,1,0:T(8,128)}, f32[1,2,32,32,128]{4,3,2,1,0:T(8,128)}) custom-call(s32[16]{0:T(128)S(1)} %get-tuple-element.72.table, f32[4,2,256,128]{3,2,1,0:T(8,128)S(1)} %get-tuple-element.85.near, f32[2,256,128]{2,1,0:T(8,128)S(1)} %collective-permute-done.10.refs_0_, f32[2,256,128]{2,1,0:T(8,128)S(1)} %collective-permute-done.11.refs_1_, ...), custom_call_target="tpu_custom_call" | custom-call | tf_op jit(solution)/shard_map/settle/pallas_call | solution.py:507
  (1 shorter events, 0.0 us)
Async XLA Ops:
  0.6 5.0 %copy-start.1 = (f32[1,2,32,32,128]{4,3,2,1,0:T(8,128)S(1)}, f32[1,2,32,32,128]{4,3,2,1,0:T(8,128)}, u32[]{:S(2)}) copy-start(f32[1,2,32,32,128]{4,3,2,1,0:T(8,128)} %solute.3) | copy-start | bytes 3145732
  0.6 5.0 %copy-start = (f32[1,2,32,32,128]{4,3,2,1,0:T(8,128)S(1)}, f32[1,2,32,32,128]{4,3,2,1,0:T(8,128)}, u32[]{:S(2)}) copy-start(f32[1,2,32,32,128]{4,3,2,1,0:T(8,128)} %phase.3) | copy-start | bytes 3145732
  2.7 10.0 %copy-start.2 = (s32[1,2]{1,0:T(1,128)S(1)}, s32[1,2]{1,0:T(1,128)}, u32[]{:S(2)}) copy-start(s32[1,2]{1,0:T(1,128)} %owner.1) | copy-start | bytes 28
  2.7 10.0 %collective-permute-start.4 = (f32[33,8,128]{2,1,0:T(8,128)}, f32[33,8,128]{2,1,0:T(8,128)S(1)}, u32[]{:S(2)}, u32[]{:S(2)}) collective-permute-start(f32[33,8,128]{2,1,0:T(8,128)} %get-tuple-element.61), channel_id=1, source_target_pairs={{0,1},{1,2},{2,3},{3,4},{4,5},{5,6},{6,7},{7,0},{8,9},{9,10},{10,1... | collective-permute-start | bytes 405512 | tf_op jit(solution)/shard_map/ppermute | solution.py:543
  4.2 8.5 %collective-permute-start.5 = (f32[33,8,128]{2,1,0:T(8,128)}, f32[33,8,128]{2,1,0:T(8,128)S(1)}, u32[]{:S(2)}, u32[]{:S(2)}) collective-permute-start(f32[33,8,128]{2,1,0:T(8,128)} %get-tuple-element.62), channel_id=1, source_target_pairs={{0,7},{1,0},{2,1},{3,2},{4,3},{5,4},{6,5},{7,6},{8,15},{9,8},{10,9... | collective-permute-start | bytes 405512 | tf_op jit(solution)/shard_map/ppermute | solution.py:544
  9.6 53.4 %collective-permute-start.7 = (f32[520,128]{1,0:T(8,128)S(1)}, f32[520,128]{1,0:T(8,128)S(1)}, u32[]{:S(2)}, u32[]{:S(2)}) collective-permute-start(f32[520,128]{1,0:T(8,128)S(1)} %get-tuple-element.69), channel_id=1, source_target_pairs={{0,5},{1,4},{2,7},{3,6},{4,1},{5,0},{6,3},{7,2},{8,13},{9,12},{10,... | collective-permute-start | bytes 798728 | tf_op jit(solution)/shard_map/ppermute | solution.py:527
  12.3 50.7 %collective-permute-start.6 = (f32[520,128]{1,0:T(8,128)S(1)}, f32[520,128]{1,0:T(8,128)S(1)}, u32[]{:S(2)}, u32[]{:S(2)}) collective-permute-start(f32[520,128]{1,0:T(8,128)S(1)} %get-tuple-element.63._), channel_id=1, source_target_pairs={{0,4},{1,5},{2,6},{3,7},{4,0},{5,1},{6,2},{7,3},{8,12},{9,13},{10,... | collective-permute-start | bytes 798728 | tf_op jit(solution)/shard_map/ppermute | solution.py:527
  12.8 8.0 %collective-permute-start.2 = (f32[608,128]{1,0:T(8,128)S(1)}, f32[608,128]{1,0:T(8,128)}, u32[]{:S(2)}, u32[]{:S(2)}) collective-permute-start(f32[608,128]{1,0:T(8,128)S(1)} %get-tuple-element.35), channel_id=1, source_target_pairs={{0,8},{8,16},{16,24},{24,0},{1,9},{9,17},{17,25},{25,1},{2,10},{10... | collective-permute-start | bytes 933896 | tf_op jit(solution)/shard_map/cond/branch_1_fun/ppermute | solution.py:560
  12.9 8.7 %collective-permute-start.3 = (f32[608,128]{1,0:T(8,128)S(1)}, f32[608,128]{1,0:T(8,128)}, u32[]{:S(2)}, u32[]{:S(2)}) collective-permute-start(f32[608,128]{1,0:T(8,128)S(1)} %get-tuple-element.36), channel_id=1, source_target_pairs={{0,24},{8,0},{16,8},{24,16},{1,25},{9,1},{17,9},{25,17},{2,26},{10... | collective-permute-start | bytes 933896 | tf_op jit(solution)/shard_map/cond/branch_1_fun/ppermute | solution.py:560
  21.5 41.5 %collective-permute-start.8 = (f32[520,128]{1,0:T(8,128)}, f32[520,128]{1,0:T(8,128)S(1)}, u32[]{:S(2)}, u32[]{:S(2)}) collective-permute-start(f32[520,128]{1,0:T(8,128)} %get-tuple-element.70), channel_id=1, source_target_pairs={{0,6},{1,7},{2,4},{3,5},{4,2},{5,3},{6,0},{7,1},{8,14},{9,15},{10,... | collective-permute-start | bytes 798728 | tf_op jit(solution)/shard_map/ppermute | solution.py:527
  34.9 28.1 %collective-permute-start.9 = (f32[520,128]{1,0:T(8,128)S(1)}, f32[520,128]{1,0:T(8,128)S(1)}, u32[]{:S(2)}, u32[]{:S(2)}) collective-permute-start(f32[520,128]{1,0:T(8,128)S(1)} %get-tuple-element.71), channel_id=1, source_target_pairs={{0,7},{1,6},{2,5},{3,4},{4,3},{5,2},{6,1},{7,0},{8,15},{9,14},{10,... | collective-permute-start | bytes 798728 | tf_op jit(solution)/shard_map/ppermute | solution.py:527
  65.2 38.9 %collective-permute-start.10 = (f32[2,256,128]{2,1,0:T(8,128)S(1)}, f32[2,256,128]{2,1,0:T(8,128)S(1)}, u32[]{:S(2)}, u32[]{:S(2)}) collective-permute-start(f32[2,256,128]{2,1,0:T(8,128)S(1)} %get-tuple-element.74), channel_id=1, source_target_pairs={{0,4},{1,5},{2,6},{3,7},{4,0},{5,1},{6,2},{7,3},{8,12},{9,13},{10,... | collective-permute-start | bytes 786440 | tf_op jit(solution)/shard_map/ppermute | solution.py:527
  65.3 38.8 %collective-permute-start.11 = (f32[2,256,128]{2,1,0:T(8,128)S(1)}, f32[2,256,128]{2,1,0:T(8,128)S(1)}, u32[]{:S(2)}, u32[]{:S(2)}) collective-permute-start(f32[2,256,128]{2,1,0:T(8,128)S(1)} %get-tuple-element.75), channel_id=1, source_target_pairs={{0,5},{1,4},{2,7},{3,6},{4,1},{5,0},{6,3},{7,2},{8,13},{9,12},{10,... | collective-permute-start | bytes 786440 | tf_op jit(solution)/shard_map/ppermute | solution.py:527
  68.2 37.7 %collective-permute-start.12 = (f32[2,256,128]{2,1,0:T(8,128)S(1)}, f32[2,256,128]{2,1,0:T(8,128)S(1)}, u32[]{:S(2)}, u32[]{:S(2)}) collective-permute-start(f32[2,256,128]{2,1,0:T(8,128)S(1)} %get-tuple-element.76), channel_id=1, source_target_pairs={{0,6},{1,7},{2,4},{3,5},{4,2},{5,3},{6,0},{7,1},{8,14},{9,15},{10,... | collective-permute-start | bytes 786440 | tf_op jit(solution)/shard_map/ppermute | solution.py:527
  68.5 42.9 %collective-permute-start.13 = (f32[2,256,128]{2,1,0:T(8,128)S(1)}, f32[2,256,128]{2,1,0:T(8,128)S(1)}, u32[]{:S(2)}, u32[]{:S(2)}) collective-permute-start(f32[2,256,128]{2,1,0:T(8,128)S(1)} %get-tuple-element.77), channel_id=1, source_target_pairs={{0,7},{1,6},{2,5},{3,4},{4,3},{5,2},{6,1},{7,0},{8,15},{9,14},{10,... | collective-permute-start | bytes 786440 | tf_op jit(solution)/shard_map/ppermute | solution.py:527

commit v16 on v15

--- a/solution.py
+++ b/solution.py
@@ -535,6 +535,10 @@
     return lax.cond(together, exchange, exchange, values)
 
 
+def in_vmem(values):
+    return pltpu.with_memory_space_constraint(values, pltpu.VMEM)
+
+
 def per_device(phase, solute, undercool, mobility, diffusivity, owner):
     _, tiles, edge, _, depth = phase.shape
     plan = Plan(lax.axis_size("gy"), tiles, edge, depth)
@@ -548,9 +552,10 @@
         for index, value in zip(plan.batches[batch], values):
             far[index] = swap(value, half + index)
 
-    first = run_inner(plan, 0, own, phase, solute)
+    own_here, phase_here, solute_here = in_vmem(own), in_vmem(phase), in_vmem(solute)
+    first = run_inner(plan, 0, own_here, phase_here, solute_here)
     send_far(0, first)
-    to_prev, to_next = pack_x(phase, solute, own, y_lo, y_hi, first[0])
+    to_prev, to_next = pack_x(phase_here, solute_here, own_here, y_lo, y_hi, first[0])
     together = owner[0, 0] >= 0
 
     def around(low, high, *values):
@@ -561,11 +566,11 @@
 
     (x_lo, x_hi), second = lax.cond(together, around, around, to_next, to_prev, own, phase, solute)
     send_far(1, second)
-    near, *third = run_outer(plan, own, phase, solute, (y_lo, y_hi, x_lo, x_hi))
+    near, *third = run_outer(plan, own_here, phase_here, solute_here, (y_lo, y_hi, in_vmem(x_lo), in_vmem(x_hi)))
     send_far(2, third)
     far = [far[index] for index in range(half)]
     near = among_half(plan, near, together)
-    near, far, table = route(plan, near, far)
+    near, far, table = route(plan, in_vmem(near), far)
     far = [swap(values, half + index) for index, values in enumerate(far)]
     near = among_half(plan, near, together)
     return tuple(settle(plan, table, near, far))

time: 114 us -> 113 us (level)
  blocking collectives: 59.6 us -> 60.8 us
    pallas_call x1, Pallas kernels: 2.2 us -> 0.9 us  [route(): pl.pallas_call(functools.partial(route_kernel, plan), in_specs=[vmem] * (...]
    all_to_all x2, blocking collectives: 59.6 us -> 60.8 us  [exchange(): lax.all_to_all(values, 'gy', 0, 0, axis_index_groups=groups, tiled=True)]
  transfers between devices with their start and end apart: 12 -> 12, of which waited for: 4 -> 4; matrix products, arithmetic and copies ran while one was open for 0% -> 0% of each run, Pallas kernels for 17% -> 18%
where the time goes in v16:
time: 113 us
  blocking collectives  60.8 us (54%)
  Pallas kernels  25.6 us (23%)
  starting transfers between devices  16.6 us (15%)
  waiting for transfers between devices  9.22 us (8%)
    all_to_all x2, blocking collectives, exchange(): lax.all_to_all(values, 'gy', 0, 0, axis_index_groups=groups, tiled=True)  60.8 us
    pallas_call x1, Pallas kernels, run_outer(): pl.pallas_call(functools.partial(outer_kernel, plan), in_specs=[vmem] * 7...  12.1 us
    ppermute x8, starting transfers between devices, swap(): lax.ppermute(values, 'gy', [(i, i ^ mask) for i in range(lax.axis_size('g...  11.9 us
    pallas_call x2, Pallas kernels, run_inner(): pl.pallas_call(functools.partial(inner_kernel, plan, batch), in_specs=[vm...  8.54 us
    ppermute x8, waiting for transfers between devices, swap(): lax.ppermute(values, 'gy', [(i, i ^ mask) for i in range(lax.axis_size('g...  6.11 us
    ppermute x1, waiting for transfers between devices, ring_swap(): lax.ppermute(low, 'gx', ring('gx', 1))  2.35 us
  transfers between devices with their start and end apart: 12, of which 4 were waited for; matrix products, arithmetic and copies ran while one was open for 0% of the time, Pallas kernels for 18%

profile of v16, /device:TPU:8, one launch (start us, length us, event | category | flops | bytes accessed | tf_op | source)
XLA Modules:
  0.0 113.0 jit_solution(3585970692594906219)
XLA Ops:
  0.6 0.0 copy-start.1
  0.6 0.0 copy-start
  0.7 2.0 %pack_y.1 = (f32[33,8,128]{2,1,0:T(8,128)}, f32[33,8,128]{2,1,0:T(8,128)}, f32[24,128]{1,0:T(8,128)S(1)}) custom-call(f32[1,2]{1,0:T(1,128)} %under.1, f32[1,2]{1,0:T(1,128)} %mobile.1, f32[1,2]{1,0:T(1,128)} %spread.1, s32[1,2]{1,0:T(1,128)} %owner.1, f32[1,2,32,32,128]{4,3,2,1,0:T(8,128)} %phase.3, f32[1,2,32,32,128]{4,3,2,1,0:T(8,128)} %phase.3, ...), custom_call_target="tpu_custom_call" | custom-call | tf_op jit(solution)/shard_map/pack_y/pallas_call | solution.py:48
  2.7 0.0 copy-start.2
  2.7 1.5 %collective-permute-start.4 = (f32[33,8,128]{2,1,0:T(8,128)}, f32[33,8,128]{2,1,0:T(8,128)S(1)}, u32[]{:S(2)}, u32[]{:S(2)}) collective-permute-start(f32[33,8,128]{2,1,0:T(8,128)} %get-tuple-element.61), channel_id=1, source_target_pairs={{0,1},{1,2},{2,3},{3,4},{4,5},{5,6},{6,7},{7,0},{8,9},{9,10},{10,1... | collective-permute-start | bytes 405512 | tf_op jit(solution)/shard_map/ppermute | solution.py:547
  4.2 1.4 %collective-permute-start.5 = (f32[33,8,128]{2,1,0:T(8,128)}, f32[33,8,128]{2,1,0:T(8,128)S(1)}, u32[]{:S(2)}, u32[]{:S(2)}) collective-permute-start(f32[33,8,128]{2,1,0:T(8,128)} %get-tuple-element.62), channel_id=1, source_target_pairs={{0,7},{1,0},{2,1},{3,2},{4,3},{5,4},{6,5},{7,6},{8,15},{9,8},{10,9... | collective-permute-start | bytes 405512 | tf_op jit(solution)/shard_map/ppermute | solution.py:548
  5.6 0.0 copy-done.1
  5.6 0.0 copy-done
  5.6 4.7 %inner.5 = (f32[520,128]{1,0:T(8,128)S(1)}, f32[520,128]{1,0:T(8,128)}) custom-call(f32[24,128]{1,0:T(8,128)S(1)} %get-tuple-element.60.own, f32[1,2,32,32,128]{4,3,2,1,0:T(8,128)S(1)} %copy-done, f32[1,2,32,32,128]{4,3,2,1,0:T(8,128)S(1)} %copy-done.1), custom_call_target="tpu_custom_call" | custom-call | flops 100000000 | bytes 25165824 | tf_op jit(solution)/shard_map/inner/pallas_call | solution.py:290
  10.3 2.6 %collective-permute-start.7 = (f32[520,128]{1,0:T(8,128)}, f32[520,128]{1,0:T(8,128)S(1)}, u32[]{:S(2)}, u32[]{:S(2)}) collective-permute-start(f32[520,128]{1,0:T(8,128)} %get-tuple-element.69), channel_id=1, source_target_pairs={{0,5},{1,4},{2,7},{3,6},{4,1},{5,0},{6,3},{7,2},{8,13},{9,12},{10,... | collective-permute-start | bytes 798728 | tf_op jit(solution)/shard_map/ppermute | solution.py:527
  13.0 0.3 collective-permute-start.6
  13.3 0.0 copy-done.2
  13.3 0.0 collective-permute-done.4.y_lo
  13.4 0.0 collective-permute-done.5.y_hi
  13.4 8.7 %conditional.3 = (f32[608,128]{1,0:T(8,128)}, f32[608,128]{1,0:T(8,128)}, f32[520,128]{1,0:T(8,128)}) conditional(s32[]{:T(128)} %bitcast, (f32[608,128]{1,0:T(8,128)S(1)}, f32[608,128]{1,0:T(8,128)S(1)}, f32[24,128]{1,0:T(8,128)S(1)}, f32[1,2,32,32,128]{4,3,2,1,0:T(8,128)S(1)}, f32[1,2,32,32,128]{4,3,2,1,0:T(8,128)S(1)}) %tuple.36, ...), branch_computations={%region_0.0_spmd, %region_1.0_spmd} | conditional | flops 100000000 | bytes 27656296 | solution.py:567
  13.4 0.1 collective-permute-start.2
  13.5 1.7 %collective-permute-start.3 = (f32[608,128]{1,0:T(8,128)S(1)}, f32[608,128]{1,0:T(8,128)}, u32[]{:S(2)}, u32[]{:S(2)}) collective-permute-start(f32[608,128]{1,0:T(8,128)S(1)} %get-tuple-element.36), channel_id=1, source_target_pairs={{0,24},{8,0},{16,8},{24,16},{1,25},{9,1},{17,9},{25,17},{2,26},{10... | collective-permute-start | bytes 933896 | tf_op jit(solution)/shard_map/cond/branch_1_fun/ppermute | solution.py:565
  15.2 3.8 %inner.4 = f32[520,128]{1,0:T(8,128)} custom-call(f32[24,128]{1,0:T(8,128)S(1)} %get-tuple-element.37.own, f32[1,2,32,32,128]{4,3,2,1,0:T(8,128)S(1)} %get-tuple-element.38.phase, f32[1,2,32,32,128]{4,3,2,1,0:T(8,128)S(1)} %get-tuple-element.39.solute), custom_call_target="tpu_custom_call" | custom-call | flops 100000000 | bytes 25165824 | tf_op jit(solution)/shard_map/cond/branch_1_fun/inner/pallas_call | solution.py:290
  19.1 2.3 %collective-permute-done.2 = f32[608,128]{1,0:T(8,128)} collective-permute-done((f32[608,128]{1,0:T(8,128)S(1)}, f32[608,128]{1,0:T(8,128)}, u32[]{:S(2)}, u32[]{:S(2)}) %collective-permute-start.2) | collective-permute-done | bytes 311328 | tf_op jit(solution)/shard_map/cond/branch_1_fun/ppermute | solution.py:565
  21.4 0.8 collective-permute-done.3
  22.2 1.6 %collective-permute-start.8 = (f32[520,128]{1,0:T(8,128)}, f32[520,128]{1,0:T(8,128)S(1)}, u32[]{:S(2)}, u32[]{:S(2)}) collective-permute-start(f32[520,128]{1,0:T(8,128)} %get-tuple-element.70), channel_id=1, source_target_pairs={{0,6},{1,7},{2,4},{3,5},{4,2},{5,3},{6,0},{7,1},{8,14},{9,15},{10,... | collective-permute-start | bytes 798728 | tf_op jit(solution)/shard_map/ppermute | solution.py:527
  23.7 12.1 %outer.1 = (f32[4,520,128]{2,1,0:T(8,128)S(1)}, f32[520,128]{1,0:T(8,128)}) custom-call(f32[24,128]{1,0:T(8,128)S(1)} %get-tuple-element.60.own, f32[1,2,32,32,128]{4,3,2,1,0:T(8,128)S(1)} %copy-done, f32[1,2,32,32,128]{4,3,2,1,0:T(8,128)S(1)} %copy-done.1, f32[33,8,128]{2,1,0:T(8,128)S(1)} %collective-permute-done.4.y_lo, ...), custom_call_target="tpu_custom_call" | custom-call | flops 100000000 | bytes 41943040 | tf_op jit(solution)/shard_map/outer/pallas_call | solution.py:393
  35.9 1.4 %collective-permute-start.9 = (f32[520,128]{1,0:T(8,128)}, f32[520,128]{1,0:T(8,128)S(1)}, u32[]{:S(2)}, u32[]{:S(2)}) collective-permute-start(f32[520,128]{1,0:T(8,128)} %get-tuple-element.71), channel_id=1, source_target_pairs={{0,7},{1,6},{2,5},{3,4},{4,3},{5,2},{6,1},{7,0},{8,15},{9,14},{10,... | collective-permute-start | bytes 798728 | tf_op jit(solution)/shard_map/ppermute | solution.py:527
  37.3 25.9 %conditional.4 = (f32[4,520,128]{2,1,0:T(8,128)S(1)}) conditional(s32[]{:T(128)} %bitcast, f32[4,520,128]{2,1,0:T(8,128)S(1)} %get-tuple-element.68, f32[4,520,128]{2,1,0:T(8,128)S(1)} %get-tuple-element.68), branch_computations={%region_2.0_spmd, %region_3.0_spmd} | conditional | bytes 2129928 | solution.py:535
  37.3 25.9 %all_to_all.17 = f32[4,520,128]{2,1,0:T(8,128)S(1)} all-to-all(f32[4,520,128]{2,1,0:T(8,128)S(1)} %param.3), channel_id=1, replica_groups={{0,1,2,3},{4,5,6,7},{8,9,10,11},{12,13,14,15},{16,17,18,19},{20,21,22,2..., dimensions={0} | all-to-all | bytes 2129920 | tf_op jit(solution)/shard_map/cond/branch_1_fun/all_to_all | solution.py:533
  63.2 0.0 collective-permute-done.7.refs_1_
  63.2 0.0 collective-permute-done.6.refs_0_
  63.2 0.0 collective-permute-done.8.refs_2_
  63.2 0.0 collective-permute-done.9.refs_3_
  63.2 0.9 route.1
  64.1 0.1 collective-permute-start.10
  64.2 2.9 %collective-permute-start.11 = (f32[2,256,128]{2,1,0:T(8,128)S(1)}, f32[2,256,128]{2,1,0:T(8,128)S(1)}, u32[]{:S(2)}, u32[]{:S(2)}) collective-permute-start(f32[2,256,128]{2,1,0:T(8,128)S(1)} %get-tuple-element.75), channel_id=1, source_target_pairs={{0,5},{1,4},{2,7},{3,6},{4,1},{5,0},{6,3},{7,2},{8,13},{9,12},{10,... | collective-permute-start | bytes 786440 | tf_op jit(solution)/shard_map/ppermute | solution.py:527
  67.1 1.1 collective-permute-start.12
  68.2 1.8 %collective-permute-start.13 = (f32[2,256,128]{2,1,0:T(8,128)S(1)}, f32[2,256,128]{2,1,0:T(8,128)S(1)}, u32[]{:S(2)}, u32[]{:S(2)}) collective-permute-start(f32[2,256,128]{2,1,0:T(8,128)S(1)} %get-tuple-element.77), channel_id=1, source_target_pairs={{0,7},{1,6},{2,5},{3,4},{4,3},{5,2},{6,1},{7,0},{8,15},{9,14},{10,... | collective-permute-start | bytes 786440 | tf_op jit(solution)/shard_map/ppermute | solution.py:527
  70.0 34.9 %conditional.5 = (f32[4,2,256,128]{3,2,1,0:T(8,128)S(1)}) conditional(s32[]{:T(128)} %bitcast, f32[4,2,256,128]{3,2,1,0:T(8,128)S(1)} %get-tuple-element.73, f32[4,2,256,128]{3,2,1,0:T(8,128)S(1)} %get-tuple-element.73), branch_computations={%region_4.0_spmd, %region_5.0_spmd} | conditional | bytes 2097160 | solution.py:535
  70.0 34.9 %all_to_all.19 = f32[4,2,256,128]{3,2,1,0:T(8,128)S(1)} all-to-all(f32[4,2,256,128]{3,2,1,0:T(8,128)S(1)} %param.5), channel_id=1, replica_groups={{0,1,2,3},{4,5,6,7},{8,9,10,11},{12,13,14,15},{16,17,18,19},{20,21,22,2..., dimensions={0} | all-to-all | bytes 2097152 | tf_op jit(solution)/shard_map/cond/branch_1_fun/all_to_all | solution.py:533
  105.0 0.0 collective-permute-done.10.refs_0_
  105.0 0.0 collective-permute-done.11.refs_1_
  105.0 0.7 collective-permute-done.12.refs_2_
  105.7 5.4 %collective-permute-done.13.refs_3_ = f32[2,256,128]{2,1,0:T(8,128)S(1)} collective-permute-done((f32[2,256,128]{2,1,0:T(8,128)S(1)}, f32[2,256,128]{2,1,0:T(8,128)S(1)}, u32[]{:S(2)}, u32[]{:S(2)}) %collective-permute-start.13) | collective-permute-done | bytes 262176 | tf_op jit(solution)/shard_map/ppermute | solution.py:527
  111.0 2.0 %settle.1 = (f32[1,2,32,32,128]{4,3,2,1,0:T(8,128)}, f32[1,2,32,32,128]{4,3,2,1,0:T(8,128)}) custom-call(s32[16]{0:T(128)S(1)} %get-tuple-element.72.table, f32[4,2,256,128]{3,2,1,0:T(8,128)S(1)} %get-tuple-element.85.near, f32[2,256,128]{2,1,0:T(8,128)S(1)} %collective-permute-done.10.refs_0_, f32[2,256,128]{2,1,0:T(8,128)S(1)} %collective-permute-done.11.refs_1_, ...), custom_call_target="tpu_custom_call" | custom-call | tf_op jit(solution)/shard_map/settle/pallas_call | solution.py:507
  (1 shorter events, 0.0 us)
Async XLA Ops:
  0.6 5.0 %copy-start.1 = (f32[1,2,32,32,128]{4,3,2,1,0:T(8,128)S(1)}, f32[1,2,32,32,128]{4,3,2,1,0:T(8,128)}, u32[]{:S(2)}) copy-start(f32[1,2,32,32,128]{4,3,2,1,0:T(8,128)} %solute.3) | copy-start | bytes 3145732
  0.6 5.0 %copy-start = (f32[1,2,32,32,128]{4,3,2,1,0:T(8,128)S(1)}, f32[1,2,32,32,128]{4,3,2,1,0:T(8,128)}, u32[]{:S(2)}) copy-start(f32[1,2,32,32,128]{4,3,2,1,0:T(8,128)} %phase.3) | copy-start | bytes 3145732
  2.7 10.6 %copy-start.2 = (s32[1,2]{1,0:T(1,128)S(1)}, s32[1,2]{1,0:T(1,128)}, u32[]{:S(2)}) copy-start(s32[1,2]{1,0:T(1,128)} %owner.1) | copy-start | bytes 28
  2.7 10.7 %collective-permute-start.4 = (f32[33,8,128]{2,1,0:T(8,128)}, f32[33,8,128]{2,1,0:T(8,128)S(1)}, u32[]{:S(2)}, u32[]{:S(2)}) collective-permute-start(f32[33,8,128]{2,1,0:T(8,128)} %get-tuple-element.61), channel_id=1, source_target_pairs={{0,1},{1,2},{2,3},{3,4},{4,5},{5,6},{6,7},{7,0},{8,9},{9,10},{10,1... | collective-permute-start | bytes 405512 | tf_op jit(solution)/shard_map/ppermute | solution.py:547
  4.2 9.2 %collective-permute-start.5 = (f32[33,8,128]{2,1,0:T(8,128)}, f32[33,8,128]{2,1,0:T(8,128)S(1)}, u32[]{:S(2)}, u32[]{:S(2)}) collective-permute-start(f32[33,8,128]{2,1,0:T(8,128)} %get-tuple-element.62), channel_id=1, source_target_pairs={{0,7},{1,0},{2,1},{3,2},{4,3},{5,4},{6,5},{7,6},{8,15},{9,8},{10,9... | collective-permute-start | bytes 405512 | tf_op jit(solution)/shard_map/ppermute | solution.py:548
  10.3 52.9 %collective-permute-start.7 = (f32[520,128]{1,0:T(8,128)}, f32[520,128]{1,0:T(8,128)S(1)}, u32[]{:S(2)}, u32[]{:S(2)}) collective-permute-start(f32[520,128]{1,0:T(8,128)} %get-tuple-element.69), channel_id=1, source_target_pairs={{0,5},{1,4},{2,7},{3,6},{4,1},{5,0},{6,3},{7,2},{8,13},{9,12},{10,... | collective-permute-start | bytes 798728 | tf_op jit(solution)/shard_map/ppermute | solution.py:527
  13.0 50.2 %collective-permute-start.6 = (f32[520,128]{1,0:T(8,128)S(1)}, f32[520,128]{1,0:T(8,128)S(1)}, u32[]{:S(2)}, u32[]{:S(2)}) collective-permute-start(f32[520,128]{1,0:T(8,128)S(1)} %get-tuple-element.63._), channel_id=1, source_target_pairs={{0,4},{1,5},{2,6},{3,7},{4,0},{5,1},{6,2},{7,3},{8,12},{9,13},{10,... | collective-permute-start | bytes 798728 | tf_op jit(solution)/shard_map/ppermute | solution.py:527
  13.4 8.0 %collective-permute-start.2 = (f32[608,128]{1,0:T(8,128)S(1)}, f32[608,128]{1,0:T(8,128)}, u32[]{:S(2)}, u32[]{:S(2)}) collective-permute-start(f32[608,128]{1,0:T(8,128)S(1)} %get-tuple-element.35), channel_id=1, source_target_pairs={{0,8},{8,16},{16,24},{24,0},{1,9},{9,17},{17,25},{25,1},{2,10},{10... | collective-permute-start | bytes 933896 | tf_op jit(solution)/shard_map/cond/branch_1_fun/ppermute | solution.py:565
  13.5 8.7 %collective-permute-start.3 = (f32[608,128]{1,0:T(8,128)S(1)}, f32[608,128]{1,0:T(8,128)}, u32[]{:S(2)}, u32[]{:S(2)}) collective-permute-start(f32[608,128]{1,0:T(8,128)S(1)} %get-tuple-element.36), channel_id=1, source_target_pairs={{0,24},{8,0},{16,8},{24,16},{1,25},{9,1},{17,9},{25,17},{2,26},{10... | collective-permute-start | bytes 933896 | tf_op jit(solution)/shard_map/cond/branch_1_fun/ppermute | solution.py:565
  22.2 41.0 %collective-permute-start.8 = (f32[520,128]{1,0:T(8,128)}, f32[520,128]{1,0:T(8,128)S(1)}, u32[]{:S(2)}, u32[]{:S(2)}) collective-permute-start(f32[520,128]{1,0:T(8,128)} %get-tuple-element.70), channel_id=1, source_target_pairs={{0,6},{1,7},{2,4},{3,5},{4,2},{5,3},{6,0},{7,1},{8,14},{9,15},{10,... | collective-permute-start | bytes 798728 | tf_op jit(solution)/shard_map/ppermute | solution.py:527
  35.9 27.3 %collective-permute-start.9 = (f32[520,128]{1,0:T(8,128)}, f32[520,128]{1,0:T(8,128)S(1)}, u32[]{:S(2)}, u32[]{:S(2)}) collective-permute-start(f32[520,128]{1,0:T(8,128)} %get-tuple-element.71), channel_id=1, source_target_pairs={{0,7},{1,6},{2,5},{3,4},{4,3},{5,2},{6,1},{7,0},{8,15},{9,14},{10,... | collective-permute-start | bytes 798728 | tf_op jit(solution)/shard_map/ppermute | solution.py:527
  64.1 40.9 %collective-permute-start.10 = (f32[2,256,128]{2,1,0:T(8,128)S(1)}, f32[2,256,128]{2,1,0:T(8,128)S(1)}, u32[]{:S(2)}, u32[]{:S(2)}) collective-permute-start(f32[2,256,128]{2,1,0:T(8,128)S(1)} %get-tuple-element.74), channel_id=1, source_target_pairs={{0,4},{1,5},{2,6},{3,7},{4,0},{5,1},{6,2},{7,3},{8,12},{9,13},{10,... | collective-permute-start | bytes 786440 | tf_op jit(solution)/shard_map/ppermute | solution.py:527
  64.2 40.8 %collective-permute-start.11 = (f32[2,256,128]{2,1,0:T(8,128)S(1)}, f32[2,256,128]{2,1,0:T(8,128)S(1)}, u32[]{:S(2)}, u32[]{:S(2)}) collective-permute-start(f32[2,256,128]{2,1,0:T(8,128)S(1)} %get-tuple-element.75), channel_id=1, source_target_pairs={{0,5},{1,4},{2,7},{3,6},{4,1},{5,0},{6,3},{7,2},{8,13},{9,12},{10,... | collective-permute-start | bytes 786440 | tf_op jit(solution)/shard_map/ppermute | solution.py:527
  67.1 38.6 %collective-permute-start.12 = (f32[2,256,128]{2,1,0:T(8,128)S(1)}, f32[2,256,128]{2,1,0:T(8,128)S(1)}, u32[]{:S(2)}, u32[]{:S(2)}) collective-permute-start(f32[2,256,128]{2,1,0:T(8,128)S(1)} %get-tuple-element.76), channel_id=1, source_target_pairs={{0,6},{1,7},{2,4},{3,5},{4,2},{5,3},{6,0},{7,1},{8,14},{9,15},{10,... | collective-permute-start | bytes 786440 | tf_op jit(solution)/shard_map/ppermute | solution.py:527
  68.2 42.9 %collective-permute-start.13 = (f32[2,256,128]{2,1,0:T(8,128)S(1)}, f32[2,256,128]{2,1,0:T(8,128)S(1)}, u32[]{:S(2)}, u32[]{:S(2)}) collective-permute-start(f32[2,256,128]{2,1,0:T(8,128)S(1)} %get-tuple-element.77), channel_id=1, source_target_pairs={{0,7},{1,6},{2,5},{3,4},{4,3},{5,2},{6,1},{7,0},{8,15},{9,14},{10,... | collective-permute-start | bytes 786440 | tf_op jit(solution)/shard_map/ppermute | solution.py:527

commit v17 on v15

--- a/solution.py
+++ b/solution.py
@@ -535,6 +535,10 @@
     return lax.cond(together, exchange, exchange, values)
 
 
+def in_vmem(values):
+    return pltpu.with_memory_space_constraint(values, pltpu.VMEM)
+
+
 def per_device(phase, solute, undercool, mobility, diffusivity, owner):
     _, tiles, edge, _, depth = phase.shape
     plan = Plan(lax.axis_size("gy"), tiles, edge, depth)
@@ -561,11 +565,11 @@
 
     (x_lo, x_hi), second = lax.cond(together, around, around, to_next, to_prev, own, phase, solute)
     send_far(1, second)
-    near, *third = run_outer(plan, own, phase, solute, (y_lo, y_hi, x_lo, x_hi))
+    near, *third = run_outer(plan, own, phase, solute, (y_lo, y_hi, in_vmem(x_lo), in_vmem(x_hi)))
     send_far(2, third)
     far = [far[index] for index in range(half)]
     near = among_half(plan, near, together)
-    near, far, table = route(plan, near, far)
+    near, far, table = route(plan, in_vmem(near), far)
     far = [swap(values, half + index) for index, values in enumerate(far)]
     near = among_half(plan, near, together)
     return tuple(settle(plan, table, near, far))

time: 114 us -> 114 us (level)
    pallas_call x1, Pallas kernels: 2.2 us -> 0.9 us  [route(): pl.pallas_call(functools.partial(route_kernel, plan), in_specs=[vmem] * (...]
  transfers between devices with their start and end apart: 12 -> 12, of which waited for: 4 -> 4; matrix products, arithmetic and copies ran while one was open for 0% -> 0% of each run, Pallas kernels for 17% -> 18%
where the time goes in v17:
time: 114 us; the launch traced here: 113 us
  blocking collectives  60.5 us (53%)
  Pallas kernels  24.9 us (22%)
  starting transfers between devices  16.8 us (15%)
  waiting for transfers between devices  10.1 us (9%)
    all_to_all x2, blocking collectives, exchange(): lax.all_to_all(values, 'gy', 0, 0, axis_index_groups=groups, tiled=True)  60.5 us
    ppermute x8, starting transfers between devices, swap(): lax.ppermute(values, 'gy', [(i, i ^ mask) for i in range(lax.axis_size('g...  12.1 us
    pallas_call x1, Pallas kernels, run_outer(): pl.pallas_call(functools.partial(outer_kernel, plan), in_specs=[vmem] * 7...  11.8 us
    pallas_call x2, Pallas kernels, run_inner(): pl.pallas_call(functools.partial(inner_kernel, plan, batch), in_specs=[vm...  8.27 us
    ppermute x8, waiting for transfers between devices, swap(): lax.ppermute(values, 'gy', [(i, i ^ mask) for i in range(lax.axis_size('g...  6.31 us
    ppermute x1, waiting for transfers between devices, ring_swap(): lax.ppermute(low, 'gx', ring('gx', 1))  3.08 us
  transfers between devices with their start and end apart: 12, of which 4 were waited for; matrix products, arithmetic and copies ran while one was open for 0% of the time, Pallas kernels for 18%

profile of v17, /device:TPU:8, one launch (start us, length us, event | category | flops | bytes accessed | tf_op | source)
XLA Modules:
  0.0 113.2 jit_solution(5895764027376097095)
XLA Ops:
  0.6 0.0 copy-start
  0.6 2.0 %pack_y.1 = (f32[33,8,128]{2,1,0:T(8,128)}, f32[33,8,128]{2,1,0:T(8,128)}, f32[24,128]{1,0:T(8,128)S(1)}) custom-call(f32[1,2]{1,0:T(1,128)} %under.1, f32[1,2]{1,0:T(1,128)} %mobile.1, f32[1,2]{1,0:T(1,128)} %spread.1, s32[1,2]{1,0:T(1,128)} %owner.1, f32[1,2,32,32,128]{4,3,2,1,0:T(8,128)} %phase.3, f32[1,2,32,32,128]{4,3,2,1,0:T(8,128)} %phase.3, ...), custom_call_target="tpu_custom_call" | custom-call | tf_op jit(solution)/shard_map/pack_y/pallas_call | solution.py:48
  2.6 0.0 copy-start.2
  2.6 0.0 copy-start.1
  2.6 1.6 %collective-permute-start.4 = (f32[33,8,128]{2,1,0:T(8,128)}, f32[33,8,128]{2,1,0:T(8,128)S(1)}, u32[]{:S(2)}, u32[]{:S(2)}) collective-permute-start(f32[33,8,128]{2,1,0:T(8,128)} %get-tuple-element.61), channel_id=1, source_target_pairs={{0,1},{1,2},{2,3},{3,4},{4,5},{5,6},{6,7},{7,0},{8,9},{9,10},{10,1... | collective-permute-start | bytes 405512 | tf_op jit(solution)/shard_map/ppermute | solution.py:547
  4.2 1.4 %collective-permute-start.5 = (f32[33,8,128]{2,1,0:T(8,128)}, f32[33,8,128]{2,1,0:T(8,128)S(1)}, u32[]{:S(2)}, u32[]{:S(2)}) collective-permute-start(f32[33,8,128]{2,1,0:T(8,128)} %get-tuple-element.62), channel_id=1, source_target_pairs={{0,7},{1,0},{2,1},{3,2},{4,3},{5,4},{6,5},{7,6},{8,15},{9,8},{10,9... | collective-permute-start | bytes 405512 | tf_op jit(solution)/shard_map/ppermute | solution.py:548
  5.6 0.0 copy-done
  5.6 5.2 %inner.5 = (f32[520,128]{1,0:T(8,128)S(1)}, f32[520,128]{1,0:T(8,128)S(1)}) custom-call(f32[24,128]{1,0:T(8,128)S(1)} %get-tuple-element.60.own, f32[1,2,32,32,128]{4,3,2,1,0:T(8,128)S(1)} %copy-done, f32[1,2,32,32,128]{4,3,2,1,0:T(8,128)} %solute.3), custom_call_target="tpu_custom_call" | custom-call | flops 100000000 | bytes 25165824 | tf_op jit(solution)/shard_map/inner/pallas_call | solution.py:290
  10.8 2.7 %collective-permute-start.7 = (f32[520,128]{1,0:T(8,128)S(1)}, f32[520,128]{1,0:T(8,128)S(1)}, u32[]{:S(2)}, u32[]{:S(2)}) collective-permute-start(f32[520,128]{1,0:T(8,128)S(1)} %get-tuple-element.69), channel_id=1, source_target_pairs={{0,5},{1,4},{2,7},{3,6},{4,1},{5,0},{6,3},{7,2},{8,13},{9,12},{10,... | collective-permute-start | bytes 798728 | tf_op jit(solution)/shard_map/ppermute | solution.py:527
  13.5 0.3 collective-permute-start.6
  13.8 0.0 copy-done.2
  13.9 0.0 collective-permute-done.4.y_lo
  13.9 0.0 collective-permute-done.5.y_hi
  13.9 0.0 copy-done.1
  14.0 8.7 %conditional.3 = (f32[608,128]{1,0:T(8,128)}, f32[608,128]{1,0:T(8,128)}, f32[520,128]{1,0:T(8,128)S(1)}) conditional(s32[]{:T(128)} %bitcast, (f32[608,128]{1,0:T(8,128)S(1)}, f32[608,128]{1,0:T(8,128)S(1)}, f32[24,128]{1,0:T(8,128)S(1)}, f32[1,2,32,32,128]{4,3,2,1,0:T(8,128)S(1)}, f32[1,2,32,32,128]{4,3,2,1,0:T(8,128)S(1)}) %tuple.36, ...), branch_computations={%region_0.0_spmd, %region_1.0_spmd} | conditional | flops 100000000 | bytes 27656296 | solution.py:566
  14.0 0.1 collective-permute-start.2
  14.1 1.7 %collective-permute-start.3 = (f32[608,128]{1,0:T(8,128)S(1)}, f32[608,128]{1,0:T(8,128)}, u32[]{:S(2)}, u32[]{:S(2)}) collective-permute-start(f32[608,128]{1,0:T(8,128)S(1)} %get-tuple-element.36), channel_id=1, source_target_pairs={{0,24},{8,0},{16,8},{24,16},{1,25},{9,1},{17,9},{25,17},{2,26},{10... | collective-permute-start | bytes 933896 | tf_op jit(solution)/shard_map/cond/branch_1_fun/ppermute | solution.py:564
  15.8 3.1 %inner.4 = f32[520,128]{1,0:T(8,128)S(1)} custom-call(f32[24,128]{1,0:T(8,128)S(1)} %get-tuple-element.37.own, f32[1,2,32,32,128]{4,3,2,1,0:T(8,128)S(1)} %get-tuple-element.38.phase, f32[1,2,32,32,128]{4,3,2,1,0:T(8,128)S(1)} %get-tuple-element.39.solute), custom_call_target="tpu_custom_call" | custom-call | flops 100000000 | bytes 25165824 | tf_op jit(solution)/shard_map/cond/branch_1_fun/inner/pallas_call | solution.py:290
  18.9 3.1 %collective-permute-done.2 = f32[608,128]{1,0:T(8,128)} collective-permute-done((f32[608,128]{1,0:T(8,128)S(1)}, f32[608,128]{1,0:T(8,128)}, u32[]{:S(2)}, u32[]{:S(2)}) %collective-permute-start.2) | collective-permute-done | bytes 311328 | tf_op jit(solution)/shard_map/cond/branch_1_fun/ppermute | solution.py:564
  21.9 0.8 collective-permute-done.3
  22.7 1.6 %collective-permute-start.8 = (f32[520,128]{1,0:T(8,128)S(1)}, f32[520,128]{1,0:T(8,128)S(1)}, u32[]{:S(2)}, u32[]{:S(2)}) collective-permute-start(f32[520,128]{1,0:T(8,128)S(1)} %get-tuple-element.70), channel_id=1, source_target_pairs={{0,6},{1,7},{2,4},{3,5},{4,2},{5,3},{6,0},{7,1},{8,14},{9,15},{10,... | collective-permute-start | bytes 798728 | tf_op jit(solution)/shard_map/ppermute | solution.py:527
  24.3 11.8 %outer.1 = (f32[4,520,128]{2,1,0:T(8,128)S(1)}, f32[520,128]{1,0:T(8,128)S(1)}) custom-call(f32[24,128]{1,0:T(8,128)S(1)} %get-tuple-element.60.own, f32[1,2,32,32,128]{4,3,2,1,0:T(8,128)S(1)} %copy-done, f32[1,2,32,32,128]{4,3,2,1,0:T(8,128)} %solute.3, f32[33,8,128]{2,1,0:T(8,128)S(1)} %collective-permute-done.4.y_lo, ...), custom_call_target="tpu_custom_call" | custom-call | flops 100000000 | bytes 41943040 | tf_op jit(solution)/shard_map/outer/pallas_call | solution.py:393
  36.1 1.5 %collective-permute-start.9 = (f32[520,128]{1,0:T(8,128)S(1)}, f32[520,128]{1,0:T(8,128)S(1)}, u32[]{:S(2)}, u32[]{:S(2)}) collective-permute-start(f32[520,128]{1,0:T(8,128)S(1)} %get-tuple-element.71), channel_id=1, source_target_pairs={{0,7},{1,6},{2,5},{3,4},{4,3},{5,2},{6,1},{7,0},{8,15},{9,14},{10,... | collective-permute-start | bytes 798728 | tf_op jit(solution)/shard_map/ppermute | solution.py:527
  37.6 25.9 %conditional.4 = (f32[4,520,128]{2,1,0:T(8,128)S(1)}) conditional(s32[]{:T(128)} %bitcast, f32[4,520,128]{2,1,0:T(8,128)S(1)} %get-tuple-element.68, f32[4,520,128]{2,1,0:T(8,128)S(1)} %get-tuple-element.68), branch_computations={%region_2.0_spmd, %region_3.0_spmd} | conditional | bytes 2129928 | solution.py:535
  37.6 25.9 %all_to_all.17 = f32[4,520,128]{2,1,0:T(8,128)S(1)} all-to-all(f32[4,520,128]{2,1,0:T(8,128)S(1)} %param.3), channel_id=1, replica_groups={{0,1,2,3},{4,5,6,7},{8,9,10,11},{12,13,14,15},{16,17,18,19},{20,21,22,2..., dimensions={0} | all-to-all | bytes 2129920 | tf_op jit(solution)/shard_map/cond/branch_1_fun/all_to_all | solution.py:533
  63.5 0.0 collective-permute-done.7.refs_1_
  63.5 0.0 collective-permute-done.6.refs_0_
  63.5 0.0 collective-permute-done.8.refs_2_
  63.5 0.0 collective-permute-done.9.refs_3_
  63.5 0.9 route.1
  64.4 0.1 collective-permute-start.10
  64.5 2.9 %collective-permute-start.11 = (f32[2,256,128]{2,1,0:T(8,128)S(1)}, f32[2,256,128]{2,1,0:T(8,128)S(1)}, u32[]{:S(2)}, u32[]{:S(2)}) collective-permute-start(f32[2,256,128]{2,1,0:T(8,128)S(1)} %get-tuple-element.75), channel_id=1, source_target_pairs={{0,5},{1,4},{2,7},{3,6},{4,1},{5,0},{6,3},{7,2},{8,13},{9,12},{10,... | collective-permute-start | bytes 786440 | tf_op jit(solution)/shard_map/ppermute | solution.py:527
  67.4 1.0 collective-permute-start.12
  68.4 1.9 %collective-permute-start.13 = (f32[2,256,128]{2,1,0:T(8,128)S(1)}, f32[2,256,128]{2,1,0:T(8,128)S(1)}, u32[]{:S(2)}, u32[]{:S(2)}) collective-permute-start(f32[2,256,128]{2,1,0:T(8,128)S(1)} %get-tuple-element.77), channel_id=1, source_target_pairs={{0,7},{1,6},{2,5},{3,4},{4,3},{5,2},{6,1},{7,0},{8,15},{9,14},{10,... | collective-permute-start | bytes 786440 | tf_op jit(solution)/shard_map/ppermute | solution.py:527
  70.3 34.7 %conditional.5 = (f32[4,2,256,128]{3,2,1,0:T(8,128)S(1)}) conditional(s32[]{:T(128)} %bitcast, f32[4,2,256,128]{3,2,1,0:T(8,128)S(1)} %get-tuple-element.73, f32[4,2,256,128]{3,2,1,0:T(8,128)S(1)} %get-tuple-element.73), branch_computations={%region_4.0_spmd, %region_5.0_spmd} | conditional | bytes 2097160 | solution.py:535
  70.3 34.7 %all_to_all.19 = f32[4,2,256,128]{3,2,1,0:T(8,128)S(1)} all-to-all(f32[4,2,256,128]{3,2,1,0:T(8,128)S(1)} %param.5), channel_id=1, replica_groups={{0,1,2,3},{4,5,6,7},{8,9,10,11},{12,13,14,15},{16,17,18,19},{20,21,22,2..., dimensions={0} | all-to-all | bytes 2097152 | tf_op jit(solution)/shard_map/cond/branch_1_fun/all_to_all | solution.py:533
  105.0 0.0 collective-permute-done.10.refs_0_
  105.0 0.0 collective-permute-done.11.refs_1_
  105.0 0.9 collective-permute-done.12.refs_2_
  105.9 5.4 %collective-permute-done.13.refs_3_ = f32[2,256,128]{2,1,0:T(8,128)S(1)} collective-permute-done((f32[2,256,128]{2,1,0:T(8,128)S(1)}, f32[2,256,128]{2,1,0:T(8,128)S(1)}, u32[]{:S(2)}, u32[]{:S(2)}) %collective-permute-start.13) | collective-permute-done | bytes 262176 | tf_op jit(solution)/shard_map/ppermute | solution.py:527
  111.3 2.0 %settle.1 = (f32[1,2,32,32,128]{4,3,2,1,0:T(8,128)}, f32[1,2,32,32,128]{4,3,2,1,0:T(8,128)}) custom-call(s32[16]{0:T(128)S(1)} %get-tuple-element.72.table, f32[4,2,256,128]{3,2,1,0:T(8,128)S(1)} %get-tuple-element.85.near, f32[2,256,128]{2,1,0:T(8,128)S(1)} %collective-permute-done.10.refs_0_, f32[2,256,128]{2,1,0:T(8,128)S(1)} %collective-permute-done.11.refs_1_, ...), custom_call_target="tpu_custom_call" | custom-call | tf_op jit(solution)/shard_map/settle/pallas_call | solution.py:507
  (1 shorter events, 0.0 us)
Async XLA Ops:
  0.6 4.9 %copy-start = (f32[1,2,32,32,128]{4,3,2,1,0:T(8,128)S(1)}, f32[1,2,32,32,128]{4,3,2,1,0:T(8,128)}, u32[]{:S(2)}) copy-start(f32[1,2,32,32,128]{4,3,2,1,0:T(8,128)} %phase.3) | copy-start | bytes 3145732
  2.6 11.2 %copy-start.2 = (s32[1,2]{1,0:T(1,128)S(1)}, s32[1,2]{1,0:T(1,128)}, u32[]{:S(2)}) copy-start(s32[1,2]{1,0:T(1,128)} %owner.1) | copy-start | bytes 28
  2.6 11.3 %copy-start.1 = (f32[1,2,32,32,128]{4,3,2,1,0:T(8,128)S(1)}, f32[1,2,32,32,128]{4,3,2,1,0:T(8,128)}, u32[]{:S(2)}) copy-start(f32[1,2,32,32,128]{4,3,2,1,0:T(8,128)} %solute.3) | copy-start | bytes 3145732
  2.6 11.3 %collective-permute-start.4 = (f32[33,8,128]{2,1,0:T(8,128)}, f32[33,8,128]{2,1,0:T(8,128)S(1)}, u32[]{:S(2)}, u32[]{:S(2)}) collective-permute-start(f32[33,8,128]{2,1,0:T(8,128)} %get-tuple-element.61), channel_id=1, source_target_pairs={{0,1},{1,2},{2,3},{3,4},{4,5},{5,6},{6,7},{7,0},{8,9},{9,10},{10,1... | collective-permute-start | bytes 405512 | tf_op jit(solution)/shard_map/ppermute | solution.py:547
  4.2 9.7 %collective-permute-start.5 = (f32[33,8,128]{2,1,0:T(8,128)}, f32[33,8,128]{2,1,0:T(8,128)S(1)}, u32[]{:S(2)}, u32[]{:S(2)}) collective-permute-start(f32[33,8,128]{2,1,0:T(8,128)} %get-tuple-element.62), channel_id=1, source_target_pairs={{0,7},{1,0},{2,1},{3,2},{4,3},{5,4},{6,5},{7,6},{8,15},{9,8},{10,9... | collective-permute-start | bytes 405512 | tf_op jit(solution)/shard_map/ppermute | solution.py:548
  10.8 52.7 %collective-permute-start.7 = (f32[520,128]{1,0:T(8,128)S(1)}, f32[520,128]{1,0:T(8,128)S(1)}, u32[]{:S(2)}, u32[]{:S(2)}) collective-permute-start(f32[520,128]{1,0:T(8,128)S(1)} %get-tuple-element.69), channel_id=1, source_target_pairs={{0,5},{1,4},{2,7},{3,6},{4,1},{5,0},{6,3},{7,2},{8,13},{9,12},{10,... | collective-permute-start | bytes 798728 | tf_op jit(solution)/shard_map/ppermute | solution.py:527
  13.5 50.0 %collective-permute-start.6 = (f32[520,128]{1,0:T(8,128)S(1)}, f32[520,128]{1,0:T(8,128)S(1)}, u32[]{:S(2)}, u32[]{:S(2)}) collective-permute-start(f32[520,128]{1,0:T(8,128)S(1)} %get-tuple-element.63._), channel_id=1, source_target_pairs={{0,4},{1,5},{2,6},{3,7},{4,0},{5,1},{6,2},{7,3},{8,12},{9,13},{10,... | collective-permute-start | bytes 798728 | tf_op jit(solution)/shard_map/ppermute | solution.py:527
  14.0 8.0 %collective-permute-start.2 = (f32[608,128]{1,0:T(8,128)S(1)}, f32[608,128]{1,0:T(8,128)}, u32[]{:S(2)}, u32[]{:S(2)}) collective-permute-start(f32[608,128]{1,0:T(8,128)S(1)} %get-tuple-element.35), channel_id=1, source_target_pairs={{0,8},{8,16},{16,24},{24,0},{1,9},{9,17},{17,25},{25,1},{2,10},{10... | collective-permute-start | bytes 933896 | tf_op jit(solution)/shard_map/cond/branch_1_fun/ppermute | solution.py:564
  14.1 8.7 %collective-permute-start.3 = (f32[608,128]{1,0:T(8,128)S(1)}, f32[608,128]{1,0:T(8,128)}, u32[]{:S(2)}, u32[]{:S(2)}) collective-permute-start(f32[608,128]{1,0:T(8,128)S(1)} %get-tuple-element.36), channel_id=1, source_target_pairs={{0,24},{8,0},{16,8},{24,16},{1,25},{9,1},{17,9},{25,17},{2,26},{10... | collective-permute-start | bytes 933896 | tf_op jit(solution)/shard_map/cond/branch_1_fun/ppermute | solution.py:564
  22.7 40.8 %collective-permute-start.8 = (f32[520,128]{1,0:T(8,128)S(1)}, f32[520,128]{1,0:T(8,128)S(1)}, u32[]{:S(2)}, u32[]{:S(2)}) collective-permute-start(f32[520,128]{1,0:T(8,128)S(1)} %get-tuple-element.70), channel_id=1, source_target_pairs={{0,6},{1,7},{2,4},{3,5},{4,2},{5,3},{6,0},{7,1},{8,14},{9,15},{10,... | collective-permute-start | bytes 798728 | tf_op jit(solution)/shard_map/ppermute | solution.py:527
  36.1 27.4 %collective-permute-start.9 = (f32[520,128]{1,0:T(8,128)S(1)}, f32[520,128]{1,0:T(8,128)S(1)}, u32[]{:S(2)}, u32[]{:S(2)}) collective-permute-start(f32[520,128]{1,0:T(8,128)S(1)} %get-tuple-element.71), channel_id=1, source_target_pairs={{0,7},{1,6},{2,5},{3,4},{4,3},{5,2},{6,1},{7,0},{8,15},{9,14},{10,... | collective-permute-start | bytes 798728 | tf_op jit(solution)/shard_map/ppermute | solution.py:527
  64.4 40.6 %collective-permute-start.10 = (f32[2,256,128]{2,1,0:T(8,128)S(1)}, f32[2,256,128]{2,1,0:T(8,128)S(1)}, u32[]{:S(2)}, u32[]{:S(2)}) collective-permute-start(f32[2,256,128]{2,1,0:T(8,128)S(1)} %get-tuple-element.74), channel_id=1, source_target_pairs={{0,4},{1,5},{2,6},{3,7},{4,0},{5,1},{6,2},{7,3},{8,12},{9,13},{10,... | collective-permute-start | bytes 786440 | tf_op jit(solution)/shard_map/ppermute | solution.py:527
  64.5 40.5 %collective-permute-start.11 = (f32[2,256,128]{2,1,0:T(8,128)S(1)}, f32[2,256,128]{2,1,0:T(8,128)S(1)}, u32[]{:S(2)}, u32[]{:S(2)}) collective-permute-start(f32[2,256,128]{2,1,0:T(8,128)S(1)} %get-tuple-element.75), channel_id=1, source_target_pairs={{0,5},{1,4},{2,7},{3,6},{4,1},{5,0},{6,3},{7,2},{8,13},{9,12},{10,... | collective-permute-start | bytes 786440 | tf_op jit(solution)/shard_map/ppermute | solution.py:527
  67.4 38.5 %collective-permute-start.12 = (f32[2,256,128]{2,1,0:T(8,128)S(1)}, f32[2,256,128]{2,1,0:T(8,128)S(1)}, u32[]{:S(2)}, u32[]{:S(2)}) collective-permute-start(f32[2,256,128]{2,1,0:T(8,128)S(1)} %get-tuple-element.76), channel_id=1, source_target_pairs={{0,6},{1,7},{2,4},{3,5},{4,2},{5,3},{6,0},{7,1},{8,14},{9,15},{10,... | collective-permute-start | bytes 786440 | tf_op jit(solution)/shard_map/ppermute | solution.py:527
  68.4 42.9 %collective-permute-start.13 = (f32[2,256,128]{2,1,0:T(8,128)S(1)}, f32[2,256,128]{2,1,0:T(8,128)S(1)}, u32[]{:S(2)}, u32[]{:S(2)}) collective-permute-start(f32[2,256,128]{2,1,0:T(8,128)S(1)} %get-tuple-element.77), channel_id=1, source_target_pairs={{0,7},{1,6},{2,5},{3,4},{4,3},{5,2},{6,1},{7,0},{8,15},{9,14},{10,... | collective-permute-start | bytes 786440 | tf_op jit(solution)/shard_map/ppermute | solution.py:527

commit v18 on v15

--- a/solution.py
+++ b/solution.py
@@ -299,11 +299,15 @@
     )(own, phase, solute)
 
 
-def outer_kernel(plan, own, phase, solute, y_lo, y_hi, x_lo, x_hi, out, *rest):
+def outer_kernel(plan, own, phase_in, solute_in, y_lo, y_hi, x_lo, x_hi, out, *rest):
     tiles, edge, depth, half = plan.tiles, plan.edge, plan.depth, plan.half
     late = plan.batches[2]
     far_outs, scratch = rest[: len(late)], rest[len(late) :]
-    pairs, coefs = (scratch[:2], scratch[2:4]), scratch[4]
+    pairs, coefs, phase, solute, sems = (scratch[:2], scratch[2:4]), *scratch[4:]
+    copies = []
+    for field, (source, target) in enumerate(((phase_in, phase), (solute_in, solute))):
+        copies.append(pltpu.make_async_copy(source, target, sems.at[field]))
+        copies[-1].start()
     cols = tiles * edge
     width = cols + 2 * W
     for zone, source in ((0, x_lo), (1, None), (2, x_hi)):
@@ -340,6 +344,8 @@
         )
         return carry
 
+    for copy in copies:
+        copy.wait()
     lax.fori_loop(0, edge, load_row, 0, unroll=UNROLL)
 
     def coefs_of(zone):
@@ -392,10 +398,12 @@
     far = jax.ShapeDtypeStruct((2 * tiles * plan.size + AUX, depth), jnp.float32)
     return pl.pallas_call(
         functools.partial(outer_kernel, plan),
-        in_specs=[vmem] * 7,
+        in_specs=[vmem] + [pl.BlockSpec(memory_space=pl.ANY)] * 2 + [vmem] * 4,
         out_specs=[vmem] * (1 + len(plan.batches[2])),
         out_shape=[near] + [far] * len(plan.batches[2]),
-        scratch_shapes=[buffer] * 4 + [pltpu.VMEM((3, KINDS, width, depth), jnp.float32)],
+        scratch_shapes=[buffer] * 4 + [pltpu.VMEM((3, KINDS, width, depth), jnp.float32)]
+        + [pltpu.VMEM(phase.shape, jnp.float32)] * 2
+        + [pltpu.SemaphoreType.DMA((2,))],
         compiler_params=pltpu.CompilerParams(vmem_limit_bytes=16 * 1024 * 1024),
         cost_estimate=pl.CostEstimate(flops=10**8, bytes_accessed=40 * 1024 * 1024, transcendentals=0),
         name="outer",
@@ -405,30 +413,40 @@
 def route_kernel(plan, near, *refs):
     pieces, tiles, half, size = plan.pieces, plan.tiles, plan.half, 2 * plan.size
     far, near_out, far_outs, table = refs[:half], refs[half], refs[half + 1 : 2 * half + 1], refs[2 * half + 1]
-    held, peers, count = refs[2 * half + 2 :]
+    held, peers, count, names, sems = refs[2 * half + 2 :]
     me = lax.axis_index("gy")
     base = me - lax.rem(me, half)
     tail = tiles * size
+    names_copy = pltpu.make_async_copy(near.at[:, pl.ds(tail, AUX), :], names, sems.at[half * tiles])
+    names_copy.start()
+    copies = []
+    for piece in range(half):
+        for tile in range(tiles):
+            source = near.at[piece, pl.ds(tile * size, size), :]
+            copy = pltpu.make_async_copy(source, held.at[(base + piece) * tiles + tile], sems.at[len(copies)])
+            copy.start()
+            copies.append(copy)
     for tile in range(tiles):
-        for piece in range(half):
-            peer = lax.rem(near[piece, tail, tile].astype(jnp.int32), pieces)
-            peers[(base + piece) * tiles + tile] = peer
         for index in range(half):
             peer = lax.rem(far[index][tail, tile].astype(jnp.int32), pieces)
             peers[(me ^ (half + index)) * tiles + tile] = peer
-    for piece in range(half):
-        for tile in range(tiles):
-            held[(base + piece) * tiles + tile] = near[piece, tile * size : (tile + 1) * size, :]
     for index in range(half):
         for tile in range(tiles):
             held[(me ^ (half + index)) * tiles + tile] = far[index][tile * size : (tile + 1) * size, :]
     for peer in range(pieces):
         count[peer] = 0
+    names_copy.wait()
+    for tile in range(tiles):
+        for piece in range(half):
+            peer = lax.rem(names[piece, 0, tile].astype(jnp.int32), pieces)
+            peers[(base + piece) * tiles + tile] = peer
     for home in range(pieces * tiles):
         peer = peers[home]
         slot = count[peer]
         table[peer * tiles + slot] = home
         count[peer] = slot + 1
+    for copy in copies:
+        copy.wait()
     for index in range(half):
         for slot in range(tiles):
             far_outs[index][slot] = held[table[(me ^ (half + index)) * tiles + slot]]
@@ -442,7 +460,7 @@
     count = plan.pieces * tiles
     results = pl.pallas_call(
         functools.partial(route_kernel, plan),
-        in_specs=[vmem] * (half + 1),
+        in_specs=[pl.BlockSpec(memory_space=pl.ANY)] + [vmem] * half,
         out_specs=[vmem] * (half + 1) + [pl.BlockSpec(memory_space=pltpu.SMEM)],
         out_shape=[jax.ShapeDtypeStruct((half, tiles, size, depth), jnp.float32)]
         + [one] * half
@@ -451,6 +469,8 @@
             pltpu.VMEM((count, size, depth), jnp.float32),
             pltpu.SMEM((count,), jnp.int32),
             pltpu.SMEM((plan.pieces,), jnp.int32),
+            pltpu.SMEM((half, AUX, depth), jnp.float32),
+            pltpu.SemaphoreType.DMA((half * tiles + 1,)),
         ],
         compiler_params=pltpu.CompilerParams(vmem_limit_bytes=16 * 1024 * 1024),
         name="route",

time: 114 us -> 115 us (level)
  transfers between devices with their start and end apart: 12 -> 12, of which waited for: 4 -> 4; matrix products, arithmetic and copies ran while one was open for 0% -> 0% of each run, Pallas kernels for 17% -> 18%
where the time goes in v18:
time: 115 us; the launch traced here: 114 us
  blocking collectives  58.9 us (51%)
  Pallas kernels  26.6 us (23%)
  starting transfers between devices  16.8 us (15%)
  waiting for transfers between devices  10.7 us (9%)
    all_to_all x2, blocking collectives, exchange(): lax.all_to_all(values, 'gy', 0, 0, axis_index_groups=groups, tiled=True)  58.9 us
    pallas_call x1, Pallas kernels, run_outer(): pl.pallas_call(functools.partial(outer_kernel, plan), in_specs=[vmem] + [...  12.7 us
    ppermute x8, starting transfers between devices, swap(): lax.ppermute(values, 'gy', [(i, i ^ mask) for i in range(lax.axis_size('g...  12.1 us
    pallas_call x2, Pallas kernels, run_inner(): pl.pallas_call(functools.partial(inner_kernel, plan, batch), in_specs=[vm...  7.82 us
    ppermute x8, waiting for transfers between devices, swap(): lax.ppermute(values, 'gy', [(i, i ^ mask) for i in range(lax.axis_size('g...  7.57 us
    ppermute x1, waiting for transfers between devices, ring_swap(): lax.ppermute(low, 'gx', ring('gx', 1))  2.35 us
  transfers between devices with their start and end apart: 12, of which 4 were waited for; matrix products, arithmetic and copies ran while one was open for 0% of the time, Pallas kernels for 18%

profile of v18, /device:TPU:8, one launch (start us, length us, event | category | flops | bytes accessed | tf_op | source)
XLA Modules:
  0.0 113.8 jit_solution(8548762216346227402)
XLA Ops:
  0.6 0.0 copy-start.1
  0.6 0.0 copy-start
  0.7 2.0 %pack_y.1 = (f32[33,8,128]{2,1,0:T(8,128)}, f32[33,8,128]{2,1,0:T(8,128)}, f32[24,128]{1,0:T(8,128)S(1)}) custom-call(f32[1,2]{1,0:T(1,128)} %under.1, f32[1,2]{1,0:T(1,128)} %mobile.1, f32[1,2]{1,0:T(1,128)} %spread.1, s32[1,2]{1,0:T(1,128)} %owner.1, f32[1,2,32,32,128]{4,3,2,1,0:T(8,128)} %phase_in.1, f32[1,2,32,32,128]{4,3,2,1,0:T(8,128)} %phase_in.1, ...), custom_call_target="tpu_custom_call" | custom-call | tf_op jit(solution)/shard_map/pack_y/pallas_call | solution.py:48
  2.7 0.0 copy-start.2
  2.7 1.5 %collective-permute-start.4 = (f32[33,8,128]{2,1,0:T(8,128)}, f32[33,8,128]{2,1,0:T(8,128)S(1)}, u32[]{:S(2)}, u32[]{:S(2)}) collective-permute-start(f32[33,8,128]{2,1,0:T(8,128)} %get-tuple-element.61), channel_id=1, source_target_pairs={{0,1},{1,2},{2,3},{3,4},{4,5},{5,6},{6,7},{7,0},{8,9},{9,10},{10,1... | collective-permute-start | bytes 405512 | tf_op jit(solution)/shard_map/ppermute | solution.py:563
  4.2 1.4 %collective-permute-start.5 = (f32[33,8,128]{2,1,0:T(8,128)}, f32[33,8,128]{2,1,0:T(8,128)S(1)}, u32[]{:S(2)}, u32[]{:S(2)}) collective-permute-start(f32[33,8,128]{2,1,0:T(8,128)} %get-tuple-element.62), channel_id=1, source_target_pairs={{0,7},{1,0},{2,1},{3,2},{4,3},{5,4},{6,5},{7,6},{8,15},{9,8},{10,9... | collective-permute-start | bytes 405512 | tf_op jit(solution)/shard_map/ppermute | solution.py:564
  5.6 0.0 copy-done.1
  5.6 0.0 copy-done
  5.6 4.0 %inner.5 = (f32[520,128]{1,0:T(8,128)S(1)}, f32[520,128]{1,0:T(8,128)S(1)}) custom-call(f32[24,128]{1,0:T(8,128)S(1)} %get-tuple-element.60.own, f32[1,2,32,32,128]{4,3,2,1,0:T(8,128)S(1)} %copy-done, f32[1,2,32,32,128]{4,3,2,1,0:T(8,128)S(1)} %copy-done.1), custom_call_target="tpu_custom_call" | custom-call | flops 100000000 | bytes 25165824 | tf_op jit(solution)/shard_map/inner/pallas_call | solution.py:290
  9.6 2.7 %collective-permute-start.7 = (f32[520,128]{1,0:T(8,128)S(1)}, f32[520,128]{1,0:T(8,128)S(1)}, u32[]{:S(2)}, u32[]{:S(2)}) collective-permute-start(f32[520,128]{1,0:T(8,128)S(1)} %get-tuple-element.69), channel_id=1, source_target_pairs={{0,5},{1,4},{2,7},{3,6},{4,1},{5,0},{6,3},{7,2},{8,13},{9,12},{10,... | collective-permute-start | bytes 798728 | tf_op jit(solution)/shard_map/ppermute | solution.py:547
  12.3 0.3 collective-permute-start.6
  12.7 0.0 copy-done.2
  12.7 0.0 collective-permute-done.4.y_lo
  12.7 0.0 collective-permute-done.5.y_hi
  12.8 8.7 %conditional.3 = (f32[608,128]{1,0:T(8,128)}, f32[608,128]{1,0:T(8,128)}, f32[520,128]{1,0:T(8,128)}) conditional(s32[]{:T(128)} %bitcast, (f32[608,128]{1,0:T(8,128)S(1)}, f32[608,128]{1,0:T(8,128)S(1)}, f32[24,128]{1,0:T(8,128)S(1)}, f32[1,2,32,32,128]{4,3,2,1,0:T(8,128)S(1)}, f32[1,2,32,32,128]{4,3,2,1,0:T(8,128)S(1)}) %tuple.36, ...), branch_computations={%region_0.0_spmd, %region_1.0_spmd} | conditional | flops 100000000 | bytes 27656296 | solution.py:582
  12.8 0.1 collective-permute-start.2
  12.9 1.7 %collective-permute-start.3 = (f32[608,128]{1,0:T(8,128)S(1)}, f32[608,128]{1,0:T(8,128)}, u32[]{:S(2)}, u32[]{:S(2)}) collective-permute-start(f32[608,128]{1,0:T(8,128)S(1)} %get-tuple-element.36), channel_id=1, source_target_pairs={{0,24},{8,0},{16,8},{24,16},{1,25},{9,1},{17,9},{25,17},{2,26},{10... | collective-permute-start | bytes 933896 | tf_op jit(solution)/shard_map/cond/branch_1_fun/ppermute | solution.py:580
  14.6 3.8 %inner.4 = f32[520,128]{1,0:T(8,128)} custom-call(f32[24,128]{1,0:T(8,128)S(1)} %get-tuple-element.37.own, f32[1,2,32,32,128]{4,3,2,1,0:T(8,128)S(1)} %get-tuple-element.38.phase, f32[1,2,32,32,128]{4,3,2,1,0:T(8,128)S(1)} %get-tuple-element.39.solute), custom_call_target="tpu_custom_call" | custom-call | flops 100000000 | bytes 25165824 | tf_op jit(solution)/shard_map/cond/branch_1_fun/inner/pallas_call | solution.py:290
  18.4 2.3 %collective-permute-done.2 = f32[608,128]{1,0:T(8,128)} collective-permute-done((f32[608,128]{1,0:T(8,128)S(1)}, f32[608,128]{1,0:T(8,128)}, u32[]{:S(2)}, u32[]{:S(2)}) %collective-permute-start.2) | collective-permute-done | bytes 311328 | tf_op jit(solution)/shard_map/cond/branch_1_fun/ppermute | solution.py:580
  20.8 0.8 collective-permute-done.3
  21.5 1.6 %collective-permute-start.8 = (f32[520,128]{1,0:T(8,128)}, f32[520,128]{1,0:T(8,128)S(1)}, u32[]{:S(2)}, u32[]{:S(2)}) collective-permute-start(f32[520,128]{1,0:T(8,128)} %get-tuple-element.70), channel_id=1, source_target_pairs={{0,6},{1,7},{2,4},{3,5},{4,2},{5,3},{6,0},{7,1},{8,14},{9,15},{10,... | collective-permute-start | bytes 798728 | tf_op jit(solution)/shard_map/ppermute | solution.py:547
  23.1 12.7 %outer.1 = (f32[4,520,128]{2,1,0:T(8,128)S(1)}, f32[520,128]{1,0:T(8,128)S(1)}) custom-call(f32[24,128]{1,0:T(8,128)S(1)} %get-tuple-element.60.own, f32[1,2,32,32,128]{4,3,2,1,0:T(8,128)S(1)} %copy-done, f32[1,2,32,32,128]{4,3,2,1,0:T(8,128)} %solute_in.1, f32[33,8,128]{2,1,0:T(8,128)S(1)} %collective-permute-done.4.y_lo, ...), custom_call_target="tpu_custom_call" | custom-call | flops 100000000 | bytes 41943040 | tf_op jit(solution)/shard_map/outer/pallas_call | solution.py:399
  35.8 1.5 %collective-permute-start.9 = (f32[520,128]{1,0:T(8,128)S(1)}, f32[520,128]{1,0:T(8,128)S(1)}, u32[]{:S(2)}, u32[]{:S(2)}) collective-permute-start(f32[520,128]{1,0:T(8,128)S(1)} %get-tuple-element.71), channel_id=1, source_target_pairs={{0,7},{1,6},{2,5},{3,4},{4,3},{5,2},{6,1},{7,0},{8,15},{9,14},{10,... | collective-permute-start | bytes 798728 | tf_op jit(solution)/shard_map/ppermute | solution.py:547
  37.3 26.6 %conditional.4 = (f32[4,520,128]{2,1,0:T(8,128)}) conditional(s32[]{:T(128)} %bitcast, f32[4,520,128]{2,1,0:T(8,128)S(1)} %get-tuple-element.68, f32[4,520,128]{2,1,0:T(8,128)S(1)} %get-tuple-element.68), branch_computations={%region_2.0_spmd, %region_3.0_spmd} | conditional | bytes 2129928 | solution.py:555
  37.3 26.6 %all_to_all.17 = f32[4,520,128]{2,1,0:T(8,128)} all-to-all(f32[4,520,128]{2,1,0:T(8,128)S(1)} %param.3), channel_id=1, replica_groups={{0,1,2,3},{4,5,6,7},{8,9,10,11},{12,13,14,15},{16,17,18,19},{20,21,22,2..., dimensions={0} | all-to-all | bytes 2129920 | tf_op jit(solution)/shard_map/cond/branch_1_fun/all_to_all | solution.py:553
  63.9 0.0 collective-permute-done.7.refs_1_
  63.9 0.0 collective-permute-done.6.refs_0_
  64.0 0.0 collective-permute-done.8.refs_2_
  64.0 0.0 collective-permute-done.9.refs_3_
  64.0 2.0 %route.1 = (f32[4,2,256,128]{3,2,1,0:T(8,128)S(1)}, f32[2,256,128]{2,1,0:T(8,128)S(1)}, f32[2,256,128]{2,1,0:T(8,128)S(1)}, f32[2,256,128]{2,1,0:T(8,128)S(1)}, ...) custom-call(f32[4,520,128]{2,1,0:T(8,128)} %get-tuple-element.84.near, f32[520,128]{1,0:T(8,128)S(1)} %collective-permute-done.6.refs_0_, ...), custom_call_target="tpu_custom_call" | custom-call | tf_op jit(solution)/shard_map/route/pallas_call | solution.py:461
  66.0 0.1 collective-permute-start.10
  66.1 2.9 %collective-permute-start.11 = (f32[2,256,128]{2,1,0:T(8,128)S(1)}, f32[2,256,128]{2,1,0:T(8,128)S(1)}, u32[]{:S(2)}, u32[]{:S(2)}) collective-permute-start(f32[2,256,128]{2,1,0:T(8,128)S(1)} %get-tuple-element.75), channel_id=1, source_target_pairs={{0,5},{1,4},{2,7},{3,6},{4,1},{5,0},{6,3},{7,2},{8,13},{9,12},{10,... | collective-permute-start | bytes 786440 | tf_op jit(solution)/shard_map/ppermute | solution.py:547
  69.0 0.0 collective-permute-start.12
  69.0 2.9 %collective-permute-start.13 = (f32[2,256,128]{2,1,0:T(8,128)S(1)}, f32[2,256,128]{2,1,0:T(8,128)S(1)}, u32[]{:S(2)}, u32[]{:S(2)}) collective-permute-start(f32[2,256,128]{2,1,0:T(8,128)S(1)} %get-tuple-element.77), channel_id=1, source_target_pairs={{0,7},{1,6},{2,5},{3,4},{4,3},{5,2},{6,1},{7,0},{8,15},{9,14},{10,... | collective-permute-start | bytes 786440 | tf_op jit(solution)/shard_map/ppermute | solution.py:547
  71.9 32.3 %conditional.5 = (f32[4,2,256,128]{3,2,1,0:T(8,128)S(1)}) conditional(s32[]{:T(128)} %bitcast, f32[4,2,256,128]{3,2,1,0:T(8,128)S(1)} %get-tuple-element.73, f32[4,2,256,128]{3,2,1,0:T(8,128)S(1)} %get-tuple-element.73), branch_computations={%region_4.0_spmd, %region_5.0_spmd} | conditional | bytes 2097160 | solution.py:555
  71.9 32.3 %all_to_all.19 = f32[4,2,256,128]{3,2,1,0:T(8,128)S(1)} all-to-all(f32[4,2,256,128]{3,2,1,0:T(8,128)S(1)} %param.5), channel_id=1, replica_groups={{0,1,2,3},{4,5,6,7},{8,9,10,11},{12,13,14,15},{16,17,18,19},{20,21,22,2..., dimensions={0} | all-to-all | bytes 2097152 | tf_op jit(solution)/shard_map/cond/branch_1_fun/all_to_all | solution.py:553
  104.2 0.0 collective-permute-done.10.refs_0_
  104.2 0.0 collective-permute-done.11.refs_1_
  104.2 2.3 %collective-permute-done.12.refs_2_ = f32[2,256,128]{2,1,0:T(8,128)S(1)} collective-permute-done((f32[2,256,128]{2,1,0:T(8,128)S(1)}, f32[2,256,128]{2,1,0:T(8,128)S(1)}, u32[]{:S(2)}, u32[]{:S(2)}) %collective-permute-start.12) | collective-permute-done | bytes 262176 | tf_op jit(solution)/shard_map/ppermute | solution.py:547
  106.5 5.3 %collective-permute-done.13.refs_3_ = f32[2,256,128]{2,1,0:T(8,128)S(1)} collective-permute-done((f32[2,256,128]{2,1,0:T(8,128)S(1)}, f32[2,256,128]{2,1,0:T(8,128)S(1)}, u32[]{:S(2)}, u32[]{:S(2)}) %collective-permute-start.13) | collective-permute-done | bytes 262176 | tf_op jit(solution)/shard_map/ppermute | solution.py:547
  111.8 2.0 %settle.1 = (f32[1,2,32,32,128]{4,3,2,1,0:T(8,128)}, f32[1,2,32,32,128]{4,3,2,1,0:T(8,128)}) custom-call(s32[16]{0:T(128)S(1)} %get-tuple-element.72.table, f32[4,2,256,128]{3,2,1,0:T(8,128)S(1)} %get-tuple-element.85.near, f32[2,256,128]{2,1,0:T(8,128)S(1)} %collective-permute-done.10.refs_0_, f32[2,256,128]{2,1,0:T(8,128)S(1)} %collective-permute-done.11.refs_1_, ...), custom_call_target="tpu_custom_call" | custom-call | tf_op jit(solution)/shard_map/settle/pallas_call | solution.py:527
  (1 shorter events, 0.0 us)
Async XLA Ops:
  0.6 5.0 %copy-start.1 = (f32[1,2,32,32,128]{4,3,2,1,0:T(8,128)S(1)}, f32[1,2,32,32,128]{4,3,2,1,0:T(8,128)}, u32[]{:S(2)}) copy-start(f32[1,2,32,32,128]{4,3,2,1,0:T(8,128)} %solute_in.1) | copy-start | bytes 3145732
  0.6 5.0 %copy-start = (f32[1,2,32,32,128]{4,3,2,1,0:T(8,128)S(1)}, f32[1,2,32,32,128]{4,3,2,1,0:T(8,128)}, u32[]{:S(2)}) copy-start(f32[1,2,32,32,128]{4,3,2,1,0:T(8,128)} %phase_in.1) | copy-start | bytes 3145732
  2.7 10.0 %copy-start.2 = (s32[1,2]{1,0:T(1,128)S(1)}, s32[1,2]{1,0:T(1,128)}, u32[]{:S(2)}) copy-start(s32[1,2]{1,0:T(1,128)} %owner.1) | copy-start | bytes 28
  2.7 10.0 %collective-permute-start.4 = (f32[33,8,128]{2,1,0:T(8,128)}, f32[33,8,128]{2,1,0:T(8,128)S(1)}, u32[]{:S(2)}, u32[]{:S(2)}) collective-permute-start(f32[33,8,128]{2,1,0:T(8,128)} %get-tuple-element.61), channel_id=1, source_target_pairs={{0,1},{1,2},{2,3},{3,4},{4,5},{5,6},{6,7},{7,0},{8,9},{9,10},{10,1... | collective-permute-start | bytes 405512 | tf_op jit(solution)/shard_map/ppermute | solution.py:563
  4.2 8.5 %collective-permute-start.5 = (f32[33,8,128]{2,1,0:T(8,128)}, f32[33,8,128]{2,1,0:T(8,128)S(1)}, u32[]{:S(2)}, u32[]{:S(2)}) collective-permute-start(f32[33,8,128]{2,1,0:T(8,128)} %get-tuple-element.62), channel_id=1, source_target_pairs={{0,7},{1,0},{2,1},{3,2},{4,3},{5,4},{6,5},{7,6},{8,15},{9,8},{10,9... | collective-permute-start | bytes 405512 | tf_op jit(solution)/shard_map/ppermute | solution.py:564
  9.6 54.3 %collective-permute-start.7 = (f32[520,128]{1,0:T(8,128)S(1)}, f32[520,128]{1,0:T(8,128)S(1)}, u32[]{:S(2)}, u32[]{:S(2)}) collective-permute-start(f32[520,128]{1,0:T(8,128)S(1)} %get-tuple-element.69), channel_id=1, source_target_pairs={{0,5},{1,4},{2,7},{3,6},{4,1},{5,0},{6,3},{7,2},{8,13},{9,12},{10,... | collective-permute-start | bytes 798728 | tf_op jit(solution)/shard_map/ppermute | solution.py:547
  12.3 51.6 %collective-permute-start.6 = (f32[520,128]{1,0:T(8,128)S(1)}, f32[520,128]{1,0:T(8,128)S(1)}, u32[]{:S(2)}, u32[]{:S(2)}) collective-permute-start(f32[520,128]{1,0:T(8,128)S(1)} %get-tuple-element.63._), channel_id=1, source_target_pairs={{0,4},{1,5},{2,6},{3,7},{4,0},{5,1},{6,2},{7,3},{8,12},{9,13},{10,... | collective-permute-start | bytes 798728 | tf_op jit(solution)/shard_map/ppermute | solution.py:547
  12.8 8.0 %collective-permute-start.2 = (f32[608,128]{1,0:T(8,128)S(1)}, f32[608,128]{1,0:T(8,128)}, u32[]{:S(2)}, u32[]{:S(2)}) collective-permute-start(f32[608,128]{1,0:T(8,128)S(1)} %get-tuple-element.35), channel_id=1, source_target_pairs={{0,8},{8,16},{16,24},{24,0},{1,9},{9,17},{17,25},{25,1},{2,10},{10... | collective-permute-start | bytes 933896 | tf_op jit(solution)/shard_map/cond/branch_1_fun/ppermute | solution.py:580
  12.9 8.7 %collective-permute-start.3 = (f32[608,128]{1,0:T(8,128)S(1)}, f32[608,128]{1,0:T(8,128)}, u32[]{:S(2)}, u32[]{:S(2)}) collective-permute-start(f32[608,128]{1,0:T(8,128)S(1)} %get-tuple-element.36), channel_id=1, source_target_pairs={{0,24},{8,0},{16,8},{24,16},{1,25},{9,1},{17,9},{25,17},{2,26},{10... | collective-permute-start | bytes 933896 | tf_op jit(solution)/shard_map/cond/branch_1_fun/ppermute | solution.py:580
  21.5 42.4 %collective-permute-start.8 = (f32[520,128]{1,0:T(8,128)}, f32[520,128]{1,0:T(8,128)S(1)}, u32[]{:S(2)}, u32[]{:S(2)}) collective-permute-start(f32[520,128]{1,0:T(8,128)} %get-tuple-element.70), channel_id=1, source_target_pairs={{0,6},{1,7},{2,4},{3,5},{4,2},{5,3},{6,0},{7,1},{8,14},{9,15},{10,... | collective-permute-start | bytes 798728 | tf_op jit(solution)/shard_map/ppermute | solution.py:547
  35.8 28.1 %collective-permute-start.9 = (f32[520,128]{1,0:T(8,128)S(1)}, f32[520,128]{1,0:T(8,128)S(1)}, u32[]{:S(2)}, u32[]{:S(2)}) collective-permute-start(f32[520,128]{1,0:T(8,128)S(1)} %get-tuple-element.71), channel_id=1, source_target_pairs={{0,7},{1,6},{2,5},{3,4},{4,3},{5,2},{6,1},{7,0},{8,15},{9,14},{10,... | collective-permute-start | bytes 798728 | tf_op jit(solution)/shard_map/ppermute | solution.py:547
  66.0 38.2 %collective-permute-start.10 = (f32[2,256,128]{2,1,0:T(8,128)S(1)}, f32[2,256,128]{2,1,0:T(8,128)S(1)}, u32[]{:S(2)}, u32[]{:S(2)}) collective-permute-start(f32[2,256,128]{2,1,0:T(8,128)S(1)} %get-tuple-element.74), channel_id=1, source_target_pairs={{0,4},{1,5},{2,6},{3,7},{4,0},{5,1},{6,2},{7,3},{8,12},{9,13},{10,... | collective-permute-start | bytes 786440 | tf_op jit(solution)/shard_map/ppermute | solution.py:547
  66.1 38.1 %collective-permute-start.11 = (f32[2,256,128]{2,1,0:T(8,128)S(1)}, f32[2,256,128]{2,1,0:T(8,128)S(1)}, u32[]{:S(2)}, u32[]{:S(2)}) collective-permute-start(f32[2,256,128]{2,1,0:T(8,128)S(1)} %get-tuple-element.75), channel_id=1, source_target_pairs={{0,5},{1,4},{2,7},{3,6},{4,1},{5,0},{6,3},{7,2},{8,13},{9,12},{10,... | collective-permute-start | bytes 786440 | tf_op jit(solution)/shard_map/ppermute | solution.py:547
  69.0 37.5 %collective-permute-start.12 = (f32[2,256,128]{2,1,0:T(8,128)S(1)}, f32[2,256,128]{2,1,0:T(8,128)S(1)}, u32[]{:S(2)}, u32[]{:S(2)}) collective-permute-start(f32[2,256,128]{2,1,0:T(8,128)S(1)} %get-tuple-element.76), channel_id=1, source_target_pairs={{0,6},{1,7},{2,4},{3,5},{4,2},{5,3},{6,0},{7,1},{8,14},{9,15},{10,... | collective-permute-start | bytes 786440 | tf_op jit(solution)/shard_map/ppermute | solution.py:547
  69.0 42.8 %collective-permute-start.13 = (f32[2,256,128]{2,1,0:T(8,128)S(1)}, f32[2,256,128]{2,1,0:T(8,128)S(1)}, u32[]{:S(2)}, u32[]{:S(2)}) collective-permute-start(f32[2,256,128]{2,1,0:T(8,128)S(1)} %get-tuple-element.77), channel_id=1, source_target_pairs={{0,7},{1,6},{2,5},{3,4},{4,3},{5,2},{6,1},{7,0},{8,15},{9,14},{10,... | collective-permute-start | bytes 786440 | tf_op jit(solution)/shard_map/ppermute | solution.py:547

commit v19 on v16

--- a/solution.py
+++ b/solution.py
@@ -218,7 +218,7 @@
 
 
 AUX = 8
-UNROLL = 8
+UNROLL = 4
 
 
 def march(count, row_of, starts, source, target, coefs_of):

time: 113 us -> 113 us (level)
  no operation moved by 1% of the time
where the time goes in v19:
time: 113 us
  blocking collectives  60.9 us (54%)
  Pallas kernels  25 us (22%)
  starting transfers between devices  16.6 us (15%)
  waiting for transfers between devices  9.4 us (8%)
    all_to_all x2, blocking collectives, exchange(): lax.all_to_all(values, 'gy', 0, 0, axis_index_groups=groups, tiled=True)  60.9 us
    pallas_call x1, Pallas kernels, run_outer(): pl.pallas_call(functools.partial(outer_kernel, plan), in_specs=[vmem] * 7...  12 us
    ppermute x8, starting transfers between devices, swap(): lax.ppermute(values, 'gy', [(i, i ^ mask) for i in range(lax.axis_size('g...  11.9 us
    pallas_call x2, Pallas kernels, run_inner(): pl.pallas_call(functools.partial(inner_kernel, plan, batch), in_specs=[vm...  8.13 us
    ppermute x8, waiting for transfers between devices, swap(): lax.ppermute(values, 'gy', [(i, i ^ mask) for i in range(lax.axis_size('g...  6.05 us
    ppermute x1, waiting for transfers between devices, ring_swap(): lax.ppermute(low, 'gx', ring('gx', 1))  2.58 us
  transfers between devices with their start and end apart: 12, of which 4 were waited for; matrix products, arithmetic and copies ran while one was open for 0% of the time, Pallas kernels for 18%

profile of v19, /device:TPU:8, one launch (start us, length us, event | category | flops | bytes accessed | tf_op | source)
XLA Modules:
  0.0 112.8 jit_solution(1569755649645039473)
XLA Ops:
  0.6 0.0 copy-start.1
  0.6 0.0 copy-start
  0.7 2.0 %pack_y.1 = (f32[33,8,128]{2,1,0:T(8,128)}, f32[33,8,128]{2,1,0:T(8,128)}, f32[24,128]{1,0:T(8,128)S(1)}) custom-call(f32[1,2]{1,0:T(1,128)} %under.1, f32[1,2]{1,0:T(1,128)} %mobile.1, f32[1,2]{1,0:T(1,128)} %spread.1, s32[1,2]{1,0:T(1,128)} %owner.1, f32[1,2,32,32,128]{4,3,2,1,0:T(8,128)} %phase.3, f32[1,2,32,32,128]{4,3,2,1,0:T(8,128)} %phase.3, ...), custom_call_target="tpu_custom_call" | custom-call | tf_op jit(solution)/shard_map/pack_y/pallas_call | solution.py:48
  2.7 0.0 copy-start.2
  2.7 1.5 %collective-permute-start.4 = (f32[33,8,128]{2,1,0:T(8,128)}, f32[33,8,128]{2,1,0:T(8,128)S(1)}, u32[]{:S(2)}, u32[]{:S(2)}) collective-permute-start(f32[33,8,128]{2,1,0:T(8,128)} %get-tuple-element.61), channel_id=1, source_target_pairs={{0,1},{1,2},{2,3},{3,4},{4,5},{5,6},{6,7},{7,0},{8,9},{9,10},{10,1... | collective-permute-start | bytes 405512 | tf_op jit(solution)/shard_map/ppermute | solution.py:547
  4.2 1.4 %collective-permute-start.5 = (f32[33,8,128]{2,1,0:T(8,128)}, f32[33,8,128]{2,1,0:T(8,128)S(1)}, u32[]{:S(2)}, u32[]{:S(2)}) collective-permute-start(f32[33,8,128]{2,1,0:T(8,128)} %get-tuple-element.62), channel_id=1, source_target_pairs={{0,7},{1,0},{2,1},{3,2},{4,3},{5,4},{6,5},{7,6},{8,15},{9,8},{10,9... | collective-permute-start | bytes 405512 | tf_op jit(solution)/shard_map/ppermute | solution.py:548
  5.6 0.0 copy-done.1
  5.6 0.0 copy-done
  5.6 4.6 %inner.5 = (f32[520,128]{1,0:T(8,128)S(1)}, f32[520,128]{1,0:T(8,128)}) custom-call(f32[24,128]{1,0:T(8,128)S(1)} %get-tuple-element.60.own, f32[1,2,32,32,128]{4,3,2,1,0:T(8,128)S(1)} %copy-done, f32[1,2,32,32,128]{4,3,2,1,0:T(8,128)S(1)} %copy-done.1), custom_call_target="tpu_custom_call" | custom-call | flops 100000000 | bytes 25165824 | tf_op jit(solution)/shard_map/inner/pallas_call | solution.py:290
  10.1 2.6 %collective-permute-start.7 = (f32[520,128]{1,0:T(8,128)}, f32[520,128]{1,0:T(8,128)S(1)}, u32[]{:S(2)}, u32[]{:S(2)}) collective-permute-start(f32[520,128]{1,0:T(8,128)} %get-tuple-element.69), channel_id=1, source_target_pairs={{0,5},{1,4},{2,7},{3,6},{4,1},{5,0},{6,3},{7,2},{8,13},{9,12},{10,... | collective-permute-start | bytes 798728 | tf_op jit(solution)/shard_map/ppermute | solution.py:527
  12.8 0.3 collective-permute-start.6
  13.1 0.0 copy-done.2
  13.2 0.0 collective-permute-done.4.y_lo
  13.2 0.0 collective-permute-done.5.y_hi
  13.3 8.7 %conditional.3 = (f32[608,128]{1,0:T(8,128)}, f32[608,128]{1,0:T(8,128)}, f32[520,128]{1,0:T(8,128)}) conditional(s32[]{:T(128)} %bitcast, (f32[608,128]{1,0:T(8,128)S(1)}, f32[608,128]{1,0:T(8,128)S(1)}, f32[24,128]{1,0:T(8,128)S(1)}, f32[1,2,32,32,128]{4,3,2,1,0:T(8,128)S(1)}, f32[1,2,32,32,128]{4,3,2,1,0:T(8,128)S(1)}) %tuple.36, ...), branch_computations={%region_0.0_spmd, %region_1.0_spmd} | conditional | flops 100000000 | bytes 27656296 | solution.py:567
  13.3 0.1 collective-permute-start.2
  13.3 1.7 %collective-permute-start.3 = (f32[608,128]{1,0:T(8,128)S(1)}, f32[608,128]{1,0:T(8,128)}, u32[]{:S(2)}, u32[]{:S(2)}) collective-permute-start(f32[608,128]{1,0:T(8,128)S(1)} %get-tuple-element.36), channel_id=1, source_target_pairs={{0,24},{8,0},{16,8},{24,16},{1,25},{9,1},{17,9},{25,17},{2,26},{10... | collective-permute-start | bytes 933896 | tf_op jit(solution)/shard_map/cond/branch_1_fun/ppermute | solution.py:565
  15.1 3.6 %inner.4 = f32[520,128]{1,0:T(8,128)} custom-call(f32[24,128]{1,0:T(8,128)S(1)} %get-tuple-element.37.own, f32[1,2,32,32,128]{4,3,2,1,0:T(8,128)S(1)} %get-tuple-element.38.phase, f32[1,2,32,32,128]{4,3,2,1,0:T(8,128)S(1)} %get-tuple-element.39.solute), custom_call_target="tpu_custom_call" | custom-call | flops 100000000 | bytes 25165824 | tf_op jit(solution)/shard_map/cond/branch_1_fun/inner/pallas_call | solution.py:290
  18.7 2.6 %collective-permute-done.2 = f32[608,128]{1,0:T(8,128)} collective-permute-done((f32[608,128]{1,0:T(8,128)S(1)}, f32[608,128]{1,0:T(8,128)}, u32[]{:S(2)}, u32[]{:S(2)}) %collective-permute-start.2) | collective-permute-done | bytes 311328 | tf_op jit(solution)/shard_map/cond/branch_1_fun/ppermute | solution.py:565
  21.2 0.8 collective-permute-done.3
  22.0 1.6 %collective-permute-start.8 = (f32[520,128]{1,0:T(8,128)}, f32[520,128]{1,0:T(8,128)S(1)}, u32[]{:S(2)}, u32[]{:S(2)}) collective-permute-start(f32[520,128]{1,0:T(8,128)} %get-tuple-element.70), channel_id=1, source_target_pairs={{0,6},{1,7},{2,4},{3,5},{4,2},{5,3},{6,0},{7,1},{8,14},{9,15},{10,... | collective-permute-start | bytes 798728 | tf_op jit(solution)/shard_map/ppermute | solution.py:527
  23.6 12.0 %outer.1 = (f32[4,520,128]{2,1,0:T(8,128)S(1)}, f32[520,128]{1,0:T(8,128)}) custom-call(f32[24,128]{1,0:T(8,128)S(1)} %get-tuple-element.60.own, f32[1,2,32,32,128]{4,3,2,1,0:T(8,128)S(1)} %copy-done, f32[1,2,32,32,128]{4,3,2,1,0:T(8,128)S(1)} %copy-done.1, f32[33,8,128]{2,1,0:T(8,128)S(1)} %collective-permute-done.4.y_lo, ...), custom_call_target="tpu_custom_call" | custom-call | flops 100000000 | bytes 41943040 | tf_op jit(solution)/shard_map/outer/pallas_call | solution.py:393
  35.5 1.4 %collective-permute-start.9 = (f32[520,128]{1,0:T(8,128)}, f32[520,128]{1,0:T(8,128)S(1)}, u32[]{:S(2)}, u32[]{:S(2)}) collective-permute-start(f32[520,128]{1,0:T(8,128)} %get-tuple-element.71), channel_id=1, source_target_pairs={{0,7},{1,6},{2,5},{3,4},{4,3},{5,2},{6,1},{7,0},{8,15},{9,14},{10,... | collective-permute-start | bytes 798728 | tf_op jit(solution)/shard_map/ppermute | solution.py:527
  37.0 25.9 %conditional.4 = (f32[4,520,128]{2,1,0:T(8,128)S(1)}) conditional(s32[]{:T(128)} %bitcast, f32[4,520,128]{2,1,0:T(8,128)S(1)} %get-tuple-element.68, f32[4,520,128]{2,1,0:T(8,128)S(1)} %get-tuple-element.68), branch_computations={%region_2.0_spmd, %region_3.0_spmd} | conditional | bytes 2129928 | solution.py:535
  37.0 25.9 %all_to_all.17 = f32[4,520,128]{2,1,0:T(8,128)S(1)} all-to-all(f32[4,520,128]{2,1,0:T(8,128)S(1)} %param.3), channel_id=1, replica_groups={{0,1,2,3},{4,5,6,7},{8,9,10,11},{12,13,14,15},{16,17,18,19},{20,21,22,2..., dimensions={0} | all-to-all | bytes 2129920 | tf_op jit(solution)/shard_map/cond/branch_1_fun/all_to_all | solution.py:533
  62.9 0.0 collective-permute-done.7.refs_1_
  62.9 0.0 collective-permute-done.6.refs_0_
  62.9 0.0 collective-permute-done.8.refs_2_
  62.9 0.0 collective-permute-done.9.refs_3_
  62.9 0.9 route.1
  63.8 0.1 collective-permute-start.10
  63.9 2.9 %collective-permute-start.11 = (f32[2,256,128]{2,1,0:T(8,128)S(1)}, f32[2,256,128]{2,1,0:T(8,128)S(1)}, u32[]{:S(2)}, u32[]{:S(2)}) collective-permute-start(f32[2,256,128]{2,1,0:T(8,128)S(1)} %get-tuple-element.75), channel_id=1, source_target_pairs={{0,5},{1,4},{2,7},{3,6},{4,1},{5,0},{6,3},{7,2},{8,13},{9,12},{10,... | collective-permute-start | bytes 786440 | tf_op jit(solution)/shard_map/ppermute | solution.py:527
  66.8 1.2 %collective-permute-start.12 = (f32[2,256,128]{2,1,0:T(8,128)S(1)}, f32[2,256,128]{2,1,0:T(8,128)S(1)}, u32[]{:S(2)}, u32[]{:S(2)}) collective-permute-start(f32[2,256,128]{2,1,0:T(8,128)S(1)} %get-tuple-element.76), channel_id=1, source_target_pairs={{0,6},{1,7},{2,4},{3,5},{4,2},{5,3},{6,0},{7,1},{8,14},{9,15},{10,... | collective-permute-start | bytes 786440 | tf_op jit(solution)/shard_map/ppermute | solution.py:527
  67.9 1.8 %collective-permute-start.13 = (f32[2,256,128]{2,1,0:T(8,128)S(1)}, f32[2,256,128]{2,1,0:T(8,128)S(1)}, u32[]{:S(2)}, u32[]{:S(2)}) collective-permute-start(f32[2,256,128]{2,1,0:T(8,128)S(1)} %get-tuple-element.77), channel_id=1, source_target_pairs={{0,7},{1,6},{2,5},{3,4},{4,3},{5,2},{6,1},{7,0},{8,15},{9,14},{10,... | collective-permute-start | bytes 786440 | tf_op jit(solution)/shard_map/ppermute | solution.py:527
  69.7 35.1 %conditional.5 = (f32[4,2,256,128]{3,2,1,0:T(8,128)S(1)}) conditional(s32[]{:T(128)} %bitcast, f32[4,2,256,128]{3,2,1,0:T(8,128)S(1)} %get-tuple-element.73, f32[4,2,256,128]{3,2,1,0:T(8,128)S(1)} %get-tuple-element.73), branch_computations={%region_4.0_spmd, %region_5.0_spmd} | conditional | bytes 2097160 | solution.py:535
  69.7 35.1 %all_to_all.19 = f32[4,2,256,128]{3,2,1,0:T(8,128)S(1)} all-to-all(f32[4,2,256,128]{3,2,1,0:T(8,128)S(1)} %param.5), channel_id=1, replica_groups={{0,1,2,3},{4,5,6,7},{8,9,10,11},{12,13,14,15},{16,17,18,19},{20,21,22,2..., dimensions={0} | all-to-all | bytes 2097152 | tf_op jit(solution)/shard_map/cond/branch_1_fun/all_to_all | solution.py:533
  104.8 0.0 collective-permute-done.10.refs_0_
  104.8 0.0 collective-permute-done.11.refs_1_
  104.8 0.7 collective-permute-done.12.refs_2_
  105.4 5.4 %collective-permute-done.13.refs_3_ = f32[2,256,128]{2,1,0:T(8,128)S(1)} collective-permute-done((f32[2,256,128]{2,1,0:T(8,128)S(1)}, f32[2,256,128]{2,1,0:T(8,128)S(1)}, u32[]{:S(2)}, u32[]{:S(2)}) %collective-permute-start.13) | collective-permute-done | bytes 262176 | tf_op jit(solution)/shard_map/ppermute | solution.py:527
  110.8 2.0 %settle.1 = (f32[1,2,32,32,128]{4,3,2,1,0:T(8,128)}, f32[1,2,32,32,128]{4,3,2,1,0:T(8,128)}) custom-call(s32[16]{0:T(128)S(1)} %get-tuple-element.72.table, f32[4,2,256,128]{3,2,1,0:T(8,128)S(1)} %get-tuple-element.85.near, f32[2,256,128]{2,1,0:T(8,128)S(1)} %collective-permute-done.10.refs_0_, f32[2,256,128]{2,1,0:T(8,128)S(1)} %collective-permute-done.11.refs_1_, ...), custom_call_target="tpu_custom_call" | custom-call | tf_op jit(solution)/shard_map/settle/pallas_call | solution.py:507
  (1 shorter events, 0.0 us)
Async XLA Ops:
  0.6 5.0 %copy-start.1 = (f32[1,2,32,32,128]{4,3,2,1,0:T(8,128)S(1)}, f32[1,2,32,32,128]{4,3,2,1,0:T(8,128)}, u32[]{:S(2)}) copy-start(f32[1,2,32,32,128]{4,3,2,1,0:T(8,128)} %solute.3) | copy-start | bytes 3145732
  0.6 5.0 %copy-start = (f32[1,2,32,32,128]{4,3,2,1,0:T(8,128)S(1)}, f32[1,2,32,32,128]{4,3,2,1,0:T(8,128)}, u32[]{:S(2)}) copy-start(f32[1,2,32,32,128]{4,3,2,1,0:T(8,128)} %phase.3) | copy-start | bytes 3145732
  2.7 10.5 %copy-start.2 = (s32[1,2]{1,0:T(1,128)S(1)}, s32[1,2]{1,0:T(1,128)}, u32[]{:S(2)}) copy-start(s32[1,2]{1,0:T(1,128)} %owner.1) | copy-start | bytes 28
  2.7 10.5 %collective-permute-start.4 = (f32[33,8,128]{2,1,0:T(8,128)}, f32[33,8,128]{2,1,0:T(8,128)S(1)}, u32[]{:S(2)}, u32[]{:S(2)}) collective-permute-start(f32[33,8,128]{2,1,0:T(8,128)} %get-tuple-element.61), channel_id=1, source_target_pairs={{0,1},{1,2},{2,3},{3,4},{4,5},{5,6},{6,7},{7,0},{8,9},{9,10},{10,1... | collective-permute-start | bytes 405512 | tf_op jit(solution)/shard_map/ppermute | solution.py:547
  4.2 9.0 %collective-permute-start.5 = (f32[33,8,128]{2,1,0:T(8,128)}, f32[33,8,128]{2,1,0:T(8,128)S(1)}, u32[]{:S(2)}, u32[]{:S(2)}) collective-permute-start(f32[33,8,128]{2,1,0:T(8,128)} %get-tuple-element.62), channel_id=1, source_target_pairs={{0,7},{1,0},{2,1},{3,2},{4,3},{5,4},{6,5},{7,6},{8,15},{9,8},{10,9... | collective-permute-start | bytes 405512 | tf_op jit(solution)/shard_map/ppermute | solution.py:548
  10.1 52.7 %collective-permute-start.7 = (f32[520,128]{1,0:T(8,128)}, f32[520,128]{1,0:T(8,128)S(1)}, u32[]{:S(2)}, u32[]{:S(2)}) collective-permute-start(f32[520,128]{1,0:T(8,128)} %get-tuple-element.69), channel_id=1, source_target_pairs={{0,5},{1,4},{2,7},{3,6},{4,1},{5,0},{6,3},{7,2},{8,13},{9,12},{10,... | collective-permute-start | bytes 798728 | tf_op jit(solution)/shard_map/ppermute | solution.py:527
  12.8 50.1 %collective-permute-start.6 = (f32[520,128]{1,0:T(8,128)S(1)}, f32[520,128]{1,0:T(8,128)S(1)}, u32[]{:S(2)}, u32[]{:S(2)}) collective-permute-start(f32[520,128]{1,0:T(8,128)S(1)} %get-tuple-element.63._), channel_id=1, source_target_pairs={{0,4},{1,5},{2,6},{3,7},{4,0},{5,1},{6,2},{7,3},{8,12},{9,13},{10,... | collective-permute-start | bytes 798728 | tf_op jit(solution)/shard_map/ppermute | solution.py:527
  13.3 8.0 %collective-permute-start.2 = (f32[608,128]{1,0:T(8,128)S(1)}, f32[608,128]{1,0:T(8,128)}, u32[]{:S(2)}, u32[]{:S(2)}) collective-permute-start(f32[608,128]{1,0:T(8,128)S(1)} %get-tuple-element.35), channel_id=1, source_target_pairs={{0,8},{8,16},{16,24},{24,0},{1,9},{9,17},{17,25},{25,1},{2,10},{10... | collective-permute-start | bytes 933896 | tf_op jit(solution)/shard_map/cond/branch_1_fun/ppermute | solution.py:565
  13.3 8.7 %collective-permute-start.3 = (f32[608,128]{1,0:T(8,128)S(1)}, f32[608,128]{1,0:T(8,128)}, u32[]{:S(2)}, u32[]{:S(2)}) collective-permute-start(f32[608,128]{1,0:T(8,128)S(1)} %get-tuple-element.36), channel_id=1, source_target_pairs={{0,24},{8,0},{16,8},{24,16},{1,25},{9,1},{17,9},{25,17},{2,26},{10... | collective-permute-start | bytes 933896 | tf_op jit(solution)/shard_map/cond/branch_1_fun/ppermute | solution.py:565
  22.0 40.9 %collective-permute-start.8 = (f32[520,128]{1,0:T(8,128)}, f32[520,128]{1,0:T(8,128)S(1)}, u32[]{:S(2)}, u32[]{:S(2)}) collective-permute-start(f32[520,128]{1,0:T(8,128)} %get-tuple-element.70), channel_id=1, source_target_pairs={{0,6},{1,7},{2,4},{3,5},{4,2},{5,3},{6,0},{7,1},{8,14},{9,15},{10,... | collective-permute-start | bytes 798728 | tf_op jit(solution)/shard_map/ppermute | solution.py:527
  35.5 27.3 %collective-permute-start.9 = (f32[520,128]{1,0:T(8,128)}, f32[520,128]{1,0:T(8,128)S(1)}, u32[]{:S(2)}, u32[]{:S(2)}) collective-permute-start(f32[520,128]{1,0:T(8,128)} %get-tuple-element.71), channel_id=1, source_target_pairs={{0,7},{1,6},{2,5},{3,4},{4,3},{5,2},{6,1},{7,0},{8,15},{9,14},{10,... | collective-permute-start | bytes 798728 | tf_op jit(solution)/shard_map/ppermute | solution.py:527
  63.8 41.0 %collective-permute-start.10 = (f32[2,256,128]{2,1,0:T(8,128)S(1)}, f32[2,256,128]{2,1,0:T(8,128)S(1)}, u32[]{:S(2)}, u32[]{:S(2)}) collective-permute-start(f32[2,256,128]{2,1,0:T(8,128)S(1)} %get-tuple-element.74), channel_id=1, source_target_pairs={{0,4},{1,5},{2,6},{3,7},{4,0},{5,1},{6,2},{7,3},{8,12},{9,13},{10,... | collective-permute-start | bytes 786440 | tf_op jit(solution)/shard_map/ppermute | solution.py:527
  63.9 40.9 %collective-permute-start.11 = (f32[2,256,128]{2,1,0:T(8,128)S(1)}, f32[2,256,128]{2,1,0:T(8,128)S(1)}, u32[]{:S(2)}, u32[]{:S(2)}) collective-permute-start(f32[2,256,128]{2,1,0:T(8,128)S(1)} %get-tuple-element.75), channel_id=1, source_target_pairs={{0,5},{1,4},{2,7},{3,6},{4,1},{5,0},{6,3},{7,2},{8,13},{9,12},{10,... | collective-permute-start | bytes 786440 | tf_op jit(solution)/shard_map/ppermute | solution.py:527
  66.8 38.6 %collective-permute-start.12 = (f32[2,256,128]{2,1,0:T(8,128)S(1)}, f32[2,256,128]{2,1,0:T(8,128)S(1)}, u32[]{:S(2)}, u32[]{:S(2)}) collective-permute-start(f32[2,256,128]{2,1,0:T(8,128)S(1)} %get-tuple-element.76), channel_id=1, source_target_pairs={{0,6},{1,7},{2,4},{3,5},{4,2},{5,3},{6,0},{7,1},{8,14},{9,15},{10,... | collective-permute-start | bytes 786440 | tf_op jit(solution)/shard_map/ppermute | solution.py:527
  67.9 42.9 %collective-permute-start.13 = (f32[2,256,128]{2,1,0:T(8,128)S(1)}, f32[2,256,128]{2,1,0:T(8,128)S(1)}, u32[]{:S(2)}, u32[]{:S(2)}) collective-permute-start(f32[2,256,128]{2,1,0:T(8,128)S(1)} %get-tuple-element.77), channel_id=1, source_target_pairs={{0,7},{1,6},{2,5},{3,4},{4,3},{5,2},{6,1},{7,0},{8,15},{9,14},{10,... | collective-permute-start | bytes 786440 | tf_op jit(solution)/shard_map/ppermute | solution.py:527

commit v20 on v19

--- a/solution.py
+++ b/solution.py
@@ -168,19 +168,13 @@
         self.middle = edge - 16
         self.size = self.rows * self.middle + self.rows_far * 8
 
-        begins = [min(W + p * self.rows, 2 * W + p * self.rows_far) for p in range(self.half)]
-        ends = [max(W + p * self.rows + self.rows, 2 * W + (p + 1) * self.rows_far) for p in range(self.half)]
-        self.span = max(end - begin for begin, end in zip(begins, ends))
         side = self.half // 2
-        self.batches = (list(range(side)), [side], list(range(side + 1, self.half)))
+        self.batches = (list(range(side)), list(range(side, self.half)))
 
     def batch_rows(self, batch, mine):
-        if batch == 0:
-            count = self.inner // 2
-            return W + mine // (self.half // 2) * count, count
-        piece = mine ^ self.batches[1][0]
-        begin = jnp.minimum(W + piece * self.rows, 2 * W + piece * self.rows_far)
-        return jnp.minimum(begin, self.edge - W - self.span), self.span
+        count = self.inner // 2
+        side = mine // (self.half // 2)
+        return W + (side if batch == 0 else 1 - side) * count, count
 
     def near_row(self, piece, row, gap):
         index = piece * self.rows_near + row
@@ -299,10 +293,8 @@
     )(own, phase, solute)
 
 
-def outer_kernel(plan, own, phase, solute, y_lo, y_hi, x_lo, x_hi, out, *rest):
+def outer_kernel(plan, own, phase, solute, y_lo, y_hi, x_lo, x_hi, out, *scratch):
     tiles, edge, depth, half = plan.tiles, plan.edge, plan.depth, plan.half
-    late = plan.batches[2]
-    far_outs, scratch = rest[: len(late)], rest[len(late) :]
     pairs, coefs = (scratch[:2], scratch[2:4]), scratch[4]
     cols = tiles * edge
     width = cols + 2 * W
@@ -351,10 +343,6 @@
     any_zone = coefs_of(lambda row: jnp.where(row < W, 0, jnp.where(row < W + edge, 1, 2)))
 
     own_zone = coefs_of(lambda row: 1)
-    mine = lax.rem(lax.axis_index("gy"), half)
-    made = plan.inner // 2
-    first_made = 2 * W + mine // (half // 2) * made
-
     def blocks(first, last):
         low, high = (first + W - shift) // 8 * 8, -(-(last + W - shift) // 8) * 8
         return list(range(PAD + shift + low, PAD + shift + high, 8))
@@ -364,21 +352,21 @@
         left = NSTEPS - step
         shift = W if step == NSTEPS else 0
         whole = blocks(-left, cols + left)
-        ends = blocks(-left, 8 + left) + blocks(cols - 8 - left, cols + left)
+        sides = blocks(-left, 8 + left) + blocks(cols - 8 - left, cols + left)
+        ends = list(sides)
         for tile in range(tiles):
             col, count = plan.columns("last", tile)
             ends += blocks(tile * edge + col - left, tile * edge + col + count + left)
-        gap, gap_rows = first_made + left, made - 2 * left
-
-        def outside(index, left=left, gap=gap, gap_rows=gap_rows):
-            row = W - left + index
-            return row + jnp.where(row < gap, 0, gap_rows)
-
-        march(edge + 2 * left - gap_rows, outside, whole, source, target, any_zone)
-        march(gap_rows, lambda i, gap=gap: gap + i, sorted(set(ends)), source, target, own_zone)
+        strip = W + left
+
+        def two(size, begin):
+            mirror = 2 * W + edge - begin - size
+            return lambda i: i + jnp.where(i < size, begin, mirror - size)
+
+        march(2 * (strip + left), two(strip + left, W - left), whole, source, target, any_zone)
+        march(2 * W, two(W, W + strip), sorted(set(ends)), source, target, own_zone)
+        march(edge - 2 * strip - 2 * W, lambda i, strip=strip: i + 2 * W + strip, sides, source, target, own_zone)
     done = pairs[NSTEPS % 2]
-    for index, far_out in zip(late, far_outs):
-        pack(plan, True, mine ^ index, done, W, PAD + W, own, far_out)
     for piece in range(half):
         pack(plan, False, piece, done, W, PAD + W, own, out.at[piece])
 
@@ -389,12 +377,11 @@
     buffer = pltpu.VMEM((edge + 2 * W, width + 2 * PAD, depth), jnp.float32)
     vmem = pl.BlockSpec(memory_space=pltpu.VMEM)
     near = jax.ShapeDtypeStruct((plan.half, 2 * tiles * plan.size + AUX, depth), jnp.float32)
-    far = jax.ShapeDtypeStruct((2 * tiles * plan.size + AUX, depth), jnp.float32)
     return pl.pallas_call(
         functools.partial(outer_kernel, plan),
         in_specs=[vmem] * 7,
-        out_specs=[vmem] * (1 + len(plan.batches[2])),
-        out_shape=[near] + [far] * len(plan.batches[2]),
+        out_specs=vmem,
+        out_shape=near,
         scratch_shapes=[buffer] * 4 + [pltpu.VMEM((3, KINDS, width, depth), jnp.float32)],
         compiler_params=pltpu.CompilerParams(vmem_limit_bytes=16 * 1024 * 1024),
         cost_estimate=pl.CostEstimate(flops=10**8, bytes_accessed=40 * 1024 * 1024, transcendentals=0),
@@ -566,8 +553,7 @@
 
     (x_lo, x_hi), second = lax.cond(together, around, around, to_next, to_prev, own, phase, solute)
     send_far(1, second)
-    near, *third = run_outer(plan, own_here, phase_here, solute_here, (y_lo, y_hi, in_vmem(x_lo), in_vmem(x_hi)))
-    send_far(2, third)
+    near = run_outer(plan, own_here, phase_here, solute_here, (y_lo, y_hi, in_vmem(x_lo), in_vmem(x_hi)))
     far = [far[index] for index in range(half)]
     near = among_half(plan, near, together)
     near, far, table = route(plan, in_vmem(near), far)

time: 113 us -> 112 us (level)
  waiting for transfers between devices: 9.4 us -> 7.99 us
    pallas_call x1, Pallas kernels: 12 us -> 9.8 us  [run_outer(): pl.pallas_call(functools.partial(outer_kernel, plan), in_specs=[vmem] * 7...]
  transfers between devices with their start and end apart: 12 -> 12, of which waited for: 4 -> 4; matrix products, arithmetic and copies ran while one was open for 0% -> 0% of each run, Pallas kernels for 18% -> 17%
where the time goes in v20:
time: 112 us
  blocking collectives  61.9 us (55%)
  Pallas kernels  25 us (22%)
  starting transfers between devices  16.5 us (15%)
  waiting for transfers between devices  7.99 us (7%)
    all_to_all x2, blocking collectives, exchange(): lax.all_to_all(values, 'gy', 0, 0, axis_index_groups=groups, tiled=True)  61.9 us
    ppermute x8, starting transfers between devices, swap(): lax.ppermute(values, 'gy', [(i, i ^ mask) for i in range(lax.axis_size('g...  11.8 us
    pallas_call x1, Pallas kernels, run_outer(): pl.pallas_call(functools.partial(outer_kernel, plan), in_specs=[vmem] * 7...  9.8 us
    pallas_call x2, Pallas kernels, run_inner(): pl.pallas_call(functools.partial(inner_kernel, plan, batch), in_specs=[vm...  9.2 us
    ppermute x8, waiting for transfers between devices, swap(): lax.ppermute(values, 'gy', [(i, i ^ mask) for i in range(lax.axis_size('g...  5.71 us
  transfers between devices with their start and end apart: 12, of which 4 were waited for; matrix products, arithmetic and copies ran while one was open for 0% of the time, Pallas kernels for 17%

profile of v20, /device:TPU:8, one launch (start us, length us, event | category | flops | bytes accessed | tf_op | source)
XLA Modules:
  0.0 112.2 jit_solution(7824431979958535687)
XLA Ops:
  0.6 0.0 copy-start.1
  0.6 0.0 copy-start
  0.7 2.0 %pack_y.1 = (f32[33,8,128]{2,1,0:T(8,128)}, f32[33,8,128]{2,1,0:T(8,128)}, f32[24,128]{1,0:T(8,128)S(1)}) custom-call(f32[1,2]{1,0:T(1,128)} %under.1, f32[1,2]{1,0:T(1,128)} %mobile.1, f32[1,2]{1,0:T(1,128)} %spread.1, s32[1,2]{1,0:T(1,128)} %owner.1, f32[1,2,32,32,128]{4,3,2,1,0:T(8,128)} %phase.3, f32[1,2,32,32,128]{4,3,2,1,0:T(8,128)} %phase.3, ...), custom_call_target="tpu_custom_call" | custom-call | tf_op jit(solution)/shard_map/pack_y/pallas_call | solution.py:48
  2.7 0.0 copy-start.2
  2.7 1.5 %collective-permute-start.4 = (f32[33,8,128]{2,1,0:T(8,128)}, f32[33,8,128]{2,1,0:T(8,128)S(1)}, u32[]{:S(2)}, u32[]{:S(2)}) collective-permute-start(f32[33,8,128]{2,1,0:T(8,128)} %get-tuple-element.64), channel_id=1, source_target_pairs={{0,1},{1,2},{2,3},{3,4},{4,5},{5,6},{6,7},{7,0},{8,9},{9,10},{10,1... | collective-permute-start | bytes 405512 | tf_op jit(solution)/shard_map/ppermute | solution.py:534
  4.2 1.4 %collective-permute-start.5 = (f32[33,8,128]{2,1,0:T(8,128)}, f32[33,8,128]{2,1,0:T(8,128)S(1)}, u32[]{:S(2)}, u32[]{:S(2)}) collective-permute-start(f32[33,8,128]{2,1,0:T(8,128)} %get-tuple-element.65), channel_id=1, source_target_pairs={{0,7},{1,0},{2,1},{3,2},{4,3},{5,4},{6,5},{7,6},{8,15},{9,8},{10,9... | collective-permute-start | bytes 405512 | tf_op jit(solution)/shard_map/ppermute | solution.py:535
  5.6 0.0 copy-done.1
  5.6 0.0 copy-done
  5.6 4.6 %inner.5 = (f32[520,128]{1,0:T(8,128)S(1)}, f32[520,128]{1,0:T(8,128)}) custom-call(f32[24,128]{1,0:T(8,128)S(1)} %get-tuple-element.63.own, f32[1,2,32,32,128]{4,3,2,1,0:T(8,128)S(1)} %copy-done, f32[1,2,32,32,128]{4,3,2,1,0:T(8,128)S(1)} %copy-done.1), custom_call_target="tpu_custom_call" | custom-call | flops 100000000 | bytes 25165824 | tf_op jit(solution)/shard_map/inner/pallas_call | solution.py:284
  10.2 2.6 %collective-permute-start.7 = (f32[520,128]{1,0:T(8,128)}, f32[520,128]{1,0:T(8,128)S(1)}, u32[]{:S(2)}, u32[]{:S(2)}) collective-permute-start(f32[520,128]{1,0:T(8,128)} %get-tuple-element.71), channel_id=1, source_target_pairs={{0,5},{1,4},{2,7},{3,6},{4,1},{5,0},{6,3},{7,2},{8,13},{9,12},{10,... | collective-permute-start | bytes 798728 | tf_op jit(solution)/shard_map/ppermute | solution.py:514
  12.8 0.3 collective-permute-start.6
  13.1 0.0 copy-done.2
  13.2 0.0 collective-permute-done.4.y_lo
  13.2 0.0 collective-permute-done.5.y_hi
  13.3 8.7 %conditional.3 = (f32[608,128]{1,0:T(8,128)}, f32[608,128]{1,0:T(8,128)}, f32[520,128]{1,0:T(8,128)}, f32[520,128]{1,0:T(8,128)}) conditional(s32[]{:T(128)} %bitcast, (f32[608,128]{1,0:T(8,128)S(1)}, f32[608,128]{1,0:T(8,128)S(1)}, f32[24,128]{1,0:T(8,128)S(1)}, f32[1,2,32,32,128]{4,3,2,1,0:T(8,128)S(1)}, ...), branch_computations={%region_0.0_spmd, %region_1.0_spmd} | conditional | flops 100000000 | bytes 27656304 | solution.py:554
  13.3 0.1 collective-permute-start.2
  13.3 1.7 %collective-permute-start.3 = (f32[608,128]{1,0:T(8,128)S(1)}, f32[608,128]{1,0:T(8,128)}, u32[]{:S(2)}, u32[]{:S(2)}) collective-permute-start(f32[608,128]{1,0:T(8,128)S(1)} %get-tuple-element.38), channel_id=1, source_target_pairs={{0,24},{8,0},{16,8},{24,16},{1,25},{9,1},{17,9},{25,17},{2,26},{10... | collective-permute-start | bytes 933896 | tf_op jit(solution)/shard_map/cond/branch_1_fun/ppermute | solution.py:552
  15.1 4.6 %inner.4 = (f32[520,128]{1,0:T(8,128)}, f32[520,128]{1,0:T(8,128)}) custom-call(f32[24,128]{1,0:T(8,128)S(1)} %get-tuple-element.39.own, f32[1,2,32,32,128]{4,3,2,1,0:T(8,128)S(1)} %get-tuple-element.40.phase, f32[1,2,32,32,128]{4,3,2,1,0:T(8,128)S(1)} %get-tuple-element.41.solute), custom_call_target="tpu_custom_call" | custom-call | flops 100000000 | bytes 25165824 | tf_op jit(solution)/shard_map/cond/branch_1_fun/inner/pallas_call | solution.py:284
  19.7 1.5 %collective-permute-done.2 = f32[608,128]{1,0:T(8,128)} collective-permute-done((f32[608,128]{1,0:T(8,128)S(1)}, f32[608,128]{1,0:T(8,128)}, u32[]{:S(2)}, u32[]{:S(2)}) %collective-permute-start.2) | collective-permute-done | bytes 311328 | tf_op jit(solution)/shard_map/cond/branch_1_fun/ppermute | solution.py:552
  21.2 0.8 collective-permute-done.3
  22.0 1.6 %collective-permute-start.8 = (f32[520,128]{1,0:T(8,128)}, f32[520,128]{1,0:T(8,128)S(1)}, u32[]{:S(2)}, u32[]{:S(2)}) collective-permute-start(f32[520,128]{1,0:T(8,128)} %get-tuple-element.72), channel_id=1, source_target_pairs={{0,6},{1,7},{2,4},{3,5},{4,2},{5,3},{6,0},{7,1},{8,14},{9,15},{10,... | collective-permute-start | bytes 798728 | tf_op jit(solution)/shard_map/ppermute | solution.py:514
  23.6 1.3 %collective-permute-start.9 = (f32[520,128]{1,0:T(8,128)}, f32[520,128]{1,0:T(8,128)}, u32[]{:S(2)}, u32[]{:S(2)}) collective-permute-start(f32[520,128]{1,0:T(8,128)} %get-tuple-element.73), channel_id=1, source_target_pairs={{0,7},{1,6},{2,5},{3,4},{4,3},{5,2},{6,1},{7,0},{8,15},{9,14},{10,... | collective-permute-start | bytes 798728 | tf_op jit(solution)/shard_map/ppermute | solution.py:514
  24.9 9.8 %outer.1 = f32[4,520,128]{2,1,0:T(8,128)S(1)} custom-call(f32[24,128]{1,0:T(8,128)S(1)} %get-tuple-element.63.own, f32[1,2,32,32,128]{4,3,2,1,0:T(8,128)S(1)} %copy-done, f32[1,2,32,32,128]{4,3,2,1,0:T(8,128)S(1)} %copy-done.1, f32[33,8,128]{2,1,0:T(8,128)S(1)} %collective-permute-done.4.y_lo, f32[33,8,128]{2,1,0:T(8,128)S(1)} %collective-permute-done.5.y_hi, ...), custom_call_target="tpu_custom_call" | custom-call | flops 100000000 | bytes 41943040 | tf_op jit(solution)/shard_map/outer/pallas_call | solution.py:380
  34.7 26.1 %conditional.4 = (f32[4,520,128]{2,1,0:T(8,128)S(1)}) conditional(s32[]{:T(128)} %bitcast, f32[4,520,128]{2,1,0:T(8,128)S(1)} %outer.1, f32[4,520,128]{2,1,0:T(8,128)S(1)} %outer.1), branch_computations={%region_2.0_spmd, %region_3.0_spmd} | conditional | bytes 2129928 | solution.py:522
  34.7 26.0 %all_to_all.17 = f32[4,520,128]{2,1,0:T(8,128)S(1)} all-to-all(f32[4,520,128]{2,1,0:T(8,128)S(1)} %param.3), channel_id=1, replica_groups={{0,1,2,3},{4,5,6,7},{8,9,10,11},{12,13,14,15},{16,17,18,19},{20,21,22,2..., dimensions={0} | all-to-all | bytes 2129920 | tf_op jit(solution)/shard_map/cond/branch_1_fun/all_to_all | solution.py:520
  60.7 0.0 collective-permute-done.7.refs_1_
  60.7 0.0 collective-permute-done.6.refs_0_
  60.7 0.0 collective-permute-done.8.refs_2_
  60.7 0.0 collective-permute-done.9.refs_3_
  60.8 1.9 %route.1 = (f32[4,2,256,128]{3,2,1,0:T(8,128)S(1)}, f32[2,256,128]{2,1,0:T(8,128)S(1)}, f32[2,256,128]{2,1,0:T(8,128)S(1)}, f32[2,256,128]{2,1,0:T(8,128)S(1)}, ...) custom-call(f32[4,520,128]{2,1,0:T(8,128)S(1)} %get-tuple-element.88.near, f32[520,128]{1,0:T(8,128)S(1)} %collective-permute-done.6.refs_0_, ...), custom_call_target="tpu_custom_call" | custom-call | tf_op jit(solution)/shard_map/route/pallas_call | solution.py:430
  62.7 1.4 %collective-permute-start.10 = (f32[2,256,128]{2,1,0:T(8,128)S(1)}, f32[2,256,128]{2,1,0:T(8,128)S(1)}, u32[]{:S(2)}, u32[]{:S(2)}) collective-permute-start(f32[2,256,128]{2,1,0:T(8,128)S(1)} %get-tuple-element.76), channel_id=1, source_target_pairs={{0,4},{1,5},{2,6},{3,7},{4,0},{5,1},{6,2},{7,3},{8,12},{9,13},{10,... | collective-permute-start | bytes 786440 | tf_op jit(solution)/shard_map/ppermute | solution.py:514
  64.1 1.3 %collective-permute-start.11 = (f32[2,256,128]{2,1,0:T(8,128)S(1)}, f32[2,256,128]{2,1,0:T(8,128)S(1)}, u32[]{:S(2)}, u32[]{:S(2)}) collective-permute-start(f32[2,256,128]{2,1,0:T(8,128)S(1)} %get-tuple-element.77), channel_id=1, source_target_pairs={{0,5},{1,4},{2,7},{3,6},{4,1},{5,0},{6,3},{7,2},{8,13},{9,12},{10,... | collective-permute-start | bytes 786440 | tf_op jit(solution)/shard_map/ppermute | solution.py:514
  65.4 1.0 collective-permute-start.12
  66.4 2.2 %collective-permute-start.13 = (f32[2,256,128]{2,1,0:T(8,128)S(1)}, f32[2,256,128]{2,1,0:T(8,128)S(1)}, u32[]{:S(2)}, u32[]{:S(2)}) collective-permute-start(f32[2,256,128]{2,1,0:T(8,128)S(1)} %get-tuple-element.79), channel_id=1, source_target_pairs={{0,7},{1,6},{2,5},{3,4},{4,3},{5,2},{6,1},{7,0},{8,15},{9,14},{10,... | collective-permute-start | bytes 786440 | tf_op jit(solution)/shard_map/ppermute | solution.py:514
  68.6 35.9 %conditional.5 = (f32[4,2,256,128]{3,2,1,0:T(8,128)S(1)}) conditional(s32[]{:T(128)} %bitcast, f32[4,2,256,128]{3,2,1,0:T(8,128)S(1)} %get-tuple-element.75, f32[4,2,256,128]{3,2,1,0:T(8,128)S(1)} %get-tuple-element.75), branch_computations={%region_4.0_spmd, %region_5.0_spmd} | conditional | bytes 2097160 | solution.py:522
  68.6 35.9 %all_to_all.19 = f32[4,2,256,128]{3,2,1,0:T(8,128)S(1)} all-to-all(f32[4,2,256,128]{3,2,1,0:T(8,128)S(1)} %param.5), channel_id=1, replica_groups={{0,1,2,3},{4,5,6,7},{8,9,10,11},{12,13,14,15},{16,17,18,19},{20,21,22,2..., dimensions={0} | all-to-all | bytes 2097152 | tf_op jit(solution)/shard_map/cond/branch_1_fun/all_to_all | solution.py:520
  104.5 0.0 collective-permute-done.10.refs_0_
  104.5 0.0 collective-permute-done.11.refs_1_
  104.5 1.0 collective-permute-done.12.refs_2_
  105.5 4.7 %collective-permute-done.13.refs_3_ = f32[2,256,128]{2,1,0:T(8,128)S(1)} collective-permute-done((f32[2,256,128]{2,1,0:T(8,128)S(1)}, f32[2,256,128]{2,1,0:T(8,128)S(1)}, u32[]{:S(2)}, u32[]{:S(2)}) %collective-permute-start.13) | collective-permute-done | bytes 262176 | tf_op jit(solution)/shard_map/ppermute | solution.py:514
  110.2 2.0 %settle.1 = (f32[1,2,32,32,128]{4,3,2,1,0:T(8,128)}, f32[1,2,32,32,128]{4,3,2,1,0:T(8,128)}) custom-call(s32[16]{0:T(128)S(1)} %get-tuple-element.74.table, f32[4,2,256,128]{3,2,1,0:T(8,128)S(1)} %get-tuple-element.89.near, f32[2,256,128]{2,1,0:T(8,128)S(1)} %collective-permute-done.10.refs_0_, f32[2,256,128]{2,1,0:T(8,128)S(1)} %collective-permute-done.11.refs_1_, ...), custom_call_target="tpu_custom_call" | custom-call | tf_op jit(solution)/shard_map/settle/pallas_call | solution.py:494
  (1 shorter events, 0.0 us)
Async XLA Ops:
  0.6 5.0 %copy-start.1 = (f32[1,2,32,32,128]{4,3,2,1,0:T(8,128)S(1)}, f32[1,2,32,32,128]{4,3,2,1,0:T(8,128)}, u32[]{:S(2)}) copy-start(f32[1,2,32,32,128]{4,3,2,1,0:T(8,128)} %solute.3) | copy-start | bytes 3145732
  0.6 5.0 %copy-start = (f32[1,2,32,32,128]{4,3,2,1,0:T(8,128)S(1)}, f32[1,2,32,32,128]{4,3,2,1,0:T(8,128)}, u32[]{:S(2)}) copy-start(f32[1,2,32,32,128]{4,3,2,1,0:T(8,128)} %phase.3) | copy-start | bytes 3145732
  2.7 10.5 %copy-start.2 = (s32[1,2]{1,0:T(1,128)S(1)}, s32[1,2]{1,0:T(1,128)}, u32[]{:S(2)}) copy-start(s32[1,2]{1,0:T(1,128)} %owner.1) | copy-start | bytes 28
  2.7 10.5 %collective-permute-start.4 = (f32[33,8,128]{2,1,0:T(8,128)}, f32[33,8,128]{2,1,0:T(8,128)S(1)}, u32[]{:S(2)}, u32[]{:S(2)}) collective-permute-start(f32[33,8,128]{2,1,0:T(8,128)} %get-tuple-element.64), channel_id=1, source_target_pairs={{0,1},{1,2},{2,3},{3,4},{4,5},{5,6},{6,7},{7,0},{8,9},{9,10},{10,1... | collective-permute-start | bytes 405512 | tf_op jit(solution)/shard_map/ppermute | solution.py:534
  4.2 9.0 %collective-permute-start.5 = (f32[33,8,128]{2,1,0:T(8,128)}, f32[33,8,128]{2,1,0:T(8,128)S(1)}, u32[]{:S(2)}, u32[]{:S(2)}) collective-permute-start(f32[33,8,128]{2,1,0:T(8,128)} %get-tuple-element.65), channel_id=1, source_target_pairs={{0,7},{1,0},{2,1},{3,2},{4,3},{5,4},{6,5},{7,6},{8,15},{9,8},{10,9... | collective-permute-start | bytes 405512 | tf_op jit(solution)/shard_map/ppermute | solution.py:535
  10.2 50.6 %collective-permute-start.7 = (f32[520,128]{1,0:T(8,128)}, f32[520,128]{1,0:T(8,128)S(1)}, u32[]{:S(2)}, u32[]{:S(2)}) collective-permute-start(f32[520,128]{1,0:T(8,128)} %get-tuple-element.71), channel_id=1, source_target_pairs={{0,5},{1,4},{2,7},{3,6},{4,1},{5,0},{6,3},{7,2},{8,13},{9,12},{10,... | collective-permute-start | bytes 798728 | tf_op jit(solution)/shard_map/ppermute | solution.py:514
  12.8 47.9 %collective-permute-start.6 = (f32[520,128]{1,0:T(8,128)S(1)}, f32[520,128]{1,0:T(8,128)S(1)}, u32[]{:S(2)}, u32[]{:S(2)}) collective-permute-start(f32[520,128]{1,0:T(8,128)S(1)} %get-tuple-element.66._), channel_id=1, source_target_pairs={{0,4},{1,5},{2,6},{3,7},{4,0},{5,1},{6,2},{7,3},{8,12},{9,13},{10,... | collective-permute-start | bytes 798728 | tf_op jit(solution)/shard_map/ppermute | solution.py:514
  13.3 8.0 %collective-permute-start.2 = (f32[608,128]{1,0:T(8,128)S(1)}, f32[608,128]{1,0:T(8,128)}, u32[]{:S(2)}, u32[]{:S(2)}) collective-permute-start(f32[608,128]{1,0:T(8,128)S(1)} %get-tuple-element.37), channel_id=1, source_target_pairs={{0,8},{8,16},{16,24},{24,0},{1,9},{9,17},{17,25},{25,1},{2,10},{10... | collective-permute-start | bytes 933896 | tf_op jit(solution)/shard_map/cond/branch_1_fun/ppermute | solution.py:552
  13.3 8.7 %collective-permute-start.3 = (f32[608,128]{1,0:T(8,128)S(1)}, f32[608,128]{1,0:T(8,128)}, u32[]{:S(2)}, u32[]{:S(2)}) collective-permute-start(f32[608,128]{1,0:T(8,128)S(1)} %get-tuple-element.38), channel_id=1, source_target_pairs={{0,24},{8,0},{16,8},{24,16},{1,25},{9,1},{17,9},{25,17},{2,26},{10... | collective-permute-start | bytes 933896 | tf_op jit(solution)/shard_map/cond/branch_1_fun/ppermute | solution.py:552
  22.0 38.7 %collective-permute-start.8 = (f32[520,128]{1,0:T(8,128)}, f32[520,128]{1,0:T(8,128)S(1)}, u32[]{:S(2)}, u32[]{:S(2)}) collective-permute-start(f32[520,128]{1,0:T(8,128)} %get-tuple-element.72), channel_id=1, source_target_pairs={{0,6},{1,7},{2,4},{3,5},{4,2},{5,3},{6,0},{7,1},{8,14},{9,15},{10,... | collective-permute-start | bytes 798728 | tf_op jit(solution)/shard_map/ppermute | solution.py:514
  23.6 37.2 %collective-permute-start.9 = (f32[520,128]{1,0:T(8,128)}, f32[520,128]{1,0:T(8,128)}, u32[]{:S(2)}, u32[]{:S(2)}) collective-permute-start(f32[520,128]{1,0:T(8,128)} %get-tuple-element.73), channel_id=1, source_target_pairs={{0,7},{1,6},{2,5},{3,4},{4,3},{5,2},{6,1},{7,0},{8,15},{9,14},{10,... | collective-permute-start | bytes 798728 | tf_op jit(solution)/shard_map/ppermute | solution.py:514
  62.7 41.8 %collective-permute-start.10 = (f32[2,256,128]{2,1,0:T(8,128)S(1)}, f32[2,256,128]{2,1,0:T(8,128)S(1)}, u32[]{:S(2)}, u32[]{:S(2)}) collective-permute-start(f32[2,256,128]{2,1,0:T(8,128)S(1)} %get-tuple-element.76), channel_id=1, source_target_pairs={{0,4},{1,5},{2,6},{3,7},{4,0},{5,1},{6,2},{7,3},{8,12},{9,13},{10,... | collective-permute-start | bytes 786440 | tf_op jit(solution)/shard_map/ppermute | solution.py:514
  64.1 40.4 %collective-permute-start.11 = (f32[2,256,128]{2,1,0:T(8,128)S(1)}, f32[2,256,128]{2,1,0:T(8,128)S(1)}, u32[]{:S(2)}, u32[]{:S(2)}) collective-permute-start(f32[2,256,128]{2,1,0:T(8,128)S(1)} %get-tuple-element.77), channel_id=1, source_target_pairs={{0,5},{1,4},{2,7},{3,6},{4,1},{5,0},{6,3},{7,2},{8,13},{9,12},{10,... | collective-permute-start | bytes 786440 | tf_op jit(solution)/shard_map/ppermute | solution.py:514
  65.4 40.1 %collective-permute-start.12 = (f32[2,256,128]{2,1,0:T(8,128)S(1)}, f32[2,256,128]{2,1,0:T(8,128)S(1)}, u32[]{:S(2)}, u32[]{:S(2)}) collective-permute-start(f32[2,256,128]{2,1,0:T(8,128)S(1)} %get-tuple-element.78), channel_id=1, source_target_pairs={{0,6},{1,7},{2,4},{3,5},{4,2},{5,3},{6,0},{7,1},{8,14},{9,15},{10,... | collective-permute-start | bytes 786440 | tf_op jit(solution)/shard_map/ppermute | solution.py:514
  66.4 43.8 %collective-permute-start.13 = (f32[2,256,128]{2,1,0:T(8,128)S(1)}, f32[2,256,128]{2,1,0:T(8,128)S(1)}, u32[]{:S(2)}, u32[]{:S(2)}) collective-permute-start(f32[2,256,128]{2,1,0:T(8,128)S(1)} %get-tuple-element.79), channel_id=1, source_target_pairs={{0,7},{1,6},{2,5},{3,4},{4,3},{5,2},{6,1},{7,0},{8,15},{9,14},{10,... | collective-permute-start | bytes 786440 | tf_op jit(solution)/shard_map/ppermute | solution.py:514

commit v21 on v20

--- a/solution.py
+++ b/solution.py
@@ -539,7 +539,7 @@
         for index, value in zip(plan.batches[batch], values):
             far[index] = swap(value, half + index)
 
-    own_here, phase_here, solute_here = in_vmem(own), in_vmem(phase), in_vmem(solute)
+    own_here, phase_here, solute_here = own, phase, solute
     first = run_inner(plan, 0, own_here, phase_here, solute_here)
     send_far(0, first)
     to_prev, to_next = pack_x(phase_here, solute_here, own_here, y_lo, y_hi, first[0])
@@ -554,7 +554,7 @@
     (x_lo, x_hi), second = lax.cond(together, around, around, to_next, to_prev, own, phase, solute)
     send_far(1, second)
     near = run_outer(plan, own_here, phase_here, solute_here, (y_lo, y_hi, in_vmem(x_lo), in_vmem(x_hi)))
-    far = [far[index] for index in range(half)]
+    far = [in_vmem(far[index]) for index in range(half)]
     near = among_half(plan, near, together)
     near, far, table = route(plan, in_vmem(near), far)
     far = [swap(values, half + index) for index, values in enumerate(far)]

time: 112 us -> 112 us (level)
  blocking collectives: 61.9 us -> 60.6 us
    all_to_all x2, blocking collectives: 61.9 us -> 60.6 us  [exchange(): lax.all_to_all(values, 'gy', 0, 0, axis_index_groups=groups, tiled=True)]
  transfers between devices with their start and end apart: 12 -> 12, of which waited for: 4 -> 4; matrix products, arithmetic and copies ran while one was open for 0% -> 0% of each run, Pallas kernels for 17% -> 18%
where the time goes in v21:
time: 112 us
  blocking collectives  60.6 us (54%)
  Pallas kernels  25.1 us (22%)
  starting transfers between devices  16.6 us (15%)
  waiting for transfers between devices  8.51 us (8%)
    all_to_all x2, blocking collectives, exchange(): lax.all_to_all(values, 'gy', 0, 0, axis_index_groups=groups, tiled=True)  60.6 us
    ppermute x8, starting transfers between devices, swap(): lax.ppermute(values, 'gy', [(i, i ^ mask) for i in range(lax.axis_size('g...  11.8 us
    pallas_call x1, Pallas kernels, run_outer(): pl.pallas_call(functools.partial(outer_kernel, plan), in_specs=[vmem] * 7...  10.2 us
    pallas_call x2, Pallas kernels, run_inner(): pl.pallas_call(functools.partial(inner_kernel, plan, batch), in_specs=[vm...  9.97 us
    ppermute x8, waiting for transfers between devices, swap(): lax.ppermute(values, 'gy', [(i, i ^ mask) for i in range(lax.axis_size('g...  6.35 us
  transfers between devices with their start and end apart: 12, of which 4 were waited for; matrix products, arithmetic and copies ran while one was open for 0% of the time, Pallas kernels for 18%

profile of v21, /device:TPU:8, one launch (start us, length us, event | category | flops | bytes accessed | tf_op | source)
XLA Modules:
  0.0 111.6 jit_solution(14858738504596139351)
XLA Ops:
  0.6 0.0 copy-start
  0.6 2.0 %pack_y.1 = (f32[33,8,128]{2,1,0:T(8,128)}, f32[33,8,128]{2,1,0:T(8,128)}, f32[24,128]{1,0:T(8,128)S(1)}) custom-call(f32[1,2]{1,0:T(1,128)} %under.1, f32[1,2]{1,0:T(1,128)} %mobile.1, f32[1,2]{1,0:T(1,128)} %spread.1, s32[1,2]{1,0:T(1,128)} %owner.1, f32[1,2,32,32,128]{4,3,2,1,0:T(8,128)} %phase.3, f32[1,2,32,32,128]{4,3,2,1,0:T(8,128)} %phase.3, ...), custom_call_target="tpu_custom_call" | custom-call | tf_op jit(solution)/shard_map/pack_y/pallas_call | solution.py:48
  2.6 0.0 copy-start.2
  2.6 0.0 copy-start.1
  2.6 1.6 %collective-permute-start.4 = (f32[33,8,128]{2,1,0:T(8,128)}, f32[33,8,128]{2,1,0:T(8,128)S(1)}, u32[]{:S(2)}, u32[]{:S(2)}) collective-permute-start(f32[33,8,128]{2,1,0:T(8,128)} %get-tuple-element.64), channel_id=1, source_target_pairs={{0,1},{1,2},{2,3},{3,4},{4,5},{5,6},{6,7},{7,0},{8,9},{9,10},{10,1... | collective-permute-start | bytes 405512 | tf_op jit(solution)/shard_map/ppermute | solution.py:534
  4.2 1.4 %collective-permute-start.5 = (f32[33,8,128]{2,1,0:T(8,128)}, f32[33,8,128]{2,1,0:T(8,128)S(1)}, u32[]{:S(2)}, u32[]{:S(2)}) collective-permute-start(f32[33,8,128]{2,1,0:T(8,128)} %get-tuple-element.65), channel_id=1, source_target_pairs={{0,7},{1,0},{2,1},{3,2},{4,3},{5,4},{6,5},{7,6},{8,15},{9,8},{10,9... | collective-permute-start | bytes 405512 | tf_op jit(solution)/shard_map/ppermute | solution.py:535
  5.6 0.0 copy-done
  5.6 5.2 %inner.5 = (f32[520,128]{1,0:T(8,128)S(1)}, f32[520,128]{1,0:T(8,128)S(1)}) custom-call(f32[24,128]{1,0:T(8,128)S(1)} %get-tuple-element.63.own, f32[1,2,32,32,128]{4,3,2,1,0:T(8,128)S(1)} %copy-done, f32[1,2,32,32,128]{4,3,2,1,0:T(8,128)} %solute.3), custom_call_target="tpu_custom_call" | custom-call | flops 100000000 | bytes 25165824 | tf_op jit(solution)/shard_map/inner/pallas_call | solution.py:284
  10.8 2.7 %collective-permute-start.7 = (f32[520,128]{1,0:T(8,128)S(1)}, f32[520,128]{1,0:T(8,128)S(1)}, u32[]{:S(2)}, u32[]{:S(2)}) collective-permute-start(f32[520,128]{1,0:T(8,128)S(1)} %get-tuple-element.71), channel_id=1, source_target_pairs={{0,5},{1,4},{2,7},{3,6},{4,1},{5,0},{6,3},{7,2},{8,13},{9,12},{10,... | collective-permute-start | bytes 798728 | tf_op jit(solution)/shard_map/ppermute | solution.py:514
  13.5 0.3 collective-permute-start.6
  13.8 0.0 copy-done.2
  13.9 0.0 collective-permute-done.4.y_lo
  13.9 0.0 collective-permute-done.5.y_hi
  13.9 0.0 copy-done.1
  14.0 8.7 %conditional.3 = (f32[608,128]{1,0:T(8,128)}, f32[608,128]{1,0:T(8,128)}, f32[520,128]{1,0:T(8,128)}, f32[520,128]{1,0:T(8,128)}) conditional(s32[]{:T(128)} %bitcast, (f32[608,128]{1,0:T(8,128)S(1)}, f32[608,128]{1,0:T(8,128)S(1)}, f32[24,128]{1,0:T(8,128)S(1)}, f32[1,2,32,32,128]{4,3,2,1,0:T(8,128)S(1)}, ...), branch_computations={%region_0.0_spmd, %region_1.0_spmd} | conditional | flops 100000000 | bytes 27656304 | solution.py:554
  14.0 0.1 collective-permute-start.2
  14.1 1.7 %collective-permute-start.3 = (f32[608,128]{1,0:T(8,128)S(1)}, f32[608,128]{1,0:T(8,128)}, u32[]{:S(2)}, u32[]{:S(2)}) collective-permute-start(f32[608,128]{1,0:T(8,128)S(1)} %get-tuple-element.38), channel_id=1, source_target_pairs={{0,24},{8,0},{16,8},{24,16},{1,25},{9,1},{17,9},{25,17},{2,26},{10... | collective-permute-start | bytes 933896 | tf_op jit(solution)/shard_map/cond/branch_1_fun/ppermute | solution.py:552
  15.8 4.8 %inner.4 = (f32[520,128]{1,0:T(8,128)}, f32[520,128]{1,0:T(8,128)}) custom-call(f32[24,128]{1,0:T(8,128)S(1)} %get-tuple-element.39.own, f32[1,2,32,32,128]{4,3,2,1,0:T(8,128)S(1)} %get-tuple-element.40.phase, f32[1,2,32,32,128]{4,3,2,1,0:T(8,128)S(1)} %get-tuple-element.41.solute), custom_call_target="tpu_custom_call" | custom-call | flops 100000000 | bytes 25165824 | tf_op jit(solution)/shard_map/cond/branch_1_fun/inner/pallas_call | solution.py:284
  20.6 1.4 %collective-permute-done.2 = f32[608,128]{1,0:T(8,128)} collective-permute-done((f32[608,128]{1,0:T(8,128)S(1)}, f32[608,128]{1,0:T(8,128)}, u32[]{:S(2)}, u32[]{:S(2)}) %collective-permute-start.2) | collective-permute-done | bytes 311328 | tf_op jit(solution)/shard_map/cond/branch_1_fun/ppermute | solution.py:552
  21.9 0.8 collective-permute-done.3
  22.7 1.6 %collective-permute-start.8 = (f32[520,128]{1,0:T(8,128)}, f32[520,128]{1,0:T(8,128)S(1)}, u32[]{:S(2)}, u32[]{:S(2)}) collective-permute-start(f32[520,128]{1,0:T(8,128)} %get-tuple-element.72), channel_id=1, source_target_pairs={{0,6},{1,7},{2,4},{3,5},{4,2},{5,3},{6,0},{7,1},{8,14},{9,15},{10,... | collective-permute-start | bytes 798728 | tf_op jit(solution)/shard_map/ppermute | solution.py:514
  24.3 1.3 %collective-permute-start.9 = (f32[520,128]{1,0:T(8,128)}, f32[520,128]{1,0:T(8,128)S(1)}, u32[]{:S(2)}, u32[]{:S(2)}) collective-permute-start(f32[520,128]{1,0:T(8,128)} %get-tuple-element.73), channel_id=1, source_target_pairs={{0,7},{1,6},{2,5},{3,4},{4,3},{5,2},{6,1},{7,0},{8,15},{9,14},{10,... | collective-permute-start | bytes 798728 | tf_op jit(solution)/shard_map/ppermute | solution.py:514
  25.6 10.2 %outer.1 = f32[4,520,128]{2,1,0:T(8,128)S(1)} custom-call(f32[24,128]{1,0:T(8,128)S(1)} %get-tuple-element.63.own, f32[1,2,32,32,128]{4,3,2,1,0:T(8,128)S(1)} %copy-done, f32[1,2,32,32,128]{4,3,2,1,0:T(8,128)} %solute.3, f32[33,8,128]{2,1,0:T(8,128)S(1)} %collective-permute-done.4.y_lo, f32[33,8,128]{2,1,0:T(8,128)S(1)} %collective-permute-done.5.y_hi, ...), custom_call_target="tpu_custom_call" | custom-call | flops 100000000 | bytes 41943040 | tf_op jit(solution)/shard_map/outer/pallas_call | solution.py:380
  35.8 26.1 %conditional.4 = (f32[4,520,128]{2,1,0:T(8,128)S(1)}) conditional(s32[]{:T(128)} %bitcast, f32[4,520,128]{2,1,0:T(8,128)S(1)} %outer.1, f32[4,520,128]{2,1,0:T(8,128)S(1)} %outer.1), branch_computations={%region_2.0_spmd, %region_3.0_spmd} | conditional | bytes 2129928 | solution.py:522
  35.8 26.0 %all_to_all.17 = f32[4,520,128]{2,1,0:T(8,128)S(1)} all-to-all(f32[4,520,128]{2,1,0:T(8,128)S(1)} %param.3), channel_id=1, replica_groups={{0,1,2,3},{4,5,6,7},{8,9,10,11},{12,13,14,15},{16,17,18,19},{20,21,22,2..., dimensions={0} | all-to-all | bytes 2129920 | tf_op jit(solution)/shard_map/cond/branch_1_fun/all_to_all | solution.py:520
  61.9 0.0 collective-permute-done.7.refs_1_
  61.9 0.0 collective-permute-done.6.refs_0_
  61.9 0.0 collective-permute-done.8.refs_2_
  61.9 0.0 collective-permute-done.9.refs_3_
  61.9 0.9 route.1
  62.8 0.8 collective-permute-start.10
  63.6 2.0 %collective-permute-start.11 = (f32[2,256,128]{2,1,0:T(8,128)S(1)}, f32[2,256,128]{2,1,0:T(8,128)S(1)}, u32[]{:S(2)}, u32[]{:S(2)}) collective-permute-start(f32[2,256,128]{2,1,0:T(8,128)S(1)} %get-tuple-element.77), channel_id=1, source_target_pairs={{0,5},{1,4},{2,7},{3,6},{4,1},{5,0},{6,3},{7,2},{8,13},{9,12},{10,... | collective-permute-start | bytes 786440 | tf_op jit(solution)/shard_map/ppermute | solution.py:514
  65.5 0.6 collective-permute-start.12
  66.1 2.6 %collective-permute-start.13 = (f32[2,256,128]{2,1,0:T(8,128)S(1)}, f32[2,256,128]{2,1,0:T(8,128)S(1)}, u32[]{:S(2)}, u32[]{:S(2)}) collective-permute-start(f32[2,256,128]{2,1,0:T(8,128)S(1)} %get-tuple-element.79), channel_id=1, source_target_pairs={{0,7},{1,6},{2,5},{3,4},{4,3},{5,2},{6,1},{7,0},{8,15},{9,14},{10,... | collective-permute-start | bytes 786440 | tf_op jit(solution)/shard_map/ppermute | solution.py:514
  68.7 34.6 %conditional.5 = (f32[4,2,256,128]{3,2,1,0:T(8,128)S(1)}) conditional(s32[]{:T(128)} %bitcast, f32[4,2,256,128]{3,2,1,0:T(8,128)S(1)} %get-tuple-element.75, f32[4,2,256,128]{3,2,1,0:T(8,128)S(1)} %get-tuple-element.75), branch_computations={%region_4.0_spmd, %region_5.0_spmd} | conditional | bytes 2097160 | solution.py:522
  68.7 34.6 %all_to_all.19 = f32[4,2,256,128]{3,2,1,0:T(8,128)S(1)} all-to-all(f32[4,2,256,128]{3,2,1,0:T(8,128)S(1)} %param.5), channel_id=1, replica_groups={{0,1,2,3},{4,5,6,7},{8,9,10,11},{12,13,14,15},{16,17,18,19},{20,21,22,2..., dimensions={0} | all-to-all | bytes 2097152 | tf_op jit(solution)/shard_map/cond/branch_1_fun/all_to_all | solution.py:520
  103.3 0.0 collective-permute-done.10.refs_0_
  103.3 0.0 collective-permute-done.11.refs_1_
  103.3 1.7 %collective-permute-done.12.refs_2_ = f32[2,256,128]{2,1,0:T(8,128)S(1)} collective-permute-done((f32[2,256,128]{2,1,0:T(8,128)S(1)}, f32[2,256,128]{2,1,0:T(8,128)S(1)}, u32[]{:S(2)}, u32[]{:S(2)}) %collective-permute-start.12) | collective-permute-done | bytes 262176 | tf_op jit(solution)/shard_map/ppermute | solution.py:514
  105.0 4.7 %collective-permute-done.13.refs_3_ = f32[2,256,128]{2,1,0:T(8,128)S(1)} collective-permute-done((f32[2,256,128]{2,1,0:T(8,128)S(1)}, f32[2,256,128]{2,1,0:T(8,128)S(1)}, u32[]{:S(2)}, u32[]{:S(2)}) %collective-permute-start.13) | collective-permute-done | bytes 262176 | tf_op jit(solution)/shard_map/ppermute | solution.py:514
  109.6 2.0 %settle.1 = (f32[1,2,32,32,128]{4,3,2,1,0:T(8,128)}, f32[1,2,32,32,128]{4,3,2,1,0:T(8,128)}) custom-call(s32[16]{0:T(128)S(1)} %get-tuple-element.74.table, f32[4,2,256,128]{3,2,1,0:T(8,128)S(1)} %get-tuple-element.89.near, f32[2,256,128]{2,1,0:T(8,128)S(1)} %collective-permute-done.10.refs_0_, f32[2,256,128]{2,1,0:T(8,128)S(1)} %collective-permute-done.11.refs_1_, ...), custom_call_target="tpu_custom_call" | custom-call | tf_op jit(solution)/shard_map/settle/pallas_call | solution.py:494
  (1 shorter events, 0.0 us)
Async XLA Ops:
  0.6 4.9 %copy-start = (f32[1,2,32,32,128]{4,3,2,1,0:T(8,128)S(1)}, f32[1,2,32,32,128]{4,3,2,1,0:T(8,128)}, u32[]{:S(2)}) copy-start(f32[1,2,32,32,128]{4,3,2,1,0:T(8,128)} %phase.3) | copy-start | bytes 3145732
  2.6 11.2 %copy-start.2 = (s32[1,2]{1,0:T(1,128)S(1)}, s32[1,2]{1,0:T(1,128)}, u32[]{:S(2)}) copy-start(s32[1,2]{1,0:T(1,128)} %owner.1) | copy-start | bytes 28
  2.6 11.3 %copy-start.1 = (f32[1,2,32,32,128]{4,3,2,1,0:T(8,128)S(1)}, f32[1,2,32,32,128]{4,3,2,1,0:T(8,128)}, u32[]{:S(2)}) copy-start(f32[1,2,32,32,128]{4,3,2,1,0:T(8,128)} %solute.3) | copy-start | bytes 3145732
  2.6 11.3 %collective-permute-start.4 = (f32[33,8,128]{2,1,0:T(8,128)}, f32[33,8,128]{2,1,0:T(8,128)S(1)}, u32[]{:S(2)}, u32[]{:S(2)}) collective-permute-start(f32[33,8,128]{2,1,0:T(8,128)} %get-tuple-element.64), channel_id=1, source_target_pairs={{0,1},{1,2},{2,3},{3,4},{4,5},{5,6},{6,7},{7,0},{8,9},{9,10},{10,1... | collective-permute-start | bytes 405512 | tf_op jit(solution)/shard_map/ppermute | solution.py:534
  4.2 9.7 %collective-permute-start.5 = (f32[33,8,128]{2,1,0:T(8,128)}, f32[33,8,128]{2,1,0:T(8,128)S(1)}, u32[]{:S(2)}, u32[]{:S(2)}) collective-permute-start(f32[33,8,128]{2,1,0:T(8,128)} %get-tuple-element.65), channel_id=1, source_target_pairs={{0,7},{1,0},{2,1},{3,2},{4,3},{5,4},{6,5},{7,6},{8,15},{9,8},{10,9... | collective-permute-start | bytes 405512 | tf_op jit(solution)/shard_map/ppermute | solution.py:535
  10.8 51.1 %collective-permute-start.7 = (f32[520,128]{1,0:T(8,128)S(1)}, f32[520,128]{1,0:T(8,128)S(1)}, u32[]{:S(2)}, u32[]{:S(2)}) collective-permute-start(f32[520,128]{1,0:T(8,128)S(1)} %get-tuple-element.71), channel_id=1, source_target_pairs={{0,5},{1,4},{2,7},{3,6},{4,1},{5,0},{6,3},{7,2},{8,13},{9,12},{10,... | collective-permute-start | bytes 798728 | tf_op jit(solution)/shard_map/ppermute | solution.py:514
  13.5 48.4 %collective-permute-start.6 = (f32[520,128]{1,0:T(8,128)S(1)}, f32[520,128]{1,0:T(8,128)S(1)}, u32[]{:S(2)}, u32[]{:S(2)}) collective-permute-start(f32[520,128]{1,0:T(8,128)S(1)} %get-tuple-element.66._), channel_id=1, source_target_pairs={{0,4},{1,5},{2,6},{3,7},{4,0},{5,1},{6,2},{7,3},{8,12},{9,13},{10,... | collective-permute-start | bytes 798728 | tf_op jit(solution)/shard_map/ppermute | solution.py:514
  14.0 8.0 %collective-permute-start.2 = (f32[608,128]{1,0:T(8,128)S(1)}, f32[608,128]{1,0:T(8,128)}, u32[]{:S(2)}, u32[]{:S(2)}) collective-permute-start(f32[608,128]{1,0:T(8,128)S(1)} %get-tuple-element.37), channel_id=1, source_target_pairs={{0,8},{8,16},{16,24},{24,0},{1,9},{9,17},{17,25},{25,1},{2,10},{10... | collective-permute-start | bytes 933896 | tf_op jit(solution)/shard_map/cond/branch_1_fun/ppermute | solution.py:552
  14.1 8.7 %collective-permute-start.3 = (f32[608,128]{1,0:T(8,128)S(1)}, f32[608,128]{1,0:T(8,128)}, u32[]{:S(2)}, u32[]{:S(2)}) collective-permute-start(f32[608,128]{1,0:T(8,128)S(1)} %get-tuple-element.38), channel_id=1, source_target_pairs={{0,24},{8,0},{16,8},{24,16},{1,25},{9,1},{17,9},{25,17},{2,26},{10... | collective-permute-start | bytes 933896 | tf_op jit(solution)/shard_map/cond/branch_1_fun/ppermute | solution.py:552
  22.7 39.2 %collective-permute-start.8 = (f32[520,128]{1,0:T(8,128)}, f32[520,128]{1,0:T(8,128)S(1)}, u32[]{:S(2)}, u32[]{:S(2)}) collective-permute-start(f32[520,128]{1,0:T(8,128)} %get-tuple-element.72), channel_id=1, source_target_pairs={{0,6},{1,7},{2,4},{3,5},{4,2},{5,3},{6,0},{7,1},{8,14},{9,15},{10,... | collective-permute-start | bytes 798728 | tf_op jit(solution)/shard_map/ppermute | solution.py:514
  24.3 37.6 %collective-permute-start.9 = (f32[520,128]{1,0:T(8,128)}, f32[520,128]{1,0:T(8,128)S(1)}, u32[]{:S(2)}, u32[]{:S(2)}) collective-permute-start(f32[520,128]{1,0:T(8,128)} %get-tuple-element.73), channel_id=1, source_target_pairs={{0,7},{1,6},{2,5},{3,4},{4,3},{5,2},{6,1},{7,0},{8,15},{9,14},{10,... | collective-permute-start | bytes 798728 | tf_op jit(solution)/shard_map/ppermute | solution.py:514
  62.8 40.5 %collective-permute-start.10 = (f32[2,256,128]{2,1,0:T(8,128)S(1)}, f32[2,256,128]{2,1,0:T(8,128)S(1)}, u32[]{:S(2)}, u32[]{:S(2)}) collective-permute-start(f32[2,256,128]{2,1,0:T(8,128)S(1)} %get-tuple-element.76), channel_id=1, source_target_pairs={{0,4},{1,5},{2,6},{3,7},{4,0},{5,1},{6,2},{7,3},{8,12},{9,13},{10,... | collective-permute-start | bytes 786440 | tf_op jit(solution)/shard_map/ppermute | solution.py:514
  63.6 39.7 %collective-permute-start.11 = (f32[2,256,128]{2,1,0:T(8,128)S(1)}, f32[2,256,128]{2,1,0:T(8,128)S(1)}, u32[]{:S(2)}, u32[]{:S(2)}) collective-permute-start(f32[2,256,128]{2,1,0:T(8,128)S(1)} %get-tuple-element.77), channel_id=1, source_target_pairs={{0,5},{1,4},{2,7},{3,6},{4,1},{5,0},{6,3},{7,2},{8,13},{9,12},{10,... | collective-permute-start | bytes 786440 | tf_op jit(solution)/shard_map/ppermute | solution.py:514
  65.5 39.4 %collective-permute-start.12 = (f32[2,256,128]{2,1,0:T(8,128)S(1)}, f32[2,256,128]{2,1,0:T(8,128)S(1)}, u32[]{:S(2)}, u32[]{:S(2)}) collective-permute-start(f32[2,256,128]{2,1,0:T(8,128)S(1)} %get-tuple-element.78), channel_id=1, source_target_pairs={{0,6},{1,7},{2,4},{3,5},{4,2},{5,3},{6,0},{7,1},{8,14},{9,15},{10,... | collective-permute-start | bytes 786440 | tf_op jit(solution)/shard_map/ppermute | solution.py:514
  66.1 43.5 %collective-permute-start.13 = (f32[2,256,128]{2,1,0:T(8,128)S(1)}, f32[2,256,128]{2,1,0:T(8,128)S(1)}, u32[]{:S(2)}, u32[]{:S(2)}) collective-permute-start(f32[2,256,128]{2,1,0:T(8,128)S(1)} %get-tuple-element.79), channel_id=1, source_target_pairs={{0,7},{1,6},{2,5},{3,4},{4,3},{5,2},{6,1},{7,0},{8,15},{9,14},{10,... | collective-permute-start | bytes 786440 | tf_op jit(solution)/shard_map/ppermute | solution.py:514

commit v22 on v21

--- a/solution.py
+++ b/solution.py
@@ -540,7 +540,7 @@
             far[index] = swap(value, half + index)
 
     own_here, phase_here, solute_here = own, phase, solute
-    first = run_inner(plan, 0, own_here, phase_here, solute_here)
+    first = run_inner(plan, 0, own_here, phase_here, in_vmem(solute_here))
     send_far(0, first)
     to_prev, to_next = pack_x(phase_here, solute_here, own_here, y_lo, y_hi, first[0])
     together = owner[0, 0] >= 0

time: 112 us -> 111 us (level)
  Pallas kernels: 25.1 us -> 23.3 us
    pallas_call x2, Pallas kernels: 9.97 us -> 8.29 us  [run_inner(): pl.pallas_call(functools.partial(inner_kernel, plan, batch), in_specs=[vm...]
  transfers between devices with their start and end apart: 12 -> 12, of which waited for: 4 -> 4; matrix products, arithmetic and copies ran while one was open for 0% -> 0% of each run, Pallas kernels for 18% -> 17%
where the time goes in v22:
time: 111 us; the launch traced here: 110 us
  blocking collectives  60.8 us (55%)
  Pallas kernels  23.3 us (21%)
  starting transfers between devices  16.6 us (15%)
  waiting for transfers between devices  8.67 us (8%)
    all_to_all x2, blocking collectives, exchange(): lax.all_to_all(values, 'gy', 0, 0, axis_index_groups=groups, tiled=True)  60.8 us
    ppermute x8, starting transfers between devices, swap(): lax.ppermute(values, 'gy', [(i, i ^ mask) for i in range(lax.axis_size('g...  11.8 us
    pallas_call x1, Pallas kernels, run_outer(): pl.pallas_call(functools.partial(outer_kernel, plan), in_specs=[vmem] * 7...  10.1 us
    pallas_call x2, Pallas kernels, run_inner(): pl.pallas_call(functools.partial(inner_kernel, plan, batch), in_specs=[vm...  8.29 us
    ppermute x8, waiting for transfers between devices, swap(): lax.ppermute(values, 'gy', [(i, i ^ mask) for i in range(lax.axis_size('g...  6.24 us
  transfers between devices with their start and end apart: 12, of which 4 were waited for; matrix products, arithmetic and copies ran while one was open for 0% of the time, Pallas kernels for 17%

profile of v22, /device:TPU:8, one launch (start us, length us, event | category | flops | bytes accessed | tf_op | source)
XLA Modules:
  0.0 110.3 jit_solution(5681847131705494035)
XLA Ops:
  0.6 0.0 copy-start
  0.6 0.0 copy-start.1
  0.7 2.0 %pack_y.1 = (f32[33,8,128]{2,1,0:T(8,128)}, f32[33,8,128]{2,1,0:T(8,128)}, f32[24,128]{1,0:T(8,128)S(1)}) custom-call(f32[1,2]{1,0:T(1,128)} %under.1, f32[1,2]{1,0:T(1,128)} %mobile.1, f32[1,2]{1,0:T(1,128)} %spread.1, s32[1,2]{1,0:T(1,128)} %owner.1, f32[1,2,32,32,128]{4,3,2,1,0:T(8,128)} %phase.3, f32[1,2,32,32,128]{4,3,2,1,0:T(8,128)} %phase.3, ...), custom_call_target="tpu_custom_call" | custom-call | tf_op jit(solution)/shard_map/pack_y/pallas_call | solution.py:48
  2.7 0.0 copy-start.3
  2.7 0.0 copy-start.2
  2.7 1.6 %collective-permute-start.4 = (f32[33,8,128]{2,1,0:T(8,128)}, f32[33,8,128]{2,1,0:T(8,128)S(1)}, u32[]{:S(2)}, u32[]{:S(2)}) collective-permute-start(f32[33,8,128]{2,1,0:T(8,128)} %get-tuple-element.64), channel_id=1, source_target_pairs={{0,1},{1,2},{2,3},{3,4},{4,5},{5,6},{6,7},{7,0},{8,9},{9,10},{10,1... | collective-permute-start | bytes 405512 | tf_op jit(solution)/shard_map/ppermute | solution.py:534
  4.2 1.4 %collective-permute-start.5 = (f32[33,8,128]{2,1,0:T(8,128)}, f32[33,8,128]{2,1,0:T(8,128)S(1)}, u32[]{:S(2)}, u32[]{:S(2)}) collective-permute-start(f32[33,8,128]{2,1,0:T(8,128)} %get-tuple-element.65), channel_id=1, source_target_pairs={{0,7},{1,0},{2,1},{3,2},{4,3},{5,4},{6,5},{7,6},{8,15},{9,8},{10,9... | collective-permute-start | bytes 405512 | tf_op jit(solution)/shard_map/ppermute | solution.py:535
  5.6 0.0 copy-done
  5.6 0.0 copy-done.1
  5.6 3.8 %inner.5 = (f32[520,128]{1,0:T(8,128)S(1)}, f32[520,128]{1,0:T(8,128)S(1)}) custom-call(f32[24,128]{1,0:T(8,128)S(1)} %get-tuple-element.63.own, f32[1,2,32,32,128]{4,3,2,1,0:T(8,128)S(1)} %copy-done.1, f32[1,2,32,32,128]{4,3,2,1,0:T(8,128)S(1)} %copy-done), custom_call_target="tpu_custom_call" | custom-call | flops 100000000 | bytes 25165824 | tf_op jit(solution)/shard_map/inner/pallas_call | solution.py:284
  9.5 2.7 %collective-permute-start.7 = (f32[520,128]{1,0:T(8,128)S(1)}, f32[520,128]{1,0:T(8,128)S(1)}, u32[]{:S(2)}, u32[]{:S(2)}) collective-permute-start(f32[520,128]{1,0:T(8,128)S(1)} %get-tuple-element.71), channel_id=1, source_target_pairs={{0,5},{1,4},{2,7},{3,6},{4,1},{5,0},{6,3},{7,2},{8,13},{9,12},{10,... | collective-permute-start | bytes 798728 | tf_op jit(solution)/shard_map/ppermute | solution.py:514
  12.2 0.3 collective-permute-start.6
  12.5 0.0 copy-done.3
  12.5 0.0 collective-permute-done.4.y_lo
  12.6 0.0 collective-permute-done.5.y_hi
  12.6 0.0 copy-done.2
  12.6 8.7 %conditional.3 = (f32[608,128]{1,0:T(8,128)}, f32[608,128]{1,0:T(8,128)}, f32[520,128]{1,0:T(8,128)S(1)}, f32[520,128]{1,0:T(8,128)}) conditional(s32[]{:T(128)} %bitcast, (f32[608,128]{1,0:T(8,128)S(1)}, f32[608,128]{1,0:T(8,128)S(1)}, f32[24,128]{1,0:T(8,128)S(1)}, f32[1,2,32,32,128]{4,3,2,1,0:T(8,128)S(1)}, ...), branch_computations={%region_0.0_spmd, %region_1.0_spmd} | conditional | flops 100000000 | bytes 27656304 | solution.py:554
  12.7 0.1 collective-permute-start.2
  12.7 1.7 %collective-permute-start.3 = (f32[608,128]{1,0:T(8,128)S(1)}, f32[608,128]{1,0:T(8,128)}, u32[]{:S(2)}, u32[]{:S(2)}) collective-permute-start(f32[608,128]{1,0:T(8,128)S(1)} %get-tuple-element.38), channel_id=1, source_target_pairs={{0,24},{8,0},{16,8},{24,16},{1,25},{9,1},{17,9},{25,17},{2,26},{10... | collective-permute-start | bytes 933896 | tf_op jit(solution)/shard_map/cond/branch_1_fun/ppermute | solution.py:552
  14.5 4.5 %inner.4 = (f32[520,128]{1,0:T(8,128)S(1)}, f32[520,128]{1,0:T(8,128)}) custom-call(f32[24,128]{1,0:T(8,128)S(1)} %get-tuple-element.39.own, f32[1,2,32,32,128]{4,3,2,1,0:T(8,128)S(1)} %get-tuple-element.40.phase, f32[1,2,32,32,128]{4,3,2,1,0:T(8,128)S(1)} %get-tuple-element.41.solute), custom_call_target="tpu_custom_call" | custom-call | flops 100000000 | bytes 25165824 | tf_op jit(solution)/shard_map/cond/branch_1_fun/inner/pallas_call | solution.py:284
  19.0 1.7 %collective-permute-done.2 = f32[608,128]{1,0:T(8,128)} collective-permute-done((f32[608,128]{1,0:T(8,128)S(1)}, f32[608,128]{1,0:T(8,128)}, u32[]{:S(2)}, u32[]{:S(2)}) %collective-permute-start.2) | collective-permute-done | bytes 311328 | tf_op jit(solution)/shard_map/cond/branch_1_fun/ppermute | solution.py:552
  20.6 0.8 collective-permute-done.3
  21.4 1.6 %collective-permute-start.8 = (f32[520,128]{1,0:T(8,128)S(1)}, f32[520,128]{1,0:T(8,128)S(1)}, u32[]{:S(2)}, u32[]{:S(2)}) collective-permute-start(f32[520,128]{1,0:T(8,128)S(1)} %get-tuple-element.72), channel_id=1, source_target_pairs={{0,6},{1,7},{2,4},{3,5},{4,2},{5,3},{6,0},{7,1},{8,14},{9,15},{10,... | collective-permute-start | bytes 798728 | tf_op jit(solution)/shard_map/ppermute | solution.py:514
  23.0 1.3 %collective-permute-start.9 = (f32[520,128]{1,0:T(8,128)}, f32[520,128]{1,0:T(8,128)S(1)}, u32[]{:S(2)}, u32[]{:S(2)}) collective-permute-start(f32[520,128]{1,0:T(8,128)} %get-tuple-element.73), channel_id=1, source_target_pairs={{0,7},{1,6},{2,5},{3,4},{4,3},{5,2},{6,1},{7,0},{8,15},{9,14},{10,... | collective-permute-start | bytes 798728 | tf_op jit(solution)/shard_map/ppermute | solution.py:514
  24.2 10.1 %outer.1 = f32[4,520,128]{2,1,0:T(8,128)S(1)} custom-call(f32[24,128]{1,0:T(8,128)S(1)} %get-tuple-element.63.own, f32[1,2,32,32,128]{4,3,2,1,0:T(8,128)} %phase.3, f32[1,2,32,32,128]{4,3,2,1,0:T(8,128)S(1)} %copy-done, f32[33,8,128]{2,1,0:T(8,128)S(1)} %collective-permute-done.4.y_lo, f32[33,8,128]{2,1,0:T(8,128)S(1)} %collective-permute-done.5.y_hi, ...), custom_call_target="tpu_custom_call" | custom-call | flops 100000000 | bytes 41943040 | tf_op jit(solution)/shard_map/outer/pallas_call | solution.py:380
  34.4 26.1 %conditional.4 = (f32[4,520,128]{2,1,0:T(8,128)S(1)}) conditional(s32[]{:T(128)} %bitcast, f32[4,520,128]{2,1,0:T(8,128)S(1)} %outer.1, f32[4,520,128]{2,1,0:T(8,128)S(1)} %outer.1), branch_computations={%region_2.0_spmd, %region_3.0_spmd} | conditional | bytes 2129928 | solution.py:522
  34.4 26.0 %all_to_all.17 = f32[4,520,128]{2,1,0:T(8,128)S(1)} all-to-all(f32[4,520,128]{2,1,0:T(8,128)S(1)} %param.3), channel_id=1, replica_groups={{0,1,2,3},{4,5,6,7},{8,9,10,11},{12,13,14,15},{16,17,18,19},{20,21,22,2..., dimensions={0} | all-to-all | bytes 2129920 | tf_op jit(solution)/shard_map/cond/branch_1_fun/all_to_all | solution.py:520
  60.4 0.0 collective-permute-done.7.refs_1_
  60.4 0.0 collective-permute-done.6.refs_0_
  60.4 0.0 collective-permute-done.8.refs_2_
  60.4 0.0 collective-permute-done.9.refs_3_
  60.5 0.9 route.1
  61.4 0.9 collective-permute-start.10
  62.3 1.8 %collective-permute-start.11 = (f32[2,256,128]{2,1,0:T(8,128)S(1)}, f32[2,256,128]{2,1,0:T(8,128)S(1)}, u32[]{:S(2)}, u32[]{:S(2)}) collective-permute-start(f32[2,256,128]{2,1,0:T(8,128)S(1)} %get-tuple-element.77), channel_id=1, source_target_pairs={{0,5},{1,4},{2,7},{3,6},{4,1},{5,0},{6,3},{7,2},{8,13},{9,12},{10,... | collective-permute-start | bytes 786440 | tf_op jit(solution)/shard_map/ppermute | solution.py:514
  64.1 0.7 collective-permute-start.12
  64.8 2.5 %collective-permute-start.13 = (f32[2,256,128]{2,1,0:T(8,128)S(1)}, f32[2,256,128]{2,1,0:T(8,128)S(1)}, u32[]{:S(2)}, u32[]{:S(2)}) collective-permute-start(f32[2,256,128]{2,1,0:T(8,128)S(1)} %get-tuple-element.79), channel_id=1, source_target_pairs={{0,7},{1,6},{2,5},{3,4},{4,3},{5,2},{6,1},{7,0},{8,15},{9,14},{10,... | collective-permute-start | bytes 786440 | tf_op jit(solution)/shard_map/ppermute | solution.py:514
  67.3 34.8 %conditional.5 = (f32[4,2,256,128]{3,2,1,0:T(8,128)S(1)}) conditional(s32[]{:T(128)} %bitcast, f32[4,2,256,128]{3,2,1,0:T(8,128)S(1)} %get-tuple-element.75, f32[4,2,256,128]{3,2,1,0:T(8,128)S(1)} %get-tuple-element.75), branch_computations={%region_4.0_spmd, %region_5.0_spmd} | conditional | bytes 2097160 | solution.py:522
  67.3 34.8 %all_to_all.19 = f32[4,2,256,128]{3,2,1,0:T(8,128)S(1)} all-to-all(f32[4,2,256,128]{3,2,1,0:T(8,128)S(1)} %param.5), channel_id=1, replica_groups={{0,1,2,3},{4,5,6,7},{8,9,10,11},{12,13,14,15},{16,17,18,19},{20,21,22,2..., dimensions={0} | all-to-all | bytes 2097152 | tf_op jit(solution)/shard_map/cond/branch_1_fun/all_to_all | solution.py:520
  102.1 0.0 collective-permute-done.10.refs_0_
  102.1 0.0 collective-permute-done.11.refs_1_
  102.1 1.6 %collective-permute-done.12.refs_2_ = f32[2,256,128]{2,1,0:T(8,128)S(1)} collective-permute-done((f32[2,256,128]{2,1,0:T(8,128)S(1)}, f32[2,256,128]{2,1,0:T(8,128)S(1)}, u32[]{:S(2)}, u32[]{:S(2)}) %collective-permute-start.12) | collective-permute-done | bytes 262176 | tf_op jit(solution)/shard_map/ppermute | solution.py:514
  103.6 4.7 %collective-permute-done.13.refs_3_ = f32[2,256,128]{2,1,0:T(8,128)S(1)} collective-permute-done((f32[2,256,128]{2,1,0:T(8,128)S(1)}, f32[2,256,128]{2,1,0:T(8,128)S(1)}, u32[]{:S(2)}, u32[]{:S(2)}) %collective-permute-start.13) | collective-permute-done | bytes 262176 | tf_op jit(solution)/shard_map/ppermute | solution.py:514
  108.3 2.0 %settle.1 = (f32[1,2,32,32,128]{4,3,2,1,0:T(8,128)}, f32[1,2,32,32,128]{4,3,2,1,0:T(8,128)}) custom-call(s32[16]{0:T(128)S(1)} %get-tuple-element.74.table, f32[4,2,256,128]{3,2,1,0:T(8,128)S(1)} %get-tuple-element.89.near, f32[2,256,128]{2,1,0:T(8,128)S(1)} %collective-permute-done.10.refs_0_, f32[2,256,128]{2,1,0:T(8,128)S(1)} %collective-permute-done.11.refs_1_, ...), custom_call_target="tpu_custom_call" | custom-call | tf_op jit(solution)/shard_map/settle/pallas_call | solution.py:494
  (1 shorter events, 0.0 us)
Async XLA Ops:
  0.6 5.0 %copy-start = (f32[1,2,32,32,128]{4,3,2,1,0:T(8,128)S(1)}, f32[1,2,32,32,128]{4,3,2,1,0:T(8,128)}, u32[]{:S(2)}) copy-start(f32[1,2,32,32,128]{4,3,2,1,0:T(8,128)} %solute.3) | copy-start | bytes 3145732
  0.6 5.0 %copy-start.1 = (f32[1,2,32,32,128]{4,3,2,1,0:T(8,128)S(1)}, f32[1,2,32,32,128]{4,3,2,1,0:T(8,128)}, u32[]{:S(2)}) copy-start(f32[1,2,32,32,128]{4,3,2,1,0:T(8,128)} %phase.3) | copy-start | bytes 3145732
  2.7 9.8 %copy-start.3 = (s32[1,2]{1,0:T(1,128)S(1)}, s32[1,2]{1,0:T(1,128)}, u32[]{:S(2)}) copy-start(s32[1,2]{1,0:T(1,128)} %owner.1) | copy-start | bytes 28
  2.7 9.9 %copy-start.2 = (f32[1,2,32,32,128]{4,3,2,1,0:T(8,128)S(1)}, f32[1,2,32,32,128]{4,3,2,1,0:T(8,128)}, u32[]{:S(2)}) copy-start(f32[1,2,32,32,128]{4,3,2,1,0:T(8,128)} %phase.3) | copy-start | bytes 3145732
  2.7 9.9 %collective-permute-start.4 = (f32[33,8,128]{2,1,0:T(8,128)}, f32[33,8,128]{2,1,0:T(8,128)S(1)}, u32[]{:S(2)}, u32[]{:S(2)}) collective-permute-start(f32[33,8,128]{2,1,0:T(8,128)} %get-tuple-element.64), channel_id=1, source_target_pairs={{0,1},{1,2},{2,3},{3,4},{4,5},{5,6},{6,7},{7,0},{8,9},{9,10},{10,1... | collective-permute-start | bytes 405512 | tf_op jit(solution)/shard_map/ppermute | solution.py:534
  4.2 8.3 %collective-permute-start.5 = (f32[33,8,128]{2,1,0:T(8,128)}, f32[33,8,128]{2,1,0:T(8,128)S(1)}, u32[]{:S(2)}, u32[]{:S(2)}) collective-permute-start(f32[33,8,128]{2,1,0:T(8,128)} %get-tuple-element.65), channel_id=1, source_target_pairs={{0,7},{1,0},{2,1},{3,2},{4,3},{5,4},{6,5},{7,6},{8,15},{9,8},{10,9... | collective-permute-start | bytes 405512 | tf_op jit(solution)/shard_map/ppermute | solution.py:535
  9.5 51.0 %collective-permute-start.7 = (f32[520,128]{1,0:T(8,128)S(1)}, f32[520,128]{1,0:T(8,128)S(1)}, u32[]{:S(2)}, u32[]{:S(2)}) collective-permute-start(f32[520,128]{1,0:T(8,128)S(1)} %get-tuple-element.71), channel_id=1, source_target_pairs={{0,5},{1,4},{2,7},{3,6},{4,1},{5,0},{6,3},{7,2},{8,13},{9,12},{10,... | collective-permute-start | bytes 798728 | tf_op jit(solution)/shard_map/ppermute | solution.py:514
  12.2 48.3 %collective-permute-start.6 = (f32[520,128]{1,0:T(8,128)S(1)}, f32[520,128]{1,0:T(8,128)S(1)}, u32[]{:S(2)}, u32[]{:S(2)}) collective-permute-start(f32[520,128]{1,0:T(8,128)S(1)} %get-tuple-element.66._), channel_id=1, source_target_pairs={{0,4},{1,5},{2,6},{3,7},{4,0},{5,1},{6,2},{7,3},{8,12},{9,13},{10,... | collective-permute-start | bytes 798728 | tf_op jit(solution)/shard_map/ppermute | solution.py:514
  12.7 8.0 %collective-permute-start.2 = (f32[608,128]{1,0:T(8,128)S(1)}, f32[608,128]{1,0:T(8,128)}, u32[]{:S(2)}, u32[]{:S(2)}) collective-permute-start(f32[608,128]{1,0:T(8,128)S(1)} %get-tuple-element.37), channel_id=1, source_target_pairs={{0,8},{8,16},{16,24},{24,0},{1,9},{9,17},{17,25},{25,1},{2,10},{10... | collective-permute-start | bytes 933896 | tf_op jit(solution)/shard_map/cond/branch_1_fun/ppermute | solution.py:552
  12.7 8.7 %collective-permute-start.3 = (f32[608,128]{1,0:T(8,128)S(1)}, f32[608,128]{1,0:T(8,128)}, u32[]{:S(2)}, u32[]{:S(2)}) collective-permute-start(f32[608,128]{1,0:T(8,128)S(1)} %get-tuple-element.38), channel_id=1, source_target_pairs={{0,24},{8,0},{16,8},{24,16},{1,25},{9,1},{17,9},{25,17},{2,26},{10... | collective-permute-start | bytes 933896 | tf_op jit(solution)/shard_map/cond/branch_1_fun/ppermute | solution.py:552
  21.4 39.1 %collective-permute-start.8 = (f32[520,128]{1,0:T(8,128)S(1)}, f32[520,128]{1,0:T(8,128)S(1)}, u32[]{:S(2)}, u32[]{:S(2)}) collective-permute-start(f32[520,128]{1,0:T(8,128)S(1)} %get-tuple-element.72), channel_id=1, source_target_pairs={{0,6},{1,7},{2,4},{3,5},{4,2},{5,3},{6,0},{7,1},{8,14},{9,15},{10,... | collective-permute-start | bytes 798728 | tf_op jit(solution)/shard_map/ppermute | solution.py:514
  23.0 37.5 %collective-permute-start.9 = (f32[520,128]{1,0:T(8,128)}, f32[520,128]{1,0:T(8,128)S(1)}, u32[]{:S(2)}, u32[]{:S(2)}) collective-permute-start(f32[520,128]{1,0:T(8,128)} %get-tuple-element.73), channel_id=1, source_target_pairs={{0,7},{1,6},{2,5},{3,4},{4,3},{5,2},{6,1},{7,0},{8,15},{9,14},{10,... | collective-permute-start | bytes 798728 | tf_op jit(solution)/shard_map/ppermute | solution.py:514
  61.4 40.7 %collective-permute-start.10 = (f32[2,256,128]{2,1,0:T(8,128)S(1)}, f32[2,256,128]{2,1,0:T(8,128)S(1)}, u32[]{:S(2)}, u32[]{:S(2)}) collective-permute-start(f32[2,256,128]{2,1,0:T(8,128)S(1)} %get-tuple-element.76), channel_id=1, source_target_pairs={{0,4},{1,5},{2,6},{3,7},{4,0},{5,1},{6,2},{7,3},{8,12},{9,13},{10,... | collective-permute-start | bytes 786440 | tf_op jit(solution)/shard_map/ppermute | solution.py:514
  62.3 39.8 %collective-permute-start.11 = (f32[2,256,128]{2,1,0:T(8,128)S(1)}, f32[2,256,128]{2,1,0:T(8,128)S(1)}, u32[]{:S(2)}, u32[]{:S(2)}) collective-permute-start(f32[2,256,128]{2,1,0:T(8,128)S(1)} %get-tuple-element.77), channel_id=1, source_target_pairs={{0,5},{1,4},{2,7},{3,6},{4,1},{5,0},{6,3},{7,2},{8,13},{9,12},{10,... | collective-permute-start | bytes 786440 | tf_op jit(solution)/shard_map/ppermute | solution.py:514
  64.1 39.5 %collective-permute-start.12 = (f32[2,256,128]{2,1,0:T(8,128)S(1)}, f32[2,256,128]{2,1,0:T(8,128)S(1)}, u32[]{:S(2)}, u32[]{:S(2)}) collective-permute-start(f32[2,256,128]{2,1,0:T(8,128)S(1)} %get-tuple-element.78), channel_id=1, source_target_pairs={{0,6},{1,7},{2,4},{3,5},{4,2},{5,3},{6,0},{7,1},{8,14},{9,15},{10,... | collective-permute-start | bytes 786440 | tf_op jit(solution)/shard_map/ppermute | solution.py:514
  64.8 43.5 %collective-permute-start.13 = (f32[2,256,128]{2,1,0:T(8,128)S(1)}, f32[2,256,128]{2,1,0:T(8,128)S(1)}, u32[]{:S(2)}, u32[]{:S(2)}) collective-permute-start(f32[2,256,128]{2,1,0:T(8,128)S(1)} %get-tuple-element.79), channel_id=1, source_target_pairs={{0,7},{1,6},{2,5},{3,4},{4,3},{5,2},{6,1},{7,0},{8,15},{9,14},{10,... | collective-permute-start | bytes 786440 | tf_op jit(solution)/shard_map/ppermute | solution.py:514

commit v23 on v22

--- a/solution.py
+++ b/solution.py
@@ -215,7 +215,7 @@
 UNROLL = 4
 
 
-def march(count, row_of, starts, source, target, coefs_of):
+def march(count, row_of, starts, source, target, coefs_of, unroll=UNROLL):
     def one_row(index, carry):
         row = row_of(index)
         for start in starts:
@@ -224,7 +224,7 @@
             target[1][row, start : start + 8, :] = new_u
         return carry
 
-    lax.fori_loop(0, count, one_row, 0, unroll=UNROLL)
+    lax.fori_loop(0, count, one_row, 0, unroll=unroll)
 
 
 def inner_kernel(plan, batch, own, phase, solute, *rest):
@@ -257,7 +257,7 @@
         margin = 8 if step == NSTEPS - 1 else W
         starts = range(PAD + margin, PAD + tiles * edge - margin, 8)
         rows = count + 2 * W - 2 * (step + 1)
-        march(rows, lambda i, step=step: step + 1 + i, starts, pairs[step % 2], pairs[(step + 1) % 2], coefs_of)
+        march(rows, lambda i, step=step: step + 1 + i, starts, pairs[step % 2], pairs[(step + 1) % 2], coefs_of, 6)
     for index, out in zip(indices, outs):
         pack(plan, True, mine ^ index, pairs[NSTEPS % 2], -base, PAD, own, out)
 

time: 111 us -> 110 us (level)
  no operation moved by 1% of the time
where the time goes in v23:
time: 110 us
  blocking collectives  60.8 us (55%)
  Pallas kernels  23.2 us (21%)
  starting transfers between devices  16.6 us (15%)
  waiting for transfers between devices  8.74 us (8%)
    all_to_all x2, blocking collectives, exchange(): lax.all_to_all(values, 'gy', 0, 0, axis_index_groups=groups, tiled=True)  60.8 us
    ppermute x8, starting transfers between devices, swap(): lax.ppermute(values, 'gy', [(i, i ^ mask) for i in range(lax.axis_size('g...  11.8 us
    pallas_call x1, Pallas kernels, run_outer(): pl.pallas_call(functools.partial(outer_kernel, plan), in_specs=[vmem] * 7...  10.1 us
    pallas_call x2, Pallas kernels, run_inner(): pl.pallas_call(functools.partial(inner_kernel, plan, batch), in_specs=[vm...  8.15 us
    ppermute x8, waiting for transfers between devices, swap(): lax.ppermute(values, 'gy', [(i, i ^ mask) for i in range(lax.axis_size('g...  6.24 us
  transfers between devices with their start and end apart: 12, of which 4 were waited for; matrix products, arithmetic and copies ran while one was open for 0% of the time, Pallas kernels for 17%

profile of v23, /device:TPU:8, one launch (start us, length us, event | category | flops | bytes accessed | tf_op | source)
XLA Modules:
  0.0 110.2 jit_solution(11843399886633941935)
XLA Ops:
  0.6 0.0 copy-start
  0.6 0.0 copy-start.1
  0.7 2.0 %pack_y.1 = (f32[33,8,128]{2,1,0:T(8,128)}, f32[33,8,128]{2,1,0:T(8,128)}, f32[24,128]{1,0:T(8,128)S(1)}) custom-call(f32[1,2]{1,0:T(1,128)} %under.1, f32[1,2]{1,0:T(1,128)} %mobile.1, f32[1,2]{1,0:T(1,128)} %spread.1, s32[1,2]{1,0:T(1,128)} %owner.1, f32[1,2,32,32,128]{4,3,2,1,0:T(8,128)} %phase.3, f32[1,2,32,32,128]{4,3,2,1,0:T(8,128)} %phase.3, ...), custom_call_target="tpu_custom_call" | custom-call | tf_op jit(solution)/shard_map/pack_y/pallas_call | solution.py:48
  2.7 0.0 copy-start.3
  2.7 0.0 copy-start.2
  2.7 1.6 %collective-permute-start.4 = (f32[33,8,128]{2,1,0:T(8,128)}, f32[33,8,128]{2,1,0:T(8,128)S(1)}, u32[]{:S(2)}, u32[]{:S(2)}) collective-permute-start(f32[33,8,128]{2,1,0:T(8,128)} %get-tuple-element.64), channel_id=1, source_target_pairs={{0,1},{1,2},{2,3},{3,4},{4,5},{5,6},{6,7},{7,0},{8,9},{9,10},{10,1... | collective-permute-start | bytes 405512 | tf_op jit(solution)/shard_map/ppermute | solution.py:534
  4.2 1.4 %collective-permute-start.5 = (f32[33,8,128]{2,1,0:T(8,128)}, f32[33,8,128]{2,1,0:T(8,128)S(1)}, u32[]{:S(2)}, u32[]{:S(2)}) collective-permute-start(f32[33,8,128]{2,1,0:T(8,128)} %get-tuple-element.65), channel_id=1, source_target_pairs={{0,7},{1,0},{2,1},{3,2},{4,3},{5,4},{6,5},{7,6},{8,15},{9,8},{10,9... | collective-permute-start | bytes 405512 | tf_op jit(solution)/shard_map/ppermute | solution.py:535
  5.6 0.0 copy-done
  5.6 0.0 copy-done.1
  5.6 3.7 %inner.5 = (f32[520,128]{1,0:T(8,128)S(1)}, f32[520,128]{1,0:T(8,128)S(1)}) custom-call(f32[24,128]{1,0:T(8,128)S(1)} %get-tuple-element.63.own, f32[1,2,32,32,128]{4,3,2,1,0:T(8,128)S(1)} %copy-done.1, f32[1,2,32,32,128]{4,3,2,1,0:T(8,128)S(1)} %copy-done), custom_call_target="tpu_custom_call" | custom-call | flops 100000000 | bytes 25165824 | tf_op jit(solution)/shard_map/inner/pallas_call | solution.py:284
  9.4 2.7 %collective-permute-start.7 = (f32[520,128]{1,0:T(8,128)S(1)}, f32[520,128]{1,0:T(8,128)S(1)}, u32[]{:S(2)}, u32[]{:S(2)}) collective-permute-start(f32[520,128]{1,0:T(8,128)S(1)} %get-tuple-element.71), channel_id=1, source_target_pairs={{0,5},{1,4},{2,7},{3,6},{4,1},{5,0},{6,3},{7,2},{8,13},{9,12},{10,... | collective-permute-start | bytes 798728 | tf_op jit(solution)/shard_map/ppermute | solution.py:514
  12.1 0.3 collective-permute-start.6
  12.4 0.0 copy-done.3
  12.5 0.0 collective-permute-done.4.y_lo
  12.5 0.0 collective-permute-done.5.y_hi
  12.5 0.0 copy-done.2
  12.6 8.7 %conditional.3 = (f32[608,128]{1,0:T(8,128)}, f32[608,128]{1,0:T(8,128)}, f32[520,128]{1,0:T(8,128)S(1)}, f32[520,128]{1,0:T(8,128)}) conditional(s32[]{:T(128)} %bitcast, (f32[608,128]{1,0:T(8,128)S(1)}, f32[608,128]{1,0:T(8,128)S(1)}, f32[24,128]{1,0:T(8,128)S(1)}, f32[1,2,32,32,128]{4,3,2,1,0:T(8,128)S(1)}, ...), branch_computations={%region_0.0_spmd, %region_1.0_spmd} | conditional | flops 100000000 | bytes 27656304 | solution.py:554
  12.6 0.1 collective-permute-start.2
  12.6 1.7 %collective-permute-start.3 = (f32[608,128]{1,0:T(8,128)S(1)}, f32[608,128]{1,0:T(8,128)}, u32[]{:S(2)}, u32[]{:S(2)}) collective-permute-start(f32[608,128]{1,0:T(8,128)S(1)} %get-tuple-element.38), channel_id=1, source_target_pairs={{0,24},{8,0},{16,8},{24,16},{1,25},{9,1},{17,9},{25,17},{2,26},{10... | collective-permute-start | bytes 933896 | tf_op jit(solution)/shard_map/cond/branch_1_fun/ppermute | solution.py:552
  14.4 4.4 %inner.4 = (f32[520,128]{1,0:T(8,128)S(1)}, f32[520,128]{1,0:T(8,128)}) custom-call(f32[24,128]{1,0:T(8,128)S(1)} %get-tuple-element.39.own, f32[1,2,32,32,128]{4,3,2,1,0:T(8,128)S(1)} %get-tuple-element.40.phase, f32[1,2,32,32,128]{4,3,2,1,0:T(8,128)S(1)} %get-tuple-element.41.solute), custom_call_target="tpu_custom_call" | custom-call | flops 100000000 | bytes 25165824 | tf_op jit(solution)/shard_map/cond/branch_1_fun/inner/pallas_call | solution.py:284
  18.8 1.7 %collective-permute-done.2 = f32[608,128]{1,0:T(8,128)} collective-permute-done((f32[608,128]{1,0:T(8,128)S(1)}, f32[608,128]{1,0:T(8,128)}, u32[]{:S(2)}, u32[]{:S(2)}) %collective-permute-start.2) | collective-permute-done | bytes 311328 | tf_op jit(solution)/shard_map/cond/branch_1_fun/ppermute | solution.py:552
  20.5 0.8 collective-permute-done.3
  21.3 1.6 %collective-permute-start.8 = (f32[520,128]{1,0:T(8,128)S(1)}, f32[520,128]{1,0:T(8,128)S(1)}, u32[]{:S(2)}, u32[]{:S(2)}) collective-permute-start(f32[520,128]{1,0:T(8,128)S(1)} %get-tuple-element.72), channel_id=1, source_target_pairs={{0,6},{1,7},{2,4},{3,5},{4,2},{5,3},{6,0},{7,1},{8,14},{9,15},{10,... | collective-permute-start | bytes 798728 | tf_op jit(solution)/shard_map/ppermute | solution.py:514
  22.9 1.3 %collective-permute-start.9 = (f32[520,128]{1,0:T(8,128)}, f32[520,128]{1,0:T(8,128)S(1)}, u32[]{:S(2)}, u32[]{:S(2)}) collective-permute-start(f32[520,128]{1,0:T(8,128)} %get-tuple-element.73), channel_id=1, source_target_pairs={{0,7},{1,6},{2,5},{3,4},{4,3},{5,2},{6,1},{7,0},{8,15},{9,14},{10,... | collective-permute-start | bytes 798728 | tf_op jit(solution)/shard_map/ppermute | solution.py:514
  24.2 10.1 %outer.1 = f32[4,520,128]{2,1,0:T(8,128)S(1)} custom-call(f32[24,128]{1,0:T(8,128)S(1)} %get-tuple-element.63.own, f32[1,2,32,32,128]{4,3,2,1,0:T(8,128)} %phase.3, f32[1,2,32,32,128]{4,3,2,1,0:T(8,128)S(1)} %copy-done, f32[33,8,128]{2,1,0:T(8,128)S(1)} %collective-permute-done.4.y_lo, f32[33,8,128]{2,1,0:T(8,128)S(1)} %collective-permute-done.5.y_hi, ...), custom_call_target="tpu_custom_call" | custom-call | flops 100000000 | bytes 41943040 | tf_op jit(solution)/shard_map/outer/pallas_call | solution.py:380
  34.3 26.1 %conditional.4 = (f32[4,520,128]{2,1,0:T(8,128)S(1)}) conditional(s32[]{:T(128)} %bitcast, f32[4,520,128]{2,1,0:T(8,128)S(1)} %outer.1, f32[4,520,128]{2,1,0:T(8,128)S(1)} %outer.1), branch_computations={%region_2.0_spmd, %region_3.0_spmd} | conditional | bytes 2129928 | solution.py:522
  34.3 26.0 %all_to_all.17 = f32[4,520,128]{2,1,0:T(8,128)S(1)} all-to-all(f32[4,520,128]{2,1,0:T(8,128)S(1)} %param.3), channel_id=1, replica_groups={{0,1,2,3},{4,5,6,7},{8,9,10,11},{12,13,14,15},{16,17,18,19},{20,21,22,2..., dimensions={0} | all-to-all | bytes 2129920 | tf_op jit(solution)/shard_map/cond/branch_1_fun/all_to_all | solution.py:520
  60.4 0.0 collective-permute-done.7.refs_1_
  60.4 0.0 collective-permute-done.6.refs_0_
  60.4 0.0 collective-permute-done.8.refs_2_
  60.4 0.0 collective-permute-done.9.refs_3_
  60.4 0.9 route.1
  61.3 0.9 collective-permute-start.10
  62.2 1.8 %collective-permute-start.11 = (f32[2,256,128]{2,1,0:T(8,128)S(1)}, f32[2,256,128]{2,1,0:T(8,128)S(1)}, u32[]{:S(2)}, u32[]{:S(2)}) collective-permute-start(f32[2,256,128]{2,1,0:T(8,128)S(1)} %get-tuple-element.77), channel_id=1, source_target_pairs={{0,5},{1,4},{2,7},{3,6},{4,1},{5,0},{6,3},{7,2},{8,13},{9,12},{10,... | collective-permute-start | bytes 786440 | tf_op jit(solution)/shard_map/ppermute | solution.py:514
  64.0 0.7 collective-permute-start.12
  64.7 2.5 %collective-permute-start.13 = (f32[2,256,128]{2,1,0:T(8,128)S(1)}, f32[2,256,128]{2,1,0:T(8,128)S(1)}, u32[]{:S(2)}, u32[]{:S(2)}) collective-permute-start(f32[2,256,128]{2,1,0:T(8,128)S(1)} %get-tuple-element.79), channel_id=1, source_target_pairs={{0,7},{1,6},{2,5},{3,4},{4,3},{5,2},{6,1},{7,0},{8,15},{9,14},{10,... | collective-permute-start | bytes 786440 | tf_op jit(solution)/shard_map/ppermute | solution.py:514
  67.2 34.8 %conditional.5 = (f32[4,2,256,128]{3,2,1,0:T(8,128)S(1)}) conditional(s32[]{:T(128)} %bitcast, f32[4,2,256,128]{3,2,1,0:T(8,128)S(1)} %get-tuple-element.75, f32[4,2,256,128]{3,2,1,0:T(8,128)S(1)} %get-tuple-element.75), branch_computations={%region_4.0_spmd, %region_5.0_spmd} | conditional | bytes 2097160 | solution.py:522
  67.2 34.8 %all_to_all.19 = f32[4,2,256,128]{3,2,1,0:T(8,128)S(1)} all-to-all(f32[4,2,256,128]{3,2,1,0:T(8,128)S(1)} %param.5), channel_id=1, replica_groups={{0,1,2,3},{4,5,6,7},{8,9,10,11},{12,13,14,15},{16,17,18,19},{20,21,22,2..., dimensions={0} | all-to-all | bytes 2097152 | tf_op jit(solution)/shard_map/cond/branch_1_fun/all_to_all | solution.py:520
  102.0 0.0 collective-permute-done.10.refs_0_
  102.0 0.0 collective-permute-done.11.refs_1_
  102.0 1.6 %collective-permute-done.12.refs_2_ = f32[2,256,128]{2,1,0:T(8,128)S(1)} collective-permute-done((f32[2,256,128]{2,1,0:T(8,128)S(1)}, f32[2,256,128]{2,1,0:T(8,128)S(1)}, u32[]{:S(2)}, u32[]{:S(2)}) %collective-permute-start.12) | collective-permute-done | bytes 262176 | tf_op jit(solution)/shard_map/ppermute | solution.py:514
  103.6 4.7 %collective-permute-done.13.refs_3_ = f32[2,256,128]{2,1,0:T(8,128)S(1)} collective-permute-done((f32[2,256,128]{2,1,0:T(8,128)S(1)}, f32[2,256,128]{2,1,0:T(8,128)S(1)}, u32[]{:S(2)}, u32[]{:S(2)}) %collective-permute-start.13) | collective-permute-done | bytes 262176 | tf_op jit(solution)/shard_map/ppermute | solution.py:514
  108.2 2.0 %settle.1 = (f32[1,2,32,32,128]{4,3,2,1,0:T(8,128)}, f32[1,2,32,32,128]{4,3,2,1,0:T(8,128)}) custom-call(s32[16]{0:T(128)S(1)} %get-tuple-element.74.table, f32[4,2,256,128]{3,2,1,0:T(8,128)S(1)} %get-tuple-element.89.near, f32[2,256,128]{2,1,0:T(8,128)S(1)} %collective-permute-done.10.refs_0_, f32[2,256,128]{2,1,0:T(8,128)S(1)} %collective-permute-done.11.refs_1_, ...), custom_call_target="tpu_custom_call" | custom-call | tf_op jit(solution)/shard_map/settle/pallas_call | solution.py:494
  (1 shorter events, 0.0 us)
Async XLA Ops:
  0.6 5.0 %copy-start = (f32[1,2,32,32,128]{4,3,2,1,0:T(8,128)S(1)}, f32[1,2,32,32,128]{4,3,2,1,0:T(8,128)}, u32[]{:S(2)}) copy-start(f32[1,2,32,32,128]{4,3,2,1,0:T(8,128)} %solute.3) | copy-start | bytes 3145732
  0.6 5.0 %copy-start.1 = (f32[1,2,32,32,128]{4,3,2,1,0:T(8,128)S(1)}, f32[1,2,32,32,128]{4,3,2,1,0:T(8,128)}, u32[]{:S(2)}) copy-start(f32[1,2,32,32,128]{4,3,2,1,0:T(8,128)} %phase.3) | copy-start | bytes 3145732
  2.7 9.8 %copy-start.3 = (s32[1,2]{1,0:T(1,128)S(1)}, s32[1,2]{1,0:T(1,128)}, u32[]{:S(2)}) copy-start(s32[1,2]{1,0:T(1,128)} %owner.1) | copy-start | bytes 28
  2.7 9.8 %copy-start.2 = (f32[1,2,32,32,128]{4,3,2,1,0:T(8,128)S(1)}, f32[1,2,32,32,128]{4,3,2,1,0:T(8,128)}, u32[]{:S(2)}) copy-start(f32[1,2,32,32,128]{4,3,2,1,0:T(8,128)} %phase.3) | copy-start | bytes 3145732
  2.7 9.8 %collective-permute-start.4 = (f32[33,8,128]{2,1,0:T(8,128)}, f32[33,8,128]{2,1,0:T(8,128)S(1)}, u32[]{:S(2)}, u32[]{:S(2)}) collective-permute-start(f32[33,8,128]{2,1,0:T(8,128)} %get-tuple-element.64), channel_id=1, source_target_pairs={{0,1},{1,2},{2,3},{3,4},{4,5},{5,6},{6,7},{7,0},{8,9},{9,10},{10,1... | collective-permute-start | bytes 405512 | tf_op jit(solution)/shard_map/ppermute | solution.py:534
  4.2 8.2 %collective-permute-start.5 = (f32[33,8,128]{2,1,0:T(8,128)}, f32[33,8,128]{2,1,0:T(8,128)S(1)}, u32[]{:S(2)}, u32[]{:S(2)}) collective-permute-start(f32[33,8,128]{2,1,0:T(8,128)} %get-tuple-element.65), channel_id=1, source_target_pairs={{0,7},{1,0},{2,1},{3,2},{4,3},{5,4},{6,5},{7,6},{8,15},{9,8},{10,9... | collective-permute-start | bytes 405512 | tf_op jit(solution)/shard_map/ppermute | solution.py:535
  9.4 51.0 %collective-permute-start.7 = (f32[520,128]{1,0:T(8,128)S(1)}, f32[520,128]{1,0:T(8,128)S(1)}, u32[]{:S(2)}, u32[]{:S(2)}) collective-permute-start(f32[520,128]{1,0:T(8,128)S(1)} %get-tuple-element.71), channel_id=1, source_target_pairs={{0,5},{1,4},{2,7},{3,6},{4,1},{5,0},{6,3},{7,2},{8,13},{9,12},{10,... | collective-permute-start | bytes 798728 | tf_op jit(solution)/shard_map/ppermute | solution.py:514
  12.1 48.3 %collective-permute-start.6 = (f32[520,128]{1,0:T(8,128)S(1)}, f32[520,128]{1,0:T(8,128)S(1)}, u32[]{:S(2)}, u32[]{:S(2)}) collective-permute-start(f32[520,128]{1,0:T(8,128)S(1)} %get-tuple-element.66._), channel_id=1, source_target_pairs={{0,4},{1,5},{2,6},{3,7},{4,0},{5,1},{6,2},{7,3},{8,12},{9,13},{10,... | collective-permute-start | bytes 798728 | tf_op jit(solution)/shard_map/ppermute | solution.py:514
  12.6 8.0 %collective-permute-start.2 = (f32[608,128]{1,0:T(8,128)S(1)}, f32[608,128]{1,0:T(8,128)}, u32[]{:S(2)}, u32[]{:S(2)}) collective-permute-start(f32[608,128]{1,0:T(8,128)S(1)} %get-tuple-element.37), channel_id=1, source_target_pairs={{0,8},{8,16},{16,24},{24,0},{1,9},{9,17},{17,25},{25,1},{2,10},{10... | collective-permute-start | bytes 933896 | tf_op jit(solution)/shard_map/cond/branch_1_fun/ppermute | solution.py:552
  12.6 8.7 %collective-permute-start.3 = (f32[608,128]{1,0:T(8,128)S(1)}, f32[608,128]{1,0:T(8,128)}, u32[]{:S(2)}, u32[]{:S(2)}) collective-permute-start(f32[608,128]{1,0:T(8,128)S(1)} %get-tuple-element.38), channel_id=1, source_target_pairs={{0,24},{8,0},{16,8},{24,16},{1,25},{9,1},{17,9},{25,17},{2,26},{10... | collective-permute-start | bytes 933896 | tf_op jit(solution)/shard_map/cond/branch_1_fun/ppermute | solution.py:552
  21.3 39.1 %collective-permute-start.8 = (f32[520,128]{1,0:T(8,128)S(1)}, f32[520,128]{1,0:T(8,128)S(1)}, u32[]{:S(2)}, u32[]{:S(2)}) collective-permute-start(f32[520,128]{1,0:T(8,128)S(1)} %get-tuple-element.72), channel_id=1, source_target_pairs={{0,6},{1,7},{2,4},{3,5},{4,2},{5,3},{6,0},{7,1},{8,14},{9,15},{10,... | collective-permute-start | bytes 798728 | tf_op jit(solution)/shard_map/ppermute | solution.py:514
  22.9 37.5 %collective-permute-start.9 = (f32[520,128]{1,0:T(8,128)}, f32[520,128]{1,0:T(8,128)S(1)}, u32[]{:S(2)}, u32[]{:S(2)}) collective-permute-start(f32[520,128]{1,0:T(8,128)} %get-tuple-element.73), channel_id=1, source_target_pairs={{0,7},{1,6},{2,5},{3,4},{4,3},{5,2},{6,1},{7,0},{8,15},{9,14},{10,... | collective-permute-start | bytes 798728 | tf_op jit(solution)/shard_map/ppermute | solution.py:514
  61.3 40.7 %collective-permute-start.10 = (f32[2,256,128]{2,1,0:T(8,128)S(1)}, f32[2,256,128]{2,1,0:T(8,128)S(1)}, u32[]{:S(2)}, u32[]{:S(2)}) collective-permute-start(f32[2,256,128]{2,1,0:T(8,128)S(1)} %get-tuple-element.76), channel_id=1, source_target_pairs={{0,4},{1,5},{2,6},{3,7},{4,0},{5,1},{6,2},{7,3},{8,12},{9,13},{10,... | collective-permute-start | bytes 786440 | tf_op jit(solution)/shard_map/ppermute | solution.py:514
  62.2 39.8 %collective-permute-start.11 = (f32[2,256,128]{2,1,0:T(8,128)S(1)}, f32[2,256,128]{2,1,0:T(8,128)S(1)}, u32[]{:S(2)}, u32[]{:S(2)}) collective-permute-start(f32[2,256,128]{2,1,0:T(8,128)S(1)} %get-tuple-element.77), channel_id=1, source_target_pairs={{0,5},{1,4},{2,7},{3,6},{4,1},{5,0},{6,3},{7,2},{8,13},{9,12},{10,... | collective-permute-start | bytes 786440 | tf_op jit(solution)/shard_map/ppermute | solution.py:514
  64.0 39.5 %collective-permute-start.12 = (f32[2,256,128]{2,1,0:T(8,128)S(1)}, f32[2,256,128]{2,1,0:T(8,128)S(1)}, u32[]{:S(2)}, u32[]{:S(2)}) collective-permute-start(f32[2,256,128]{2,1,0:T(8,128)S(1)} %get-tuple-element.78), channel_id=1, source_target_pairs={{0,6},{1,7},{2,4},{3,5},{4,2},{5,3},{6,0},{7,1},{8,14},{9,15},{10,... | collective-permute-start | bytes 786440 | tf_op jit(solution)/shard_map/ppermute | solution.py:514
  64.7 43.5 %collective-permute-start.13 = (f32[2,256,128]{2,1,0:T(8,128)S(1)}, f32[2,256,128]{2,1,0:T(8,128)S(1)}, u32[]{:S(2)}, u32[]{:S(2)}) collective-permute-start(f32[2,256,128]{2,1,0:T(8,128)S(1)} %get-tuple-element.79), channel_id=1, source_target_pairs={{0,7},{1,6},{2,5},{3,4},{4,3},{5,2},{6,1},{7,0},{8,15},{9,14},{10,... | collective-permute-start | bytes 786440 | tf_op jit(solution)/shard_map/ppermute | solution.py:514

commit v24 on v22

--- a/solution.py
+++ b/solution.py
@@ -553,7 +553,7 @@
 
     (x_lo, x_hi), second = lax.cond(together, around, around, to_next, to_prev, own, phase, solute)
     send_far(1, second)
-    near = run_outer(plan, own_here, phase_here, solute_here, (y_lo, y_hi, in_vmem(x_lo), in_vmem(x_hi)))
+    near = run_outer(plan, own_here, in_vmem(phase_here), solute_here, (y_lo, y_hi, in_vmem(x_lo), in_vmem(x_hi)))
     far = [in_vmem(far[index]) for index in range(half)]
     near = among_half(plan, near, together)
     near, far, table = route(plan, in_vmem(near), far)

time: 111 us -> 112 us (level)
  Pallas kernels: 23.3 us -> 25 us
where the time goes in v24:
time: 112 us
  blocking collectives  61.9 us (55%)
  Pallas kernels  25 us (22%)
  starting transfers between devices  16.5 us (15%)
  waiting for transfers between devices  7.99 us (7%)
    all_to_all x2, blocking collectives, exchange(): lax.all_to_all(values, 'gy', 0, 0, axis_index_groups=groups, tiled=True)  61.9 us
    ppermute x8, starting transfers between devices, swap(): lax.ppermute(values, 'gy', [(i, i ^ mask) for i in range(lax.axis_size('g...  11.8 us
    pallas_call x1, Pallas kernels, run_outer(): pl.pallas_call(functools.partial(outer_kernel, plan), in_specs=[vmem] * 7...  9.8 us
    pallas_call x2, Pallas kernels, run_inner(): pl.pallas_call(functools.partial(inner_kernel, plan, batch), in_specs=[vm...  9.2 us
    ppermute x8, waiting for transfers between devices, swap(): lax.ppermute(values, 'gy', [(i, i ^ mask) for i in range(lax.axis_size('g...  5.71 us
  transfers between devices with their start and end apart: 12, of which 4 were waited for; matrix products, arithmetic and copies ran while one was open for 0% of the time, Pallas kernels for 17%

profile of v24, /device:TPU:8, one launch (start us, length us, event | category | flops | bytes accessed | tf_op | source)
XLA Modules:
  0.0 112.2 jit_solution(6870851989146716515)
XLA Ops:
  0.6 0.0 copy-start.1
  0.6 0.0 copy-start
  0.7 2.0 %pack_y.1 = (f32[33,8,128]{2,1,0:T(8,128)}, f32[33,8,128]{2,1,0:T(8,128)}, f32[24,128]{1,0:T(8,128)S(1)}) custom-call(f32[1,2]{1,0:T(1,128)} %under.1, f32[1,2]{1,0:T(1,128)} %mobile.1, f32[1,2]{1,0:T(1,128)} %spread.1, s32[1,2]{1,0:T(1,128)} %owner.1, f32[1,2,32,32,128]{4,3,2,1,0:T(8,128)} %phase.3, f32[1,2,32,32,128]{4,3,2,1,0:T(8,128)} %phase.3, ...), custom_call_target="tpu_custom_call" | custom-call | tf_op jit(solution)/shard_map/pack_y/pallas_call | solution.py:48
  2.7 0.0 copy-start.2
  2.7 1.5 %collective-permute-start.4 = (f32[33,8,128]{2,1,0:T(8,128)}, f32[33,8,128]{2,1,0:T(8,128)S(1)}, u32[]{:S(2)}, u32[]{:S(2)}) collective-permute-start(f32[33,8,128]{2,1,0:T(8,128)} %get-tuple-element.64), channel_id=1, source_target_pairs={{0,1},{1,2},{2,3},{3,4},{4,5},{5,6},{6,7},{7,0},{8,9},{9,10},{10,1... | collective-permute-start | bytes 405512 | tf_op jit(solution)/shard_map/ppermute | solution.py:534
  4.2 1.4 %collective-permute-start.5 = (f32[33,8,128]{2,1,0:T(8,128)}, f32[33,8,128]{2,1,0:T(8,128)S(1)}, u32[]{:S(2)}, u32[]{:S(2)}) collective-permute-start(f32[33,8,128]{2,1,0:T(8,128)} %get-tuple-element.65), channel_id=1, source_target_pairs={{0,7},{1,0},{2,1},{3,2},{4,3},{5,4},{6,5},{7,6},{8,15},{9,8},{10,9... | collective-permute-start | bytes 405512 | tf_op jit(solution)/shard_map/ppermute | solution.py:535
  5.6 0.0 copy-done.1
  5.6 0.0 copy-done
  5.6 4.6 %inner.5 = (f32[520,128]{1,0:T(8,128)S(1)}, f32[520,128]{1,0:T(8,128)}) custom-call(f32[24,128]{1,0:T(8,128)S(1)} %get-tuple-element.63.own, f32[1,2,32,32,128]{4,3,2,1,0:T(8,128)S(1)} %copy-done, f32[1,2,32,32,128]{4,3,2,1,0:T(8,128)S(1)} %copy-done.1), custom_call_target="tpu_custom_call" | custom-call | flops 100000000 | bytes 25165824 | tf_op jit(solution)/shard_map/inner/pallas_call | solution.py:284
  10.2 2.6 %collective-permute-start.7 = (f32[520,128]{1,0:T(8,128)}, f32[520,128]{1,0:T(8,128)S(1)}, u32[]{:S(2)}, u32[]{:S(2)}) collective-permute-start(f32[520,128]{1,0:T(8,128)} %get-tuple-element.71), channel_id=1, source_target_pairs={{0,5},{1,4},{2,7},{3,6},{4,1},{5,0},{6,3},{7,2},{8,13},{9,12},{10,... | collective-permute-start | bytes 798728 | tf_op jit(solution)/shard_map/ppermute | solution.py:514
  12.8 0.3 collective-permute-start.6
  13.1 0.0 copy-done.2
  13.2 0.0 collective-permute-done.4.y_lo
  13.2 0.0 collective-permute-done.5.y_hi
  13.3 8.7 %conditional.3 = (f32[608,128]{1,0:T(8,128)}, f32[608,128]{1,0:T(8,128)}, f32[520,128]{1,0:T(8,128)}, f32[520,128]{1,0:T(8,128)}) conditional(s32[]{:T(128)} %bitcast, (f32[608,128]{1,0:T(8,128)S(1)}, f32[608,128]{1,0:T(8,128)S(1)}, f32[24,128]{1,0:T(8,128)S(1)}, f32[1,2,32,32,128]{4,3,2,1,0:T(8,128)S(1)}, ...), branch_computations={%region_0.0_spmd, %region_1.0_spmd} | conditional | flops 100000000 | bytes 27656304 | solution.py:554
  13.3 0.1 collective-permute-start.2
  13.3 1.7 %collective-permute-start.3 = (f32[608,128]{1,0:T(8,128)S(1)}, f32[608,128]{1,0:T(8,128)}, u32[]{:S(2)}, u32[]{:S(2)}) collective-permute-start(f32[608,128]{1,0:T(8,128)S(1)} %get-tuple-element.38), channel_id=1, source_target_pairs={{0,24},{8,0},{16,8},{24,16},{1,25},{9,1},{17,9},{25,17},{2,26},{10... | collective-permute-start | bytes 933896 | tf_op jit(solution)/shard_map/cond/branch_1_fun/ppermute | solution.py:552
  15.1 4.6 %inner.4 = (f32[520,128]{1,0:T(8,128)}, f32[520,128]{1,0:T(8,128)}) custom-call(f32[24,128]{1,0:T(8,128)S(1)} %get-tuple-element.39.own, f32[1,2,32,32,128]{4,3,2,1,0:T(8,128)S(1)} %get-tuple-element.40.phase, f32[1,2,32,32,128]{4,3,2,1,0:T(8,128)S(1)} %get-tuple-element.41.solute), custom_call_target="tpu_custom_call" | custom-call | flops 100000000 | bytes 25165824 | tf_op jit(solution)/shard_map/cond/branch_1_fun/inner/pallas_call | solution.py:284
  19.7 1.5 %collective-permute-done.2 = f32[608,128]{1,0:T(8,128)} collective-permute-done((f32[608,128]{1,0:T(8,128)S(1)}, f32[608,128]{1,0:T(8,128)}, u32[]{:S(2)}, u32[]{:S(2)}) %collective-permute-start.2) | collective-permute-done | bytes 311328 | tf_op jit(solution)/shard_map/cond/branch_1_fun/ppermute | solution.py:552
  21.2 0.8 collective-permute-done.3
  22.0 1.6 %collective-permute-start.8 = (f32[520,128]{1,0:T(8,128)}, f32[520,128]{1,0:T(8,128)S(1)}, u32[]{:S(2)}, u32[]{:S(2)}) collective-permute-start(f32[520,128]{1,0:T(8,128)} %get-tuple-element.72), channel_id=1, source_target_pairs={{0,6},{1,7},{2,4},{3,5},{4,2},{5,3},{6,0},{7,1},{8,14},{9,15},{10,... | collective-permute-start | bytes 798728 | tf_op jit(solution)/shard_map/ppermute | solution.py:514
  23.6 1.3 %collective-permute-start.9 = (f32[520,128]{1,0:T(8,128)}, f32[520,128]{1,0:T(8,128)}, u32[]{:S(2)}, u32[]{:S(2)}) collective-permute-start(f32[520,128]{1,0:T(8,128)} %get-tuple-element.73), channel_id=1, source_target_pairs={{0,7},{1,6},{2,5},{3,4},{4,3},{5,2},{6,1},{7,0},{8,15},{9,14},{10,... | collective-permute-start | bytes 798728 | tf_op jit(solution)/shard_map/ppermute | solution.py:514
  24.9 9.8 %outer.1 = f32[4,520,128]{2,1,0:T(8,128)S(1)} custom-call(f32[24,128]{1,0:T(8,128)S(1)} %get-tuple-element.63.own, f32[1,2,32,32,128]{4,3,2,1,0:T(8,128)S(1)} %copy-done, f32[1,2,32,32,128]{4,3,2,1,0:T(8,128)S(1)} %copy-done.1, f32[33,8,128]{2,1,0:T(8,128)S(1)} %collective-permute-done.4.y_lo, f32[33,8,128]{2,1,0:T(8,128)S(1)} %collective-permute-done.5.y_hi, ...), custom_call_target="tpu_custom_call" | custom-call | flops 100000000 | bytes 41943040 | tf_op jit(solution)/shard_map/outer/pallas_call | solution.py:380
  34.7 26.1 %conditional.4 = (f32[4,520,128]{2,1,0:T(8,128)S(1)}) conditional(s32[]{:T(128)} %bitcast, f32[4,520,128]{2,1,0:T(8,128)S(1)} %outer.1, f32[4,520,128]{2,1,0:T(8,128)S(1)} %outer.1), branch_computations={%region_2.0_spmd, %region_3.0_spmd} | conditional | bytes 2129928 | solution.py:522
  34.7 26.0 %all_to_all.17 = f32[4,520,128]{2,1,0:T(8,128)S(1)} all-to-all(f32[4,520,128]{2,1,0:T(8,128)S(1)} %param.3), channel_id=1, replica_groups={{0,1,2,3},{4,5,6,7},{8,9,10,11},{12,13,14,15},{16,17,18,19},{20,21,22,2..., dimensions={0} | all-to-all | bytes 2129920 | tf_op jit(solution)/shard_map/cond/branch_1_fun/all_to_all | solution.py:520
  60.7 0.0 collective-permute-done.7.refs_1_
  60.7 0.0 collective-permute-done.6.refs_0_
  60.7 0.0 collective-permute-done.8.refs_2_
  60.7 0.0 collective-permute-done.9.refs_3_
  60.8 1.9 %route.1 = (f32[4,2,256,128]{3,2,1,0:T(8,128)S(1)}, f32[2,256,128]{2,1,0:T(8,128)S(1)}, f32[2,256,128]{2,1,0:T(8,128)S(1)}, f32[2,256,128]{2,1,0:T(8,128)S(1)}, ...) custom-call(f32[4,520,128]{2,1,0:T(8,128)S(1)} %get-tuple-element.88.near, f32[520,128]{1,0:T(8,128)S(1)} %collective-permute-done.6.refs_0_, ...), custom_call_target="tpu_custom_call" | custom-call | tf_op jit(solution)/shard_map/route/pallas_call | solution.py:430
  62.7 1.4 %collective-permute-start.10 = (f32[2,256,128]{2,1,0:T(8,128)S(1)}, f32[2,256,128]{2,1,0:T(8,128)S(1)}, u32[]{:S(2)}, u32[]{:S(2)}) collective-permute-start(f32[2,256,128]{2,1,0:T(8,128)S(1)} %get-tuple-element.76), channel_id=1, source_target_pairs={{0,4},{1,5},{2,6},{3,7},{4,0},{5,1},{6,2},{7,3},{8,12},{9,13},{10,... | collective-permute-start | bytes 786440 | tf_op jit(solution)/shard_map/ppermute | solution.py:514
  64.1 1.3 %collective-permute-start.11 = (f32[2,256,128]{2,1,0:T(8,128)S(1)}, f32[2,256,128]{2,1,0:T(8,128)S(1)}, u32[]{:S(2)}, u32[]{:S(2)}) collective-permute-start(f32[2,256,128]{2,1,0:T(8,128)S(1)} %get-tuple-element.77), channel_id=1, source_target_pairs={{0,5},{1,4},{2,7},{3,6},{4,1},{5,0},{6,3},{7,2},{8,13},{9,12},{10,... | collective-permute-start | bytes 786440 | tf_op jit(solution)/shard_map/ppermute | solution.py:514
  65.4 1.0 collective-permute-start.12
  66.4 2.2 %collective-permute-start.13 = (f32[2,256,128]{2,1,0:T(8,128)S(1)}, f32[2,256,128]{2,1,0:T(8,128)S(1)}, u32[]{:S(2)}, u32[]{:S(2)}) collective-permute-start(f32[2,256,128]{2,1,0:T(8,128)S(1)} %get-tuple-element.79), channel_id=1, source_target_pairs={{0,7},{1,6},{2,5},{3,4},{4,3},{5,2},{6,1},{7,0},{8,15},{9,14},{10,... | collective-permute-start | bytes 786440 | tf_op jit(solution)/shard_map/ppermute | solution.py:514
  68.6 35.9 %conditional.5 = (f32[4,2,256,128]{3,2,1,0:T(8,128)S(1)}) conditional(s32[]{:T(128)} %bitcast, f32[4,2,256,128]{3,2,1,0:T(8,128)S(1)} %get-tuple-element.75, f32[4,2,256,128]{3,2,1,0:T(8,128)S(1)} %get-tuple-element.75), branch_computations={%region_4.0_spmd, %region_5.0_spmd} | conditional | bytes 2097160 | solution.py:522
  68.6 35.9 %all_to_all.19 = f32[4,2,256,128]{3,2,1,0:T(8,128)S(1)} all-to-all(f32[4,2,256,128]{3,2,1,0:T(8,128)S(1)} %param.5), channel_id=1, replica_groups={{0,1,2,3},{4,5,6,7},{8,9,10,11},{12,13,14,15},{16,17,18,19},{20,21,22,2..., dimensions={0} | all-to-all | bytes 2097152 | tf_op jit(solution)/shard_map/cond/branch_1_fun/all_to_all | solution.py:520
  104.5 0.0 collective-permute-done.10.refs_0_
  104.5 0.0 collective-permute-done.11.refs_1_
  104.5 1.0 collective-permute-done.12.refs_2_
  105.5 4.7 %collective-permute-done.13.refs_3_ = f32[2,256,128]{2,1,0:T(8,128)S(1)} collective-permute-done((f32[2,256,128]{2,1,0:T(8,128)S(1)}, f32[2,256,128]{2,1,0:T(8,128)S(1)}, u32[]{:S(2)}, u32[]{:S(2)}) %collective-permute-start.13) | collective-permute-done | bytes 262176 | tf_op jit(solution)/shard_map/ppermute | solution.py:514
  110.2 2.0 %settle.1 = (f32[1,2,32,32,128]{4,3,2,1,0:T(8,128)}, f32[1,2,32,32,128]{4,3,2,1,0:T(8,128)}) custom-call(s32[16]{0:T(128)S(1)} %get-tuple-element.74.table, f32[4,2,256,128]{3,2,1,0:T(8,128)S(1)} %get-tuple-element.89.near, f32[2,256,128]{2,1,0:T(8,128)S(1)} %collective-permute-done.10.refs_0_, f32[2,256,128]{2,1,0:T(8,128)S(1)} %collective-permute-done.11.refs_1_, ...), custom_call_target="tpu_custom_call" | custom-call | tf_op jit(solution)/shard_map/settle/pallas_call | solution.py:494
  (1 shorter events, 0.0 us)
Async XLA Ops:
  0.6 5.0 %copy-start.1 = (f32[1,2,32,32,128]{4,3,2,1,0:T(8,128)S(1)}, f32[1,2,32,32,128]{4,3,2,1,0:T(8,128)}, u32[]{:S(2)}) copy-start(f32[1,2,32,32,128]{4,3,2,1,0:T(8,128)} %solute.3) | copy-start | bytes 3145732
  0.6 5.0 %copy-start = (f32[1,2,32,32,128]{4,3,2,1,0:T(8,128)S(1)}, f32[1,2,32,32,128]{4,3,2,1,0:T(8,128)}, u32[]{:S(2)}) copy-start(f32[1,2,32,32,128]{4,3,2,1,0:T(8,128)} %phase.3) | copy-start | bytes 3145732
  2.7 10.5 %copy-start.2 = (s32[1,2]{1,0:T(1,128)S(1)}, s32[1,2]{1,0:T(1,128)}, u32[]{:S(2)}) copy-start(s32[1,2]{1,0:T(1,128)} %owner.1) | copy-start | bytes 28
  2.7 10.5 %collective-permute-start.4 = (f32[33,8,128]{2,1,0:T(8,128)}, f32[33,8,128]{2,1,0:T(8,128)S(1)}, u32[]{:S(2)}, u32[]{:S(2)}) collective-permute-start(f32[33,8,128]{2,1,0:T(8,128)} %get-tuple-element.64), channel_id=1, source_target_pairs={{0,1},{1,2},{2,3},{3,4},{4,5},{5,6},{6,7},{7,0},{8,9},{9,10},{10,1... | collective-permute-start | bytes 405512 | tf_op jit(solution)/shard_map/ppermute | solution.py:534
  4.2 9.0 %collective-permute-start.5 = (f32[33,8,128]{2,1,0:T(8,128)}, f32[33,8,128]{2,1,0:T(8,128)S(1)}, u32[]{:S(2)}, u32[]{:S(2)}) collective-permute-start(f32[33,8,128]{2,1,0:T(8,128)} %get-tuple-element.65), channel_id=1, source_target_pairs={{0,7},{1,0},{2,1},{3,2},{4,3},{5,4},{6,5},{7,6},{8,15},{9,8},{10,9... | collective-permute-start | bytes 405512 | tf_op jit(solution)/shard_map/ppermute | solution.py:535
  10.2 50.6 %collective-permute-start.7 = (f32[520,128]{1,0:T(8,128)}, f32[520,128]{1,0:T(8,128)S(1)}, u32[]{:S(2)}, u32[]{:S(2)}) collective-permute-start(f32[520,128]{1,0:T(8,128)} %get-tuple-element.71), channel_id=1, source_target_pairs={{0,5},{1,4},{2,7},{3,6},{4,1},{5,0},{6,3},{7,2},{8,13},{9,12},{10,... | collective-permute-start | bytes 798728 | tf_op jit(solution)/shard_map/ppermute | solution.py:514
  12.8 47.9 %collective-permute-start.6 = (f32[520,128]{1,0:T(8,128)S(1)}, f32[520,128]{1,0:T(8,128)S(1)}, u32[]{:S(2)}, u32[]{:S(2)}) collective-permute-start(f32[520,128]{1,0:T(8,128)S(1)} %get-tuple-element.66._), channel_id=1, source_target_pairs={{0,4},{1,5},{2,6},{3,7},{4,0},{5,1},{6,2},{7,3},{8,12},{9,13},{10,... | collective-permute-start | bytes 798728 | tf_op jit(solution)/shard_map/ppermute | solution.py:514
  13.3 8.0 %collective-permute-start.2 = (f32[608,128]{1,0:T(8,128)S(1)}, f32[608,128]{1,0:T(8,128)}, u32[]{:S(2)}, u32[]{:S(2)}) collective-permute-start(f32[608,128]{1,0:T(8,128)S(1)} %get-tuple-element.37), channel_id=1, source_target_pairs={{0,8},{8,16},{16,24},{24,0},{1,9},{9,17},{17,25},{25,1},{2,10},{10... | collective-permute-start | bytes 933896 | tf_op jit(solution)/shard_map/cond/branch_1_fun/ppermute | solution.py:552
  13.3 8.7 %collective-permute-start.3 = (f32[608,128]{1,0:T(8,128)S(1)}, f32[608,128]{1,0:T(8,128)}, u32[]{:S(2)}, u32[]{:S(2)}) collective-permute-start(f32[608,128]{1,0:T(8,128)S(1)} %get-tuple-element.38), channel_id=1, source_target_pairs={{0,24},{8,0},{16,8},{24,16},{1,25},{9,1},{17,9},{25,17},{2,26},{10... | collective-permute-start | bytes 933896 | tf_op jit(solution)/shard_map/cond/branch_1_fun/ppermute | solution.py:552
  22.0 38.7 %collective-permute-start.8 = (f32[520,128]{1,0:T(8,128)}, f32[520,128]{1,0:T(8,128)S(1)}, u32[]{:S(2)}, u32[]{:S(2)}) collective-permute-start(f32[520,128]{1,0:T(8,128)} %get-tuple-element.72), channel_id=1, source_target_pairs={{0,6},{1,7},{2,4},{3,5},{4,2},{5,3},{6,0},{7,1},{8,14},{9,15},{10,... | collective-permute-start | bytes 798728 | tf_op jit(solution)/shard_map/ppermute | solution.py:514
  23.6 37.2 %collective-permute-start.9 = (f32[520,128]{1,0:T(8,128)}, f32[520,128]{1,0:T(8,128)}, u32[]{:S(2)}, u32[]{:S(2)}) collective-permute-start(f32[520,128]{1,0:T(8,128)} %get-tuple-element.73), channel_id=1, source_target_pairs={{0,7},{1,6},{2,5},{3,4},{4,3},{5,2},{6,1},{7,0},{8,15},{9,14},{10,... | collective-permute-start | bytes 798728 | tf_op jit(solution)/shard_map/ppermute | solution.py:514
  62.7 41.8 %collective-permute-start.10 = (f32[2,256,128]{2,1,0:T(8,128)S(1)}, f32[2,256,128]{2,1,0:T(8,128)S(1)}, u32[]{:S(2)}, u32[]{:S(2)}) collective-permute-start(f32[2,256,128]{2,1,0:T(8,128)S(1)} %get-tuple-element.76), channel_id=1, source_target_pairs={{0,4},{1,5},{2,6},{3,7},{4,0},{5,1},{6,2},{7,3},{8,12},{9,13},{10,... | collective-permute-start | bytes 786440 | tf_op jit(solution)/shard_map/ppermute | solution.py:514
  64.1 40.4 %collective-permute-start.11 = (f32[2,256,128]{2,1,0:T(8,128)S(1)}, f32[2,256,128]{2,1,0:T(8,128)S(1)}, u32[]{:S(2)}, u32[]{:S(2)}) collective-permute-start(f32[2,256,128]{2,1,0:T(8,128)S(1)} %get-tuple-element.77), channel_id=1, source_target_pairs={{0,5},{1,4},{2,7},{3,6},{4,1},{5,0},{6,3},{7,2},{8,13},{9,12},{10,... | collective-permute-start | bytes 786440 | tf_op jit(solution)/shard_map/ppermute | solution.py:514
  65.4 40.1 %collective-permute-start.12 = (f32[2,256,128]{2,1,0:T(8,128)S(1)}, f32[2,256,128]{2,1,0:T(8,128)S(1)}, u32[]{:S(2)}, u32[]{:S(2)}) collective-permute-start(f32[2,256,128]{2,1,0:T(8,128)S(1)} %get-tuple-element.78), channel_id=1, source_target_pairs={{0,6},{1,7},{2,4},{3,5},{4,2},{5,3},{6,0},{7,1},{8,14},{9,15},{10,... | collective-permute-start | bytes 786440 | tf_op jit(solution)/shard_map/ppermute | solution.py:514
  66.4 43.8 %collective-permute-start.13 = (f32[2,256,128]{2,1,0:T(8,128)S(1)}, f32[2,256,128]{2,1,0:T(8,128)S(1)}, u32[]{:S(2)}, u32[]{:S(2)}) collective-permute-start(f32[2,256,128]{2,1,0:T(8,128)S(1)} %get-tuple-element.79), channel_id=1, source_target_pairs={{0,7},{1,6},{2,5},{3,4},{4,3},{5,2},{6,1},{7,0},{8,15},{9,14},{10,... | collective-permute-start | bytes 786440 | tf_op jit(solution)/shard_map/ppermute | solution.py:514
